TPU v7x, 32 devices: a whole 2x2x4 slice. The times are simulated.
32 devices in a mesh: grp: 2 (over y), chol: 8 (over z, core), walk: 2 (over x), orb: 1.
Axes of the slice: x: 2, y: 2, z: 4, core: 2. Of those that a mesh axis runs over, the one named last changes fastest.
Arguments:
- green_blocks: bfloat16 [16, 1024, 256], P(('grp', 'walk'), 'chol', 'orb'), parts along dimension 0, may hold values from -6 to 6
- half_chol: bfloat16 [32, 1024, 256], P(('grp', 'chol'), None, 'orb'), parts along dimension 0, may hold values from -0.125 to 0.125
- full_chol: bfloat16 [32, 1024, 1024], P(('grp', 'chol'), 'orb'), parts along dimension 0, may hold values from -0.125 to 0.125
- meanfield: float32 [32], P(('grp', 'chol')), parts along dimension 0, may hold values from -60 to 60
- noise_draws: float32 [16, 16], P(('grp', 'walk'), 'chol'), parts along dimension 0, may hold values from -6 to 6
- orbitals: float32 [1, 1024, 16, 256], P('orb', 'chol', ('grp', 'walk')), parts along dimension 2, may hold values from -6 to 6
Outputs:
- walkers_next: float32 [1, 1024, 16, 256], P('orb', 'chol', ('grp', 'walk')), parts along dimension 2
- bias_shift: float32 [16, 16], P(('grp', 'walk'), 'chol'), parts along dimension 0
There are 2 independent parts, one for each index of `grp`. A program takes and returns all parts, laid end to end along the dimension named above; each array names one. Nothing has to cross between parts.
All inputs are finite; a program needn't handle non-finite values.
Results may differ from a plain program's by a relative error of at most 0.0015.
Values may be sent and summed in bfloat16 or wider, within the bound.
No kernel may reach another device: no remote copies, remote signals or barrier semaphores. Data moves between devices by JAX's collectives and lax.ppermute only.
A program may use at most 64 MiB of HBM per device.

v0:
```python
import jax
import jax.numpy as jnp
from jax import lax
from jax.sharding import PartitionSpec as P

time_root = 0.1


def per_device(green_blocks, half_chol, full_chol, meanfield, noise_draws, orbitals):
    walkers_here = green_blocks.shape[0]
    chol_here = half_chol.shape[0]
    half_rows = full_chol.shape[1]
    orbital_count = full_chol.shape[2]
    occupied = orbitals.shape[3]
    rows_here = orbitals.shape[1]
    partial_bias = jnp.einsum(
        "wki,cki->wc",
        lax.all_gather(green_blocks, "chol", axis=1, tiled=True),
        half_chol,
        preferred_element_type=jnp.float32,
    )
    force_bias = lax.psum(partial_bias, "orb")
    bias_shift = jnp.clip(time_root * (force_bias - meanfield[None, :]), -1.0, 1.0)
    shifted_field = noise_draws - bias_shift
    combined = jnp.zeros((walkers_here, half_rows, orbital_count), jnp.float32)
    for chol_index in range(chol_here):
        combined = combined + shifted_field[:, chol_index, None, None] * full_chol[chol_index][
            None
        ].astype(jnp.float32)
    operator_rows = (time_root * combined).astype(jnp.bfloat16)

    def apply_operator(vector):
        both_halves = lax.all_gather(vector, "orb", axis=0, tiled=True)
        fold_start = jnp.zeros((walkers_here, half_rows, occupied), jnp.float32)
        running = fold_start
        shard_piece = lax.all_gather(both_halves, "chol", axis=1, tiled=True)
        row_count = shard_piece.shape[1]
        for half_index in range(shard_piece.shape[0]):
            col_block = lax.dynamic_slice_in_dim(
                operator_rows, half_index * half_rows, row_count, 2
            )
            running = running + lax.dot_general(
                col_block,
                shard_piece[half_index],
                (((2,), (0,)), ((0,), (1,))),
                preferred_element_type=jnp.float32,
            )
        summed = lax.psum(running, "chol")
        chol_slot = lax.axis_index("chol")
        owned_rows = lax.dynamic_slice_in_dim(summed, chol_slot * rows_here, rows_here, 1)
        return jnp.transpose(owned_rows, (1, 0, 2))[None]

    first_term = apply_operator(orbitals.astype(jnp.bfloat16))
    second_term = apply_operator(first_term.astype(jnp.bfloat16))
    walkers_next = orbitals + first_term + 0.5 * second_term
    return (walkers_next, bias_shift)


def solution(mesh):
    placed = (
        P(("grp", "walk"), "chol", "orb"),
        P(("grp", "chol"), None, "orb"),
        P(("grp", "chol"), "orb", None),
        P(("grp", "chol")),
        P(("grp", "walk"), "chol"),
        P("orb", "chol", ("grp", "walk"), None),
    )
    return jax.shard_map(
        per_device,
        mesh=mesh,
        in_specs=placed,
        out_specs=(P("orb", "chol", ("grp", "walk"), None), P(("grp", "walk"), "chol")),
        check_vma=False,
    )
```

profile of v0, /device:TPU:0, one launch (start us, length us, event | category | flops | bytes accessed | tf_op | source)
XLA Modules:
  0.0 320.3 jit_solution(9149850155638346892)
XLA Ops:
  7.2 0.0 all-gather.5.cloned.1.call-start
  7.2 1.8 copy.8
  9.0 0.0 all-gather.5.cloned.1.call-update
  9.1 0.0 all-gather.7.cloned.1.call-start
  9.1 1.8 copy.15
  10.9 0.0 all-gather.7.cloned.1.call-update
  11.0 0.0 all-reduce.3.cloned.1.call-start
  11.0 2.6 copy.9
  13.6 0.0 copy-start.1
  13.6 0.0 copy-start.2
  13.6 6.6 %bitcast_convert_fusion.1 = (f32[1024,1024]{1,0:T(8,128)}, f32[1024,1024]{1,0:T(8,128)}) fusion(bf16[2,1024,1024]{2,1,0:T(8,128)(2,1)} %param.8), kind=kLoop, calls=%fused_computation.14 | loop fusion | flops 2097152 | bytes 12582912 | tf_op jit(solution)/shard_map/mul | solution.py:27
  20.3 23.5 %all-gather.5.cloned.1.call-done = bf16[4,1024,256]{1,0,2:T(4,128)(2,1)} async-done(((bf16[4,128,256]{1,0,2:T(4,128)(2,1)}), bf16[4,1024,256]{1,0,2:T(4,128)(2,1)}) %all-gather.5.cloned.1.call-update) | async-done | bytes 2097168 | tf_op jit(solution)/shard_map/all_gather | solution.py:18
  43.7 0.0 copy-done.1
  43.7 0.0 copy-done.2
  43.7 5.0 %fusion.18 = (f32[4,2]{0,1:T(2,128)S(1)}, f32[4,2]{0,1:T(2,128)}) fusion(f32[4,2]{0,1:T(2,128)S(1)} %copy-done.1, f32[2]{0:T(128)S(1)} %copy-done.2, bf16[4,1024,256]{1,0,2:T(4,128)(2,1)} %all-gather.5.cloned.1.call-done, bf16[2,1024,256]{1,0,2:T(2,128)(2,1)S(1)} %copy.9), kind=kOutput, calls=%fused_computation.28 | convolution fusion | flops 4194336 | bytes 3145832 | tf_op jit(solution)/shard_map/wki,cki->wc/dot_general | solution.py:16
  48.7 24.8 %all-gather.7.cloned.1.call-done = bf16[1,1024,4,256]{3,1,2,0:T(8,128)(2,1)} async-done(((bf16[1,128,4,256]{3,1,2,0:T(8,128)(2,1)}), bf16[1,1024,4,256]{3,1,2,0:T(8,128)(2,1)}) %all-gather.7.cloned.1.call-update) | async-done | bytes 2097168 | tf_op jit(solution)/shard_map/all_gather | solution.py:36
  73.5 7.1 %fusion.1 = f32[4,1024,256]{2,1,0:T(8,128)} fusion(f32[1024,1024]{1,0:T(8,128)} %get-tuple-element.5, f32[4]{0:T(128)S(1)} %get-tuple-element.7, f32[1024,1024]{1,0:T(8,128)} %get-tuple-element.4, f32[4]{0:T(128)S(1)} %get-tuple-element.6, bf16[1,1024,4,256]{3,1,2,0:T(8,128)(2,1)} %all-gather.7.cloned.1.call-done), kind=kOutput, calls=%fused_computation.2 | convolution fusion | flops 2168455168 | bytes 14680096 | tf_op jit(solution)/shard_map/dot_general | solution.py:42
  80.6 0.0 all-reduce.3.cloned.1.call-update
  80.7 0.0 all-gather.9.cloned.1.call-start
  80.7 96.1 %all-reduce.3.cloned.1.call-done = f32[4,1024,256]{2,1,0:T(8,128)} async-done(((f32[4,1024,256]{2,1,0:T(8,128)}), f32[4,1024,256]{2,1,0:T(8,128)}) %all-reduce.3.cloned.1.call-update) | async-done | bytes 4194320 | tf_op jit(solution)/shard_map/psum | solution.py:48
  176.8 1.8 bitcast_convert_fusion.2
  178.6 0.0 all-gather.9.cloned.1.call-update
  178.6 0.0 all-reduce.5.cloned.1.call-start
  178.6 29.4 %all-gather.9.cloned.1.call-done = bf16[1024,4,256]{2,0,1:T(8,128)(2,1)} async-done(((bf16[128,4,256]{2,0,1:T(8,128)(2,1)}), bf16[1024,4,256]{2,0,1:T(8,128)(2,1)}) %all-gather.9.cloned.1.call-update) | async-done | bytes 2097168 | tf_op jit(solution)/shard_map/all_gather | solution.py:36
  208.0 7.1 %fusion = f32[4,1024,256]{2,1,0:T(8,128)} fusion(bf16[1024,4,256]{2,0,1:T(8,128)(2,1)} %all-gather.9.cloned.1.call-done, f32[1024,1024]{1,0:T(8,128)} %get-tuple-element.5, f32[4]{0:T(128)S(1)} %get-tuple-element.7, f32[1024,1024]{1,0:T(8,128)} %get-tuple-element.4, f32[4]{0:T(128)S(1)} %get-tuple-element.6), kind=kOutput, calls=%fused_computation.1 | convolution fusion | flops 2168455168 | bytes 14680096 | tf_op jit(solution)/shard_map/dot_general | solution.py:42
  215.1 0.0 copy-start
  215.1 0.0 all-reduce.5.cloned.1.call-update
  215.1 96.2 %all-reduce.5.cloned.1.call-done = f32[4,1024,256]{2,1,0:T(8,128)} async-done(((f32[4,1024,256]{2,1,0:T(8,128)}), f32[4,1024,256]{2,1,0:T(8,128)}) %all-reduce.5.cloned.1.call-update) | async-done | bytes 4194320 | tf_op jit(solution)/shard_map/psum | solution.py:48
  311.3 0.0 copy-done
  311.3 1.4 bitcast_add_fusion
  312.7 1.1 copy.12
  (1 shorter events, 0.0 us)
Async XLA Ops:
  7.2 36.6 %all-gather.5.cloned.1.call-start = ((), (), s32[]{:S(2)}) async-start(), calls=%async_computation | async-start | bytes 2359296 | tf_op jit(solution)/shard_map/all_gather | solution.py:18
  9.1 64.5 %all-gather.7.cloned.1.call-start = ((), (), s32[]{:S(2)}) async-start(), calls=%async_computation.1 | async-start | bytes 2359296 | tf_op jit(solution)/shard_map/all_gather | solution.py:36
  11.0 165.8 %all-reduce.3.cloned.1.call-start = ((), (), s32[]{:S(2)}) async-start(), calls=%async_computation.2 | async-start | bytes 8388608 | tf_op jit(solution)/shard_map/psum | solution.py:48
  13.6 30.1 %copy-start.1 = (f32[4,2]{0,1:T(2,128)S(1)}, f32[4,2]{0,1:T(2,128)}, u32[]{:S(2)}) copy-start(f32[4,2]{0,1:T(2,128)} %param.10) | copy-start | bytes 100
  13.6 30.1 %copy-start.2 = (f32[2]{0:T(128)S(1)}, f32[2]{0:T(128)}, u32[]{:S(2)}) copy-start(f32[2]{0:T(128)} %param.9) | copy-start | bytes 28
  80.7 127.4 %all-gather.9.cloned.1.call-start = ((), (), s32[]{:S(2)}) async-start(), calls=%async_computation.4 | async-start | bytes 2359296 | tf_op jit(solution)/shard_map/all_gather | solution.py:36
  178.6 132.7 %all-reduce.5.cloned.1.call-start = ((), (), s32[]{:S(2)}) async-start(), calls=%async_computation.3 | async-start | bytes 8388608 | tf_op jit(solution)/shard_map/psum | solution.py:48
  215.1 96.2 %copy-start = (f32[1,128,4,256]{3,2,1,0:T(4,128)S(1)}, f32[1,128,4,256]{3,2,1,0:T(4,128)}, u32[]{:S(2)}) copy-start(f32[1,128,4,256]{3,2,1,0:T(4,128)} %param.11) | copy-start | bytes 1572868
Sparse Core Ops, SparseCore 0:
  10.2 33.5 all-gather.4
  45.3 28.1 all-gather.6
  80.8 95.9 all-reduce.2
  178.8 29.1 all-gather.8
  215.3 95.9 all-reduce.4
where the time goes:
time: 321 us; the launch traced here: 320 us
  waiting for transfers between devices  270 us (84%)
  matrix products  19.2 us (6%)
  between operations  13.8 us (4%)
  local copies, waits for them, and re-layouts  9.18 us (3%)
  other arithmetic  7.99 us (2%)
    psum x2, waiting for transfers between devices, apply_operator(): summed = lax.psum(running, 'chol')  192 us
    all_gather x2, waiting for transfers between devices, apply_operator(): shard_piece = lax.all_gather(both_halves, 'chol', axis=1, tiled=True)  54.2 us
    all_gather x1, waiting for transfers between devices, per_device(): lax.all_gather(green_blocks, 'chol', axis=1, tiled=True)  23.5 us
    dot_general x2, matrix products, apply_operator(): lax.dot_general(col_block, shard_piece[half_index], (((2,), (0,)), ((0,),...  14.2 us
    unnamed x10, local copies, waits for them, and re-layouts  7.4 us
    mul x1, other arithmetic, per_device(): shifted_field[:, chol_index, None, None]  6.62 us
  transfers between devices with their start and end apart: 5, of which 5 were waited for; matrix products, arithmetic and copies ran while one was open for 5% of the time, Pallas kernels for 0%

commit v1 on v0

--- a/solution.py
+++ b/solution.py
@@ -6,7 +6,7 @@
 time_root = 0.1
 
 
-def per_device(green_blocks, half_chol, full_chol, meanfield, noise_draws, orbitals):
+def general_device(green_blocks, half_chol, full_chol, meanfield, noise_draws, orbitals):
     walkers_here = green_blocks.shape[0]
     chol_here = half_chol.shape[0]
     half_rows = full_chol.shape[1]
@@ -31,8 +31,7 @@
 
     def apply_operator(vector):
         both_halves = lax.all_gather(vector, "orb", axis=0, tiled=True)
-        fold_start = jnp.zeros((walkers_here, half_rows, occupied), jnp.float32)
-        running = fold_start
+        running = jnp.zeros((walkers_here, half_rows, occupied), jnp.float32)
         shard_piece = lax.all_gather(both_halves, "chol", axis=1, tiled=True)
         row_count = shard_piece.shape[1]
         for half_index in range(shard_piece.shape[0]):
@@ -56,6 +55,115 @@
     return (walkers_next, bias_shift)
 
 
+def row_device(chips):
+    devices = 2 * chips
+
+    def ring(value, step):
+        pairs = [(i, (i + 2 * step) % devices) for i in range(devices)]
+        return lax.ppermute(value, "chol", pairs)
+
+    def core(value):
+        return lax.ppermute(value, "chol", [(i, i ^ 1) for i in range(devices)])
+
+    def across(value):
+        return lax.ppermute(value, "walk", [(0, 1), (1, 0)])
+
+    def gather_ring(value):
+        half = value.shape[0] // 2
+        below = ring(value, 1)
+        above = ring(value, -1)
+        far = jnp.concatenate([ring(below[:half], 1), ring(above[half:], -1)])
+        return [value, above, far, below]
+
+    def device(green_blocks, half_chol, full_chol, meanfield, noise_draws, orbitals):
+        slot = lax.axis_index("chol")
+        z, k = slot // 2, slot % 2
+        x = lax.axis_index("walk")
+        walkers, rows_here, occupied = green_blocks.shape
+        order = full_chol.shape[2]
+        half_rows = full_chol.shape[1]
+        chip_rows = 2 * rows_here
+
+        def gather_rows(value):
+            mine = gather_ring(value)
+            theirs = [core(block) for block in mine]
+            blocks = []
+            for a, b in zip(mine, theirs, strict=True):
+                blocks.append(jnp.where(k == 0, a, b))
+                blocks.append(jnp.where(k == 0, b, a))
+            relative = jnp.stack(blocks, 1)
+            relative = jnp.roll(relative, 2 * z, axis=1)
+            return relative.reshape(walkers, half_rows, occupied)
+
+        mine_here = lax.dynamic_index_in_dim(full_chol, x, 0, False)
+        by_chip = mine_here.reshape(chips, 2, rows_here, order)
+
+        def for_chip(step):
+            return lax.dynamic_index_in_dim(by_chip, (z + step) % chips, 0, False)
+
+        far = for_chip(2)
+        far_low, far_high = ring(far[0], 1), ring(far[1], -1)
+        below, above = ring(for_chip(1), 1), ring(for_chip(-1), -1)
+        far_here = jnp.stack([ring(far_low, 1), ring(far_high, -1)])
+
+        half_by = half_chol.reshape(-1, chips, 2, rows_here, occupied)
+        half_mine = lax.dynamic_index_in_dim(half_by, k, 2, False)
+        half_theirs = core(lax.dynamic_index_in_dim(half_by, 1 - k, 2, False))
+        green_ring = gather_ring(green_blocks)
+        green_here = jnp.roll(jnp.stack(green_ring, 1), z, axis=1)
+        dims = "wzki,czki->wc"
+        bias_mine = jnp.einsum(dims, green_here, half_mine, preferred_element_type=jnp.float32)
+        bias_theirs = jnp.einsum(dims, green_here, half_theirs, preferred_element_type=jnp.float32)
+        force_bias = bias_mine + core(bias_theirs)
+        bias_shift = jnp.clip(time_root * (force_bias - meanfield[None, :]), -1.0, 1.0)
+        shifted_field = noise_draws - bias_shift
+        field_here = jnp.where(x == 0, shifted_field, shifted_field[:, ::-1])
+        field_chip = jnp.stack([field_here, core(field_here)], 1)
+        fields = [field_chip, ring(field_chip, -1), ring(field_chip, 2), ring(field_chip, 1)]
+
+        def pick(pair):
+            return jnp.where(k == 0, pair[0], pair[1]), jnp.where(k == 0, pair[1], pair[0])
+
+        def spread(pair):
+            mine, send = pick(pair)
+            both = jnp.stack([mine, core(send)])
+            return jnp.stack([both, across(both)], 1)
+
+        full_by = full_chol.reshape(2, chips, 2, rows_here, order)
+        own = lax.dynamic_index_in_dim(full_by, z, 1, False)
+        own = jnp.where(x == 0, own, own[::-1])
+        own_mine = jnp.where(k == 0, own[:, 0], own[:, 1])
+        own_send = jnp.where(k == 0, own[:, 1], own[:, 0])
+        own_rows = jnp.stack([own_mine, core(own_send)])
+        chol_rows = [own_rows, spread(above), spread(far_here), spread(below)]
+
+        summed = jnp.zeros((walkers, rows_here, order), jnp.float32)
+        for field, chols in zip(fields, chol_rows, strict=True):
+            for source in range(2):
+                wide = chols[source].astype(jnp.float32)
+                block = (
+                    field[:, source, 0, None, None] * wide[0]
+                    + field[:, source, 1, None, None] * wide[1]
+                )
+                summed = summed + (time_root * block).astype(jnp.bfloat16).astype(jnp.float32)
+        high = summed.astype(jnp.bfloat16)
+        low = (summed - high.astype(jnp.float32)).astype(jnp.bfloat16)
+
+        def apply_operator(vector):
+            dims = (((2,), (1,)), ((0,), (0,)))
+            return lax.dot_general(
+                high, vector, dims, preferred_element_type=jnp.float32
+            ) + lax.dot_general(low, vector, dims, preferred_element_type=jnp.float32)
+
+        start = jnp.transpose(orbitals[0], (1, 0, 2))
+        first_term = apply_operator(gather_rows(start.astype(jnp.bfloat16)))
+        second_term = apply_operator(gather_rows(first_term.astype(jnp.bfloat16)))
+        walkers_next = start + first_term + 0.5 * second_term
+        return (jnp.transpose(walkers_next, (1, 0, 2))[None], bias_shift)
+
+    return device
+
+
 def solution(mesh):
     placed = (
         P(("grp", "walk"), "chol", "orb"),
@@ -65,6 +173,11 @@
         P(("grp", "walk"), "chol"),
         P("orb", "chol", ("grp", "walk"), None),
     )
+    sizes = mesh.shape
+    if sizes["orb"] == 1 and sizes["walk"] == 2 and sizes["chol"] == 8:
+        per_device = row_device(sizes["chol"] // 2)
+    else:
+        per_device = general_device
     return jax.shard_map(
         per_device,
         mesh=mesh,

time: 321 us -> 191 us (0.60)
  waiting for transfers between devices: 270 us -> 85.6 us
  starting transfers between devices: 0.21 us -> 46.8 us
  local copies, waits for them, and re-layouts: 9.18 us -> 32.3 us
  matrix products: 19.2 us -> 4.86 us
  between operations: 13.8 us -> 1.21 us
  other arithmetic: 7.99 us -> 19.1 us
    psum x2 -> x0, waiting for transfers between devices: 192 us -> none  [apply_operator(): summed = lax.psum(running, 'chol')]
    ppermute x0 -> x39, waiting for transfers between devices: none -> 85.6 us  [the longest x21 54.4 us: ring(): return lax.ppermute(value, 'chol', pairs)]
    all_gather x3 -> x0, waiting for transfers between devices: 77.7 us -> none  [the longest x2 54.2 us: apply_operator(): shard_piece = lax.all_gather(both_halves, 'chol', axis=1, tiled=True)]
    ppermute x0 -> x39, starting transfers between devices: none -> 46.8 us  [the longest x21 40.9 us: ring(): return lax.ppermute(value, 'chol', pairs)]
    dot_general x3 -> x6, matrix products: 19.2 us -> 4.86 us  [the longest x1 1.48 us: device(): jnp.einsum(dims, green_here, half_theirs, preferred_element_type=jnp.floa...]
    unnamed x10 -> x40, local copies, waits for them, and re-layouts: 7.4 us -> 17.7 us
    unnamed x0 -> x16, other arithmetic: none -> 6.88 us
    mul x1 -> x0, other arithmetic: 6.62 us -> none  [per_device(): shifted_field[:, chol_index, None, None]]
  transfers between devices with their start and end apart: 5 -> 39, of which waited for: 5 -> 17; matrix products, arithmetic and copies ran while one was open for 5% -> 24% of each run, Pallas kernels for 0% -> 0%
where the time goes in v1:
time: 191 us; the launch traced here: 190 us
  waiting for transfers between devices  85.6 us (45%)
  starting transfers between devices  46.8 us (25%)
  local copies, waits for them, and re-layouts  32.3 us (17%)
  other arithmetic  19.1 us (10%)
  matrix products  4.86 us (3%)
    ppermute x21, waiting for transfers between devices, ring(): return lax.ppermute(value, 'chol', pairs)  54.4 us
    ppermute x21, starting transfers between devices, ring(): return lax.ppermute(value, 'chol', pairs)  40.9 us
    ppermute x3, waiting for transfers between devices, across(): return lax.ppermute(value, 'walk', [(0, 1), (1, 0)])  28.7 us
    unnamed x40, local copies, waits for them, and re-layouts  17.7 us
    unnamed x16, other arithmetic  6.88 us
    slice x6, local copies, waits for them, and re-layouts, gather_ring(): far = jnp.concatenate([ring(below[:half], 1), ring(above[half:], -1)])  3.98 us
  transfers between devices with their start and end apart: 39, of which 17 were waited for; matrix products, arithmetic and copies ran while one was open for 24% of the time, Pallas kernels for 0%

profile of v1, /device:TPU:0, one launch (start us, length us, event | category | flops | bytes accessed | tf_op | source)
XLA Modules:
  0.0 189.8 jit_solution(12440644943916340204)
XLA Ops:
  0.6 1.1 copy.38
  1.8 5.1 %collective-permute-start = (bf16[4,128,256]{1,0,2:T(4,128)(2,1)S(1)}, bf16[4,128,256]{1,0,2:T(4,128)(2,1)}, u32[]{:S(2)}, u32[]{:S(2)}) collective-permute-start(bf16[4,128,256]{1,0,2:T(4,128)(2,1)S(1)} %copy.38), channel_id=1, source_target_pairs={{0,12},{2,14},{4,0},{6,2},{8,4},{10,6},{12,8},{14,10},{1,13},{3,15... | collective-permute-start | bytes 786440 | tf_op jit(solution)/shard_map/ppermute | solution.py:63
  6.9 1.8 copy.64
  8.7 3.8 %collective-permute-start.24 = (bf16[4,128,256]{2,1,0:T(8,128)(2,1)}, bf16[4,128,256]{2,1,0:T(8,128)(2,1)}, u32[]{:S(2)}, u32[]{:S(2)}) collective-permute-start(bf16[4,128,256]{2,1,0:T(8,128)(2,1)} %bitcast.213), channel_id=1, source_target_pairs={{0,12},{2,14},{4,0},{6,2},{8,4},{10,6},{12,8},{14,10},{1,13},{3,15... | collective-permute-start | bytes 786440 | tf_op jit(solution)/shard_map/ppermute | solution.py:63
  13.4 1.8 constant_dynamic-slice_fusion
  15.2 1.3 dynamic-slice_bitcast_fusion
  22.0 2.0 %copy.55 = bf16[2,4,1,128,256]{3,0,1,4,2:T(2,128)(2,1)} copy(bf16[2,4,1,128,256]{4,3,2,1,0:T(8,128)(2,1)} %get-tuple-element.38) | data formatting | bytes 1048576
  24.0 2.0 %copy.54 = bf16[2,4,1,128,256]{3,0,1,4,2:T(2,128)(2,1)} copy(bf16[2,4,1,128,256]{4,3,2,1,0:T(8,128)(2,1)} %get-tuple-element.37) | data formatting | bytes 1048576
  26.1 3.9 %collective-permute-start.15 = (bf16[128,1024]{1,0:T(8,128)(2,1)}, bf16[128,1024]{1,0:T(8,128)(2,1)S(1)}, u32[]{:S(2)}, u32[]{:S(2)}) collective-permute-start(bf16[128,1024]{1,0:T(8,128)(2,1)} %get-tuple-element.12), channel_id=1, source_target_pairs={{0,12},{2,14},{4,0},{6,2},{8,4},{10,6},{12,8},{14,10},{1,13},{3,15... | collective-permute-start | bytes 786440 | tf_op jit(solution)/shard_map/ppermute | solution.py:63
  31.1 2.1 %collective-permute-start.9 = (bf16[2,128,1024]{2,1,0:T(8,128)(2,1)}, bf16[2,128,1024]{2,1,0:T(8,128)(2,1)S(1)}, u32[]{:S(2)}, u32[]{:S(2)}) collective-permute-start(bf16[2,128,1024]{2,1,0:T(8,128)(2,1)} %get-tuple-element.9), channel_id=1, source_target_pairs={{0,12},{2,14},{4,0},{6,2},{8,4},{10,6},{12,8},{14,10},{1,13},{3,15... | collective-permute-start | bytes 1572872 | tf_op jit(solution)/shard_map/ppermute | solution.py:63
  33.1 1.1 slice.231
  35.2 1.1 bitcast_dynamic-update-slice_fusion.16
  36.3 3.9 %collective-permute-start.3 = (bf16[2,128,256]{1,0,2:T(2,128)(2,1)S(1)}, bf16[2,128,256]{1,0,2:T(2,128)(2,1)S(1)}, u32[]{:S(2)}, u32[]{:S(2)}) collective-permute-start(bf16[2,128,256]{1,0,2:T(2,128)(2,1)S(1)} %slice.231), channel_id=1, source_target_pairs={{0,12},{2,14},{4,0},{6,2},{8,4},{10,6},{12,8},{14,10},{1,13},{3,15... | collective-permute-start | bytes 393224 | tf_op jit(solution)/shard_map/ppermute | solution.py:63
  41.1 1.8 bitcast_dynamic-update-slice_fusion
  42.9 14.0 %collective-permute-done.2 = bf16[2,128,256]{1,0,2:T(2,128)(2,1)S(1)} collective-permute-done((bf16[2,128,256]{1,0,2:T(2,128)(2,1)S(1)}, bf16[2,128,256]{1,0,2:T(2,128)(2,1)S(1)}, u32[]{:S(2)}, u32[]{:S(2)}) %collective-permute-start.2) | collective-permute-done | bytes 131104 | tf_op jit(solution)/shard_map/ppermute | solution.py:63
  56.9 1.4 collective-permute-done.3
  58.3 1.2 collective-permute-start.27
  60.5 1.8 bitcast_dynamic-update-slice_fusion.18
  63.2 1.8 bitcast_dynamic-update-slice_fusion.1
  66.0 2.6 %collective-permute-start.28 = (bf16[2,128,256]{2,1,0:T(8,128)(2,1)S(1)}, bf16[2,128,256]{2,1,0:T(8,128)(2,1)S(1)}, u32[]{:S(2)}, u32[]{:S(2)}) collective-permute-start(bf16[2,128,256]{2,1,0:T(8,128)(2,1)S(1)} %slice.273), channel_id=1, source_target_pairs={{0,12},{2,14},{4,0},{6,2},{8,4},{10,6},{12,8},{14,10},{1,13},{3,15... | collective-permute-start | bytes 393224 | tf_op jit(solution)/shard_map/ppermute | solution.py:63
  68.6 1.8 bitcast_dynamic-update-slice_fusion.19
  71.3 1.1 collective-permute-done.28
  72.4 4.3 %collective-permute-start.16 = (bf16[128,1024]{1,0:T(8,128)(2,1)S(1)}, bf16[128,1024]{1,0:T(8,128)(2,1)S(1)}, u32[]{:S(2)}, u32[]{:S(2)}) collective-permute-start(bf16[128,1024]{1,0:T(8,128)(2,1)S(1)} %collective-permute-done.15), channel_id=1, source_target_pairs={{0,12},{2,14},{4,0},{6,2},{8,4},{10,6},{12,8},{14,10},{1,13},{3,15... | collective-permute-start | bytes 786440 | tf_op jit(solution)/shard_map/ppermute | solution.py:63
  78.2 14.6 %collective-permute-done.14 = bf16[128,1024]{1,0:T(8,128)(2,1)S(1)} collective-permute-done((bf16[128,1024]{1,0:T(8,128)(2,1)S(1)}, bf16[128,1024]{1,0:T(8,128)(2,1)S(1)}, u32[]{:S(2)}, u32[]{:S(2)}) %collective-permute-start.14) | collective-permute-done | bytes 262176 | tf_op jit(solution)/shard_map/ppermute | solution.py:63
  92.8 2.6 %collective-permute-done.16 = bf16[128,1024]{1,0:T(8,128)(2,1)S(1)} collective-permute-done((bf16[128,1024]{1,0:T(8,128)(2,1)S(1)}, bf16[128,1024]{1,0:T(8,128)(2,1)S(1)}, u32[]{:S(2)}, u32[]{:S(2)}) %collective-permute-start.16) | collective-permute-done | bytes 262176 | tf_op jit(solution)/shard_map/ppermute | solution.py:63
  97.6 1.5 convolution_bitcast_fusion
  99.1 1.1 slice_bitcast_fusion.13
  101.9 1.3 fusion.34
  103.3 1.1 collective-permute-done.6
  104.4 2.8 %collective-permute-start.8 = (f32[4,2,2]{0,2,1:T(2,128)S(1)}, f32[4,2,2]{0,2,1:T(2,128)S(1)}, u32[]{:S(2)}, u32[]{:S(2)}) collective-permute-start(f32[4,2,2]{0,2,1:T(2,128)S(1)} %pad_maximum_fusion.6), channel_id=1, source_target_pairs={{0,12},{2,14},{4,0},{6,2},{8,4},{10,6},{12,8},{14,10},{1,13},{3,15... | collective-permute-start | bytes 200 | tf_op jit(solution)/shard_map/ppermute | solution.py:63
  107.2 1.3 collective-permute-done.8
  108.5 1.6 collective-permute-start.12
  110.1 2.9 %collective-permute-done.12 = f32[4,2,2]{0,2,1:T(2,128)S(1)} collective-permute-done((f32[4,2,2]{0,2,1:T(2,128)S(1)}, f32[4,2,2]{0,2,1:T(2,128)S(1)}, u32[]{:S(2)}, u32[]{:S(2)}) %collective-permute-start.12) | collective-permute-done | bytes 96 | tf_op jit(solution)/shard_map/ppermute | solution.py:63
  113.0 1.7 collective-permute-start.19
  114.7 3.9 %collective-permute-done.19 = f32[4,2,2]{0,2,1:T(2,128)S(1)} collective-permute-done((f32[4,2,2]{0,2,1:T(2,128)S(1)}, f32[4,2,2]{0,2,1:T(2,128)S(1)}, u32[]{:S(2)}, u32[]{:S(2)}) %collective-permute-start.19) | collective-permute-done | bytes 96 | tf_op jit(solution)/shard_map/ppermute | solution.py:63
  121.8 1.6 collective-permute-start.18
  127.8 1.6 collective-permute-start.22
  129.4 7.2 %collective-permute-done.18 = bf16[2,128,1024]{2,1,0:T(8,128)(2,1)S(1)} collective-permute-done((bf16[2,128,1024]{2,1,0:T(8,128)(2,1)S(1)}, bf16[2,128,1024]{2,1,0:T(8,128)(2,1)S(1)}, u32[]{:S(2)}, u32[]{:S(2)}) %collective-permute-start.18) | collective-permute-done | bytes 524320 | tf_op jit(solution)/shard_map/ppermute | solution.py:69
  136.9 10.9 %collective-permute-done.11 = bf16[2,128,1024]{2,1,0:T(8,128)(2,1)S(1)} collective-permute-done((bf16[2,128,1024]{2,1,0:T(8,128)(2,1)S(1)}, bf16[2,128,1024]{2,1,0:T(8,128)(2,1)S(1)}, u32[]{:S(2)}, u32[]{:S(2)}) %collective-permute-start.11) | collective-permute-done | bytes 524320 | tf_op jit(solution)/shard_map/ppermute | solution.py:69
  148.1 10.6 %collective-permute-done.22 = bf16[2,128,1024]{2,1,0:T(8,128)(2,1)S(1)} collective-permute-done((bf16[2,128,1024]{2,1,0:T(8,128)(2,1)S(1)}, bf16[2,128,1024]{2,1,0:T(8,128)(2,1)S(1)}, u32[]{:S(2)}, u32[]{:S(2)}) %collective-permute-start.22) | collective-permute-done | bytes 524320 | tf_op jit(solution)/shard_map/ppermute | solution.py:69
  160.2 3.3 %convert_add_fusion = f32[4,128,1024]{2,1,0:T(8,128)S(1)} fusion(f32[128,1024]{1,0:T(8,128)S(1)} %get-tuple-element.36, f32[4]{0:T(128)S(1)} %get-tuple-element.60, f32[128,1024]{1,0:T(8,128)S(1)} %get-tuple-element.35, f32[4]{0:T(128)S(1)} %get-tuple-element.61, f32[128,1024]{1,0:T(8,128)S(1)} %get-tuple-element.71, f32[4]{0:T(128)S(1)} %get-tuple-element.62, ...), kind=kLoop, calls=%fused_computation.7 | loop fusion | flops 28835840 | bytes 10486016 | tf_op jit(solution)/shard_map/add | solution.py:148
  164.5 3.8 %collective-permute-start.32 = (bf16[4,128,256]{2,1,0:T(8,128)(2,1)S(1)}, bf16[4,128,256]{2,1,0:T(8,128)(2,1)S(1)}, u32[]{:S(2)}, u32[]{:S(2)}) collective-permute-start(bf16[4,128,256]{2,1,0:T(8,128)(2,1)S(1)} %get-tuple-element.69), channel_id=1, source_target_pairs={{0,12},{2,14},{4,0},{6,2},{8,4},{10,6},{12,8},{14,10},{1,13},{3,15... | collective-permute-start | bytes 786440 | tf_op jit(solution)/shard_map/ppermute | solution.py:63
  168.3 7.2 %collective-permute-done.34 = bf16[4,128,256]{2,1,0:T(8,128)(2,1)S(1)} collective-permute-done((bf16[4,128,256]{2,1,0:T(8,128)(2,1)S(1)}, bf16[4,128,256]{2,1,0:T(8,128)(2,1)S(1)}, u32[]{:S(2)}, u32[]{:S(2)}) %collective-permute-start.34) | collective-permute-done | bytes 262176 | tf_op jit(solution)/shard_map/ppermute | solution.py:63
  175.6 2.5 %collective-permute-done.32 = bf16[4,128,256]{2,1,0:T(8,128)(2,1)S(1)} collective-permute-done((bf16[4,128,256]{2,1,0:T(8,128)(2,1)S(1)}, bf16[4,128,256]{2,1,0:T(8,128)(2,1)S(1)}, u32[]{:S(2)}, u32[]{:S(2)}) %collective-permute-start.32) | collective-permute-done | bytes 262176 | tf_op jit(solution)/shard_map/ppermute | solution.py:63
  178.1 3.1 %collective-permute-start.36 = (bf16[2,128,256]{2,1,0:T(8,128)(2,1)S(1)}, bf16[2,128,256]{2,1,0:T(8,128)(2,1)S(1)}, u32[]{:S(2)}, u32[]{:S(2)}) collective-permute-start(bf16[2,128,256]{2,1,0:T(8,128)(2,1)S(1)} %slice.275), channel_id=1, source_target_pairs={{0,12},{2,14},{4,0},{6,2},{8,4},{10,6},{12,8},{14,10},{1,13},{3,15... | collective-permute-start | bytes 393224 | tf_op jit(solution)/shard_map/ppermute | solution.py:63
  181.9 2.0 %collective-permute-done.35 = bf16[2,128,256]{2,1,0:T(8,128)(2,1)S(1)} collective-permute-done((bf16[2,128,256]{2,1,0:T(8,128)(2,1)S(1)}, bf16[2,128,256]{2,1,0:T(8,128)(2,1)S(1)}, u32[]{:S(2)}, u32[]{:S(2)}) %collective-permute-start.35) | collective-permute-done | bytes 131104 | tf_op jit(solution)/shard_map/ppermute | solution.py:63
  185.0 1.4 collective-permute-done.37
  188.7 1.1 copy.51
  (138 shorter events, 33.3 us)
Async XLA Ops:
  1.8 29.3 %collective-permute-start = (bf16[4,128,256]{1,0,2:T(4,128)(2,1)S(1)}, bf16[4,128,256]{1,0,2:T(4,128)(2,1)}, u32[]{:S(2)}, u32[]{:S(2)}) collective-permute-start(bf16[4,128,256]{1,0,2:T(4,128)(2,1)S(1)} %copy.38), channel_id=1, source_target_pairs={{0,12},{2,14},{4,0},{6,2},{8,4},{10,6},{12,8},{14,10},{1,13},{3,15... | collective-permute-start | bytes 786440 | tf_op jit(solution)/shard_map/ppermute | solution.py:63
  6.9 19.3 %collective-permute-start.1 = (bf16[4,128,256]{1,0,2:T(4,128)(2,1)S(1)}, bf16[4,128,256]{1,0,2:T(4,128)(2,1)}, u32[]{:S(2)}, u32[]{:S(2)}) collective-permute-start(bf16[4,128,256]{1,0,2:T(4,128)(2,1)S(1)} %copy.38), channel_id=1, source_target_pairs={{0,4},{2,6},{4,8},{6,10},{8,12},{10,14},{12,0},{14,2},{1,5},{3,7},... | collective-permute-start | bytes 786440 | tf_op jit(solution)/shard_map/ppermute | solution.py:63
  8.7 17.3 %collective-permute-start.23 = (bf16[4,128,256]{2,1,0:T(8,128)(2,1)}, bf16[4,128,256]{2,1,0:T(8,128)(2,1)}, u32[]{:S(2)}, u32[]{:S(2)}) collective-permute-start(bf16[4,128,256]{2,1,0:T(8,128)(2,1)} %bitcast.213), channel_id=1, source_target_pairs={{0,2},{2,0},{4,6},{6,4},{8,10},{10,8},{12,14},{14,12},{1,3},{3,1},... | collective-permute-start | bytes 786440 | tf_op jit(solution)/shard_map/ppermute | solution.py:66
  8.7 27.6 %collective-permute-start.24 = (bf16[4,128,256]{2,1,0:T(8,128)(2,1)}, bf16[4,128,256]{2,1,0:T(8,128)(2,1)}, u32[]{:S(2)}, u32[]{:S(2)}) collective-permute-start(bf16[4,128,256]{2,1,0:T(8,128)(2,1)} %bitcast.213), channel_id=1, source_target_pairs={{0,12},{2,14},{4,0},{6,2},{8,4},{10,6},{12,8},{14,10},{1,13},{3,15... | collective-permute-start | bytes 786440 | tf_op jit(solution)/shard_map/ppermute | solution.py:63
  12.5 21.7 %collective-permute-start.26 = (bf16[4,128,256]{2,1,0:T(8,128)(2,1)}, bf16[4,128,256]{2,1,0:T(8,128)(2,1)}, u32[]{:S(2)}, u32[]{:S(2)}) collective-permute-start(bf16[4,128,256]{2,1,0:T(8,128)(2,1)} %bitcast.213), channel_id=1, source_target_pairs={{0,4},{2,6},{4,8},{6,10},{8,12},{10,14},{12,0},{14,2},{1,5},{3,7},... | collective-permute-start | bytes 786440 | tf_op jit(solution)/shard_map/ppermute | solution.py:63
  21.2 4.8 %copy-start = (f32[1,128,4,256]{3,2,1,0:T(4,128)S(1)}, f32[1,128,4,256]{3,2,1,0:T(4,128)}, u32[]{:S(2)}) copy-start(f32[1,128,4,256]{3,2,1,0:T(4,128)} %param.13) | copy-start | bytes 1572868
  26.0 44.4 %collective-permute-start.13 = (bf16[128,1024]{1,0:T(8,128)(2,1)}, bf16[128,1024]{1,0:T(8,128)(2,1)S(1)}, u32[]{:S(2)}, u32[]{:S(2)}) collective-permute-start(bf16[128,1024]{1,0:T(8,128)(2,1)} %get-tuple-element.11), channel_id=1, source_target_pairs={{0,4},{2,6},{4,8},{6,10},{8,12},{10,14},{12,0},{14,2},{1,5},{3,7},... | collective-permute-start | bytes 786440 | tf_op jit(solution)/shard_map/ppermute | solution.py:63
  26.1 44.4 %collective-permute-start.15 = (bf16[128,1024]{1,0:T(8,128)(2,1)}, bf16[128,1024]{1,0:T(8,128)(2,1)S(1)}, u32[]{:S(2)}, u32[]{:S(2)}) collective-permute-start(bf16[128,1024]{1,0:T(8,128)(2,1)} %get-tuple-element.12), channel_id=1, source_target_pairs={{0,12},{2,14},{4,0},{6,2},{8,4},{10,6},{12,8},{14,10},{1,13},{3,15... | collective-permute-start | bytes 786440 | tf_op jit(solution)/shard_map/ppermute | solution.py:63
  31.1 45.6 %collective-permute-start.9 = (bf16[2,128,1024]{2,1,0:T(8,128)(2,1)}, bf16[2,128,1024]{2,1,0:T(8,128)(2,1)S(1)}, u32[]{:S(2)}, u32[]{:S(2)}) collective-permute-start(bf16[2,128,1024]{2,1,0:T(8,128)(2,1)} %get-tuple-element.9), channel_id=1, source_target_pairs={{0,12},{2,14},{4,0},{6,2},{8,4},{10,6},{12,8},{14,10},{1,13},{3,15... | collective-permute-start | bytes 1572872 | tf_op jit(solution)/shard_map/ppermute | solution.py:63
  34.2 22.7 %collective-permute-start.2 = (bf16[2,128,256]{1,0,2:T(2,128)(2,1)S(1)}, bf16[2,128,256]{1,0,2:T(2,128)(2,1)S(1)}, u32[]{:S(2)}, u32[]{:S(2)}) collective-permute-start(bf16[2,128,256]{1,0,2:T(2,128)(2,1)S(1)} %slice.230), channel_id=1, source_target_pairs={{0,4},{2,6},{4,8},{6,10},{8,12},{10,14},{12,0},{14,2},{1,5},{3,7},... | collective-permute-start | bytes 393224 | tf_op jit(solution)/shard_map/ppermute | solution.py:63
  36.3 34.1 %copy-start.10 = (bf16[2,128,1024]{2,1,0:T(8,128)(2,1)S(1)}, bf16[2,128,1024]{2,1,0:T(8,128)(2,1)}, u32[]{:S(2)}) copy-start(bf16[2,128,1024]{2,1,0:T(8,128)(2,1)} %get-tuple-element.10) | copy-start | bytes 1572868
  36.3 22.0 %collective-permute-start.3 = (bf16[2,128,256]{1,0,2:T(2,128)(2,1)S(1)}, bf16[2,128,256]{1,0,2:T(2,128)(2,1)S(1)}, u32[]{:S(2)}, u32[]{:S(2)}) collective-permute-start(bf16[2,128,256]{1,0,2:T(2,128)(2,1)S(1)} %slice.231), channel_id=1, source_target_pairs={{0,12},{2,14},{4,0},{6,2},{8,4},{10,6},{12,8},{14,10},{1,13},{3,15... | collective-permute-start | bytes 393224 | tf_op jit(solution)/shard_map/ppermute | solution.py:63
  41.1 35.6 %copy-start.9 = (bf16[2,4,1,128,256]{3,0,1,4,2:T(2,128)(2,1)S(1)}, bf16[2,4,1,128,256]{3,0,1,4,2:T(2,128)(2,1)}, u32[]{:S(2)}) copy-start(bf16[2,4,1,128,256]{3,0,1,4,2:T(2,128)(2,1)} %copy.55) | copy-start | bytes 1572868
  56.9 20.7 %collective-permute-start.7 = (bf16[2,128,1024]{2,1,0:T(8,128)(2,1)}, bf16[2,128,1024]{2,1,0:T(8,128)(2,1)S(1)}, u32[]{:S(2)}, u32[]{:S(2)}) collective-permute-start(bf16[2,128,1024]{2,1,0:T(8,128)(2,1)} %get-tuple-element.16), channel_id=1, source_target_pairs={{0,2},{2,0},{4,6},{6,4},{8,10},{10,8},{12,14},{14,12},{1,3},{3,1},... | collective-permute-start | bytes 1572872 | tf_op jit(solution)/shard_map/ppermute | solution.py:66
  58.3 7.7 %collective-permute-start.27 = (bf16[2,128,256]{2,1,0:T(8,128)(2,1)S(1)}, bf16[2,128,256]{2,1,0:T(8,128)(2,1)S(1)}, u32[]{:S(2)}, u32[]{:S(2)}) collective-permute-start(bf16[2,128,256]{2,1,0:T(8,128)(2,1)S(1)} %slice.272), channel_id=1, source_target_pairs={{0,4},{2,6},{4,8},{6,10},{8,12},{10,14},{12,0},{14,2},{1,5},{3,7},... | collective-permute-start | bytes 393224 | tf_op jit(solution)/shard_map/ppermute | solution.py:63
  66.0 6.4 %collective-permute-start.28 = (bf16[2,128,256]{2,1,0:T(8,128)(2,1)S(1)}, bf16[2,128,256]{2,1,0:T(8,128)(2,1)S(1)}, u32[]{:S(2)}, u32[]{:S(2)}) collective-permute-start(bf16[2,128,256]{2,1,0:T(8,128)(2,1)S(1)} %slice.273), channel_id=1, source_target_pairs={{0,12},{2,14},{4,0},{6,2},{8,4},{10,6},{12,8},{14,10},{1,13},{3,15... | collective-permute-start | bytes 393224 | tf_op jit(solution)/shard_map/ppermute | solution.py:63
  70.4 25.8 %collective-permute-start.20 = (bf16[2,128,1024]{2,1,0:T(8,128)(2,1)S(1)}, bf16[2,128,1024]{2,1,0:T(8,128)(2,1)S(1)}, u32[]{:S(2)}, u32[]{:S(2)}) collective-permute-start(bf16[2,128,1024]{2,1,0:T(8,128)(2,1)S(1)} %copy-done.10), channel_id=1, source_target_pairs={{0,4},{2,6},{4,8},{6,10},{8,12},{10,14},{12,0},{14,2},{1,5},{3,7},... | collective-permute-start | bytes 1572872 | tf_op jit(solution)/shard_map/ppermute | solution.py:63
  70.5 22.3 %collective-permute-start.14 = (bf16[128,1024]{1,0:T(8,128)(2,1)S(1)}, bf16[128,1024]{1,0:T(8,128)(2,1)S(1)}, u32[]{:S(2)}, u32[]{:S(2)}) collective-permute-start(bf16[128,1024]{1,0:T(8,128)(2,1)S(1)} %collective-permute-done.13), channel_id=1, source_target_pairs={{0,4},{2,6},{4,8},{6,10},{8,12},{10,14},{12,0},{14,2},{1,5},{3,7},... | collective-permute-start | bytes 786440 | tf_op jit(solution)/shard_map/ppermute | solution.py:63
  72.4 23.0 %collective-permute-start.16 = (bf16[128,1024]{1,0:T(8,128)(2,1)S(1)}, bf16[128,1024]{1,0:T(8,128)(2,1)S(1)}, u32[]{:S(2)}, u32[]{:S(2)}) collective-permute-start(bf16[128,1024]{1,0:T(8,128)(2,1)S(1)} %collective-permute-done.15), channel_id=1, source_target_pairs={{0,12},{2,14},{4,0},{6,2},{8,4},{10,6},{12,8},{14,10},{1,13},{3,15... | collective-permute-start | bytes 786440 | tf_op jit(solution)/shard_map/ppermute | solution.py:63
  76.7 20.9 %collective-permute-start.4 = (bf16[2,4,128,256]{2,0,1,3:T(2,128)(2,1)S(1)}, bf16[2,4,128,256]{2,0,1,3:T(2,128)(2,1)S(1)}, u32[]{:S(2)}, u32[]{:S(2)}) collective-permute-start(bf16[2,4,128,256]{2,0,1,3:T(2,128)(2,1)S(1)} %bitcast.222), channel_id=1, source_target_pairs={{0,2},{2,0},{4,6},{6,4},{8,10},{10,8},{12,14},{14,12},{1,3},{3,1},... | collective-permute-start | bytes 1572872 | tf_op jit(solution)/shard_map/ppermute | solution.py:66
  77.6 20.0 %copy-start.11 = (bf16[4,8,128,256]{2,0,1,3:T(4,128)(2,1)S(1)}, bf16[4,8,128,256]{2,0,1,3:T(4,128)(2,1)}, u32[]{:S(2)}) copy-start(bf16[4,8,128,256]{2,0,1,3:T(4,128)(2,1)} %bitcast_dynamic-update-slice_fusion.19) | copy-start | bytes 6291460
  77.6 22.6 %collective-permute-start.25 = (bf16[4,128,256]{2,1,0:T(8,128)(2,1)}, bf16[4,128,256]{2,1,0:T(8,128)(2,1)S(1)}, u32[]{:S(2)}, u32[]{:S(2)}) collective-permute-start(bf16[4,128,256]{2,1,0:T(8,128)(2,1)} %collective-permute-done.24), channel_id=1, source_target_pairs={{0,2},{2,0},{4,6},{6,4},{8,10},{10,8},{12,14},{14,12},{1,3},{3,1},... | collective-permute-start | bytes 786440 | tf_op jit(solution)/shard_map/ppermute | solution.py:66
  92.8 26.9 %collective-permute-start.30 = (bf16[4,128,256]{2,1,0:T(8,128)(2,1)}, bf16[4,128,256]{2,1,0:T(8,128)(2,1)}, u32[]{:S(2)}, u32[]{:S(2)}) collective-permute-start(bf16[4,128,256]{2,1,0:T(8,128)(2,1)} %collective-permute-done.26), channel_id=1, source_target_pairs={{0,2},{2,0},{4,6},{6,4},{8,10},{10,8},{12,14},{14,12},{1,3},{3,1},... | collective-permute-start | bytes 786440 | tf_op jit(solution)/shard_map/ppermute | solution.py:66
  95.4 23.2 %collective-permute-start.29 = (bf16[4,128,256]{2,1,0:T(8,128)(2,1)S(1)}, bf16[4,128,256]{2,1,0:T(8,128)(2,1)}, u32[]{:S(2)}, u32[]{:S(2)}) collective-permute-start(bf16[4,128,256]{2,1,0:T(8,128)(2,1)S(1)} %constant_dynamic-update-slice_fusion), channel_id=1, source_target_pairs={{0,2},{2,0},{4,6},{6,4},{8,10},{10,8},{12,14},{14,12},{1,3},{3,1},... | collective-permute-start | bytes 786440 | tf_op jit(solution)/shard_map/ppermute | solution.py:66
  96.2 24.5 %collective-permute-start.17 = (bf16[128,1024]{1,0:T(8,128)(2,1)}, bf16[128,1024]{1,0:T(8,128)(2,1)}, u32[]{:S(2)}, u32[]{:S(2)}) collective-permute-start(bf16[128,1024]{1,0:T(8,128)(2,1)} %get-tuple-element.46), channel_id=1, source_target_pairs={{0,2},{2,0},{4,6},{6,4},{8,10},{10,8},{12,14},{14,12},{1,3},{3,1},... | collective-permute-start | bytes 786440 | tf_op jit(solution)/shard_map/ppermute | solution.py:66
  97.6 27.7 %collective-permute-start.10 = (bf16[128,1024]{1,0:T(8,128)(2,1)}, bf16[128,1024]{1,0:T(8,128)(2,1)}, u32[]{:S(2)}, u32[]{:S(2)}) collective-permute-start(bf16[128,1024]{1,0:T(8,128)(2,1)} %get-tuple-element.42), channel_id=1, source_target_pairs={{0,2},{2,0},{4,6},{6,4},{8,10},{10,8},{12,14},{14,12},{1,3},{3,1},... | collective-permute-start | bytes 786440 | tf_op jit(solution)/shard_map/ppermute | solution.py:66
  99.1 2.7 %copy-start.8 = (bf16[2,4,1,128,256]{3,0,1,4,2:T(2,128)(2,1)S(1)}, bf16[2,4,1,128,256]{3,0,1,4,2:T(2,128)(2,1)}, u32[]{:S(2)}) copy-start(bf16[2,4,1,128,256]{3,0,1,4,2:T(2,128)(2,1)} %copy.54) | copy-start | bytes 1572868
  99.1 2.7 %copy-start.12 = (f32[4,2]{0,1:T(2,128)S(1)}, f32[4,2]{0,1:T(2,128)}, u32[]{:S(2)}) copy-start(f32[4,2]{0,1:T(2,128)} %param.12) | copy-start | bytes 100
  99.1 2.8 %copy-start.13 = (f32[2]{0:T(128)S(1)}, f32[2]{0:T(128)}, u32[]{:S(2)}) copy-start(f32[2]{0:T(128)} %param.11) | copy-start | bytes 28
  100.2 1.6 collective-permute-start.5
  103.2 17.6 %copy-start.7 = (bf16[1,128,1024]{2,1,0:T(8,128)(2,1)S(1)}, bf16[1,128,1024]{2,1,0:T(8,128)(2,1)}, u32[]{:S(2)}) copy-start(bf16[1,128,1024]{2,1,0:T(8,128)(2,1)} %get-tuple-element.45) | copy-start | bytes 786436
  103.2 1.2 collective-permute-start.6
  104.4 4.1 %collective-permute-start.8 = (f32[4,2,2]{0,2,1:T(2,128)S(1)}, f32[4,2,2]{0,2,1:T(2,128)S(1)}, u32[]{:S(2)}, u32[]{:S(2)}) collective-permute-start(f32[4,2,2]{0,2,1:T(2,128)S(1)} %pad_maximum_fusion.6), channel_id=1, source_target_pairs={{0,12},{2,14},{4,0},{6,2},{8,4},{10,6},{12,8},{14,10},{1,13},{3,15... | collective-permute-start | bytes 200 | tf_op jit(solution)/shard_map/ppermute | solution.py:63
  108.5 4.5 %collective-permute-start.12 = (f32[4,2,2]{0,2,1:T(2,128)S(1)}, f32[4,2,2]{0,2,1:T(2,128)S(1)}, u32[]{:S(2)}, u32[]{:S(2)}) collective-permute-start(f32[4,2,2]{0,2,1:T(2,128)S(1)} %pad_maximum_fusion.6), channel_id=1, source_target_pairs={{0,8},{2,10},{4,12},{6,14},{8,0},{10,2},{12,4},{14,6},{1,9},{3,11}... | collective-permute-start | bytes 200 | tf_op jit(solution)/shard_map/ppermute | solution.py:63
  113.0 5.6 %collective-permute-start.19 = (f32[4,2,2]{0,2,1:T(2,128)S(1)}, f32[4,2,2]{0,2,1:T(2,128)S(1)}, u32[]{:S(2)}, u32[]{:S(2)}) collective-permute-start(f32[4,2,2]{0,2,1:T(2,128)S(1)} %pad_maximum_fusion.6), channel_id=1, source_target_pairs={{0,4},{2,6},{4,8},{6,10},{8,12},{10,14},{12,0},{14,2},{1,5},{3,7},... | collective-permute-start | bytes 200 | tf_op jit(solution)/shard_map/ppermute | solution.py:63
  118.6 9.1 %collective-permute-start.21 = (bf16[128,1024]{1,0:T(8,128)(2,1)}, bf16[128,1024]{1,0:T(8,128)(2,1)S(1)}, u32[]{:S(2)}, u32[]{:S(2)}) collective-permute-start(bf16[128,1024]{1,0:T(8,128)(2,1)} %get-tuple-element.50), channel_id=1, source_target_pairs={{0,2},{2,0},{4,6},{6,4},{8,10},{10,8},{12,14},{14,12},{1,3},{3,1},... | collective-permute-start | bytes 786440 | tf_op jit(solution)/shard_map/ppermute | solution.py:66
  121.8 14.8 %collective-permute-start.18 = (bf16[2,128,1024]{2,1,0:T(8,128)(2,1)S(1)}, bf16[2,128,1024]{2,1,0:T(8,128)(2,1)S(1)}, u32[]{:S(2)}, u32[]{:S(2)}) collective-permute-start(bf16[2,128,1024]{2,1,0:T(8,128)(2,1)S(1)} %get-tuple-element.44), channel_id=1, source_target_pairs={{0,1},{1,0},{2,3},{3,2},{4,5},{5,4},{6,7},{7,6},{8,9},{9,8},{10,11... | collective-permute-start | bytes 1572872 | tf_op jit(solution)/shard_map/ppermute | solution.py:69
  125.2 2.6 %copy-start.6 = (bf16[1,128,1024]{2,1,0:T(8,128)(2,1)S(1)}, bf16[1,128,1024]{2,1,0:T(8,128)(2,1)}, u32[]{:S(2)}) copy-start(bf16[1,128,1024]{2,1,0:T(8,128)(2,1)} %get-tuple-element.49) | copy-start | bytes 786436
  127.1 20.7 %collective-permute-start.11 = (bf16[2,128,1024]{2,1,0:T(8,128)(2,1)S(1)}, bf16[2,128,1024]{2,1,0:T(8,128)(2,1)S(1)}, u32[]{:S(2)}, u32[]{:S(2)}) collective-permute-start(bf16[2,128,1024]{2,1,0:T(8,128)(2,1)S(1)} %get-tuple-element.40), channel_id=1, source_target_pairs={{0,1},{1,0},{2,3},{3,2},{4,5},{5,4},{6,7},{7,6},{8,9},{9,8},{10,11... | collective-permute-start | bytes 1572872 | tf_op jit(solution)/shard_map/ppermute | solution.py:69
  127.8 30.9 %collective-permute-start.22 = (bf16[2,128,1024]{2,1,0:T(8,128)(2,1)S(1)}, bf16[2,128,1024]{2,1,0:T(8,128)(2,1)S(1)}, u32[]{:S(2)}, u32[]{:S(2)}) collective-permute-start(bf16[2,128,1024]{2,1,0:T(8,128)(2,1)S(1)} %get-tuple-element.48), channel_id=1, source_target_pairs={{0,1},{1,0},{2,3},{3,2},{4,5},{5,4},{6,7},{7,6},{8,9},{9,8},{10,11... | collective-permute-start | bytes 1572872 | tf_op jit(solution)/shard_map/ppermute | solution.py:69
  164.4 11.1 %collective-permute-start.34 = (bf16[4,128,256]{2,1,0:T(8,128)(2,1)S(1)}, bf16[4,128,256]{2,1,0:T(8,128)(2,1)S(1)}, u32[]{:S(2)}, u32[]{:S(2)}) collective-permute-start(bf16[4,128,256]{2,1,0:T(8,128)(2,1)S(1)} %get-tuple-element.69), channel_id=1, source_target_pairs={{0,4},{2,6},{4,8},{6,10},{8,12},{10,14},{12,0},{14,2},{1,5},{3,7},... | collective-permute-start | bytes 786440 | tf_op jit(solution)/shard_map/ppermute | solution.py:63
  164.5 13.6 %collective-permute-start.32 = (bf16[4,128,256]{2,1,0:T(8,128)(2,1)S(1)}, bf16[4,128,256]{2,1,0:T(8,128)(2,1)S(1)}, u32[]{:S(2)}, u32[]{:S(2)}) collective-permute-start(bf16[4,128,256]{2,1,0:T(8,128)(2,1)S(1)} %get-tuple-element.69), channel_id=1, source_target_pairs={{0,12},{2,14},{4,0},{6,2},{8,4},{10,6},{12,8},{14,10},{1,13},{3,15... | collective-permute-start | bytes 786440 | tf_op jit(solution)/shard_map/ppermute | solution.py:63
  168.3 13.4 %collective-permute-start.31 = (bf16[4,128,256]{2,1,0:T(8,128)(2,1)S(1)}, bf16[4,128,256]{2,1,0:T(8,128)(2,1)S(1)}, u32[]{:S(2)}, u32[]{:S(2)}) collective-permute-start(bf16[4,128,256]{2,1,0:T(8,128)(2,1)S(1)} %get-tuple-element.69), channel_id=1, source_target_pairs={{0,2},{2,0},{4,6},{6,4},{8,10},{10,8},{12,14},{14,12},{1,3},{3,1},... | collective-permute-start | bytes 786440 | tf_op jit(solution)/shard_map/ppermute | solution.py:66
  175.5 8.4 %collective-permute-start.35 = (bf16[2,128,256]{2,1,0:T(8,128)(2,1)S(1)}, bf16[2,128,256]{2,1,0:T(8,128)(2,1)S(1)}, u32[]{:S(2)}, u32[]{:S(2)}) collective-permute-start(bf16[2,128,256]{2,1,0:T(8,128)(2,1)S(1)} %slice.274), channel_id=1, source_target_pairs={{0,4},{2,6},{4,8},{6,10},{8,12},{10,14},{12,0},{14,2},{1,5},{3,7},... | collective-permute-start | bytes 393224 | tf_op jit(solution)/shard_map/ppermute | solution.py:63
  178.1 6.6 %collective-permute-start.36 = (bf16[2,128,256]{2,1,0:T(8,128)(2,1)S(1)}, bf16[2,128,256]{2,1,0:T(8,128)(2,1)S(1)}, u32[]{:S(2)}, u32[]{:S(2)}) collective-permute-start(bf16[2,128,256]{2,1,0:T(8,128)(2,1)S(1)} %slice.275), channel_id=1, source_target_pairs={{0,12},{2,14},{4,0},{6,2},{8,4},{10,6},{12,8},{14,10},{1,13},{3,15... | collective-permute-start | bytes 393224 | tf_op jit(solution)/shard_map/ppermute | solution.py:63
  181.3 3.6 %collective-permute-start.33 = (bf16[4,128,256]{2,1,0:T(8,128)(2,1)S(1)}, bf16[4,128,256]{2,1,0:T(8,128)(2,1)S(1)}, u32[]{:S(2)}, u32[]{:S(2)}) collective-permute-start(bf16[4,128,256]{2,1,0:T(8,128)(2,1)S(1)} %collective-permute-done.32), channel_id=1, source_target_pairs={{0,2},{2,0},{4,6},{6,4},{8,10},{10,8},{12,14},{14,12},{1,3},{3,1},... | collective-permute-start | bytes 786440 | tf_op jit(solution)/shard_map/ppermute | solution.py:66
  181.3 5.2 %collective-permute-start.38 = (bf16[4,128,256]{2,1,0:T(8,128)(2,1)S(1)}, bf16[4,128,256]{2,1,0:T(8,128)(2,1)S(1)}, u32[]{:S(2)}, u32[]{:S(2)}) collective-permute-start(bf16[4,128,256]{2,1,0:T(8,128)(2,1)S(1)} %collective-permute-done.34), channel_id=1, source_target_pairs={{0,2},{2,0},{4,6},{6,4},{8,10},{10,8},{12,14},{14,12},{1,3},{3,1},... | collective-permute-start | bytes 786440 | tf_op jit(solution)/shard_map/ppermute | solution.py:66
  184.8 1.6 collective-permute-start.37
  (5 other events, 6.1 us)

commit v2 on v0

--- a/solution.py
+++ b/solution.py
@@ -1,12 +1,16 @@
+import functools
+
 import jax
 import jax.numpy as jnp
 from jax import lax
+from jax.experimental import pallas as pl
+from jax.experimental.pallas import tpu as pltpu
 from jax.sharding import PartitionSpec as P
 
 time_root = 0.1
 
 
-def per_device(green_blocks, half_chol, full_chol, meanfield, noise_draws, orbitals):
+def general_device(green_blocks, half_chol, full_chol, meanfield, noise_draws, orbitals):
     walkers_here = green_blocks.shape[0]
     chol_here = half_chol.shape[0]
     half_rows = full_chol.shape[1]
@@ -31,8 +35,7 @@
 
     def apply_operator(vector):
         both_halves = lax.all_gather(vector, "orb", axis=0, tiled=True)
-        fold_start = jnp.zeros((walkers_here, half_rows, occupied), jnp.float32)
-        running = fold_start
+        running = jnp.zeros((walkers_here, half_rows, occupied), jnp.float32)
         shard_piece = lax.all_gather(both_halves, "chol", axis=1, tiled=True)
         row_count = shard_piece.shape[1]
         for half_index in range(shard_piece.shape[0]):
@@ -56,6 +59,410 @@
     return (walkers_next, bias_shift)
 
 
+vmem_spec = pl.BlockSpec(memory_space=pltpu.VMEM)
+any_spec = pl.BlockSpec(memory_space=pl.ANY)
+wide = jnp.float32
+narrow = jnp.bfloat16
+
+
+def after(value, *others):
+    return lax.optimization_barrier((value, *others))[0]
+
+
+def place(chips):
+    slot = lax.axis_index("chol")
+    return slot // 2, slot % 2, lax.axis_index("walk")
+
+
+def cut_kernel(chips, rows, wanted, full_ref, *refs):
+    z, k, x = place(chips)
+    outs, sem = refs[:-1], refs[-1]
+    copies = []
+    for index, (step, crossed, both) in enumerate(wanted):
+        core = 1 - k if crossed else k
+        start = pl.multiple_of((2 * lax.rem(z + step + chips, chips) + core) * rows, rows)
+        picked = pl.ds(start, rows)
+        source = full_ref.at[:, picked, :] if both else full_ref.at[x, picked, :]
+        copies.append(pltpu.make_async_copy(source, outs[index], sem.at[index]))
+        copies[-1].start()
+    for copy in copies:
+        copy.wait()
+
+
+def cut(chips, rows, full_chol, wanted):
+    order = full_chol.shape[2]
+    shapes = [
+        jax.ShapeDtypeStruct((2, rows, order) if both else (rows, order), narrow)
+        for _, _, both in wanted
+    ]
+    return pl.pallas_call(
+        functools.partial(cut_kernel, chips, rows, wanted),
+        out_shape=shapes,
+        in_specs=[any_spec],
+        out_specs=[vmem_spec] * len(wanted),
+        scratch_shapes=[pltpu.SemaphoreType.DMA((len(wanted),))],
+        name="cut_rows",
+    )(full_chol)
+
+
+def start_kernel(orbitals_ref, out_ref):
+    for walker in range(out_ref.shape[0]):
+        out_ref[walker] = orbitals_ref[0, :, walker, :].astype(narrow)
+
+
+def walker_major(orbitals):
+    _, rows, walkers, occupied = orbitals.shape
+    return pl.pallas_call(
+        start_kernel,
+        out_shape=jax.ShapeDtypeStruct((walkers, rows, occupied), narrow),
+        in_specs=[vmem_spec],
+        out_specs=vmem_spec,
+        name="walker_major",
+    )(orbitals)
+
+
+def bias_kernel(chips, here_ref, above_ref, low_ref, high_ref, below_ref, mine_ref, theirs_ref, out_ref):
+    z, k, _ = place(chips)
+    walkers, rows, occupied = here_ref.shape
+    vectors = mine_ref.shape[0]
+    half = walkers // 2
+    step_rows = 16
+    totals = [jnp.zeros((8, 128), wide) for _ in range(2 * vectors * walkers)]
+    for step, green in ((0, here_ref), (1, above_ref), (2, None), (-1, below_ref)):
+        base = (2 * lax.rem(z + step + chips, chips) + k) * rows
+
+        def add(index, totals, base=base, green=green):
+            here = pl.multiple_of(index * step_rows, step_rows)
+            there = pl.multiple_of(base + index * step_rows, step_rows)
+            picked = pl.ds(here, step_rows)
+            if green is None:
+                greens = [low_ref[w, picked, :] for w in range(half)]
+                greens += [high_ref[w, picked, :] for w in range(half)]
+            else:
+                greens = [green[w, picked, :] for w in range(walkers)]
+            greens = [g.astype(wide) for g in greens]
+            totals = list(totals)
+            for c in range(2 * vectors):
+                chol_ref = mine_ref if c < vectors else theirs_ref
+                chol = chol_ref[c % vectors, pl.ds(there, step_rows), :].astype(wide)
+                for w in range(walkers):
+                    product = greens[w] * chol
+                    tiles = [
+                        product[r : r + 8, n : n + 128]
+                        for r in range(0, step_rows, 8)
+                        for n in range(0, occupied, 128)
+                    ]
+                    totals[c * walkers + w] = totals[c * walkers + w] + sum(tiles[1:], tiles[0])
+            return tuple(totals)
+
+        totals = lax.fori_loop(0, rows // step_rows, add, tuple(totals))
+    for index, total in enumerate(totals):
+        value = jnp.sum(jnp.sum(total, axis=0, keepdims=True), axis=1, keepdims=True)
+        out_ref[pl.ds(index, 1), :] = jnp.broadcast_to(value, (1, 128))
+
+
+def chip_bias(chips, here, above, low, high, below, mine, theirs):
+    entries = 2 * mine.shape[0] * here.shape[0]
+    return pl.pallas_call(
+        functools.partial(bias_kernel, chips),
+        out_shape=jax.ShapeDtypeStruct((entries, 128), wide),
+        in_specs=[vmem_spec] * 7,
+        out_specs=vmem_spec,
+        name="chip_bias",
+    )(here, above, low, high, below, mine, theirs)
+
+
+def field_kernel(mine_ref, theirs_ref, noise_ref, noise_there_ref, shift_ref, field_ref):
+    half = mine_ref.shape[0] // 2
+    low, high = pl.ds(0, half), pl.ds(half, half)
+    for rows, other, consts in ((low, high, noise_ref), (high, low, noise_there_ref)):
+        force = mine_ref[rows, :] + theirs_ref[other, :]
+        shift = jnp.clip(time_root * (force - consts[high, :]), -1.0, 1.0)
+        field_ref[rows, :] = consts[low, :] - shift
+        if rows is low:
+            shift_ref[...] = shift
+
+
+def chip_field(mine, theirs, noise, noise_there):
+    entries = mine.shape[0]
+    return pl.pallas_call(
+        field_kernel,
+        out_shape=[
+            jax.ShapeDtypeStruct((entries // 2, 128), wide),
+            jax.ShapeDtypeStruct((entries, 128), wide),
+        ],
+        in_specs=[vmem_spec] * 4,
+        out_specs=[vmem_spec] * 2,
+        name="chip_field",
+    )(mine, theirs, noise, noise_there)
+
+
+def build_operator(x, walkers, sources, summed_ref, summed_in_ref, emit):
+    rows, order = summed_ref.shape[1:]
+    high, across = 16, 256
+    columns = order // across
+
+    def tile(index, carry):
+        row = pl.multiple_of((index // columns) * high, high)
+        column = pl.multiple_of((index % columns) * across, across)
+        picked = (pl.ds(row, high), pl.ds(column, across))
+        sums = [None if summed_in_ref is None else summed_in_ref[(w, *picked)] for w in range(walkers)]
+        for field_ref, first, near, other in sources:
+            one = near(picked).astype(wide)
+            two = other(picked).astype(wide)
+            for w in range(walkers):
+                scale_one = field_ref[pl.ds(first + x * walkers + w, 1), :]
+                scale_two = field_ref[pl.ds(first + (1 - x) * walkers + w, 1), :]
+                scale_one = jnp.concatenate([scale_one] * (across // 128), 1)
+                scale_two = jnp.concatenate([scale_two] * (across // 128), 1)
+                block = time_root * (scale_one * one + scale_two * two)
+                block = block.astype(narrow).astype(wide)
+                sums[w] = block if sums[w] is None else sums[w] + block
+        for w in range(walkers):
+            emit(w, picked, sums[w])
+        return carry
+
+    lax.fori_loop(0, (rows // high) * columns, tile, 0)
+
+
+def plain(ref):
+    return lambda picked: ref[picked]
+
+
+def pair_sources(x, field_ref, walkers, near_own, other_own, near_theirs, other_theirs):
+    vectors = 2
+    return [
+        (field_ref, 0, plain(near_own), plain(other_own)),
+        (field_ref, vectors * walkers, plain(near_theirs), plain(other_theirs)),
+    ]
+
+
+def early_kernel(chips, walkers, field_here, field_above, field_below, own_ref, own_theirs, *refs):
+    _, _, x = place(chips)
+    blocks, summed_ref = refs[:-1], refs[-1]
+    sources = []
+    for ref, first in ((own_ref, 0), (own_theirs, 2 * walkers)):
+        sources.append(
+            (
+                field_here,
+                first,
+                lambda picked, ref=ref: ref[(x, *picked)],
+                lambda picked, ref=ref: ref[(1 - x, *picked)],
+            )
+        )
+    sources += pair_sources(x, field_above, walkers, *blocks[:4])
+    sources += pair_sources(x, field_below, walkers, *blocks[4:])
+
+    def emit(w, picked, value):
+        summed_ref[(w, *picked)] = value
+
+    build_operator(x, walkers, sources, summed_ref, None, emit)
+
+
+def early_operator(chips, walkers, fields, own, own_theirs, blocks):
+    rows, order = blocks[0].shape
+    return pl.pallas_call(
+        functools.partial(early_kernel, chips, walkers),
+        out_shape=jax.ShapeDtypeStruct((walkers, rows, order), wide),
+        in_specs=[vmem_spec] * (5 + len(blocks)),
+        out_specs=vmem_spec,
+        compiler_params=pltpu.CompilerParams(vmem_limit_bytes=24 << 20),
+        name="early_operator",
+    )(*fields, own, own_theirs, *blocks)
+
+
+def collect(chips, vector_ref, pieces):
+    z, k, _ = place(chips)
+    for step, crossed, first, ref in pieces:
+        count, rows, _ = ref.shape
+        core = 1 - k if crossed else k
+        start = pl.multiple_of((2 * lax.rem(z + step + chips, chips) + core) * rows, rows)
+        for w in range(count):
+            vector_ref[first + w, pl.ds(start, rows), :] = ref[w]
+
+
+def vector_pieces(refs):
+    here, above, low, high, below, here_t, above_t, low_t, high_t, below_t = refs
+    half = low.shape[0]
+    return [
+        (0, False, 0, here),
+        (1, False, 0, above),
+        (2, False, 0, low),
+        (2, False, half, high),
+        (-1, False, 0, below),
+        (0, True, 0, here_t),
+        (1, True, 0, above_t),
+        (2, True, 0, low_t),
+        (2, True, half, high_t),
+        (-1, True, 0, below_t),
+    ]
+
+
+def first_kernel(chips, walkers, summed_in, field_far, *refs):
+    blocks, refs = refs[:4], refs[4:]
+    pieces, refs = refs[:10], refs[10:]
+    operator_ref, first_ref, narrow_ref, vector_ref = refs
+    rows = summed_in.shape[1]
+    _, _, x = place(chips)
+    collect(chips, vector_ref, vector_pieces(pieces))
+
+    def emit(w, picked, value):
+        row, column = picked
+        top = value.astype(narrow)
+        operator_ref[w, row, column] = top
+        rest = (value - top.astype(wide)).astype(narrow)
+        operator_ref[w, pl.ds(rows + row.start, row.size), column] = rest
+
+    build_operator(
+        x, walkers, pair_sources(x, field_far, walkers, *blocks), summed_in, summed_in, emit
+    )
+    for w in range(walkers):
+        both = jnp.dot(operator_ref[w], vector_ref[w], preferred_element_type=wide)
+        term = both[:rows] + both[rows:]
+        first_ref[w] = term
+        narrow_ref[w] = term.astype(narrow)
+
+
+def first_application(chips, summed, field_far, blocks, pieces):
+    walkers, rows, order = summed.shape
+    occupied = pieces[0].shape[2]
+    return pl.pallas_call(
+        functools.partial(first_kernel, chips, walkers),
+        out_shape=[
+            jax.ShapeDtypeStruct((walkers, 2 * rows, order), narrow),
+            jax.ShapeDtypeStruct((walkers, rows, occupied), wide),
+            jax.ShapeDtypeStruct((walkers, rows, occupied), narrow),
+        ],
+        in_specs=[vmem_spec] * 16,
+        out_specs=[vmem_spec] * 3,
+        scratch_shapes=[pltpu.VMEM((walkers, order, occupied), narrow)],
+        compiler_params=pltpu.CompilerParams(vmem_limit_bytes=24 << 20),
+        name="first_application",
+    )(summed, field_far, *blocks, *pieces)
+
+
+def second_kernel(chips, operator_ref, first_ref, orbitals_ref, *refs):
+    pieces, (out_ref, vector_ref) = refs[:10], refs[10:]
+    walkers, rows, _ = first_ref.shape
+    collect(chips, vector_ref, vector_pieces(pieces))
+    for w in range(walkers):
+        both = jnp.dot(operator_ref[w], vector_ref[w], preferred_element_type=wide)
+        second = both[:rows] + both[rows:]
+        out_ref[0, :, w, :] = orbitals_ref[0, :, w, :] + first_ref[w] + 0.5 * second
+
+
+def second_application(chips, operator, first_term, orbitals, pieces):
+    walkers, _, order = operator.shape
+    occupied = orbitals.shape[3]
+    return pl.pallas_call(
+        functools.partial(second_kernel, chips),
+        out_shape=jax.ShapeDtypeStruct(orbitals.shape, wide),
+        in_specs=[vmem_spec] * 13,
+        out_specs=vmem_spec,
+        scratch_shapes=[pltpu.VMEM((walkers, order, occupied), narrow)],
+        compiler_params=pltpu.CompilerParams(vmem_limit_bytes=24 << 20),
+        name="second_application",
+    )(operator, first_term, orbitals, *pieces)
+
+
+def row_device(chips):
+    devices = 2 * chips
+
+    def ring(value, step):
+        pairs = [(i, (i + 2 * step) % devices) for i in range(devices)]
+        return lax.ppermute(value, "chol", pairs)
+
+    def core(value):
+        return lax.ppermute(value, "chol", [(i, i ^ 1) for i in range(devices)])
+
+    def across(value):
+        return lax.ppermute(value, "walk", [(0, 1), (1, 0)])
+
+    def gather_ring(value):
+        half = value.shape[0] // 2
+        below, above = ring(value, 1), ring(value, -1)
+        low, high = ring(below[:half], 1), ring(above[half:], -1)
+        return [value, above, low, high, below]
+
+    def device(green_blocks, half_chol, full_chol, meanfield, noise_draws, orbitals):
+        walkers, rows, _ = green_blocks.shape
+        vectors = half_chol.shape[0]
+        slot = lax.axis_index("chol")
+
+        half_theirs = core(half_chol)
+        cross_up, cross_down = cut(chips, rows, full_chol, ((1, True, False), (-1, True, False)))
+        straight_up, straight_down, far_up, far_down, own_cross = cut(
+            chips,
+            rows,
+            after(full_chol, cross_up),
+            (
+                (1, False, False),
+                (-1, False, False),
+                (2, False, False),
+                (2, True, False),
+                (0, True, True),
+            ),
+        )
+        start = walker_major(orbitals)
+        constants = jnp.concatenate(
+            [noise_draws.T.reshape(-1), jnp.repeat(meanfield, walkers)]
+        )
+        constants = jnp.broadcast_to(constants[:, None], (2 * vectors * walkers, 128))
+        constants_there = core(constants)
+        cross_below, cross_above = ring(cross_up, 1), ring(cross_down, -1)
+        own_theirs = core(own_cross)
+        below, above = ring(straight_up, 1), ring(straight_down, -1)
+        green = after(green_blocks, cross_below, cross_above)
+        green_pieces = gather_ring(green)
+        far_up, far_down = after((far_up, far_down), below, above)
+        far_half, far_half_cross = ring(far_up, 1), ring(far_down, -1)
+        start = after(start, far_half, far_half_cross)
+        start_pieces = gather_ring(start)
+        far, far_cross = ring(far_half, 1), ring(far_half_cross, -1)
+
+        above_theirs, below_theirs = core(cross_above), core(cross_below)
+        above_theirs_x, below_theirs_x = across(above_theirs), across(below_theirs)
+        above_x, below_x = across(above), across(below)
+        far_theirs = core(far_cross)
+        far_x, far_theirs_x = across(far), across(far_theirs)
+
+        bias = chip_bias(chips, *green_pieces, half_chol, half_theirs)
+        shift_rows, field = chip_field(bias, core(bias), constants, constants_there)
+        field_above, field_below, field_far = ring(field, -1), ring(field, 1), ring(field, 2)
+        bias_shift = shift_rows[:, 0].reshape(vectors, walkers).T
+
+        own = lax.dynamic_slice_in_dim(full_chol, slot * rows, rows, 1)
+        summed = early_operator(
+            chips,
+            walkers,
+            (field, field_above, field_below),
+            own,
+            own_theirs,
+            (
+                *(above, above_x, above_theirs, above_theirs_x),
+                *(below, below_x, below_theirs, below_theirs_x),
+            ),
+        )
+        operator, first_term, first_narrow = first_application(
+            chips,
+            summed,
+            field_far,
+            (far, far_x, far_theirs, far_theirs_x),
+            [*start_pieces, *[core(piece) for piece in start_pieces]],
+        )
+        first_pieces = gather_ring(first_narrow)
+        walkers_next = second_application(
+            chips,
+            operator,
+            first_term,
+            orbitals,
+            [*first_pieces, *[core(piece) for piece in first_pieces]],
+        )
+        return (walkers_next, bias_shift)
+
+    return device
+
+
 def solution(mesh):
     placed = (
         P(("grp", "walk"), "chol", "orb"),
@@ -65,6 +472,11 @@
         P(("grp", "walk"), "chol"),
         P("orb", "chol", ("grp", "walk"), None),
     )
+    sizes = mesh.shape
+    if sizes["orb"] == 1 and sizes["walk"] == 2 and sizes["chol"] == 8:
+        per_device = row_device(sizes["chol"] // 2)
+    else:
+        per_device = general_device
     return jax.shard_map(
         per_device,
         mesh=mesh,

time: 321 us -> 152 us (0.47)
  waiting for transfers between devices: 270 us -> 70.3 us
  starting transfers between devices: 0.21 us -> 50.6 us
  Pallas kernels: 0 us -> 22.7 us
  matrix products: 19.2 us -> 0 us
  between operations: 13.8 us -> 0.92 us
  other arithmetic: 7.99 us -> 0.08 us
    psum x2 -> x0, waiting for transfers between devices: 192 us -> none  [apply_operator(): summed = lax.psum(running, 'chol')]
    all_gather x3 -> x0, waiting for transfers between devices: 77.7 us -> none  [the longest x2 54.2 us: apply_operator(): shard_piece = lax.all_gather(both_halves, 'chol', axis=1, tiled=True)]
    ppermute x0 -> x46, waiting for transfers between devices: none -> 70.3 us  [the longest x23 68.5 us: ring(): return lax.ppermute(value, 'chol', pairs)]
    ppermute x0 -> x46, starting transfers between devices: none -> 50.6 us  [the longest x23 41.2 us: ring(): return lax.ppermute(value, 'chol', pairs)]
    pallas_call x0 -> x8, Pallas kernels: none -> 22.7 us  [the longest x1 4.67 us: first_application(): pl.pallas_call(functools.partial(first_kernel, chips, walkers), out_shape...]
    dot_general x3 -> x0, matrix products: 19.2 us -> none  [the longest x2 14.2 us: apply_operator(): lax.dot_general(col_block, shard_piece[half_index], (((2,), (0,)), ((0,),...]
    mul x1 -> x0, other arithmetic: 6.62 us -> none  [per_device(): shifted_field[:, chol_index, None, None]]
    unnamed x10 -> x38, local copies, waits for them, and re-layouts: 7.4 us -> 4.42 us
  transfers between devices with their start and end apart: 5 -> 46, of which waited for: 5 -> 21; matrix products, arithmetic and copies ran while one was open for 5% -> 2% of each run, Pallas kernels for 0% -> 9%
where the time goes in v2:
time: 152 us; the launch traced here: 151 us
  waiting for transfers between devices  70.3 us (46%)
  starting transfers between devices  50.6 us (33%)
  Pallas kernels  22.7 us (15%)
  local copies, waits for them, and re-layouts  6.63 us (4%)
    ppermute x23, waiting for transfers between devices, ring(): return lax.ppermute(value, 'chol', pairs)  68.5 us
    ppermute x23, starting transfers between devices, ring(): return lax.ppermute(value, 'chol', pairs)  41.2 us
    ppermute x6, starting transfers between devices, across(): return lax.ppermute(value, 'walk', [(0, 1), (1, 0)])  7.75 us
    pallas_call x1, Pallas kernels, first_application(): pl.pallas_call(functools.partial(first_kernel, chips, walkers), out_shape...  4.67 us
    pallas_call x2, Pallas kernels, cut(): pl.pallas_call(functools.partial(cut_kernel, chips, rows, wanted), out_sh...  4.46 us
    unnamed x38, local copies, waits for them, and re-layouts  4.42 us
    pallas_call x1, Pallas kernels, chip_bias(): pl.pallas_call(functools.partial(bias_kernel, chips), out_shape=jax.Shape...  3.48 us
    pallas_call x1, Pallas kernels, early_operator(): pl.pallas_call(functools.partial(early_kernel, chips, walkers), out_shape...  3.34 us
  transfers between devices with their start and end apart: 46, of which 21 were waited for; matrix products, arithmetic and copies ran while one was open for 2% of the time, Pallas kernels for 9%

profile of v2, /device:TPU:0, one launch (start us, length us, event | category | flops | bytes accessed | tf_op | source)
XLA Modules:
  0.0 151.2 jit_solution(13056977696286230095)
XLA Ops:
  0.7 1.9 %cut_rows.2 = (bf16[128,1024]{1,0:T(8,128)(2,1)}, bf16[128,1024]{1,0:T(8,128)(2,1)}) custom-call(bf16[2,1024,1024]{2,1,0:T(8,128)(2,1)} %full_ref.2), custom_call_target="tpu_custom_call" | custom-call | tf_op jit(solution)/shard_map/cut_rows/pallas_call | solution.py:98
  2.6 3.1 %collective-permute-start = (bf16[128,1024]{1,0:T(8,128)(2,1)}, bf16[128,1024]{1,0:T(8,128)(2,1)}, u32[]{:S(2)}, u32[]{:S(2)}) collective-permute-start(bf16[128,1024]{1,0:T(8,128)(2,1)} %get-tuple-element.19), channel_id=1, source_target_pairs={{0,4},{2,6},{4,8},{6,10},{8,12},{10,14},{12,0},{14,2},{1,5},{3,7},... | collective-permute-start | bytes 786440 | tf_op jit(solution)/shard_map/ppermute | solution.py:373
  5.7 2.1 %collective-permute-start.1 = (bf16[128,1024]{1,0:T(8,128)(2,1)}, bf16[128,1024]{1,0:T(8,128)(2,1)S(1)}, u32[]{:S(2)}, u32[]{:S(2)}) collective-permute-start(bf16[128,1024]{1,0:T(8,128)(2,1)} %get-tuple-element.20), channel_id=1, source_target_pairs={{0,12},{2,14},{4,0},{6,2},{8,4},{10,6},{12,8},{14,10},{1,13},{3,15... | collective-permute-start | bytes 786440 | tf_op jit(solution)/shard_map/ppermute | solution.py:373
  7.8 2.5 %cut_rows.3 = (bf16[128,1024]{1,0:T(8,128)(2,1)}, bf16[128,1024]{1,0:T(8,128)(2,1)}, bf16[128,1024]{1,0:T(8,128)(2,1)}, bf16[128,1024]{1,0:T(8,128)(2,1)}, bf16[2,128,1024]{2,1,0:T(8,128)(2,1)}) custom-call(bf16[2,1024,1024]{2,1,0:T(8,128)(2,1)} %full_ref.2), custom_call_target="tpu_custom_call" | custom-call | tf_op jit(solution)/shard_map/cut_rows/pallas_call | solution.py:98
  10.3 2.0 %collective-permute-start.12 = (bf16[128,1024]{1,0:T(8,128)(2,1)}, bf16[128,1024]{1,0:T(8,128)(2,1)S(1)}, u32[]{:S(2)}, u32[]{:S(2)}) collective-permute-start(bf16[128,1024]{1,0:T(8,128)(2,1)} %get-tuple-element.25), channel_id=1, source_target_pairs={{0,12},{2,14},{4,0},{6,2},{8,4},{10,6},{12,8},{14,10},{1,13},{3,15... | collective-permute-start | bytes 786440 | tf_op jit(solution)/shard_map/ppermute | solution.py:373
  12.4 2.8 %collective-permute-done = bf16[128,1024]{1,0:T(8,128)(2,1)} collective-permute-done((bf16[128,1024]{1,0:T(8,128)(2,1)}, bf16[128,1024]{1,0:T(8,128)(2,1)}, u32[]{:S(2)}, u32[]{:S(2)}) %collective-permute-start) | collective-permute-done | bytes 262176 | tf_op jit(solution)/shard_map/ppermute | solution.py:373
  15.2 4.8 %collective-permute-done.1 = bf16[128,1024]{1,0:T(8,128)(2,1)S(1)} collective-permute-done((bf16[128,1024]{1,0:T(8,128)(2,1)}, bf16[128,1024]{1,0:T(8,128)(2,1)S(1)}, u32[]{:S(2)}, u32[]{:S(2)}) %collective-permute-start.1) | collective-permute-done | bytes 262176 | tf_op jit(solution)/shard_map/ppermute | solution.py:373
  20.0 4.7 %collective-permute-start.3 = (bf16[4,128,256]{2,1,0:T(8,128)(2,1)S(1)}, bf16[4,128,256]{2,1,0:T(8,128)(2,1)S(1)}, u32[]{:S(2)}, u32[]{:S(2)}) collective-permute-start(bf16[4,128,256]{2,1,0:T(8,128)(2,1)S(1)} %copy-done.11), channel_id=1, source_target_pairs={{0,4},{2,6},{4,8},{6,10},{8,12},{10,14},{12,0},{14,2},{1,5},{3,7},... | collective-permute-start | bytes 786440 | tf_op jit(solution)/shard_map/ppermute | solution.py:373
  24.7 3.8 %collective-permute-start.2 = (bf16[4,128,256]{2,1,0:T(8,128)(2,1)S(1)}, bf16[4,128,256]{2,1,0:T(8,128)(2,1)S(1)}, u32[]{:S(2)}, u32[]{:S(2)}) collective-permute-start(bf16[4,128,256]{2,1,0:T(8,128)(2,1)S(1)} %copy-done.11), channel_id=1, source_target_pairs={{0,12},{2,14},{4,0},{6,2},{8,4},{10,6},{12,8},{14,10},{1,13},{3,15... | collective-permute-start | bytes 786440 | tf_op jit(solution)/shard_map/ppermute | solution.py:373
  28.5 1.5 collective-permute-start.13
  30.4 1.7 %collective-permute-done.16.refs_4_ = bf16[128,1024]{1,0:T(8,128)(2,1)S(1)} collective-permute-done((bf16[128,1024]{1,0:T(8,128)(2,1)}, bf16[128,1024]{1,0:T(8,128)(2,1)S(1)}, u32[]{:S(2)}, u32[]{:S(2)}) %collective-permute-start.16) | collective-permute-done | bytes 262176 | tf_op jit(solution)/shard_map/ppermute | solution.py:373
  32.2 5.4 %collective-permute-done.3.below_ref = bf16[4,128,256]{2,1,0:T(8,128)(2,1)S(1)} collective-permute-done((bf16[4,128,256]{2,1,0:T(8,128)(2,1)S(1)}, bf16[4,128,256]{2,1,0:T(8,128)(2,1)S(1)}, u32[]{:S(2)}, u32[]{:S(2)}) %collective-permute-start.3) | collective-permute-done | bytes 262176 | tf_op jit(solution)/shard_map/ppermute | solution.py:373
  37.6 7.6 %collective-permute-start.24 = (bf16[128,1024]{1,0:T(8,128)(2,1)}, bf16[128,1024]{1,0:T(8,128)(2,1)}, u32[]{:S(2)}, u32[]{:S(2)}) collective-permute-start(bf16[128,1024]{1,0:T(8,128)(2,1)} %get-tuple-element.30), channel_id=1, source_target_pairs={{0,12},{2,14},{4,0},{6,2},{8,4},{10,6},{12,8},{14,10},{1,13},{3,15... | collective-permute-start | bytes 786440 | tf_op jit(solution)/shard_map/ppermute | solution.py:373
  45.2 2.3 %collective-permute-done.2.above_ref = bf16[4,128,256]{2,1,0:T(8,128)(2,1)S(1)} collective-permute-done((bf16[4,128,256]{2,1,0:T(8,128)(2,1)S(1)}, bf16[4,128,256]{2,1,0:T(8,128)(2,1)S(1)}, u32[]{:S(2)}, u32[]{:S(2)}) %collective-permute-start.2) | collective-permute-done | bytes 262176 | tf_op jit(solution)/shard_map/ppermute | solution.py:373
  47.5 1.3 collective-permute-start.17
  49.0 4.1 %collective-permute-done.24 = bf16[128,1024]{1,0:T(8,128)(2,1)} collective-permute-done((bf16[128,1024]{1,0:T(8,128)(2,1)}, bf16[128,1024]{1,0:T(8,128)(2,1)}, u32[]{:S(2)}, u32[]{:S(2)}) %collective-permute-start.24) | collective-permute-done | bytes 262176 | tf_op jit(solution)/shard_map/ppermute | solution.py:373
  53.1 2.3 %walker_major.1.refs_4_ = bf16[4,128,256]{2,1,0:T(8,128)(2,1)} custom-call(f32[1,128,4,256]{3,2,1,0:T(4,128)} %orbitals_ref.3), custom_call_target="tpu_custom_call" | custom-call | tf_op jit(solution)/shard_map/walker_major/pallas_call | solution.py:115
  57.3 3.3 %collective-permute-start.5 = (bf16[2,128,256]{2,1,0:T(8,128)(2,1)S(1)}, bf16[2,128,256]{2,1,0:T(8,128)(2,1)S(1)}, u32[]{:S(2)}, u32[]{:S(2)}) collective-permute-start(bf16[2,128,256]{2,1,0:T(8,128)(2,1)S(1)} %slice.29), channel_id=1, source_target_pairs={{0,12},{2,14},{4,0},{6,2},{8,4},{10,6},{12,8},{14,10},{1,13},{3,15... | collective-permute-start | bytes 393224 | tf_op jit(solution)/shard_map/ppermute | solution.py:373
  60.6 1.3 collective-permute-start.19
  62.0 8.3 %collective-permute-done.4.low_ref = bf16[2,128,256]{2,1,0:T(8,128)(2,1)S(1)} collective-permute-done((bf16[2,128,256]{2,1,0:T(8,128)(2,1)S(1)}, bf16[2,128,256]{2,1,0:T(8,128)(2,1)S(1)}, u32[]{:S(2)}, u32[]{:S(2)}) %collective-permute-start.4) | collective-permute-done | bytes 131104 | tf_op jit(solution)/shard_map/ppermute | solution.py:373
  70.2 1.4 collective-permute-done.5.high_ref
  71.6 1.2 collective-permute-start.15
  72.8 1.5 %collective-permute-start.25 = (bf16[128,1024]{1,0:T(8,128)(2,1)}, bf16[128,1024]{1,0:T(8,128)(2,1)}, u32[]{:S(2)}, u32[]{:S(2)}) collective-permute-start(bf16[128,1024]{1,0:T(8,128)(2,1)} %collective-permute-done.24), channel_id=1, source_target_pairs={{0,12},{2,14},{4,0},{6,2},{8,4},{10,6},{12,8},{14,10},{1,13},{3,15... | collective-permute-start | bytes 786440 | tf_op jit(solution)/shard_map/ppermute | solution.py:373
  74.9 4.2 %collective-permute-done.28.refs_5_ = bf16[4,128,256]{2,1,0:T(8,128)(2,1)S(1)} collective-permute-done((bf16[4,128,256]{2,1,0:T(8,128)(2,1)}, bf16[4,128,256]{2,1,0:T(8,128)(2,1)S(1)}, u32[]{:S(2)}, u32[]{:S(2)}) %collective-permute-start.28) | collective-permute-done | bytes 262176 | tf_op jit(solution)/shard_map/ppermute | solution.py:373
  79.9 1.3 collective-permute-start.22
  81.2 2.1 %collective-permute-done.25 = bf16[128,1024]{1,0:T(8,128)(2,1)} collective-permute-done((bf16[128,1024]{1,0:T(8,128)(2,1)}, bf16[128,1024]{1,0:T(8,128)(2,1)}, u32[]{:S(2)}, u32[]{:S(2)}) %collective-permute-start.25) | collective-permute-done | bytes 262176 | tf_op jit(solution)/shard_map/ppermute | solution.py:373
  83.3 2.4 %collective-permute-start.31 = (bf16[2,128,256]{2,1,0:T(8,128)(2,1)S(1)}, bf16[2,128,256]{2,1,0:T(8,128)(2,1)}, u32[]{:S(2)}, u32[]{:S(2)}) collective-permute-start(bf16[2,128,256]{2,1,0:T(8,128)(2,1)S(1)} %slice.31), channel_id=1, source_target_pairs={{0,12},{2,14},{4,0},{6,2},{8,4},{10,6},{12,8},{14,10},{1,13},{3,15... | collective-permute-start | bytes 393224 | tf_op jit(solution)/shard_map/ppermute | solution.py:373
  86.6 7.7 %collective-permute-done.31.refs_7_ = bf16[2,128,256]{2,1,0:T(8,128)(2,1)} collective-permute-done((bf16[2,128,256]{2,1,0:T(8,128)(2,1)S(1)}, bf16[2,128,256]{2,1,0:T(8,128)(2,1)}, u32[]{:S(2)}, u32[]{:S(2)}) %collective-permute-start.31) | collective-permute-done | bytes 131104 | tf_op jit(solution)/shard_map/ppermute | solution.py:373
  94.8 3.5 %chip_bias.1.mine_ref = f32[16,128]{1,0:T(8,128)} custom-call(bf16[4,128,256]{2,1,0:T(8,128)(2,1)} %here_ref, bf16[4,128,256]{2,1,0:T(8,128)(2,1)} %copy-done.10, bf16[2,128,256]{2,1,0:T(8,128)(2,1)} %copy-done.12, bf16[2,128,256]{2,1,0:T(8,128)(2,1)} %copy-done.13, bf16[4,128,256]{2,1,0:T(8,128)(2,1)} %copy-done.9, bf16[2,1024,256]{2,1,0:T(8,128)(2,1)} %mine_ref.1, ...), custom_call_target="tpu_custom_call" | custom-call | tf_op jit(solution)/shard_map/chip_bias/pallas_call | solution.py:166
  98.9 1.5 collective-permute-start.23
  101.3 1.4 chip_field.1
  103.3 5.1 %collective-permute-done.10.field_below = f32[16,128]{1,0:T(8,128)S(1)} collective-permute-done((f32[16,128]{1,0:T(8,128)}, f32[16,128]{1,0:T(8,128)S(1)}, u32[]{:S(2)}, u32[]{:S(2)}) %collective-permute-start.10) | collective-permute-done | bytes 8224 | tf_op jit(solution)/shard_map/ppermute | solution.py:373
  108.4 3.9 %collective-permute-done.9.field_above = f32[16,128]{1,0:T(8,128)S(1)} collective-permute-done((f32[16,128]{1,0:T(8,128)}, f32[16,128]{1,0:T(8,128)S(1)}, u32[]{:S(2)}, u32[]{:S(2)}) %collective-permute-start.9) | collective-permute-done | bytes 8224 | tf_op jit(solution)/shard_map/ppermute | solution.py:373
  112.2 1.1 constant_dynamic-slice_fusion.own_ref
  113.3 0.9 copy-done.7
  115.0 3.3 %early_operator.1.summed_in = f32[4,128,1024]{2,1,0:T(8,128)S(1)} custom-call(f32[16,128]{1,0:T(8,128)S(1)} %copy-done.8, f32[16,128]{1,0:T(8,128)S(1)} %collective-permute-done.9.field_above, f32[16,128]{1,0:T(8,128)S(1)} %collective-permute-done.10.field_below, bf16[2,128,1024]{2,1,0:T(8,128)(2,1)S(1)} %constant_dynamic-slice_fusion.own_ref, ...), custom_call_target="tpu_custom_call" | custom-call | tf_op jit(solution)/shard_map/early_operator/pallas_call | solution.py:264
  118.4 1.0 copy-done.5
  119.4 4.7 %first_application.1 = (bf16[4,256,1024]{2,1,0:T(8,128)(2,1)S(1)}, f32[4,128,256]{2,1,0:T(8,128)S(1)}, bf16[4,128,256]{2,1,0:T(8,128)(2,1)}) custom-call(f32[4,128,1024]{2,1,0:T(8,128)S(1)} %early_operator.1.summed_in, f32[16,128]{1,0:T(8,128)S(1)} %collective-permute-done.20.field_far, bf16[128,1024]{1,0:T(8,128)(2,1)} %collective-permute-done.22.refs_0_, ...), custom_call_target="tpu_custom_call" | custom-call | tf_op jit(solution)/shard_map/first_application/pallas_call | solution.py:329
  124.1 2.4 %collective-permute-start.38 = (bf16[4,128,256]{2,1,0:T(8,128)(2,1)}, bf16[4,128,256]{2,1,0:T(8,128)(2,1)S(1)}, u32[]{:S(2)}, u32[]{:S(2)}) collective-permute-start(bf16[4,128,256]{2,1,0:T(8,128)(2,1)} %get-tuple-element.34.refs_0_), channel_id=1, source_target_pairs={{0,4},{2,6},{4,8},{6,10},{8,12},{10,14},{12,0},{14,2},{1,5},{3,7},... | collective-permute-start | bytes 786440 | tf_op jit(solution)/shard_map/ppermute | solution.py:373
  126.4 1.5 collective-permute-start.37
  127.9 7.5 %collective-permute-done.38.refs_4_ = bf16[4,128,256]{2,1,0:T(8,128)(2,1)S(1)} collective-permute-done((bf16[4,128,256]{2,1,0:T(8,128)(2,1)}, bf16[4,128,256]{2,1,0:T(8,128)(2,1)S(1)}, u32[]{:S(2)}, u32[]{:S(2)}) %collective-permute-start.38) | collective-permute-done | bytes 262176 | tf_op jit(solution)/shard_map/ppermute | solution.py:373
  135.4 1.0 collective-permute-start.39
  136.4 2.8 %collective-permute-done.37.refs_1_ = bf16[4,128,256]{2,1,0:T(8,128)(2,1)S(1)} collective-permute-done((bf16[4,128,256]{2,1,0:T(8,128)(2,1)}, bf16[4,128,256]{2,1,0:T(8,128)(2,1)S(1)}, u32[]{:S(2)}, u32[]{:S(2)}) %collective-permute-start.37) | collective-permute-done | bytes 262176 | tf_op jit(solution)/shard_map/ppermute | solution.py:373
  139.2 2.1 %collective-permute-start.40 = (bf16[2,128,256]{2,1,0:T(8,128)(2,1)S(1)}, bf16[2,128,256]{2,1,0:T(8,128)(2,1)}, u32[]{:S(2)}, u32[]{:S(2)}) collective-permute-start(bf16[2,128,256]{2,1,0:T(8,128)(2,1)S(1)} %slice.33), channel_id=1, source_target_pairs={{0,12},{2,14},{4,0},{6,2},{8,4},{10,6},{12,8},{14,10},{1,13},{3,15... | collective-permute-start | bytes 393224 | tf_op jit(solution)/shard_map/ppermute | solution.py:373
  141.8 1.3 collective-permute-done.39.refs_2_
  143.1 2.2 %collective-permute-done.40.refs_3_ = bf16[2,128,256]{2,1,0:T(8,128)(2,1)} collective-permute-done((bf16[2,128,256]{2,1,0:T(8,128)(2,1)S(1)}, bf16[2,128,256]{2,1,0:T(8,128)(2,1)}, u32[]{:S(2)}, u32[]{:S(2)}) %collective-permute-start.40) | collective-permute-done | bytes 131104 | tf_op jit(solution)/shard_map/ppermute | solution.py:373
  147.0 1.0 copy-done.3
  148.1 3.2 %second_application.1 = f32[1,128,4,256]{3,2,1,0:T(4,128)} custom-call(bf16[4,256,1024]{2,1,0:T(8,128)(2,1)S(1)} %get-tuple-element.32.operator_ref, f32[4,128,256]{2,1,0:T(8,128)S(1)} %copy-done.3, f32[1,128,4,256]{3,2,1,0:T(4,128)S(1)} %copy-done, bf16[4,128,256]{2,1,0:T(8,128)(2,1)} %get-tuple-element.34.refs_0_, ...), custom_call_target="tpu_custom_call" | custom-call | tf_op jit(solution)/shard_map/second_application/pallas_call | solution.py:357
  (104 shorter events, 10.4 us)
Async XLA Ops:
  2.6 12.6 %collective-permute-start = (bf16[128,1024]{1,0:T(8,128)(2,1)}, bf16[128,1024]{1,0:T(8,128)(2,1)}, u32[]{:S(2)}, u32[]{:S(2)}) collective-permute-start(bf16[128,1024]{1,0:T(8,128)(2,1)} %get-tuple-element.19), channel_id=1, source_target_pairs={{0,4},{2,6},{4,8},{6,10},{8,12},{10,14},{12,0},{14,2},{1,5},{3,7},... | collective-permute-start | bytes 786440 | tf_op jit(solution)/shard_map/ppermute | solution.py:373
  5.7 14.3 %collective-permute-start.1 = (bf16[128,1024]{1,0:T(8,128)(2,1)}, bf16[128,1024]{1,0:T(8,128)(2,1)S(1)}, u32[]{:S(2)}, u32[]{:S(2)}) collective-permute-start(bf16[128,1024]{1,0:T(8,128)(2,1)} %get-tuple-element.20), channel_id=1, source_target_pairs={{0,12},{2,14},{4,0},{6,2},{8,4},{10,6},{12,8},{14,10},{1,13},{3,15... | collective-permute-start | bytes 786440 | tf_op jit(solution)/shard_map/ppermute | solution.py:373
  10.3 18.2 %collective-permute-start.12 = (bf16[128,1024]{1,0:T(8,128)(2,1)}, bf16[128,1024]{1,0:T(8,128)(2,1)S(1)}, u32[]{:S(2)}, u32[]{:S(2)}) collective-permute-start(bf16[128,1024]{1,0:T(8,128)(2,1)} %get-tuple-element.25), channel_id=1, source_target_pairs={{0,12},{2,14},{4,0},{6,2},{8,4},{10,6},{12,8},{14,10},{1,13},{3,15... | collective-permute-start | bytes 786440 | tf_op jit(solution)/shard_map/ppermute | solution.py:373
  12.3 19.8 %collective-permute-start.16 = (bf16[128,1024]{1,0:T(8,128)(2,1)}, bf16[128,1024]{1,0:T(8,128)(2,1)S(1)}, u32[]{:S(2)}, u32[]{:S(2)}) collective-permute-start(bf16[128,1024]{1,0:T(8,128)(2,1)} %get-tuple-element.26), channel_id=1, source_target_pairs={{0,4},{2,6},{4,8},{6,10},{8,12},{10,14},{12,0},{14,2},{1,5},{3,7},... | collective-permute-start | bytes 786440 | tf_op jit(solution)/shard_map/ppermute | solution.py:373
  20.0 17.6 %collective-permute-start.3 = (bf16[4,128,256]{2,1,0:T(8,128)(2,1)S(1)}, bf16[4,128,256]{2,1,0:T(8,128)(2,1)S(1)}, u32[]{:S(2)}, u32[]{:S(2)}) collective-permute-start(bf16[4,128,256]{2,1,0:T(8,128)(2,1)S(1)} %copy-done.11), channel_id=1, source_target_pairs={{0,4},{2,6},{4,8},{6,10},{8,12},{10,14},{12,0},{14,2},{1,5},{3,7},... | collective-permute-start | bytes 786440 | tf_op jit(solution)/shard_map/ppermute | solution.py:373
  24.7 22.8 %collective-permute-start.2 = (bf16[4,128,256]{2,1,0:T(8,128)(2,1)S(1)}, bf16[4,128,256]{2,1,0:T(8,128)(2,1)S(1)}, u32[]{:S(2)}, u32[]{:S(2)}) collective-permute-start(bf16[4,128,256]{2,1,0:T(8,128)(2,1)S(1)} %copy-done.11), channel_id=1, source_target_pairs={{0,12},{2,14},{4,0},{6,2},{8,4},{10,6},{12,8},{14,10},{1,13},{3,15... | collective-permute-start | bytes 786440 | tf_op jit(solution)/shard_map/ppermute | solution.py:373
  28.5 18.9 %collective-permute-start.13 = (bf16[128,1024]{1,0:T(8,128)(2,1)S(1)}, bf16[128,1024]{1,0:T(8,128)(2,1)S(1)}, u32[]{:S(2)}, u32[]{:S(2)}) collective-permute-start(bf16[128,1024]{1,0:T(8,128)(2,1)S(1)} %collective-permute-done.12.refs_0_), channel_id=1, source_target_pairs={{0,1},{1,0},{2,3},{3,2},{4,5},{5,4},{6,7},{7,6},{8,9},{9,8},{10,11... | collective-permute-start | bytes 786440 | tf_op jit(solution)/shard_map/ppermute | solution.py:379
  30.4 70.9 %copy-start.14 = (f32[16,128]{1,0:T(8,128)}, f32[16,128]{1,0:T(8,128)S(1)}, u32[]{:S(2)}) copy-start(f32[16,128]{1,0:T(8,128)S(1)} %broadcast_in_dim.10.noise_ref) | copy-start | bytes 24580
  30.4 1.7 %collective-permute-start.8 = (f32[16,128]{1,0:T(8,128)S(1)}, f32[16,128]{1,0:T(8,128)S(1)}, u32[]{:S(2)}, u32[]{:S(2)}) collective-permute-start(f32[16,128]{1,0:T(8,128)S(1)} %broadcast_in_dim.10.noise_ref), channel_id=1, source_target_pairs={{0,2},{2,0},{4,6},{6,4},{8,10},{10,8},{12,14},{14,12},{1,3},{3,1},... | collective-permute-start | bytes 24584 | tf_op jit(solution)/shard_map/ppermute | solution.py:376
  32.1 24.6 %collective-permute-start.11 = (bf16[2,128,1024]{2,1,0:T(8,128)(2,1)}, bf16[2,128,1024]{2,1,0:T(8,128)(2,1)S(1)}, u32[]{:S(2)}, u32[]{:S(2)}) collective-permute-start(bf16[2,128,1024]{2,1,0:T(8,128)(2,1)} %get-tuple-element.24), channel_id=1, source_target_pairs={{0,2},{2,0},{4,6},{6,4},{8,10},{10,8},{12,14},{14,12},{1,3},{3,1},... | collective-permute-start | bytes 1572872 | tf_op jit(solution)/shard_map/ppermute | solution.py:376
  32.1 69.2 %copy-start.15 = (f32[16,128]{1,0:T(8,128)}, f32[16,128]{1,0:T(8,128)S(1)}, u32[]{:S(2)}) copy-start(f32[16,128]{1,0:T(8,128)S(1)} %collective-permute-done.8.noise_there_ref) | copy-start | bytes 24580
  32.1 16.9 %collective-permute-start.21 = (bf16[128,1024]{1,0:T(8,128)(2,1)}, bf16[128,1024]{1,0:T(8,128)(2,1)}, u32[]{:S(2)}, u32[]{:S(2)}) collective-permute-start(bf16[128,1024]{1,0:T(8,128)(2,1)} %get-tuple-element.29), channel_id=1, source_target_pairs={{0,4},{2,6},{4,8},{6,10},{8,12},{10,14},{12,0},{14,2},{1,5},{3,7},... | collective-permute-start | bytes 786440 | tf_op jit(solution)/shard_map/ppermute | solution.py:373
  37.6 15.5 %collective-permute-start.24 = (bf16[128,1024]{1,0:T(8,128)(2,1)}, bf16[128,1024]{1,0:T(8,128)(2,1)}, u32[]{:S(2)}, u32[]{:S(2)}) collective-permute-start(bf16[128,1024]{1,0:T(8,128)(2,1)} %get-tuple-element.30), channel_id=1, source_target_pairs={{0,12},{2,14},{4,0},{6,2},{8,4},{10,6},{12,8},{14,10},{1,13},{3,15... | collective-permute-start | bytes 786440 | tf_op jit(solution)/shard_map/ppermute | solution.py:373
  47.4 46.9 %collective-permute-start.6 = (bf16[2,1024,256]{2,1,0:T(8,128)(2,1)}, bf16[2,1024,256]{2,1,0:T(8,128)(2,1)}, u32[]{:S(2)}, u32[]{:S(2)}) collective-permute-start(bf16[2,1024,256]{2,1,0:T(8,128)(2,1)} %mine_ref.1), channel_id=1, source_target_pairs={{0,2},{2,0},{4,6},{6,4},{8,10},{10,8},{12,14},{14,12},{1,3},{3,1},... | collective-permute-start | bytes 3145736 | tf_op jit(solution)/shard_map/ppermute | solution.py:376
  47.5 8.7 %collective-permute-start.17 = (bf16[128,1024]{1,0:T(8,128)(2,1)S(1)}, bf16[128,1024]{1,0:T(8,128)(2,1)S(1)}, u32[]{:S(2)}, u32[]{:S(2)}) collective-permute-start(bf16[128,1024]{1,0:T(8,128)(2,1)S(1)} %collective-permute-done.16.refs_4_), channel_id=1, source_target_pairs={{0,1},{1,0},{2,3},{3,2},{4,5},{5,4},{6,7},{7,6},{8,9},{9,8},{10,11... | collective-permute-start | bytes 786440 | tf_op jit(solution)/shard_map/ppermute | solution.py:379
  49.0 8.3 %collective-permute-start.18 = (bf16[128,1024]{1,0:T(8,128)(2,1)}, bf16[128,1024]{1,0:T(8,128)(2,1)S(1)}, u32[]{:S(2)}, u32[]{:S(2)}) collective-permute-start(bf16[128,1024]{1,0:T(8,128)(2,1)} %collective-permute-done), channel_id=1, source_target_pairs={{0,2},{2,0},{4,6},{6,4},{8,10},{10,8},{12,14},{14,12},{1,3},{3,1},... | collective-permute-start | bytes 786440 | tf_op jit(solution)/shard_map/ppermute | solution.py:376
  53.1 7.6 %collective-permute-start.14 = (bf16[128,1024]{1,0:T(8,128)(2,1)S(1)}, bf16[128,1024]{1,0:T(8,128)(2,1)S(1)}, u32[]{:S(2)}, u32[]{:S(2)}) collective-permute-start(bf16[128,1024]{1,0:T(8,128)(2,1)S(1)} %collective-permute-done.1), channel_id=1, source_target_pairs={{0,2},{2,0},{4,6},{6,4},{8,10},{10,8},{12,14},{14,12},{1,3},{3,1},... | collective-permute-start | bytes 786440 | tf_op jit(solution)/shard_map/ppermute | solution.py:376
  56.2 16.7 %collective-permute-start.29 = (bf16[4,128,256]{2,1,0:T(8,128)(2,1)}, bf16[4,128,256]{2,1,0:T(8,128)(2,1)S(1)}, u32[]{:S(2)}, u32[]{:S(2)}) collective-permute-start(bf16[4,128,256]{2,1,0:T(8,128)(2,1)} %walker_major.1.refs_4_), channel_id=1, source_target_pairs={{0,4},{2,6},{4,8},{6,10},{8,12},{10,14},{12,0},{14,2},{1,5},{3,7},... | collective-permute-start | bytes 786440 | tf_op jit(solution)/shard_map/ppermute | solution.py:373
  56.7 13.6 %collective-permute-start.4 = (bf16[2,128,256]{2,1,0:T(8,128)(2,1)S(1)}, bf16[2,128,256]{2,1,0:T(8,128)(2,1)S(1)}, u32[]{:S(2)}, u32[]{:S(2)}) collective-permute-start(bf16[2,128,256]{2,1,0:T(8,128)(2,1)S(1)} %slice.28), channel_id=1, source_target_pairs={{0,4},{2,6},{4,8},{6,10},{8,12},{10,14},{12,0},{14,2},{1,5},{3,7},... | collective-permute-start | bytes 393224 | tf_op jit(solution)/shard_map/ppermute | solution.py:373
  57.3 14.3 %collective-permute-start.5 = (bf16[2,128,256]{2,1,0:T(8,128)(2,1)S(1)}, bf16[2,128,256]{2,1,0:T(8,128)(2,1)S(1)}, u32[]{:S(2)}, u32[]{:S(2)}) collective-permute-start(bf16[2,128,256]{2,1,0:T(8,128)(2,1)S(1)} %slice.29), channel_id=1, source_target_pairs={{0,12},{2,14},{4,0},{6,2},{8,4},{10,6},{12,8},{14,10},{1,13},{3,15... | collective-permute-start | bytes 393224 | tf_op jit(solution)/shard_map/ppermute | solution.py:373
  60.6 13.7 %collective-permute-start.19 = (bf16[128,1024]{1,0:T(8,128)(2,1)S(1)}, bf16[128,1024]{1,0:T(8,128)(2,1)S(1)}, u32[]{:S(2)}, u32[]{:S(2)}) collective-permute-start(bf16[128,1024]{1,0:T(8,128)(2,1)S(1)} %collective-permute-done.18.refs_6_), channel_id=1, source_target_pairs={{0,1},{1,0},{2,3},{3,2},{4,5},{5,4},{6,7},{7,6},{8,9},{9,8},{10,11... | collective-permute-start | bytes 786440 | tf_op jit(solution)/shard_map/ppermute | solution.py:379
  70.2 8.9 %collective-permute-start.28 = (bf16[4,128,256]{2,1,0:T(8,128)(2,1)}, bf16[4,128,256]{2,1,0:T(8,128)(2,1)S(1)}, u32[]{:S(2)}, u32[]{:S(2)}) collective-permute-start(bf16[4,128,256]{2,1,0:T(8,128)(2,1)} %walker_major.1.refs_4_), channel_id=1, source_target_pairs={{0,12},{2,14},{4,0},{6,2},{8,4},{10,6},{12,8},{14,10},{1,13},{3,15... | collective-permute-start | bytes 786440 | tf_op jit(solution)/shard_map/ppermute | solution.py:373
  71.6 7.6 %collective-permute-start.15 = (bf16[128,1024]{1,0:T(8,128)(2,1)S(1)}, bf16[128,1024]{1,0:T(8,128)(2,1)S(1)}, u32[]{:S(2)}, u32[]{:S(2)}) collective-permute-start(bf16[128,1024]{1,0:T(8,128)(2,1)S(1)} %collective-permute-done.14.refs_2_), channel_id=1, source_target_pairs={{0,1},{1,0},{2,3},{3,2},{4,5},{5,4},{6,7},{7,6},{8,9},{9,8},{10,11... | collective-permute-start | bytes 786440 | tf_op jit(solution)/shard_map/ppermute | solution.py:379
  72.8 10.5 %collective-permute-start.25 = (bf16[128,1024]{1,0:T(8,128)(2,1)}, bf16[128,1024]{1,0:T(8,128)(2,1)}, u32[]{:S(2)}, u32[]{:S(2)}) collective-permute-start(bf16[128,1024]{1,0:T(8,128)(2,1)} %collective-permute-done.24), channel_id=1, source_target_pairs={{0,12},{2,14},{4,0},{6,2},{8,4},{10,6},{12,8},{14,10},{1,13},{3,15... | collective-permute-start | bytes 786440 | tf_op jit(solution)/shard_map/ppermute | solution.py:373
  74.4 12.2 %collective-permute-start.30 = (bf16[2,128,256]{2,1,0:T(8,128)(2,1)S(1)}, bf16[2,128,256]{2,1,0:T(8,128)(2,1)S(1)}, u32[]{:S(2)}, u32[]{:S(2)}) collective-permute-start(bf16[2,128,256]{2,1,0:T(8,128)(2,1)S(1)} %slice.30), channel_id=1, source_target_pairs={{0,4},{2,6},{4,8},{6,10},{8,12},{10,14},{12,0},{14,2},{1,5},{3,7},... | collective-permute-start | bytes 393224 | tf_op jit(solution)/shard_map/ppermute | solution.py:373
  79.2 19.2 %collective-permute-start.32 = (bf16[4,128,256]{2,1,0:T(8,128)(2,1)}, bf16[4,128,256]{2,1,0:T(8,128)(2,1)S(1)}, u32[]{:S(2)}, u32[]{:S(2)}) collective-permute-start(bf16[4,128,256]{2,1,0:T(8,128)(2,1)} %walker_major.1.refs_4_), channel_id=1, source_target_pairs={{0,2},{2,0},{4,6},{6,4},{8,10},{10,8},{12,14},{14,12},{1,3},{3,1},... | collective-permute-start | bytes 786440 | tf_op jit(solution)/shard_map/ppermute | solution.py:376
  79.9 18.4 %collective-permute-start.22 = (bf16[128,1024]{1,0:T(8,128)(2,1)}, bf16[128,1024]{1,0:T(8,128)(2,1)}, u32[]{:S(2)}, u32[]{:S(2)}) collective-permute-start(bf16[128,1024]{1,0:T(8,128)(2,1)} %collective-permute-done.21), channel_id=1, source_target_pairs={{0,4},{2,6},{4,8},{6,10},{8,12},{10,14},{12,0},{14,2},{1,5},{3,7},... | collective-permute-start | bytes 786440 | tf_op jit(solution)/shard_map/ppermute | solution.py:373
  83.3 11.0 %collective-permute-start.31 = (bf16[2,128,256]{2,1,0:T(8,128)(2,1)S(1)}, bf16[2,128,256]{2,1,0:T(8,128)(2,1)}, u32[]{:S(2)}, u32[]{:S(2)}) collective-permute-start(bf16[2,128,256]{2,1,0:T(8,128)(2,1)S(1)} %slice.31), channel_id=1, source_target_pairs={{0,12},{2,14},{4,0},{6,2},{8,4},{10,6},{12,8},{14,10},{1,13},{3,15... | collective-permute-start | bytes 393224 | tf_op jit(solution)/shard_map/ppermute | solution.py:373
  86.6 12.3 %collective-permute-start.26 = (bf16[128,1024]{1,0:T(8,128)(2,1)}, bf16[128,1024]{1,0:T(8,128)(2,1)}, u32[]{:S(2)}, u32[]{:S(2)}) collective-permute-start(bf16[128,1024]{1,0:T(8,128)(2,1)} %collective-permute-done.25), channel_id=1, source_target_pairs={{0,2},{2,0},{4,6},{6,4},{8,10},{10,8},{12,14},{14,12},{1,3},{3,1},... | collective-permute-start | bytes 786440 | tf_op jit(solution)/shard_map/ppermute | solution.py:376
  94.3 4.5 %collective-permute-start.34 = (bf16[2,128,256]{2,1,0:T(8,128)(2,1)S(1)}, bf16[2,128,256]{2,1,0:T(8,128)(2,1)}, u32[]{:S(2)}, u32[]{:S(2)}) collective-permute-start(bf16[2,128,256]{2,1,0:T(8,128)(2,1)S(1)} %collective-permute-done.30.refs_6_), channel_id=1, source_target_pairs={{0,2},{2,0},{4,6},{6,4},{8,10},{10,8},{12,14},{14,12},{1,3},{3,1},... | collective-permute-start | bytes 393224 | tf_op jit(solution)/shard_map/ppermute | solution.py:376
  94.3 8.4 %collective-permute-start.35 = (bf16[2,128,256]{2,1,0:T(8,128)(2,1)}, bf16[2,128,256]{2,1,0:T(8,128)(2,1)}, u32[]{:S(2)}, u32[]{:S(2)}) collective-permute-start(bf16[2,128,256]{2,1,0:T(8,128)(2,1)} %collective-permute-done.31.refs_7_), channel_id=1, source_target_pairs={{0,2},{2,0},{4,6},{6,4},{8,10},{10,8},{12,14},{14,12},{1,3},{3,1},... | collective-permute-start | bytes 393224 | tf_op jit(solution)/shard_map/ppermute | solution.py:376
  98.3 2.1 %collective-permute-start.7 = (f32[16,128]{1,0:T(8,128)}, f32[16,128]{1,0:T(8,128)}, u32[]{:S(2)}, u32[]{:S(2)}) collective-permute-start(f32[16,128]{1,0:T(8,128)} %chip_bias.1.mine_ref), channel_id=1, source_target_pairs={{0,2},{2,0},{4,6},{6,4},{8,10},{10,8},{12,14},{14,12},{1,3},{3,1},... | collective-permute-start | bytes 24584 | tf_op jit(solution)/shard_map/ppermute | solution.py:376
  98.3 20.0 %collective-permute-start.33 = (bf16[4,128,256]{2,1,0:T(8,128)(2,1)S(1)}, bf16[4,128,256]{2,1,0:T(8,128)(2,1)}, u32[]{:S(2)}, u32[]{:S(2)}) collective-permute-start(bf16[4,128,256]{2,1,0:T(8,128)(2,1)S(1)} %collective-permute-done.28.refs_5_), channel_id=1, source_target_pairs={{0,2},{2,0},{4,6},{6,4},{8,10},{10,8},{12,14},{14,12},{1,3},{3,1},... | collective-permute-start | bytes 786440 | tf_op jit(solution)/shard_map/ppermute | solution.py:376
  98.8 19.5 %collective-permute-start.36 = (bf16[4,128,256]{2,1,0:T(8,128)(2,1)S(1)}, bf16[4,128,256]{2,1,0:T(8,128)(2,1)}, u32[]{:S(2)}, u32[]{:S(2)}) collective-permute-start(bf16[4,128,256]{2,1,0:T(8,128)(2,1)S(1)} %collective-permute-done.29.refs_8_), channel_id=1, source_target_pairs={{0,2},{2,0},{4,6},{6,4},{8,10},{10,8},{12,14},{14,12},{1,3},{3,1},... | collective-permute-start | bytes 786440 | tf_op jit(solution)/shard_map/ppermute | solution.py:376
  98.9 19.4 %collective-permute-start.23 = (bf16[128,1024]{1,0:T(8,128)(2,1)}, bf16[128,1024]{1,0:T(8,128)(2,1)}, u32[]{:S(2)}, u32[]{:S(2)}) collective-permute-start(bf16[128,1024]{1,0:T(8,128)(2,1)} %collective-permute-done.22.refs_0_), channel_id=1, source_target_pairs={{0,1},{1,0},{2,3},{3,2},{4,5},{5,4},{6,7},{7,6},{8,9},{9,8},{10,11... | collective-permute-start | bytes 786440 | tf_op jit(solution)/shard_map/ppermute | solution.py:379
  100.4 17.9 %collective-permute-start.27 = (bf16[128,1024]{1,0:T(8,128)(2,1)}, bf16[128,1024]{1,0:T(8,128)(2,1)}, u32[]{:S(2)}, u32[]{:S(2)}) collective-permute-start(bf16[128,1024]{1,0:T(8,128)(2,1)} %collective-permute-done.26.refs_2_), channel_id=1, source_target_pairs={{0,1},{1,0},{2,3},{3,2},{4,5},{5,4},{6,7},{7,6},{8,9},{9,8},{10,11... | collective-permute-start | bytes 786440 | tf_op jit(solution)/shard_map/ppermute | solution.py:379
  102.7 5.7 %collective-permute-start.10 = (f32[16,128]{1,0:T(8,128)}, f32[16,128]{1,0:T(8,128)S(1)}, u32[]{:S(2)}, u32[]{:S(2)}) collective-permute-start(f32[16,128]{1,0:T(8,128)} %get-tuple-element.22.field_here), channel_id=1, source_target_pairs={{0,4},{2,6},{4,8},{6,10},{8,12},{10,14},{12,0},{14,2},{1,5},{3,7},... | collective-permute-start | bytes 24584 | tf_op jit(solution)/shard_map/ppermute | solution.py:373
  108.4 3.9 %collective-permute-start.9 = (f32[16,128]{1,0:T(8,128)}, f32[16,128]{1,0:T(8,128)S(1)}, u32[]{:S(2)}, u32[]{:S(2)}) collective-permute-start(f32[16,128]{1,0:T(8,128)} %get-tuple-element.22.field_here), channel_id=1, source_target_pairs={{0,12},{2,14},{4,0},{6,2},{8,4},{10,6},{12,8},{14,10},{1,13},{3,15... | collective-permute-start | bytes 24584 | tf_op jit(solution)/shard_map/ppermute | solution.py:373
  112.2 6.1 %collective-permute-start.20 = (f32[16,128]{1,0:T(8,128)}, f32[16,128]{1,0:T(8,128)S(1)}, u32[]{:S(2)}, u32[]{:S(2)}) collective-permute-start(f32[16,128]{1,0:T(8,128)} %get-tuple-element.22.field_here), channel_id=1, source_target_pairs={{0,8},{2,10},{4,12},{6,14},{8,0},{10,2},{12,4},{14,6},{1,9},{3,11}... | collective-permute-start | bytes 24584 | tf_op jit(solution)/shard_map/ppermute | solution.py:373
  124.1 11.3 %collective-permute-start.38 = (bf16[4,128,256]{2,1,0:T(8,128)(2,1)}, bf16[4,128,256]{2,1,0:T(8,128)(2,1)S(1)}, u32[]{:S(2)}, u32[]{:S(2)}) collective-permute-start(bf16[4,128,256]{2,1,0:T(8,128)(2,1)} %get-tuple-element.34.refs_0_), channel_id=1, source_target_pairs={{0,4},{2,6},{4,8},{6,10},{8,12},{10,14},{12,0},{14,2},{1,5},{3,7},... | collective-permute-start | bytes 786440 | tf_op jit(solution)/shard_map/ppermute | solution.py:373
  126.4 12.8 %collective-permute-start.37 = (bf16[4,128,256]{2,1,0:T(8,128)(2,1)}, bf16[4,128,256]{2,1,0:T(8,128)(2,1)S(1)}, u32[]{:S(2)}, u32[]{:S(2)}) collective-permute-start(bf16[4,128,256]{2,1,0:T(8,128)(2,1)} %get-tuple-element.34.refs_0_), channel_id=1, source_target_pairs={{0,12},{2,14},{4,0},{6,2},{8,4},{10,6},{12,8},{14,10},{1,13},{3,15... | collective-permute-start | bytes 786440 | tf_op jit(solution)/shard_map/ppermute | solution.py:373
  127.9 18.2 %collective-permute-start.41 = (bf16[4,128,256]{2,1,0:T(8,128)(2,1)}, bf16[4,128,256]{2,1,0:T(8,128)(2,1)S(1)}, u32[]{:S(2)}, u32[]{:S(2)}) collective-permute-start(bf16[4,128,256]{2,1,0:T(8,128)(2,1)} %get-tuple-element.34.refs_0_), channel_id=1, source_target_pairs={{0,2},{2,0},{4,6},{6,4},{8,10},{10,8},{12,14},{14,12},{1,3},{3,1},... | collective-permute-start | bytes 786440 | tf_op jit(solution)/shard_map/ppermute | solution.py:376
  135.4 7.8 %collective-permute-start.39 = (bf16[2,128,256]{2,1,0:T(8,128)(2,1)S(1)}, bf16[2,128,256]{2,1,0:T(8,128)(2,1)S(1)}, u32[]{:S(2)}, u32[]{:S(2)}) collective-permute-start(bf16[2,128,256]{2,1,0:T(8,128)(2,1)S(1)} %slice.32), channel_id=1, source_target_pairs={{0,4},{2,6},{4,8},{6,10},{8,12},{10,14},{12,0},{14,2},{1,5},{3,7},... | collective-permute-start | bytes 393224 | tf_op jit(solution)/shard_map/ppermute | solution.py:373
  139.2 6.1 %collective-permute-start.40 = (bf16[2,128,256]{2,1,0:T(8,128)(2,1)S(1)}, bf16[2,128,256]{2,1,0:T(8,128)(2,1)}, u32[]{:S(2)}, u32[]{:S(2)}) collective-permute-start(bf16[2,128,256]{2,1,0:T(8,128)(2,1)S(1)} %slice.33), channel_id=1, source_target_pairs={{0,12},{2,14},{4,0},{6,2},{8,4},{10,6},{12,8},{14,10},{1,13},{3,15... | collective-permute-start | bytes 393224 | tf_op jit(solution)/shard_map/ppermute | solution.py:373
  141.3 5.7 %collective-permute-start.42 = (bf16[4,128,256]{2,1,0:T(8,128)(2,1)S(1)}, bf16[4,128,256]{2,1,0:T(8,128)(2,1)}, u32[]{:S(2)}, u32[]{:S(2)}) collective-permute-start(bf16[4,128,256]{2,1,0:T(8,128)(2,1)S(1)} %collective-permute-done.37.refs_1_), channel_id=1, source_target_pairs={{0,2},{2,0},{4,6},{6,4},{8,10},{10,8},{12,14},{14,12},{1,3},{3,1},... | collective-permute-start | bytes 786440 | tf_op jit(solution)/shard_map/ppermute | solution.py:376
  141.3 5.7 %collective-permute-start.45 = (bf16[4,128,256]{2,1,0:T(8,128)(2,1)S(1)}, bf16[4,128,256]{2,1,0:T(8,128)(2,1)}, u32[]{:S(2)}, u32[]{:S(2)}) collective-permute-start(bf16[4,128,256]{2,1,0:T(8,128)(2,1)S(1)} %collective-permute-done.38.refs_4_), channel_id=1, source_target_pairs={{0,2},{2,0},{4,6},{6,4},{8,10},{10,8},{12,14},{14,12},{1,3},{3,1},... | collective-permute-start | bytes 786440 | tf_op jit(solution)/shard_map/ppermute | solution.py:376
  143.1 2.9 %collective-permute-start.43 = (bf16[2,128,256]{2,1,0:T(8,128)(2,1)S(1)}, bf16[2,128,256]{2,1,0:T(8,128)(2,1)}, u32[]{:S(2)}, u32[]{:S(2)}) collective-permute-start(bf16[2,128,256]{2,1,0:T(8,128)(2,1)S(1)} %collective-permute-done.39.refs_2_), channel_id=1, source_target_pairs={{0,2},{2,0},{4,6},{6,4},{8,10},{10,8},{12,14},{14,12},{1,3},{3,1},... | collective-permute-start | bytes 393224 | tf_op jit(solution)/shard_map/ppermute | solution.py:376
  145.3 1.7 %collective-permute-start.44 = (bf16[2,128,256]{2,1,0:T(8,128)(2,1)}, bf16[2,128,256]{2,1,0:T(8,128)(2,1)}, u32[]{:S(2)}, u32[]{:S(2)}) collective-permute-start(bf16[2,128,256]{2,1,0:T(8,128)(2,1)} %collective-permute-done.40.refs_3_), channel_id=1, source_target_pairs={{0,2},{2,0},{4,6},{6,4},{8,10},{10,8},{12,14},{14,12},{1,3},{3,1},... | collective-permute-start | bytes 393224 | tf_op jit(solution)/shard_map/ppermute | solution.py:376
  (17 other events, 280.1 us)

commit v3 on v2

v3 whole, which is shorter than its diff:
```python
import functools

import jax
import jax.numpy as jnp
from jax import lax
from jax.experimental import pallas as pl
from jax.experimental.pallas import tpu as pltpu
from jax.sharding import PartitionSpec as P

time_root = 0.1


def general_device(green_blocks, half_chol, full_chol, meanfield, noise_draws, orbitals):
    walkers_here = green_blocks.shape[0]
    chol_here = half_chol.shape[0]
    half_rows = full_chol.shape[1]
    orbital_count = full_chol.shape[2]
    occupied = orbitals.shape[3]
    rows_here = orbitals.shape[1]
    partial_bias = jnp.einsum(
        "wki,cki->wc",
        lax.all_gather(green_blocks, "chol", axis=1, tiled=True),
        half_chol,
        preferred_element_type=jnp.float32,
    )
    force_bias = lax.psum(partial_bias, "orb")
    bias_shift = jnp.clip(time_root * (force_bias - meanfield[None, :]), -1.0, 1.0)
    shifted_field = noise_draws - bias_shift
    combined = jnp.zeros((walkers_here, half_rows, orbital_count), jnp.float32)
    for chol_index in range(chol_here):
        combined = combined + shifted_field[:, chol_index, None, None] * full_chol[chol_index][
            None
        ].astype(jnp.float32)
    operator_rows = (time_root * combined).astype(jnp.bfloat16)

    def apply_operator(vector):
        both_halves = lax.all_gather(vector, "orb", axis=0, tiled=True)
        running = jnp.zeros((walkers_here, half_rows, occupied), jnp.float32)
        shard_piece = lax.all_gather(both_halves, "chol", axis=1, tiled=True)
        row_count = shard_piece.shape[1]
        for half_index in range(shard_piece.shape[0]):
            col_block = lax.dynamic_slice_in_dim(
                operator_rows, half_index * half_rows, row_count, 2
            )
            running = running + lax.dot_general(
                col_block,
                shard_piece[half_index],
                (((2,), (0,)), ((0,), (1,))),
                preferred_element_type=jnp.float32,
            )
        summed = lax.psum(running, "chol")
        chol_slot = lax.axis_index("chol")
        owned_rows = lax.dynamic_slice_in_dim(summed, chol_slot * rows_here, rows_here, 1)
        return jnp.transpose(owned_rows, (1, 0, 2))[None]

    first_term = apply_operator(orbitals.astype(jnp.bfloat16))
    second_term = apply_operator(first_term.astype(jnp.bfloat16))
    walkers_next = orbitals + first_term + 0.5 * second_term
    return (walkers_next, bias_shift)


vmem_spec = pl.BlockSpec(memory_space=pltpu.VMEM)
any_spec = pl.BlockSpec(memory_space=pl.ANY)
wide = jnp.float32
narrow = jnp.bfloat16
small = pltpu.CompilerParams(vmem_limit_bytes=16 << 20)


def after(value, *others):
    return lax.optimization_barrier((value, *others))[0]


def place(chips):
    slot = lax.axis_index("chol")
    return slot // 2, slot % 2, lax.axis_index("walk")


def cut_kernel(chips, rows, wanted, full_ref, *refs):
    z, k, x = place(chips)
    outs, sem = refs[:-1], refs[-1]
    copies = []
    for index, (step, crossed, both) in enumerate(wanted):
        core = 1 - k if crossed else k
        start = pl.multiple_of((2 * lax.rem(z + step + chips, chips) + core) * rows, rows)
        picked = pl.ds(start, rows)
        source = full_ref.at[:, picked, :] if both else full_ref.at[x, picked, :]
        copies.append(pltpu.make_async_copy(source, outs[index], sem.at[index]))
        copies[-1].start()
    for copy in copies:
        copy.wait()


def cut(chips, rows, full_chol, wanted):
    order = full_chol.shape[2]
    shapes = [
        jax.ShapeDtypeStruct((2, rows, order) if both else (rows, order), narrow)
        for _, _, both in wanted
    ]
    return pl.pallas_call(
        functools.partial(cut_kernel, chips, rows, wanted),
        out_shape=shapes,
        in_specs=[any_spec],
        out_specs=[vmem_spec] * len(wanted),
        scratch_shapes=[pltpu.SemaphoreType.DMA((len(wanted),))],
        compiler_params=small,
        name="cut_rows",
    )(full_chol)


def start_kernel(orbitals_ref, out_ref):
    for walker in range(out_ref.shape[0]):
        out_ref[walker] = orbitals_ref[0, :, walker, :].astype(narrow)


def walker_major(orbitals):
    _, rows, walkers, occupied = orbitals.shape
    return pl.pallas_call(
        start_kernel,
        out_shape=jax.ShapeDtypeStruct((walkers, rows, occupied), narrow),
        in_specs=[vmem_spec],
        out_specs=vmem_spec,
        compiler_params=small,
        name="walker_major",
    )(orbitals)


def bias_kernel(chips, here_ref, above_ref, low_ref, high_ref, below_ref, mine_ref, theirs_ref, out_ref):
    z, k, _ = place(chips)
    walkers, rows, occupied = here_ref.shape
    vectors = mine_ref.shape[0]
    half = walkers // 2
    step_rows = 16
    totals = [jnp.zeros((8, 128), wide) for _ in range(2 * vectors * walkers)]
    for step, green in ((0, here_ref), (1, above_ref), (2, None), (-1, below_ref)):
        base = (2 * lax.rem(z + step + chips, chips) + k) * rows

        def add(index, totals, base=base, green=green):
            here = pl.multiple_of(index * step_rows, step_rows)
            there = pl.multiple_of(base + index * step_rows, step_rows)
            picked = pl.ds(here, step_rows)
            if green is None:
                greens = [low_ref[w, picked, :] for w in range(half)]
                greens += [high_ref[w, picked, :] for w in range(half)]
            else:
                greens = [green[w, picked, :] for w in range(walkers)]
            greens = [g.astype(wide) for g in greens]
            totals = list(totals)
            for c in range(2 * vectors):
                chol_ref = mine_ref if c < vectors else theirs_ref
                chol = chol_ref[c % vectors, pl.ds(there, step_rows), :].astype(wide)
                for w in range(walkers):
                    product = greens[w] * chol
                    tiles = [
                        product[r : r + 8, n : n + 128]
                        for r in range(0, step_rows, 8)
                        for n in range(0, occupied, 128)
                    ]
                    totals[c * walkers + w] = totals[c * walkers + w] + sum(tiles[1:], tiles[0])
            return tuple(totals)

        totals = lax.fori_loop(0, rows // step_rows, add, tuple(totals))
    for index, total in enumerate(totals):
        value = jnp.sum(jnp.sum(total, axis=0, keepdims=True), axis=1, keepdims=True)
        out_ref[pl.ds(index, 1), :] = jnp.broadcast_to(value, (1, 128))


def chip_bias(chips, here, above, low, high, below, mine, theirs):
    entries = 2 * mine.shape[0] * here.shape[0]
    return pl.pallas_call(
        functools.partial(bias_kernel, chips),
        out_shape=jax.ShapeDtypeStruct((entries, 128), wide),
        in_specs=[vmem_spec] * 7,
        out_specs=vmem_spec,
        compiler_params=small,
        name="chip_bias",
    )(here, above, low, high, below, mine, theirs)


def field_kernel(gathered_ref, shift_ref, field_ref):
    devices, entries, _ = gathered_ref.shape
    part = entries // 4
    here = lax.axis_index("chol")
    for device in range(devices):
        mine, other = gathered_ref.at[device], gathered_ref.at[device ^ 1]
        force = mine[:part, :] + other[part : 2 * part, :]
        noise, mean = mine[2 * part : 3 * part, :], mine[3 * part :, :]
        shift = jnp.clip(time_root * (force - mean), -1.0, 1.0)
        field_ref[device * part : (device + 1) * part, :] = noise - shift

        @pl.when(here == device)
        def _(shift=shift):
            shift_ref[...] = shift


def all_fields(gathered):
    devices, entries, lanes = gathered.shape
    part = entries // 4
    return pl.pallas_call(
        field_kernel,
        out_shape=[
            jax.ShapeDtypeStruct((part, lanes), wide),
            jax.ShapeDtypeStruct((devices * part, lanes), wide),
        ],
        in_specs=[vmem_spec],
        out_specs=[vmem_spec] * 2,
        compiler_params=small,
        name="all_fields",
    )(gathered)


def block_operators(z, x, chips, walkers, field_ref, sources, picked):
    tiles = []
    for step, core, near, other in sources:
        chip = lax.rem(z + step + chips, chips)
        first = (2 * chip + core) * 2 * walkers
        one, two = near(picked).astype(wide), other(picked).astype(wide)
        copies = one.shape[1] // 128
        tiles.append([])
        for w in range(walkers):
            scale_one = field_ref[pl.ds(first + x * walkers + w, 1), :]
            scale_two = field_ref[pl.ds(first + (1 - x) * walkers + w, 1), :]
            scale_one = jnp.concatenate([scale_one] * copies, 1)
            scale_two = jnp.concatenate([scale_two] * copies, 1)
            block = time_root * (scale_one * one + scale_two * two)
            tiles[-1].append(block.astype(narrow))
    return tiles


def over_tiles(rows, order, body):
    high, across = 16, 256
    columns = order // across

    def tile(index, carry):
        row = pl.multiple_of((index // columns) * high, high)
        column = pl.multiple_of((index % columns) * across, across)
        body((pl.ds(row, high), pl.ds(column, across)))
        return carry

    lax.fori_loop(0, (rows // high) * columns, tile, 0)


def of_pair(ref, index):
    return lambda picked: ref[(index, *picked)]


def of_one(ref):
    return lambda picked: ref[picked]


def early_kernel(chips, walkers, field_ref, own, own_theirs, far, far_x, far_theirs, far_theirs_x, summed_ref):
    z, k, x = place(chips)
    sources = [
        (0, k, of_pair(own, x), of_pair(own, 1 - x)),
        (0, 1 - k, of_pair(own_theirs, x), of_pair(own_theirs, 1 - x)),
        (2, k, of_one(far), of_one(far_x)),
        (2, 1 - k, of_one(far_theirs), of_one(far_theirs_x)),
    ]

    def body(picked):
        tiles = block_operators(z, x, chips, walkers, field_ref, sources, picked)
        for w in range(walkers):
            parts = [block[w].astype(wide) for block in tiles]
            summed_ref[(w, *picked)] = sum(parts[1:], parts[0])

    over_tiles(*summed_ref.shape[1:], body)


def early_operator(chips, walkers, field, own, own_theirs, blocks):
    rows, order = blocks[0].shape
    return pl.pallas_call(
        functools.partial(early_kernel, chips, walkers),
        out_shape=jax.ShapeDtypeStruct((walkers, rows, order), wide),
        in_specs=[vmem_spec] * (3 + len(blocks)),
        out_specs=vmem_spec,
        compiler_params=small,
        name="early_operator",
    )(field, own, own_theirs, *blocks)


def collect(chips, vector_ref, pieces, absolute=True):
    z, k, _ = place(chips)
    for step, crossed, first, ref in pieces:
        count, rows, _ = ref.shape
        core = 1 - k if crossed else k
        chip = 2 * lax.rem(z + step + chips, chips) if absolute else 0
        start = pl.multiple_of((chip + core) * rows, rows)
        for w in range(count):
            vector_ref[first + w, pl.ds(start, rows), :] = ref[w]


def vector_pieces(refs):
    here, above, low, high, below, here_t, above_t, low_t, high_t, below_t = refs
    half = low.shape[0]
    return [
        (0, False, 0, here),
        (1, False, 0, above),
        (2, False, 0, low),
        (2, False, half, high),
        (-1, False, 0, below),
        (0, True, 0, here_t),
        (1, True, 0, above_t),
        (2, True, 0, low_t),
        (2, True, half, high_t),
        (-1, True, 0, below_t),
    ]


def middle_kernel(chips, summed_ref, field_ref, above_theirs, below_theirs, *refs):
    pieces, (operator_ref, vector_ref, first_ref) = refs[:10], refs[10:]
    walkers, rows, order = summed_ref.shape
    z, k, x = place(chips)
    collect(chips, vector_ref, vector_pieces(pieces))
    sources = [
        (1, 1 - k, of_pair(above_theirs, x), of_pair(above_theirs, 1 - x)),
        (-1, 1 - k, of_pair(below_theirs, x), of_pair(below_theirs, 1 - x)),
    ]

    def body(picked):
        tiles = block_operators(z, x, chips, walkers, field_ref, sources, picked)
        row, column = picked
        for w in range(walkers):
            value = summed_ref[(w, *picked)]
            for block in tiles:
                value = value + block[w].astype(wide)
            top = value.astype(narrow)
            operator_ref[w, row, column] = top
            rest = (value - top.astype(wide)).astype(narrow)
            operator_ref[w, pl.ds(rows + row.start, row.size), column] = rest

    over_tiles(rows, order, body)
    for w in range(walkers):
        both = jnp.dot(operator_ref[w], vector_ref[w], preferred_element_type=wide)
        first_ref[w] = both[:rows] + both[rows:]


def middle_operator(chips, summed, field, above_theirs, below_theirs, pieces):
    walkers, rows, order = summed.shape
    occupied = pieces[0].shape[2]
    return pl.pallas_call(
        functools.partial(middle_kernel, chips),
        out_shape=[
            jax.ShapeDtypeStruct((walkers, 2 * rows, order), narrow),
            jax.ShapeDtypeStruct((walkers, order, occupied), narrow),
            jax.ShapeDtypeStruct((walkers, rows, occupied), wide),
        ],
        in_specs=[vmem_spec] * 14,
        out_specs=[vmem_spec] * 3,
        compiler_params=small,
        name="middle_operator",
    )(summed, field, above_theirs, below_theirs, *pieces)


def first_kernel(chips, field_ref, above, below, vector_ref, partial_ref, operator_ref, first_ref, narrow_ref):
    walkers, rows, _ = partial_ref.shape
    order = vector_ref.shape[1]
    z, k, x = place(chips)
    sources = [
        (1, k, of_pair(above, x), of_pair(above, 1 - x)),
        (-1, k, of_pair(below, x), of_pair(below, 1 - x)),
    ]

    def body(picked):
        tiles = block_operators(z, x, chips, walkers, field_ref, sources, picked)
        row, column = picked
        for w in range(walkers):
            operator_ref[w, row, column] = tiles[0][w]
            operator_ref[w, pl.ds(rows + row.start, row.size), column] = tiles[1][w]

    over_tiles(rows, order, body)
    for w in range(walkers):
        both = jnp.dot(operator_ref[w], vector_ref[w], preferred_element_type=wide)
        term = partial_ref[w] + (both[:rows] + both[rows:])
        first_ref[w] = term
        narrow_ref[w] = term.astype(narrow)


def first_application(chips, field, above, below, vector, partial):
    walkers, rows, occupied = partial.shape
    order = vector.shape[1]
    return pl.pallas_call(
        functools.partial(first_kernel, chips),
        out_shape=[
            jax.ShapeDtypeStruct((walkers, 2 * rows, order), narrow),
            jax.ShapeDtypeStruct((walkers, rows, occupied), wide),
            jax.ShapeDtypeStruct((walkers, rows, occupied), narrow),
        ],
        in_specs=[vmem_spec] * 5,
        out_specs=[vmem_spec] * 3,
        compiler_params=small,
        name="first_application",
    )(field, above, below, vector, partial)


def applied(chips, step, z, operators, vector, rows, w):
    chip_rows = 2 * rows
    start = pl.multiple_of(lax.rem(z + step + chips, chips) * chip_rows, chip_rows)
    total = None
    for operator_ref in operators:
        both = jnp.dot(
            operator_ref[w, :, pl.ds(start, chip_rows)], vector, preferred_element_type=wide
        )
        part = both[:rows] + both[rows:]
        total = part if total is None else total + part
    return total


def near_kernel(chips, early_ref, late_ref, first_ref, orbitals_ref, *refs):
    here, above, below, here_t, above_t, below_t, out_ref, vector_ref = refs
    walkers, rows, _ = first_ref.shape
    z, _, _ = place(chips)
    for index, (mine, theirs) in enumerate(((here, here_t), (above, above_t), (below, below_t))):
        pieces = [(0, False, 0, mine), (0, True, 0, theirs)]
        collect(chips, vector_ref.at[index], pieces, absolute=False)
    for w in range(walkers):
        second = None
        for index, step in enumerate((0, 1, -1)):
            part = applied(chips, step, z, (early_ref, late_ref), vector_ref[index, w], rows, w)
            second = part if second is None else second + part
        out_ref[w] = orbitals_ref[0, :, w, :] + first_ref[w] + 0.5 * second


def near_application(chips, early, late, first_term, orbitals, pieces):
    walkers, rows, occupied = first_term.shape
    return pl.pallas_call(
        functools.partial(near_kernel, chips),
        out_shape=jax.ShapeDtypeStruct(first_term.shape, wide),
        in_specs=[vmem_spec] * 10,
        out_specs=vmem_spec,
        scratch_shapes=[pltpu.VMEM((3, walkers, 2 * rows, occupied), narrow)],
        compiler_params=small,
        name="near_application",
    )(early, late, first_term, orbitals, *pieces)


def far_kernel(chips, early_ref, late_ref, base_ref, low, high, low_t, high_t, out_ref, vector_ref):
    walkers, rows, _ = base_ref.shape
    z, _, _ = place(chips)
    half = low.shape[0]
    pieces = [(0, False, 0, low), (0, False, half, high), (0, True, 0, low_t), (0, True, half, high_t)]
    collect(chips, vector_ref, pieces, absolute=False)
    for w in range(walkers):
        second = applied(chips, 2, z, (early_ref, late_ref), vector_ref[w], rows, w)
        out_ref[0, :, w, :] = base_ref[w] + 0.5 * second


def far_application(chips, early, late, base, pieces):
    walkers, rows, occupied = base.shape
    return pl.pallas_call(
        functools.partial(far_kernel, chips),
        out_shape=jax.ShapeDtypeStruct((1, rows, walkers, occupied), wide),
        in_specs=[vmem_spec] * 7,
        out_specs=vmem_spec,
        scratch_shapes=[pltpu.VMEM((walkers, 2 * rows, occupied), narrow)],
        compiler_params=small,
        name="far_application",
    )(early, late, base, *pieces)


def row_device(chips):
    devices = 2 * chips

    def ring(value, step):
        pairs = [(i, (i + 2 * step) % devices) for i in range(devices)]
        return lax.ppermute(value, "chol", pairs)

    def core(value):
        return lax.ppermute(value, "chol", [(i, i ^ 1) for i in range(devices)])

    def across(value):
        return lax.ppermute(value, "walk", [(0, 1), (1, 0)])

    def gather_ring(value):
        half = value.shape[0] // 2
        below, above = ring(value, 1), ring(value, -1)
        low, high = ring(below[:half], 1), ring(above[half:], -1)
        return [value, above, low, high, below]

    def device(green_blocks, half_chol, full_chol, meanfield, noise_draws, orbitals):
        walkers, rows, _ = green_blocks.shape
        vectors = half_chol.shape[0]
        slot = lax.axis_index("chol")

        half_theirs = core(half_chol)
        green_pieces = gather_ring(green_blocks)
        far_up, far_down = cut(chips, rows, full_chol, ((2, False, False), (2, True, False)))
        far_half, far_half_cross = ring(far_up, 1), ring(far_down, -1)
        cross_up, cross_down, own_cross = cut(
            chips,
            rows,
            after(full_chol, far_up),
            ((1, True, True), (-1, True, True), (0, True, True)),
        )
        cross_below, cross_above = ring(cross_up, 1), ring(cross_down, -1)
        own_theirs = core(own_cross)
        straight_up, straight_down = cut(
            chips, rows, after(full_chol, cross_up), ((1, False, True), (-1, False, True))
        )
        far, far_cross = ring(far_half, 1), ring(far_half_cross, -1)
        straight_up, straight_down = after((straight_up, straight_down), far_half, far_half_cross)
        below, above = ring(straight_up, 1), ring(straight_down, -1)
        start = after(walker_major(orbitals), far, far_cross)
        start_pieces = gather_ring(start)

        far_theirs = core(far_cross)
        far_x, far_theirs_x = across(far), across(far_theirs)

        bias = chip_bias(chips, *green_pieces, half_chol, half_theirs)
        constants = jnp.concatenate([noise_draws.T.reshape(-1), jnp.repeat(meanfield, walkers)])
        constants = jnp.broadcast_to(constants[:, None], bias.shape)
        gathered = lax.all_gather(jnp.concatenate([bias, constants]), "chol")
        shift_rows, field = all_fields(gathered)
        bias_shift = shift_rows[:, 0].reshape(vectors, walkers).T

        own = lax.dynamic_slice_in_dim(full_chol, slot * rows, rows, 1)
        summed = early_operator(
            chips,
            walkers,
            field,
            own,
            own_theirs,
            (far, far_x, far_theirs, far_theirs_x),
        )
        early, vector, partial = middle_operator(
            chips,
            summed,
            field,
            core(cross_above),
            core(cross_below),
            [*start_pieces, *[core(piece) for piece in start_pieces]],
        )
        late, first_term, first_narrow = first_application(
            chips, field, above, below, vector, partial
        )
        here, above, low, high, below = gather_ring(first_narrow)
        base = near_application(
            chips,
            early,
            late,
            first_term,
            orbitals,
            [here, above, below, core(here), core(above), core(below)],
        )
        walkers_next = far_application(
            chips, early, late, base, [low, high, core(low), core(high)]
        )
        return (walkers_next, bias_shift)

    return device


def solution(mesh):
    placed = (
        P(("grp", "walk"), "chol", "orb"),
        P(("grp", "chol"), None, "orb"),
        P(("grp", "chol"), "orb", None),
        P(("grp", "chol")),
        P(("grp", "walk"), "chol"),
        P("orb", "chol", ("grp", "walk"), None),
    )
    sizes = mesh.shape
    if sizes["orb"] == 1 and sizes["walk"] == 2 and sizes["chol"] == 8:
        per_device = row_device(sizes["chol"] // 2)
    else:
        per_device = general_device
    return jax.shard_map(
        per_device,
        mesh=mesh,
        in_specs=placed,
        out_specs=(P("orb", "chol", ("grp", "walk"), None), P(("grp", "walk"), "chol")),
        check_vma=False,
    )
```

time: 152 us -> 180 us (1.18)
  blocking collectives: 0 us -> 25.6 us
  local copies, waits for them, and re-layouts: 6.63 us -> 15.4 us
  starting transfers between devices: 50.6 us -> 43.9 us
  waiting for transfers between devices: 70.3 us -> 76.5 us
  Pallas kernels: 22.7 us -> 16.7 us
    all_gather x0 -> x1, blocking collectives: none -> 25.6 us  [device(): gathered = lax.all_gather(jnp.concatenate([bias, constants]), 'chol')]
    ppermute x23 -> x20, waiting for transfers between devices: 68.5 us -> 76.5 us  [ring(): return lax.ppermute(value, 'chol', pairs)]
    unnamed x38 -> x72, local copies, waits for them, and re-layouts: 4.42 us -> 12.3 us
    ppermute x6 -> x2, starting transfers between devices: 7.75 us -> 3.04 us  [across(): return lax.ppermute(value, 'walk', [(0, 1), (1, 0)])]
    pallas_call x2 -> x3, Pallas kernels: 4.46 us -> 1.27 us  [cut(): pl.pallas_call(functools.partial(cut_kernel, chips, rows, wanted), out_sh...]
    pallas_call x1, Pallas kernels: 3.48 us -> 1 us  [chip_bias(): pl.pallas_call(functools.partial(bias_kernel, chips), out_shape=jax.Shape...]
    pallas_call x3 -> x5, Pallas kernels: 9.18 us -> 11.6 us  [the longest x1 3.83 us: middle_operator(): pl.pallas_call(functools.partial(middle_kernel, chips), out_shape=[jax.Sh...]
    ppermute x23 -> x20, starting transfers between devices: 41.2 us -> 39.2 us  [ring(): return lax.ppermute(value, 'chol', pairs)]
  transfers between devices with their start and end apart: 46 -> 37, of which waited for: 21 -> 15; matrix products, arithmetic and copies ran while one was open for 2% -> 2% of each run, Pallas kernels for 9% -> 6%
where the time goes in v3:
time: 180 us; the launch traced here: 179 us
  waiting for transfers between devices  76.5 us (42%)
  starting transfers between devices  43.9 us (24%)
  blocking collectives  25.6 us (14%)
  Pallas kernels  16.7 us (9%)
  local copies, waits for them, and re-layouts  15.4 us (9%)
    ppermute x20, waiting for transfers between devices, ring(): return lax.ppermute(value, 'chol', pairs)  76.5 us
    ppermute x20, starting transfers between devices, ring(): return lax.ppermute(value, 'chol', pairs)  39.2 us
    all_gather x1, blocking collectives, device(): gathered = lax.all_gather(jnp.concatenate([bias, constants]), 'chol')  25.6 us
    unnamed x72, local copies, waits for them, and re-layouts  12.3 us
    pallas_call x1, Pallas kernels, middle_operator(): pl.pallas_call(functools.partial(middle_kernel, chips), out_shape=[jax.Sh...  3.83 us
  transfers between devices with their start and end apart: 37, of which 15 were waited for; matrix products, arithmetic and copies ran while one was open for 2% of the time, Pallas kernels for 6%

profile of v3, /device:TPU:0, one launch (start us, length us, event | category | flops | bytes accessed | tf_op | source)
XLA Modules:
  0.0 179.5 jit_solution(16743290931648004836)
XLA Ops:
  0.6 2.2 %copy-done = bf16[2,1024,1024]{2,1,0:T(8,128)(2,1)S(1)} copy-done((bf16[2,1024,1024]{2,1,0:T(8,128)(2,1)S(1)}, bf16[2,1024,1024]{2,1,0:T(8,128)(2,1)}, u32[]{:S(2)}) %copy-start) | copy-done | bytes 4194328
  2.9 5.1 %collective-permute-start.9 = (bf16[128,1024]{1,0:T(8,128)(2,1)S(1)}, bf16[128,1024]{1,0:T(8,128)(2,1)S(1)}, u32[]{:S(2)}, u32[]{:S(2)}) collective-permute-start(bf16[128,1024]{1,0:T(8,128)(2,1)S(1)} %get-tuple-element.26), channel_id=1, source_target_pairs={{0,12},{2,14},{4,0},{6,2},{8,4},{10,6},{12,8},{14,10},{1,13},{3,15... | collective-permute-start | bytes 786440 | tf_op jit(solution)/shard_map/ppermute | solution.py:464
  8.0 0.8 collective-permute-start
  8.8 1.2 collective-permute-start.1
  10.1 4.7 %collective-permute-done.9 = bf16[128,1024]{1,0:T(8,128)(2,1)S(1)} collective-permute-done((bf16[128,1024]{1,0:T(8,128)(2,1)S(1)}, bf16[128,1024]{1,0:T(8,128)(2,1)S(1)}, u32[]{:S(2)}, u32[]{:S(2)}) %collective-permute-start.9) | collective-permute-done | bytes 262176 | tf_op jit(solution)/shard_map/ppermute | solution.py:464
  14.7 4.4 %collective-permute-start.10 = (bf16[128,1024]{1,0:T(8,128)(2,1)S(1)}, bf16[128,1024]{1,0:T(8,128)(2,1)S(1)}, u32[]{:S(2)}, u32[]{:S(2)}) collective-permute-start(bf16[128,1024]{1,0:T(8,128)(2,1)S(1)} %collective-permute-done.9), channel_id=1, source_target_pairs={{0,12},{2,14},{4,0},{6,2},{8,4},{10,6},{12,8},{14,10},{1,13},{3,15... | collective-permute-start | bytes 786440 | tf_op jit(solution)/shard_map/ppermute | solution.py:464
  19.1 1.2 collective-permute-done.above_ref
  20.4 4.3 %collective-permute-start.3 = (bf16[2,128,256]{2,1,0:T(8,128)(2,1)S(1)}, bf16[2,128,256]{2,1,0:T(8,128)(2,1)S(1)}, u32[]{:S(2)}, u32[]{:S(2)}) collective-permute-start(bf16[2,128,256]{2,1,0:T(8,128)(2,1)S(1)} %slice.29), channel_id=1, source_target_pairs={{0,12},{2,14},{4,0},{6,2},{8,4},{10,6},{12,8},{14,10},{1,13},{3,15... | collective-permute-start | bytes 393224 | tf_op jit(solution)/shard_map/ppermute | solution.py:464
  25.0 2.0 %collective-permute-done.1.below_ref = bf16[4,128,256]{2,1,0:T(8,128)(2,1)S(1)} collective-permute-done((bf16[4,128,256]{2,1,0:T(8,128)(2,1)S(1)}, bf16[4,128,256]{2,1,0:T(8,128)(2,1)S(1)}, u32[]{:S(2)}, u32[]{:S(2)}) %collective-permute-start.1) | collective-permute-done | bytes 262176 | tf_op jit(solution)/shard_map/ppermute | solution.py:464
  27.0 2.2 %collective-permute-start.13 = (bf16[2,128,1024]{2,1,0:T(8,128)(2,1)S(1)}, bf16[2,128,1024]{2,1,0:T(8,128)(2,1)}, u32[]{:S(2)}, u32[]{:S(2)}) collective-permute-start(bf16[2,128,1024]{2,1,0:T(8,128)(2,1)S(1)} %get-tuple-element.27), channel_id=1, source_target_pairs={{0,12},{2,14},{4,0},{6,2},{8,4},{10,6},{12,8},{14,10},{1,13},{3,15... | collective-permute-start | bytes 1572872 | tf_op jit(solution)/shard_map/ppermute | solution.py:464
  29.2 3.3 %collective-permute-done.6 = bf16[128,1024]{1,0:T(8,128)(2,1)S(1)} collective-permute-done((bf16[128,1024]{1,0:T(8,128)(2,1)S(1)}, bf16[128,1024]{1,0:T(8,128)(2,1)S(1)}, u32[]{:S(2)}, u32[]{:S(2)}) %collective-permute-start.6) | collective-permute-done | bytes 262176 | tf_op jit(solution)/shard_map/ppermute | solution.py:464
  32.5 1.6 collective-permute-start.15
  34.1 6.0 %collective-permute-done.3.high_ref = bf16[2,128,256]{2,1,0:T(8,128)(2,1)S(1)} collective-permute-done((bf16[2,128,256]{2,1,0:T(8,128)(2,1)S(1)}, bf16[2,128,256]{2,1,0:T(8,128)(2,1)S(1)}, u32[]{:S(2)}, u32[]{:S(2)}) %collective-permute-start.3) | collective-permute-done | bytes 131104 | tf_op jit(solution)/shard_map/ppermute | solution.py:464
  40.5 27.4 %collective-permute-done.7.far = bf16[128,1024]{1,0:T(8,128)(2,1)S(1)} collective-permute-done((bf16[128,1024]{1,0:T(8,128)(2,1)S(1)}, bf16[128,1024]{1,0:T(8,128)(2,1)S(1)}, u32[]{:S(2)}, u32[]{:S(2)}) %collective-permute-start.7) | collective-permute-done | bytes 262176 | tf_op jit(solution)/shard_map/ppermute | solution.py:464
  67.9 1.6 collective-permute-start.2
  70.0 4.9 %collective-permute-done.2.low_ref = bf16[2,128,256]{2,1,0:T(8,128)(2,1)S(1)} collective-permute-done((bf16[2,128,256]{2,1,0:T(8,128)(2,1)S(1)}, bf16[2,128,256]{2,1,0:T(8,128)(2,1)S(1)}, u32[]{:S(2)}, u32[]{:S(2)}) %collective-permute-start.2) | collective-permute-done | bytes 131104 | tf_op jit(solution)/shard_map/ppermute | solution.py:464
  76.4 3.8 %collective-permute-start.17 = (bf16[4,128,256]{2,1,0:T(8,128)(2,1)S(1)}, bf16[4,128,256]{2,1,0:T(8,128)(2,1)S(1)}, u32[]{:S(2)}, u32[]{:S(2)}) collective-permute-start(bf16[4,128,256]{2,1,0:T(8,128)(2,1)S(1)} %walker_major.1.refs_0_), channel_id=1, source_target_pairs={{0,12},{2,14},{4,0},{6,2},{8,4},{10,6},{12,8},{14,10},{1,13},{3,15... | collective-permute-start | bytes 786440 | tf_op jit(solution)/shard_map/ppermute | solution.py:464
  80.7 6.0 %collective-permute-done.18.refs_4_ = bf16[4,128,256]{2,1,0:T(8,128)(2,1)} collective-permute-done((bf16[4,128,256]{2,1,0:T(8,128)(2,1)S(1)}, bf16[4,128,256]{2,1,0:T(8,128)(2,1)}, u32[]{:S(2)}, u32[]{:S(2)}) %collective-permute-start.18) | collective-permute-done | bytes 262176 | tf_op jit(solution)/shard_map/ppermute | solution.py:464
  86.8 1.5 collective-permute-start.8
  88.2 0.9 slice.30
  89.2 1.3 collective-permute-start.19
  90.6 2.6 %collective-permute-start.20 = (bf16[2,128,256]{2,1,0:T(8,128)(2,1)S(1)}, bf16[2,128,256]{2,1,0:T(8,128)(2,1)S(1)}, u32[]{:S(2)}, u32[]{:S(2)}) collective-permute-start(bf16[2,128,256]{2,1,0:T(8,128)(2,1)S(1)} %slice.31), channel_id=1, source_target_pairs={{0,12},{2,14},{4,0},{6,2},{8,4},{10,6},{12,8},{14,10},{1,13},{3,15... | collective-permute-start | bytes 393224 | tf_op jit(solution)/shard_map/ppermute | solution.py:464
  93.2 1.6 collective-permute-start.12
  94.7 2.2 %collective-permute-done.19.refs_2_ = bf16[2,128,256]{2,1,0:T(8,128)(2,1)S(1)} collective-permute-done((bf16[2,128,256]{2,1,0:T(8,128)(2,1)S(1)}, bf16[2,128,256]{2,1,0:T(8,128)(2,1)S(1)}, u32[]{:S(2)}, u32[]{:S(2)}) %collective-permute-start.19) | collective-permute-done | bytes 131104 | tf_op jit(solution)/shard_map/ppermute | solution.py:464
  96.9 1.3 collective-permute-done.20.refs_3_
  98.7 1.1 cut_rows.5
  100.5 2.0 %collective-permute-start.26 = (bf16[2,128,1024]{2,1,0:T(8,128)(2,1)}, bf16[2,128,1024]{2,1,0:T(8,128)(2,1)}, u32[]{:S(2)}, u32[]{:S(2)}) collective-permute-start(bf16[2,128,1024]{2,1,0:T(8,128)(2,1)} %get-tuple-element.34), channel_id=1, source_target_pairs={{0,12},{2,14},{4,0},{6,2},{8,4},{10,6},{12,8},{14,10},{1,13},{3,15... | collective-permute-start | bytes 1572872 | tf_op jit(solution)/shard_map/ppermute | solution.py:464
  104.8 1.2 constant_dynamic-slice_fusion.own
  105.9 0.9 copy-done.13
  106.9 0.9 copy-done.25
  107.8 1.0 chip_bias.1
  109.0 25.6 %all-gather = f32[256,128]{1,0:T(8,128)S(1)} all-gather(f32[32,128]{1,0:T(8,128)S(1)} %pad_maximum_fusion), channel_id=2, replica_groups=mesh['grp'=2,'chol'=8,'walk'=2,'orb'=1] {'chol'}, dimensions={0}, use_global_device_ids=true | all-gather | bytes 147456 | tf_op jit(solution)/shard_map/all_gather | solution.py:510
  134.7 2.3 %early_operator.1.summed_ref = f32[4,128,1024]{2,1,0:T(8,128)S(1)} custom-call(f32[64,128]{1,0:T(8,128)S(1)} %get-tuple-element.22.field_ref, bf16[2,128,1024]{2,1,0:T(8,128)(2,1)S(1)} %constant_dynamic-slice_fusion.own, bf16[2,128,1024]{2,1,0:T(8,128)(2,1)S(1)} %copy-done.11, bf16[128,1024]{1,0:T(8,128)(2,1)S(1)} %copy-done.15, ...), custom_call_target="tpu_custom_call" | custom-call | tf_op jit(solution)/shard_map/early_operator/pallas_call | solution.py:270
  137.2 3.8 %middle_operator.1 = (bf16[4,256,1024]{2,1,0:T(8,128)(2,1)S(1)}, bf16[4,1024,256]{2,1,0:T(8,128)(2,1)S(1)}, f32[4,128,256]{2,1,0:T(8,128)S(1)}) custom-call(f32[4,128,1024]{2,1,0:T(8,128)S(1)} %early_operator.1.summed_ref, f32[64,128]{1,0:T(8,128)S(1)} %get-tuple-element.22.field_ref, bf16[2,128,1024]{2,1,0:T(8,128)(2,1)} %collective-permute-done.14.above_theirs, ...), custom_call_target="tpu_custom_call" | custom-call | tf_op jit(solution)/shard_map/middle_operator/pallas_call | solution.py:339
  141.0 3.0 %first_application.1 = (bf16[4,256,1024]{2,1,0:T(8,128)(2,1)S(1)}, f32[4,128,256]{2,1,0:T(8,128)S(1)}, bf16[4,128,256]{2,1,0:T(8,128)(2,1)S(1)}) custom-call(f32[64,128]{1,0:T(8,128)S(1)} %get-tuple-element.22.field_ref, bf16[2,128,1024]{2,1,0:T(8,128)(2,1)} %collective-permute-done.26.above, bf16[2,128,1024]{2,1,0:T(8,128)(2,1)} %collective-permute-done.27.below, ...), custom_call_target="tpu_custom_call" | custom-call | tf_op jit(solution)/shard_map/first_application/pallas_call | solution.py:380
  144.1 1.3 copy-done.2
  146.2 1.5 collective-permute-start.29
  147.6 2.4 %collective-permute-start.28 = (bf16[4,128,256]{2,1,0:T(8,128)(2,1)S(1)}, bf16[4,128,256]{2,1,0:T(8,128)(2,1)S(1)}, u32[]{:S(2)}, u32[]{:S(2)}) collective-permute-start(bf16[4,128,256]{2,1,0:T(8,128)(2,1)S(1)} %get-tuple-element.40.refs_0_), channel_id=1, source_target_pairs={{0,12},{2,14},{4,0},{6,2},{8,4},{10,6},{12,8},{14,10},{1,13},{3,15... | collective-permute-start | bytes 786440 | tf_op jit(solution)/shard_map/ppermute | solution.py:464
  150.0 7.1 %collective-permute-done.29.refs_2_ = bf16[4,128,256]{2,1,0:T(8,128)(2,1)S(1)} collective-permute-done((bf16[4,128,256]{2,1,0:T(8,128)(2,1)S(1)}, bf16[4,128,256]{2,1,0:T(8,128)(2,1)S(1)}, u32[]{:S(2)}, u32[]{:S(2)}) %collective-permute-start.29) | collective-permute-done | bytes 262176 | tf_op jit(solution)/shard_map/ppermute | solution.py:464
  157.1 4.4 %collective-permute-done.28.refs_1_ = bf16[4,128,256]{2,1,0:T(8,128)(2,1)S(1)} collective-permute-done((bf16[4,128,256]{2,1,0:T(8,128)(2,1)S(1)}, bf16[4,128,256]{2,1,0:T(8,128)(2,1)S(1)}, u32[]{:S(2)}, u32[]{:S(2)}) %collective-permute-start.28) | collective-permute-done | bytes 262176 | tf_op jit(solution)/shard_map/ppermute | solution.py:464
  161.5 1.3 collective-permute-start.33
  162.8 2.6 %collective-permute-start.34 = (bf16[2,128,256]{2,1,0:T(8,128)(2,1)S(1)}, bf16[2,128,256]{2,1,0:T(8,128)(2,1)}, u32[]{:S(2)}, u32[]{:S(2)}) collective-permute-start(bf16[2,128,256]{2,1,0:T(8,128)(2,1)S(1)} %slice.33), channel_id=1, source_target_pairs={{0,12},{2,14},{4,0},{6,2},{8,4},{10,6},{12,8},{14,10},{1,13},{3,15... | collective-permute-start | bytes 393224 | tf_op jit(solution)/shard_map/ppermute | solution.py:464
  165.5 4.2 %collective-permute-done.33.low = bf16[2,128,256]{2,1,0:T(8,128)(2,1)S(1)} collective-permute-done((bf16[2,128,256]{2,1,0:T(8,128)(2,1)S(1)}, bf16[2,128,256]{2,1,0:T(8,128)(2,1)S(1)}, u32[]{:S(2)}, u32[]{:S(2)}) %collective-permute-start.33) | collective-permute-done | bytes 131104 | tf_op jit(solution)/shard_map/ppermute | solution.py:464
  169.7 1.6 collective-permute-done.34.high
  172.1 1.6 copy-done.3
  173.7 1.0 copy-done.9
  174.8 2.2 %near_application.1.base_ref = f32[4,128,256]{2,1,0:T(8,128)S(1)} custom-call(bf16[4,256,1024]{2,1,0:T(8,128)(2,1)S(1)} %get-tuple-element.30.early_ref, bf16[4,256,1024]{2,1,0:T(8,128)(2,1)S(1)} %copy-done.3, f32[4,128,256]{2,1,0:T(8,128)S(1)} %copy-done.9, f32[1,128,4,256]{3,2,1,0:T(4,128)S(1)} %copy-done.4, ...), custom_call_target="tpu_custom_call" | custom-call | tf_op jit(solution)/shard_map/near_application/pallas_call | solution.py:424
  177.0 2.4 %far_application.1 = f32[1,128,4,256]{3,2,1,0:T(4,128)} custom-call(bf16[4,256,1024]{2,1,0:T(8,128)(2,1)S(1)} %get-tuple-element.30.early_ref, bf16[4,256,1024]{2,1,0:T(8,128)(2,1)S(1)} %copy-done.3, f32[4,128,256]{2,1,0:T(8,128)S(1)} %near_application.1.base_ref, bf16[2,128,256]{2,1,0:T(8,128)(2,1)S(1)} %collective-permute-done.33.low, ...), custom_call_target="tpu_custom_call" | custom-call | tf_op jit(solution)/shard_map/far_application/pallas_call | solution.py:448
  (124 shorter events, 8.6 us)
Async XLA Ops:
  2.9 11.9 %collective-permute-start.9 = (bf16[128,1024]{1,0:T(8,128)(2,1)S(1)}, bf16[128,1024]{1,0:T(8,128)(2,1)S(1)}, u32[]{:S(2)}, u32[]{:S(2)}) collective-permute-start(bf16[128,1024]{1,0:T(8,128)(2,1)S(1)} %get-tuple-element.26), channel_id=1, source_target_pairs={{0,12},{2,14},{4,0},{6,2},{8,4},{10,6},{12,8},{14,10},{1,13},{3,15... | collective-permute-start | bytes 786440 | tf_op jit(solution)/shard_map/ppermute | solution.py:464
  8.0 12.4 %collective-permute-start = (bf16[4,128,256]{2,1,0:T(8,128)(2,1)S(1)}, bf16[4,128,256]{2,1,0:T(8,128)(2,1)S(1)}, u32[]{:S(2)}, u32[]{:S(2)}) collective-permute-start(bf16[4,128,256]{2,1,0:T(8,128)(2,1)S(1)} %copy-done.12), channel_id=1, source_target_pairs={{0,12},{2,14},{4,0},{6,2},{8,4},{10,6},{12,8},{14,10},{1,13},{3,15... | collective-permute-start | bytes 786440 | tf_op jit(solution)/shard_map/ppermute | solution.py:464
  8.8 18.2 %collective-permute-start.1 = (bf16[4,128,256]{2,1,0:T(8,128)(2,1)S(1)}, bf16[4,128,256]{2,1,0:T(8,128)(2,1)S(1)}, u32[]{:S(2)}, u32[]{:S(2)}) collective-permute-start(bf16[4,128,256]{2,1,0:T(8,128)(2,1)S(1)} %copy-done.12), channel_id=1, source_target_pairs={{0,4},{2,6},{4,8},{6,10},{8,12},{10,14},{12,0},{14,2},{1,5},{3,7},... | collective-permute-start | bytes 786440 | tf_op jit(solution)/shard_map/ppermute | solution.py:464
  10.0 22.5 %collective-permute-start.6 = (bf16[128,1024]{1,0:T(8,128)(2,1)S(1)}, bf16[128,1024]{1,0:T(8,128)(2,1)S(1)}, u32[]{:S(2)}, u32[]{:S(2)}) collective-permute-start(bf16[128,1024]{1,0:T(8,128)(2,1)S(1)} %get-tuple-element.23), channel_id=1, source_target_pairs={{0,4},{2,6},{4,8},{6,10},{8,12},{10,14},{12,0},{14,2},{1,5},{3,7},... | collective-permute-start | bytes 786440 | tf_op jit(solution)/shard_map/ppermute | solution.py:464
  14.7 25.3 %collective-permute-start.10 = (bf16[128,1024]{1,0:T(8,128)(2,1)S(1)}, bf16[128,1024]{1,0:T(8,128)(2,1)S(1)}, u32[]{:S(2)}, u32[]{:S(2)}) collective-permute-start(bf16[128,1024]{1,0:T(8,128)(2,1)S(1)} %collective-permute-done.9), channel_id=1, source_target_pairs={{0,12},{2,14},{4,0},{6,2},{8,4},{10,6},{12,8},{14,10},{1,13},{3,15... | collective-permute-start | bytes 786440 | tf_op jit(solution)/shard_map/ppermute | solution.py:464
  20.4 19.7 %copy-start.5 = (bf16[2,1024,256]{2,1,0:T(8,128)(2,1)S(1)}, bf16[2,1024,256]{2,1,0:T(8,128)(2,1)}, u32[]{:S(2)}) copy-start(bf16[2,1024,256]{2,1,0:T(8,128)(2,1)} %mine_ref.1) | copy-start | bytes 3145732
  20.4 49.1 %copy-start.4 = (f32[1,128,4,256]{3,2,1,0:T(4,128)S(1)}, f32[1,128,4,256]{3,2,1,0:T(4,128)}, u32[]{:S(2)}) copy-start(f32[1,128,4,256]{3,2,1,0:T(4,128)} %orbitals_ref.3) | copy-start | bytes 1572868
  20.4 78.3 %copy-start.1 = (bf16[2,1024,1024]{2,1,0:T(8,128)(2,1)S(1)}, bf16[2,1024,1024]{2,1,0:T(8,128)(2,1)}, u32[]{:S(2)}) copy-start(bf16[2,1024,1024]{2,1,0:T(8,128)(2,1)} %full_ref.3) | copy-start | bytes 12582916
  20.4 19.7 %collective-permute-start.3 = (bf16[2,128,256]{2,1,0:T(8,128)(2,1)S(1)}, bf16[2,128,256]{2,1,0:T(8,128)(2,1)S(1)}, u32[]{:S(2)}, u32[]{:S(2)}) collective-permute-start(bf16[2,128,256]{2,1,0:T(8,128)(2,1)S(1)} %slice.29), channel_id=1, source_target_pairs={{0,12},{2,14},{4,0},{6,2},{8,4},{10,6},{12,8},{14,10},{1,13},{3,15... | collective-permute-start | bytes 393224 | tf_op jit(solution)/shard_map/ppermute | solution.py:464
  24.9 50.7 %collective-permute-start.5 = (bf16[2,128,1024]{2,1,0:T(8,128)(2,1)S(1)}, bf16[2,128,1024]{2,1,0:T(8,128)(2,1)S(1)}, u32[]{:S(2)}, u32[]{:S(2)}) collective-permute-start(bf16[2,128,1024]{2,1,0:T(8,128)(2,1)S(1)} %get-tuple-element.25), channel_id=1, source_target_pairs={{0,2},{2,0},{4,6},{6,4},{8,10},{10,8},{12,14},{14,12},{1,3},{3,1},... | collective-permute-start | bytes 1572872 | tf_op jit(solution)/shard_map/ppermute | solution.py:467
  27.0 53.2 %collective-permute-start.13 = (bf16[2,128,1024]{2,1,0:T(8,128)(2,1)S(1)}, bf16[2,128,1024]{2,1,0:T(8,128)(2,1)}, u32[]{:S(2)}, u32[]{:S(2)}) collective-permute-start(bf16[2,128,1024]{2,1,0:T(8,128)(2,1)S(1)} %get-tuple-element.27), channel_id=1, source_target_pairs={{0,12},{2,14},{4,0},{6,2},{8,4},{10,6},{12,8},{14,10},{1,13},{3,15... | collective-permute-start | bytes 1572872 | tf_op jit(solution)/shard_map/ppermute | solution.py:464
  32.5 47.7 %collective-permute-start.15 = (bf16[2,128,1024]{2,1,0:T(8,128)(2,1)S(1)}, bf16[2,128,1024]{2,1,0:T(8,128)(2,1)}, u32[]{:S(2)}, u32[]{:S(2)}) collective-permute-start(bf16[2,128,1024]{2,1,0:T(8,128)(2,1)S(1)} %get-tuple-element.28), channel_id=1, source_target_pairs={{0,4},{2,6},{4,8},{6,10},{8,12},{10,14},{12,0},{14,2},{1,5},{3,7},... | collective-permute-start | bytes 1572872 | tf_op jit(solution)/shard_map/ppermute | solution.py:464
  40.1 64.3 %collective-permute-start.4 = (bf16[2,1024,256]{2,1,0:T(8,128)(2,1)S(1)}, bf16[2,1024,256]{2,1,0:T(8,128)(2,1)S(1)}, u32[]{:S(2)}, u32[]{:S(2)}) collective-permute-start(bf16[2,1024,256]{2,1,0:T(8,128)(2,1)S(1)} %copy-done.5), channel_id=1, source_target_pairs={{0,2},{2,0},{4,6},{6,4},{8,10},{10,8},{12,14},{14,12},{1,3},{3,1},... | collective-permute-start | bytes 3145736 | tf_op jit(solution)/shard_map/ppermute | solution.py:467
  40.1 27.8 %collective-permute-start.7 = (bf16[128,1024]{1,0:T(8,128)(2,1)S(1)}, bf16[128,1024]{1,0:T(8,128)(2,1)S(1)}, u32[]{:S(2)}, u32[]{:S(2)}) collective-permute-start(bf16[128,1024]{1,0:T(8,128)(2,1)S(1)} %collective-permute-done.6), channel_id=1, source_target_pairs={{0,4},{2,6},{4,8},{6,10},{8,12},{10,14},{12,0},{14,2},{1,5},{3,7},... | collective-permute-start | bytes 786440 | tf_op jit(solution)/shard_map/ppermute | solution.py:464
  67.9 31.9 %copy-start.14 = (bf16[128,1024]{1,0:T(8,128)(2,1)}, bf16[128,1024]{1,0:T(8,128)(2,1)S(1)}, u32[]{:S(2)}) copy-start(bf16[128,1024]{1,0:T(8,128)(2,1)S(1)} %collective-permute-done.7.far) | copy-start | bytes 786436
  67.9 7.1 %collective-permute-start.2 = (bf16[2,128,256]{2,1,0:T(8,128)(2,1)S(1)}, bf16[2,128,256]{2,1,0:T(8,128)(2,1)S(1)}, u32[]{:S(2)}, u32[]{:S(2)}) collective-permute-start(bf16[2,128,256]{2,1,0:T(8,128)(2,1)S(1)} %slice.28), channel_id=1, source_target_pairs={{0,4},{2,6},{4,8},{6,10},{8,12},{10,14},{12,0},{14,2},{1,5},{3,7},... | collective-permute-start | bytes 393224 | tf_op jit(solution)/shard_map/ppermute | solution.py:464
  75.6 11.2 %collective-permute-start.18 = (bf16[4,128,256]{2,1,0:T(8,128)(2,1)S(1)}, bf16[4,128,256]{2,1,0:T(8,128)(2,1)}, u32[]{:S(2)}, u32[]{:S(2)}) collective-permute-start(bf16[4,128,256]{2,1,0:T(8,128)(2,1)S(1)} %walker_major.1.refs_0_), channel_id=1, source_target_pairs={{0,4},{2,6},{4,8},{6,10},{8,12},{10,14},{12,0},{14,2},{1,5},{3,7},... | collective-permute-start | bytes 786440 | tf_op jit(solution)/shard_map/ppermute | solution.py:464
  76.4 12.8 %collective-permute-start.17 = (bf16[4,128,256]{2,1,0:T(8,128)(2,1)S(1)}, bf16[4,128,256]{2,1,0:T(8,128)(2,1)S(1)}, u32[]{:S(2)}, u32[]{:S(2)}) collective-permute-start(bf16[4,128,256]{2,1,0:T(8,128)(2,1)S(1)} %walker_major.1.refs_0_), channel_id=1, source_target_pairs={{0,12},{2,14},{4,0},{6,2},{8,4},{10,6},{12,8},{14,10},{1,13},{3,15... | collective-permute-start | bytes 786440 | tf_op jit(solution)/shard_map/ppermute | solution.py:464
  80.2 10.3 %collective-permute-start.11 = (bf16[128,1024]{1,0:T(8,128)(2,1)S(1)}, bf16[128,1024]{1,0:T(8,128)(2,1)S(1)}, u32[]{:S(2)}, u32[]{:S(2)}) collective-permute-start(bf16[128,1024]{1,0:T(8,128)(2,1)S(1)} %collective-permute-done.10), channel_id=1, source_target_pairs={{0,2},{2,0},{4,6},{6,4},{8,10},{10,8},{12,14},{14,12},{1,3},{3,1},... | collective-permute-start | bytes 786440 | tf_op jit(solution)/shard_map/ppermute | solution.py:467
  80.2 12.9 %collective-permute-start.21 = (bf16[4,128,256]{2,1,0:T(8,128)(2,1)S(1)}, bf16[4,128,256]{2,1,0:T(8,128)(2,1)S(1)}, u32[]{:S(2)}, u32[]{:S(2)}) collective-permute-start(bf16[4,128,256]{2,1,0:T(8,128)(2,1)S(1)} %walker_major.1.refs_0_), channel_id=1, source_target_pairs={{0,2},{2,0},{4,6},{6,4},{8,10},{10,8},{12,14},{14,12},{1,3},{3,1},... | collective-permute-start | bytes 786440 | tf_op jit(solution)/shard_map/ppermute | solution.py:467
  86.8 11.5 %collective-permute-start.8 = (bf16[128,1024]{1,0:T(8,128)(2,1)S(1)}, bf16[128,1024]{1,0:T(8,128)(2,1)S(1)}, u32[]{:S(2)}, u32[]{:S(2)}) collective-permute-start(bf16[128,1024]{1,0:T(8,128)(2,1)S(1)} %collective-permute-done.7.far), channel_id=1, source_target_pairs={{0,1},{1,0},{2,3},{3,2},{4,5},{5,4},{6,7},{7,6},{8,9},{9,8},{10,11... | collective-permute-start | bytes 786440 | tf_op jit(solution)/shard_map/ppermute | solution.py:470
  89.2 7.7 %collective-permute-start.19 = (bf16[2,128,256]{2,1,0:T(8,128)(2,1)S(1)}, bf16[2,128,256]{2,1,0:T(8,128)(2,1)S(1)}, u32[]{:S(2)}, u32[]{:S(2)}) collective-permute-start(bf16[2,128,256]{2,1,0:T(8,128)(2,1)S(1)} %slice.30), channel_id=1, source_target_pairs={{0,4},{2,6},{4,8},{6,10},{8,12},{10,14},{12,0},{14,2},{1,5},{3,7},... | collective-permute-start | bytes 393224 | tf_op jit(solution)/shard_map/ppermute | solution.py:464
  90.5 13.9 %copy-start.34 = (f32[4,2]{0,1:T(2,128)S(1)}, f32[4,2]{0,1:T(2,128)}, u32[]{:S(2)}) copy-start(f32[4,2]{0,1:T(2,128)} %param.10) | copy-start | bytes 100
  90.5 14.0 %copy-start.35 = (f32[2]{0:T(128)S(1)}, f32[2]{0:T(128)}, u32[]{:S(2)}) copy-start(f32[2]{0:T(128)} %param.9) | copy-start | bytes 28
  90.6 7.6 %collective-permute-start.20 = (bf16[2,128,256]{2,1,0:T(8,128)(2,1)S(1)}, bf16[2,128,256]{2,1,0:T(8,128)(2,1)S(1)}, u32[]{:S(2)}, u32[]{:S(2)}) collective-permute-start(bf16[2,128,256]{2,1,0:T(8,128)(2,1)S(1)} %slice.31), channel_id=1, source_target_pairs={{0,12},{2,14},{4,0},{6,2},{8,4},{10,6},{12,8},{14,10},{1,13},{3,15... | collective-permute-start | bytes 393224 | tf_op jit(solution)/shard_map/ppermute | solution.py:464
  93.2 10.0 %collective-permute-start.12 = (bf16[128,1024]{1,0:T(8,128)(2,1)S(1)}, bf16[128,1024]{1,0:T(8,128)(2,1)S(1)}, u32[]{:S(2)}, u32[]{:S(2)}) collective-permute-start(bf16[128,1024]{1,0:T(8,128)(2,1)S(1)} %collective-permute-done.11.far_theirs), channel_id=1, source_target_pairs={{0,1},{1,0},{2,3},{3,2},{4,5},{5,4},{6,7},{7,6},{8,9},{9,8},{10,11... | collective-permute-start | bytes 786440 | tf_op jit(solution)/shard_map/ppermute | solution.py:470
  96.9 2.9 %collective-permute-start.23 = (bf16[2,128,256]{2,1,0:T(8,128)(2,1)S(1)}, bf16[2,128,256]{2,1,0:T(8,128)(2,1)S(1)}, u32[]{:S(2)}, u32[]{:S(2)}) collective-permute-start(bf16[2,128,256]{2,1,0:T(8,128)(2,1)S(1)} %collective-permute-done.19.refs_2_), channel_id=1, source_target_pairs={{0,2},{2,0},{4,6},{6,4},{8,10},{10,8},{12,14},{14,12},{1,3},{3,1},... | collective-permute-start | bytes 393224 | tf_op jit(solution)/shard_map/ppermute | solution.py:467
  98.2 4.3 %collective-permute-start.24 = (bf16[2,128,256]{2,1,0:T(8,128)(2,1)S(1)}, bf16[2,128,256]{2,1,0:T(8,128)(2,1)S(1)}, u32[]{:S(2)}, u32[]{:S(2)}) collective-permute-start(bf16[2,128,256]{2,1,0:T(8,128)(2,1)S(1)} %collective-permute-done.20.refs_3_), channel_id=1, source_target_pairs={{0,2},{2,0},{4,6},{6,4},{8,10},{10,8},{12,14},{14,12},{1,3},{3,1},... | collective-permute-start | bytes 393224 | tf_op jit(solution)/shard_map/ppermute | solution.py:467
  98.2 10.6 %collective-permute-start.25 = (bf16[4,128,256]{2,1,0:T(8,128)(2,1)}, bf16[4,128,256]{2,1,0:T(8,128)(2,1)}, u32[]{:S(2)}, u32[]{:S(2)}) collective-permute-start(bf16[4,128,256]{2,1,0:T(8,128)(2,1)} %collective-permute-done.18.refs_4_), channel_id=1, source_target_pairs={{0,2},{2,0},{4,6},{6,4},{8,10},{10,8},{12,14},{14,12},{1,3},{3,1},... | collective-permute-start | bytes 786440 | tf_op jit(solution)/shard_map/ppermute | solution.py:467
  100.5 40.5 %collective-permute-start.26 = (bf16[2,128,1024]{2,1,0:T(8,128)(2,1)}, bf16[2,128,1024]{2,1,0:T(8,128)(2,1)}, u32[]{:S(2)}, u32[]{:S(2)}) collective-permute-start(bf16[2,128,1024]{2,1,0:T(8,128)(2,1)} %get-tuple-element.34), channel_id=1, source_target_pairs={{0,12},{2,14},{4,0},{6,2},{8,4},{10,6},{12,8},{14,10},{1,13},{3,15... | collective-permute-start | bytes 1572872 | tf_op jit(solution)/shard_map/ppermute | solution.py:464
  103.2 33.9 %collective-permute-start.14 = (bf16[2,128,1024]{2,1,0:T(8,128)(2,1)}, bf16[2,128,1024]{2,1,0:T(8,128)(2,1)}, u32[]{:S(2)}, u32[]{:S(2)}) collective-permute-start(bf16[2,128,1024]{2,1,0:T(8,128)(2,1)} %collective-permute-done.13), channel_id=1, source_target_pairs={{0,2},{2,0},{4,6},{6,4},{8,10},{10,8},{12,14},{14,12},{1,3},{3,1},... | collective-permute-start | bytes 1572872 | tf_op jit(solution)/shard_map/ppermute | solution.py:467
  103.9 33.2 %collective-permute-start.16 = (bf16[2,128,1024]{2,1,0:T(8,128)(2,1)}, bf16[2,128,1024]{2,1,0:T(8,128)(2,1)}, u32[]{:S(2)}, u32[]{:S(2)}) collective-permute-start(bf16[2,128,1024]{2,1,0:T(8,128)(2,1)} %collective-permute-done.15), channel_id=1, source_target_pairs={{0,2},{2,0},{4,6},{6,4},{8,10},{10,8},{12,14},{14,12},{1,3},{3,1},... | collective-permute-start | bytes 1572872 | tf_op jit(solution)/shard_map/ppermute | solution.py:467
  104.4 36.6 %collective-permute-start.27 = (bf16[2,128,1024]{2,1,0:T(8,128)(2,1)}, bf16[2,128,1024]{2,1,0:T(8,128)(2,1)}, u32[]{:S(2)}, u32[]{:S(2)}) collective-permute-start(bf16[2,128,1024]{2,1,0:T(8,128)(2,1)} %get-tuple-element.35), channel_id=1, source_target_pairs={{0,4},{2,6},{4,8},{6,10},{8,12},{10,14},{12,0},{14,2},{1,5},{3,7},... | collective-permute-start | bytes 1572872 | tf_op jit(solution)/shard_map/ppermute | solution.py:464
  104.8 29.9 %copy-start.11 = (bf16[2,128,1024]{2,1,0:T(8,128)(2,1)S(1)}, bf16[2,128,1024]{2,1,0:T(8,128)(2,1)}, u32[]{:S(2)}) copy-start(bf16[2,128,1024]{2,1,0:T(8,128)(2,1)} %copy-done.10) | copy-start | bytes 1572868
  104.8 29.9 %copy-start.15 = (bf16[128,1024]{1,0:T(8,128)(2,1)S(1)}, bf16[128,1024]{1,0:T(8,128)(2,1)}, u32[]{:S(2)}) copy-start(bf16[128,1024]{1,0:T(8,128)(2,1)} %copy-done.14) | copy-start | bytes 786436
  107.8 26.9 %copy-start.19 = (bf16[128,1024]{1,0:T(8,128)(2,1)S(1)}, bf16[128,1024]{1,0:T(8,128)(2,1)}, u32[]{:S(2)}) copy-start(bf16[128,1024]{1,0:T(8,128)(2,1)} %copy-done.18) | copy-start | bytes 786436
  107.8 26.9 %copy-start.21 = (bf16[128,1024]{1,0:T(8,128)(2,1)S(1)}, bf16[128,1024]{1,0:T(8,128)(2,1)}, u32[]{:S(2)}) copy-start(bf16[128,1024]{1,0:T(8,128)(2,1)} %copy-done.20) | copy-start | bytes 786436
  107.8 26.9 %copy-start.23 = (bf16[128,1024]{1,0:T(8,128)(2,1)S(1)}, bf16[128,1024]{1,0:T(8,128)(2,1)}, u32[]{:S(2)}) copy-start(bf16[128,1024]{1,0:T(8,128)(2,1)} %copy-done.22) | copy-start | bytes 786436
  108.8 28.3 %collective-permute-start.22 = (bf16[4,128,256]{2,1,0:T(8,128)(2,1)S(1)}, bf16[4,128,256]{2,1,0:T(8,128)(2,1)S(1)}, u32[]{:S(2)}, u32[]{:S(2)}) collective-permute-start(bf16[4,128,256]{2,1,0:T(8,128)(2,1)S(1)} %copy-done.7), channel_id=1, source_target_pairs={{0,2},{2,0},{4,6},{6,4},{8,10},{10,8},{12,14},{14,12},{1,3},{3,1},... | collective-permute-start | bytes 786440 | tf_op jit(solution)/shard_map/ppermute | solution.py:467
  146.2 11.0 %collective-permute-start.29 = (bf16[4,128,256]{2,1,0:T(8,128)(2,1)S(1)}, bf16[4,128,256]{2,1,0:T(8,128)(2,1)S(1)}, u32[]{:S(2)}, u32[]{:S(2)}) collective-permute-start(bf16[4,128,256]{2,1,0:T(8,128)(2,1)S(1)} %get-tuple-element.40.refs_0_), channel_id=1, source_target_pairs={{0,4},{2,6},{4,8},{6,10},{8,12},{10,14},{12,0},{14,2},{1,5},{3,7},... | collective-permute-start | bytes 786440 | tf_op jit(solution)/shard_map/ppermute | solution.py:464
  147.6 13.9 %collective-permute-start.28 = (bf16[4,128,256]{2,1,0:T(8,128)(2,1)S(1)}, bf16[4,128,256]{2,1,0:T(8,128)(2,1)S(1)}, u32[]{:S(2)}, u32[]{:S(2)}) collective-permute-start(bf16[4,128,256]{2,1,0:T(8,128)(2,1)S(1)} %get-tuple-element.40.refs_0_), channel_id=1, source_target_pairs={{0,12},{2,14},{4,0},{6,2},{8,4},{10,6},{12,8},{14,10},{1,13},{3,15... | collective-permute-start | bytes 786440 | tf_op jit(solution)/shard_map/ppermute | solution.py:464
  150.0 22.1 %collective-permute-start.30 = (bf16[4,128,256]{2,1,0:T(8,128)(2,1)S(1)}, bf16[4,128,256]{2,1,0:T(8,128)(2,1)}, u32[]{:S(2)}, u32[]{:S(2)}) collective-permute-start(bf16[4,128,256]{2,1,0:T(8,128)(2,1)S(1)} %get-tuple-element.40.refs_0_), channel_id=1, source_target_pairs={{0,2},{2,0},{4,6},{6,4},{8,10},{10,8},{12,14},{14,12},{1,3},{3,1},... | collective-permute-start | bytes 786440 | tf_op jit(solution)/shard_map/ppermute | solution.py:467
  157.1 15.0 %collective-permute-start.32 = (bf16[4,128,256]{2,1,0:T(8,128)(2,1)S(1)}, bf16[4,128,256]{2,1,0:T(8,128)(2,1)}, u32[]{:S(2)}, u32[]{:S(2)}) collective-permute-start(bf16[4,128,256]{2,1,0:T(8,128)(2,1)S(1)} %collective-permute-done.29.refs_2_), channel_id=1, source_target_pairs={{0,2},{2,0},{4,6},{6,4},{8,10},{10,8},{12,14},{14,12},{1,3},{3,1},... | collective-permute-start | bytes 786440 | tf_op jit(solution)/shard_map/ppermute | solution.py:467
  161.5 10.6 %collective-permute-start.31 = (bf16[4,128,256]{2,1,0:T(8,128)(2,1)S(1)}, bf16[4,128,256]{2,1,0:T(8,128)(2,1)}, u32[]{:S(2)}, u32[]{:S(2)}) collective-permute-start(bf16[4,128,256]{2,1,0:T(8,128)(2,1)S(1)} %collective-permute-done.28.refs_1_), channel_id=1, source_target_pairs={{0,2},{2,0},{4,6},{6,4},{8,10},{10,8},{12,14},{14,12},{1,3},{3,1},... | collective-permute-start | bytes 786440 | tf_op jit(solution)/shard_map/ppermute | solution.py:467
  161.5 8.2 %collective-permute-start.33 = (bf16[2,128,256]{2,1,0:T(8,128)(2,1)S(1)}, bf16[2,128,256]{2,1,0:T(8,128)(2,1)S(1)}, u32[]{:S(2)}, u32[]{:S(2)}) collective-permute-start(bf16[2,128,256]{2,1,0:T(8,128)(2,1)S(1)} %slice.32), channel_id=1, source_target_pairs={{0,4},{2,6},{4,8},{6,10},{8,12},{10,14},{12,0},{14,2},{1,5},{3,7},... | collective-permute-start | bytes 393224 | tf_op jit(solution)/shard_map/ppermute | solution.py:464
  162.8 8.5 %collective-permute-start.34 = (bf16[2,128,256]{2,1,0:T(8,128)(2,1)S(1)}, bf16[2,128,256]{2,1,0:T(8,128)(2,1)}, u32[]{:S(2)}, u32[]{:S(2)}) collective-permute-start(bf16[2,128,256]{2,1,0:T(8,128)(2,1)S(1)} %slice.33), channel_id=1, source_target_pairs={{0,12},{2,14},{4,0},{6,2},{8,4},{10,6},{12,8},{14,10},{1,13},{3,15... | collective-permute-start | bytes 393224 | tf_op jit(solution)/shard_map/ppermute | solution.py:464
  169.7 7.3 %collective-permute-start.35 = (bf16[2,128,256]{2,1,0:T(8,128)(2,1)S(1)}, bf16[2,128,256]{2,1,0:T(8,128)(2,1)}, u32[]{:S(2)}, u32[]{:S(2)}) collective-permute-start(bf16[2,128,256]{2,1,0:T(8,128)(2,1)S(1)} %collective-permute-done.33.low), channel_id=1, source_target_pairs={{0,2},{2,0},{4,6},{6,4},{8,10},{10,8},{12,14},{14,12},{1,3},{3,1},... | collective-permute-start | bytes 393224 | tf_op jit(solution)/shard_map/ppermute | solution.py:467
  171.4 5.6 %collective-permute-start.36 = (bf16[2,128,256]{2,1,0:T(8,128)(2,1)}, bf16[2,128,256]{2,1,0:T(8,128)(2,1)}, u32[]{:S(2)}, u32[]{:S(2)}) collective-permute-start(bf16[2,128,256]{2,1,0:T(8,128)(2,1)} %collective-permute-done.34.high), channel_id=1, source_target_pairs={{0,2},{2,0},{4,6},{6,4},{8,10},{10,8},{12,14},{14,12},{1,3},{3,1},... | collective-permute-start | bytes 393224 | tf_op jit(solution)/shard_map/ppermute | solution.py:467
  (25 other events, 59.6 us)

commit v4 on v0

--- a/solution.py
+++ b/solution.py
@@ -1,12 +1,16 @@
+import functools
+
 import jax
 import jax.numpy as jnp
 from jax import lax
+from jax.experimental import pallas as pl
+from jax.experimental.pallas import tpu as pltpu
 from jax.sharding import PartitionSpec as P
 
 time_root = 0.1
 
 
-def per_device(green_blocks, half_chol, full_chol, meanfield, noise_draws, orbitals):
+def general_device(green_blocks, half_chol, full_chol, meanfield, noise_draws, orbitals):
     walkers_here = green_blocks.shape[0]
     chol_here = half_chol.shape[0]
     half_rows = full_chol.shape[1]
@@ -31,8 +35,7 @@
 
     def apply_operator(vector):
         both_halves = lax.all_gather(vector, "orb", axis=0, tiled=True)
-        fold_start = jnp.zeros((walkers_here, half_rows, occupied), jnp.float32)
-        running = fold_start
+        running = jnp.zeros((walkers_here, half_rows, occupied), jnp.float32)
         shard_piece = lax.all_gather(both_halves, "chol", axis=1, tiled=True)
         row_count = shard_piece.shape[1]
         for half_index in range(shard_piece.shape[0]):
@@ -56,6 +59,427 @@
     return (walkers_next, bias_shift)
 
 
+vmem_spec = pl.BlockSpec(memory_space=pltpu.VMEM)
+any_spec = pl.BlockSpec(memory_space=pl.ANY)
+wide = jnp.float32
+narrow = jnp.bfloat16
+small = pltpu.CompilerParams(vmem_limit_bytes=16 << 20)
+
+
+def after(value, *others):
+    return lax.optimization_barrier((value, *others))[0]
+
+
+def place():
+    slot = lax.axis_index("chol")
+    return slot // 2, slot % 2, lax.axis_index("walk")
+
+
+def flipped(z, step):
+    return lax.bitwise_xor(z, jnp.int32(step))
+
+
+def cut_kernel(rows, wanted, full_ref, *refs):
+    z, k, x = place()
+    outs, sem = refs[:-1], refs[-1]
+    copies = []
+    for index, (step, crossed, both) in enumerate(wanted):
+        core = 1 - k if crossed else k
+        start = pl.multiple_of((2 * flipped(z, step) + core) * rows, rows)
+        picked = pl.ds(start, rows)
+        source = full_ref.at[:, picked, :] if both else full_ref.at[x, picked, :]
+        copies.append(pltpu.make_async_copy(source, outs[index], sem.at[index]))
+        copies[-1].start()
+    for copy in copies:
+        copy.wait()
+
+
+def cut(rows, full_chol, wanted):
+    order = full_chol.shape[2]
+    shapes = [
+        jax.ShapeDtypeStruct((2, rows, order) if both else (rows, order), narrow)
+        for _, _, both in wanted
+    ]
+    return pl.pallas_call(
+        functools.partial(cut_kernel, rows, wanted),
+        out_shape=shapes,
+        in_specs=[any_spec],
+        out_specs=[vmem_spec] * len(wanted),
+        scratch_shapes=[pltpu.SemaphoreType.DMA((len(wanted),))],
+        compiler_params=small,
+        name="cut_rows",
+    )(full_chol)
+
+
+def start_kernel(orbitals_ref, out_ref):
+    for walker in range(out_ref.shape[0]):
+        out_ref[walker] = orbitals_ref[0, :, walker, :].astype(narrow)
+
+
+def walker_major(orbitals):
+    _, rows, walkers, occupied = orbitals.shape
+    return pl.pallas_call(
+        start_kernel,
+        out_shape=jax.ShapeDtypeStruct((walkers, rows, occupied), narrow),
+        in_specs=[vmem_spec],
+        out_specs=vmem_spec,
+        compiler_params=small,
+        name="walker_major",
+    )(orbitals)
+
+
+def bias_kernel(here_ref, one_ref, two_ref, three_ref, mine_ref, theirs_ref, out_ref):
+    z, k, _ = place()
+    walkers, rows, occupied = here_ref.shape
+    vectors = mine_ref.shape[0]
+    step_rows = 16
+    totals = [jnp.zeros((8, 128), wide) for _ in range(2 * vectors * walkers)]
+    for step, green in enumerate((here_ref, one_ref, two_ref, three_ref)):
+        base = (2 * flipped(z, step) + k) * rows
+
+        def add(index, totals, base=base, green=green):
+            here = pl.multiple_of(index * step_rows, step_rows)
+            there = pl.multiple_of(base + index * step_rows, step_rows)
+            picked = pl.ds(here, step_rows)
+            greens = [green[w, picked, :] for w in range(walkers)]
+            greens = [g.astype(wide) for g in greens]
+            totals = list(totals)
+            for c in range(2 * vectors):
+                chol_ref = mine_ref if c < vectors else theirs_ref
+                chol = chol_ref[c % vectors, pl.ds(there, step_rows), :].astype(wide)
+                for w in range(walkers):
+                    product = greens[w] * chol
+                    tiles = [
+                        product[r : r + 8, n : n + 128]
+                        for r in range(0, step_rows, 8)
+                        for n in range(0, occupied, 128)
+                    ]
+                    totals[c * walkers + w] = totals[c * walkers + w] + sum(tiles[1:], tiles[0])
+            return tuple(totals)
+
+        totals = lax.fori_loop(0, rows // step_rows, add, tuple(totals))
+    for index, total in enumerate(totals):
+        value = jnp.sum(jnp.sum(total, axis=0, keepdims=True), axis=1, keepdims=True)
+        out_ref[pl.ds(index, 1), :] = jnp.broadcast_to(value, (1, 128))
+
+
+def chip_bias(green, mine, theirs):
+    entries = 2 * mine.shape[0] * green[0].shape[0]
+    return pl.pallas_call(
+        bias_kernel,
+        out_shape=jax.ShapeDtypeStruct((entries, 128), wide),
+        in_specs=[vmem_spec] * 6,
+        out_specs=vmem_spec,
+        compiler_params=small,
+        name="chip_bias",
+    )(*green, mine, theirs)
+
+
+def field_kernel(mine_ref, theirs_ref, noise_ref, noise_there_ref, shift_ref, field_ref):
+    half = mine_ref.shape[0] // 2
+    low, high = pl.ds(0, half), pl.ds(half, half)
+    for rows, other, consts in ((low, high, noise_ref), (high, low, noise_there_ref)):
+        force = mine_ref[rows, :] + theirs_ref[other, :]
+        shift = jnp.clip(time_root * (force - consts[high, :]), -1.0, 1.0)
+        field_ref[rows, :] = consts[low, :] - shift
+        if rows is low:
+            shift_ref[...] = shift
+
+
+def chip_field(mine, theirs, noise, noise_there):
+    entries = mine.shape[0]
+    return pl.pallas_call(
+        field_kernel,
+        out_shape=[
+            jax.ShapeDtypeStruct((entries // 2, 128), wide),
+            jax.ShapeDtypeStruct((entries, 128), wide),
+        ],
+        in_specs=[vmem_spec] * 4,
+        out_specs=[vmem_spec] * 2,
+        compiler_params=small,
+        name="chip_field",
+    )(mine, theirs, noise, noise_there)
+
+
+def block_operators(x, walkers, sources, picked):
+    tiles = []
+    for field_ref, crossed, near, other in sources:
+        first = 2 * walkers * crossed
+        one, two = near(picked).astype(wide), other(picked).astype(wide)
+        copies = one.shape[1] // 128
+        tiles.append([])
+        for w in range(walkers):
+            scale_one = field_ref[pl.ds(first + x * walkers + w, 1), :]
+            scale_two = field_ref[pl.ds(first + (1 - x) * walkers + w, 1), :]
+            scale_one = jnp.concatenate([scale_one] * copies, 1)
+            scale_two = jnp.concatenate([scale_two] * copies, 1)
+            block = time_root * (scale_one * one + scale_two * two)
+            tiles[-1].append(block.astype(narrow))
+    return tiles
+
+
+def over_tiles(rows, order, body):
+    high, across = 16, 256
+    columns = order // across
+
+    def tile(index, carry):
+        row = pl.multiple_of((index // columns) * high, high)
+        column = pl.multiple_of((index % columns) * across, across)
+        body((pl.ds(row, high), pl.ds(column, across)))
+        return carry
+
+    lax.fori_loop(0, (rows // high) * columns, tile, 0)
+
+
+def of_pair(ref, index):
+    return lambda picked: ref[(index, *picked)]
+
+
+def of_one(ref):
+    return lambda picked: ref[picked]
+
+
+def both_cores(field_ref, mine, mine_x, theirs, theirs_x):
+    return [
+        (field_ref, 0, of_one(mine), of_one(mine_x)),
+        (field_ref, 1, of_one(theirs), of_one(theirs_x)),
+    ]
+
+
+def early_kernel(walkers, field_here, field_one, field_two, own, own_theirs, *refs):
+    blocks, summed_ref = refs[:-1], refs[-1]
+    _, _, x = place()
+    sources = [
+        (field_here, 0, of_pair(own, x), of_pair(own, 1 - x)),
+        (field_here, 1, of_pair(own_theirs, x), of_pair(own_theirs, 1 - x)),
+    ]
+    sources += both_cores(field_one, *blocks[:4]) + both_cores(field_two, *blocks[4:])
+
+    def body(picked):
+        tiles = block_operators(x, walkers, sources, picked)
+        for w in range(walkers):
+            parts = [block[w].astype(wide) for block in tiles]
+            summed_ref[(w, *picked)] = sum(parts[1:], parts[0])
+
+    over_tiles(*summed_ref.shape[1:], body)
+
+
+def early_operator(walkers, fields, own, own_theirs, blocks):
+    rows, order = blocks[0].shape
+    return pl.pallas_call(
+        functools.partial(early_kernel, walkers),
+        out_shape=jax.ShapeDtypeStruct((walkers, rows, order), wide),
+        in_specs=[vmem_spec] * (5 + len(blocks)),
+        out_specs=vmem_spec,
+        compiler_params=small,
+        name="early_operator",
+    )(*fields, own, own_theirs, *blocks)
+
+
+def late_kernel(summed_ref, field_ref, *refs):
+    blocks, operator_ref = refs[:-1], refs[-1]
+    walkers, rows, order = summed_ref.shape
+    _, _, x = place()
+    sources = both_cores(field_ref, *blocks)
+
+    def body(picked):
+        tiles = block_operators(x, walkers, sources, picked)
+        row, column = picked
+        for w in range(walkers):
+            value = summed_ref[(w, *picked)]
+            for block in tiles:
+                value = value + block[w].astype(wide)
+            top = value.astype(narrow)
+            operator_ref[w, row, column] = top
+            rest = (value - top.astype(wide)).astype(narrow)
+            operator_ref[w, pl.ds(rows + row.start, row.size), column] = rest
+
+    over_tiles(rows, order, body)
+
+
+def split_operator(summed, field, blocks):
+    walkers, rows, order = summed.shape
+    return pl.pallas_call(
+        late_kernel,
+        out_shape=jax.ShapeDtypeStruct((walkers, 2 * rows, order), narrow),
+        in_specs=[vmem_spec] * (2 + len(blocks)),
+        out_specs=vmem_spec,
+        compiler_params=small,
+        name="split_operator",
+    )(summed, field, *blocks)
+
+
+def applied(operator_ref, vector_ref, step, mine, theirs):
+    z, k, _ = place()
+    _, rows, _ = mine.shape
+    vector_ref[:, pl.ds(pl.multiple_of(k * rows, rows), rows), :] = mine[...]
+    vector_ref[:, pl.ds(pl.multiple_of((1 - k) * rows, rows), rows), :] = theirs[...]
+    start = pl.multiple_of(flipped(z, step) * 2 * rows, 2 * rows)
+
+    def of_walker(w):
+        both = jnp.dot(
+            operator_ref[w, :, pl.ds(start, 2 * rows)],
+            vector_ref[w],
+            preferred_element_type=wide,
+        )
+        return both[:rows] + both[rows:]
+
+    return of_walker
+
+
+def near_kernel(operator_ref, *refs):
+    pieces, (out_ref, vector_ref) = refs[:6], refs[6:]
+    parts = [
+        applied(operator_ref, vector_ref.at[step], step, pieces[step], pieces[3 + step])
+        for step in range(3)
+    ]
+    for w in range(out_ref.shape[0]):
+        out_ref[w] = parts[0](w) + parts[1](w) + parts[2](w)
+
+
+def near_application(operator, pieces):
+    walkers, rows, occupied = pieces[0].shape
+    return pl.pallas_call(
+        near_kernel,
+        out_shape=jax.ShapeDtypeStruct((walkers, rows, occupied), wide),
+        in_specs=[vmem_spec] * 7,
+        out_specs=vmem_spec,
+        scratch_shapes=[pltpu.VMEM((3, walkers, 2 * rows, occupied), narrow)],
+        compiler_params=small,
+        name="near_application",
+    )(operator, *pieces)
+
+
+def first_kernel(operator_ref, partial_ref, mine, theirs, first_ref, narrow_ref, vector_ref):
+    part = applied(operator_ref, vector_ref, 3, mine, theirs)
+    for w in range(first_ref.shape[0]):
+        term = partial_ref[w] + part(w)
+        first_ref[w] = term
+        narrow_ref[w] = term.astype(narrow)
+
+
+def first_application(operator, partial, mine, theirs):
+    walkers, rows, occupied = mine.shape
+    return pl.pallas_call(
+        first_kernel,
+        out_shape=[
+            jax.ShapeDtypeStruct((walkers, rows, occupied), wide),
+            jax.ShapeDtypeStruct((walkers, rows, occupied), narrow),
+        ],
+        in_specs=[vmem_spec] * 4,
+        out_specs=[vmem_spec] * 2,
+        scratch_shapes=[pltpu.VMEM((walkers, 2 * rows, occupied), narrow)],
+        compiler_params=small,
+        name="first_application",
+    )(operator, partial, mine, theirs)
+
+
+def second_kernel(operator_ref, partial_ref, first_ref, orbitals_ref, mine, theirs, out_ref, vector_ref):
+    part = applied(operator_ref, vector_ref, 3, mine, theirs)
+    for w in range(first_ref.shape[0]):
+        second = partial_ref[w] + part(w)
+        out_ref[0, :, w, :] = orbitals_ref[0, :, w, :] + first_ref[w] + 0.5 * second
+
+
+def second_application(operator, partial, first_term, orbitals, mine, theirs):
+    walkers, rows, occupied = mine.shape
+    return pl.pallas_call(
+        second_kernel,
+        out_shape=jax.ShapeDtypeStruct(orbitals.shape, wide),
+        in_specs=[vmem_spec] * 6,
+        out_specs=vmem_spec,
+        scratch_shapes=[pltpu.VMEM((walkers, 2 * rows, occupied), narrow)],
+        compiler_params=small,
+        name="second_application",
+    )(operator, partial, first_term, orbitals, mine, theirs)
+
+
+def to_chip(value, step):
+    return lax.ppermute(value, "chol", [(i, i ^ (2 * step)) for i in range(8)])
+
+
+def to_core(value):
+    return lax.ppermute(value, "chol", [(i, i ^ 1) for i in range(8)])
+
+
+def across(value):
+    return lax.ppermute(value, "walk", [(0, 1), (1, 0)])
+
+
+def row_device(green_blocks, half_chol, full_chol, meanfield, noise_draws, orbitals):
+    walkers, rows, _ = green_blocks.shape
+    vectors = half_chol.shape[0]
+
+    green_two, green_one = to_chip(green_blocks, 2), to_chip(green_blocks, 1)
+    half_theirs = to_core(half_chol)
+    constants = jnp.concatenate([noise_draws.T.reshape(-1), jnp.repeat(meanfield, walkers)])
+    constants = jnp.broadcast_to(constants[:, None], (2 * vectors * walkers, 128))
+    constants_theirs = to_core(constants)
+
+    cross, straight = {}, {}
+    cross[2], straight[2] = cut(rows, full_chol, ((2, True, False), (2, False, False)))
+    cross[1], straight[1], cross[3], straight[3], own, own_cross = cut(
+        rows,
+        after(full_chol, cross[2]),
+        (
+            (1, True, False),
+            (1, False, False),
+            (3, True, False),
+            (3, False, False),
+            (0, False, True),
+            (0, True, True),
+        ),
+    )
+    own_theirs = to_core(own_cross)
+    blocks = {}
+
+    def exchange(step):
+        theirs = to_core(to_chip(cross[step], step))
+        mine = to_chip(straight[step], step)
+        blocks[step] = (mine, across(mine), theirs, across(theirs))
+        return mine
+
+    second_mine = exchange(2)
+    green_three = to_chip(green_two, 1)
+    cross[1], straight[1] = after((cross[1], straight[1]), green_two)
+    first_mine = exchange(1)
+    cross[3], straight[3] = after((cross[3], straight[3]), green_three)
+    exchange(3)
+
+    start = after(walker_major(orbitals), second_mine, first_mine)
+    start_two, start_one = to_chip(start, 2), to_chip(start, 1)
+    start_three = to_chip(start_two, 1)
+
+    green = (green_blocks, green_one, green_two, green_three)
+    bias = chip_bias(green, half_chol, half_theirs)
+    shift_rows, field = chip_field(bias, to_core(bias), constants, constants_theirs)
+    field_one, field_two, field_three = (to_chip(field, step) for step in (1, 2, 3))
+    bias_shift = shift_rows[:, 0].reshape(vectors, walkers).T
+
+    summed = early_operator(
+        walkers,
+        (field, field_one, field_two),
+        own,
+        own_theirs,
+        (*blocks[1], *blocks[2]),
+    )
+    operator = split_operator(summed, field_three, blocks[3])
+
+    near = [start, start_one, start_two]
+    partial = near_application(operator, [*near, *[to_core(piece) for piece in near]])
+    first_term, first_narrow = first_application(
+        operator, partial, start_three, to_core(start_three)
+    )
+    first_two, first_one = to_chip(first_narrow, 2), to_chip(first_narrow, 1)
+    first_three = to_chip(first_two, 1)
+    near = [first_narrow, first_one, first_two]
+    partial = near_application(operator, [*near, *[to_core(piece) for piece in near]])
+    walkers_next = second_application(
+        operator, partial, first_term, orbitals, first_three, to_core(first_three)
+    )
+    return (walkers_next, bias_shift)
+
+
 def solution(mesh):
     placed = (
         P(("grp", "walk"), "chol", "orb"),
@@ -65,6 +489,11 @@
         P(("grp", "walk"), "chol"),
         P("orb", "chol", ("grp", "walk"), None),
     )
+    sizes = mesh.shape
+    if sizes["orb"] == 1 and sizes["walk"] == 2 and sizes["chol"] == 8:
+        per_device = row_device
+    else:
+        per_device = general_device
     return jax.shard_map(
         per_device,
         mesh=mesh,

time: 321 us -> 136 us (0.42)
  waiting for transfers between devices: 270 us -> 80.4 us
  starting transfers between devices: 0.21 us -> 35.8 us
  matrix products: 19.2 us -> 0 us
  between operations: 13.8 us -> 0.85 us
  Pallas kernels: 0 us -> 12.9 us
  other arithmetic: 7.99 us -> 0.08 us
  local copies, waits for them, and re-layouts: 9.18 us -> 5.46 us
    psum x2 -> x0, waiting for transfers between devices: 192 us -> none  [apply_operator(): summed = lax.psum(running, 'chol')]
    ppermute x0 -> x39, waiting for transfers between devices: none -> 80.4 us  [the longest x18 73.2 us: to_chip(): return lax.ppermute(value, 'chol', [(i, i ^ 2 * step) for i in range(8)])]
    all_gather x3 -> x0, waiting for transfers between devices: 77.7 us -> none  [the longest x2 54.2 us: apply_operator(): shard_piece = lax.all_gather(both_halves, 'chol', axis=1, tiled=True)]
    ppermute x0 -> x39, starting transfers between devices: none -> 35.8 us  [the longest x18 26.5 us: to_chip(): return lax.ppermute(value, 'chol', [(i, i ^ 2 * step) for i in range(8)])]
    dot_general x3 -> x0, matrix products: 19.2 us -> none  [the longest x2 14.2 us: apply_operator(): lax.dot_general(col_block, shard_piece[half_index], (((2,), (0,)), ((0,),...]
    pallas_call x0 -> x11, Pallas kernels: none -> 12.9 us  [the longest x1 3.33 us: early_operator(): pl.pallas_call(functools.partial(early_kernel, walkers), out_shape=jax.Sh...]
    mul x1 -> x0, other arithmetic: 6.62 us -> none  [per_device(): shifted_field[:, chol_index, None, None]]
    unnamed x10 -> x14, local copies, waits for them, and re-layouts: 7.4 us -> 4.4 us
  transfers between devices with their start and end apart: 5 -> 39, of which waited for: 5 -> 16; matrix products, arithmetic and copies ran while one was open for 5% -> 1% of each run, Pallas kernels for 0% -> 8%
where the time goes in v4:
time: 136 us; the launch traced here: 135 us
  waiting for transfers between devices  80.4 us (59%)
  starting transfers between devices  35.8 us (26%)
  Pallas kernels  12.9 us (9%)
  local copies, waits for them, and re-layouts  5.46 us (4%)
    ppermute x18, waiting for transfers between devices, to_chip(): return lax.ppermute(value, 'chol', [(i, i ^ 2 * step) for i in range(8)])  73.2 us
    ppermute x18, starting transfers between devices, to_chip(): return lax.ppermute(value, 'chol', [(i, i ^ 2 * step) for i in range(8)])  26.5 us
    ppermute x6, starting transfers between devices, across(): return lax.ppermute(value, 'walk', [(0, 1), (1, 0)])  7.17 us
    ppermute x6, waiting for transfers between devices, across(): return lax.ppermute(value, 'walk', [(0, 1), (1, 0)])  7.14 us
    unnamed x14, local copies, waits for them, and re-layouts  4.4 us
    pallas_call x1, Pallas kernels, early_operator(): pl.pallas_call(functools.partial(early_kernel, walkers), out_shape=jax.Sh...  3.33 us
  transfers between devices with their start and end apart: 39, of which 16 were waited for; matrix products, arithmetic and copies ran while one was open for 1% of the time, Pallas kernels for 8%

profile of v4, /device:TPU:0, one launch (start us, length us, event | category | flops | bytes accessed | tf_op | source)
XLA Modules:
  0.0 135.5 jit_solution(18022331712002234739)
XLA Ops:
  0.6 0.5 collective-permute-start.3
  1.1 3.7 %collective-permute-start.1 = (bf16[4,128,256]{2,1,0:T(8,128)(2,1)}, bf16[4,128,256]{2,1,0:T(8,128)(2,1)S(1)}, u32[]{:S(2)}, u32[]{:S(2)}) collective-permute-start(bf16[4,128,256]{2,1,0:T(8,128)(2,1)} %here_ref.1), channel_id=1, source_target_pairs={{0,8},{2,10},{4,12},{6,14},{8,0},{10,2},{12,4},{14,6},{1,9},{3,11}... | collective-permute-start | bytes 786440 | tf_op jit(solution)/shard_map/ppermute | solution.py:398
  4.8 1.6 %collective-permute-start = (bf16[4,128,256]{2,1,0:T(8,128)(2,1)}, bf16[4,128,256]{2,1,0:T(8,128)(2,1)S(1)}, u32[]{:S(2)}, u32[]{:S(2)}) collective-permute-start(bf16[4,128,256]{2,1,0:T(8,128)(2,1)} %here_ref.1), channel_id=1, source_target_pairs={{0,4},{2,6},{4,0},{6,2},{8,12},{10,14},{12,8},{14,10},{1,5},{3,7},... | collective-permute-start | bytes 786440 | tf_op jit(solution)/shard_map/ppermute | solution.py:398
  6.4 2.2 %copy-done = bf16[2,1024,1024]{2,1,0:T(8,128)(2,1)S(1)} copy-done((bf16[2,1024,1024]{2,1,0:T(8,128)(2,1)S(1)}, bf16[2,1024,1024]{2,1,0:T(8,128)(2,1)}, u32[]{:S(2)}) %copy-start) | copy-done | bytes 4194328
  8.6 0.9 cut_rows.2
  9.8 2.6 %collective-permute-start.14 = (bf16[128,1024]{1,0:T(8,128)(2,1)}, bf16[128,1024]{1,0:T(8,128)(2,1)S(1)}, u32[]{:S(2)}, u32[]{:S(2)}) collective-permute-start(bf16[128,1024]{1,0:T(8,128)(2,1)} %get-tuple-element.29), channel_id=1, source_target_pairs={{0,8},{2,10},{4,12},{6,14},{8,0},{10,2},{12,4},{14,6},{1,9},{3,11}... | collective-permute-start | bytes 786440 | tf_op jit(solution)/shard_map/ppermute | solution.py:398
  12.8 5.1 %collective-permute-done.1.two_ref = bf16[4,128,256]{2,1,0:T(8,128)(2,1)S(1)} collective-permute-done((bf16[4,128,256]{2,1,0:T(8,128)(2,1)}, bf16[4,128,256]{2,1,0:T(8,128)(2,1)S(1)}, u32[]{:S(2)}, u32[]{:S(2)}) %collective-permute-start.1) | collective-permute-done | bytes 262176 | tf_op jit(solution)/shard_map/ppermute | solution.py:398
  18.0 2.2 %copy-done.1 = bf16[2,1024,1024]{2,1,0:T(8,128)(2,1)S(1)} copy-done((bf16[2,1024,1024]{2,1,0:T(8,128)(2,1)S(1)}, bf16[2,1024,1024]{2,1,0:T(8,128)(2,1)}, u32[]{:S(2)}) %copy-start.1) | copy-done | bytes 4194328
  20.4 0.6 collective-permute-start.8
  21.0 0.7 collective-permute-start.9
  21.7 13.1 %collective-permute-done.16 = bf16[128,1024]{1,0:T(8,128)(2,1)} collective-permute-done((bf16[128,1024]{1,0:T(8,128)(2,1)}, bf16[128,1024]{1,0:T(8,128)(2,1)}, u32[]{:S(2)}, u32[]{:S(2)}) %collective-permute-start.16) | collective-permute-done | bytes 262176 | tf_op jit(solution)/shard_map/ppermute | solution.py:398
  34.8 0.5 collective-permute-start.11
  35.3 4.8 %collective-permute-done.14.refs_4_ = bf16[128,1024]{1,0:T(8,128)(2,1)S(1)} collective-permute-done((bf16[128,1024]{1,0:T(8,128)(2,1)}, bf16[128,1024]{1,0:T(8,128)(2,1)S(1)}, u32[]{:S(2)}, u32[]{:S(2)}) %collective-permute-start.14) | collective-permute-done | bytes 262176 | tf_op jit(solution)/shard_map/ppermute | solution.py:398
  40.2 0.7 collective-permute-start.2
  40.9 4.9 %collective-permute-done.11 = bf16[128,1024]{1,0:T(8,128)(2,1)S(1)} collective-permute-done((bf16[128,1024]{1,0:T(8,128)(2,1)S(1)}, bf16[128,1024]{1,0:T(8,128)(2,1)S(1)}, u32[]{:S(2)}, u32[]{:S(2)}) %collective-permute-start.11) | collective-permute-done | bytes 262176 | tf_op jit(solution)/shard_map/ppermute | solution.py:398
  45.8 1.6 %collective-permute-start.15 = (bf16[128,1024]{1,0:T(8,128)(2,1)S(1)}, bf16[128,1024]{1,0:T(8,128)(2,1)S(1)}, u32[]{:S(2)}, u32[]{:S(2)}) collective-permute-start(bf16[128,1024]{1,0:T(8,128)(2,1)S(1)} %collective-permute-done.14.refs_4_), channel_id=1, source_target_pairs={{0,1},{1,0},{2,3},{3,2},{4,5},{5,4},{6,7},{7,6},{8,9},{9,8},{10,11... | collective-permute-start | bytes 786440 | tf_op jit(solution)/shard_map/ppermute | solution.py:406
  47.3 4.0 %collective-permute-done.2.three_ref = bf16[4,128,256]{2,1,0:T(8,128)(2,1)S(1)} collective-permute-done((bf16[4,128,256]{2,1,0:T(8,128)(2,1)S(1)}, bf16[4,128,256]{2,1,0:T(8,128)(2,1)S(1)}, u32[]{:S(2)}, u32[]{:S(2)}) %collective-permute-start.2) | collective-permute-done | bytes 262176 | tf_op jit(solution)/shard_map/ppermute | solution.py:398
  51.3 1.6 %collective-permute-start.10 = (bf16[128,1024]{1,0:T(8,128)(2,1)S(1)}, bf16[128,1024]{1,0:T(8,128)(2,1)S(1)}, u32[]{:S(2)}, u32[]{:S(2)}) collective-permute-start(bf16[128,1024]{1,0:T(8,128)(2,1)S(1)} %collective-permute-done.9.refs_0_), channel_id=1, source_target_pairs={{0,1},{1,0},{2,3},{3,2},{4,5},{5,4},{6,7},{7,6},{8,9},{9,8},{10,11... | collective-permute-start | bytes 786440 | tf_op jit(solution)/shard_map/ppermute | solution.py:406
  52.9 0.5 collective-permute-start.18
  53.4 0.5 collective-permute-done.15.refs_5_
  53.9 3.8 %collective-permute-start.22 = (bf16[128,1024]{1,0:T(8,128)(2,1)S(1)}, bf16[128,1024]{1,0:T(8,128)(2,1)S(1)}, u32[]{:S(2)}, u32[]{:S(2)}) collective-permute-start(bf16[128,1024]{1,0:T(8,128)(2,1)S(1)} %get-tuple-element.33), channel_id=1, source_target_pairs={{0,12},{2,14},{4,8},{6,10},{8,4},{10,6},{12,0},{14,2},{1,13},{3,15... | collective-permute-start | bytes 786440 | tf_op jit(solution)/shard_map/ppermute | solution.py:398
  57.7 2.8 %collective-permute-done.10.refs_1_ = bf16[128,1024]{1,0:T(8,128)(2,1)S(1)} collective-permute-done((bf16[128,1024]{1,0:T(8,128)(2,1)S(1)}, bf16[128,1024]{1,0:T(8,128)(2,1)S(1)}, u32[]{:S(2)}, u32[]{:S(2)}) %collective-permute-start.10) | collective-permute-done | bytes 262176 | tf_op jit(solution)/shard_map/ppermute | solution.py:406
  60.5 4.0 %collective-permute-start.20 = (bf16[128,1024]{1,0:T(8,128)(2,1)S(1)}, bf16[128,1024]{1,0:T(8,128)(2,1)S(1)}, u32[]{:S(2)}, u32[]{:S(2)}) collective-permute-start(bf16[128,1024]{1,0:T(8,128)(2,1)S(1)} %get-tuple-element.32), channel_id=1, source_target_pairs={{0,12},{2,14},{4,8},{6,10},{8,4},{10,6},{12,0},{14,2},{1,13},{3,15... | collective-permute-start | bytes 786440 | tf_op jit(solution)/shard_map/ppermute | solution.py:398
  64.5 0.5 walker_major.1.refs_0_
  65.1 1.0 chip_bias.1.mine_ref
  66.2 0.6 collective-permute-start.25
  66.8 1.5 %collective-permute-start.13 = (bf16[128,1024]{1,0:T(8,128)(2,1)S(1)}, bf16[128,1024]{1,0:T(8,128)(2,1)S(1)}, u32[]{:S(2)}, u32[]{:S(2)}) collective-permute-start(bf16[128,1024]{1,0:T(8,128)(2,1)S(1)} %collective-permute-done.12.refs_2_), channel_id=1, source_target_pairs={{0,1},{1,0},{2,3},{3,2},{4,5},{5,4},{6,7},{7,6},{8,9},{9,8},{10,11... | collective-permute-start | bytes 786440 | tf_op jit(solution)/shard_map/ppermute | solution.py:406
  68.3 3.5 %collective-permute-done.20.refs_0_ = bf16[128,1024]{1,0:T(8,128)(2,1)S(1)} collective-permute-done((bf16[128,1024]{1,0:T(8,128)(2,1)S(1)}, bf16[128,1024]{1,0:T(8,128)(2,1)S(1)}, u32[]{:S(2)}, u32[]{:S(2)}) %collective-permute-start.20) | collective-permute-done | bytes 262176 | tf_op jit(solution)/shard_map/ppermute | solution.py:398
  71.8 18.4 %collective-permute-done.26.refs_2_ = bf16[4,128,256]{2,1,0:T(8,128)(2,1)S(1)} collective-permute-done((bf16[4,128,256]{2,1,0:T(8,128)(2,1)S(1)}, bf16[4,128,256]{2,1,0:T(8,128)(2,1)S(1)}, u32[]{:S(2)}, u32[]{:S(2)}) %collective-permute-start.26) | collective-permute-done | bytes 262176 | tf_op jit(solution)/shard_map/ppermute | solution.py:398
  90.2 1.5 %collective-permute-start.21 = (bf16[128,1024]{1,0:T(8,128)(2,1)S(1)}, bf16[128,1024]{1,0:T(8,128)(2,1)S(1)}, u32[]{:S(2)}, u32[]{:S(2)}) collective-permute-start(bf16[128,1024]{1,0:T(8,128)(2,1)S(1)} %collective-permute-done.20.refs_0_), channel_id=1, source_target_pairs={{0,1},{1,0},{2,3},{3,2},{4,5},{5,4},{6,7},{7,6},{8,9},{9,8},{10,11... | collective-permute-start | bytes 786440 | tf_op jit(solution)/shard_map/ppermute | solution.py:406
  91.7 2.1 %collective-permute-start.6 = (f32[16,128]{1,0:T(8,128)S(1)}, f32[16,128]{1,0:T(8,128)S(1)}, u32[]{:S(2)}, u32[]{:S(2)}) collective-permute-start(f32[16,128]{1,0:T(8,128)S(1)} %get-tuple-element.20.field_here), channel_id=1, source_target_pairs={{0,4},{2,6},{4,0},{6,2},{8,12},{10,14},{12,8},{14,10},{1,5},{3,7},... | collective-permute-start | bytes 24584 | tf_op jit(solution)/shard_map/ppermute | solution.py:398
  93.8 1.3 collective-permute-start.7
  95.1 1.4 %collective-permute-start.19 = (f32[16,128]{1,0:T(8,128)S(1)}, f32[16,128]{1,0:T(8,128)S(1)}, u32[]{:S(2)}, u32[]{:S(2)}) collective-permute-start(f32[16,128]{1,0:T(8,128)S(1)} %get-tuple-element.20.field_here), channel_id=1, source_target_pairs={{0,12},{2,14},{4,8},{6,10},{8,4},{10,6},{12,0},{14,2},{1,13},{3,15... | collective-permute-start | bytes 24584 | tf_op jit(solution)/shard_map/ppermute | solution.py:398
  96.5 1.2 collective-permute-done.21.refs_1_
  97.8 1.6 %collective-permute-done.30.mine = bf16[4,128,256]{2,1,0:T(8,128)(2,1)S(1)} collective-permute-done((bf16[4,128,256]{2,1,0:T(8,128)(2,1)S(1)}, bf16[4,128,256]{2,1,0:T(8,128)(2,1)S(1)}, u32[]{:S(2)}, u32[]{:S(2)}) %collective-permute-start.30) | collective-permute-done | bytes 262176 | tf_op jit(solution)/shard_map/ppermute | solution.py:398
  99.3 0.5 collective-permute-start.24
  99.9 0.5 collective-permute-start.28
  100.5 3.3 %early_operator.1.summed_ref = f32[4,128,1024]{2,1,0:T(8,128)S(1)} custom-call(f32[16,128]{1,0:T(8,128)S(1)} %get-tuple-element.20.field_here, f32[16,128]{1,0:T(8,128)S(1)} %collective-permute-done.6.field_one, f32[16,128]{1,0:T(8,128)S(1)} %collective-permute-done.7.field_two, bf16[2,128,1024]{2,1,0:T(8,128)(2,1)S(1)} %get-tuple-element.23.own, ...), custom_call_target="tpu_custom_call" | custom-call | tf_op jit(solution)/shard_map/early_operator/pallas_call | solution.py:269
  103.9 2.6 %collective-permute-done.24.refs_3_ = bf16[128,1024]{1,0:T(8,128)(2,1)S(1)} collective-permute-done((bf16[128,1024]{1,0:T(8,128)(2,1)S(1)}, bf16[128,1024]{1,0:T(8,128)(2,1)S(1)}, u32[]{:S(2)}, u32[]{:S(2)}) %collective-permute-start.24) | collective-permute-done | bytes 262176 | tf_op jit(solution)/shard_map/ppermute | solution.py:406
  106.5 1.6 %split_operator.1.operator_ref = bf16[4,256,1024]{2,1,0:T(8,128)(2,1)S(1)} custom-call(f32[4,128,1024]{2,1,0:T(8,128)S(1)} %early_operator.1.summed_ref, f32[16,128]{1,0:T(8,128)S(1)} %collective-permute-done.19.field_ref, bf16[128,1024]{1,0:T(8,128)(2,1)S(1)} %collective-permute-done.20.refs_0_, bf16[128,1024]{1,0:T(8,128)(2,1)S(1)} %collective-permute-done.21.refs_1_, ...), custom_call_target="tpu_custom_call" | custom-call | tf_op jit(solution)/shard_map/split_operator/pallas_call | solution.py:302
  108.1 0.7 near_application.2.partial_ref
  109.2 0.8 collective-permute-start.33
  110.0 2.2 %collective-permute-start.32 = (bf16[4,128,256]{2,1,0:T(8,128)(2,1)S(1)}, bf16[4,128,256]{2,1,0:T(8,128)(2,1)}, u32[]{:S(2)}, u32[]{:S(2)}) collective-permute-start(bf16[4,128,256]{2,1,0:T(8,128)(2,1)S(1)} %get-tuple-element.35.refs_0_), channel_id=1, source_target_pairs={{0,4},{2,6},{4,0},{6,2},{8,12},{10,14},{12,8},{14,10},{1,5},{3,7},... | collective-permute-start | bytes 786440 | tf_op jit(solution)/shard_map/ppermute | solution.py:398
  112.2 9.8 %collective-permute-done.33.refs_2_ = bf16[4,128,256]{2,1,0:T(8,128)(2,1)} collective-permute-done((bf16[4,128,256]{2,1,0:T(8,128)(2,1)S(1)}, bf16[4,128,256]{2,1,0:T(8,128)(2,1)}, u32[]{:S(2)}, u32[]{:S(2)}) %collective-permute-start.33) | collective-permute-done | bytes 262176 | tf_op jit(solution)/shard_map/ppermute | solution.py:398
  122.6 7.7 %collective-permute-done.37.mine = bf16[4,128,256]{2,1,0:T(8,128)(2,1)} collective-permute-done((bf16[4,128,256]{2,1,0:T(8,128)(2,1)}, bf16[4,128,256]{2,1,0:T(8,128)(2,1)}, u32[]{:S(2)}, u32[]{:S(2)}) %collective-permute-start.37) | collective-permute-done | bytes 262176 | tf_op jit(solution)/shard_map/ppermute | solution.py:398
  130.5 0.6 reshape_squeeze.3
  131.1 1.9 %near_application.3.partial_ref = f32[4,128,256]{2,1,0:T(8,128)S(1)} custom-call(bf16[4,256,1024]{2,1,0:T(8,128)(2,1)S(1)} %split_operator.1.operator_ref, bf16[4,128,256]{2,1,0:T(8,128)(2,1)S(1)} %get-tuple-element.35.refs_0_, bf16[4,128,256]{2,1,0:T(8,128)(2,1)} %collective-permute-done.32.refs_1_, bf16[4,128,256]{2,1,0:T(8,128)(2,1)} %collective-permute-done.33.refs_2_, ...), custom_call_target="tpu_custom_call" | custom-call | tf_op jit(solution)/shard_map/near_application/pallas_call | solution.py:342
  133.1 2.4 %second_application.1 = f32[1,128,4,256]{3,2,1,0:T(4,128)} custom-call(bf16[4,256,1024]{2,1,0:T(8,128)(2,1)S(1)} %split_operator.1.operator_ref, f32[4,128,256]{2,1,0:T(8,128)S(1)} %near_application.3.partial_ref, f32[4,128,256]{2,1,0:T(8,128)S(1)} %get-tuple-element.36.first_ref, f32[1,128,4,256]{3,2,1,0:T(4,128)S(1)} %copy-done.2, ...), custom_call_target="tpu_custom_call" | custom-call | tf_op jit(solution)/shard_map/second_application/pallas_call | solution.py:386
  (62 shorter events, 2.6 us)
Async XLA Ops:
  0.6 64.4 %collective-permute-start.3 = (bf16[2,1024,256]{2,1,0:T(8,128)(2,1)}, bf16[2,1024,256]{2,1,0:T(8,128)(2,1)S(1)}, u32[]{:S(2)}, u32[]{:S(2)}) collective-permute-start(bf16[2,1024,256]{2,1,0:T(8,128)(2,1)} %mine_ref.1), channel_id=1, source_target_pairs={{0,2},{2,0},{4,6},{6,4},{8,10},{10,8},{12,14},{14,12},{1,3},{3,1},... | collective-permute-start | bytes 3145736 | tf_op jit(solution)/shard_map/ppermute | solution.py:402
  1.1 16.8 %collective-permute-start.1 = (bf16[4,128,256]{2,1,0:T(8,128)(2,1)}, bf16[4,128,256]{2,1,0:T(8,128)(2,1)S(1)}, u32[]{:S(2)}, u32[]{:S(2)}) collective-permute-start(bf16[4,128,256]{2,1,0:T(8,128)(2,1)} %here_ref.1), channel_id=1, source_target_pairs={{0,8},{2,10},{4,12},{6,14},{8,0},{10,2},{12,4},{14,6},{1,9},{3,11}... | collective-permute-start | bytes 786440 | tf_op jit(solution)/shard_map/ppermute | solution.py:398
  4.8 16.2 %collective-permute-start = (bf16[4,128,256]{2,1,0:T(8,128)(2,1)}, bf16[4,128,256]{2,1,0:T(8,128)(2,1)S(1)}, u32[]{:S(2)}, u32[]{:S(2)}) collective-permute-start(bf16[4,128,256]{2,1,0:T(8,128)(2,1)} %here_ref.1), channel_id=1, source_target_pairs={{0,4},{2,6},{4,0},{6,2},{8,12},{10,14},{12,8},{14,10},{1,5},{3,7},... | collective-permute-start | bytes 786440 | tf_op jit(solution)/shard_map/ppermute | solution.py:398
  6.4 2.2 %copy-start = (bf16[2,1024,1024]{2,1,0:T(8,128)(2,1)S(1)}, bf16[2,1024,1024]{2,1,0:T(8,128)(2,1)}, u32[]{:S(2)}) copy-start(bf16[2,1024,1024]{2,1,0:T(8,128)(2,1)} %full_ref.2) | copy-start | bytes 12582916
  8.6 3.9 %copy-start.6 = (f32[2]{0:T(128)S(1)}, f32[2]{0:T(128)}, u32[]{:S(2)}) copy-start(f32[2]{0:T(128)} %param.9) | copy-start | bytes 28
  8.6 4.0 %copy-start.5 = (f32[4,2]{0,1:T(2,128)S(1)}, f32[4,2]{0,1:T(2,128)}, u32[]{:S(2)}) copy-start(f32[4,2]{0,1:T(2,128)} %param.10) | copy-start | bytes 100
  9.4 25.4 %collective-permute-start.16 = (bf16[128,1024]{1,0:T(8,128)(2,1)}, bf16[128,1024]{1,0:T(8,128)(2,1)}, u32[]{:S(2)}, u32[]{:S(2)}) collective-permute-start(bf16[128,1024]{1,0:T(8,128)(2,1)} %get-tuple-element.21), channel_id=1, source_target_pairs={{0,8},{2,10},{4,12},{6,14},{8,0},{10,2},{12,4},{14,6},{1,9},{3,11}... | collective-permute-start | bytes 786440 | tf_op jit(solution)/shard_map/ppermute | solution.py:398
  9.8 30.3 %collective-permute-start.14 = (bf16[128,1024]{1,0:T(8,128)(2,1)}, bf16[128,1024]{1,0:T(8,128)(2,1)S(1)}, u32[]{:S(2)}, u32[]{:S(2)}) collective-permute-start(bf16[128,1024]{1,0:T(8,128)(2,1)} %get-tuple-element.29), channel_id=1, source_target_pairs={{0,8},{2,10},{4,12},{6,14},{8,0},{10,2},{12,4},{14,6},{1,9},{3,11}... | collective-permute-start | bytes 786440 | tf_op jit(solution)/shard_map/ppermute | solution.py:398
  18.0 2.4 %collective-permute-start.5 = (f32[16,128]{1,0:T(8,128)S(1)}, f32[16,128]{1,0:T(8,128)S(1)}, u32[]{:S(2)}, u32[]{:S(2)}) collective-permute-start(f32[16,128]{1,0:T(8,128)S(1)} %broadcast_in_dim.10.noise_ref), channel_id=1, source_target_pairs={{0,2},{2,0},{4,6},{6,4},{8,10},{10,8},{12,14},{14,12},{1,3},{3,1},... | collective-permute-start | bytes 24584 | tf_op jit(solution)/shard_map/ppermute | solution.py:402
  18.0 2.2 %copy-start.1 = (bf16[2,1024,1024]{2,1,0:T(8,128)(2,1)S(1)}, bf16[2,1024,1024]{2,1,0:T(8,128)(2,1)}, u32[]{:S(2)}) copy-start(bf16[2,1024,1024]{2,1,0:T(8,128)(2,1)} %full_ref.2) | copy-start | bytes 12582916
  20.2 44.3 %copy-start.2 = (f32[1,128,4,256]{3,2,1,0:T(4,128)S(1)}, f32[1,128,4,256]{3,2,1,0:T(4,128)}, u32[]{:S(2)}) copy-start(f32[1,128,4,256]{3,2,1,0:T(4,128)} %orbitals_ref.3) | copy-start | bytes 1572868
  20.2 44.9 %copy-start.3 = (bf16[2,1024,256]{2,1,0:T(8,128)(2,1)S(1)}, bf16[2,1024,256]{2,1,0:T(8,128)(2,1)}, u32[]{:S(2)}) copy-start(bf16[2,1024,256]{2,1,0:T(8,128)(2,1)} %mine_ref.1) | copy-start | bytes 3145732
  20.2 44.9 %copy-start.4 = (bf16[4,128,256]{2,1,0:T(8,128)(2,1)S(1)}, bf16[4,128,256]{2,1,0:T(8,128)(2,1)}, u32[]{:S(2)}) copy-start(bf16[4,128,256]{2,1,0:T(8,128)(2,1)} %here_ref.1) | copy-start | bytes 786436
  20.4 32.4 %collective-permute-start.8 = (bf16[2,128,1024]{2,1,0:T(8,128)(2,1)S(1)}, bf16[2,128,1024]{2,1,0:T(8,128)(2,1)S(1)}, u32[]{:S(2)}, u32[]{:S(2)}) collective-permute-start(bf16[2,128,1024]{2,1,0:T(8,128)(2,1)S(1)} %get-tuple-element.24), channel_id=1, source_target_pairs={{0,2},{2,0},{4,6},{6,4},{8,10},{10,8},{12,14},{14,12},{1,3},{3,1},... | collective-permute-start | bytes 1572872 | tf_op jit(solution)/shard_map/ppermute | solution.py:402
  21.0 19.9 %collective-permute-start.9 = (bf16[128,1024]{1,0:T(8,128)(2,1)S(1)}, bf16[128,1024]{1,0:T(8,128)(2,1)S(1)}, u32[]{:S(2)}, u32[]{:S(2)}) collective-permute-start(bf16[128,1024]{1,0:T(8,128)(2,1)S(1)} %get-tuple-element.27), channel_id=1, source_target_pairs={{0,4},{2,6},{4,0},{6,2},{8,12},{10,14},{12,8},{14,10},{1,5},{3,7},... | collective-permute-start | bytes 786440 | tf_op jit(solution)/shard_map/ppermute | solution.py:398
  34.8 11.0 %collective-permute-start.11 = (bf16[128,1024]{1,0:T(8,128)(2,1)S(1)}, bf16[128,1024]{1,0:T(8,128)(2,1)S(1)}, u32[]{:S(2)}, u32[]{:S(2)}) collective-permute-start(bf16[128,1024]{1,0:T(8,128)(2,1)S(1)} %get-tuple-element.28), channel_id=1, source_target_pairs={{0,4},{2,6},{4,0},{6,2},{8,12},{10,14},{12,8},{14,10},{1,5},{3,7},... | collective-permute-start | bytes 786440 | tf_op jit(solution)/shard_map/ppermute | solution.py:398
  40.2 11.1 %collective-permute-start.2 = (bf16[4,128,256]{2,1,0:T(8,128)(2,1)S(1)}, bf16[4,128,256]{2,1,0:T(8,128)(2,1)S(1)}, u32[]{:S(2)}, u32[]{:S(2)}) collective-permute-start(bf16[4,128,256]{2,1,0:T(8,128)(2,1)S(1)} %collective-permute-done.1.two_ref), channel_id=1, source_target_pairs={{0,4},{2,6},{4,0},{6,2},{8,12},{10,14},{12,8},{14,10},{1,5},{3,7},... | collective-permute-start | bytes 786440 | tf_op jit(solution)/shard_map/ppermute | solution.py:398
  40.9 12.0 %collective-permute-start.17 = (bf16[128,1024]{1,0:T(8,128)(2,1)}, bf16[128,1024]{1,0:T(8,128)(2,1)S(1)}, u32[]{:S(2)}, u32[]{:S(2)}) collective-permute-start(bf16[128,1024]{1,0:T(8,128)(2,1)} %collective-permute-done.16), channel_id=1, source_target_pairs={{0,2},{2,0},{4,6},{6,4},{8,10},{10,8},{12,14},{14,12},{1,3},{3,1},... | collective-permute-start | bytes 786440 | tf_op jit(solution)/shard_map/ppermute | solution.py:402
  45.8 8.1 %collective-permute-start.15 = (bf16[128,1024]{1,0:T(8,128)(2,1)S(1)}, bf16[128,1024]{1,0:T(8,128)(2,1)S(1)}, u32[]{:S(2)}, u32[]{:S(2)}) collective-permute-start(bf16[128,1024]{1,0:T(8,128)(2,1)S(1)} %collective-permute-done.14.refs_4_), channel_id=1, source_target_pairs={{0,1},{1,0},{2,3},{3,2},{4,5},{5,4},{6,7},{7,6},{8,9},{9,8},{10,11... | collective-permute-start | bytes 786440 | tf_op jit(solution)/shard_map/ppermute | solution.py:406
  51.3 9.2 %collective-permute-start.10 = (bf16[128,1024]{1,0:T(8,128)(2,1)S(1)}, bf16[128,1024]{1,0:T(8,128)(2,1)S(1)}, u32[]{:S(2)}, u32[]{:S(2)}) collective-permute-start(bf16[128,1024]{1,0:T(8,128)(2,1)S(1)} %collective-permute-done.9.refs_0_), channel_id=1, source_target_pairs={{0,1},{1,0},{2,3},{3,2},{4,5},{5,4},{6,7},{7,6},{8,9},{9,8},{10,11... | collective-permute-start | bytes 786440 | tf_op jit(solution)/shard_map/ppermute | solution.py:406
  52.9 13.3 %collective-permute-start.12 = (bf16[128,1024]{1,0:T(8,128)(2,1)S(1)}, bf16[128,1024]{1,0:T(8,128)(2,1)S(1)}, u32[]{:S(2)}, u32[]{:S(2)}) collective-permute-start(bf16[128,1024]{1,0:T(8,128)(2,1)S(1)} %collective-permute-done.11), channel_id=1, source_target_pairs={{0,2},{2,0},{4,6},{6,4},{8,10},{10,8},{12,14},{14,12},{1,3},{3,1},... | collective-permute-start | bytes 786440 | tf_op jit(solution)/shard_map/ppermute | solution.py:402
  52.9 13.4 %collective-permute-start.18 = (bf16[128,1024]{1,0:T(8,128)(2,1)S(1)}, bf16[128,1024]{1,0:T(8,128)(2,1)S(1)}, u32[]{:S(2)}, u32[]{:S(2)}) collective-permute-start(bf16[128,1024]{1,0:T(8,128)(2,1)S(1)} %collective-permute-done.17.refs_6_), channel_id=1, source_target_pairs={{0,1},{1,0},{2,3},{3,2},{4,5},{5,4},{6,7},{7,6},{8,9},{9,8},{10,11... | collective-permute-start | bytes 786440 | tf_op jit(solution)/shard_map/ppermute | solution.py:406
  53.9 12.9 %collective-permute-start.22 = (bf16[128,1024]{1,0:T(8,128)(2,1)S(1)}, bf16[128,1024]{1,0:T(8,128)(2,1)S(1)}, u32[]{:S(2)}, u32[]{:S(2)}) collective-permute-start(bf16[128,1024]{1,0:T(8,128)(2,1)S(1)} %get-tuple-element.33), channel_id=1, source_target_pairs={{0,12},{2,14},{4,8},{6,10},{8,4},{10,6},{12,0},{14,2},{1,13},{3,15... | collective-permute-start | bytes 786440 | tf_op jit(solution)/shard_map/ppermute | solution.py:398
  60.5 11.3 %collective-permute-start.20 = (bf16[128,1024]{1,0:T(8,128)(2,1)S(1)}, bf16[128,1024]{1,0:T(8,128)(2,1)S(1)}, u32[]{:S(2)}, u32[]{:S(2)}) collective-permute-start(bf16[128,1024]{1,0:T(8,128)(2,1)S(1)} %get-tuple-element.32), channel_id=1, source_target_pairs={{0,12},{2,14},{4,8},{6,10},{8,4},{10,6},{12,0},{14,2},{1,13},{3,15... | collective-permute-start | bytes 786440 | tf_op jit(solution)/shard_map/ppermute | solution.py:398
  65.0 25.2 %collective-permute-start.26 = (bf16[4,128,256]{2,1,0:T(8,128)(2,1)S(1)}, bf16[4,128,256]{2,1,0:T(8,128)(2,1)S(1)}, u32[]{:S(2)}, u32[]{:S(2)}) collective-permute-start(bf16[4,128,256]{2,1,0:T(8,128)(2,1)S(1)} %walker_major.1.refs_0_), channel_id=1, source_target_pairs={{0,8},{2,10},{4,12},{6,14},{8,0},{10,2},{12,4},{14,6},{1,9},{3,11}... | collective-permute-start | bytes 786440 | tf_op jit(solution)/shard_map/ppermute | solution.py:398
  66.1 25.6 %collective-permute-start.4 = (f32[16,128]{1,0:T(8,128)S(1)}, f32[16,128]{1,0:T(8,128)S(1)}, u32[]{:S(2)}, u32[]{:S(2)}) collective-permute-start(f32[16,128]{1,0:T(8,128)S(1)} %chip_bias.1.mine_ref), channel_id=1, source_target_pairs={{0,2},{2,0},{4,6},{6,4},{8,10},{10,8},{12,14},{14,12},{1,3},{3,1},... | collective-permute-start | bytes 24584 | tf_op jit(solution)/shard_map/ppermute | solution.py:402
  66.2 25.5 %collective-permute-start.25 = (bf16[4,128,256]{2,1,0:T(8,128)(2,1)S(1)}, bf16[4,128,256]{2,1,0:T(8,128)(2,1)S(1)}, u32[]{:S(2)}, u32[]{:S(2)}) collective-permute-start(bf16[4,128,256]{2,1,0:T(8,128)(2,1)S(1)} %walker_major.1.refs_0_), channel_id=1, source_target_pairs={{0,4},{2,6},{4,0},{6,2},{8,12},{10,14},{12,8},{14,10},{1,5},{3,7},... | collective-permute-start | bytes 786440 | tf_op jit(solution)/shard_map/ppermute | solution.py:398
  66.8 27.0 %collective-permute-start.13 = (bf16[128,1024]{1,0:T(8,128)(2,1)S(1)}, bf16[128,1024]{1,0:T(8,128)(2,1)S(1)}, u32[]{:S(2)}, u32[]{:S(2)}) collective-permute-start(bf16[128,1024]{1,0:T(8,128)(2,1)S(1)} %collective-permute-done.12.refs_2_), channel_id=1, source_target_pairs={{0,1},{1,0},{2,3},{3,2},{4,5},{5,4},{6,7},{7,6},{8,9},{9,8},{10,11... | collective-permute-start | bytes 786440 | tf_op jit(solution)/shard_map/ppermute | solution.py:406
  71.8 23.3 %collective-permute-start.23 = (bf16[128,1024]{1,0:T(8,128)(2,1)S(1)}, bf16[128,1024]{1,0:T(8,128)(2,1)S(1)}, u32[]{:S(2)}, u32[]{:S(2)}) collective-permute-start(bf16[128,1024]{1,0:T(8,128)(2,1)S(1)} %collective-permute-done.22), channel_id=1, source_target_pairs={{0,2},{2,0},{4,6},{6,4},{8,10},{10,8},{12,14},{14,12},{1,3},{3,1},... | collective-permute-start | bytes 786440 | tf_op jit(solution)/shard_map/ppermute | solution.py:402
  90.2 7.5 %collective-permute-start.21 = (bf16[128,1024]{1,0:T(8,128)(2,1)S(1)}, bf16[128,1024]{1,0:T(8,128)(2,1)S(1)}, u32[]{:S(2)}, u32[]{:S(2)}) collective-permute-start(bf16[128,1024]{1,0:T(8,128)(2,1)S(1)} %collective-permute-done.20.refs_0_), channel_id=1, source_target_pairs={{0,1},{1,0},{2,3},{3,2},{4,5},{5,4},{6,7},{7,6},{8,9},{9,8},{10,11... | collective-permute-start | bytes 786440 | tf_op jit(solution)/shard_map/ppermute | solution.py:406
  91.7 7.6 %collective-permute-start.30 = (bf16[4,128,256]{2,1,0:T(8,128)(2,1)S(1)}, bf16[4,128,256]{2,1,0:T(8,128)(2,1)S(1)}, u32[]{:S(2)}, u32[]{:S(2)}) collective-permute-start(bf16[4,128,256]{2,1,0:T(8,128)(2,1)S(1)} %collective-permute-done.26.refs_2_), channel_id=1, source_target_pairs={{0,4},{2,6},{4,0},{6,2},{8,12},{10,14},{12,8},{14,10},{1,5},{3,7},... | collective-permute-start | bytes 786440 | tf_op jit(solution)/shard_map/ppermute | solution.py:398
  91.7 8.1 %collective-permute-start.6 = (f32[16,128]{1,0:T(8,128)S(1)}, f32[16,128]{1,0:T(8,128)S(1)}, u32[]{:S(2)}, u32[]{:S(2)}) collective-permute-start(f32[16,128]{1,0:T(8,128)S(1)} %get-tuple-element.20.field_here), channel_id=1, source_target_pairs={{0,4},{2,6},{4,0},{6,2},{8,12},{10,14},{12,8},{14,10},{1,5},{3,7},... | collective-permute-start | bytes 24584 | tf_op jit(solution)/shard_map/ppermute | solution.py:398
  93.8 6.1 %collective-permute-start.7 = (f32[16,128]{1,0:T(8,128)S(1)}, f32[16,128]{1,0:T(8,128)S(1)}, u32[]{:S(2)}, u32[]{:S(2)}) collective-permute-start(f32[16,128]{1,0:T(8,128)S(1)} %get-tuple-element.20.field_here), channel_id=1, source_target_pairs={{0,8},{2,10},{4,12},{6,14},{8,0},{10,2},{12,4},{14,6},{1,9},{3,11}... | collective-permute-start | bytes 24584 | tf_op jit(solution)/shard_map/ppermute | solution.py:398
  95.1 5.4 %collective-permute-start.19 = (f32[16,128]{1,0:T(8,128)S(1)}, f32[16,128]{1,0:T(8,128)S(1)}, u32[]{:S(2)}, u32[]{:S(2)}) collective-permute-start(f32[16,128]{1,0:T(8,128)S(1)} %get-tuple-element.20.field_here), channel_id=1, source_target_pairs={{0,12},{2,14},{4,8},{6,10},{8,4},{10,6},{12,0},{14,2},{1,13},{3,15... | collective-permute-start | bytes 24584 | tf_op jit(solution)/shard_map/ppermute | solution.py:398
  97.7 10.3 %collective-permute-start.27 = (bf16[4,128,256]{2,1,0:T(8,128)(2,1)S(1)}, bf16[4,128,256]{2,1,0:T(8,128)(2,1)S(1)}, u32[]{:S(2)}, u32[]{:S(2)}) collective-permute-start(bf16[4,128,256]{2,1,0:T(8,128)(2,1)S(1)} %walker_major.1.refs_0_), channel_id=1, source_target_pairs={{0,2},{2,0},{4,6},{6,4},{8,10},{10,8},{12,14},{14,12},{1,3},{3,1},... | collective-permute-start | bytes 786440 | tf_op jit(solution)/shard_map/ppermute | solution.py:402
  99.3 7.2 %collective-permute-start.24 = (bf16[128,1024]{1,0:T(8,128)(2,1)S(1)}, bf16[128,1024]{1,0:T(8,128)(2,1)S(1)}, u32[]{:S(2)}, u32[]{:S(2)}) collective-permute-start(bf16[128,1024]{1,0:T(8,128)(2,1)S(1)} %collective-permute-done.23.refs_2_), channel_id=1, source_target_pairs={{0,1},{1,0},{2,3},{3,2},{4,5},{5,4},{6,7},{7,6},{8,9},{9,8},{10,11... | collective-permute-start | bytes 786440 | tf_op jit(solution)/shard_map/ppermute | solution.py:406
  99.9 8.2 %collective-permute-start.29 = (bf16[4,128,256]{2,1,0:T(8,128)(2,1)S(1)}, bf16[4,128,256]{2,1,0:T(8,128)(2,1)S(1)}, u32[]{:S(2)}, u32[]{:S(2)}) collective-permute-start(bf16[4,128,256]{2,1,0:T(8,128)(2,1)S(1)} %collective-permute-done.26.refs_2_), channel_id=1, source_target_pairs={{0,2},{2,0},{4,6},{6,4},{8,10},{10,8},{12,14},{14,12},{1,3},{3,1},... | collective-permute-start | bytes 786440 | tf_op jit(solution)/shard_map/ppermute | solution.py:402
  99.9 8.2 %collective-permute-start.28 = (bf16[4,128,256]{2,1,0:T(8,128)(2,1)S(1)}, bf16[4,128,256]{2,1,0:T(8,128)(2,1)S(1)}, u32[]{:S(2)}, u32[]{:S(2)}) collective-permute-start(bf16[4,128,256]{2,1,0:T(8,128)(2,1)S(1)} %collective-permute-done.25.refs_1_), channel_id=1, source_target_pairs={{0,2},{2,0},{4,6},{6,4},{8,10},{10,8},{12,14},{14,12},{1,3},{3,1},... | collective-permute-start | bytes 786440 | tf_op jit(solution)/shard_map/ppermute | solution.py:402
  100.5 8.3 %collective-permute-start.31 = (bf16[4,128,256]{2,1,0:T(8,128)(2,1)S(1)}, bf16[4,128,256]{2,1,0:T(8,128)(2,1)S(1)}, u32[]{:S(2)}, u32[]{:S(2)}) collective-permute-start(bf16[4,128,256]{2,1,0:T(8,128)(2,1)S(1)} %collective-permute-done.30.mine), channel_id=1, source_target_pairs={{0,2},{2,0},{4,6},{6,4},{8,10},{10,8},{12,14},{14,12},{1,3},{3,1},... | collective-permute-start | bytes 786440 | tf_op jit(solution)/shard_map/ppermute | solution.py:402
  109.2 12.7 %collective-permute-start.33 = (bf16[4,128,256]{2,1,0:T(8,128)(2,1)S(1)}, bf16[4,128,256]{2,1,0:T(8,128)(2,1)}, u32[]{:S(2)}, u32[]{:S(2)}) collective-permute-start(bf16[4,128,256]{2,1,0:T(8,128)(2,1)S(1)} %get-tuple-element.35.refs_0_), channel_id=1, source_target_pairs={{0,8},{2,10},{4,12},{6,14},{8,0},{10,2},{12,4},{14,6},{1,9},{3,11}... | collective-permute-start | bytes 786440 | tf_op jit(solution)/shard_map/ppermute | solution.py:398
  110.0 12.1 %collective-permute-start.32 = (bf16[4,128,256]{2,1,0:T(8,128)(2,1)S(1)}, bf16[4,128,256]{2,1,0:T(8,128)(2,1)}, u32[]{:S(2)}, u32[]{:S(2)}) collective-permute-start(bf16[4,128,256]{2,1,0:T(8,128)(2,1)S(1)} %get-tuple-element.35.refs_0_), channel_id=1, source_target_pairs={{0,4},{2,6},{4,0},{6,2},{8,12},{10,14},{12,8},{14,10},{1,5},{3,7},... | collective-permute-start | bytes 786440 | tf_op jit(solution)/shard_map/ppermute | solution.py:398
  121.9 8.4 %collective-permute-start.37 = (bf16[4,128,256]{2,1,0:T(8,128)(2,1)}, bf16[4,128,256]{2,1,0:T(8,128)(2,1)}, u32[]{:S(2)}, u32[]{:S(2)}) collective-permute-start(bf16[4,128,256]{2,1,0:T(8,128)(2,1)} %collective-permute-done.33.refs_2_), channel_id=1, source_target_pairs={{0,4},{2,6},{4,0},{6,2},{8,12},{10,14},{12,8},{14,10},{1,5},{3,7},... | collective-permute-start | bytes 786440 | tf_op jit(solution)/shard_map/ppermute | solution.py:398
  121.9 9.2 %collective-permute-start.34 = (bf16[4,128,256]{2,1,0:T(8,128)(2,1)S(1)}, bf16[4,128,256]{2,1,0:T(8,128)(2,1)}, u32[]{:S(2)}, u32[]{:S(2)}) collective-permute-start(bf16[4,128,256]{2,1,0:T(8,128)(2,1)S(1)} %get-tuple-element.35.refs_0_), channel_id=1, source_target_pairs={{0,2},{2,0},{4,6},{6,4},{8,10},{10,8},{12,14},{14,12},{1,3},{3,1},... | collective-permute-start | bytes 786440 | tf_op jit(solution)/shard_map/ppermute | solution.py:402
  122.1 9.0 %collective-permute-start.35 = (bf16[4,128,256]{2,1,0:T(8,128)(2,1)}, bf16[4,128,256]{2,1,0:T(8,128)(2,1)}, u32[]{:S(2)}, u32[]{:S(2)}) collective-permute-start(bf16[4,128,256]{2,1,0:T(8,128)(2,1)} %collective-permute-done.32.refs_1_), channel_id=1, source_target_pairs={{0,2},{2,0},{4,6},{6,4},{8,10},{10,8},{12,14},{14,12},{1,3},{3,1},... | collective-permute-start | bytes 786440 | tf_op jit(solution)/shard_map/ppermute | solution.py:402
  122.5 8.7 %collective-permute-start.36 = (bf16[4,128,256]{2,1,0:T(8,128)(2,1)}, bf16[4,128,256]{2,1,0:T(8,128)(2,1)}, u32[]{:S(2)}, u32[]{:S(2)}) collective-permute-start(bf16[4,128,256]{2,1,0:T(8,128)(2,1)} %collective-permute-done.33.refs_2_), channel_id=1, source_target_pairs={{0,2},{2,0},{4,6},{6,4},{8,10},{10,8},{12,14},{14,12},{1,3},{3,1},... | collective-permute-start | bytes 786440 | tf_op jit(solution)/shard_map/ppermute | solution.py:402
  130.4 2.7 %collective-permute-start.38 = (bf16[4,128,256]{2,1,0:T(8,128)(2,1)}, bf16[4,128,256]{2,1,0:T(8,128)(2,1)}, u32[]{:S(2)}, u32[]{:S(2)}) collective-permute-start(bf16[4,128,256]{2,1,0:T(8,128)(2,1)} %collective-permute-done.37.mine), channel_id=1, source_target_pairs={{0,2},{2,0},{4,6},{6,4},{8,10},{10,8},{12,14},{14,12},{1,3},{3,1},... | collective-permute-start | bytes 786440 | tf_op jit(solution)/shard_map/ppermute | solution.py:402

commit v5 on v4

--- a/solution.py
+++ b/solution.py
@@ -60,10 +60,11 @@
 
 
 vmem_spec = pl.BlockSpec(memory_space=pltpu.VMEM)
-any_spec = pl.BlockSpec(memory_space=pl.ANY)
+hbm_spec = pl.BlockSpec(memory_space=pltpu.HBM)
 wide = jnp.float32
 narrow = jnp.bfloat16
-small = pltpu.CompilerParams(vmem_limit_bytes=16 << 20)
+small = pltpu.CompilerParams(vmem_limit_bytes=8 << 20)
+large = pltpu.CompilerParams(vmem_limit_bytes=16 << 20)
 
 
 def after(value, *others):
@@ -103,7 +104,7 @@
     return pl.pallas_call(
         functools.partial(cut_kernel, rows, wanted),
         out_shape=shapes,
-        in_specs=[any_spec],
+        in_specs=[hbm_spec],
         out_specs=[vmem_spec] * len(wanted),
         scratch_shapes=[pltpu.SemaphoreType.DMA((len(wanted),))],
         compiler_params=small,
@@ -183,15 +184,18 @@
         shift = jnp.clip(time_root * (force - consts[high, :]), -1.0, 1.0)
         field_ref[rows, :] = consts[low, :] - shift
         if rows is low:
-            shift_ref[...] = shift
-
-
-def chip_field(mine, theirs, noise, noise_there):
+            walkers, vectors = shift_ref.shape
+            for vector in range(vectors):
+                part = shift[vector * walkers : (vector + 1) * walkers, :1]
+                shift_ref[:, vector : vector + 1] = part
+
+
+def chip_field(mine, theirs, noise, noise_there, walkers):
     entries = mine.shape[0]
     return pl.pallas_call(
         field_kernel,
         out_shape=[
-            jax.ShapeDtypeStruct((entries // 2, 128), wide),
+            jax.ShapeDtypeStruct((walkers, entries // 2 // walkers), wide),
             jax.ShapeDtypeStruct((entries, 128), wide),
         ],
         in_specs=[vmem_spec] * 4,
@@ -271,7 +275,7 @@
         out_shape=jax.ShapeDtypeStruct((walkers, rows, order), wide),
         in_specs=[vmem_spec] * (5 + len(blocks)),
         out_specs=vmem_spec,
-        compiler_params=small,
+        compiler_params=large,
         name="early_operator",
     )(*fields, own, own_theirs, *blocks)
 
@@ -304,7 +308,7 @@
         out_shape=jax.ShapeDtypeStruct((walkers, 2 * rows, order), narrow),
         in_specs=[vmem_spec] * (2 + len(blocks)),
         out_specs=vmem_spec,
-        compiler_params=small,
+        compiler_params=large,
         name="split_operator",
     )(summed, field, *blocks)
 
@@ -416,45 +420,43 @@
     constants = jnp.broadcast_to(constants[:, None], (2 * vectors * walkers, 128))
     constants_theirs = to_core(constants)
 
+    green_three = to_chip(green_two, 1)
+
     cross, straight = {}, {}
     cross[2], straight[2] = cut(rows, full_chol, ((2, True, False), (2, False, False)))
-    cross[1], straight[1], cross[3], straight[3], own, own_cross = cut(
+    cross[3], straight[3], cross[1], straight[1], own, own_cross = cut(
         rows,
         after(full_chol, cross[2]),
         (
+            (3, True, False),
+            (3, False, False),
             (1, True, False),
             (1, False, False),
-            (3, True, False),
-            (3, False, False),
             (0, False, True),
             (0, True, True),
         ),
     )
     own_theirs = to_core(own_cross)
+
+    green = (green_blocks, green_one, green_two, green_three)
+    bias = chip_bias(green, half_chol, half_theirs)
+    bias_shift, field = chip_field(bias, to_core(bias), constants, constants_theirs, walkers)
+    field_one, field_two, field_three = (to_chip(field, step) for step in (1, 2, 3))
+
+    cross_mine, mine = {}, {}
+    cross_mine[2], mine[2] = to_chip(cross[2], 2), to_chip(straight[2], 2)
+    cross_mine[3] = to_chip(cross[3], 3)
+    mine[3] = to_chip(after(straight[3], cross_mine[2]), 3)
+    cross_mine[1] = to_chip(after(cross[1], green_three), 1)
+    mine[1] = to_chip(after(straight[1], field_one), 1)
     blocks = {}
-
-    def exchange(step):
-        theirs = to_core(to_chip(cross[step], step))
-        mine = to_chip(straight[step], step)
-        blocks[step] = (mine, across(mine), theirs, across(theirs))
-        return mine
-
-    second_mine = exchange(2)
-    green_three = to_chip(green_two, 1)
-    cross[1], straight[1] = after((cross[1], straight[1]), green_two)
-    first_mine = exchange(1)
-    cross[3], straight[3] = after((cross[3], straight[3]), green_three)
-    exchange(3)
-
-    start = after(walker_major(orbitals), second_mine, first_mine)
+    for step in (2, 3, 1):
+        theirs = to_core(cross_mine[step])
+        blocks[step] = (mine[step], across(mine[step]), theirs, across(theirs))
+
+    start = after(walker_major(orbitals), mine[2], cross_mine[3])
     start_two, start_one = to_chip(start, 2), to_chip(start, 1)
     start_three = to_chip(start_two, 1)
-
-    green = (green_blocks, green_one, green_two, green_three)
-    bias = chip_bias(green, half_chol, half_theirs)
-    shift_rows, field = chip_field(bias, to_core(bias), constants, constants_theirs)
-    field_one, field_two, field_three = (to_chip(field, step) for step in (1, 2, 3))
-    bias_shift = shift_rows[:, 0].reshape(vectors, walkers).T
 
     summed = early_operator(
         walkers,

time: 136 us -> 137 us (level)
  starting transfers between devices: 35.8 us -> 51.9 us
  waiting for transfers between devices: 80.4 us -> 66.5 us
    ppermute x18, waiting for transfers between devices: 73.2 us -> 50.4 us  [to_chip(): return lax.ppermute(value, 'chol', [(i, i ^ 2 * step) for i in range(8)])]
    ppermute x18, starting transfers between devices: 26.5 us -> 36.8 us  [to_chip(): return lax.ppermute(value, 'chol', [(i, i ^ 2 * step) for i in range(8)])]
    ppermute x6, waiting for transfers between devices: 7.14 us -> 15.4 us  [across(): return lax.ppermute(value, 'walk', [(0, 1), (1, 0)])]
    ppermute x6, starting transfers between devices: 7.17 us -> 12.7 us  [across(): return lax.ppermute(value, 'walk', [(0, 1), (1, 0)])]
    unnamed x14 -> x15, local copies, waits for them, and re-layouts: 4.4 us -> 5.23 us
  transfers between devices with their start and end apart: 39 -> 39, of which waited for: 16 -> 17; matrix products, arithmetic and copies ran while one was open for 1% -> 1% of each run, Pallas kernels for 8% -> 7%
where the time goes in v5:
time: 137 us
  waiting for transfers between devices  66.5 us (49%)
  starting transfers between devices  51.9 us (38%)
  Pallas kernels  12.2 us (9%)
  local copies, waits for them, and re-layouts  5.54 us (4%)
    ppermute x18, waiting for transfers between devices, to_chip(): return lax.ppermute(value, 'chol', [(i, i ^ 2 * step) for i in range(8)])  50.4 us
    ppermute x18, starting transfers between devices, to_chip(): return lax.ppermute(value, 'chol', [(i, i ^ 2 * step) for i in range(8)])  36.8 us
    ppermute x6, waiting for transfers between devices, across(): return lax.ppermute(value, 'walk', [(0, 1), (1, 0)])  15.4 us
    ppermute x6, starting transfers between devices, across(): return lax.ppermute(value, 'walk', [(0, 1), (1, 0)])  12.7 us
    unnamed x15, local copies, waits for them, and re-layouts  5.23 us
    pallas_call x1, Pallas kernels, early_operator(): pl.pallas_call(functools.partial(early_kernel, walkers), out_shape=jax.Sh...  3.33 us
  transfers between devices with their start and end apart: 39, of which 17 were waited for; matrix products, arithmetic and copies ran while one was open for 1% of the time, Pallas kernels for 7%

profile of v5, /device:TPU:0, one launch (start us, length us, event | category | flops | bytes accessed | tf_op | source)
XLA Modules:
  0.0 137.0 jit_solution(5479168299949265937)
XLA Ops:
  0.6 0.5 collective-permute-start.3
  1.1 3.7 %collective-permute-start.1 = (bf16[4,128,256]{2,1,0:T(8,128)(2,1)}, bf16[4,128,256]{2,1,0:T(8,128)(2,1)S(1)}, u32[]{:S(2)}, u32[]{:S(2)}) collective-permute-start(bf16[4,128,256]{2,1,0:T(8,128)(2,1)} %here_ref.1), channel_id=1, source_target_pairs={{0,8},{2,10},{4,12},{6,14},{8,0},{10,2},{12,4},{14,6},{1,9},{3,11}... | collective-permute-start | bytes 786440 | tf_op jit(solution)/shard_map/ppermute | solution.py:402
  4.8 1.6 %collective-permute-start = (bf16[4,128,256]{2,1,0:T(8,128)(2,1)}, bf16[4,128,256]{2,1,0:T(8,128)(2,1)S(1)}, u32[]{:S(2)}, u32[]{:S(2)}) collective-permute-start(bf16[4,128,256]{2,1,0:T(8,128)(2,1)} %here_ref.1), channel_id=1, source_target_pairs={{0,4},{2,6},{4,0},{6,2},{8,12},{10,14},{12,8},{14,10},{1,5},{3,7},... | collective-permute-start | bytes 786440 | tf_op jit(solution)/shard_map/ppermute | solution.py:402
  6.4 2.2 %copy-done = bf16[2,1024,1024]{2,1,0:T(8,128)(2,1)S(1)} copy-done((bf16[2,1024,1024]{2,1,0:T(8,128)(2,1)S(1)}, bf16[2,1024,1024]{2,1,0:T(8,128)(2,1)}, u32[]{:S(2)}) %copy-start) | copy-done | bytes 4194328
  8.6 0.4 collective-permute-start.16
  9.6 2.2 %copy-done.1 = bf16[2,1024,1024]{2,1,0:T(8,128)(2,1)S(1)} copy-done((bf16[2,1024,1024]{2,1,0:T(8,128)(2,1)S(1)}, bf16[2,1024,1024]{2,1,0:T(8,128)(2,1)}, u32[]{:S(2)}) %copy-start.1) | copy-done | bytes 4194328
  12.1 0.6 collective-permute-start.8
  12.6 5.3 %collective-permute-done.1.two_ref = bf16[4,128,256]{2,1,0:T(8,128)(2,1)S(1)} collective-permute-done((bf16[4,128,256]{2,1,0:T(8,128)(2,1)}, bf16[4,128,256]{2,1,0:T(8,128)(2,1)S(1)}, u32[]{:S(2)}, u32[]{:S(2)}) %collective-permute-start.1) | collective-permute-done | bytes 262176 | tf_op jit(solution)/shard_map/ppermute | solution.py:402
  17.9 0.8 collective-permute-done.one_ref
  18.7 3.4 %collective-permute-start.2 = (bf16[4,128,256]{2,1,0:T(8,128)(2,1)S(1)}, bf16[4,128,256]{2,1,0:T(8,128)(2,1)S(1)}, u32[]{:S(2)}, u32[]{:S(2)}) collective-permute-start(bf16[4,128,256]{2,1,0:T(8,128)(2,1)S(1)} %collective-permute-done.1.two_ref), channel_id=1, source_target_pairs={{0,4},{2,6},{4,0},{6,2},{8,12},{10,14},{12,8},{14,10},{1,5},{3,7},... | collective-permute-start | bytes 786440 | tf_op jit(solution)/shard_map/ppermute | solution.py:402
  22.2 12.5 %collective-permute-done.16 = bf16[128,1024]{1,0:T(8,128)(2,1)S(1)} collective-permute-done((bf16[128,1024]{1,0:T(8,128)(2,1)S(1)}, bf16[128,1024]{1,0:T(8,128)(2,1)S(1)}, u32[]{:S(2)}, u32[]{:S(2)}) %collective-permute-start.16) | collective-permute-done | bytes 262176 | tf_op jit(solution)/shard_map/ppermute | solution.py:402
  34.7 3.3 %collective-permute-start.22 = (bf16[128,1024]{1,0:T(8,128)(2,1)S(1)}, bf16[128,1024]{1,0:T(8,128)(2,1)S(1)}, u32[]{:S(2)}, u32[]{:S(2)}) collective-permute-start(bf16[128,1024]{1,0:T(8,128)(2,1)S(1)} %get-tuple-element.31), channel_id=1, source_target_pairs={{0,12},{2,14},{4,8},{6,10},{8,4},{10,6},{12,0},{14,2},{1,13},{3,15... | collective-permute-start | bytes 786440 | tf_op jit(solution)/shard_map/ppermute | solution.py:402
  38.0 7.9 %collective-permute-done.14.refs_4_ = bf16[128,1024]{1,0:T(8,128)(2,1)S(1)} collective-permute-done((bf16[128,1024]{1,0:T(8,128)(2,1)S(1)}, bf16[128,1024]{1,0:T(8,128)(2,1)S(1)}, u32[]{:S(2)}, u32[]{:S(2)}) %collective-permute-start.14) | collective-permute-done | bytes 262176 | tf_op jit(solution)/shard_map/ppermute | solution.py:402
  45.9 1.7 %collective-permute-start.15 = (bf16[128,1024]{1,0:T(8,128)(2,1)S(1)}, bf16[128,1024]{1,0:T(8,128)(2,1)S(1)}, u32[]{:S(2)}, u32[]{:S(2)}) collective-permute-start(bf16[128,1024]{1,0:T(8,128)(2,1)S(1)} %collective-permute-done.14.refs_4_), channel_id=1, source_target_pairs={{0,1},{1,0},{2,3},{3,2},{4,5},{5,4},{6,7},{7,6},{8,9},{9,8},{10,11... | collective-permute-start | bytes 786440 | tf_op jit(solution)/shard_map/ppermute | solution.py:410
  47.7 3.1 %collective-permute-start.20 = (bf16[128,1024]{1,0:T(8,128)(2,1)S(1)}, bf16[128,1024]{1,0:T(8,128)(2,1)S(1)}, u32[]{:S(2)}, u32[]{:S(2)}) collective-permute-start(bf16[128,1024]{1,0:T(8,128)(2,1)S(1)} %get-tuple-element.30), channel_id=1, source_target_pairs={{0,12},{2,14},{4,8},{6,10},{8,4},{10,6},{12,0},{14,2},{1,13},{3,15... | collective-permute-start | bytes 786440 | tf_op jit(solution)/shard_map/ppermute | solution.py:402
  50.8 3.7 %collective-permute-start.11 = (bf16[128,1024]{1,0:T(8,128)(2,1)S(1)}, bf16[128,1024]{1,0:T(8,128)(2,1)S(1)}, u32[]{:S(2)}, u32[]{:S(2)}) collective-permute-start(bf16[128,1024]{1,0:T(8,128)(2,1)S(1)} %get-tuple-element.27), channel_id=1, source_target_pairs={{0,4},{2,6},{4,0},{6,2},{8,12},{10,14},{12,8},{14,10},{1,5},{3,7},... | collective-permute-start | bytes 786440 | tf_op jit(solution)/shard_map/ppermute | solution.py:402
  54.5 1.0 chip_bias.1.mine_ref
  55.6 0.5 walker_major.1.refs_0_
  56.1 0.6 collective-permute-done.4.theirs_ref
  57.0 1.4 %collective-permute-start.6 = (f32[16,128]{1,0:T(8,128)S(1)}, f32[16,128]{1,0:T(8,128)S(1)}, u32[]{:S(2)}, u32[]{:S(2)}) collective-permute-start(f32[16,128]{1,0:T(8,128)S(1)} %get-tuple-element.19.field_here), channel_id=1, source_target_pairs={{0,4},{2,6},{4,0},{6,2},{8,12},{10,14},{12,8},{14,10},{1,5},{3,7},... | collective-permute-start | bytes 24584 | tf_op jit(solution)/shard_map/ppermute | solution.py:402
  58.7 6.2 %collective-permute-start.25 = (bf16[4,128,256]{2,1,0:T(8,128)(2,1)S(1)}, bf16[4,128,256]{2,1,0:T(8,128)(2,1)S(1)}, u32[]{:S(2)}, u32[]{:S(2)}) collective-permute-start(bf16[4,128,256]{2,1,0:T(8,128)(2,1)S(1)} %walker_major.1.refs_0_), channel_id=1, source_target_pairs={{0,4},{2,6},{4,0},{6,2},{8,12},{10,14},{12,8},{14,10},{1,5},{3,7},... | collective-permute-start | bytes 786440 | tf_op jit(solution)/shard_map/ppermute | solution.py:402
  64.9 3.8 %collective-permute-start.18 = (bf16[128,1024]{1,0:T(8,128)(2,1)S(1)}, bf16[128,1024]{1,0:T(8,128)(2,1)S(1)}, u32[]{:S(2)}, u32[]{:S(2)}) collective-permute-start(bf16[128,1024]{1,0:T(8,128)(2,1)S(1)} %collective-permute-done.17.refs_6_), channel_id=1, source_target_pairs={{0,1},{1,0},{2,3},{3,2},{4,5},{5,4},{6,7},{7,6},{8,9},{9,8},{10,11... | collective-permute-start | bytes 786440 | tf_op jit(solution)/shard_map/ppermute | solution.py:410
  68.9 2.5 %collective-permute-start.9 = (bf16[128,1024]{1,0:T(8,128)(2,1)S(1)}, bf16[128,1024]{1,0:T(8,128)(2,1)S(1)}, u32[]{:S(2)}, u32[]{:S(2)}) collective-permute-start(bf16[128,1024]{1,0:T(8,128)(2,1)S(1)} %get-tuple-element.25), channel_id=1, source_target_pairs={{0,4},{2,6},{4,0},{6,2},{8,12},{10,14},{12,8},{14,10},{1,5},{3,7},... | collective-permute-start | bytes 786440 | tf_op jit(solution)/shard_map/ppermute | solution.py:402
  71.4 3.5 %collective-permute-done.26.refs_2_ = bf16[4,128,256]{2,1,0:T(8,128)(2,1)S(1)} collective-permute-done((bf16[4,128,256]{2,1,0:T(8,128)(2,1)S(1)}, bf16[4,128,256]{2,1,0:T(8,128)(2,1)S(1)}, u32[]{:S(2)}, u32[]{:S(2)}) %collective-permute-start.26) | collective-permute-done | bytes 262176 | tf_op jit(solution)/shard_map/ppermute | solution.py:402
  74.9 4.3 %collective-permute-start.21 = (bf16[128,1024]{1,0:T(8,128)(2,1)S(1)}, bf16[128,1024]{1,0:T(8,128)(2,1)S(1)}, u32[]{:S(2)}, u32[]{:S(2)}) collective-permute-start(bf16[128,1024]{1,0:T(8,128)(2,1)S(1)} %collective-permute-done.20.refs_0_), channel_id=1, source_target_pairs={{0,1},{1,0},{2,3},{3,2},{4,5},{5,4},{6,7},{7,6},{8,9},{9,8},{10,11... | collective-permute-start | bytes 786440 | tf_op jit(solution)/shard_map/ppermute | solution.py:410
  79.2 0.5 collective-permute-start.24
  79.8 2.5 %collective-permute-start.30 = (bf16[4,128,256]{2,1,0:T(8,128)(2,1)S(1)}, bf16[4,128,256]{2,1,0:T(8,128)(2,1)S(1)}, u32[]{:S(2)}, u32[]{:S(2)}) collective-permute-start(bf16[4,128,256]{2,1,0:T(8,128)(2,1)S(1)} %collective-permute-done.26.refs_2_), channel_id=1, source_target_pairs={{0,4},{2,6},{4,0},{6,2},{8,12},{10,14},{12,8},{14,10},{1,5},{3,7},... | collective-permute-start | bytes 786440 | tf_op jit(solution)/shard_map/ppermute | solution.py:402
  82.2 0.8 collective-permute-done.9.refs_0_
  83.1 2.3 %collective-permute-start.10 = (bf16[128,1024]{1,0:T(8,128)(2,1)S(1)}, bf16[128,1024]{1,0:T(8,128)(2,1)S(1)}, u32[]{:S(2)}, u32[]{:S(2)}) collective-permute-start(bf16[128,1024]{1,0:T(8,128)(2,1)S(1)} %collective-permute-done.9.refs_0_), channel_id=1, source_target_pairs={{0,1},{1,0},{2,3},{3,2},{4,5},{5,4},{6,7},{7,6},{8,9},{9,8},{10,11... | collective-permute-start | bytes 786440 | tf_op jit(solution)/shard_map/ppermute | solution.py:410
  85.4 1.0 collective-permute-done.21.refs_1_
  86.4 0.9 collective-permute-start.7
  87.3 4.7 %collective-permute-done.24.refs_3_ = bf16[128,1024]{1,0:T(8,128)(2,1)S(1)} collective-permute-done((bf16[128,1024]{1,0:T(8,128)(2,1)S(1)}, bf16[128,1024]{1,0:T(8,128)(2,1)S(1)}, u32[]{:S(2)}, u32[]{:S(2)}) %collective-permute-start.24) | collective-permute-done | bytes 262176 | tf_op jit(solution)/shard_map/ppermute | solution.py:410
  92.0 0.5 collective-permute-start.29
  92.6 5.0 %collective-permute-done.13.refs_3_ = bf16[128,1024]{1,0:T(8,128)(2,1)S(1)} collective-permute-done((bf16[128,1024]{1,0:T(8,128)(2,1)S(1)}, bf16[128,1024]{1,0:T(8,128)(2,1)S(1)}, u32[]{:S(2)}, u32[]{:S(2)}) %collective-permute-start.13) | collective-permute-done | bytes 262176 | tf_op jit(solution)/shard_map/ppermute | solution.py:410
  97.6 4.7 %collective-permute-done.10.refs_1_ = bf16[128,1024]{1,0:T(8,128)(2,1)S(1)} collective-permute-done((bf16[128,1024]{1,0:T(8,128)(2,1)S(1)}, bf16[128,1024]{1,0:T(8,128)(2,1)S(1)}, u32[]{:S(2)}, u32[]{:S(2)}) %collective-permute-start.10) | collective-permute-done | bytes 262176 | tf_op jit(solution)/shard_map/ppermute | solution.py:410
  102.3 1.7 %collective-permute-start.19 = (f32[16,128]{1,0:T(8,128)S(1)}, f32[16,128]{1,0:T(8,128)S(1)}, u32[]{:S(2)}, u32[]{:S(2)}) collective-permute-start(f32[16,128]{1,0:T(8,128)S(1)} %get-tuple-element.19.field_here), channel_id=1, source_target_pairs={{0,12},{2,14},{4,8},{6,10},{8,4},{10,6},{12,0},{14,2},{1,13},{3,15... | collective-permute-start | bytes 24584 | tf_op jit(solution)/shard_map/ppermute | solution.py:402
  104.0 3.3 %early_operator.1.summed_ref = f32[4,128,1024]{2,1,0:T(8,128)S(1)} custom-call(f32[16,128]{1,0:T(8,128)S(1)} %get-tuple-element.19.field_here, f32[16,128]{1,0:T(8,128)S(1)} %collective-permute-done.6.field_one, f32[16,128]{1,0:T(8,128)S(1)} %collective-permute-done.7.field_two, bf16[2,128,1024]{2,1,0:T(8,128)(2,1)S(1)} %get-tuple-element.22.own, ...), custom_call_target="tpu_custom_call" | custom-call | tf_op jit(solution)/shard_map/early_operator/pallas_call | solution.py:273
  107.3 0.4 collective-permute-done.19.field_ref
  107.7 1.6 %split_operator.1.operator_ref = bf16[4,256,1024]{2,1,0:T(8,128)(2,1)S(1)} custom-call(f32[4,128,1024]{2,1,0:T(8,128)S(1)} %early_operator.1.summed_ref, f32[16,128]{1,0:T(8,128)S(1)} %collective-permute-done.19.field_ref, bf16[128,1024]{1,0:T(8,128)(2,1)S(1)} %collective-permute-done.20.refs_0_, bf16[128,1024]{1,0:T(8,128)(2,1)S(1)} %collective-permute-done.21.refs_1_, ...), custom_call_target="tpu_custom_call" | custom-call | tf_op jit(solution)/shard_map/split_operator/pallas_call | solution.py:306
  109.4 0.7 near_application.2.partial_ref
  110.1 0.4 first_application.1
  110.5 2.3 %collective-permute-start.32 = (bf16[4,128,256]{2,1,0:T(8,128)(2,1)S(1)}, bf16[4,128,256]{2,1,0:T(8,128)(2,1)}, u32[]{:S(2)}, u32[]{:S(2)}) collective-permute-start(bf16[4,128,256]{2,1,0:T(8,128)(2,1)S(1)} %get-tuple-element.33.refs_0_), channel_id=1, source_target_pairs={{0,4},{2,6},{4,0},{6,2},{8,12},{10,14},{12,8},{14,10},{1,5},{3,7},... | collective-permute-start | bytes 786440 | tf_op jit(solution)/shard_map/ppermute | solution.py:402
  112.8 10.6 %collective-permute-done.33.refs_2_ = bf16[4,128,256]{2,1,0:T(8,128)(2,1)} collective-permute-done((bf16[4,128,256]{2,1,0:T(8,128)(2,1)S(1)}, bf16[4,128,256]{2,1,0:T(8,128)(2,1)}, u32[]{:S(2)}, u32[]{:S(2)}) %collective-permute-start.33) | collective-permute-done | bytes 262176 | tf_op jit(solution)/shard_map/ppermute | solution.py:402
  123.6 0.4 collective-permute-start.35
  124.1 7.8 %collective-permute-done.37.mine = bf16[4,128,256]{2,1,0:T(8,128)(2,1)} collective-permute-done((bf16[4,128,256]{2,1,0:T(8,128)(2,1)}, bf16[4,128,256]{2,1,0:T(8,128)(2,1)}, u32[]{:S(2)}, u32[]{:S(2)}) %collective-permute-start.37) | collective-permute-done | bytes 262176 | tf_op jit(solution)/shard_map/ppermute | solution.py:402
  131.9 0.6 copy.8
  132.6 1.9 %near_application.3.partial_ref = f32[4,128,256]{2,1,0:T(8,128)S(1)} custom-call(bf16[4,256,1024]{2,1,0:T(8,128)(2,1)S(1)} %split_operator.1.operator_ref, bf16[4,128,256]{2,1,0:T(8,128)(2,1)S(1)} %get-tuple-element.33.refs_0_, bf16[4,128,256]{2,1,0:T(8,128)(2,1)} %collective-permute-done.32.refs_1_, bf16[4,128,256]{2,1,0:T(8,128)(2,1)} %collective-permute-done.33.refs_2_, ...), custom_call_target="tpu_custom_call" | custom-call | tf_op jit(solution)/shard_map/near_application/pallas_call | solution.py:346
  134.6 2.4 %second_application.1 = f32[1,128,4,256]{3,2,1,0:T(4,128)} custom-call(bf16[4,256,1024]{2,1,0:T(8,128)(2,1)S(1)} %split_operator.1.operator_ref, f32[4,128,256]{2,1,0:T(8,128)S(1)} %near_application.3.partial_ref, f32[4,128,256]{2,1,0:T(8,128)S(1)} %get-tuple-element.34.first_ref, f32[1,128,4,256]{3,2,1,0:T(4,128)S(1)} %copy-done.2, ...), custom_call_target="tpu_custom_call" | custom-call | tf_op jit(solution)/shard_map/second_application/pallas_call | solution.py:390
  (61 shorter events, 2.2 us)
Async XLA Ops:
  0.6 50.1 %collective-permute-start.3 = (bf16[2,1024,256]{2,1,0:T(8,128)(2,1)}, bf16[2,1024,256]{2,1,0:T(8,128)(2,1)S(1)}, u32[]{:S(2)}, u32[]{:S(2)}) collective-permute-start(bf16[2,1024,256]{2,1,0:T(8,128)(2,1)} %mine_ref.1), channel_id=1, source_target_pairs={{0,2},{2,0},{4,6},{6,4},{8,10},{10,8},{12,14},{14,12},{1,3},{3,1},... | collective-permute-start | bytes 3145736 | tf_op jit(solution)/shard_map/ppermute | solution.py:406
  1.1 16.8 %collective-permute-start.1 = (bf16[4,128,256]{2,1,0:T(8,128)(2,1)}, bf16[4,128,256]{2,1,0:T(8,128)(2,1)S(1)}, u32[]{:S(2)}, u32[]{:S(2)}) collective-permute-start(bf16[4,128,256]{2,1,0:T(8,128)(2,1)} %here_ref.1), channel_id=1, source_target_pairs={{0,8},{2,10},{4,12},{6,14},{8,0},{10,2},{12,4},{14,6},{1,9},{3,11}... | collective-permute-start | bytes 786440 | tf_op jit(solution)/shard_map/ppermute | solution.py:402
  4.8 13.9 %collective-permute-start = (bf16[4,128,256]{2,1,0:T(8,128)(2,1)}, bf16[4,128,256]{2,1,0:T(8,128)(2,1)S(1)}, u32[]{:S(2)}, u32[]{:S(2)}) collective-permute-start(bf16[4,128,256]{2,1,0:T(8,128)(2,1)} %here_ref.1), channel_id=1, source_target_pairs={{0,4},{2,6},{4,0},{6,2},{8,12},{10,14},{12,8},{14,10},{1,5},{3,7},... | collective-permute-start | bytes 786440 | tf_op jit(solution)/shard_map/ppermute | solution.py:402
  6.4 2.2 %copy-start = (bf16[2,1024,1024]{2,1,0:T(8,128)(2,1)S(1)}, bf16[2,1024,1024]{2,1,0:T(8,128)(2,1)}, u32[]{:S(2)}) copy-start(bf16[2,1024,1024]{2,1,0:T(8,128)(2,1)} %full_ref.2) | copy-start | bytes 12582916
  8.6 0.7 copy-start.6
  8.6 0.8 copy-start.5
  8.6 26.1 %collective-permute-start.16 = (bf16[128,1024]{1,0:T(8,128)(2,1)S(1)}, bf16[128,1024]{1,0:T(8,128)(2,1)S(1)}, u32[]{:S(2)}, u32[]{:S(2)}) collective-permute-start(bf16[128,1024]{1,0:T(8,128)(2,1)S(1)} %get-tuple-element.20), channel_id=1, source_target_pairs={{0,8},{2,10},{4,12},{6,14},{8,0},{10,2},{12,4},{14,6},{1,9},{3,11}... | collective-permute-start | bytes 786440 | tf_op jit(solution)/shard_map/ppermute | solution.py:402
  9.6 2.4 %collective-permute-start.5 = (f32[16,128]{1,0:T(8,128)S(1)}, f32[16,128]{1,0:T(8,128)S(1)}, u32[]{:S(2)}, u32[]{:S(2)}) collective-permute-start(f32[16,128]{1,0:T(8,128)S(1)} %broadcast_in_dim.10.noise_ref), channel_id=1, source_target_pairs={{0,2},{2,0},{4,6},{6,4},{8,10},{10,8},{12,14},{14,12},{1,3},{3,1},... | collective-permute-start | bytes 24584 | tf_op jit(solution)/shard_map/ppermute | solution.py:406
  9.6 2.2 %copy-start.1 = (bf16[2,1024,1024]{2,1,0:T(8,128)(2,1)S(1)}, bf16[2,1024,1024]{2,1,0:T(8,128)(2,1)}, u32[]{:S(2)}) copy-start(bf16[2,1024,1024]{2,1,0:T(8,128)(2,1)} %full_ref.2) | copy-start | bytes 12582916
  11.8 42.7 %copy-start.3 = (bf16[2,1024,256]{2,1,0:T(8,128)(2,1)S(1)}, bf16[2,1024,256]{2,1,0:T(8,128)(2,1)}, u32[]{:S(2)}) copy-start(bf16[2,1024,256]{2,1,0:T(8,128)(2,1)} %mine_ref.1) | copy-start | bytes 3145732
  11.8 42.7 %copy-start.4 = (bf16[4,128,256]{2,1,0:T(8,128)(2,1)S(1)}, bf16[4,128,256]{2,1,0:T(8,128)(2,1)}, u32[]{:S(2)}) copy-start(bf16[4,128,256]{2,1,0:T(8,128)(2,1)} %here_ref.1) | copy-start | bytes 786436
  12.0 43.5 %copy-start.2 = (f32[1,128,4,256]{3,2,1,0:T(4,128)S(1)}, f32[1,128,4,256]{3,2,1,0:T(4,128)}, u32[]{:S(2)}) copy-start(f32[1,128,4,256]{3,2,1,0:T(4,128)} %orbitals_ref.3) | copy-start | bytes 1572868
  12.1 43.4 %collective-permute-start.8 = (bf16[2,128,1024]{2,1,0:T(8,128)(2,1)S(1)}, bf16[2,128,1024]{2,1,0:T(8,128)(2,1)S(1)}, u32[]{:S(2)}, u32[]{:S(2)}) collective-permute-start(bf16[2,128,1024]{2,1,0:T(8,128)(2,1)S(1)} %get-tuple-element.23), channel_id=1, source_target_pairs={{0,2},{2,0},{4,6},{6,4},{8,10},{10,8},{12,14},{14,12},{1,3},{3,1},... | collective-permute-start | bytes 1572872 | tf_op jit(solution)/shard_map/ppermute | solution.py:406
  17.9 28.0 %collective-permute-start.14 = (bf16[128,1024]{1,0:T(8,128)(2,1)S(1)}, bf16[128,1024]{1,0:T(8,128)(2,1)S(1)}, u32[]{:S(2)}, u32[]{:S(2)}) collective-permute-start(bf16[128,1024]{1,0:T(8,128)(2,1)S(1)} %get-tuple-element.28), channel_id=1, source_target_pairs={{0,8},{2,10},{4,12},{6,14},{8,0},{10,2},{12,4},{14,6},{1,9},{3,11}... | collective-permute-start | bytes 786440 | tf_op jit(solution)/shard_map/ppermute | solution.py:402
  18.7 27.2 %collective-permute-start.2 = (bf16[4,128,256]{2,1,0:T(8,128)(2,1)S(1)}, bf16[4,128,256]{2,1,0:T(8,128)(2,1)S(1)}, u32[]{:S(2)}, u32[]{:S(2)}) collective-permute-start(bf16[4,128,256]{2,1,0:T(8,128)(2,1)S(1)} %collective-permute-done.1.two_ref), channel_id=1, source_target_pairs={{0,4},{2,6},{4,0},{6,2},{8,12},{10,14},{12,8},{14,10},{1,5},{3,7},... | collective-permute-start | bytes 786440 | tf_op jit(solution)/shard_map/ppermute | solution.py:402
  34.7 13.0 %collective-permute-start.22 = (bf16[128,1024]{1,0:T(8,128)(2,1)S(1)}, bf16[128,1024]{1,0:T(8,128)(2,1)S(1)}, u32[]{:S(2)}, u32[]{:S(2)}) collective-permute-start(bf16[128,1024]{1,0:T(8,128)(2,1)S(1)} %get-tuple-element.31), channel_id=1, source_target_pairs={{0,12},{2,14},{4,8},{6,10},{8,4},{10,6},{12,0},{14,2},{1,13},{3,15... | collective-permute-start | bytes 786440 | tf_op jit(solution)/shard_map/ppermute | solution.py:402
  45.9 11.0 %collective-permute-start.17 = (bf16[128,1024]{1,0:T(8,128)(2,1)S(1)}, bf16[128,1024]{1,0:T(8,128)(2,1)S(1)}, u32[]{:S(2)}, u32[]{:S(2)}) collective-permute-start(bf16[128,1024]{1,0:T(8,128)(2,1)S(1)} %collective-permute-done.16), channel_id=1, source_target_pairs={{0,2},{2,0},{4,6},{6,4},{8,10},{10,8},{12,14},{14,12},{1,3},{3,1},... | collective-permute-start | bytes 786440 | tf_op jit(solution)/shard_map/ppermute | solution.py:406
  45.9 11.0 %collective-permute-start.15 = (bf16[128,1024]{1,0:T(8,128)(2,1)S(1)}, bf16[128,1024]{1,0:T(8,128)(2,1)S(1)}, u32[]{:S(2)}, u32[]{:S(2)}) collective-permute-start(bf16[128,1024]{1,0:T(8,128)(2,1)S(1)} %collective-permute-done.14.refs_4_), channel_id=1, source_target_pairs={{0,1},{1,0},{2,3},{3,2},{4,5},{5,4},{6,7},{7,6},{8,9},{9,8},{10,11... | collective-permute-start | bytes 786440 | tf_op jit(solution)/shard_map/ppermute | solution.py:410
  47.7 11.0 %collective-permute-start.20 = (bf16[128,1024]{1,0:T(8,128)(2,1)S(1)}, bf16[128,1024]{1,0:T(8,128)(2,1)S(1)}, u32[]{:S(2)}, u32[]{:S(2)}) collective-permute-start(bf16[128,1024]{1,0:T(8,128)(2,1)S(1)} %get-tuple-element.30), channel_id=1, source_target_pairs={{0,12},{2,14},{4,8},{6,10},{8,4},{10,6},{12,0},{14,2},{1,13},{3,15... | collective-permute-start | bytes 786440 | tf_op jit(solution)/shard_map/ppermute | solution.py:402
  50.8 14.1 %collective-permute-start.11 = (bf16[128,1024]{1,0:T(8,128)(2,1)S(1)}, bf16[128,1024]{1,0:T(8,128)(2,1)S(1)}, u32[]{:S(2)}, u32[]{:S(2)}) collective-permute-start(bf16[128,1024]{1,0:T(8,128)(2,1)S(1)} %get-tuple-element.27), channel_id=1, source_target_pairs={{0,4},{2,6},{4,0},{6,2},{8,12},{10,14},{12,8},{14,10},{1,5},{3,7},... | collective-permute-start | bytes 786440 | tf_op jit(solution)/shard_map/ppermute | solution.py:402
  55.5 1.2 collective-permute-start.4
  56.7 12.2 %collective-permute-start.23 = (bf16[128,1024]{1,0:T(8,128)(2,1)S(1)}, bf16[128,1024]{1,0:T(8,128)(2,1)S(1)}, u32[]{:S(2)}, u32[]{:S(2)}) collective-permute-start(bf16[128,1024]{1,0:T(8,128)(2,1)S(1)} %collective-permute-done.22), channel_id=1, source_target_pairs={{0,2},{2,0},{4,6},{6,4},{8,10},{10,8},{12,14},{14,12},{1,3},{3,1},... | collective-permute-start | bytes 786440 | tf_op jit(solution)/shard_map/ppermute | solution.py:406
  56.9 17.9 %collective-permute-start.26 = (bf16[4,128,256]{2,1,0:T(8,128)(2,1)S(1)}, bf16[4,128,256]{2,1,0:T(8,128)(2,1)S(1)}, u32[]{:S(2)}, u32[]{:S(2)}) collective-permute-start(bf16[4,128,256]{2,1,0:T(8,128)(2,1)S(1)} %walker_major.1.refs_0_), channel_id=1, source_target_pairs={{0,8},{2,10},{4,12},{6,14},{8,0},{10,2},{12,4},{14,6},{1,9},{3,11}... | collective-permute-start | bytes 786440 | tf_op jit(solution)/shard_map/ppermute | solution.py:402
  57.0 11.9 %collective-permute-start.6 = (f32[16,128]{1,0:T(8,128)S(1)}, f32[16,128]{1,0:T(8,128)S(1)}, u32[]{:S(2)}, u32[]{:S(2)}) collective-permute-start(f32[16,128]{1,0:T(8,128)S(1)} %get-tuple-element.19.field_here), channel_id=1, source_target_pairs={{0,4},{2,6},{4,0},{6,2},{8,12},{10,14},{12,8},{14,10},{1,5},{3,7},... | collective-permute-start | bytes 24584 | tf_op jit(solution)/shard_map/ppermute | solution.py:402
  58.7 20.5 %collective-permute-start.25 = (bf16[4,128,256]{2,1,0:T(8,128)(2,1)S(1)}, bf16[4,128,256]{2,1,0:T(8,128)(2,1)S(1)}, u32[]{:S(2)}, u32[]{:S(2)}) collective-permute-start(bf16[4,128,256]{2,1,0:T(8,128)(2,1)S(1)} %walker_major.1.refs_0_), channel_id=1, source_target_pairs={{0,4},{2,6},{4,0},{6,2},{8,12},{10,14},{12,8},{14,10},{1,5},{3,7},... | collective-permute-start | bytes 786440 | tf_op jit(solution)/shard_map/ppermute | solution.py:402
  64.9 14.9 %collective-permute-start.18 = (bf16[128,1024]{1,0:T(8,128)(2,1)S(1)}, bf16[128,1024]{1,0:T(8,128)(2,1)S(1)}, u32[]{:S(2)}, u32[]{:S(2)}) collective-permute-start(bf16[128,1024]{1,0:T(8,128)(2,1)S(1)} %collective-permute-done.17.refs_6_), channel_id=1, source_target_pairs={{0,1},{1,0},{2,3},{3,2},{4,5},{5,4},{6,7},{7,6},{8,9},{9,8},{10,11... | collective-permute-start | bytes 786440 | tf_op jit(solution)/shard_map/ppermute | solution.py:410
  68.9 13.3 %collective-permute-start.12 = (bf16[128,1024]{1,0:T(8,128)(2,1)S(1)}, bf16[128,1024]{1,0:T(8,128)(2,1)S(1)}, u32[]{:S(2)}, u32[]{:S(2)}) collective-permute-start(bf16[128,1024]{1,0:T(8,128)(2,1)S(1)} %collective-permute-done.11), channel_id=1, source_target_pairs={{0,2},{2,0},{4,6},{6,4},{8,10},{10,8},{12,14},{14,12},{1,3},{3,1},... | collective-permute-start | bytes 786440 | tf_op jit(solution)/shard_map/ppermute | solution.py:406
  68.9 14.2 %collective-permute-start.9 = (bf16[128,1024]{1,0:T(8,128)(2,1)S(1)}, bf16[128,1024]{1,0:T(8,128)(2,1)S(1)}, u32[]{:S(2)}, u32[]{:S(2)}) collective-permute-start(bf16[128,1024]{1,0:T(8,128)(2,1)S(1)} %get-tuple-element.25), channel_id=1, source_target_pairs={{0,4},{2,6},{4,0},{6,2},{8,12},{10,14},{12,8},{14,10},{1,5},{3,7},... | collective-permute-start | bytes 786440 | tf_op jit(solution)/shard_map/ppermute | solution.py:402
  74.9 11.5 %collective-permute-start.21 = (bf16[128,1024]{1,0:T(8,128)(2,1)S(1)}, bf16[128,1024]{1,0:T(8,128)(2,1)S(1)}, u32[]{:S(2)}, u32[]{:S(2)}) collective-permute-start(bf16[128,1024]{1,0:T(8,128)(2,1)S(1)} %collective-permute-done.20.refs_0_), channel_id=1, source_target_pairs={{0,1},{1,0},{2,3},{3,2},{4,5},{5,4},{6,7},{7,6},{8,9},{9,8},{10,11... | collective-permute-start | bytes 786440 | tf_op jit(solution)/shard_map/ppermute | solution.py:410
  79.2 12.8 %collective-permute-start.24 = (bf16[128,1024]{1,0:T(8,128)(2,1)S(1)}, bf16[128,1024]{1,0:T(8,128)(2,1)S(1)}, u32[]{:S(2)}, u32[]{:S(2)}) collective-permute-start(bf16[128,1024]{1,0:T(8,128)(2,1)S(1)} %collective-permute-done.23.refs_2_), channel_id=1, source_target_pairs={{0,1},{1,0},{2,3},{3,2},{4,5},{5,4},{6,7},{7,6},{8,9},{9,8},{10,11... | collective-permute-start | bytes 786440 | tf_op jit(solution)/shard_map/ppermute | solution.py:410
  79.8 12.2 %collective-permute-start.30 = (bf16[4,128,256]{2,1,0:T(8,128)(2,1)S(1)}, bf16[4,128,256]{2,1,0:T(8,128)(2,1)S(1)}, u32[]{:S(2)}, u32[]{:S(2)}) collective-permute-start(bf16[4,128,256]{2,1,0:T(8,128)(2,1)S(1)} %collective-permute-done.26.refs_2_), channel_id=1, source_target_pairs={{0,4},{2,6},{4,0},{6,2},{8,12},{10,14},{12,8},{14,10},{1,5},{3,7},... | collective-permute-start | bytes 786440 | tf_op jit(solution)/shard_map/ppermute | solution.py:402
  82.2 15.3 %collective-permute-start.13 = (bf16[128,1024]{1,0:T(8,128)(2,1)S(1)}, bf16[128,1024]{1,0:T(8,128)(2,1)S(1)}, u32[]{:S(2)}, u32[]{:S(2)}) collective-permute-start(bf16[128,1024]{1,0:T(8,128)(2,1)S(1)} %collective-permute-done.12.refs_2_), channel_id=1, source_target_pairs={{0,1},{1,0},{2,3},{3,2},{4,5},{5,4},{6,7},{7,6},{8,9},{9,8},{10,11... | collective-permute-start | bytes 786440 | tf_op jit(solution)/shard_map/ppermute | solution.py:410
  83.1 19.2 %collective-permute-start.10 = (bf16[128,1024]{1,0:T(8,128)(2,1)S(1)}, bf16[128,1024]{1,0:T(8,128)(2,1)S(1)}, u32[]{:S(2)}, u32[]{:S(2)}) collective-permute-start(bf16[128,1024]{1,0:T(8,128)(2,1)S(1)} %collective-permute-done.9.refs_0_), channel_id=1, source_target_pairs={{0,1},{1,0},{2,3},{3,2},{4,5},{5,4},{6,7},{7,6},{8,9},{9,8},{10,11... | collective-permute-start | bytes 786440 | tf_op jit(solution)/shard_map/ppermute | solution.py:410
  86.4 6.1 %collective-permute-start.7 = (f32[16,128]{1,0:T(8,128)S(1)}, f32[16,128]{1,0:T(8,128)S(1)}, u32[]{:S(2)}, u32[]{:S(2)}) collective-permute-start(f32[16,128]{1,0:T(8,128)S(1)} %get-tuple-element.19.field_here), channel_id=1, source_target_pairs={{0,8},{2,10},{4,12},{6,14},{8,0},{10,2},{12,4},{14,6},{1,9},{3,11}... | collective-permute-start | bytes 24584 | tf_op jit(solution)/shard_map/ppermute | solution.py:402
  92.0 17.4 %collective-permute-start.27 = (bf16[4,128,256]{2,1,0:T(8,128)(2,1)S(1)}, bf16[4,128,256]{2,1,0:T(8,128)(2,1)S(1)}, u32[]{:S(2)}, u32[]{:S(2)}) collective-permute-start(bf16[4,128,256]{2,1,0:T(8,128)(2,1)S(1)} %walker_major.1.refs_0_), channel_id=1, source_target_pairs={{0,2},{2,0},{4,6},{6,4},{8,10},{10,8},{12,14},{14,12},{1,3},{3,1},... | collective-permute-start | bytes 786440 | tf_op jit(solution)/shard_map/ppermute | solution.py:406
  92.0 17.4 %collective-permute-start.29 = (bf16[4,128,256]{2,1,0:T(8,128)(2,1)S(1)}, bf16[4,128,256]{2,1,0:T(8,128)(2,1)S(1)}, u32[]{:S(2)}, u32[]{:S(2)}) collective-permute-start(bf16[4,128,256]{2,1,0:T(8,128)(2,1)S(1)} %collective-permute-done.26.refs_2_), channel_id=1, source_target_pairs={{0,2},{2,0},{4,6},{6,4},{8,10},{10,8},{12,14},{14,12},{1,3},{3,1},... | collective-permute-start | bytes 786440 | tf_op jit(solution)/shard_map/ppermute | solution.py:406
  92.5 16.9 %collective-permute-start.28 = (bf16[4,128,256]{2,1,0:T(8,128)(2,1)S(1)}, bf16[4,128,256]{2,1,0:T(8,128)(2,1)S(1)}, u32[]{:S(2)}, u32[]{:S(2)}) collective-permute-start(bf16[4,128,256]{2,1,0:T(8,128)(2,1)S(1)} %collective-permute-done.25.refs_1_), channel_id=1, source_target_pairs={{0,2},{2,0},{4,6},{6,4},{8,10},{10,8},{12,14},{14,12},{1,3},{3,1},... | collective-permute-start | bytes 786440 | tf_op jit(solution)/shard_map/ppermute | solution.py:406
  97.6 12.5 %collective-permute-start.31 = (bf16[4,128,256]{2,1,0:T(8,128)(2,1)S(1)}, bf16[4,128,256]{2,1,0:T(8,128)(2,1)S(1)}, u32[]{:S(2)}, u32[]{:S(2)}) collective-permute-start(bf16[4,128,256]{2,1,0:T(8,128)(2,1)S(1)} %collective-permute-done.30.mine), channel_id=1, source_target_pairs={{0,2},{2,0},{4,6},{6,4},{8,10},{10,8},{12,14},{14,12},{1,3},{3,1},... | collective-permute-start | bytes 786440 | tf_op jit(solution)/shard_map/ppermute | solution.py:406
  102.3 5.4 %collective-permute-start.19 = (f32[16,128]{1,0:T(8,128)S(1)}, f32[16,128]{1,0:T(8,128)S(1)}, u32[]{:S(2)}, u32[]{:S(2)}) collective-permute-start(f32[16,128]{1,0:T(8,128)S(1)} %get-tuple-element.19.field_here), channel_id=1, source_target_pairs={{0,12},{2,14},{4,8},{6,10},{8,4},{10,6},{12,0},{14,2},{1,13},{3,15... | collective-permute-start | bytes 24584 | tf_op jit(solution)/shard_map/ppermute | solution.py:402
  110.4 13.0 %collective-permute-start.33 = (bf16[4,128,256]{2,1,0:T(8,128)(2,1)S(1)}, bf16[4,128,256]{2,1,0:T(8,128)(2,1)}, u32[]{:S(2)}, u32[]{:S(2)}) collective-permute-start(bf16[4,128,256]{2,1,0:T(8,128)(2,1)S(1)} %get-tuple-element.33.refs_0_), channel_id=1, source_target_pairs={{0,8},{2,10},{4,12},{6,14},{8,0},{10,2},{12,4},{14,6},{1,9},{3,11}... | collective-permute-start | bytes 786440 | tf_op jit(solution)/shard_map/ppermute | solution.py:402
  110.5 13.1 %collective-permute-start.32 = (bf16[4,128,256]{2,1,0:T(8,128)(2,1)S(1)}, bf16[4,128,256]{2,1,0:T(8,128)(2,1)}, u32[]{:S(2)}, u32[]{:S(2)}) collective-permute-start(bf16[4,128,256]{2,1,0:T(8,128)(2,1)S(1)} %get-tuple-element.33.refs_0_), channel_id=1, source_target_pairs={{0,4},{2,6},{4,0},{6,2},{8,12},{10,14},{12,8},{14,10},{1,5},{3,7},... | collective-permute-start | bytes 786440 | tf_op jit(solution)/shard_map/ppermute | solution.py:402
  123.5 8.5 %collective-permute-start.37 = (bf16[4,128,256]{2,1,0:T(8,128)(2,1)}, bf16[4,128,256]{2,1,0:T(8,128)(2,1)}, u32[]{:S(2)}, u32[]{:S(2)}) collective-permute-start(bf16[4,128,256]{2,1,0:T(8,128)(2,1)} %collective-permute-done.33.refs_2_), channel_id=1, source_target_pairs={{0,4},{2,6},{4,0},{6,2},{8,12},{10,14},{12,8},{14,10},{1,5},{3,7},... | collective-permute-start | bytes 786440 | tf_op jit(solution)/shard_map/ppermute | solution.py:402
  123.5 9.1 %collective-permute-start.34 = (bf16[4,128,256]{2,1,0:T(8,128)(2,1)S(1)}, bf16[4,128,256]{2,1,0:T(8,128)(2,1)}, u32[]{:S(2)}, u32[]{:S(2)}) collective-permute-start(bf16[4,128,256]{2,1,0:T(8,128)(2,1)S(1)} %get-tuple-element.33.refs_0_), channel_id=1, source_target_pairs={{0,2},{2,0},{4,6},{6,4},{8,10},{10,8},{12,14},{14,12},{1,3},{3,1},... | collective-permute-start | bytes 786440 | tf_op jit(solution)/shard_map/ppermute | solution.py:406
  123.6 9.0 %collective-permute-start.35 = (bf16[4,128,256]{2,1,0:T(8,128)(2,1)}, bf16[4,128,256]{2,1,0:T(8,128)(2,1)}, u32[]{:S(2)}, u32[]{:S(2)}) collective-permute-start(bf16[4,128,256]{2,1,0:T(8,128)(2,1)} %collective-permute-done.32.refs_1_), channel_id=1, source_target_pairs={{0,2},{2,0},{4,6},{6,4},{8,10},{10,8},{12,14},{14,12},{1,3},{3,1},... | collective-permute-start | bytes 786440 | tf_op jit(solution)/shard_map/ppermute | solution.py:406
  124.0 8.6 %collective-permute-start.36 = (bf16[4,128,256]{2,1,0:T(8,128)(2,1)}, bf16[4,128,256]{2,1,0:T(8,128)(2,1)}, u32[]{:S(2)}, u32[]{:S(2)}) collective-permute-start(bf16[4,128,256]{2,1,0:T(8,128)(2,1)} %collective-permute-done.33.refs_2_), channel_id=1, source_target_pairs={{0,2},{2,0},{4,6},{6,4},{8,10},{10,8},{12,14},{14,12},{1,3},{3,1},... | collective-permute-start | bytes 786440 | tf_op jit(solution)/shard_map/ppermute | solution.py:406
  131.9 2.6 %collective-permute-start.38 = (bf16[4,128,256]{2,1,0:T(8,128)(2,1)}, bf16[4,128,256]{2,1,0:T(8,128)(2,1)}, u32[]{:S(2)}, u32[]{:S(2)}) collective-permute-start(bf16[4,128,256]{2,1,0:T(8,128)(2,1)} %collective-permute-done.37.mine), channel_id=1, source_target_pairs={{0,2},{2,0},{4,6},{6,4},{8,10},{10,8},{12,14},{14,12},{1,3},{3,1},... | collective-permute-start | bytes 786440 | tf_op jit(solution)/shard_map/ppermute | solution.py:406

commit v6 on v5

--- a/solution.py
+++ b/solution.py
@@ -378,24 +378,47 @@
     )(operator, partial, mine, theirs)
 
 
-def second_kernel(operator_ref, partial_ref, first_ref, orbitals_ref, mine, theirs, out_ref, vector_ref):
+def base_kernel(operator_ref, first_ref, orbitals_ref, *refs):
+    pieces, (out_ref, vector_ref) = refs[:6], refs[6:]
+    parts = [
+        applied(operator_ref, vector_ref.at[step], step, pieces[step], pieces[3 + step])
+        for step in range(3)
+    ]
+    for w in range(first_ref.shape[0]):
+        second = parts[0](w) + parts[1](w) + parts[2](w)
+        out_ref[w] = orbitals_ref[0, :, w, :] + first_ref[w] + 0.5 * second
+
+
+def base_application(operator, first_term, orbitals, pieces):
+    walkers, rows, occupied = first_term.shape
+    return pl.pallas_call(
+        base_kernel,
+        out_shape=jax.ShapeDtypeStruct(first_term.shape, wide),
+        in_specs=[vmem_spec] * 9,
+        out_specs=vmem_spec,
+        scratch_shapes=[pltpu.VMEM((3, walkers, 2 * rows, occupied), narrow)],
+        compiler_params=small,
+        name="base_application",
+    )(operator, first_term, orbitals, *pieces)
+
+
+def second_kernel(operator_ref, base_ref, mine, theirs, out_ref, vector_ref):
     part = applied(operator_ref, vector_ref, 3, mine, theirs)
-    for w in range(first_ref.shape[0]):
-        second = partial_ref[w] + part(w)
-        out_ref[0, :, w, :] = orbitals_ref[0, :, w, :] + first_ref[w] + 0.5 * second
-
-
-def second_application(operator, partial, first_term, orbitals, mine, theirs):
+    for w in range(base_ref.shape[0]):
+        out_ref[0, :, w, :] = base_ref[w] + 0.5 * part(w)
+
+
+def second_application(operator, base, mine, theirs):
     walkers, rows, occupied = mine.shape
     return pl.pallas_call(
         second_kernel,
-        out_shape=jax.ShapeDtypeStruct(orbitals.shape, wide),
-        in_specs=[vmem_spec] * 6,
+        out_shape=jax.ShapeDtypeStruct((1, rows, walkers, occupied), wide),
+        in_specs=[vmem_spec] * 4,
         out_specs=vmem_spec,
         scratch_shapes=[pltpu.VMEM((walkers, 2 * rows, occupied), narrow)],
         compiler_params=small,
         name="second_application",
-    )(operator, partial, first_term, orbitals, mine, theirs)
+    )(operator, base, mine, theirs)
 
 
 def to_chip(value, step):
@@ -443,20 +466,24 @@
     bias_shift, field = chip_field(bias, to_core(bias), constants, constants_theirs, walkers)
     field_one, field_two, field_three = (to_chip(field, step) for step in (1, 2, 3))
 
-    cross_mine, mine = {}, {}
+    cross_mine, mine, theirs, mine_x, theirs_x = {}, {}, {}, {}, {}
     cross_mine[2], mine[2] = to_chip(cross[2], 2), to_chip(straight[2], 2)
     cross_mine[3] = to_chip(cross[3], 3)
-    mine[3] = to_chip(after(straight[3], cross_mine[2]), 3)
-    cross_mine[1] = to_chip(after(cross[1], green_three), 1)
-    mine[1] = to_chip(after(straight[1], field_one), 1)
-    blocks = {}
-    for step in (2, 3, 1):
-        theirs = to_core(cross_mine[step])
-        blocks[step] = (mine[step], across(mine[step]), theirs, across(theirs))
-
-    start = after(walker_major(orbitals), mine[2], cross_mine[3])
+    theirs[2] = to_core(after(cross_mine[2], field))
+    mine[3] = to_chip(after(straight[3], theirs[2]), 3)
+    cross[1], straight[1] = after((cross[1], straight[1]), field_one)
+    cross_mine[1], mine[1] = to_chip(cross[1], 1), to_chip(straight[1], 1)
+    theirs_x[2] = across(after(theirs[2], field_one))
+    mine_x[2] = across(mine[2])
+    for step in (3, 1):
+        theirs[step] = to_core(cross_mine[step])
+        theirs_x[step], mine_x[step] = across(theirs[step]), across(mine[step])
+    blocks = {step: (mine[step], mine_x[step], theirs[step], theirs_x[step]) for step in mine}
+
+    start = after(walker_major(orbitals), theirs_x[2], theirs[3], field_two, field_three)
     start_two, start_one = to_chip(start, 2), to_chip(start, 1)
-    start_three = to_chip(start_two, 1)
+    hops = (mine_x[2], theirs_x[3], mine_x[1], theirs_x[1], mine[3])
+    start_three = to_chip(after(start_two, *hops), 1)
 
     summed = early_operator(
         walkers,
@@ -470,14 +497,16 @@
     near = [start, start_one, start_two]
     partial = near_application(operator, [*near, *[to_core(piece) for piece in near]])
     first_term, first_narrow = first_application(
-        operator, partial, start_three, to_core(start_three)
+        operator, partial, start_three, to_core(after(start_three, partial))
     )
     first_two, first_one = to_chip(first_narrow, 2), to_chip(first_narrow, 1)
     first_three = to_chip(first_two, 1)
     near = [first_narrow, first_one, first_two]
-    partial = near_application(operator, [*near, *[to_core(piece) for piece in near]])
+    base = base_application(
+        operator, first_term, orbitals, [*near, *[to_core(piece) for piece in near]]
+    )
     walkers_next = second_application(
-        operator, partial, first_term, orbitals, first_three, to_core(first_three)
+        operator, base, first_three, to_core(after(first_three, base))
     )
     return (walkers_next, bias_shift)
 

time: 137 us -> 133 us (0.971)
  starting transfers between devices: 51.9 us -> 41.3 us
  waiting for transfers between devices: 66.5 us -> 74.3 us
  Pallas kernels: 12.2 us -> 10.6 us
    ppermute x18, waiting for transfers between devices: 50.4 us -> 70.3 us  [to_chip(): return lax.ppermute(value, 'chol', [(i, i ^ 2 * step) for i in range(8)])]
    ppermute x6, waiting for transfers between devices: 15.4 us -> 0.02 us  [across(): return lax.ppermute(value, 'walk', [(0, 1), (1, 0)])]
    ppermute x18, starting transfers between devices: 36.8 us -> 31.8 us  [to_chip(): return lax.ppermute(value, 'chol', [(i, i ^ 2 * step) for i in range(8)])]
    ppermute x6, starting transfers between devices: 12.7 us -> 7.91 us  [across(): return lax.ppermute(value, 'walk', [(0, 1), (1, 0)])]
    ppermute x15, waiting for transfers between devices: 0.66 us -> 3.96 us  [to_core(): return lax.ppermute(value, 'chol', [(i, i ^ 1) for i in range(8)])]
    pallas_call x2 -> x1, Pallas kernels: 2.64 us -> 0.7 us  [near_application(): pl.pallas_call(near_kernel, out_shape=jax.ShapeDtypeStruct((walkers, rows...]
where the time goes in v6:
time: 133 us; the launch traced here: 132 us
  waiting for transfers between devices  74.3 us (56%)
  starting transfers between devices  41.3 us (31%)
  Pallas kernels  10.6 us (8%)
  local copies, waits for them, and re-layouts  5.35 us (4%)
    ppermute x18, waiting for transfers between devices, to_chip(): return lax.ppermute(value, 'chol', [(i, i ^ 2 * step) for i in range(8)])  70.3 us
    ppermute x18, starting transfers between devices, to_chip(): return lax.ppermute(value, 'chol', [(i, i ^ 2 * step) for i in range(8)])  31.8 us
    ppermute x6, starting transfers between devices, across(): return lax.ppermute(value, 'walk', [(0, 1), (1, 0)])  7.91 us
    unnamed x15, local copies, waits for them, and re-layouts  5.04 us
    ppermute x15, waiting for transfers between devices, to_core(): return lax.ppermute(value, 'chol', [(i, i ^ 1) for i in range(8)])  3.96 us
    pallas_call x1, Pallas kernels, early_operator(): pl.pallas_call(functools.partial(early_kernel, walkers), out_shape=jax.Sh...  3.33 us
  transfers between devices with their start and end apart: 39, of which 17 were waited for; matrix products, arithmetic and copies ran while one was open for 1% of the time, Pallas kernels for 7%

profile of v6, /device:TPU:0, one launch (start us, length us, event | category | flops | bytes accessed | tf_op | source)
XLA Modules:
  0.0 132.4 jit_solution(341977034046379361)
XLA Ops:
  1.1 3.7 %collective-permute-start.1 = (bf16[4,128,256]{2,1,0:T(8,128)(2,1)}, bf16[4,128,256]{2,1,0:T(8,128)(2,1)S(1)}, u32[]{:S(2)}, u32[]{:S(2)}) collective-permute-start(bf16[4,128,256]{2,1,0:T(8,128)(2,1)} %here_ref.1), channel_id=1, source_target_pairs={{0,8},{2,10},{4,12},{6,14},{8,0},{10,2},{12,4},{14,6},{1,9},{3,11}... | collective-permute-start | bytes 786440 | tf_op jit(solution)/shard_map/ppermute | solution.py:425
  4.8 1.6 %collective-permute-start = (bf16[4,128,256]{2,1,0:T(8,128)(2,1)}, bf16[4,128,256]{2,1,0:T(8,128)(2,1)S(1)}, u32[]{:S(2)}, u32[]{:S(2)}) collective-permute-start(bf16[4,128,256]{2,1,0:T(8,128)(2,1)} %here_ref.1), channel_id=1, source_target_pairs={{0,4},{2,6},{4,0},{6,2},{8,12},{10,14},{12,8},{14,10},{1,5},{3,7},... | collective-permute-start | bytes 786440 | tf_op jit(solution)/shard_map/ppermute | solution.py:425
  6.4 11.3 %collective-permute-done.1.two_ref = bf16[4,128,256]{2,1,0:T(8,128)(2,1)S(1)} collective-permute-done((bf16[4,128,256]{2,1,0:T(8,128)(2,1)}, bf16[4,128,256]{2,1,0:T(8,128)(2,1)S(1)}, u32[]{:S(2)}, u32[]{:S(2)}) %collective-permute-start.1) | collective-permute-done | bytes 262176 | tf_op jit(solution)/shard_map/ppermute | solution.py:425
  17.6 0.7 collective-permute-start.2
  18.4 2.2 %copy-done = bf16[2,1024,1024]{2,1,0:T(8,128)(2,1)S(1)} copy-done((bf16[2,1024,1024]{2,1,0:T(8,128)(2,1)S(1)}, bf16[2,1024,1024]{2,1,0:T(8,128)(2,1)}, u32[]{:S(2)}) %copy-start) | copy-done | bytes 4194328
  20.6 0.8 cut_rows.2
  21.4 3.3 %collective-permute-start.16 = (bf16[128,1024]{1,0:T(8,128)(2,1)}, bf16[128,1024]{1,0:T(8,128)(2,1)}, u32[]{:S(2)}, u32[]{:S(2)}) collective-permute-start(bf16[128,1024]{1,0:T(8,128)(2,1)} %get-tuple-element.25), channel_id=1, source_target_pairs={{0,8},{2,10},{4,12},{6,14},{8,0},{10,2},{12,4},{14,6},{1,9},{3,11}... | collective-permute-start | bytes 786440 | tf_op jit(solution)/shard_map/ppermute | solution.py:425
  25.1 0.5 collective-permute-done.2.three_ref
  25.7 1.0 chip_bias.1.mine_ref
  26.7 3.2 %collective-permute-start.14 = (bf16[128,1024]{1,0:T(8,128)(2,1)S(1)}, bf16[128,1024]{1,0:T(8,128)(2,1)S(1)}, u32[]{:S(2)}, u32[]{:S(2)}) collective-permute-start(bf16[128,1024]{1,0:T(8,128)(2,1)S(1)} %get-tuple-element.33), channel_id=1, source_target_pairs={{0,8},{2,10},{4,12},{6,14},{8,0},{10,2},{12,4},{14,6},{1,9},{3,11}... | collective-permute-start | bytes 786440 | tf_op jit(solution)/shard_map/ppermute | solution.py:425
  29.9 2.2 %copy-done.1 = bf16[2,1024,1024]{2,1,0:T(8,128)(2,1)S(1)} copy-done((bf16[2,1024,1024]{2,1,0:T(8,128)(2,1)S(1)}, bf16[2,1024,1024]{2,1,0:T(8,128)(2,1)}, u32[]{:S(2)}) %copy-start.1) | copy-done | bytes 4194328
  32.3 1.9 %collective-permute-start.22 = (bf16[128,1024]{1,0:T(8,128)(2,1)S(1)}, bf16[128,1024]{1,0:T(8,128)(2,1)S(1)}, u32[]{:S(2)}, u32[]{:S(2)}) collective-permute-start(bf16[128,1024]{1,0:T(8,128)(2,1)S(1)} %get-tuple-element.38), channel_id=1, source_target_pairs={{0,12},{2,14},{4,8},{6,10},{8,4},{10,6},{12,0},{14,2},{1,13},{3,15... | collective-permute-start | bytes 786440 | tf_op jit(solution)/shard_map/ppermute | solution.py:425
  34.3 14.7 %collective-permute-done.16 = bf16[128,1024]{1,0:T(8,128)(2,1)} collective-permute-done((bf16[128,1024]{1,0:T(8,128)(2,1)}, bf16[128,1024]{1,0:T(8,128)(2,1)}, u32[]{:S(2)}, u32[]{:S(2)}) %collective-permute-start.16) | collective-permute-done | bytes 262176 | tf_op jit(solution)/shard_map/ppermute | solution.py:425
  49.1 5.5 %collective-permute-done.14.refs_4_ = bf16[128,1024]{1,0:T(8,128)(2,1)S(1)} collective-permute-done((bf16[128,1024]{1,0:T(8,128)(2,1)S(1)}, bf16[128,1024]{1,0:T(8,128)(2,1)S(1)}, u32[]{:S(2)}, u32[]{:S(2)}) %collective-permute-start.14) | collective-permute-done | bytes 262176 | tf_op jit(solution)/shard_map/ppermute | solution.py:425
  54.6 1.5 %collective-permute-start.15 = (bf16[128,1024]{1,0:T(8,128)(2,1)S(1)}, bf16[128,1024]{1,0:T(8,128)(2,1)S(1)}, u32[]{:S(2)}, u32[]{:S(2)}) collective-permute-start(bf16[128,1024]{1,0:T(8,128)(2,1)S(1)} %collective-permute-done.14.refs_4_), channel_id=1, source_target_pairs={{0,1},{1,0},{2,3},{3,2},{4,5},{5,4},{6,7},{7,6},{8,9},{9,8},{10,11... | collective-permute-start | bytes 786440 | tf_op jit(solution)/shard_map/ppermute | solution.py:433
  56.0 3.8 %collective-permute-start.11 = (bf16[128,1024]{1,0:T(8,128)(2,1)S(1)}, bf16[128,1024]{1,0:T(8,128)(2,1)S(1)}, u32[]{:S(2)}, u32[]{:S(2)}) collective-permute-start(bf16[128,1024]{1,0:T(8,128)(2,1)S(1)} %get-tuple-element.32), channel_id=1, source_target_pairs={{0,4},{2,6},{4,0},{6,2},{8,12},{10,14},{12,8},{14,10},{1,5},{3,7},... | collective-permute-start | bytes 786440 | tf_op jit(solution)/shard_map/ppermute | solution.py:425
  59.9 1.5 %collective-permute-start.18 = (bf16[128,1024]{1,0:T(8,128)(2,1)S(1)}, bf16[128,1024]{1,0:T(8,128)(2,1)S(1)}, u32[]{:S(2)}, u32[]{:S(2)}) collective-permute-start(bf16[128,1024]{1,0:T(8,128)(2,1)S(1)} %collective-permute-done.17.refs_6_), channel_id=1, source_target_pairs={{0,1},{1,0},{2,3},{3,2},{4,5},{5,4},{6,7},{7,6},{8,9},{9,8},{10,11... | collective-permute-start | bytes 786440 | tf_op jit(solution)/shard_map/ppermute | solution.py:433
  61.3 1.0 collective-permute-start.7
  62.4 1.4 %collective-permute-start.19 = (f32[16,128]{1,0:T(8,128)S(1)}, f32[16,128]{1,0:T(8,128)S(1)}, u32[]{:S(2)}, u32[]{:S(2)}) collective-permute-start(f32[16,128]{1,0:T(8,128)S(1)} %get-tuple-element.24.field_here), channel_id=1, source_target_pairs={{0,12},{2,14},{4,8},{6,10},{8,4},{10,6},{12,0},{14,2},{1,13},{3,15... | collective-permute-start | bytes 24584 | tf_op jit(solution)/shard_map/ppermute | solution.py:425
  63.8 1.0 collective-permute-start.9
  64.8 1.8 %collective-permute-done.7.field_two = f32[16,128]{1,0:T(8,128)S(1)} collective-permute-done((f32[16,128]{1,0:T(8,128)S(1)}, f32[16,128]{1,0:T(8,128)S(1)}, u32[]{:S(2)}, u32[]{:S(2)}) %collective-permute-start.7) | collective-permute-done | bytes 8224 | tf_op jit(solution)/shard_map/ppermute | solution.py:425
  66.7 1.5 %collective-permute-start.24 = (bf16[128,1024]{1,0:T(8,128)(2,1)S(1)}, bf16[128,1024]{1,0:T(8,128)(2,1)S(1)}, u32[]{:S(2)}, u32[]{:S(2)}) collective-permute-start(bf16[128,1024]{1,0:T(8,128)(2,1)S(1)} %collective-permute-done.23.refs_2_), channel_id=1, source_target_pairs={{0,1},{1,0},{2,3},{3,2},{4,5},{5,4},{6,7},{7,6},{8,9},{9,8},{10,11... | collective-permute-start | bytes 786440 | tf_op jit(solution)/shard_map/ppermute | solution.py:433
  68.1 1.5 %collective-permute-done.19.field_ref = f32[16,128]{1,0:T(8,128)S(1)} collective-permute-done((f32[16,128]{1,0:T(8,128)S(1)}, f32[16,128]{1,0:T(8,128)S(1)}, u32[]{:S(2)}, u32[]{:S(2)}) %collective-permute-start.19) | collective-permute-done | bytes 8224 | tf_op jit(solution)/shard_map/ppermute | solution.py:425
  69.7 1.4 %collective-permute-start.20 = (bf16[128,1024]{1,0:T(8,128)(2,1)S(1)}, bf16[128,1024]{1,0:T(8,128)(2,1)S(1)}, u32[]{:S(2)}, u32[]{:S(2)}) collective-permute-start(bf16[128,1024]{1,0:T(8,128)(2,1)S(1)} %get-tuple-element.37), channel_id=1, source_target_pairs={{0,12},{2,14},{4,8},{6,10},{8,4},{10,6},{12,0},{14,2},{1,13},{3,15... | collective-permute-start | bytes 786440 | tf_op jit(solution)/shard_map/ppermute | solution.py:425
  71.6 0.5 walker_major.1.refs_0_
  72.2 0.6 collective-permute-done.9.refs_0_
  72.8 1.5 %collective-permute-start.10 = (bf16[128,1024]{1,0:T(8,128)(2,1)S(1)}, bf16[128,1024]{1,0:T(8,128)(2,1)S(1)}, u32[]{:S(2)}, u32[]{:S(2)}) collective-permute-start(bf16[128,1024]{1,0:T(8,128)(2,1)S(1)} %collective-permute-done.9.refs_0_), channel_id=1, source_target_pairs={{0,1},{1,0},{2,3},{3,2},{4,5},{5,4},{6,7},{7,6},{8,9},{9,8},{10,11... | collective-permute-start | bytes 786440 | tf_op jit(solution)/shard_map/ppermute | solution.py:433
  74.3 3.4 %collective-permute-start.25 = (bf16[4,128,256]{2,1,0:T(8,128)(2,1)S(1)}, bf16[4,128,256]{2,1,0:T(8,128)(2,1)S(1)}, u32[]{:S(2)}, u32[]{:S(2)}) collective-permute-start(bf16[4,128,256]{2,1,0:T(8,128)(2,1)S(1)} %walker_major.1.refs_0_), channel_id=1, source_target_pairs={{0,4},{2,6},{4,0},{6,2},{8,12},{10,14},{12,8},{14,10},{1,5},{3,7},... | collective-permute-start | bytes 786440 | tf_op jit(solution)/shard_map/ppermute | solution.py:425
  77.7 3.3 %collective-permute-done.20.refs_0_ = bf16[128,1024]{1,0:T(8,128)(2,1)S(1)} collective-permute-done((bf16[128,1024]{1,0:T(8,128)(2,1)S(1)}, bf16[128,1024]{1,0:T(8,128)(2,1)S(1)}, u32[]{:S(2)}, u32[]{:S(2)}) %collective-permute-start.20) | collective-permute-done | bytes 262176 | tf_op jit(solution)/shard_map/ppermute | solution.py:425
  81.0 3.1 %collective-permute-start.26 = (bf16[4,128,256]{2,1,0:T(8,128)(2,1)S(1)}, bf16[4,128,256]{2,1,0:T(8,128)(2,1)S(1)}, u32[]{:S(2)}, u32[]{:S(2)}) collective-permute-start(bf16[4,128,256]{2,1,0:T(8,128)(2,1)S(1)} %walker_major.1.refs_0_), channel_id=1, source_target_pairs={{0,8},{2,10},{4,12},{6,14},{8,0},{10,2},{12,4},{14,6},{1,9},{3,11}... | collective-permute-start | bytes 786440 | tf_op jit(solution)/shard_map/ppermute | solution.py:425
  84.1 0.6 collective-permute-start.13
  84.7 4.0 %collective-permute-done.25.refs_1_ = bf16[4,128,256]{2,1,0:T(8,128)(2,1)S(1)} collective-permute-done((bf16[4,128,256]{2,1,0:T(8,128)(2,1)S(1)}, bf16[4,128,256]{2,1,0:T(8,128)(2,1)S(1)}, u32[]{:S(2)}, u32[]{:S(2)}) %collective-permute-start.25) | collective-permute-done | bytes 262176 | tf_op jit(solution)/shard_map/ppermute | solution.py:425
  88.7 1.5 %collective-permute-start.21 = (bf16[128,1024]{1,0:T(8,128)(2,1)S(1)}, bf16[128,1024]{1,0:T(8,128)(2,1)S(1)}, u32[]{:S(2)}, u32[]{:S(2)}) collective-permute-start(bf16[128,1024]{1,0:T(8,128)(2,1)S(1)} %collective-permute-done.20.refs_0_), channel_id=1, source_target_pairs={{0,1},{1,0},{2,3},{3,2},{4,5},{5,4},{6,7},{7,6},{8,9},{9,8},{10,11... | collective-permute-start | bytes 786440 | tf_op jit(solution)/shard_map/ppermute | solution.py:433
  90.2 4.9 %collective-permute-done.26.refs_2_ = bf16[4,128,256]{2,1,0:T(8,128)(2,1)S(1)} collective-permute-done((bf16[4,128,256]{2,1,0:T(8,128)(2,1)S(1)}, bf16[4,128,256]{2,1,0:T(8,128)(2,1)S(1)}, u32[]{:S(2)}, u32[]{:S(2)}) %collective-permute-start.26) | collective-permute-done | bytes 262176 | tf_op jit(solution)/shard_map/ppermute | solution.py:425
  95.6 3.3 %early_operator.1.summed_ref = f32[4,128,1024]{2,1,0:T(8,128)S(1)} custom-call(f32[16,128]{1,0:T(8,128)S(1)} %get-tuple-element.24.field_here, f32[16,128]{1,0:T(8,128)S(1)} %collective-permute-done.6.field_one, f32[16,128]{1,0:T(8,128)S(1)} %collective-permute-done.7.field_two, bf16[2,128,1024]{2,1,0:T(8,128)(2,1)S(1)} %get-tuple-element.27.own, ...), custom_call_target="tpu_custom_call" | custom-call | tf_op jit(solution)/shard_map/early_operator/pallas_call | solution.py:273
  99.0 1.6 %split_operator.1.operator_ref = bf16[4,256,1024]{2,1,0:T(8,128)(2,1)S(1)} custom-call(f32[4,128,1024]{2,1,0:T(8,128)S(1)} %early_operator.1.summed_ref, f32[16,128]{1,0:T(8,128)S(1)} %collective-permute-done.19.field_ref, bf16[128,1024]{1,0:T(8,128)(2,1)S(1)} %collective-permute-done.20.refs_0_, bf16[128,1024]{1,0:T(8,128)(2,1)S(1)} %collective-permute-done.21.refs_1_, ...), custom_call_target="tpu_custom_call" | custom-call | tf_op jit(solution)/shard_map/split_operator/pallas_call | solution.py:306
  100.6 0.7 near_application.1.partial_ref
  101.3 2.6 %collective-permute-done.30.mine = bf16[4,128,256]{2,1,0:T(8,128)(2,1)S(1)} collective-permute-done((bf16[4,128,256]{2,1,0:T(8,128)(2,1)S(1)}, bf16[4,128,256]{2,1,0:T(8,128)(2,1)S(1)}, u32[]{:S(2)}, u32[]{:S(2)}) %collective-permute-start.30) | collective-permute-done | bytes 262176 | tf_op jit(solution)/shard_map/ppermute | solution.py:425
  103.9 1.5 %collective-permute-done.31.theirs = bf16[4,128,256]{2,1,0:T(8,128)(2,1)S(1)} collective-permute-done((bf16[4,128,256]{2,1,0:T(8,128)(2,1)S(1)}, bf16[4,128,256]{2,1,0:T(8,128)(2,1)S(1)}, u32[]{:S(2)}, u32[]{:S(2)}) %collective-permute-start.31) | collective-permute-done | bytes 262176 | tf_op jit(solution)/shard_map/ppermute | solution.py:429
  106.2 1.7 %collective-permute-start.33 = (bf16[4,128,256]{2,1,0:T(8,128)(2,1)S(1)}, bf16[4,128,256]{2,1,0:T(8,128)(2,1)S(1)}, u32[]{:S(2)}, u32[]{:S(2)}) collective-permute-start(bf16[4,128,256]{2,1,0:T(8,128)(2,1)S(1)} %get-tuple-element.43.refs_0_), channel_id=1, source_target_pairs={{0,8},{2,10},{4,12},{6,14},{8,0},{10,2},{12,4},{14,6},{1,9},{3,11}... | collective-permute-start | bytes 786440 | tf_op jit(solution)/shard_map/ppermute | solution.py:425
  107.9 10.7 %collective-permute-done.32.refs_1_ = bf16[4,128,256]{2,1,0:T(8,128)(2,1)S(1)} collective-permute-done((bf16[4,128,256]{2,1,0:T(8,128)(2,1)S(1)}, bf16[4,128,256]{2,1,0:T(8,128)(2,1)S(1)}, u32[]{:S(2)}, u32[]{:S(2)}) %collective-permute-start.32) | collective-permute-done | bytes 262176 | tf_op jit(solution)/shard_map/ppermute | solution.py:425
  118.6 2.2 %collective-permute-done.33.refs_2_ = bf16[4,128,256]{2,1,0:T(8,128)(2,1)S(1)} collective-permute-done((bf16[4,128,256]{2,1,0:T(8,128)(2,1)S(1)}, bf16[4,128,256]{2,1,0:T(8,128)(2,1)S(1)}, u32[]{:S(2)}, u32[]{:S(2)}) %collective-permute-start.33) | collective-permute-done | bytes 262176 | tf_op jit(solution)/shard_map/ppermute | solution.py:425
  120.9 1.5 %collective-permute-done.36.refs_5_ = bf16[4,128,256]{2,1,0:T(8,128)(2,1)S(1)} collective-permute-done((bf16[4,128,256]{2,1,0:T(8,128)(2,1)S(1)}, bf16[4,128,256]{2,1,0:T(8,128)(2,1)S(1)}, u32[]{:S(2)}, u32[]{:S(2)}) %collective-permute-start.36) | collective-permute-done | bytes 262176 | tf_op jit(solution)/shard_map/ppermute | solution.py:429
  122.4 0.8 base_application.1.base_ref
  123.2 6.4 %collective-permute-done.37.mine = bf16[4,128,256]{2,1,0:T(8,128)(2,1)S(1)} collective-permute-done((bf16[4,128,256]{2,1,0:T(8,128)(2,1)S(1)}, bf16[4,128,256]{2,1,0:T(8,128)(2,1)S(1)}, u32[]{:S(2)}, u32[]{:S(2)}) %collective-permute-start.37) | collective-permute-done | bytes 262176 | tf_op jit(solution)/shard_map/ppermute | solution.py:425
  129.6 0.6 copy.8
  130.3 0.9 collective-permute-done.38.theirs
  131.1 1.2 second_application.1
  (61 shorter events, 3.1 us)
Async XLA Ops:
  0.6 25.0 %collective-permute-start.3 = (bf16[2,1024,256]{2,1,0:T(8,128)(2,1)}, bf16[2,1024,256]{2,1,0:T(8,128)(2,1)S(1)}, u32[]{:S(2)}, u32[]{:S(2)}) collective-permute-start(bf16[2,1024,256]{2,1,0:T(8,128)(2,1)} %mine_ref.1), channel_id=1, source_target_pairs={{0,2},{2,0},{4,6},{6,4},{8,10},{10,8},{12,14},{14,12},{1,3},{3,1},... | collective-permute-start | bytes 3145736 | tf_op jit(solution)/shard_map/ppermute | solution.py:429
  1.1 16.5 %collective-permute-start.1 = (bf16[4,128,256]{2,1,0:T(8,128)(2,1)}, bf16[4,128,256]{2,1,0:T(8,128)(2,1)S(1)}, u32[]{:S(2)}, u32[]{:S(2)}) collective-permute-start(bf16[4,128,256]{2,1,0:T(8,128)(2,1)} %here_ref.1), channel_id=1, source_target_pairs={{0,8},{2,10},{4,12},{6,14},{8,0},{10,2},{12,4},{14,6},{1,9},{3,11}... | collective-permute-start | bytes 786440 | tf_op jit(solution)/shard_map/ppermute | solution.py:425
  4.8 20.3 %collective-permute-start = (bf16[4,128,256]{2,1,0:T(8,128)(2,1)}, bf16[4,128,256]{2,1,0:T(8,128)(2,1)S(1)}, u32[]{:S(2)}, u32[]{:S(2)}) collective-permute-start(bf16[4,128,256]{2,1,0:T(8,128)(2,1)} %here_ref.1), channel_id=1, source_target_pairs={{0,4},{2,6},{4,0},{6,2},{8,12},{10,14},{12,8},{14,10},{1,5},{3,7},... | collective-permute-start | bytes 786440 | tf_op jit(solution)/shard_map/ppermute | solution.py:425
  17.6 8.0 %collective-permute-start.2 = (bf16[4,128,256]{2,1,0:T(8,128)(2,1)S(1)}, bf16[4,128,256]{2,1,0:T(8,128)(2,1)S(1)}, u32[]{:S(2)}, u32[]{:S(2)}) collective-permute-start(bf16[4,128,256]{2,1,0:T(8,128)(2,1)S(1)} %collective-permute-done.1.two_ref), channel_id=1, source_target_pairs={{0,4},{2,6},{4,0},{6,2},{8,12},{10,14},{12,8},{14,10},{1,5},{3,7},... | collective-permute-start | bytes 786440 | tf_op jit(solution)/shard_map/ppermute | solution.py:425
  18.4 2.2 %copy-start = (bf16[2,1024,1024]{2,1,0:T(8,128)(2,1)S(1)}, bf16[2,1024,1024]{2,1,0:T(8,128)(2,1)}, u32[]{:S(2)}) copy-start(bf16[2,1024,1024]{2,1,0:T(8,128)(2,1)} %full_ref.2) | copy-start | bytes 12582916
  20.6 4.1 %copy-start.6 = (f32[2]{0:T(128)S(1)}, f32[2]{0:T(128)}, u32[]{:S(2)}) copy-start(f32[2]{0:T(128)} %param.9) | copy-start | bytes 28
  20.6 4.3 %copy-start.5 = (f32[4,2]{0,1:T(2,128)S(1)}, f32[4,2]{0,1:T(2,128)}, u32[]{:S(2)}) copy-start(f32[4,2]{0,1:T(2,128)} %param.10) | copy-start | bytes 100
  20.6 5.1 %copy-start.3 = (bf16[2,1024,256]{2,1,0:T(8,128)(2,1)S(1)}, bf16[2,1024,256]{2,1,0:T(8,128)(2,1)}, u32[]{:S(2)}) copy-start(bf16[2,1024,256]{2,1,0:T(8,128)(2,1)} %mine_ref.1) | copy-start | bytes 3145732
  20.6 5.1 %copy-start.4 = (bf16[4,128,256]{2,1,0:T(8,128)(2,1)S(1)}, bf16[4,128,256]{2,1,0:T(8,128)(2,1)}, u32[]{:S(2)}) copy-start(bf16[4,128,256]{2,1,0:T(8,128)(2,1)} %here_ref.1) | copy-start | bytes 786436
  21.4 27.7 %collective-permute-start.16 = (bf16[128,1024]{1,0:T(8,128)(2,1)}, bf16[128,1024]{1,0:T(8,128)(2,1)}, u32[]{:S(2)}, u32[]{:S(2)}) collective-permute-start(bf16[128,1024]{1,0:T(8,128)(2,1)} %get-tuple-element.25), channel_id=1, source_target_pairs={{0,8},{2,10},{4,12},{6,14},{8,0},{10,2},{12,4},{14,6},{1,9},{3,11}... | collective-permute-start | bytes 786440 | tf_op jit(solution)/shard_map/ppermute | solution.py:425
  25.1 9.1 %collective-permute-start.5 = (f32[16,128]{1,0:T(8,128)S(1)}, f32[16,128]{1,0:T(8,128)S(1)}, u32[]{:S(2)}, u32[]{:S(2)}) collective-permute-start(f32[16,128]{1,0:T(8,128)S(1)} %broadcast_in_dim.10.noise_ref), channel_id=1, source_target_pairs={{0,2},{2,0},{4,6},{6,4},{8,10},{10,8},{12,14},{14,12},{1,3},{3,1},... | collective-permute-start | bytes 24584 | tf_op jit(solution)/shard_map/ppermute | solution.py:429
  26.7 7.6 %collective-permute-start.4 = (f32[16,128]{1,0:T(8,128)S(1)}, f32[16,128]{1,0:T(8,128)S(1)}, u32[]{:S(2)}, u32[]{:S(2)}) collective-permute-start(f32[16,128]{1,0:T(8,128)S(1)} %chip_bias.1.mine_ref), channel_id=1, source_target_pairs={{0,2},{2,0},{4,6},{6,4},{8,10},{10,8},{12,14},{14,12},{1,3},{3,1},... | collective-permute-start | bytes 24584 | tf_op jit(solution)/shard_map/ppermute | solution.py:429
  26.7 27.8 %collective-permute-start.14 = (bf16[128,1024]{1,0:T(8,128)(2,1)S(1)}, bf16[128,1024]{1,0:T(8,128)(2,1)S(1)}, u32[]{:S(2)}, u32[]{:S(2)}) collective-permute-start(bf16[128,1024]{1,0:T(8,128)(2,1)S(1)} %get-tuple-element.33), channel_id=1, source_target_pairs={{0,8},{2,10},{4,12},{6,14},{8,0},{10,2},{12,4},{14,6},{1,9},{3,11}... | collective-permute-start | bytes 786440 | tf_op jit(solution)/shard_map/ppermute | solution.py:425
  29.9 2.2 %copy-start.1 = (bf16[2,1024,1024]{2,1,0:T(8,128)(2,1)S(1)}, bf16[2,1024,1024]{2,1,0:T(8,128)(2,1)}, u32[]{:S(2)}) copy-start(bf16[2,1024,1024]{2,1,0:T(8,128)(2,1)} %full_ref.2) | copy-start | bytes 12582916
  32.1 39.6 %copy-start.2 = (f32[1,128,4,256]{3,2,1,0:T(4,128)S(1)}, f32[1,128,4,256]{3,2,1,0:T(4,128)}, u32[]{:S(2)}) copy-start(f32[1,128,4,256]{3,2,1,0:T(4,128)} %orbitals_ref.3) | copy-start | bytes 1572868
  32.3 23.7 %collective-permute-start.22 = (bf16[128,1024]{1,0:T(8,128)(2,1)S(1)}, bf16[128,1024]{1,0:T(8,128)(2,1)S(1)}, u32[]{:S(2)}, u32[]{:S(2)}) collective-permute-start(bf16[128,1024]{1,0:T(8,128)(2,1)S(1)} %get-tuple-element.38), channel_id=1, source_target_pairs={{0,12},{2,14},{4,8},{6,10},{8,4},{10,6},{12,0},{14,2},{1,13},{3,15... | collective-permute-start | bytes 786440 | tf_op jit(solution)/shard_map/ppermute | solution.py:425
  49.1 10.8 %collective-permute-start.17 = (bf16[128,1024]{1,0:T(8,128)(2,1)}, bf16[128,1024]{1,0:T(8,128)(2,1)S(1)}, u32[]{:S(2)}, u32[]{:S(2)}) collective-permute-start(bf16[128,1024]{1,0:T(8,128)(2,1)} %collective-permute-done.16), channel_id=1, source_target_pairs={{0,2},{2,0},{4,6},{6,4},{8,10},{10,8},{12,14},{14,12},{1,3},{3,1},... | collective-permute-start | bytes 786440 | tf_op jit(solution)/shard_map/ppermute | solution.py:429
  49.1 7.0 %collective-permute-start.6 = (f32[16,128]{1,0:T(8,128)S(1)}, f32[16,128]{1,0:T(8,128)S(1)}, u32[]{:S(2)}, u32[]{:S(2)}) collective-permute-start(f32[16,128]{1,0:T(8,128)S(1)} %get-tuple-element.24.field_here), channel_id=1, source_target_pairs={{0,4},{2,6},{4,0},{6,2},{8,12},{10,14},{12,8},{14,10},{1,5},{3,7},... | collective-permute-start | bytes 24584 | tf_op jit(solution)/shard_map/ppermute | solution.py:425
  54.6 7.8 %collective-permute-start.15 = (bf16[128,1024]{1,0:T(8,128)(2,1)S(1)}, bf16[128,1024]{1,0:T(8,128)(2,1)S(1)}, u32[]{:S(2)}, u32[]{:S(2)}) collective-permute-start(bf16[128,1024]{1,0:T(8,128)(2,1)S(1)} %collective-permute-done.14.refs_4_), channel_id=1, source_target_pairs={{0,1},{1,0},{2,3},{3,2},{4,5},{5,4},{6,7},{7,6},{8,9},{9,8},{10,11... | collective-permute-start | bytes 786440 | tf_op jit(solution)/shard_map/ppermute | solution.py:433
  56.0 7.8 %collective-permute-start.23 = (bf16[128,1024]{1,0:T(8,128)(2,1)S(1)}, bf16[128,1024]{1,0:T(8,128)(2,1)S(1)}, u32[]{:S(2)}, u32[]{:S(2)}) collective-permute-start(bf16[128,1024]{1,0:T(8,128)(2,1)S(1)} %collective-permute-done.22), channel_id=1, source_target_pairs={{0,2},{2,0},{4,6},{6,4},{8,10},{10,8},{12,14},{14,12},{1,3},{3,1},... | collective-permute-start | bytes 786440 | tf_op jit(solution)/shard_map/ppermute | solution.py:429
  56.0 15.1 %collective-permute-start.11 = (bf16[128,1024]{1,0:T(8,128)(2,1)S(1)}, bf16[128,1024]{1,0:T(8,128)(2,1)S(1)}, u32[]{:S(2)}, u32[]{:S(2)}) collective-permute-start(bf16[128,1024]{1,0:T(8,128)(2,1)S(1)} %get-tuple-element.32), channel_id=1, source_target_pairs={{0,4},{2,6},{4,0},{6,2},{8,12},{10,14},{12,8},{14,10},{1,5},{3,7},... | collective-permute-start | bytes 786440 | tf_op jit(solution)/shard_map/ppermute | solution.py:425
  59.9 11.3 %collective-permute-start.18 = (bf16[128,1024]{1,0:T(8,128)(2,1)S(1)}, bf16[128,1024]{1,0:T(8,128)(2,1)S(1)}, u32[]{:S(2)}, u32[]{:S(2)}) collective-permute-start(bf16[128,1024]{1,0:T(8,128)(2,1)S(1)} %collective-permute-done.17.refs_6_), channel_id=1, source_target_pairs={{0,1},{1,0},{2,3},{3,2},{4,5},{5,4},{6,7},{7,6},{8,9},{9,8},{10,11... | collective-permute-start | bytes 786440 | tf_op jit(solution)/shard_map/ppermute | solution.py:433
  61.3 5.3 %collective-permute-start.7 = (f32[16,128]{1,0:T(8,128)S(1)}, f32[16,128]{1,0:T(8,128)S(1)}, u32[]{:S(2)}, u32[]{:S(2)}) collective-permute-start(f32[16,128]{1,0:T(8,128)S(1)} %get-tuple-element.24.field_here), channel_id=1, source_target_pairs={{0,8},{2,10},{4,12},{6,14},{8,0},{10,2},{12,4},{14,6},{1,9},{3,11}... | collective-permute-start | bytes 24584 | tf_op jit(solution)/shard_map/ppermute | solution.py:425
  62.4 7.3 %collective-permute-start.19 = (f32[16,128]{1,0:T(8,128)S(1)}, f32[16,128]{1,0:T(8,128)S(1)}, u32[]{:S(2)}, u32[]{:S(2)}) collective-permute-start(f32[16,128]{1,0:T(8,128)S(1)} %get-tuple-element.24.field_here), channel_id=1, source_target_pairs={{0,12},{2,14},{4,8},{6,10},{8,4},{10,6},{12,0},{14,2},{1,13},{3,15... | collective-permute-start | bytes 24584 | tf_op jit(solution)/shard_map/ppermute | solution.py:425
  63.8 9.0 %collective-permute-start.9 = (bf16[128,1024]{1,0:T(8,128)(2,1)S(1)}, bf16[128,1024]{1,0:T(8,128)(2,1)S(1)}, u32[]{:S(2)}, u32[]{:S(2)}) collective-permute-start(bf16[128,1024]{1,0:T(8,128)(2,1)S(1)} %get-tuple-element.31), channel_id=1, source_target_pairs={{0,4},{2,6},{4,0},{6,2},{8,12},{10,14},{12,8},{14,10},{1,5},{3,7},... | collective-permute-start | bytes 786440 | tf_op jit(solution)/shard_map/ppermute | solution.py:425
  66.7 7.6 %collective-permute-start.24 = (bf16[128,1024]{1,0:T(8,128)(2,1)S(1)}, bf16[128,1024]{1,0:T(8,128)(2,1)S(1)}, u32[]{:S(2)}, u32[]{:S(2)}) collective-permute-start(bf16[128,1024]{1,0:T(8,128)(2,1)S(1)} %collective-permute-done.23.refs_2_), channel_id=1, source_target_pairs={{0,1},{1,0},{2,3},{3,2},{4,5},{5,4},{6,7},{7,6},{8,9},{9,8},{10,11... | collective-permute-start | bytes 786440 | tf_op jit(solution)/shard_map/ppermute | solution.py:433
  69.7 11.3 %collective-permute-start.20 = (bf16[128,1024]{1,0:T(8,128)(2,1)S(1)}, bf16[128,1024]{1,0:T(8,128)(2,1)S(1)}, u32[]{:S(2)}, u32[]{:S(2)}) collective-permute-start(bf16[128,1024]{1,0:T(8,128)(2,1)S(1)} %get-tuple-element.37), channel_id=1, source_target_pairs={{0,12},{2,14},{4,8},{6,10},{8,4},{10,6},{12,0},{14,2},{1,13},{3,15... | collective-permute-start | bytes 786440 | tf_op jit(solution)/shard_map/ppermute | solution.py:425
  71.1 13.0 %collective-permute-start.12 = (bf16[128,1024]{1,0:T(8,128)(2,1)S(1)}, bf16[128,1024]{1,0:T(8,128)(2,1)S(1)}, u32[]{:S(2)}, u32[]{:S(2)}) collective-permute-start(bf16[128,1024]{1,0:T(8,128)(2,1)S(1)} %collective-permute-done.11), channel_id=1, source_target_pairs={{0,2},{2,0},{4,6},{6,4},{8,10},{10,8},{12,14},{14,12},{1,3},{3,1},... | collective-permute-start | bytes 786440 | tf_op jit(solution)/shard_map/ppermute | solution.py:429
  71.1 24.5 %collective-permute-start.8 = (bf16[2,128,1024]{2,1,0:T(8,128)(2,1)S(1)}, bf16[2,128,1024]{2,1,0:T(8,128)(2,1)S(1)}, u32[]{:S(2)}, u32[]{:S(2)}) collective-permute-start(bf16[2,128,1024]{2,1,0:T(8,128)(2,1)S(1)} %get-tuple-element.28), channel_id=1, source_target_pairs={{0,2},{2,0},{4,6},{6,4},{8,10},{10,8},{12,14},{14,12},{1,3},{3,1},... | collective-permute-start | bytes 1572872 | tf_op jit(solution)/shard_map/ppermute | solution.py:429
  72.8 11.9 %collective-permute-start.10 = (bf16[128,1024]{1,0:T(8,128)(2,1)S(1)}, bf16[128,1024]{1,0:T(8,128)(2,1)S(1)}, u32[]{:S(2)}, u32[]{:S(2)}) collective-permute-start(bf16[128,1024]{1,0:T(8,128)(2,1)S(1)} %collective-permute-done.9.refs_0_), channel_id=1, source_target_pairs={{0,1},{1,0},{2,3},{3,2},{4,5},{5,4},{6,7},{7,6},{8,9},{9,8},{10,11... | collective-permute-start | bytes 786440 | tf_op jit(solution)/shard_map/ppermute | solution.py:433
  74.3 14.4 %collective-permute-start.25 = (bf16[4,128,256]{2,1,0:T(8,128)(2,1)S(1)}, bf16[4,128,256]{2,1,0:T(8,128)(2,1)S(1)}, u32[]{:S(2)}, u32[]{:S(2)}) collective-permute-start(bf16[4,128,256]{2,1,0:T(8,128)(2,1)S(1)} %walker_major.1.refs_0_), channel_id=1, source_target_pairs={{0,4},{2,6},{4,0},{6,2},{8,12},{10,14},{12,8},{14,10},{1,5},{3,7},... | collective-permute-start | bytes 786440 | tf_op jit(solution)/shard_map/ppermute | solution.py:425
  81.0 14.1 %collective-permute-start.26 = (bf16[4,128,256]{2,1,0:T(8,128)(2,1)S(1)}, bf16[4,128,256]{2,1,0:T(8,128)(2,1)S(1)}, u32[]{:S(2)}, u32[]{:S(2)}) collective-permute-start(bf16[4,128,256]{2,1,0:T(8,128)(2,1)S(1)} %walker_major.1.refs_0_), channel_id=1, source_target_pairs={{0,8},{2,10},{4,12},{6,14},{8,0},{10,2},{12,4},{14,6},{1,9},{3,11}... | collective-permute-start | bytes 786440 | tf_op jit(solution)/shard_map/ppermute | solution.py:425
  84.1 11.0 %collective-permute-start.13 = (bf16[128,1024]{1,0:T(8,128)(2,1)S(1)}, bf16[128,1024]{1,0:T(8,128)(2,1)S(1)}, u32[]{:S(2)}, u32[]{:S(2)}) collective-permute-start(bf16[128,1024]{1,0:T(8,128)(2,1)S(1)} %collective-permute-done.12.refs_2_), channel_id=1, source_target_pairs={{0,1},{1,0},{2,3},{3,2},{4,5},{5,4},{6,7},{7,6},{8,9},{9,8},{10,11... | collective-permute-start | bytes 786440 | tf_op jit(solution)/shard_map/ppermute | solution.py:433
  84.7 15.9 %collective-permute-start.27 = (bf16[4,128,256]{2,1,0:T(8,128)(2,1)S(1)}, bf16[4,128,256]{2,1,0:T(8,128)(2,1)S(1)}, u32[]{:S(2)}, u32[]{:S(2)}) collective-permute-start(bf16[4,128,256]{2,1,0:T(8,128)(2,1)S(1)} %walker_major.1.refs_0_), channel_id=1, source_target_pairs={{0,2},{2,0},{4,6},{6,4},{8,10},{10,8},{12,14},{14,12},{1,3},{3,1},... | collective-permute-start | bytes 786440 | tf_op jit(solution)/shard_map/ppermute | solution.py:429
  88.7 10.3 %collective-permute-start.21 = (bf16[128,1024]{1,0:T(8,128)(2,1)S(1)}, bf16[128,1024]{1,0:T(8,128)(2,1)S(1)}, u32[]{:S(2)}, u32[]{:S(2)}) collective-permute-start(bf16[128,1024]{1,0:T(8,128)(2,1)S(1)} %collective-permute-done.20.refs_0_), channel_id=1, source_target_pairs={{0,1},{1,0},{2,3},{3,2},{4,5},{5,4},{6,7},{7,6},{8,9},{9,8},{10,11... | collective-permute-start | bytes 786440 | tf_op jit(solution)/shard_map/ppermute | solution.py:433
  95.1 5.5 %collective-permute-start.28 = (bf16[4,128,256]{2,1,0:T(8,128)(2,1)S(1)}, bf16[4,128,256]{2,1,0:T(8,128)(2,1)S(1)}, u32[]{:S(2)}, u32[]{:S(2)}) collective-permute-start(bf16[4,128,256]{2,1,0:T(8,128)(2,1)S(1)} %collective-permute-done.25.refs_1_), channel_id=1, source_target_pairs={{0,2},{2,0},{4,6},{6,4},{8,10},{10,8},{12,14},{14,12},{1,3},{3,1},... | collective-permute-start | bytes 786440 | tf_op jit(solution)/shard_map/ppermute | solution.py:429
  95.1 5.5 %collective-permute-start.29 = (bf16[4,128,256]{2,1,0:T(8,128)(2,1)S(1)}, bf16[4,128,256]{2,1,0:T(8,128)(2,1)S(1)}, u32[]{:S(2)}, u32[]{:S(2)}) collective-permute-start(bf16[4,128,256]{2,1,0:T(8,128)(2,1)S(1)} %collective-permute-done.26.refs_2_), channel_id=1, source_target_pairs={{0,2},{2,0},{4,6},{6,4},{8,10},{10,8},{12,14},{14,12},{1,3},{3,1},... | collective-permute-start | bytes 786440 | tf_op jit(solution)/shard_map/ppermute | solution.py:429
  95.6 8.3 %collective-permute-start.30 = (bf16[4,128,256]{2,1,0:T(8,128)(2,1)S(1)}, bf16[4,128,256]{2,1,0:T(8,128)(2,1)S(1)}, u32[]{:S(2)}, u32[]{:S(2)}) collective-permute-start(bf16[4,128,256]{2,1,0:T(8,128)(2,1)S(1)} %collective-permute-done.26.refs_2_), channel_id=1, source_target_pairs={{0,4},{2,6},{4,0},{6,2},{8,12},{10,14},{12,8},{14,10},{1,5},{3,7},... | collective-permute-start | bytes 786440 | tf_op jit(solution)/shard_map/ppermute | solution.py:425
  103.9 1.5 %collective-permute-start.31 = (bf16[4,128,256]{2,1,0:T(8,128)(2,1)S(1)}, bf16[4,128,256]{2,1,0:T(8,128)(2,1)S(1)}, u32[]{:S(2)}, u32[]{:S(2)}) collective-permute-start(bf16[4,128,256]{2,1,0:T(8,128)(2,1)S(1)} %collective-permute-done.30.mine), channel_id=1, source_target_pairs={{0,2},{2,0},{4,6},{6,4},{8,10},{10,8},{12,14},{14,12},{1,3},{3,1},... | collective-permute-start | bytes 786440 | tf_op jit(solution)/shard_map/ppermute | solution.py:429
  105.8 12.8 %collective-permute-start.32 = (bf16[4,128,256]{2,1,0:T(8,128)(2,1)S(1)}, bf16[4,128,256]{2,1,0:T(8,128)(2,1)S(1)}, u32[]{:S(2)}, u32[]{:S(2)}) collective-permute-start(bf16[4,128,256]{2,1,0:T(8,128)(2,1)S(1)} %get-tuple-element.43.refs_0_), channel_id=1, source_target_pairs={{0,4},{2,6},{4,0},{6,2},{8,12},{10,14},{12,8},{14,10},{1,5},{3,7},... | collective-permute-start | bytes 786440 | tf_op jit(solution)/shard_map/ppermute | solution.py:425
  106.2 14.7 %collective-permute-start.33 = (bf16[4,128,256]{2,1,0:T(8,128)(2,1)S(1)}, bf16[4,128,256]{2,1,0:T(8,128)(2,1)S(1)}, u32[]{:S(2)}, u32[]{:S(2)}) collective-permute-start(bf16[4,128,256]{2,1,0:T(8,128)(2,1)S(1)} %get-tuple-element.43.refs_0_), channel_id=1, source_target_pairs={{0,8},{2,10},{4,12},{6,14},{8,0},{10,2},{12,4},{14,6},{1,9},{3,11}... | collective-permute-start | bytes 786440 | tf_op jit(solution)/shard_map/ppermute | solution.py:425
  107.9 13.0 %collective-permute-start.34 = (bf16[4,128,256]{2,1,0:T(8,128)(2,1)S(1)}, bf16[4,128,256]{2,1,0:T(8,128)(2,1)S(1)}, u32[]{:S(2)}, u32[]{:S(2)}) collective-permute-start(bf16[4,128,256]{2,1,0:T(8,128)(2,1)S(1)} %get-tuple-element.43.refs_0_), channel_id=1, source_target_pairs={{0,2},{2,0},{4,6},{6,4},{8,10},{10,8},{12,14},{14,12},{1,3},{3,1},... | collective-permute-start | bytes 786440 | tf_op jit(solution)/shard_map/ppermute | solution.py:429
  118.6 2.3 %collective-permute-start.35 = (bf16[4,128,256]{2,1,0:T(8,128)(2,1)S(1)}, bf16[4,128,256]{2,1,0:T(8,128)(2,1)S(1)}, u32[]{:S(2)}, u32[]{:S(2)}) collective-permute-start(bf16[4,128,256]{2,1,0:T(8,128)(2,1)S(1)} %collective-permute-done.32.refs_1_), channel_id=1, source_target_pairs={{0,2},{2,0},{4,6},{6,4},{8,10},{10,8},{12,14},{14,12},{1,3},{3,1},... | collective-permute-start | bytes 786440 | tf_op jit(solution)/shard_map/ppermute | solution.py:429
  120.9 1.5 %collective-permute-start.36 = (bf16[4,128,256]{2,1,0:T(8,128)(2,1)S(1)}, bf16[4,128,256]{2,1,0:T(8,128)(2,1)S(1)}, u32[]{:S(2)}, u32[]{:S(2)}) collective-permute-start(bf16[4,128,256]{2,1,0:T(8,128)(2,1)S(1)} %collective-permute-done.33.refs_2_), channel_id=1, source_target_pairs={{0,2},{2,0},{4,6},{6,4},{8,10},{10,8},{12,14},{14,12},{1,3},{3,1},... | collective-permute-start | bytes 786440 | tf_op jit(solution)/shard_map/ppermute | solution.py:429
  120.9 8.7 %collective-permute-start.37 = (bf16[4,128,256]{2,1,0:T(8,128)(2,1)S(1)}, bf16[4,128,256]{2,1,0:T(8,128)(2,1)S(1)}, u32[]{:S(2)}, u32[]{:S(2)}) collective-permute-start(bf16[4,128,256]{2,1,0:T(8,128)(2,1)S(1)} %collective-permute-done.33.refs_2_), channel_id=1, source_target_pairs={{0,4},{2,6},{4,0},{6,2},{8,12},{10,14},{12,8},{14,10},{1,5},{3,7},... | collective-permute-start | bytes 786440 | tf_op jit(solution)/shard_map/ppermute | solution.py:425
  129.6 1.5 %collective-permute-start.38 = (bf16[4,128,256]{2,1,0:T(8,128)(2,1)S(1)}, bf16[4,128,256]{2,1,0:T(8,128)(2,1)S(1)}, u32[]{:S(2)}, u32[]{:S(2)}) collective-permute-start(bf16[4,128,256]{2,1,0:T(8,128)(2,1)S(1)} %collective-permute-done.37.mine), channel_id=1, source_target_pairs={{0,2},{2,0},{4,6},{6,4},{8,10},{10,8},{12,14},{14,12},{1,3},{3,1},... | collective-permute-start | bytes 786440 | tf_op jit(solution)/shard_map/ppermute | solution.py:429

commit v7 on v6

--- a/solution.py
+++ b/solution.py
@@ -65,6 +65,7 @@
 narrow = jnp.bfloat16
 small = pltpu.CompilerParams(vmem_limit_bytes=8 << 20)
 large = pltpu.CompilerParams(vmem_limit_bytes=16 << 20)
+brief = pl.CostEstimate(flops=0, bytes_accessed=0, transcendentals=0)
 
 
 def after(value, *others):
@@ -108,6 +109,7 @@
         out_specs=[vmem_spec] * len(wanted),
         scratch_shapes=[pltpu.SemaphoreType.DMA((len(wanted),))],
         compiler_params=small,
+        cost_estimate=brief,
         name="cut_rows",
     )(full_chol)
 
@@ -125,6 +127,7 @@
         in_specs=[vmem_spec],
         out_specs=vmem_spec,
         compiler_params=small,
+        cost_estimate=brief,
         name="walker_major",
     )(orbitals)
 
@@ -172,6 +175,7 @@
         in_specs=[vmem_spec] * 6,
         out_specs=vmem_spec,
         compiler_params=small,
+        cost_estimate=brief,
         name="chip_bias",
     )(*green, mine, theirs)
 
@@ -184,10 +188,13 @@
         shift = jnp.clip(time_root * (force - consts[high, :]), -1.0, 1.0)
         field_ref[rows, :] = consts[low, :] - shift
         if rows is low:
-            walkers, vectors = shift_ref.shape
+            vectors, walkers = shift_ref.shape
+            row = lax.broadcasted_iota(jnp.int32, (walkers, 128), 0)
+            lane = lax.broadcasted_iota(jnp.int32, (walkers, 128), 1)
             for vector in range(vectors):
-                part = shift[vector * walkers : (vector + 1) * walkers, :1]
-                shift_ref[:, vector : vector + 1] = part
+                part = shift[vector * walkers : (vector + 1) * walkers, :]
+                picked = jnp.sum(jnp.where(row == lane, part, 0.0), axis=0, keepdims=True)
+                shift_ref[vector : vector + 1, :] = picked[:, :walkers]
 
 
 def chip_field(mine, theirs, noise, noise_there, walkers):
@@ -195,12 +202,13 @@
     return pl.pallas_call(
         field_kernel,
         out_shape=[
-            jax.ShapeDtypeStruct((walkers, entries // 2 // walkers), wide),
+            jax.ShapeDtypeStruct((entries // 2 // walkers, walkers), wide),
             jax.ShapeDtypeStruct((entries, 128), wide),
         ],
         in_specs=[vmem_spec] * 4,
         out_specs=[vmem_spec] * 2,
         compiler_params=small,
+        cost_estimate=brief,
         name="chip_field",
     )(mine, theirs, noise, noise_there)
 
@@ -276,6 +284,7 @@
         in_specs=[vmem_spec] * (5 + len(blocks)),
         out_specs=vmem_spec,
         compiler_params=large,
+        cost_estimate=brief,
         name="early_operator",
     )(*fields, own, own_theirs, *blocks)
 
@@ -309,6 +318,7 @@
         in_specs=[vmem_spec] * (2 + len(blocks)),
         out_specs=vmem_spec,
         compiler_params=large,
+        cost_estimate=brief,
         name="split_operator",
     )(summed, field, *blocks)
 
@@ -350,6 +360,7 @@
         out_specs=vmem_spec,
         scratch_shapes=[pltpu.VMEM((3, walkers, 2 * rows, occupied), narrow)],
         compiler_params=small,
+        cost_estimate=brief,
         name="near_application",
     )(operator, *pieces)
 
@@ -374,6 +385,7 @@
         out_specs=[vmem_spec] * 2,
         scratch_shapes=[pltpu.VMEM((walkers, 2 * rows, occupied), narrow)],
         compiler_params=small,
+        cost_estimate=brief,
         name="first_application",
     )(operator, partial, mine, theirs)
 
@@ -398,6 +410,7 @@
         out_specs=vmem_spec,
         scratch_shapes=[pltpu.VMEM((3, walkers, 2 * rows, occupied), narrow)],
         compiler_params=small,
+        cost_estimate=brief,
         name="base_application",
     )(operator, first_term, orbitals, *pieces)
 
@@ -417,6 +430,7 @@
         out_specs=vmem_spec,
         scratch_shapes=[pltpu.VMEM((walkers, 2 * rows, occupied), narrow)],
         compiler_params=small,
+        cost_estimate=brief,
         name="second_application",
     )(operator, base, mine, theirs)
 
@@ -446,19 +460,12 @@
     green_three = to_chip(green_two, 1)
 
     cross, straight = {}, {}
-    cross[2], straight[2] = cut(rows, full_chol, ((2, True, False), (2, False, False)))
-    cross[3], straight[3], cross[1], straight[1], own, own_cross = cut(
-        rows,
-        after(full_chol, cross[2]),
-        (
-            (3, True, False),
-            (3, False, False),
-            (1, True, False),
-            (1, False, False),
-            (0, False, True),
-            (0, True, True),
-        ),
-    )
+    wanted = [(step, crossed, False) for step in (2, 3, 1) for crossed in (True, False)]
+    wanted += [(0, False, True), (0, True, True)]
+    pieces = cut(rows, after(full_chol, half_theirs), wanted)
+    for index, step in enumerate((2, 3, 1)):
+        cross[step], straight[step] = pieces[2 * index : 2 * index + 2]
+    own, own_cross = pieces[6:]
     own_theirs = to_core(own_cross)
 
     green = (green_blocks, green_one, green_two, green_three)
@@ -469,7 +476,7 @@
     cross_mine, mine, theirs, mine_x, theirs_x = {}, {}, {}, {}, {}
     cross_mine[2], mine[2] = to_chip(cross[2], 2), to_chip(straight[2], 2)
     cross_mine[3] = to_chip(cross[3], 3)
-    theirs[2] = to_core(after(cross_mine[2], field))
+    theirs[2] = to_core(after(cross_mine[2], field, own_theirs))
     mine[3] = to_chip(after(straight[3], theirs[2]), 3)
     cross[1], straight[1] = after((cross[1], straight[1]), field_one)
     cross_mine[1], mine[1] = to_chip(cross[1], 1), to_chip(straight[1], 1)
@@ -508,7 +515,7 @@
     walkers_next = second_application(
         operator, base, first_three, to_core(after(first_three, base))
     )
-    return (walkers_next, bias_shift)
+    return (walkers_next, bias_shift.T)
 
 
 def solution(mesh):

time: 133 us -> 139 us (1.045)
  waiting for transfers between devices: 74.3 us -> 87.4 us
  starting transfers between devices: 41.3 us -> 30.6 us
  Pallas kernels: 10.6 us -> 13.4 us
    ppermute x6, waiting for transfers between devices: 0.02 us -> 22 us  [across(): return lax.ppermute(value, 'walk', [(0, 1), (1, 0)])]
    ppermute x18, waiting for transfers between devices: 70.3 us -> 59.7 us  [to_chip(): return lax.ppermute(value, 'chol', [(i, i ^ 2 * step) for i in range(8)])]
    ppermute x18, starting transfers between devices: 31.8 us -> 22 us  [to_chip(): return lax.ppermute(value, 'chol', [(i, i ^ 2 * step) for i in range(8)])]
    ppermute x15, waiting for transfers between devices: 3.96 us -> 5.72 us  [to_core(): return lax.ppermute(value, 'chol', [(i, i ^ 1) for i in range(8)])]
    unnamed x15 -> x32, local copies, waits for them, and re-layouts: 5.04 us -> 5.71 us
  transfers between devices with their start and end apart: 39 -> 39, of which waited for: 17 -> 20; matrix products, arithmetic and copies ran while one was open for 1% -> 0% of each run, Pallas kernels for 7% -> 9%
where the time goes in v7:
time: 139 us; the launch traced here: 138 us
  waiting for transfers between devices  87.4 us (63%)
  starting transfers between devices  30.6 us (22%)
  Pallas kernels  13.4 us (10%)
  local copies, waits for them, and re-layouts  6.01 us (4%)
    ppermute x18, waiting for transfers between devices, to_chip(): return lax.ppermute(value, 'chol', [(i, i ^ 2 * step) for i in range(8)])  59.7 us
    ppermute x6, waiting for transfers between devices, across(): return lax.ppermute(value, 'walk', [(0, 1), (1, 0)])  22 us
    ppermute x18, starting transfers between devices, to_chip(): return lax.ppermute(value, 'chol', [(i, i ^ 2 * step) for i in range(8)])  22 us
    ppermute x6, starting transfers between devices, across(): return lax.ppermute(value, 'walk', [(0, 1), (1, 0)])  7.1 us
    ppermute x15, waiting for transfers between devices, to_core(): return lax.ppermute(value, 'chol', [(i, i ^ 1) for i in range(8)])  5.72 us
    unnamed x32, local copies, waits for them, and re-layouts  5.71 us
    pallas_call x1, Pallas kernels, early_operator(): pl.pallas_call(functools.partial(early_kernel, walkers), out_shape=jax.Sh...  4.37 us
  transfers between devices with their start and end apart: 39, of which 20 were waited for; matrix products, arithmetic and copies ran while one was open for 0% of the time, Pallas kernels for 9%

profile of v7, /device:TPU:0, one launch (start us, length us, event | category | flops | bytes accessed | tf_op | source)
XLA Modules:
  0.0 138.4 jit_solution(3956026090341220714)
XLA Ops:
  1.1 3.7 %collective-permute-start.1 = (bf16[4,128,256]{2,1,0:T(8,128)(2,1)}, bf16[4,128,256]{2,1,0:T(8,128)(2,1)}, u32[]{:S(2)}, u32[]{:S(2)}) collective-permute-start(bf16[4,128,256]{2,1,0:T(8,128)(2,1)} %here_ref.1), channel_id=1, source_target_pairs={{0,8},{2,10},{4,12},{6,14},{8,0},{10,2},{12,4},{14,6},{1,9},{3,11}... | collective-permute-start | bytes 786440 | tf_op jit(solution)/shard_map/ppermute | solution.py:439
  4.8 2.2 %copy-done = bf16[2,1024,1024]{2,1,0:T(8,128)(2,1)S(1)} copy-done((bf16[2,1024,1024]{2,1,0:T(8,128)(2,1)S(1)}, bf16[2,1024,1024]{2,1,0:T(8,128)(2,1)}, u32[]{:S(2)}) %copy-start) | copy-done | bytes 4194328
  7.0 1.2 cut_rows.1
  8.2 0.7 copy-done.4
  8.9 0.7 copy-done.6
  9.6 0.7 copy-done.8
  10.3 0.7 copy-done.10
  11.0 0.7 copy-done.12
  11.9 1.8 %collective-permute-start = (bf16[4,128,256]{2,1,0:T(8,128)(2,1)S(1)}, bf16[4,128,256]{2,1,0:T(8,128)(2,1)}, u32[]{:S(2)}, u32[]{:S(2)}) collective-permute-start(bf16[4,128,256]{2,1,0:T(8,128)(2,1)S(1)} %copy-done.3), channel_id=1, source_target_pairs={{0,4},{2,6},{4,0},{6,2},{8,12},{10,14},{12,8},{14,10},{1,5},{3,7},... | collective-permute-start | bytes 786440 | tf_op jit(solution)/shard_map/ppermute | solution.py:439
  13.6 4.1 %collective-permute-done.1.two_ref = bf16[4,128,256]{2,1,0:T(8,128)(2,1)} collective-permute-done((bf16[4,128,256]{2,1,0:T(8,128)(2,1)}, bf16[4,128,256]{2,1,0:T(8,128)(2,1)}, u32[]{:S(2)}, u32[]{:S(2)}) %collective-permute-start.1) | collective-permute-done | bytes 262176 | tf_op jit(solution)/shard_map/ppermute | solution.py:439
  17.7 0.7 collective-permute-start.2
  18.4 3.4 %collective-permute-start.16 = (bf16[128,1024]{1,0:T(8,128)(2,1)}, bf16[128,1024]{1,0:T(8,128)(2,1)}, u32[]{:S(2)}, u32[]{:S(2)}) collective-permute-start(bf16[128,1024]{1,0:T(8,128)(2,1)} %get-tuple-element.33), channel_id=1, source_target_pairs={{0,8},{2,10},{4,12},{6,14},{8,0},{10,2},{12,4},{14,6},{1,9},{3,11}... | collective-permute-start | bytes 786440 | tf_op jit(solution)/shard_map/ppermute | solution.py:439
  22.3 6.6 %collective-permute-done.one_ref = bf16[4,128,256]{2,1,0:T(8,128)(2,1)} collective-permute-done((bf16[4,128,256]{2,1,0:T(8,128)(2,1)S(1)}, bf16[4,128,256]{2,1,0:T(8,128)(2,1)}, u32[]{:S(2)}, u32[]{:S(2)}) %collective-permute-start) | collective-permute-done | bytes 262176 | tf_op jit(solution)/shard_map/ppermute | solution.py:439
  28.9 5.6 %collective-permute-done.2.three_ref = bf16[4,128,256]{2,1,0:T(8,128)(2,1)} collective-permute-done((bf16[4,128,256]{2,1,0:T(8,128)(2,1)}, bf16[4,128,256]{2,1,0:T(8,128)(2,1)}, u32[]{:S(2)}, u32[]{:S(2)}) %collective-permute-start.2) | collective-permute-done | bytes 262176 | tf_op jit(solution)/shard_map/ppermute | solution.py:439
  34.5 2.1 %chip_bias.1.mine_ref = f32[16,128]{1,0:T(8,128)S(1)} custom-call(bf16[4,128,256]{2,1,0:T(8,128)(2,1)S(1)} %copy-done.3, bf16[4,128,256]{2,1,0:T(8,128)(2,1)} %collective-permute-done.one_ref, bf16[4,128,256]{2,1,0:T(8,128)(2,1)} %collective-permute-done.1.two_ref, bf16[4,128,256]{2,1,0:T(8,128)(2,1)} %collective-permute-done.2.three_ref, ...), custom_call_target="tpu_custom_call" | custom-call | tf_op jit(solution)/shard_map/chip_bias/pallas_call | solution.py:172
  36.7 1.1 collective-permute-done.4.theirs_ref
  37.8 0.6 chip_field.1
  38.6 4.0 %collective-permute-start.7 = (f32[16,128]{1,0:T(8,128)S(1)}, f32[16,128]{1,0:T(8,128)S(1)}, u32[]{:S(2)}, u32[]{:S(2)}) collective-permute-start(f32[16,128]{1,0:T(8,128)S(1)} %get-tuple-element.24.field_here), channel_id=1, source_target_pairs={{0,8},{2,10},{4,12},{6,14},{8,0},{10,2},{12,4},{14,6},{1,9},{3,11}... | collective-permute-start | bytes 24584 | tf_op jit(solution)/shard_map/ppermute | solution.py:439
  43.3 3.7 %collective-permute-start.14 = (bf16[128,1024]{1,0:T(8,128)(2,1)S(1)}, bf16[128,1024]{1,0:T(8,128)(2,1)S(1)}, u32[]{:S(2)}, u32[]{:S(2)}) collective-permute-start(bf16[128,1024]{1,0:T(8,128)(2,1)S(1)} %copy-done.9), channel_id=1, source_target_pairs={{0,8},{2,10},{4,12},{6,14},{8,0},{10,2},{12,4},{14,6},{1,9},{3,11}... | collective-permute-start | bytes 786440 | tf_op jit(solution)/shard_map/ppermute | solution.py:439
  47.1 1.6 %collective-permute-start.19 = (f32[16,128]{1,0:T(8,128)S(1)}, f32[16,128]{1,0:T(8,128)S(1)}, u32[]{:S(2)}, u32[]{:S(2)}) collective-permute-start(f32[16,128]{1,0:T(8,128)S(1)} %get-tuple-element.24.field_here), channel_id=1, source_target_pairs={{0,12},{2,14},{4,8},{6,10},{8,4},{10,6},{12,0},{14,2},{1,13},{3,15... | collective-permute-start | bytes 24584 | tf_op jit(solution)/shard_map/ppermute | solution.py:439
  48.7 4.9 %collective-permute-done.22 = bf16[128,1024]{1,0:T(8,128)(2,1)S(1)} collective-permute-done((bf16[128,1024]{1,0:T(8,128)(2,1)S(1)}, bf16[128,1024]{1,0:T(8,128)(2,1)S(1)}, u32[]{:S(2)}, u32[]{:S(2)}) %collective-permute-start.22) | collective-permute-done | bytes 262176 | tf_op jit(solution)/shard_map/ppermute | solution.py:439
  53.6 6.5 %collective-permute-done.11 = bf16[128,1024]{1,0:T(8,128)(2,1)S(1)} collective-permute-done((bf16[128,1024]{1,0:T(8,128)(2,1)S(1)}, bf16[128,1024]{1,0:T(8,128)(2,1)S(1)}, u32[]{:S(2)}, u32[]{:S(2)}) %collective-permute-start.11) | collective-permute-done | bytes 262176 | tf_op jit(solution)/shard_map/ppermute | solution.py:439
  60.1 9.8 %collective-permute-done.19.field_ref = f32[16,128]{1,0:T(8,128)S(1)} collective-permute-done((f32[16,128]{1,0:T(8,128)S(1)}, f32[16,128]{1,0:T(8,128)S(1)}, u32[]{:S(2)}, u32[]{:S(2)}) %collective-permute-start.19) | collective-permute-done | bytes 8224 | tf_op jit(solution)/shard_map/ppermute | solution.py:439
  69.9 1.5 %collective-permute-start.18 = (bf16[128,1024]{1,0:T(8,128)(2,1)S(1)}, bf16[128,1024]{1,0:T(8,128)(2,1)S(1)}, u32[]{:S(2)}, u32[]{:S(2)}) collective-permute-start(bf16[128,1024]{1,0:T(8,128)(2,1)S(1)} %collective-permute-done.17.refs_6_), channel_id=1, source_target_pairs={{0,1},{1,0},{2,3},{3,2},{4,5},{5,4},{6,7},{7,6},{8,9},{9,8},{10,11... | collective-permute-start | bytes 786440 | tf_op jit(solution)/shard_map/ppermute | solution.py:447
  71.9 1.5 %collective-permute-start.10 = (bf16[128,1024]{1,0:T(8,128)(2,1)S(1)}, bf16[128,1024]{1,0:T(8,128)(2,1)S(1)}, u32[]{:S(2)}, u32[]{:S(2)}) collective-permute-start(bf16[128,1024]{1,0:T(8,128)(2,1)S(1)} %collective-permute-done.9.refs_0_), channel_id=1, source_target_pairs={{0,1},{1,0},{2,3},{3,2},{4,5},{5,4},{6,7},{7,6},{8,9},{9,8},{10,11... | collective-permute-start | bytes 786440 | tf_op jit(solution)/shard_map/ppermute | solution.py:447
  73.9 0.6 collective-permute-start.24
  74.6 1.5 %collective-permute-start.13 = (bf16[128,1024]{1,0:T(8,128)(2,1)S(1)}, bf16[128,1024]{1,0:T(8,128)(2,1)S(1)}, u32[]{:S(2)}, u32[]{:S(2)}) collective-permute-start(bf16[128,1024]{1,0:T(8,128)(2,1)S(1)} %collective-permute-done.12.refs_2_), channel_id=1, source_target_pairs={{0,1},{1,0},{2,3},{3,2},{4,5},{5,4},{6,7},{7,6},{8,9},{9,8},{10,11... | collective-permute-start | bytes 786440 | tf_op jit(solution)/shard_map/ppermute | solution.py:447
  76.0 3.1 %collective-permute-done.18.refs_7_ = bf16[128,1024]{1,0:T(8,128)(2,1)S(1)} collective-permute-done((bf16[128,1024]{1,0:T(8,128)(2,1)S(1)}, bf16[128,1024]{1,0:T(8,128)(2,1)S(1)}, u32[]{:S(2)}, u32[]{:S(2)}) %collective-permute-start.18) | collective-permute-done | bytes 262176 | tf_op jit(solution)/shard_map/ppermute | solution.py:447
  79.6 5.1 %collective-permute-done.15.refs_5_ = bf16[128,1024]{1,0:T(8,128)(2,1)S(1)} collective-permute-done((bf16[128,1024]{1,0:T(8,128)(2,1)S(1)}, bf16[128,1024]{1,0:T(8,128)(2,1)S(1)}, u32[]{:S(2)}, u32[]{:S(2)}) %collective-permute-start.15) | collective-permute-done | bytes 262176 | tf_op jit(solution)/shard_map/ppermute | solution.py:447
  84.8 5.6 %collective-permute-done.10.refs_1_ = bf16[128,1024]{1,0:T(8,128)(2,1)S(1)} collective-permute-done((bf16[128,1024]{1,0:T(8,128)(2,1)S(1)}, bf16[128,1024]{1,0:T(8,128)(2,1)S(1)}, u32[]{:S(2)}, u32[]{:S(2)}) %collective-permute-start.10) | collective-permute-done | bytes 262176 | tf_op jit(solution)/shard_map/ppermute | solution.py:447
  90.4 5.6 %collective-permute-done.24.refs_3_ = bf16[128,1024]{1,0:T(8,128)(2,1)S(1)} collective-permute-done((bf16[128,1024]{1,0:T(8,128)(2,1)S(1)}, bf16[128,1024]{1,0:T(8,128)(2,1)S(1)}, u32[]{:S(2)}, u32[]{:S(2)}) %collective-permute-start.24) | collective-permute-done | bytes 262176 | tf_op jit(solution)/shard_map/ppermute | solution.py:447
  96.0 1.5 %collective-permute-start.21 = (bf16[128,1024]{1,0:T(8,128)(2,1)S(1)}, bf16[128,1024]{1,0:T(8,128)(2,1)S(1)}, u32[]{:S(2)}, u32[]{:S(2)}) collective-permute-start(bf16[128,1024]{1,0:T(8,128)(2,1)S(1)} %collective-permute-done.20.refs_0_), channel_id=1, source_target_pairs={{0,1},{1,0},{2,3},{3,2},{4,5},{5,4},{6,7},{7,6},{8,9},{9,8},{10,11... | collective-permute-start | bytes 786440 | tf_op jit(solution)/shard_map/ppermute | solution.py:447
  97.5 2.6 %collective-permute-done.13.refs_3_ = bf16[128,1024]{1,0:T(8,128)(2,1)S(1)} collective-permute-done((bf16[128,1024]{1,0:T(8,128)(2,1)S(1)}, bf16[128,1024]{1,0:T(8,128)(2,1)S(1)}, u32[]{:S(2)}, u32[]{:S(2)}) %collective-permute-start.13) | collective-permute-done | bytes 262176 | tf_op jit(solution)/shard_map/ppermute | solution.py:447
  100.1 0.9 collective-permute-done.25.refs_1_
  101.4 4.4 %early_operator.1.summed_ref = f32[4,128,1024]{2,1,0:T(8,128)S(1)} custom-call(f32[16,128]{1,0:T(8,128)S(1)} %get-tuple-element.24.field_here, f32[16,128]{1,0:T(8,128)S(1)} %collective-permute-done.6.field_one, f32[16,128]{1,0:T(8,128)S(1)} %collective-permute-done.7.field_two, bf16[2,128,1024]{2,1,0:T(8,128)(2,1)S(1)} %get-tuple-element.26.own, ...), custom_call_target="tpu_custom_call" | custom-call | tf_op jit(solution)/shard_map/early_operator/pallas_call | solution.py:281
  105.8 1.6 %split_operator.1.operator_ref = bf16[4,256,1024]{2,1,0:T(8,128)(2,1)S(1)} custom-call(f32[4,128,1024]{2,1,0:T(8,128)S(1)} %early_operator.1.summed_ref, f32[16,128]{1,0:T(8,128)S(1)} %collective-permute-done.19.field_ref, bf16[128,1024]{1,0:T(8,128)(2,1)S(1)} %collective-permute-done.20.refs_0_, bf16[128,1024]{1,0:T(8,128)(2,1)S(1)} %collective-permute-done.21.refs_1_, ...), custom_call_target="tpu_custom_call" | custom-call | tf_op jit(solution)/shard_map/split_operator/pallas_call | solution.py:315
  107.5 0.7 near_application.1.partial_ref
  108.2 1.5 %collective-permute-done.30.mine = bf16[4,128,256]{2,1,0:T(8,128)(2,1)S(1)} collective-permute-done((bf16[4,128,256]{2,1,0:T(8,128)(2,1)S(1)}, bf16[4,128,256]{2,1,0:T(8,128)(2,1)S(1)}, u32[]{:S(2)}, u32[]{:S(2)}) %collective-permute-start.30) | collective-permute-done | bytes 262176 | tf_op jit(solution)/shard_map/ppermute | solution.py:439
  109.6 1.5 %collective-permute-done.31.theirs = bf16[4,128,256]{2,1,0:T(8,128)(2,1)S(1)} collective-permute-done((bf16[4,128,256]{2,1,0:T(8,128)(2,1)S(1)}, bf16[4,128,256]{2,1,0:T(8,128)(2,1)S(1)}, u32[]{:S(2)}, u32[]{:S(2)}) %collective-permute-start.31) | collective-permute-done | bytes 262176 | tf_op jit(solution)/shard_map/ppermute | solution.py:443
  111.5 0.7 collective-permute-start.32
  112.2 1.1 collective-permute-start.33
  113.4 10.8 %collective-permute-done.32.refs_1_ = bf16[4,128,256]{2,1,0:T(8,128)(2,1)S(1)} collective-permute-done((bf16[4,128,256]{2,1,0:T(8,128)(2,1)S(1)}, bf16[4,128,256]{2,1,0:T(8,128)(2,1)S(1)}, u32[]{:S(2)}, u32[]{:S(2)}) %collective-permute-start.32) | collective-permute-done | bytes 262176 | tf_op jit(solution)/shard_map/ppermute | solution.py:439
  124.2 2.7 %collective-permute-done.33.refs_2_ = bf16[4,128,256]{2,1,0:T(8,128)(2,1)S(1)} collective-permute-done((bf16[4,128,256]{2,1,0:T(8,128)(2,1)S(1)}, bf16[4,128,256]{2,1,0:T(8,128)(2,1)S(1)}, u32[]{:S(2)}, u32[]{:S(2)}) %collective-permute-start.33) | collective-permute-done | bytes 262176 | tf_op jit(solution)/shard_map/ppermute | solution.py:439
  126.9 1.5 %collective-permute-done.36.refs_5_ = bf16[4,128,256]{2,1,0:T(8,128)(2,1)S(1)} collective-permute-done((bf16[4,128,256]{2,1,0:T(8,128)(2,1)S(1)}, bf16[4,128,256]{2,1,0:T(8,128)(2,1)S(1)}, u32[]{:S(2)}, u32[]{:S(2)}) %collective-permute-start.36) | collective-permute-done | bytes 262176 | tf_op jit(solution)/shard_map/ppermute | solution.py:443
  128.4 0.8 base_application.1.base_ref
  129.2 6.4 %collective-permute-done.37.mine = bf16[4,128,256]{2,1,0:T(8,128)(2,1)S(1)} collective-permute-done((bf16[4,128,256]{2,1,0:T(8,128)(2,1)S(1)}, bf16[4,128,256]{2,1,0:T(8,128)(2,1)S(1)}, u32[]{:S(2)}, u32[]{:S(2)}) %collective-permute-start.37) | collective-permute-done | bytes 262176 | tf_op jit(solution)/shard_map/ppermute | solution.py:439
  135.6 1.5 %collective-permute-done.38.theirs = bf16[4,128,256]{2,1,0:T(8,128)(2,1)S(1)} collective-permute-done((bf16[4,128,256]{2,1,0:T(8,128)(2,1)S(1)}, bf16[4,128,256]{2,1,0:T(8,128)(2,1)S(1)}, u32[]{:S(2)}, u32[]{:S(2)}) %collective-permute-start.38) | collective-permute-done | bytes 262176 | tf_op jit(solution)/shard_map/ppermute | solution.py:443
  137.1 1.2 second_application.1
  (77 shorter events, 4.7 us)
Async XLA Ops:
  0.6 4.2 %collective-permute-start.3 = (bf16[2,1024,256]{2,1,0:T(8,128)(2,1)}, bf16[2,1024,256]{2,1,0:T(8,128)(2,1)S(1)}, u32[]{:S(2)}, u32[]{:S(2)}) collective-permute-start(bf16[2,1024,256]{2,1,0:T(8,128)(2,1)} %mine_ref.1), channel_id=1, source_target_pairs={{0,2},{2,0},{4,6},{6,4},{8,10},{10,8},{12,14},{14,12},{1,3},{3,1},... | collective-permute-start | bytes 3145736 | tf_op jit(solution)/shard_map/ppermute | solution.py:443
  1.1 16.6 %collective-permute-start.1 = (bf16[4,128,256]{2,1,0:T(8,128)(2,1)}, bf16[4,128,256]{2,1,0:T(8,128)(2,1)}, u32[]{:S(2)}, u32[]{:S(2)}) collective-permute-start(bf16[4,128,256]{2,1,0:T(8,128)(2,1)} %here_ref.1), channel_id=1, source_target_pairs={{0,8},{2,10},{4,12},{6,14},{8,0},{10,2},{12,4},{14,6},{1,9},{3,11}... | collective-permute-start | bytes 786440 | tf_op jit(solution)/shard_map/ppermute | solution.py:439
  7.0 14.9 %copy-start.15 = (f32[2]{0:T(128)S(1)}, f32[2]{0:T(128)}, u32[]{:S(2)}) copy-start(f32[2]{0:T(128)} %param.9) | copy-start | bytes 28
  7.0 15.0 %copy-start.14 = (f32[4,2]{0,1:T(2,128)S(1)}, f32[4,2]{0,1:T(2,128)}, u32[]{:S(2)}) copy-start(f32[4,2]{0,1:T(2,128)} %param.10) | copy-start | bytes 100
  7.0 27.5 %copy-start.2 = (bf16[2,1024,256]{2,1,0:T(8,128)(2,1)S(1)}, bf16[2,1024,256]{2,1,0:T(8,128)(2,1)}, u32[]{:S(2)}) copy-start(bf16[2,1024,256]{2,1,0:T(8,128)(2,1)} %mine_ref.1) | copy-start | bytes 3145732
  11.7 61.7 %copy-start.1 = (f32[1,128,4,256]{3,2,1,0:T(4,128)S(1)}, f32[1,128,4,256]{3,2,1,0:T(4,128)}, u32[]{:S(2)}) copy-start(f32[1,128,4,256]{3,2,1,0:T(4,128)} %orbitals_ref.3) | copy-start | bytes 1572868
  11.7 26.7 %collective-permute-start.8 = (bf16[2,128,1024]{2,1,0:T(8,128)(2,1)}, bf16[2,128,1024]{2,1,0:T(8,128)(2,1)}, u32[]{:S(2)}, u32[]{:S(2)}) collective-permute-start(bf16[2,128,1024]{2,1,0:T(8,128)(2,1)} %get-tuple-element.27), channel_id=1, source_target_pairs={{0,2},{2,0},{4,6},{6,4},{8,10},{10,8},{12,14},{14,12},{1,3},{3,1},... | collective-permute-start | bytes 1572872 | tf_op jit(solution)/shard_map/ppermute | solution.py:443
  11.9 17.1 %collective-permute-start = (bf16[4,128,256]{2,1,0:T(8,128)(2,1)S(1)}, bf16[4,128,256]{2,1,0:T(8,128)(2,1)}, u32[]{:S(2)}, u32[]{:S(2)}) collective-permute-start(bf16[4,128,256]{2,1,0:T(8,128)(2,1)S(1)} %copy-done.3), channel_id=1, source_target_pairs={{0,4},{2,6},{4,0},{6,2},{8,12},{10,14},{12,8},{14,10},{1,5},{3,7},... | collective-permute-start | bytes 786440 | tf_op jit(solution)/shard_map/ppermute | solution.py:439
  17.7 16.7 %collective-permute-start.2 = (bf16[4,128,256]{2,1,0:T(8,128)(2,1)}, bf16[4,128,256]{2,1,0:T(8,128)(2,1)}, u32[]{:S(2)}, u32[]{:S(2)}) collective-permute-start(bf16[4,128,256]{2,1,0:T(8,128)(2,1)} %collective-permute-done.1.two_ref), channel_id=1, source_target_pairs={{0,4},{2,6},{4,0},{6,2},{8,12},{10,14},{12,8},{14,10},{1,5},{3,7},... | collective-permute-start | bytes 786440 | tf_op jit(solution)/shard_map/ppermute | solution.py:439
  18.4 20.0 %collective-permute-start.16 = (bf16[128,1024]{1,0:T(8,128)(2,1)}, bf16[128,1024]{1,0:T(8,128)(2,1)}, u32[]{:S(2)}, u32[]{:S(2)}) collective-permute-start(bf16[128,1024]{1,0:T(8,128)(2,1)} %get-tuple-element.33), channel_id=1, source_target_pairs={{0,8},{2,10},{4,12},{6,14},{8,0},{10,2},{12,4},{14,6},{1,9},{3,11}... | collective-permute-start | bytes 786440 | tf_op jit(solution)/shard_map/ppermute | solution.py:439
  22.1 20.5 %copy-start.13 = (bf16[128,1024]{1,0:T(8,128)(2,1)S(1)}, bf16[128,1024]{1,0:T(8,128)(2,1)}, u32[]{:S(2)}) copy-start(bf16[128,1024]{1,0:T(8,128)(2,1)} %copy-done.12) | copy-start | bytes 786436
  22.1 20.8 %copy-start.11 = (bf16[128,1024]{1,0:T(8,128)(2,1)S(1)}, bf16[128,1024]{1,0:T(8,128)(2,1)}, u32[]{:S(2)}) copy-start(bf16[128,1024]{1,0:T(8,128)(2,1)} %copy-done.10) | copy-start | bytes 786436
  22.1 21.1 %copy-start.9 = (bf16[128,1024]{1,0:T(8,128)(2,1)S(1)}, bf16[128,1024]{1,0:T(8,128)(2,1)}, u32[]{:S(2)}) copy-start(bf16[128,1024]{1,0:T(8,128)(2,1)} %copy-done.8) | copy-start | bytes 786436
  22.1 24.9 %copy-start.7 = (bf16[128,1024]{1,0:T(8,128)(2,1)S(1)}, bf16[128,1024]{1,0:T(8,128)(2,1)}, u32[]{:S(2)}) copy-start(bf16[128,1024]{1,0:T(8,128)(2,1)} %copy-done.6) | copy-start | bytes 786436
  22.1 57.0 %copy-start.5 = (bf16[128,1024]{1,0:T(8,128)(2,1)S(1)}, bf16[128,1024]{1,0:T(8,128)(2,1)}, u32[]{:S(2)}) copy-start(bf16[128,1024]{1,0:T(8,128)(2,1)} %copy-done.4) | copy-start | bytes 786436
  22.3 14.4 %collective-permute-start.5 = (f32[16,128]{1,0:T(8,128)S(1)}, f32[16,128]{1,0:T(8,128)S(1)}, u32[]{:S(2)}, u32[]{:S(2)}) collective-permute-start(f32[16,128]{1,0:T(8,128)S(1)} %broadcast_in_dim.10.noise_ref), channel_id=1, source_target_pairs={{0,2},{2,0},{4,6},{6,4},{8,10},{10,8},{12,14},{14,12},{1,3},{3,1},... | collective-permute-start | bytes 24584 | tf_op jit(solution)/shard_map/ppermute | solution.py:443
  36.6 1.2 collective-permute-start.4
  38.4 4.5 %collective-permute-start.6 = (f32[16,128]{1,0:T(8,128)S(1)}, f32[16,128]{1,0:T(8,128)S(1)}, u32[]{:S(2)}, u32[]{:S(2)}) collective-permute-start(f32[16,128]{1,0:T(8,128)S(1)} %get-tuple-element.24.field_here), channel_id=1, source_target_pairs={{0,4},{2,6},{4,0},{6,2},{8,12},{10,14},{12,8},{14,10},{1,5},{3,7},... | collective-permute-start | bytes 24584 | tf_op jit(solution)/shard_map/ppermute | solution.py:439
  38.4 8.7 %collective-permute-start.17 = (bf16[128,1024]{1,0:T(8,128)(2,1)}, bf16[128,1024]{1,0:T(8,128)(2,1)S(1)}, u32[]{:S(2)}, u32[]{:S(2)}) collective-permute-start(bf16[128,1024]{1,0:T(8,128)(2,1)} %collective-permute-done.16), channel_id=1, source_target_pairs={{0,2},{2,0},{4,6},{6,4},{8,10},{10,8},{12,14},{14,12},{1,3},{3,1},... | collective-permute-start | bytes 786440 | tf_op jit(solution)/shard_map/ppermute | solution.py:443
  38.6 8.4 %collective-permute-start.7 = (f32[16,128]{1,0:T(8,128)S(1)}, f32[16,128]{1,0:T(8,128)S(1)}, u32[]{:S(2)}, u32[]{:S(2)}) collective-permute-start(f32[16,128]{1,0:T(8,128)S(1)} %get-tuple-element.24.field_here), channel_id=1, source_target_pairs={{0,8},{2,10},{4,12},{6,14},{8,0},{10,2},{12,4},{14,6},{1,9},{3,11}... | collective-permute-start | bytes 24584 | tf_op jit(solution)/shard_map/ppermute | solution.py:439
  42.6 11.0 %collective-permute-start.22 = (bf16[128,1024]{1,0:T(8,128)(2,1)S(1)}, bf16[128,1024]{1,0:T(8,128)(2,1)S(1)}, u32[]{:S(2)}, u32[]{:S(2)}) collective-permute-start(bf16[128,1024]{1,0:T(8,128)(2,1)S(1)} %copy-done.13), channel_id=1, source_target_pairs={{0,12},{2,14},{4,8},{6,10},{8,4},{10,6},{12,0},{14,2},{1,13},{3,15... | collective-permute-start | bytes 786440 | tf_op jit(solution)/shard_map/ppermute | solution.py:439
  42.9 17.2 %collective-permute-start.11 = (bf16[128,1024]{1,0:T(8,128)(2,1)S(1)}, bf16[128,1024]{1,0:T(8,128)(2,1)S(1)}, u32[]{:S(2)}, u32[]{:S(2)}) collective-permute-start(bf16[128,1024]{1,0:T(8,128)(2,1)S(1)} %copy-done.11), channel_id=1, source_target_pairs={{0,4},{2,6},{4,0},{6,2},{8,12},{10,14},{12,8},{14,10},{1,5},{3,7},... | collective-permute-start | bytes 786440 | tf_op jit(solution)/shard_map/ppermute | solution.py:439
  43.3 28.1 %collective-permute-start.14 = (bf16[128,1024]{1,0:T(8,128)(2,1)S(1)}, bf16[128,1024]{1,0:T(8,128)(2,1)S(1)}, u32[]{:S(2)}, u32[]{:S(2)}) collective-permute-start(bf16[128,1024]{1,0:T(8,128)(2,1)S(1)} %copy-done.9), channel_id=1, source_target_pairs={{0,8},{2,10},{4,12},{6,14},{8,0},{10,2},{12,4},{14,6},{1,9},{3,11}... | collective-permute-start | bytes 786440 | tf_op jit(solution)/shard_map/ppermute | solution.py:439
  47.0 24.9 %collective-permute-start.9 = (bf16[128,1024]{1,0:T(8,128)(2,1)S(1)}, bf16[128,1024]{1,0:T(8,128)(2,1)S(1)}, u32[]{:S(2)}, u32[]{:S(2)}) collective-permute-start(bf16[128,1024]{1,0:T(8,128)(2,1)S(1)} %copy-done.7), channel_id=1, source_target_pairs={{0,4},{2,6},{4,0},{6,2},{8,12},{10,14},{12,8},{14,10},{1,5},{3,7},... | collective-permute-start | bytes 786440 | tf_op jit(solution)/shard_map/ppermute | solution.py:439
  47.1 22.8 %collective-permute-start.19 = (f32[16,128]{1,0:T(8,128)S(1)}, f32[16,128]{1,0:T(8,128)S(1)}, u32[]{:S(2)}, u32[]{:S(2)}) collective-permute-start(f32[16,128]{1,0:T(8,128)S(1)} %get-tuple-element.24.field_here), channel_id=1, source_target_pairs={{0,12},{2,14},{4,8},{6,10},{8,4},{10,6},{12,0},{14,2},{1,13},{3,15... | collective-permute-start | bytes 24584 | tf_op jit(solution)/shard_map/ppermute | solution.py:439
  53.6 20.3 %collective-permute-start.23 = (bf16[128,1024]{1,0:T(8,128)(2,1)S(1)}, bf16[128,1024]{1,0:T(8,128)(2,1)S(1)}, u32[]{:S(2)}, u32[]{:S(2)}) collective-permute-start(bf16[128,1024]{1,0:T(8,128)(2,1)S(1)} %collective-permute-done.22), channel_id=1, source_target_pairs={{0,2},{2,0},{4,6},{6,4},{8,10},{10,8},{12,14},{14,12},{1,3},{3,1},... | collective-permute-start | bytes 786440 | tf_op jit(solution)/shard_map/ppermute | solution.py:443
  60.1 14.4 %collective-permute-start.12 = (bf16[128,1024]{1,0:T(8,128)(2,1)S(1)}, bf16[128,1024]{1,0:T(8,128)(2,1)S(1)}, u32[]{:S(2)}, u32[]{:S(2)}) collective-permute-start(bf16[128,1024]{1,0:T(8,128)(2,1)S(1)} %collective-permute-done.11), channel_id=1, source_target_pairs={{0,2},{2,0},{4,6},{6,4},{8,10},{10,8},{12,14},{14,12},{1,3},{3,1},... | collective-permute-start | bytes 786440 | tf_op jit(solution)/shard_map/ppermute | solution.py:443
  69.9 9.2 %collective-permute-start.18 = (bf16[128,1024]{1,0:T(8,128)(2,1)S(1)}, bf16[128,1024]{1,0:T(8,128)(2,1)S(1)}, u32[]{:S(2)}, u32[]{:S(2)}) collective-permute-start(bf16[128,1024]{1,0:T(8,128)(2,1)S(1)} %collective-permute-done.17.refs_6_), channel_id=1, source_target_pairs={{0,1},{1,0},{2,3},{3,2},{4,5},{5,4},{6,7},{7,6},{8,9},{9,8},{10,11... | collective-permute-start | bytes 786440 | tf_op jit(solution)/shard_map/ppermute | solution.py:447
  71.4 13.4 %collective-permute-start.15 = (bf16[128,1024]{1,0:T(8,128)(2,1)S(1)}, bf16[128,1024]{1,0:T(8,128)(2,1)S(1)}, u32[]{:S(2)}, u32[]{:S(2)}) collective-permute-start(bf16[128,1024]{1,0:T(8,128)(2,1)S(1)} %collective-permute-done.14.refs_4_), channel_id=1, source_target_pairs={{0,1},{1,0},{2,3},{3,2},{4,5},{5,4},{6,7},{7,6},{8,9},{9,8},{10,11... | collective-permute-start | bytes 786440 | tf_op jit(solution)/shard_map/ppermute | solution.py:447
  71.9 18.4 %collective-permute-start.10 = (bf16[128,1024]{1,0:T(8,128)(2,1)S(1)}, bf16[128,1024]{1,0:T(8,128)(2,1)S(1)}, u32[]{:S(2)}, u32[]{:S(2)}) collective-permute-start(bf16[128,1024]{1,0:T(8,128)(2,1)S(1)} %collective-permute-done.9.refs_0_), channel_id=1, source_target_pairs={{0,1},{1,0},{2,3},{3,2},{4,5},{5,4},{6,7},{7,6},{8,9},{9,8},{10,11... | collective-permute-start | bytes 786440 | tf_op jit(solution)/shard_map/ppermute | solution.py:447
  73.9 22.0 %collective-permute-start.24 = (bf16[128,1024]{1,0:T(8,128)(2,1)S(1)}, bf16[128,1024]{1,0:T(8,128)(2,1)S(1)}, u32[]{:S(2)}, u32[]{:S(2)}) collective-permute-start(bf16[128,1024]{1,0:T(8,128)(2,1)S(1)} %collective-permute-done.23.refs_2_), channel_id=1, source_target_pairs={{0,1},{1,0},{2,3},{3,2},{4,5},{5,4},{6,7},{7,6},{8,9},{9,8},{10,11... | collective-permute-start | bytes 786440 | tf_op jit(solution)/shard_map/ppermute | solution.py:447
  74.6 25.5 %collective-permute-start.13 = (bf16[128,1024]{1,0:T(8,128)(2,1)S(1)}, bf16[128,1024]{1,0:T(8,128)(2,1)S(1)}, u32[]{:S(2)}, u32[]{:S(2)}) collective-permute-start(bf16[128,1024]{1,0:T(8,128)(2,1)S(1)} %collective-permute-done.12.refs_2_), channel_id=1, source_target_pairs={{0,1},{1,0},{2,3},{3,2},{4,5},{5,4},{6,7},{7,6},{8,9},{9,8},{10,11... | collective-permute-start | bytes 786440 | tf_op jit(solution)/shard_map/ppermute | solution.py:447
  79.1 16.9 %collective-permute-start.20 = (bf16[128,1024]{1,0:T(8,128)(2,1)S(1)}, bf16[128,1024]{1,0:T(8,128)(2,1)S(1)}, u32[]{:S(2)}, u32[]{:S(2)}) collective-permute-start(bf16[128,1024]{1,0:T(8,128)(2,1)S(1)} %copy-done.5), channel_id=1, source_target_pairs={{0,12},{2,14},{4,8},{6,10},{8,4},{10,6},{12,0},{14,2},{1,13},{3,15... | collective-permute-start | bytes 786440 | tf_op jit(solution)/shard_map/ppermute | solution.py:439
  84.8 15.3 %collective-permute-start.26 = (bf16[4,128,256]{2,1,0:T(8,128)(2,1)S(1)}, bf16[4,128,256]{2,1,0:T(8,128)(2,1)S(1)}, u32[]{:S(2)}, u32[]{:S(2)}) collective-permute-start(bf16[4,128,256]{2,1,0:T(8,128)(2,1)S(1)} %walker_major.1.refs_0_), channel_id=1, source_target_pairs={{0,8},{2,10},{4,12},{6,14},{8,0},{10,2},{12,4},{14,6},{1,9},{3,11}... | collective-permute-start | bytes 786440 | tf_op jit(solution)/shard_map/ppermute | solution.py:439
  90.4 10.5 %collective-permute-start.25 = (bf16[4,128,256]{2,1,0:T(8,128)(2,1)S(1)}, bf16[4,128,256]{2,1,0:T(8,128)(2,1)S(1)}, u32[]{:S(2)}, u32[]{:S(2)}) collective-permute-start(bf16[4,128,256]{2,1,0:T(8,128)(2,1)S(1)} %walker_major.1.refs_0_), channel_id=1, source_target_pairs={{0,4},{2,6},{4,0},{6,2},{8,12},{10,14},{12,8},{14,10},{1,5},{3,7},... | collective-permute-start | bytes 786440 | tf_op jit(solution)/shard_map/ppermute | solution.py:439
  96.0 11.4 %collective-permute-start.27 = (bf16[4,128,256]{2,1,0:T(8,128)(2,1)S(1)}, bf16[4,128,256]{2,1,0:T(8,128)(2,1)S(1)}, u32[]{:S(2)}, u32[]{:S(2)}) collective-permute-start(bf16[4,128,256]{2,1,0:T(8,128)(2,1)S(1)} %walker_major.1.refs_0_), channel_id=1, source_target_pairs={{0,2},{2,0},{4,6},{6,4},{8,10},{10,8},{12,14},{14,12},{1,3},{3,1},... | collective-permute-start | bytes 786440 | tf_op jit(solution)/shard_map/ppermute | solution.py:443
  96.0 9.8 %collective-permute-start.21 = (bf16[128,1024]{1,0:T(8,128)(2,1)S(1)}, bf16[128,1024]{1,0:T(8,128)(2,1)S(1)}, u32[]{:S(2)}, u32[]{:S(2)}) collective-permute-start(bf16[128,1024]{1,0:T(8,128)(2,1)S(1)} %collective-permute-done.20.refs_0_), channel_id=1, source_target_pairs={{0,1},{1,0},{2,3},{3,2},{4,5},{5,4},{6,7},{7,6},{8,9},{9,8},{10,11... | collective-permute-start | bytes 786440 | tf_op jit(solution)/shard_map/ppermute | solution.py:447
  100.9 6.5 %collective-permute-start.28 = (bf16[4,128,256]{2,1,0:T(8,128)(2,1)S(1)}, bf16[4,128,256]{2,1,0:T(8,128)(2,1)S(1)}, u32[]{:S(2)}, u32[]{:S(2)}) collective-permute-start(bf16[4,128,256]{2,1,0:T(8,128)(2,1)S(1)} %collective-permute-done.25.refs_1_), channel_id=1, source_target_pairs={{0,2},{2,0},{4,6},{6,4},{8,10},{10,8},{12,14},{14,12},{1,3},{3,1},... | collective-permute-start | bytes 786440 | tf_op jit(solution)/shard_map/ppermute | solution.py:443
  100.9 6.5 %collective-permute-start.29 = (bf16[4,128,256]{2,1,0:T(8,128)(2,1)S(1)}, bf16[4,128,256]{2,1,0:T(8,128)(2,1)S(1)}, u32[]{:S(2)}, u32[]{:S(2)}) collective-permute-start(bf16[4,128,256]{2,1,0:T(8,128)(2,1)S(1)} %collective-permute-done.26.refs_2_), channel_id=1, source_target_pairs={{0,2},{2,0},{4,6},{6,4},{8,10},{10,8},{12,14},{14,12},{1,3},{3,1},... | collective-permute-start | bytes 786440 | tf_op jit(solution)/shard_map/ppermute | solution.py:443
  101.4 8.2 %collective-permute-start.30 = (bf16[4,128,256]{2,1,0:T(8,128)(2,1)S(1)}, bf16[4,128,256]{2,1,0:T(8,128)(2,1)S(1)}, u32[]{:S(2)}, u32[]{:S(2)}) collective-permute-start(bf16[4,128,256]{2,1,0:T(8,128)(2,1)S(1)} %collective-permute-done.26.refs_2_), channel_id=1, source_target_pairs={{0,4},{2,6},{4,0},{6,2},{8,12},{10,14},{12,8},{14,10},{1,5},{3,7},... | collective-permute-start | bytes 786440 | tf_op jit(solution)/shard_map/ppermute | solution.py:439
  109.6 1.5 %collective-permute-start.31 = (bf16[4,128,256]{2,1,0:T(8,128)(2,1)S(1)}, bf16[4,128,256]{2,1,0:T(8,128)(2,1)S(1)}, u32[]{:S(2)}, u32[]{:S(2)}) collective-permute-start(bf16[4,128,256]{2,1,0:T(8,128)(2,1)S(1)} %collective-permute-done.30.mine), channel_id=1, source_target_pairs={{0,2},{2,0},{4,6},{6,4},{8,10},{10,8},{12,14},{14,12},{1,3},{3,1},... | collective-permute-start | bytes 786440 | tf_op jit(solution)/shard_map/ppermute | solution.py:443
  111.5 12.6 %collective-permute-start.32 = (bf16[4,128,256]{2,1,0:T(8,128)(2,1)S(1)}, bf16[4,128,256]{2,1,0:T(8,128)(2,1)S(1)}, u32[]{:S(2)}, u32[]{:S(2)}) collective-permute-start(bf16[4,128,256]{2,1,0:T(8,128)(2,1)S(1)} %get-tuple-element.43.refs_0_), channel_id=1, source_target_pairs={{0,4},{2,6},{4,0},{6,2},{8,12},{10,14},{12,8},{14,10},{1,5},{3,7},... | collective-permute-start | bytes 786440 | tf_op jit(solution)/shard_map/ppermute | solution.py:439
  112.2 14.6 %collective-permute-start.33 = (bf16[4,128,256]{2,1,0:T(8,128)(2,1)S(1)}, bf16[4,128,256]{2,1,0:T(8,128)(2,1)S(1)}, u32[]{:S(2)}, u32[]{:S(2)}) collective-permute-start(bf16[4,128,256]{2,1,0:T(8,128)(2,1)S(1)} %get-tuple-element.43.refs_0_), channel_id=1, source_target_pairs={{0,8},{2,10},{4,12},{6,14},{8,0},{10,2},{12,4},{14,6},{1,9},{3,11}... | collective-permute-start | bytes 786440 | tf_op jit(solution)/shard_map/ppermute | solution.py:439
  113.4 13.5 %collective-permute-start.34 = (bf16[4,128,256]{2,1,0:T(8,128)(2,1)S(1)}, bf16[4,128,256]{2,1,0:T(8,128)(2,1)S(1)}, u32[]{:S(2)}, u32[]{:S(2)}) collective-permute-start(bf16[4,128,256]{2,1,0:T(8,128)(2,1)S(1)} %get-tuple-element.43.refs_0_), channel_id=1, source_target_pairs={{0,2},{2,0},{4,6},{6,4},{8,10},{10,8},{12,14},{14,12},{1,3},{3,1},... | collective-permute-start | bytes 786440 | tf_op jit(solution)/shard_map/ppermute | solution.py:443
  124.2 2.7 %collective-permute-start.35 = (bf16[4,128,256]{2,1,0:T(8,128)(2,1)S(1)}, bf16[4,128,256]{2,1,0:T(8,128)(2,1)S(1)}, u32[]{:S(2)}, u32[]{:S(2)}) collective-permute-start(bf16[4,128,256]{2,1,0:T(8,128)(2,1)S(1)} %collective-permute-done.32.refs_1_), channel_id=1, source_target_pairs={{0,2},{2,0},{4,6},{6,4},{8,10},{10,8},{12,14},{14,12},{1,3},{3,1},... | collective-permute-start | bytes 786440 | tf_op jit(solution)/shard_map/ppermute | solution.py:443
  126.9 1.5 %collective-permute-start.36 = (bf16[4,128,256]{2,1,0:T(8,128)(2,1)S(1)}, bf16[4,128,256]{2,1,0:T(8,128)(2,1)S(1)}, u32[]{:S(2)}, u32[]{:S(2)}) collective-permute-start(bf16[4,128,256]{2,1,0:T(8,128)(2,1)S(1)} %collective-permute-done.33.refs_2_), channel_id=1, source_target_pairs={{0,2},{2,0},{4,6},{6,4},{8,10},{10,8},{12,14},{14,12},{1,3},{3,1},... | collective-permute-start | bytes 786440 | tf_op jit(solution)/shard_map/ppermute | solution.py:443
  126.9 8.7 %collective-permute-start.37 = (bf16[4,128,256]{2,1,0:T(8,128)(2,1)S(1)}, bf16[4,128,256]{2,1,0:T(8,128)(2,1)S(1)}, u32[]{:S(2)}, u32[]{:S(2)}) collective-permute-start(bf16[4,128,256]{2,1,0:T(8,128)(2,1)S(1)} %collective-permute-done.33.refs_2_), channel_id=1, source_target_pairs={{0,4},{2,6},{4,0},{6,2},{8,12},{10,14},{12,8},{14,10},{1,5},{3,7},... | collective-permute-start | bytes 786440 | tf_op jit(solution)/shard_map/ppermute | solution.py:439
  135.6 1.5 %collective-permute-start.38 = (bf16[4,128,256]{2,1,0:T(8,128)(2,1)S(1)}, bf16[4,128,256]{2,1,0:T(8,128)(2,1)S(1)}, u32[]{:S(2)}, u32[]{:S(2)}) collective-permute-start(bf16[4,128,256]{2,1,0:T(8,128)(2,1)S(1)} %collective-permute-done.37.mine), channel_id=1, source_target_pairs={{0,2},{2,0},{4,6},{6,4},{8,10},{10,8},{12,14},{14,12},{1,3},{3,1},... | collective-permute-start | bytes 786440 | tf_op jit(solution)/shard_map/ppermute | solution.py:443
  (7 other events, 10.6 us)

commit v8 on v7

--- a/solution.py
+++ b/solution.py
@@ -65,7 +65,6 @@
 narrow = jnp.bfloat16
 small = pltpu.CompilerParams(vmem_limit_bytes=8 << 20)
 large = pltpu.CompilerParams(vmem_limit_bytes=16 << 20)
-brief = pl.CostEstimate(flops=0, bytes_accessed=0, transcendentals=0)
 
 
 def after(value, *others):
@@ -81,37 +80,46 @@
     return lax.bitwise_xor(z, jnp.int32(step))
 
 
-def cut_kernel(rows, wanted, full_ref, *refs):
+def pack_kernel(full_ref, green_ref, one_ref, two_ref, three_ref, own_ref, cross_ref, sem):
     z, k, x = place()
-    outs, sem = refs[:-1], refs[-1]
+    walkers, rows, occupied = green_ref.shape
     copies = []
-    for index, (step, crossed, both) in enumerate(wanted):
-        core = 1 - k if crossed else k
-        start = pl.multiple_of((2 * flipped(z, step) + core) * rows, rows)
-        picked = pl.ds(start, rows)
-        source = full_ref.at[:, picked, :] if both else full_ref.at[x, picked, :]
-        copies.append(pltpu.make_async_copy(source, outs[index], sem.at[index]))
+
+    def copy(source, target):
+        copies.append(pltpu.make_async_copy(source, target, sem.at[len(copies)]))
         copies[-1].start()
-    for copy in copies:
-        copy.wait()
-
-
-def cut(rows, full_chol, wanted):
+
+    def of_chip(step, core):
+        return pl.ds(pl.multiple_of((2 * flipped(z, step) + core) * rows, rows), rows)
+
+    for step, message, top in ((2, two_ref, rows), (1, one_ref, rows), (3, three_ref, 0)):
+        for index, core in enumerate((1 - k, k)):
+            copy(
+                full_ref.at[x, of_chip(step, core), :],
+                message.at[pl.ds(top + index * rows, rows), :],
+            )
+    copy(full_ref.at[:, of_chip(0, k), :], own_ref)
+    copy(full_ref.at[:, of_chip(0, 1 - k), :], cross_ref)
+    for each in copies:
+        each.wait()
+    for message in (two_ref, one_ref):
+        for w in range(walkers):
+            message[:rows, w * occupied : (w + 1) * occupied] = green_ref[w]
+
+
+def packed(full_chol, green_blocks):
     order = full_chol.shape[2]
-    shapes = [
-        jax.ShapeDtypeStruct((2, rows, order) if both else (rows, order), narrow)
-        for _, _, both in wanted
-    ]
-    return pl.pallas_call(
-        functools.partial(cut_kernel, rows, wanted),
-        out_shape=shapes,
-        in_specs=[hbm_spec],
-        out_specs=[vmem_spec] * len(wanted),
-        scratch_shapes=[pltpu.SemaphoreType.DMA((len(wanted),))],
-        compiler_params=small,
-        cost_estimate=brief,
-        name="cut_rows",
-    )(full_chol)
+    rows = green_blocks.shape[1]
+    shapes = [(3 * rows, order), (3 * rows, order), (2 * rows, order)] + [(2, rows, order)] * 2
+    return pl.pallas_call(
+        pack_kernel,
+        out_shape=[jax.ShapeDtypeStruct(shape, narrow) for shape in shapes],
+        in_specs=[hbm_spec, vmem_spec],
+        out_specs=[vmem_spec] * 5,
+        scratch_shapes=[pltpu.SemaphoreType.DMA((8,))],
+        compiler_params=small,
+        name="packed",
+    )(full_chol, green_blocks)
 
 
 def start_kernel(orbitals_ref, out_ref):
@@ -127,7 +135,6 @@
         in_specs=[vmem_spec],
         out_specs=vmem_spec,
         compiler_params=small,
-        cost_estimate=brief,
         name="walker_major",
     )(orbitals)
 
@@ -141,11 +148,14 @@
     for step, green in enumerate((here_ref, one_ref, two_ref, three_ref)):
         base = (2 * flipped(z, step) + k) * rows
 
-        def add(index, totals, base=base, green=green):
+        def add(index, totals, step=step, base=base, green=green):
             here = pl.multiple_of(index * step_rows, step_rows)
             there = pl.multiple_of(base + index * step_rows, step_rows)
             picked = pl.ds(here, step_rows)
-            greens = [green[w, picked, :] for w in range(walkers)]
+            if step == 0:
+                greens = [green[w, picked, :] for w in range(walkers)]
+            else:
+                greens = [green[picked, w * occupied : (w + 1) * occupied] for w in range(walkers)]
             greens = [g.astype(wide) for g in greens]
             totals = list(totals)
             for c in range(2 * vectors):
@@ -175,7 +185,6 @@
         in_specs=[vmem_spec] * 6,
         out_specs=vmem_spec,
         compiler_params=small,
-        cost_estimate=brief,
         name="chip_bias",
     )(*green, mine, theirs)
 
@@ -197,18 +206,17 @@
                 shift_ref[vector : vector + 1, :] = picked[:, :walkers]
 
 
-def chip_field(mine, theirs, noise, noise_there, walkers):
+def chip_field(mine, theirs, noise, noise_there, vectors):
     entries = mine.shape[0]
     return pl.pallas_call(
         field_kernel,
         out_shape=[
-            jax.ShapeDtypeStruct((entries // 2 // walkers, walkers), wide),
+            jax.ShapeDtypeStruct((vectors, entries // 2 // vectors), wide),
             jax.ShapeDtypeStruct((entries, 128), wide),
         ],
         in_specs=[vmem_spec] * 4,
         out_specs=[vmem_spec] * 2,
         compiler_params=small,
-        cost_estimate=brief,
         name="chip_field",
     )(mine, theirs, noise, noise_there)
 
@@ -247,14 +255,15 @@
     return lambda picked: ref[(index, *picked)]
 
 
-def of_one(ref):
-    return lambda picked: ref[picked]
-
-
-def both_cores(field_ref, mine, mine_x, theirs, theirs_x):
+def below(ref, top):
+    return lambda picked: ref[pl.ds(top + picked[0].start, picked[0].size), picked[1]]
+
+
+def both_cores(field_ref, rows, mine, mine_x, theirs, theirs_x):
+    top = mine.shape[0] - 2 * rows
     return [
-        (field_ref, 0, of_one(mine), of_one(mine_x)),
-        (field_ref, 1, of_one(theirs), of_one(theirs_x)),
+        (field_ref, 0, below(mine, top + rows), below(mine_x, rows)),
+        (field_ref, 1, below(theirs, top), below(theirs_x, 0)),
     ]
 
 
@@ -265,7 +274,9 @@
         (field_here, 0, of_pair(own, x), of_pair(own, 1 - x)),
         (field_here, 1, of_pair(own_theirs, x), of_pair(own_theirs, 1 - x)),
     ]
-    sources += both_cores(field_one, *blocks[:4]) + both_cores(field_two, *blocks[4:])
+    rows = own.shape[1]
+    sources += both_cores(field_one, rows, *blocks[:4])
+    sources += both_cores(field_two, rows, *blocks[4:])
 
     def body(picked):
         tiles = block_operators(x, walkers, sources, picked)
@@ -277,14 +288,13 @@
 
 
 def early_operator(walkers, fields, own, own_theirs, blocks):
-    rows, order = blocks[0].shape
+    _, rows, order = own.shape
     return pl.pallas_call(
         functools.partial(early_kernel, walkers),
         out_shape=jax.ShapeDtypeStruct((walkers, rows, order), wide),
         in_specs=[vmem_spec] * (5 + len(blocks)),
         out_specs=vmem_spec,
         compiler_params=large,
-        cost_estimate=brief,
         name="early_operator",
     )(*fields, own, own_theirs, *blocks)
 
@@ -293,7 +303,7 @@
     blocks, operator_ref = refs[:-1], refs[-1]
     walkers, rows, order = summed_ref.shape
     _, _, x = place()
-    sources = both_cores(field_ref, *blocks)
+    sources = both_cores(field_ref, rows, *blocks)
 
     def body(picked):
         tiles = block_operators(x, walkers, sources, picked)
@@ -318,7 +328,6 @@
         in_specs=[vmem_spec] * (2 + len(blocks)),
         out_specs=vmem_spec,
         compiler_params=large,
-        cost_estimate=brief,
         name="split_operator",
     )(summed, field, *blocks)
 
@@ -360,7 +369,6 @@
         out_specs=vmem_spec,
         scratch_shapes=[pltpu.VMEM((3, walkers, 2 * rows, occupied), narrow)],
         compiler_params=small,
-        cost_estimate=brief,
         name="near_application",
     )(operator, *pieces)
 
@@ -385,7 +393,6 @@
         out_specs=[vmem_spec] * 2,
         scratch_shapes=[pltpu.VMEM((walkers, 2 * rows, occupied), narrow)],
         compiler_params=small,
-        cost_estimate=brief,
         name="first_application",
     )(operator, partial, mine, theirs)
 
@@ -410,7 +417,6 @@
         out_specs=vmem_spec,
         scratch_shapes=[pltpu.VMEM((3, walkers, 2 * rows, occupied), narrow)],
         compiler_params=small,
-        cost_estimate=brief,
         name="base_application",
     )(operator, first_term, orbitals, *pieces)
 
@@ -430,7 +436,6 @@
         out_specs=vmem_spec,
         scratch_shapes=[pltpu.VMEM((walkers, 2 * rows, occupied), narrow)],
         compiler_params=small,
-        cost_estimate=brief,
         name="second_application",
     )(operator, base, mine, theirs)
 
@@ -451,46 +456,29 @@
     walkers, rows, _ = green_blocks.shape
     vectors = half_chol.shape[0]
 
-    green_two, green_one = to_chip(green_blocks, 2), to_chip(green_blocks, 1)
     half_theirs = to_core(half_chol)
     constants = jnp.concatenate([noise_draws.T.reshape(-1), jnp.repeat(meanfield, walkers)])
     constants = jnp.broadcast_to(constants[:, None], (2 * vectors * walkers, 128))
     constants_theirs = to_core(constants)
-
-    green_three = to_chip(green_two, 1)
-
-    cross, straight = {}, {}
-    wanted = [(step, crossed, False) for step in (2, 3, 1) for crossed in (True, False)]
-    wanted += [(0, False, True), (0, True, True)]
-    pieces = cut(rows, after(full_chol, half_theirs), wanted)
-    for index, step in enumerate((2, 3, 1)):
-        cross[step], straight[step] = pieces[2 * index : 2 * index + 2]
-    own, own_cross = pieces[6:]
+    one, two, three, own, own_cross = packed(full_chol, green_blocks)
+    two, one = to_chip(two, 2), to_chip(one, 1)
     own_theirs = to_core(own_cross)
-
-    green = (green_blocks, green_one, green_two, green_three)
-    bias = chip_bias(green, half_chol, half_theirs)
-    bias_shift, field = chip_field(bias, to_core(bias), constants, constants_theirs, walkers)
+    three = to_chip(after(three, one, half_theirs, own_theirs, constants_theirs), 3)
+    green_three = to_chip(two[:rows], 1)
+
+    one_x = across(one[rows:])
+    two_x = across(after(two[rows:], one_x))
+    three_x = across(after(three, two_x))
+    messages = {1: (one, one_x), 2: (two, two_x), 3: (three, three_x)}
+    blocks = {step: [*both, *[to_core(each) for each in both]] for step, both in messages.items()}
+
+    bias = chip_bias((green_blocks, one, two, green_three), half_chol, half_theirs)
+    bias_shift, field = chip_field(bias, to_core(bias), constants, constants_theirs, vectors)
     field_one, field_two, field_three = (to_chip(field, step) for step in (1, 2, 3))
 
-    cross_mine, mine, theirs, mine_x, theirs_x = {}, {}, {}, {}, {}
-    cross_mine[2], mine[2] = to_chip(cross[2], 2), to_chip(straight[2], 2)
-    cross_mine[3] = to_chip(cross[3], 3)
-    theirs[2] = to_core(after(cross_mine[2], field, own_theirs))
-    mine[3] = to_chip(after(straight[3], theirs[2]), 3)
-    cross[1], straight[1] = after((cross[1], straight[1]), field_one)
-    cross_mine[1], mine[1] = to_chip(cross[1], 1), to_chip(straight[1], 1)
-    theirs_x[2] = across(after(theirs[2], field_one))
-    mine_x[2] = across(mine[2])
-    for step in (3, 1):
-        theirs[step] = to_core(cross_mine[step])
-        theirs_x[step], mine_x[step] = across(theirs[step]), across(mine[step])
-    blocks = {step: (mine[step], mine_x[step], theirs[step], theirs_x[step]) for step in mine}
-
-    start = after(walker_major(orbitals), theirs_x[2], theirs[3], field_two, field_three)
+    start = after(walker_major(orbitals), two)
     start_two, start_one = to_chip(start, 2), to_chip(start, 1)
-    hops = (mine_x[2], theirs_x[3], mine_x[1], theirs_x[1], mine[3])
-    start_three = to_chip(after(start_two, *hops), 1)
+    start_three = to_chip(start_two, 1)
 
     summed = early_operator(
         walkers,

time: 139 us -> 134 us (0.964)
  waiting for transfers between devices: 87.4 us -> 84 us
    ppermute x6 -> x3, waiting for transfers between devices: 22 us -> 7.68 us  [across(): return lax.ppermute(value, 'walk', [(0, 1), (1, 0)])]
    ppermute x18 -> x13, waiting for transfers between devices: 59.7 us -> 69.1 us  [to_chip(): return lax.ppermute(value, 'chol', [(i, i ^ 2 * step) for i in range(8)])]
    ppermute x6 -> x3, starting transfers between devices: 7.1 us -> 3.43 us  [across(): return lax.ppermute(value, 'walk', [(0, 1), (1, 0)])]
    ppermute x18 -> x13, starting transfers between devices: 22 us -> 24.4 us  [to_chip(): return lax.ppermute(value, 'chol', [(i, i ^ 2 * step) for i in range(8)])]
    ppermute x15 -> x18, waiting for transfers between devices: 5.72 us -> 7.2 us  [to_core(): return lax.ppermute(value, 'chol', [(i, i ^ 1) for i in range(8)])]
    unnamed x32 -> x20, local copies, waits for them, and re-layouts: 5.71 us -> 4.77 us
  transfers between devices with their start and end apart: 39 -> 34, of which waited for: 20 -> 17; matrix products, arithmetic and copies ran while one was open for 0% -> 1% of each run, Pallas kernels for 9% -> 8%
where the time goes in v8:
time: 134 us
  waiting for transfers between devices  84 us (63%)
  starting transfers between devices  29.4 us (22%)
  Pallas kernels  13.9 us (10%)
  local copies, waits for them, and re-layouts  5.99 us (4%)
    ppermute x13, waiting for transfers between devices, to_chip(): return lax.ppermute(value, 'chol', [(i, i ^ 2 * step) for i in range(8)])  69.1 us
    ppermute x13, starting transfers between devices, to_chip(): return lax.ppermute(value, 'chol', [(i, i ^ 2 * step) for i in range(8)])  24.4 us
    ppermute x3, waiting for transfers between devices, across(): return lax.ppermute(value, 'walk', [(0, 1), (1, 0)])  7.68 us
    ppermute x18, waiting for transfers between devices, to_core(): return lax.ppermute(value, 'chol', [(i, i ^ 1) for i in range(8)])  7.2 us
    unnamed x20, local copies, waits for them, and re-layouts  4.77 us
    pallas_call x1, Pallas kernels, early_operator(): pl.pallas_call(functools.partial(early_kernel, walkers), out_shape=jax.Sh...  4.54 us
    ppermute x3, starting transfers between devices, across(): return lax.ppermute(value, 'walk', [(0, 1), (1, 0)])  3.43 us
  transfers between devices with their start and end apart: 34, of which 17 were waited for; matrix products, arithmetic and copies ran while one was open for 1% of the time, Pallas kernels for 8%

profile of v8, /device:TPU:0, one launch (start us, length us, event | category | flops | bytes accessed | tf_op | source)
XLA Modules:
  0.0 134.1 jit_solution(14293789537223466706)
XLA Ops:
  0.6 2.2 %copy-done = bf16[2,1024,1024]{2,1,0:T(8,128)(2,1)S(1)} copy-done((bf16[2,1024,1024]{2,1,0:T(8,128)(2,1)S(1)}, bf16[2,1024,1024]{2,1,0:T(8,128)(2,1)}, u32[]{:S(2)}) %copy-start) | copy-done | bytes 4194328
  2.8 0.9 copy-done.2
  3.8 1.3 packed.1
  5.1 0.8 copy-done.5
  5.9 0.8 copy-done.7
  6.8 3.0 %collective-permute-start = (bf16[384,1024]{1,0:T(8,128)(2,1)S(1)}, bf16[384,1024]{1,0:T(8,128)(2,1)S(1)}, u32[]{:S(2)}, u32[]{:S(2)}) collective-permute-start(bf16[384,1024]{1,0:T(8,128)(2,1)S(1)} %get-tuple-element.17), channel_id=1, source_target_pairs={{0,4},{2,6},{4,0},{6,2},{8,12},{10,14},{12,8},{14,10},{1,5},{3,7},... | collective-permute-start | bytes 2359304 | tf_op jit(solution)/shard_map/ppermute | solution.py:444
  9.8 2.6 %collective-permute-start.1 = (bf16[384,1024]{1,0:T(8,128)(2,1)}, bf16[384,1024]{1,0:T(8,128)(2,1)S(1)}, u32[]{:S(2)}, u32[]{:S(2)}) collective-permute-start(bf16[384,1024]{1,0:T(8,128)(2,1)} %get-tuple-element.18), channel_id=1, source_target_pairs={{0,8},{2,10},{4,12},{6,14},{8,0},{10,2},{12,4},{14,6},{1,9},{3,11}... | collective-permute-start | bytes 2359304 | tf_op jit(solution)/shard_map/ppermute | solution.py:444
  12.4 0.2 collective-permute-start.8
  12.6 30.3 %collective-permute-done.one_ref.refs_0_ = bf16[384,1024]{1,0:T(8,128)(2,1)S(1)} collective-permute-done((bf16[384,1024]{1,0:T(8,128)(2,1)S(1)}, bf16[384,1024]{1,0:T(8,128)(2,1)S(1)}, u32[]{:S(2)}, u32[]{:S(2)}) %collective-permute-start) | collective-permute-done | bytes 786464 | tf_op jit(solution)/shard_map/ppermute | solution.py:444
  42.9 0.9 slice.13
  43.7 1.7 %collective-permute-start.9 = (bf16[256,1024]{1,0:T(8,128)(2,1)}, bf16[256,1024]{1,0:T(8,128)(2,1)}, u32[]{:S(2)}, u32[]{:S(2)}) collective-permute-start(bf16[256,1024]{1,0:T(8,128)(2,1)} %slice.13), channel_id=1, source_target_pairs={{0,1},{1,0},{2,3},{3,2},{4,5},{5,4},{6,7},{7,6},{8,9},{9,8},{10,11... | collective-permute-start | bytes 1572872 | tf_op jit(solution)/shard_map/ppermute | solution.py:452
  45.8 1.2 collective-permute-done.5.noise_there_ref
  47.0 2.5 %collective-permute-start.16 = (bf16[256,1024]{1,0:T(8,128)(2,1)}, bf16[256,1024]{1,0:T(8,128)(2,1)S(1)}, u32[]{:S(2)}, u32[]{:S(2)}) collective-permute-start(bf16[256,1024]{1,0:T(8,128)(2,1)} %copy-done.7), channel_id=1, source_target_pairs={{0,12},{2,14},{4,8},{6,10},{8,4},{10,6},{12,0},{14,2},{1,13},{3,15... | collective-permute-start | bytes 1572872 | tf_op jit(solution)/shard_map/ppermute | solution.py:444
  49.5 7.7 %collective-permute-done.9.refs_1_ = bf16[256,1024]{1,0:T(8,128)(2,1)} collective-permute-done((bf16[256,1024]{1,0:T(8,128)(2,1)}, bf16[256,1024]{1,0:T(8,128)(2,1)}, u32[]{:S(2)}, u32[]{:S(2)}) %collective-permute-start.9) | collective-permute-done | bytes 524320 | tf_op jit(solution)/shard_map/ppermute | solution.py:452
  57.2 1.3 collective-permute-start.12
  58.6 0.5 walker_major.1.refs_0_
  59.2 3.1 %collective-permute-start.21 = (bf16[4,128,256]{2,1,0:T(8,128)(2,1)S(1)}, bf16[4,128,256]{2,1,0:T(8,128)(2,1)S(1)}, u32[]{:S(2)}, u32[]{:S(2)}) collective-permute-start(bf16[4,128,256]{2,1,0:T(8,128)(2,1)S(1)} %walker_major.1.refs_0_), channel_id=1, source_target_pairs={{0,8},{2,10},{4,12},{6,14},{8,0},{10,2},{12,4},{14,6},{1,9},{3,11}... | collective-permute-start | bytes 786440 | tf_op jit(solution)/shard_map/ppermute | solution.py:444
  62.2 6.5 %collective-permute-done.2.three_ref = bf16[128,1024]{1,0:T(8,128)(2,1)S(1)} collective-permute-done((bf16[128,1024]{1,0:T(8,128)(2,1)S(1)}, bf16[128,1024]{1,0:T(8,128)(2,1)S(1)}, u32[]{:S(2)}, u32[]{:S(2)}) %collective-permute-start.2) | collective-permute-done | bytes 262176 | tf_op jit(solution)/shard_map/ppermute | solution.py:444
  68.7 2.2 %chip_bias.1.mine_ref = f32[16,128]{1,0:T(8,128)S(1)} custom-call(bf16[4,128,256]{2,1,0:T(8,128)(2,1)S(1)} %copy-done.3, bf16[384,1024]{1,0:T(8,128)(2,1)S(1)} %collective-permute-done.one_ref.refs_0_, bf16[384,1024]{1,0:T(8,128)(2,1)S(1)} %collective-permute-done.1.two_ref.refs_4_, bf16[128,1024]{1,0:T(8,128)(2,1)S(1)} %collective-permute-done.2.three_ref, ...), custom_call_target="tpu_custom_call" | custom-call | tf_op jit(solution)/shard_map/chip_bias/pallas_call | solution.py:182
  71.1 7.3 %collective-permute-start.20 = (bf16[4,128,256]{2,1,0:T(8,128)(2,1)S(1)}, bf16[4,128,256]{2,1,0:T(8,128)(2,1)S(1)}, u32[]{:S(2)}, u32[]{:S(2)}) collective-permute-start(bf16[4,128,256]{2,1,0:T(8,128)(2,1)S(1)} %walker_major.1.refs_0_), channel_id=1, source_target_pairs={{0,4},{2,6},{4,0},{6,2},{8,12},{10,14},{12,8},{14,10},{1,5},{3,7},... | collective-permute-start | bytes 786440 | tf_op jit(solution)/shard_map/ppermute | solution.py:444
  78.4 0.4 collective-permute-start.17
  78.8 0.6 chip_field.1
  79.4 3.4 %collective-permute-done.21.refs_2_ = bf16[4,128,256]{2,1,0:T(8,128)(2,1)S(1)} collective-permute-done((bf16[4,128,256]{2,1,0:T(8,128)(2,1)S(1)}, bf16[4,128,256]{2,1,0:T(8,128)(2,1)S(1)}, u32[]{:S(2)}, u32[]{:S(2)}) %collective-permute-start.21) | collective-permute-done | bytes 262176 | tf_op jit(solution)/shard_map/ppermute | solution.py:444
  82.7 5.6 %collective-permute-done.20.refs_1_ = bf16[4,128,256]{2,1,0:T(8,128)(2,1)S(1)} collective-permute-done((bf16[4,128,256]{2,1,0:T(8,128)(2,1)S(1)}, bf16[4,128,256]{2,1,0:T(8,128)(2,1)S(1)}, u32[]{:S(2)}, u32[]{:S(2)}) %collective-permute-start.20) | collective-permute-done | bytes 262176 | tf_op jit(solution)/shard_map/ppermute | solution.py:444
  88.3 0.6 collective-permute-start.7
  88.9 2.0 %collective-permute-start.15 = (f32[16,128]{1,0:T(8,128)S(1)}, f32[16,128]{1,0:T(8,128)S(1)}, u32[]{:S(2)}, u32[]{:S(2)}) collective-permute-start(f32[16,128]{1,0:T(8,128)S(1)} %get-tuple-element.19.field_here), channel_id=1, source_target_pairs={{0,12},{2,14},{4,8},{6,10},{8,4},{10,6},{12,0},{14,2},{1,13},{3,15... | collective-permute-start | bytes 24584 | tf_op jit(solution)/shard_map/ppermute | solution.py:444
  90.9 2.0 %collective-permute-done.7.field_two = f32[16,128]{1,0:T(8,128)S(1)} collective-permute-done((f32[16,128]{1,0:T(8,128)S(1)}, f32[16,128]{1,0:T(8,128)S(1)}, u32[]{:S(2)}, u32[]{:S(2)}) %collective-permute-start.7) | collective-permute-done | bytes 8224 | tf_op jit(solution)/shard_map/ppermute | solution.py:444
  92.9 1.5 %collective-permute-done.15.field_ref = f32[16,128]{1,0:T(8,128)S(1)} collective-permute-done((f32[16,128]{1,0:T(8,128)S(1)}, f32[16,128]{1,0:T(8,128)S(1)}, u32[]{:S(2)}, u32[]{:S(2)}) %collective-permute-start.15) | collective-permute-done | bytes 8224 | tf_op jit(solution)/shard_map/ppermute | solution.py:444
  94.4 0.5 collective-permute-start.14
  95.0 0.4 collective-permute-start.22
  95.5 0.8 collective-permute-done.18.refs_2_
  96.4 0.6 collective-permute-done.14.refs_7_
  97.0 0.7 collective-permute-start.25
  97.7 4.5 %early_operator.1.summed_ref = f32[4,128,1024]{2,1,0:T(8,128)S(1)} custom-call(f32[16,128]{1,0:T(8,128)S(1)} %get-tuple-element.19.field_here, f32[16,128]{1,0:T(8,128)S(1)} %collective-permute-done.6.field_one, f32[16,128]{1,0:T(8,128)S(1)} %collective-permute-done.7.field_two, bf16[2,128,1024]{2,1,0:T(8,128)(2,1)S(1)} %copy-done.6, ...), custom_call_target="tpu_custom_call" | custom-call | tf_op jit(solution)/shard_map/early_operator/pallas_call | solution.py:292
  102.2 1.6 %split_operator.1.operator_ref = bf16[4,256,1024]{2,1,0:T(8,128)(2,1)S(1)} custom-call(f32[4,128,1024]{2,1,0:T(8,128)S(1)} %early_operator.1.summed_ref, f32[16,128]{1,0:T(8,128)S(1)} %collective-permute-done.15.field_ref, bf16[256,1024]{1,0:T(8,128)(2,1)S(1)} %collective-permute-done.16.refs_0_, bf16[256,1024]{1,0:T(8,128)(2,1)S(1)} %collective-permute-done.17.refs_1_, ...), custom_call_target="tpu_custom_call" | custom-call | tf_op jit(solution)/shard_map/split_operator/pallas_call | solution.py:325
  103.9 0.7 near_application.1.partial_ref
  104.6 0.8 collective-permute-done.25.mine
  105.4 1.5 %collective-permute-done.26.theirs = bf16[4,128,256]{2,1,0:T(8,128)(2,1)S(1)} collective-permute-done((bf16[4,128,256]{2,1,0:T(8,128)(2,1)S(1)}, bf16[4,128,256]{2,1,0:T(8,128)(2,1)S(1)}, u32[]{:S(2)}, u32[]{:S(2)}) %collective-permute-start.26) | collective-permute-done | bytes 262176 | tf_op jit(solution)/shard_map/ppermute | solution.py:448
  106.9 0.4 first_application.1
  107.3 0.7 collective-permute-start.27
  108.0 1.9 %collective-permute-start.28 = (bf16[4,128,256]{2,1,0:T(8,128)(2,1)S(1)}, bf16[4,128,256]{2,1,0:T(8,128)(2,1)S(1)}, u32[]{:S(2)}, u32[]{:S(2)}) collective-permute-start(bf16[4,128,256]{2,1,0:T(8,128)(2,1)S(1)} %get-tuple-element.29.refs_0_), channel_id=1, source_target_pairs={{0,8},{2,10},{4,12},{6,14},{8,0},{10,2},{12,4},{14,6},{1,9},{3,11}... | collective-permute-start | bytes 786440 | tf_op jit(solution)/shard_map/ppermute | solution.py:444
  109.9 10.8 %collective-permute-done.27.refs_1_ = bf16[4,128,256]{2,1,0:T(8,128)(2,1)S(1)} collective-permute-done((bf16[4,128,256]{2,1,0:T(8,128)(2,1)S(1)}, bf16[4,128,256]{2,1,0:T(8,128)(2,1)S(1)}, u32[]{:S(2)}, u32[]{:S(2)}) %collective-permute-start.27) | collective-permute-done | bytes 262176 | tf_op jit(solution)/shard_map/ppermute | solution.py:444
  120.7 1.9 %collective-permute-done.28.refs_2_ = bf16[4,128,256]{2,1,0:T(8,128)(2,1)S(1)} collective-permute-done((bf16[4,128,256]{2,1,0:T(8,128)(2,1)S(1)}, bf16[4,128,256]{2,1,0:T(8,128)(2,1)S(1)}, u32[]{:S(2)}, u32[]{:S(2)}) %collective-permute-start.28) | collective-permute-done | bytes 262176 | tf_op jit(solution)/shard_map/ppermute | solution.py:444
  122.7 1.5 %collective-permute-done.31.refs_5_ = bf16[4,128,256]{2,1,0:T(8,128)(2,1)S(1)} collective-permute-done((bf16[4,128,256]{2,1,0:T(8,128)(2,1)S(1)}, bf16[4,128,256]{2,1,0:T(8,128)(2,1)S(1)}, u32[]{:S(2)}, u32[]{:S(2)}) %collective-permute-start.31) | collective-permute-done | bytes 262176 | tf_op jit(solution)/shard_map/ppermute | solution.py:448
  124.2 0.7 base_application.1.base_ref
  124.9 6.4 %collective-permute-done.32.mine = bf16[4,128,256]{2,1,0:T(8,128)(2,1)S(1)} collective-permute-done((bf16[4,128,256]{2,1,0:T(8,128)(2,1)S(1)}, bf16[4,128,256]{2,1,0:T(8,128)(2,1)S(1)}, u32[]{:S(2)}, u32[]{:S(2)}) %collective-permute-start.32) | collective-permute-done | bytes 262176 | tf_op jit(solution)/shard_map/ppermute | solution.py:444
  131.4 1.5 %collective-permute-done.33.theirs = bf16[4,128,256]{2,1,0:T(8,128)(2,1)S(1)} collective-permute-done((bf16[4,128,256]{2,1,0:T(8,128)(2,1)S(1)}, bf16[4,128,256]{2,1,0:T(8,128)(2,1)S(1)}, u32[]{:S(2)}, u32[]{:S(2)}) %collective-permute-start.33) | collective-permute-done | bytes 262176 | tf_op jit(solution)/shard_map/ppermute | solution.py:448
  132.9 1.2 second_application.1
  (58 shorter events, 1.0 us)
Async XLA Ops:
  0.6 2.2 %copy-start = (bf16[2,1024,1024]{2,1,0:T(8,128)(2,1)S(1)}, bf16[2,1024,1024]{2,1,0:T(8,128)(2,1)}, u32[]{:S(2)}) copy-start(bf16[2,1024,1024]{2,1,0:T(8,128)(2,1)} %full_ref.1) | copy-start | bytes 12582916
  2.8 0.9 copy-start.2
  3.8 6.0 %copy-start.4 = (bf16[2,1024,256]{2,1,0:T(8,128)(2,1)S(1)}, bf16[2,1024,256]{2,1,0:T(8,128)(2,1)}, u32[]{:S(2)}) copy-start(bf16[2,1024,256]{2,1,0:T(8,128)(2,1)} %mine_ref.1) | copy-start | bytes 3145732
  3.8 41.6 %copy-start.9 = (f32[2]{0:T(128)S(1)}, f32[2]{0:T(128)}, u32[]{:S(2)}) copy-start(f32[2]{0:T(128)} %param.9) | copy-start | bytes 28
  3.8 41.8 %copy-start.8 = (f32[4,2]{0,1:T(2,128)S(1)}, f32[4,2]{0,1:T(2,128)}, u32[]{:S(2)}) copy-start(f32[4,2]{0,1:T(2,128)} %param.10) | copy-start | bytes 100
  5.1 0.8 copy-start.5
  5.9 0.8 copy-start.7
  6.7 51.9 %copy-start.1 = (f32[1,128,4,256]{3,2,1,0:T(4,128)S(1)}, f32[1,128,4,256]{3,2,1,0:T(4,128)}, u32[]{:S(2)}) copy-start(f32[1,128,4,256]{3,2,1,0:T(4,128)} %orbitals_ref.3) | copy-start | bytes 1572868
  6.8 62.0 %copy-start.3 = (bf16[4,128,256]{2,1,0:T(8,128)(2,1)S(1)}, bf16[4,128,256]{2,1,0:T(8,128)(2,1)}, u32[]{:S(2)}) copy-start(bf16[4,128,256]{2,1,0:T(8,128)(2,1)} %here_ref.1) | copy-start | bytes 786436
  6.8 36.1 %collective-permute-start = (bf16[384,1024]{1,0:T(8,128)(2,1)S(1)}, bf16[384,1024]{1,0:T(8,128)(2,1)S(1)}, u32[]{:S(2)}, u32[]{:S(2)}) collective-permute-start(bf16[384,1024]{1,0:T(8,128)(2,1)S(1)} %get-tuple-element.17), channel_id=1, source_target_pairs={{0,4},{2,6},{4,0},{6,2},{8,12},{10,14},{12,8},{14,10},{1,5},{3,7},... | collective-permute-start | bytes 2359304 | tf_op jit(solution)/shard_map/ppermute | solution.py:444
  9.8 37.2 %collective-permute-start.3 = (bf16[2,1024,256]{2,1,0:T(8,128)(2,1)S(1)}, bf16[2,1024,256]{2,1,0:T(8,128)(2,1)}, u32[]{:S(2)}, u32[]{:S(2)}) collective-permute-start(bf16[2,1024,256]{2,1,0:T(8,128)(2,1)S(1)} %copy-done.4), channel_id=1, source_target_pairs={{0,2},{2,0},{4,6},{6,4},{8,10},{10,8},{12,14},{14,12},{1,3},{3,1},... | collective-permute-start | bytes 3145736 | tf_op jit(solution)/shard_map/ppermute | solution.py:448
  9.8 39.7 %collective-permute-start.1 = (bf16[384,1024]{1,0:T(8,128)(2,1)}, bf16[384,1024]{1,0:T(8,128)(2,1)S(1)}, u32[]{:S(2)}, u32[]{:S(2)}) collective-permute-start(bf16[384,1024]{1,0:T(8,128)(2,1)} %get-tuple-element.18), channel_id=1, source_target_pairs={{0,8},{2,10},{4,12},{6,14},{8,0},{10,2},{12,4},{14,6},{1,9},{3,11}... | collective-permute-start | bytes 2359304 | tf_op jit(solution)/shard_map/ppermute | solution.py:444
  12.4 34.6 %collective-permute-start.8 = (bf16[2,128,1024]{2,1,0:T(8,128)(2,1)}, bf16[2,128,1024]{2,1,0:T(8,128)(2,1)}, u32[]{:S(2)}, u32[]{:S(2)}) collective-permute-start(bf16[2,128,1024]{2,1,0:T(8,128)(2,1)} %get-tuple-element.21), channel_id=1, source_target_pairs={{0,2},{2,0},{4,6},{6,4},{8,10},{10,8},{12,14},{14,12},{1,3},{3,1},... | collective-permute-start | bytes 1572872 | tf_op jit(solution)/shard_map/ppermute | solution.py:448
  43.7 13.4 %collective-permute-start.9 = (bf16[256,1024]{1,0:T(8,128)(2,1)}, bf16[256,1024]{1,0:T(8,128)(2,1)}, u32[]{:S(2)}, u32[]{:S(2)}) collective-permute-start(bf16[256,1024]{1,0:T(8,128)(2,1)} %slice.13), channel_id=1, source_target_pairs={{0,1},{1,0},{2,3},{3,2},{4,5},{5,4},{6,7},{7,6},{8,9},{9,8},{10,11... | collective-permute-start | bytes 1572872 | tf_op jit(solution)/shard_map/ppermute | solution.py:452
  45.8 1.2 collective-permute-start.5
  47.0 24.1 %collective-permute-start.16 = (bf16[256,1024]{1,0:T(8,128)(2,1)}, bf16[256,1024]{1,0:T(8,128)(2,1)S(1)}, u32[]{:S(2)}, u32[]{:S(2)}) collective-permute-start(bf16[256,1024]{1,0:T(8,128)(2,1)} %copy-done.7), channel_id=1, source_target_pairs={{0,12},{2,14},{4,8},{6,10},{8,4},{10,6},{12,0},{14,2},{1,13},{3,15... | collective-permute-start | bytes 1572872 | tf_op jit(solution)/shard_map/ppermute | solution.py:444
  57.2 21.2 %collective-permute-start.12 = (bf16[256,1024]{1,0:T(8,128)(2,1)S(1)}, bf16[256,1024]{1,0:T(8,128)(2,1)S(1)}, u32[]{:S(2)}, u32[]{:S(2)}) collective-permute-start(bf16[256,1024]{1,0:T(8,128)(2,1)S(1)} %slice.14), channel_id=1, source_target_pairs={{0,1},{1,0},{2,3},{3,2},{4,5},{5,4},{6,7},{7,6},{8,9},{9,8},{10,11... | collective-permute-start | bytes 1572872 | tf_op jit(solution)/shard_map/ppermute | solution.py:452
  58.5 35.9 %collective-permute-start.13 = (bf16[384,1024]{1,0:T(8,128)(2,1)S(1)}, bf16[384,1024]{1,0:T(8,128)(2,1)S(1)}, u32[]{:S(2)}, u32[]{:S(2)}) collective-permute-start(bf16[384,1024]{1,0:T(8,128)(2,1)S(1)} %collective-permute-done.1.two_ref.refs_4_), channel_id=1, source_target_pairs={{0,2},{2,0},{4,6},{6,4},{8,10},{10,8},{12,14},{14,12},{1,3},{3,1},... | collective-permute-start | bytes 2359304 | tf_op jit(solution)/shard_map/ppermute | solution.py:448
  58.5 10.2 %collective-permute-start.2 = (bf16[128,1024]{1,0:T(8,128)(2,1)S(1)}, bf16[128,1024]{1,0:T(8,128)(2,1)S(1)}, u32[]{:S(2)}, u32[]{:S(2)}) collective-permute-start(bf16[128,1024]{1,0:T(8,128)(2,1)S(1)} %slice.12), channel_id=1, source_target_pairs={{0,4},{2,6},{4,0},{6,2},{8,12},{10,14},{12,8},{14,10},{1,5},{3,7},... | collective-permute-start | bytes 786440 | tf_op jit(solution)/shard_map/ppermute | solution.py:444
  59.1 38.5 %copy-start.6 = (bf16[2,128,1024]{2,1,0:T(8,128)(2,1)S(1)}, bf16[2,128,1024]{2,1,0:T(8,128)(2,1)}, u32[]{:S(2)}) copy-start(bf16[2,128,1024]{2,1,0:T(8,128)(2,1)} %copy-done.5) | copy-start | bytes 1572868
  59.2 23.6 %collective-permute-start.21 = (bf16[4,128,256]{2,1,0:T(8,128)(2,1)S(1)}, bf16[4,128,256]{2,1,0:T(8,128)(2,1)S(1)}, u32[]{:S(2)}, u32[]{:S(2)}) collective-permute-start(bf16[4,128,256]{2,1,0:T(8,128)(2,1)S(1)} %walker_major.1.refs_0_), channel_id=1, source_target_pairs={{0,8},{2,10},{4,12},{6,14},{8,0},{10,2},{12,4},{14,6},{1,9},{3,11}... | collective-permute-start | bytes 786440 | tf_op jit(solution)/shard_map/ppermute | solution.py:444
  70.9 7.4 %collective-permute-start.4 = (f32[16,128]{1,0:T(8,128)S(1)}, f32[16,128]{1,0:T(8,128)S(1)}, u32[]{:S(2)}, u32[]{:S(2)}) collective-permute-start(f32[16,128]{1,0:T(8,128)S(1)} %chip_bias.1.mine_ref), channel_id=1, source_target_pairs={{0,2},{2,0},{4,6},{6,4},{8,10},{10,8},{12,14},{14,12},{1,3},{3,1},... | collective-permute-start | bytes 24584 | tf_op jit(solution)/shard_map/ppermute | solution.py:448
  71.1 17.3 %collective-permute-start.20 = (bf16[4,128,256]{2,1,0:T(8,128)(2,1)S(1)}, bf16[4,128,256]{2,1,0:T(8,128)(2,1)S(1)}, u32[]{:S(2)}, u32[]{:S(2)}) collective-permute-start(bf16[4,128,256]{2,1,0:T(8,128)(2,1)S(1)} %walker_major.1.refs_0_), channel_id=1, source_target_pairs={{0,4},{2,6},{4,0},{6,2},{8,12},{10,14},{12,8},{14,10},{1,5},{3,7},... | collective-permute-start | bytes 786440 | tf_op jit(solution)/shard_map/ppermute | solution.py:444
  78.4 16.6 %collective-permute-start.10 = (bf16[384,1024]{1,0:T(8,128)(2,1)S(1)}, bf16[384,1024]{1,0:T(8,128)(2,1)S(1)}, u32[]{:S(2)}, u32[]{:S(2)}) collective-permute-start(bf16[384,1024]{1,0:T(8,128)(2,1)S(1)} %collective-permute-done.one_ref.refs_0_), channel_id=1, source_target_pairs={{0,2},{2,0},{4,6},{6,4},{8,10},{10,8},{12,14},{14,12},{1,3},{3,1},... | collective-permute-start | bytes 2359304 | tf_op jit(solution)/shard_map/ppermute | solution.py:448
  78.4 16.5 %collective-permute-start.17 = (bf16[256,1024]{1,0:T(8,128)(2,1)S(1)}, bf16[256,1024]{1,0:T(8,128)(2,1)S(1)}, u32[]{:S(2)}, u32[]{:S(2)}) collective-permute-start(bf16[256,1024]{1,0:T(8,128)(2,1)S(1)} %collective-permute-done.16.refs_0_), channel_id=1, source_target_pairs={{0,1},{1,0},{2,3},{3,2},{4,5},{5,4},{6,7},{7,6},{8,9},{9,8},{10,11... | collective-permute-start | bytes 1572872 | tf_op jit(solution)/shard_map/ppermute | solution.py:452
  82.7 6.2 %collective-permute-start.6 = (f32[16,128]{1,0:T(8,128)S(1)}, f32[16,128]{1,0:T(8,128)S(1)}, u32[]{:S(2)}, u32[]{:S(2)}) collective-permute-start(f32[16,128]{1,0:T(8,128)S(1)} %get-tuple-element.19.field_here), channel_id=1, source_target_pairs={{0,4},{2,6},{4,0},{6,2},{8,12},{10,14},{12,8},{14,10},{1,5},{3,7},... | collective-permute-start | bytes 24584 | tf_op jit(solution)/shard_map/ppermute | solution.py:444
  88.3 4.5 %collective-permute-start.7 = (f32[16,128]{1,0:T(8,128)S(1)}, f32[16,128]{1,0:T(8,128)S(1)}, u32[]{:S(2)}, u32[]{:S(2)}) collective-permute-start(f32[16,128]{1,0:T(8,128)S(1)} %get-tuple-element.19.field_here), channel_id=1, source_target_pairs={{0,8},{2,10},{4,12},{6,14},{8,0},{10,2},{12,4},{14,6},{1,9},{3,11}... | collective-permute-start | bytes 24584 | tf_op jit(solution)/shard_map/ppermute | solution.py:444
  88.9 5.4 %collective-permute-start.15 = (f32[16,128]{1,0:T(8,128)S(1)}, f32[16,128]{1,0:T(8,128)S(1)}, u32[]{:S(2)}, u32[]{:S(2)}) collective-permute-start(f32[16,128]{1,0:T(8,128)S(1)} %get-tuple-element.19.field_here), channel_id=1, source_target_pairs={{0,12},{2,14},{4,8},{6,10},{8,4},{10,6},{12,0},{14,2},{1,13},{3,15... | collective-permute-start | bytes 24584 | tf_op jit(solution)/shard_map/ppermute | solution.py:444
  92.9 2.5 %collective-permute-start.11 = (bf16[256,1024]{1,0:T(8,128)(2,1)}, bf16[256,1024]{1,0:T(8,128)(2,1)S(1)}, u32[]{:S(2)}, u32[]{:S(2)}) collective-permute-start(bf16[256,1024]{1,0:T(8,128)(2,1)} %collective-permute-done.9.refs_1_), channel_id=1, source_target_pairs={{0,2},{2,0},{4,6},{6,4},{8,10},{10,8},{12,14},{14,12},{1,3},{3,1},... | collective-permute-start | bytes 1572872 | tf_op jit(solution)/shard_map/ppermute | solution.py:448
  94.4 1.9 %collective-permute-start.18 = (bf16[256,1024]{1,0:T(8,128)(2,1)S(1)}, bf16[256,1024]{1,0:T(8,128)(2,1)S(1)}, u32[]{:S(2)}, u32[]{:S(2)}) collective-permute-start(bf16[256,1024]{1,0:T(8,128)(2,1)S(1)} %collective-permute-done.16.refs_0_), channel_id=1, source_target_pairs={{0,2},{2,0},{4,6},{6,4},{8,10},{10,8},{12,14},{14,12},{1,3},{3,1},... | collective-permute-start | bytes 1572872 | tf_op jit(solution)/shard_map/ppermute | solution.py:448
  94.4 2.7 %collective-permute-start.14 = (bf16[256,1024]{1,0:T(8,128)(2,1)S(1)}, bf16[256,1024]{1,0:T(8,128)(2,1)S(1)}, u32[]{:S(2)}, u32[]{:S(2)}) collective-permute-start(bf16[256,1024]{1,0:T(8,128)(2,1)S(1)} %collective-permute-done.12.refs_5_), channel_id=1, source_target_pairs={{0,2},{2,0},{4,6},{6,4},{8,10},{10,8},{12,14},{14,12},{1,3},{3,1},... | collective-permute-start | bytes 1572872 | tf_op jit(solution)/shard_map/ppermute | solution.py:448
  94.9 7.4 %collective-permute-start.19 = (bf16[256,1024]{1,0:T(8,128)(2,1)S(1)}, bf16[256,1024]{1,0:T(8,128)(2,1)S(1)}, u32[]{:S(2)}, u32[]{:S(2)}) collective-permute-start(bf16[256,1024]{1,0:T(8,128)(2,1)S(1)} %collective-permute-done.17.refs_1_), channel_id=1, source_target_pairs={{0,2},{2,0},{4,6},{6,4},{8,10},{10,8},{12,14},{14,12},{1,3},{3,1},... | collective-permute-start | bytes 1572872 | tf_op jit(solution)/shard_map/ppermute | solution.py:448
  95.0 8.9 %collective-permute-start.22 = (bf16[4,128,256]{2,1,0:T(8,128)(2,1)S(1)}, bf16[4,128,256]{2,1,0:T(8,128)(2,1)S(1)}, u32[]{:S(2)}, u32[]{:S(2)}) collective-permute-start(bf16[4,128,256]{2,1,0:T(8,128)(2,1)S(1)} %walker_major.1.refs_0_), channel_id=1, source_target_pairs={{0,2},{2,0},{4,6},{6,4},{8,10},{10,8},{12,14},{14,12},{1,3},{3,1},... | collective-permute-start | bytes 786440 | tf_op jit(solution)/shard_map/ppermute | solution.py:448
  95.4 8.5 %collective-permute-start.24 = (bf16[4,128,256]{2,1,0:T(8,128)(2,1)S(1)}, bf16[4,128,256]{2,1,0:T(8,128)(2,1)S(1)}, u32[]{:S(2)}, u32[]{:S(2)}) collective-permute-start(bf16[4,128,256]{2,1,0:T(8,128)(2,1)S(1)} %collective-permute-done.21.refs_2_), channel_id=1, source_target_pairs={{0,2},{2,0},{4,6},{6,4},{8,10},{10,8},{12,14},{14,12},{1,3},{3,1},... | collective-permute-start | bytes 786440 | tf_op jit(solution)/shard_map/ppermute | solution.py:448
  96.3 7.6 %collective-permute-start.23 = (bf16[4,128,256]{2,1,0:T(8,128)(2,1)S(1)}, bf16[4,128,256]{2,1,0:T(8,128)(2,1)S(1)}, u32[]{:S(2)}, u32[]{:S(2)}) collective-permute-start(bf16[4,128,256]{2,1,0:T(8,128)(2,1)S(1)} %collective-permute-done.20.refs_1_), channel_id=1, source_target_pairs={{0,2},{2,0},{4,6},{6,4},{8,10},{10,8},{12,14},{14,12},{1,3},{3,1},... | collective-permute-start | bytes 786440 | tf_op jit(solution)/shard_map/ppermute | solution.py:448
  97.0 8.3 %collective-permute-start.25 = (bf16[4,128,256]{2,1,0:T(8,128)(2,1)S(1)}, bf16[4,128,256]{2,1,0:T(8,128)(2,1)S(1)}, u32[]{:S(2)}, u32[]{:S(2)}) collective-permute-start(bf16[4,128,256]{2,1,0:T(8,128)(2,1)S(1)} %collective-permute-done.21.refs_2_), channel_id=1, source_target_pairs={{0,4},{2,6},{4,0},{6,2},{8,12},{10,14},{12,8},{14,10},{1,5},{3,7},... | collective-permute-start | bytes 786440 | tf_op jit(solution)/shard_map/ppermute | solution.py:444
  105.4 1.5 %collective-permute-start.26 = (bf16[4,128,256]{2,1,0:T(8,128)(2,1)S(1)}, bf16[4,128,256]{2,1,0:T(8,128)(2,1)S(1)}, u32[]{:S(2)}, u32[]{:S(2)}) collective-permute-start(bf16[4,128,256]{2,1,0:T(8,128)(2,1)S(1)} %collective-permute-done.25.mine), channel_id=1, source_target_pairs={{0,2},{2,0},{4,6},{6,4},{8,10},{10,8},{12,14},{14,12},{1,3},{3,1},... | collective-permute-start | bytes 786440 | tf_op jit(solution)/shard_map/ppermute | solution.py:448
  107.3 13.4 %collective-permute-start.27 = (bf16[4,128,256]{2,1,0:T(8,128)(2,1)S(1)}, bf16[4,128,256]{2,1,0:T(8,128)(2,1)S(1)}, u32[]{:S(2)}, u32[]{:S(2)}) collective-permute-start(bf16[4,128,256]{2,1,0:T(8,128)(2,1)S(1)} %get-tuple-element.29.refs_0_), channel_id=1, source_target_pairs={{0,4},{2,6},{4,0},{6,2},{8,12},{10,14},{12,8},{14,10},{1,5},{3,7},... | collective-permute-start | bytes 786440 | tf_op jit(solution)/shard_map/ppermute | solution.py:444
  108.0 14.6 %collective-permute-start.28 = (bf16[4,128,256]{2,1,0:T(8,128)(2,1)S(1)}, bf16[4,128,256]{2,1,0:T(8,128)(2,1)S(1)}, u32[]{:S(2)}, u32[]{:S(2)}) collective-permute-start(bf16[4,128,256]{2,1,0:T(8,128)(2,1)S(1)} %get-tuple-element.29.refs_0_), channel_id=1, source_target_pairs={{0,8},{2,10},{4,12},{6,14},{8,0},{10,2},{12,4},{14,6},{1,9},{3,11}... | collective-permute-start | bytes 786440 | tf_op jit(solution)/shard_map/ppermute | solution.py:444
  109.9 12.8 %collective-permute-start.29 = (bf16[4,128,256]{2,1,0:T(8,128)(2,1)S(1)}, bf16[4,128,256]{2,1,0:T(8,128)(2,1)S(1)}, u32[]{:S(2)}, u32[]{:S(2)}) collective-permute-start(bf16[4,128,256]{2,1,0:T(8,128)(2,1)S(1)} %get-tuple-element.29.refs_0_), channel_id=1, source_target_pairs={{0,2},{2,0},{4,6},{6,4},{8,10},{10,8},{12,14},{14,12},{1,3},{3,1},... | collective-permute-start | bytes 786440 | tf_op jit(solution)/shard_map/ppermute | solution.py:448
  120.7 2.0 %collective-permute-start.30 = (bf16[4,128,256]{2,1,0:T(8,128)(2,1)S(1)}, bf16[4,128,256]{2,1,0:T(8,128)(2,1)S(1)}, u32[]{:S(2)}, u32[]{:S(2)}) collective-permute-start(bf16[4,128,256]{2,1,0:T(8,128)(2,1)S(1)} %collective-permute-done.27.refs_1_), channel_id=1, source_target_pairs={{0,2},{2,0},{4,6},{6,4},{8,10},{10,8},{12,14},{14,12},{1,3},{3,1},... | collective-permute-start | bytes 786440 | tf_op jit(solution)/shard_map/ppermute | solution.py:448
  122.6 1.5 %collective-permute-start.31 = (bf16[4,128,256]{2,1,0:T(8,128)(2,1)S(1)}, bf16[4,128,256]{2,1,0:T(8,128)(2,1)S(1)}, u32[]{:S(2)}, u32[]{:S(2)}) collective-permute-start(bf16[4,128,256]{2,1,0:T(8,128)(2,1)S(1)} %collective-permute-done.28.refs_2_), channel_id=1, source_target_pairs={{0,2},{2,0},{4,6},{6,4},{8,10},{10,8},{12,14},{14,12},{1,3},{3,1},... | collective-permute-start | bytes 786440 | tf_op jit(solution)/shard_map/ppermute | solution.py:448
  122.6 8.7 %collective-permute-start.32 = (bf16[4,128,256]{2,1,0:T(8,128)(2,1)S(1)}, bf16[4,128,256]{2,1,0:T(8,128)(2,1)S(1)}, u32[]{:S(2)}, u32[]{:S(2)}) collective-permute-start(bf16[4,128,256]{2,1,0:T(8,128)(2,1)S(1)} %collective-permute-done.28.refs_2_), channel_id=1, source_target_pairs={{0,4},{2,6},{4,0},{6,2},{8,12},{10,14},{12,8},{14,10},{1,5},{3,7},... | collective-permute-start | bytes 786440 | tf_op jit(solution)/shard_map/ppermute | solution.py:444
  131.4 1.5 %collective-permute-start.33 = (bf16[4,128,256]{2,1,0:T(8,128)(2,1)S(1)}, bf16[4,128,256]{2,1,0:T(8,128)(2,1)S(1)}, u32[]{:S(2)}, u32[]{:S(2)}) collective-permute-start(bf16[4,128,256]{2,1,0:T(8,128)(2,1)S(1)} %collective-permute-done.32.mine), channel_id=1, source_target_pairs={{0,2},{2,0},{4,6},{6,4},{8,10},{10,8},{12,14},{14,12},{1,3},{3,1},... | collective-permute-start | bytes 786440 | tf_op jit(solution)/shard_map/ppermute | solution.py:448

commit v9 on v8

--- a/solution.py
+++ b/solution.py
@@ -117,7 +117,6 @@
         in_specs=[hbm_spec, vmem_spec],
         out_specs=[vmem_spec] * 5,
         scratch_shapes=[pltpu.SemaphoreType.DMA((8,))],
-        compiler_params=small,
         name="packed",
     )(full_chol, green_blocks)
 
@@ -466,9 +465,7 @@
     three = to_chip(after(three, one, half_theirs, own_theirs, constants_theirs), 3)
     green_three = to_chip(two[:rows], 1)
 
-    one_x = across(one[rows:])
-    two_x = across(after(two[rows:], one_x))
-    three_x = across(after(three, two_x))
+    one_x, two_x, three_x = across(one[rows:]), across(two[rows:]), across(three)
     messages = {1: (one, one_x), 2: (two, two_x), 3: (three, three_x)}
     blocks = {step: [*both, *[to_core(each) for each in both]] for step, both in messages.items()}
 
@@ -476,9 +473,9 @@
     bias_shift, field = chip_field(bias, to_core(bias), constants, constants_theirs, vectors)
     field_one, field_two, field_three = (to_chip(field, step) for step in (1, 2, 3))
 
-    start = after(walker_major(orbitals), two)
+    start = after(walker_major(orbitals), field_two, blocks[1][2], blocks[2][2])
     start_two, start_one = to_chip(start, 2), to_chip(start, 1)
-    start_three = to_chip(start_two, 1)
+    start_three = to_chip(after(start_two, blocks[1][3], blocks[2][3], blocks[3][2]), 1)
 
     summed = early_operator(
         walkers,

time: 134 us -> 144 us (1.075)
  waiting for transfers between devices: 84 us -> 92.4 us
  local copies, waits for them, and re-layouts: 5.99 us -> 0.42 us
  starting transfers between devices: 29.4 us -> 34.4 us
  Pallas kernels: 13.9 us -> 15.7 us
    ppermute x3, waiting for transfers between devices: 7.68 us -> 17.9 us  [across(): return lax.ppermute(value, 'walk', [(0, 1), (1, 0)])]
    unnamed x20 -> x12, local copies, waits for them, and re-layouts: 4.77 us -> 0.03 us
    ppermute x13, starting transfers between devices: 24.4 us -> 27.4 us  [to_chip(): return lax.ppermute(value, 'chol', [(i, i ^ 2 * step) for i in range(8)])]
    pallas_call x1, Pallas kernels: 1.33 us -> 4.35 us  [packed(): pl.pallas_call(pack_kernel, out_shape=[jax.ShapeDtypeStruct(shape, narrow...]
  transfers between devices with their start and end apart: 34 -> 34, of which waited for: 17 -> 16; matrix products, arithmetic and copies ran while one was open for 1% -> 0% of each run, Pallas kernels for 8% -> 10%
where the time goes in v9:
time: 144 us
  waiting for transfers between devices  92.4 us (64%)
  starting transfers between devices  34.4 us (24%)
  Pallas kernels  15.7 us (11%)
    ppermute x13, waiting for transfers between devices, to_chip(): return lax.ppermute(value, 'chol', [(i, i ^ 2 * step) for i in range(8)])  68 us
    ppermute x13, starting transfers between devices, to_chip(): return lax.ppermute(value, 'chol', [(i, i ^ 2 * step) for i in range(8)])  27.4 us
    ppermute x3, waiting for transfers between devices, across(): return lax.ppermute(value, 'walk', [(0, 1), (1, 0)])  17.9 us
    ppermute x18, waiting for transfers between devices, to_core(): return lax.ppermute(value, 'chol', [(i, i ^ 1) for i in range(8)])  6.43 us
    ppermute x3, starting transfers between devices, across(): return lax.ppermute(value, 'walk', [(0, 1), (1, 0)])  4.61 us
    pallas_call x1, Pallas kernels, packed(): pl.pallas_call(pack_kernel, out_shape=[jax.ShapeDtypeStruct(shape, narrow...  4.35 us
    pallas_call x1, Pallas kernels, early_operator(): pl.pallas_call(functools.partial(early_kernel, walkers), out_shape=jax.Sh...  3.36 us
  transfers between devices with their start and end apart: 34, of which 16 were waited for; matrix products, arithmetic and copies ran while one was open for 0% of the time, Pallas kernels for 10%

profile of v9, /device:TPU:0, one launch (start us, length us, event | category | flops | bytes accessed | tf_op | source)
XLA Modules:
  0.0 143.8 jit_solution(1353735955539015288)
XLA Ops:
  0.7 0.5 collective-permute-start.3
  1.2 4.3 %packed.1 = (bf16[384,1024]{1,0:T(8,128)(2,1)}, bf16[384,1024]{1,0:T(8,128)(2,1)}, bf16[256,1024]{1,0:T(8,128)(2,1)}, bf16[2,128,1024]{2,1,0:T(8,128)(2,1)}, bf16[2,128,1024]{2,1,0:T(8,128)(2,1)}) custom-call(bf16[2,1024,1024]{2,1,0:T(8,128)(2,1)} %full_ref.1, bf16[4,128,256]{2,1,0:T(8,128)(2,1)} %here_ref.1), custom_call_target="tpu_custom_call" | custom-call | tf_op jit(solution)/shard_map/packed/pallas_call | solution.py:114
  5.5 3.8 %collective-permute-start.1 = (bf16[384,1024]{1,0:T(8,128)(2,1)}, bf16[384,1024]{1,0:T(8,128)(2,1)S(1)}, u32[]{:S(2)}, u32[]{:S(2)}) collective-permute-start(bf16[384,1024]{1,0:T(8,128)(2,1)} %get-tuple-element.17), channel_id=1, source_target_pairs={{0,8},{2,10},{4,12},{6,14},{8,0},{10,2},{12,4},{14,6},{1,9},{3,11}... | collective-permute-start | bytes 2359304 | tf_op jit(solution)/shard_map/ppermute | solution.py:443
  9.3 1.6 %collective-permute-start = (bf16[384,1024]{1,0:T(8,128)(2,1)}, bf16[384,1024]{1,0:T(8,128)(2,1)S(1)}, u32[]{:S(2)}, u32[]{:S(2)}) collective-permute-start(bf16[384,1024]{1,0:T(8,128)(2,1)} %get-tuple-element.16), channel_id=1, source_target_pairs={{0,4},{2,6},{4,0},{6,2},{8,12},{10,14},{12,8},{14,10},{1,5},{3,7},... | collective-permute-start | bytes 2359304 | tf_op jit(solution)/shard_map/ppermute | solution.py:443
  11.0 0.1 reshape.12
  11.0 0.1 reshape.11
  11.1 33.5 %collective-permute-done.1.two_ref.refs_4_ = bf16[384,1024]{1,0:T(8,128)(2,1)S(1)} collective-permute-done((bf16[384,1024]{1,0:T(8,128)(2,1)}, bf16[384,1024]{1,0:T(8,128)(2,1)S(1)}, u32[]{:S(2)}, u32[]{:S(2)}) %collective-permute-start.1) | collective-permute-done | bytes 786464 | tf_op jit(solution)/shard_map/ppermute | solution.py:443
  44.6 0.8 collective-permute-start.2
  45.4 0.1 pad_maximum_fusion
  45.6 0.5 collective-permute-start.10
  46.1 0.7 collective-permute-done.5.noise_there_ref
  46.8 2.7 %collective-permute-start.16 = (bf16[256,1024]{1,0:T(8,128)(2,1)}, bf16[256,1024]{1,0:T(8,128)(2,1)S(1)}, u32[]{:S(2)}, u32[]{:S(2)}) collective-permute-start(bf16[256,1024]{1,0:T(8,128)(2,1)} %get-tuple-element.22), channel_id=1, source_target_pairs={{0,12},{2,14},{4,8},{6,10},{8,4},{10,6},{12,0},{14,2},{1,13},{3,15... | collective-permute-start | bytes 1572872 | tf_op jit(solution)/shard_map/ppermute | solution.py:443
  49.5 1.6 %collective-permute-start.9 = (bf16[256,1024]{1,0:T(8,128)(2,1)S(1)}, bf16[256,1024]{1,0:T(8,128)(2,1)S(1)}, u32[]{:S(2)}, u32[]{:S(2)}) collective-permute-start(bf16[256,1024]{1,0:T(8,128)(2,1)S(1)} %slice.13), channel_id=1, source_target_pairs={{0,1},{1,0},{2,3},{3,2},{4,5},{5,4},{6,7},{7,6},{8,9},{9,8},{10,11... | collective-permute-start | bytes 1572872 | tf_op jit(solution)/shard_map/ppermute | solution.py:451
  51.1 1.5 %collective-permute-done.2.three_ref = bf16[128,1024]{1,0:T(8,128)(2,1)S(1)} collective-permute-done((bf16[128,1024]{1,0:T(8,128)(2,1)S(1)}, bf16[128,1024]{1,0:T(8,128)(2,1)S(1)}, u32[]{:S(2)}, u32[]{:S(2)}) %collective-permute-start.2) | collective-permute-done | bytes 262176 | tf_op jit(solution)/shard_map/ppermute | solution.py:443
  52.6 2.2 %chip_bias.1.mine_ref = f32[16,128]{1,0:T(8,128)S(1)} custom-call(bf16[4,128,256]{2,1,0:T(8,128)(2,1)S(1)} %copy-done.1, bf16[384,1024]{1,0:T(8,128)(2,1)S(1)} %collective-permute-done.one_ref.refs_0_, bf16[384,1024]{1,0:T(8,128)(2,1)S(1)} %collective-permute-done.1.two_ref.refs_4_, bf16[128,1024]{1,0:T(8,128)(2,1)S(1)} %collective-permute-done.2.three_ref, ...), custom_call_target="tpu_custom_call" | custom-call | tf_op jit(solution)/shard_map/chip_bias/pallas_call | solution.py:181
  54.9 1.2 collective-permute-done.4.theirs_ref
  56.1 0.6 chip_field.1
  56.7 13.1 %collective-permute-start.7 = (f32[16,128]{1,0:T(8,128)S(1)}, f32[16,128]{1,0:T(8,128)S(1)}, u32[]{:S(2)}, u32[]{:S(2)}) collective-permute-start(f32[16,128]{1,0:T(8,128)S(1)} %get-tuple-element.18.field_here), channel_id=1, source_target_pairs={{0,8},{2,10},{4,12},{6,14},{8,0},{10,2},{12,4},{14,6},{1,9},{3,11}... | collective-permute-start | bytes 24584 | tf_op jit(solution)/shard_map/ppermute | solution.py:443
  69.8 1.6 %collective-permute-start.12 = (bf16[256,1024]{1,0:T(8,128)(2,1)S(1)}, bf16[256,1024]{1,0:T(8,128)(2,1)S(1)}, u32[]{:S(2)}, u32[]{:S(2)}) collective-permute-start(bf16[256,1024]{1,0:T(8,128)(2,1)S(1)} %slice.14), channel_id=1, source_target_pairs={{0,1},{1,0},{2,3},{3,2},{4,5},{5,4},{6,7},{7,6},{8,9},{9,8},{10,11... | collective-permute-start | bytes 1572872 | tf_op jit(solution)/shard_map/ppermute | solution.py:451
  71.4 2.7 %collective-permute-done.7.field_two = f32[16,128]{1,0:T(8,128)S(1)} collective-permute-done((f32[16,128]{1,0:T(8,128)S(1)}, f32[16,128]{1,0:T(8,128)S(1)}, u32[]{:S(2)}, u32[]{:S(2)}) %collective-permute-start.7) | collective-permute-done | bytes 8224 | tf_op jit(solution)/shard_map/ppermute | solution.py:443
  74.1 1.5 %collective-permute-start.17 = (bf16[256,1024]{1,0:T(8,128)(2,1)S(1)}, bf16[256,1024]{1,0:T(8,128)(2,1)S(1)}, u32[]{:S(2)}, u32[]{:S(2)}) collective-permute-start(bf16[256,1024]{1,0:T(8,128)(2,1)S(1)} %collective-permute-done.16.refs_0_), channel_id=1, source_target_pairs={{0,1},{1,0},{2,3},{3,2},{4,5},{5,4},{6,7},{7,6},{8,9},{9,8},{10,11... | collective-permute-start | bytes 1572872 | tf_op jit(solution)/shard_map/ppermute | solution.py:451
  75.6 0.2 collective-permute-start.11
  75.8 8.9 %collective-permute-done.12.refs_5_ = bf16[256,1024]{1,0:T(8,128)(2,1)S(1)} collective-permute-done((bf16[256,1024]{1,0:T(8,128)(2,1)S(1)}, bf16[256,1024]{1,0:T(8,128)(2,1)S(1)}, u32[]{:S(2)}, u32[]{:S(2)}) %collective-permute-start.12) | collective-permute-done | bytes 524320 | tf_op jit(solution)/shard_map/ppermute | solution.py:451
  84.7 0.5 collective-permute-start.18
  85.2 0.5 walker_major.1.refs_0_
  85.8 9.0 %collective-permute-done.17.refs_1_ = bf16[256,1024]{1,0:T(8,128)(2,1)S(1)} collective-permute-done((bf16[256,1024]{1,0:T(8,128)(2,1)S(1)}, bf16[256,1024]{1,0:T(8,128)(2,1)S(1)}, u32[]{:S(2)}, u32[]{:S(2)}) %collective-permute-start.17) | collective-permute-done | bytes 524320 | tf_op jit(solution)/shard_map/ppermute | solution.py:451
  94.8 2.5 %collective-permute-start.20 = (bf16[4,128,256]{2,1,0:T(8,128)(2,1)S(1)}, bf16[4,128,256]{2,1,0:T(8,128)(2,1)S(1)}, u32[]{:S(2)}, u32[]{:S(2)}) collective-permute-start(bf16[4,128,256]{2,1,0:T(8,128)(2,1)S(1)} %walker_major.1.refs_0_), channel_id=1, source_target_pairs={{0,4},{2,6},{4,0},{6,2},{8,12},{10,14},{12,8},{14,10},{1,5},{3,7},... | collective-permute-start | bytes 786440 | tf_op jit(solution)/shard_map/ppermute | solution.py:443
  97.3 0.1 collective-permute-start.6
  97.4 3.2 %collective-permute-done.21.refs_2_ = bf16[4,128,256]{2,1,0:T(8,128)(2,1)S(1)} collective-permute-done((bf16[4,128,256]{2,1,0:T(8,128)(2,1)S(1)}, bf16[4,128,256]{2,1,0:T(8,128)(2,1)S(1)}, u32[]{:S(2)}, u32[]{:S(2)}) %collective-permute-start.21) | collective-permute-done | bytes 262176 | tf_op jit(solution)/shard_map/ppermute | solution.py:443
  100.6 1.2 collective-permute-start.15
  101.8 4.7 %collective-permute-done.6.field_one = f32[16,128]{1,0:T(8,128)S(1)} collective-permute-done((f32[16,128]{1,0:T(8,128)S(1)}, f32[16,128]{1,0:T(8,128)S(1)}, u32[]{:S(2)}, u32[]{:S(2)}) %collective-permute-start.6) | collective-permute-done | bytes 8224 | tf_op jit(solution)/shard_map/ppermute | solution.py:443
  106.5 0.1 collective-permute-start.24
  106.6 0.4 collective-permute-start.23
  107.0 3.4 %early_operator.1.summed_ref = f32[4,128,1024]{2,1,0:T(8,128)S(1)} custom-call(f32[16,128]{1,0:T(8,128)S(1)} %get-tuple-element.18.field_here, f32[16,128]{1,0:T(8,128)S(1)} %collective-permute-done.6.field_one, f32[16,128]{1,0:T(8,128)S(1)} %collective-permute-done.7.field_two, bf16[2,128,1024]{2,1,0:T(8,128)(2,1)S(1)} %copy-done.3, ...), custom_call_target="tpu_custom_call" | custom-call | tf_op jit(solution)/shard_map/early_operator/pallas_call | solution.py:291
  110.4 1.6 %split_operator.1.operator_ref = bf16[4,256,1024]{2,1,0:T(8,128)(2,1)S(1)} custom-call(f32[4,128,1024]{2,1,0:T(8,128)S(1)} %early_operator.1.summed_ref, f32[16,128]{1,0:T(8,128)S(1)} %collective-permute-done.15.field_ref, bf16[256,1024]{1,0:T(8,128)(2,1)S(1)} %collective-permute-done.16.refs_0_, bf16[256,1024]{1,0:T(8,128)(2,1)S(1)} %collective-permute-done.17.refs_1_, ...), custom_call_target="tpu_custom_call" | custom-call | tf_op jit(solution)/shard_map/split_operator/pallas_call | solution.py:324
  112.0 0.7 near_application.1.partial_ref
  112.8 2.6 %collective-permute-done.25.mine = bf16[4,128,256]{2,1,0:T(8,128)(2,1)S(1)} collective-permute-done((bf16[4,128,256]{2,1,0:T(8,128)(2,1)S(1)}, bf16[4,128,256]{2,1,0:T(8,128)(2,1)S(1)}, u32[]{:S(2)}, u32[]{:S(2)}) %collective-permute-start.25) | collective-permute-done | bytes 262176 | tf_op jit(solution)/shard_map/ppermute | solution.py:443
  115.3 1.5 %collective-permute-done.26.theirs = bf16[4,128,256]{2,1,0:T(8,128)(2,1)S(1)} collective-permute-done((bf16[4,128,256]{2,1,0:T(8,128)(2,1)S(1)}, bf16[4,128,256]{2,1,0:T(8,128)(2,1)S(1)}, u32[]{:S(2)}, u32[]{:S(2)}) %collective-permute-start.26) | collective-permute-done | bytes 262176 | tf_op jit(solution)/shard_map/ppermute | solution.py:447
  116.9 0.4 first_application.1
  117.2 0.3 collective-permute-start.27
  117.6 1.3 collective-permute-start.28
  118.9 10.7 %collective-permute-done.27.refs_1_ = bf16[4,128,256]{2,1,0:T(8,128)(2,1)S(1)} collective-permute-done((bf16[4,128,256]{2,1,0:T(8,128)(2,1)S(1)}, bf16[4,128,256]{2,1,0:T(8,128)(2,1)S(1)}, u32[]{:S(2)}, u32[]{:S(2)}) %collective-permute-start.27) | collective-permute-done | bytes 262176 | tf_op jit(solution)/shard_map/ppermute | solution.py:443
  129.6 2.7 %collective-permute-done.28.refs_2_ = bf16[4,128,256]{2,1,0:T(8,128)(2,1)S(1)} collective-permute-done((bf16[4,128,256]{2,1,0:T(8,128)(2,1)S(1)}, bf16[4,128,256]{2,1,0:T(8,128)(2,1)S(1)}, u32[]{:S(2)}, u32[]{:S(2)}) %collective-permute-start.28) | collective-permute-done | bytes 262176 | tf_op jit(solution)/shard_map/ppermute | solution.py:443
  132.3 1.5 %collective-permute-done.31.refs_5_ = bf16[4,128,256]{2,1,0:T(8,128)(2,1)S(1)} collective-permute-done((bf16[4,128,256]{2,1,0:T(8,128)(2,1)S(1)}, bf16[4,128,256]{2,1,0:T(8,128)(2,1)S(1)}, u32[]{:S(2)}, u32[]{:S(2)}) %collective-permute-start.31) | collective-permute-done | bytes 262176 | tf_op jit(solution)/shard_map/ppermute | solution.py:447
  133.8 0.8 base_application.1.base_ref
  134.6 6.4 %collective-permute-done.32.mine = bf16[4,128,256]{2,1,0:T(8,128)(2,1)S(1)} collective-permute-done((bf16[4,128,256]{2,1,0:T(8,128)(2,1)S(1)}, bf16[4,128,256]{2,1,0:T(8,128)(2,1)S(1)}, u32[]{:S(2)}, u32[]{:S(2)}) %collective-permute-start.32) | collective-permute-done | bytes 262176 | tf_op jit(solution)/shard_map/ppermute | solution.py:443
  141.0 1.5 %collective-permute-done.33.theirs = bf16[4,128,256]{2,1,0:T(8,128)(2,1)S(1)} collective-permute-done((bf16[4,128,256]{2,1,0:T(8,128)(2,1)S(1)}, bf16[4,128,256]{2,1,0:T(8,128)(2,1)S(1)}, u32[]{:S(2)}, u32[]{:S(2)}) %collective-permute-start.33) | collective-permute-done | bytes 262176 | tf_op jit(solution)/shard_map/ppermute | solution.py:447
  142.5 1.2 second_application.1
  (50 shorter events, 0.5 us)
Async XLA Ops:
  0.6 52.0 %copy-start.2 = (bf16[2,1024,256]{2,1,0:T(8,128)(2,1)S(1)}, bf16[2,1024,256]{2,1,0:T(8,128)(2,1)}, u32[]{:S(2)}) copy-start(bf16[2,1024,256]{2,1,0:T(8,128)(2,1)} %mine_ref.1) | copy-start | bytes 3145732
  0.6 52.0 %copy-start.1 = (bf16[4,128,256]{2,1,0:T(8,128)(2,1)S(1)}, bf16[4,128,256]{2,1,0:T(8,128)(2,1)}, u32[]{:S(2)}) copy-start(bf16[4,128,256]{2,1,0:T(8,128)(2,1)} %here_ref.1) | copy-start | bytes 786436
  0.7 10.2 %copy-start.5 = (f32[2]{0:T(128)S(1)}, f32[2]{0:T(128)}, u32[]{:S(2)}) copy-start(f32[2]{0:T(128)} %param.9) | copy-start | bytes 28
  0.7 10.4 %copy-start.4 = (f32[4,2]{0,1:T(2,128)S(1)}, f32[4,2]{0,1:T(2,128)}, u32[]{:S(2)}) copy-start(f32[4,2]{0,1:T(2,128)} %param.10) | copy-start | bytes 100
  0.7 46.1 %collective-permute-start.3 = (bf16[2,1024,256]{2,1,0:T(8,128)(2,1)}, bf16[2,1024,256]{2,1,0:T(8,128)(2,1)}, u32[]{:S(2)}, u32[]{:S(2)}) collective-permute-start(bf16[2,1024,256]{2,1,0:T(8,128)(2,1)} %mine_ref.1), channel_id=1, source_target_pairs={{0,2},{2,0},{4,6},{6,4},{8,10},{10,8},{12,14},{14,12},{1,3},{3,1},... | collective-permute-start | bytes 3145736 | tf_op jit(solution)/shard_map/ppermute | solution.py:447
  5.5 39.0 %collective-permute-start.1 = (bf16[384,1024]{1,0:T(8,128)(2,1)}, bf16[384,1024]{1,0:T(8,128)(2,1)S(1)}, u32[]{:S(2)}, u32[]{:S(2)}) collective-permute-start(bf16[384,1024]{1,0:T(8,128)(2,1)} %get-tuple-element.17), channel_id=1, source_target_pairs={{0,8},{2,10},{4,12},{6,14},{8,0},{10,2},{12,4},{14,6},{1,9},{3,11}... | collective-permute-start | bytes 2359304 | tf_op jit(solution)/shard_map/ppermute | solution.py:443
  9.3 36.3 %collective-permute-start = (bf16[384,1024]{1,0:T(8,128)(2,1)}, bf16[384,1024]{1,0:T(8,128)(2,1)S(1)}, u32[]{:S(2)}, u32[]{:S(2)}) collective-permute-start(bf16[384,1024]{1,0:T(8,128)(2,1)} %get-tuple-element.16), channel_id=1, source_target_pairs={{0,4},{2,6},{4,0},{6,2},{8,12},{10,14},{12,8},{14,10},{1,5},{3,7},... | collective-permute-start | bytes 2359304 | tf_op jit(solution)/shard_map/ppermute | solution.py:443
  10.9 35.9 %collective-permute-start.8 = (bf16[2,128,1024]{2,1,0:T(8,128)(2,1)}, bf16[2,128,1024]{2,1,0:T(8,128)(2,1)S(1)}, u32[]{:S(2)}, u32[]{:S(2)}) collective-permute-start(bf16[2,128,1024]{2,1,0:T(8,128)(2,1)} %get-tuple-element.20), channel_id=1, source_target_pairs={{0,2},{2,0},{4,6},{6,4},{8,10},{10,8},{12,14},{14,12},{1,3},{3,1},... | collective-permute-start | bytes 1572872 | tf_op jit(solution)/shard_map/ppermute | solution.py:447
  44.6 8.0 %collective-permute-start.2 = (bf16[128,1024]{1,0:T(8,128)(2,1)S(1)}, bf16[128,1024]{1,0:T(8,128)(2,1)S(1)}, u32[]{:S(2)}, u32[]{:S(2)}) collective-permute-start(bf16[128,1024]{1,0:T(8,128)(2,1)S(1)} %slice.12), channel_id=1, source_target_pairs={{0,4},{2,6},{4,0},{6,2},{8,12},{10,14},{12,8},{14,10},{1,5},{3,7},... | collective-permute-start | bytes 786440 | tf_op jit(solution)/shard_map/ppermute | solution.py:443
  45.6 1.2 collective-permute-start.5
  45.6 39.1 %collective-permute-start.10 = (bf16[384,1024]{1,0:T(8,128)(2,1)S(1)}, bf16[384,1024]{1,0:T(8,128)(2,1)S(1)}, u32[]{:S(2)}, u32[]{:S(2)}) collective-permute-start(bf16[384,1024]{1,0:T(8,128)(2,1)S(1)} %collective-permute-done.one_ref.refs_0_), channel_id=1, source_target_pairs={{0,2},{2,0},{4,6},{6,4},{8,10},{10,8},{12,14},{14,12},{1,3},{3,1},... | collective-permute-start | bytes 2359304 | tf_op jit(solution)/shard_map/ppermute | solution.py:447
  46.8 27.3 %collective-permute-start.16 = (bf16[256,1024]{1,0:T(8,128)(2,1)}, bf16[256,1024]{1,0:T(8,128)(2,1)S(1)}, u32[]{:S(2)}, u32[]{:S(2)}) collective-permute-start(bf16[256,1024]{1,0:T(8,128)(2,1)} %get-tuple-element.22), channel_id=1, source_target_pairs={{0,12},{2,14},{4,8},{6,10},{8,4},{10,6},{12,0},{14,2},{1,13},{3,15... | collective-permute-start | bytes 1572872 | tf_op jit(solution)/shard_map/ppermute | solution.py:443
  49.5 35.7 %copy-start = (f32[1,128,4,256]{3,2,1,0:T(4,128)S(1)}, f32[1,128,4,256]{3,2,1,0:T(4,128)}, u32[]{:S(2)}) copy-start(f32[1,128,4,256]{3,2,1,0:T(4,128)} %orbitals_ref.3) | copy-start | bytes 1572868
  49.5 57.5 %copy-start.3 = (bf16[2,128,1024]{2,1,0:T(8,128)(2,1)S(1)}, bf16[2,128,1024]{2,1,0:T(8,128)(2,1)}, u32[]{:S(2)}) copy-start(bf16[2,128,1024]{2,1,0:T(8,128)(2,1)} %get-tuple-element.19.own) | copy-start | bytes 1572868
  49.5 26.0 %collective-permute-start.9 = (bf16[256,1024]{1,0:T(8,128)(2,1)S(1)}, bf16[256,1024]{1,0:T(8,128)(2,1)S(1)}, u32[]{:S(2)}, u32[]{:S(2)}) collective-permute-start(bf16[256,1024]{1,0:T(8,128)(2,1)S(1)} %slice.13), channel_id=1, source_target_pairs={{0,1},{1,0},{2,3},{3,2},{4,5},{5,4},{6,7},{7,6},{8,9},{9,8},{10,11... | collective-permute-start | bytes 1572872 | tf_op jit(solution)/shard_map/ppermute | solution.py:451
  54.9 1.2 collective-permute-start.4
  56.7 17.4 %collective-permute-start.7 = (f32[16,128]{1,0:T(8,128)S(1)}, f32[16,128]{1,0:T(8,128)S(1)}, u32[]{:S(2)}, u32[]{:S(2)}) collective-permute-start(f32[16,128]{1,0:T(8,128)S(1)} %get-tuple-element.18.field_here), channel_id=1, source_target_pairs={{0,8},{2,10},{4,12},{6,14},{8,0},{10,2},{12,4},{14,6},{1,9},{3,11}... | collective-permute-start | bytes 24584 | tf_op jit(solution)/shard_map/ppermute | solution.py:443
  69.8 14.9 %collective-permute-start.12 = (bf16[256,1024]{1,0:T(8,128)(2,1)S(1)}, bf16[256,1024]{1,0:T(8,128)(2,1)S(1)}, u32[]{:S(2)}, u32[]{:S(2)}) collective-permute-start(bf16[256,1024]{1,0:T(8,128)(2,1)S(1)} %slice.14), channel_id=1, source_target_pairs={{0,1},{1,0},{2,3},{3,2},{4,5},{5,4},{6,7},{7,6},{8,9},{9,8},{10,11... | collective-permute-start | bytes 1572872 | tf_op jit(solution)/shard_map/ppermute | solution.py:451
  74.1 11.6 %collective-permute-start.13 = (bf16[384,1024]{1,0:T(8,128)(2,1)S(1)}, bf16[384,1024]{1,0:T(8,128)(2,1)S(1)}, u32[]{:S(2)}, u32[]{:S(2)}) collective-permute-start(bf16[384,1024]{1,0:T(8,128)(2,1)S(1)} %collective-permute-done.1.two_ref.refs_4_), channel_id=1, source_target_pairs={{0,2},{2,0},{4,6},{6,4},{8,10},{10,8},{12,14},{14,12},{1,3},{3,1},... | collective-permute-start | bytes 2359304 | tf_op jit(solution)/shard_map/ppermute | solution.py:447
  74.1 20.7 %collective-permute-start.17 = (bf16[256,1024]{1,0:T(8,128)(2,1)S(1)}, bf16[256,1024]{1,0:T(8,128)(2,1)S(1)}, u32[]{:S(2)}, u32[]{:S(2)}) collective-permute-start(bf16[256,1024]{1,0:T(8,128)(2,1)S(1)} %collective-permute-done.16.refs_0_), channel_id=1, source_target_pairs={{0,1},{1,0},{2,3},{3,2},{4,5},{5,4},{6,7},{7,6},{8,9},{9,8},{10,11... | collective-permute-start | bytes 1572872 | tf_op jit(solution)/shard_map/ppermute | solution.py:451
  75.6 19.2 %collective-permute-start.11 = (bf16[256,1024]{1,0:T(8,128)(2,1)S(1)}, bf16[256,1024]{1,0:T(8,128)(2,1)S(1)}, u32[]{:S(2)}, u32[]{:S(2)}) collective-permute-start(bf16[256,1024]{1,0:T(8,128)(2,1)S(1)} %collective-permute-done.9.refs_1_), channel_id=1, source_target_pairs={{0,2},{2,0},{4,6},{6,4},{8,10},{10,8},{12,14},{14,12},{1,3},{3,1},... | collective-permute-start | bytes 1572872 | tf_op jit(solution)/shard_map/ppermute | solution.py:447
  84.7 12.6 %collective-permute-start.14 = (bf16[256,1024]{1,0:T(8,128)(2,1)S(1)}, bf16[256,1024]{1,0:T(8,128)(2,1)S(1)}, u32[]{:S(2)}, u32[]{:S(2)}) collective-permute-start(bf16[256,1024]{1,0:T(8,128)(2,1)S(1)} %collective-permute-done.12.refs_5_), channel_id=1, source_target_pairs={{0,2},{2,0},{4,6},{6,4},{8,10},{10,8},{12,14},{14,12},{1,3},{3,1},... | collective-permute-start | bytes 1572872 | tf_op jit(solution)/shard_map/ppermute | solution.py:447
  84.7 17.1 %collective-permute-start.18 = (bf16[256,1024]{1,0:T(8,128)(2,1)S(1)}, bf16[256,1024]{1,0:T(8,128)(2,1)S(1)}, u32[]{:S(2)}, u32[]{:S(2)}) collective-permute-start(bf16[256,1024]{1,0:T(8,128)(2,1)S(1)} %collective-permute-done.16.refs_0_), channel_id=1, source_target_pairs={{0,2},{2,0},{4,6},{6,4},{8,10},{10,8},{12,14},{14,12},{1,3},{3,1},... | collective-permute-start | bytes 1572872 | tf_op jit(solution)/shard_map/ppermute | solution.py:447
  85.7 14.9 %collective-permute-start.21 = (bf16[4,128,256]{2,1,0:T(8,128)(2,1)S(1)}, bf16[4,128,256]{2,1,0:T(8,128)(2,1)S(1)}, u32[]{:S(2)}, u32[]{:S(2)}) collective-permute-start(bf16[4,128,256]{2,1,0:T(8,128)(2,1)S(1)} %walker_major.1.refs_0_), channel_id=1, source_target_pairs={{0,8},{2,10},{4,12},{6,14},{8,0},{10,2},{12,4},{14,6},{1,9},{3,11}... | collective-permute-start | bytes 786440 | tf_op jit(solution)/shard_map/ppermute | solution.py:443
  94.8 15.6 %collective-permute-start.19 = (bf16[256,1024]{1,0:T(8,128)(2,1)S(1)}, bf16[256,1024]{1,0:T(8,128)(2,1)S(1)}, u32[]{:S(2)}, u32[]{:S(2)}) collective-permute-start(bf16[256,1024]{1,0:T(8,128)(2,1)S(1)} %collective-permute-done.17.refs_1_), channel_id=1, source_target_pairs={{0,2},{2,0},{4,6},{6,4},{8,10},{10,8},{12,14},{14,12},{1,3},{3,1},... | collective-permute-start | bytes 1572872 | tf_op jit(solution)/shard_map/ppermute | solution.py:447
  94.8 11.8 %collective-permute-start.20 = (bf16[4,128,256]{2,1,0:T(8,128)(2,1)S(1)}, bf16[4,128,256]{2,1,0:T(8,128)(2,1)S(1)}, u32[]{:S(2)}, u32[]{:S(2)}) collective-permute-start(bf16[4,128,256]{2,1,0:T(8,128)(2,1)S(1)} %walker_major.1.refs_0_), channel_id=1, source_target_pairs={{0,4},{2,6},{4,0},{6,2},{8,12},{10,14},{12,8},{14,10},{1,5},{3,7},... | collective-permute-start | bytes 786440 | tf_op jit(solution)/shard_map/ppermute | solution.py:443
  97.3 9.2 %collective-permute-start.6 = (f32[16,128]{1,0:T(8,128)S(1)}, f32[16,128]{1,0:T(8,128)S(1)}, u32[]{:S(2)}, u32[]{:S(2)}) collective-permute-start(f32[16,128]{1,0:T(8,128)S(1)} %get-tuple-element.18.field_here), channel_id=1, source_target_pairs={{0,4},{2,6},{4,0},{6,2},{8,12},{10,14},{12,8},{14,10},{1,5},{3,7},... | collective-permute-start | bytes 24584 | tf_op jit(solution)/shard_map/ppermute | solution.py:443
  100.6 6.4 %collective-permute-start.15 = (f32[16,128]{1,0:T(8,128)S(1)}, f32[16,128]{1,0:T(8,128)S(1)}, u32[]{:S(2)}, u32[]{:S(2)}) collective-permute-start(f32[16,128]{1,0:T(8,128)S(1)} %get-tuple-element.18.field_here), channel_id=1, source_target_pairs={{0,12},{2,14},{4,8},{6,10},{8,4},{10,6},{12,0},{14,2},{1,13},{3,15... | collective-permute-start | bytes 24584 | tf_op jit(solution)/shard_map/ppermute | solution.py:443
  101.8 10.2 %collective-permute-start.22 = (bf16[4,128,256]{2,1,0:T(8,128)(2,1)S(1)}, bf16[4,128,256]{2,1,0:T(8,128)(2,1)S(1)}, u32[]{:S(2)}, u32[]{:S(2)}) collective-permute-start(bf16[4,128,256]{2,1,0:T(8,128)(2,1)S(1)} %walker_major.1.refs_0_), channel_id=1, source_target_pairs={{0,2},{2,0},{4,6},{6,4},{8,10},{10,8},{12,14},{14,12},{1,3},{3,1},... | collective-permute-start | bytes 786440 | tf_op jit(solution)/shard_map/ppermute | solution.py:447
  106.5 5.5 %collective-permute-start.24 = (bf16[4,128,256]{2,1,0:T(8,128)(2,1)S(1)}, bf16[4,128,256]{2,1,0:T(8,128)(2,1)S(1)}, u32[]{:S(2)}, u32[]{:S(2)}) collective-permute-start(bf16[4,128,256]{2,1,0:T(8,128)(2,1)S(1)} %collective-permute-done.21.refs_2_), channel_id=1, source_target_pairs={{0,2},{2,0},{4,6},{6,4},{8,10},{10,8},{12,14},{14,12},{1,3},{3,1},... | collective-permute-start | bytes 786440 | tf_op jit(solution)/shard_map/ppermute | solution.py:447
  106.6 5.4 %collective-permute-start.23 = (bf16[4,128,256]{2,1,0:T(8,128)(2,1)S(1)}, bf16[4,128,256]{2,1,0:T(8,128)(2,1)S(1)}, u32[]{:S(2)}, u32[]{:S(2)}) collective-permute-start(bf16[4,128,256]{2,1,0:T(8,128)(2,1)S(1)} %collective-permute-done.20.refs_1_), channel_id=1, source_target_pairs={{0,2},{2,0},{4,6},{6,4},{8,10},{10,8},{12,14},{14,12},{1,3},{3,1},... | collective-permute-start | bytes 786440 | tf_op jit(solution)/shard_map/ppermute | solution.py:447
  107.0 8.3 %collective-permute-start.25 = (bf16[4,128,256]{2,1,0:T(8,128)(2,1)S(1)}, bf16[4,128,256]{2,1,0:T(8,128)(2,1)S(1)}, u32[]{:S(2)}, u32[]{:S(2)}) collective-permute-start(bf16[4,128,256]{2,1,0:T(8,128)(2,1)S(1)} %collective-permute-done.21.refs_2_), channel_id=1, source_target_pairs={{0,4},{2,6},{4,0},{6,2},{8,12},{10,14},{12,8},{14,10},{1,5},{3,7},... | collective-permute-start | bytes 786440 | tf_op jit(solution)/shard_map/ppermute | solution.py:443
  115.3 1.5 %collective-permute-start.26 = (bf16[4,128,256]{2,1,0:T(8,128)(2,1)S(1)}, bf16[4,128,256]{2,1,0:T(8,128)(2,1)S(1)}, u32[]{:S(2)}, u32[]{:S(2)}) collective-permute-start(bf16[4,128,256]{2,1,0:T(8,128)(2,1)S(1)} %collective-permute-done.25.mine), channel_id=1, source_target_pairs={{0,2},{2,0},{4,6},{6,4},{8,10},{10,8},{12,14},{14,12},{1,3},{3,1},... | collective-permute-start | bytes 786440 | tf_op jit(solution)/shard_map/ppermute | solution.py:447
  117.2 12.4 %collective-permute-start.27 = (bf16[4,128,256]{2,1,0:T(8,128)(2,1)S(1)}, bf16[4,128,256]{2,1,0:T(8,128)(2,1)S(1)}, u32[]{:S(2)}, u32[]{:S(2)}) collective-permute-start(bf16[4,128,256]{2,1,0:T(8,128)(2,1)S(1)} %get-tuple-element.27.refs_0_), channel_id=1, source_target_pairs={{0,4},{2,6},{4,0},{6,2},{8,12},{10,14},{12,8},{14,10},{1,5},{3,7},... | collective-permute-start | bytes 786440 | tf_op jit(solution)/shard_map/ppermute | solution.py:443
  117.6 14.7 %collective-permute-start.28 = (bf16[4,128,256]{2,1,0:T(8,128)(2,1)S(1)}, bf16[4,128,256]{2,1,0:T(8,128)(2,1)S(1)}, u32[]{:S(2)}, u32[]{:S(2)}) collective-permute-start(bf16[4,128,256]{2,1,0:T(8,128)(2,1)S(1)} %get-tuple-element.27.refs_0_), channel_id=1, source_target_pairs={{0,8},{2,10},{4,12},{6,14},{8,0},{10,2},{12,4},{14,6},{1,9},{3,11}... | collective-permute-start | bytes 786440 | tf_op jit(solution)/shard_map/ppermute | solution.py:443
  118.9 13.4 %collective-permute-start.29 = (bf16[4,128,256]{2,1,0:T(8,128)(2,1)S(1)}, bf16[4,128,256]{2,1,0:T(8,128)(2,1)S(1)}, u32[]{:S(2)}, u32[]{:S(2)}) collective-permute-start(bf16[4,128,256]{2,1,0:T(8,128)(2,1)S(1)} %get-tuple-element.27.refs_0_), channel_id=1, source_target_pairs={{0,2},{2,0},{4,6},{6,4},{8,10},{10,8},{12,14},{14,12},{1,3},{3,1},... | collective-permute-start | bytes 786440 | tf_op jit(solution)/shard_map/ppermute | solution.py:447
  129.6 2.7 %collective-permute-start.30 = (bf16[4,128,256]{2,1,0:T(8,128)(2,1)S(1)}, bf16[4,128,256]{2,1,0:T(8,128)(2,1)S(1)}, u32[]{:S(2)}, u32[]{:S(2)}) collective-permute-start(bf16[4,128,256]{2,1,0:T(8,128)(2,1)S(1)} %collective-permute-done.27.refs_1_), channel_id=1, source_target_pairs={{0,2},{2,0},{4,6},{6,4},{8,10},{10,8},{12,14},{14,12},{1,3},{3,1},... | collective-permute-start | bytes 786440 | tf_op jit(solution)/shard_map/ppermute | solution.py:447
  132.3 1.5 %collective-permute-start.31 = (bf16[4,128,256]{2,1,0:T(8,128)(2,1)S(1)}, bf16[4,128,256]{2,1,0:T(8,128)(2,1)S(1)}, u32[]{:S(2)}, u32[]{:S(2)}) collective-permute-start(bf16[4,128,256]{2,1,0:T(8,128)(2,1)S(1)} %collective-permute-done.28.refs_2_), channel_id=1, source_target_pairs={{0,2},{2,0},{4,6},{6,4},{8,10},{10,8},{12,14},{14,12},{1,3},{3,1},... | collective-permute-start | bytes 786440 | tf_op jit(solution)/shard_map/ppermute | solution.py:447
  132.3 8.7 %collective-permute-start.32 = (bf16[4,128,256]{2,1,0:T(8,128)(2,1)S(1)}, bf16[4,128,256]{2,1,0:T(8,128)(2,1)S(1)}, u32[]{:S(2)}, u32[]{:S(2)}) collective-permute-start(bf16[4,128,256]{2,1,0:T(8,128)(2,1)S(1)} %collective-permute-done.28.refs_2_), channel_id=1, source_target_pairs={{0,4},{2,6},{4,0},{6,2},{8,12},{10,14},{12,8},{14,10},{1,5},{3,7},... | collective-permute-start | bytes 786440 | tf_op jit(solution)/shard_map/ppermute | solution.py:443
  141.0 1.5 %collective-permute-start.33 = (bf16[4,128,256]{2,1,0:T(8,128)(2,1)S(1)}, bf16[4,128,256]{2,1,0:T(8,128)(2,1)S(1)}, u32[]{:S(2)}, u32[]{:S(2)}) collective-permute-start(bf16[4,128,256]{2,1,0:T(8,128)(2,1)S(1)} %collective-permute-done.32.mine), channel_id=1, source_target_pairs={{0,2},{2,0},{4,6},{6,4},{8,10},{10,8},{12,14},{14,12},{1,3},{3,1},... | collective-permute-start | bytes 786440 | tf_op jit(solution)/shard_map/ppermute | solution.py:447

commit v10 on v9

--- a/solution.py
+++ b/solution.py
@@ -462,20 +462,32 @@
     one, two, three, own, own_cross = packed(full_chol, green_blocks)
     two, one = to_chip(two, 2), to_chip(one, 1)
     own_theirs = to_core(own_cross)
-    three = to_chip(after(three, one, half_theirs, own_theirs, constants_theirs), 3)
+
+    one_theirs = to_core(after(one, half_theirs, own_theirs, constants_theirs))
+    one_x = across(one[rows:])
+    three = to_chip(after(three, one_theirs), 3)
+    two_x = across(two[rows:])
     green_three = to_chip(two[:rows], 1)
-
-    one_x, two_x, three_x = across(one[rows:]), across(two[rows:]), across(three)
-    messages = {1: (one, one_x), 2: (two, two_x), 3: (three, three_x)}
-    blocks = {step: [*both, *[to_core(each) for each in both]] for step, both in messages.items()}
+    two_theirs = to_core(two)
 
     bias = chip_bias((green_blocks, one, two, green_three), half_chol, half_theirs)
-    bias_shift, field = chip_field(bias, to_core(bias), constants, constants_theirs, vectors)
-    field_one, field_two, field_three = (to_chip(field, step) for step in (1, 2, 3))
-
-    start = after(walker_major(orbitals), field_two, blocks[1][2], blocks[2][2])
+    bias_theirs = to_core(after(bias, two_theirs))
+    bias_shift, field = chip_field(bias, bias_theirs, constants, constants_theirs, vectors)
+    one_x_theirs = to_core(after(one_x, field))
+
+    start = after(walker_major(orbitals), one_x_theirs)
     start_two, start_one = to_chip(start, 2), to_chip(start, 1)
-    start_three = to_chip(after(start_two, blocks[1][3], blocks[2][3], blocks[3][2]), 1)
+    two_x_theirs = to_core(two_x)
+    three_x, three_theirs = across(three), to_core(three)
+    late_field = after(field, two_x_theirs, three_theirs)
+    field_one, field_two, field_three = (to_chip(late_field, step) for step in (1, 2, 3))
+    start_three = to_chip(after(start_two, field_one, field_two, field_three), 1)
+    three_x_theirs = to_core(three_x)
+    blocks = {
+        1: (one, one_x, one_theirs, one_x_theirs),
+        2: (two, two_x, two_theirs, two_x_theirs),
+        3: (three, three_x, three_theirs, three_x_theirs),
+    }
 
     summed = early_operator(
         walkers,

time: 144 us -> 132 us (0.917)
  starting transfers between devices: 34.4 us -> 22.3 us
    ppermute x13, starting transfers between devices: 27.4 us -> 17.6 us  [to_chip(): return lax.ppermute(value, 'chol', [(i, i ^ 2 * step) for i in range(8)])]
    ppermute x3, waiting for transfers between devices: 17.9 us -> 10.4 us  [across(): return lax.ppermute(value, 'walk', [(0, 1), (1, 0)])]
    ppermute x13, waiting for transfers between devices: 68 us -> 75 us  [to_chip(): return lax.ppermute(value, 'chol', [(i, i ^ 2 * step) for i in range(8)])]
    ppermute x3, starting transfers between devices: 4.61 us -> 2.69 us  [across(): return lax.ppermute(value, 'walk', [(0, 1), (1, 0)])]
  transfers between devices with their start and end apart: 34 -> 34, of which waited for: 16 -> 16; matrix products, arithmetic and copies ran while one was open for 0% -> 0% of each run, Pallas kernels for 10% -> 11%
where the time goes in v10:
time: 132 us
  waiting for transfers between devices  92.2 us (70%)
  starting transfers between devices  22.3 us (17%)
  Pallas kernels  15.7 us (12%)
    ppermute x13, waiting for transfers between devices, to_chip(): return lax.ppermute(value, 'chol', [(i, i ^ 2 * step) for i in range(8)])  75 us
    ppermute x13, starting transfers between devices, to_chip(): return lax.ppermute(value, 'chol', [(i, i ^ 2 * step) for i in range(8)])  17.6 us
    ppermute x3, waiting for transfers between devices, across(): return lax.ppermute(value, 'walk', [(0, 1), (1, 0)])  10.4 us
    ppermute x18, waiting for transfers between devices, to_core(): return lax.ppermute(value, 'chol', [(i, i ^ 1) for i in range(8)])  6.81 us
    pallas_call x1, Pallas kernels, packed(): pl.pallas_call(pack_kernel, out_shape=[jax.ShapeDtypeStruct(shape, narrow...  4.35 us
    pallas_call x1, Pallas kernels, early_operator(): pl.pallas_call(functools.partial(early_kernel, walkers), out_shape=jax.Sh...  3.34 us
    ppermute x3, starting transfers between devices, across(): return lax.ppermute(value, 'walk', [(0, 1), (1, 0)])  2.69 us
  transfers between devices with their start and end apart: 34, of which 16 were waited for; matrix products, arithmetic and copies ran while one was open for 0% of the time, Pallas kernels for 11%

profile of v10, /device:TPU:0, one launch (start us, length us, event | category | flops | bytes accessed | tf_op | source)
XLA Modules:
  0.0 131.5 jit_solution(63650414426647582)
XLA Ops:
  0.7 0.5 collective-permute-start.3
  1.2 4.3 %packed.1 = (bf16[384,1024]{1,0:T(8,128)(2,1)}, bf16[384,1024]{1,0:T(8,128)(2,1)}, bf16[256,1024]{1,0:T(8,128)(2,1)}, bf16[2,128,1024]{2,1,0:T(8,128)(2,1)}, bf16[2,128,1024]{2,1,0:T(8,128)(2,1)}) custom-call(bf16[2,1024,1024]{2,1,0:T(8,128)(2,1)} %full_ref.1, bf16[4,128,256]{2,1,0:T(8,128)(2,1)} %here_ref.1), custom_call_target="tpu_custom_call" | custom-call | tf_op jit(solution)/shard_map/packed/pallas_call | solution.py:114
  5.5 2.7 %collective-permute-start = (bf16[384,1024]{1,0:T(8,128)(2,1)}, bf16[384,1024]{1,0:T(8,128)(2,1)S(1)}, u32[]{:S(2)}, u32[]{:S(2)}) collective-permute-start(bf16[384,1024]{1,0:T(8,128)(2,1)} %get-tuple-element.20), channel_id=1, source_target_pairs={{0,4},{2,6},{4,0},{6,2},{8,12},{10,14},{12,8},{14,10},{1,5},{3,7},... | collective-permute-start | bytes 2359304 | tf_op jit(solution)/shard_map/ppermute | solution.py:443
  8.2 0.2 collective-permute-start.9
  8.4 2.6 %collective-permute-start.1 = (bf16[384,1024]{1,0:T(8,128)(2,1)}, bf16[384,1024]{1,0:T(8,128)(2,1)S(1)}, u32[]{:S(2)}, u32[]{:S(2)}) collective-permute-start(bf16[384,1024]{1,0:T(8,128)(2,1)} %get-tuple-element.21), channel_id=1, source_target_pairs={{0,8},{2,10},{4,12},{6,14},{8,0},{10,2},{12,4},{14,6},{1,9},{3,11}... | collective-permute-start | bytes 2359304 | tf_op jit(solution)/shard_map/ppermute | solution.py:443
  11.1 0.1 reshape.12
  11.2 0.1 reshape.11
  11.4 1.1 collective-permute-done.6.noise_there_ref
  12.6 30.5 %collective-permute-done.one_ref.refs_0_ = bf16[384,1024]{1,0:T(8,128)(2,1)S(1)} collective-permute-done((bf16[384,1024]{1,0:T(8,128)(2,1)}, bf16[384,1024]{1,0:T(8,128)(2,1)S(1)}, u32[]{:S(2)}, u32[]{:S(2)}) %collective-permute-start) | collective-permute-done | bytes 786464 | tf_op jit(solution)/shard_map/ppermute | solution.py:443
  43.1 3.1 %collective-permute-done.1.two_ref.refs_4_ = bf16[384,1024]{1,0:T(8,128)(2,1)S(1)} collective-permute-done((bf16[384,1024]{1,0:T(8,128)(2,1)}, bf16[384,1024]{1,0:T(8,128)(2,1)S(1)}, u32[]{:S(2)}, u32[]{:S(2)}) %collective-permute-start.1) | collective-permute-done | bytes 786464 | tf_op jit(solution)/shard_map/ppermute | solution.py:443
  46.2 1.6 %collective-permute-start.15 = (bf16[256,1024]{1,0:T(8,128)(2,1)S(1)}, bf16[256,1024]{1,0:T(8,128)(2,1)S(1)}, u32[]{:S(2)}, u32[]{:S(2)}) collective-permute-start(bf16[256,1024]{1,0:T(8,128)(2,1)S(1)} %slice.14), channel_id=1, source_target_pairs={{0,1},{1,0},{2,3},{3,2},{4,5},{5,4},{6,7},{7,6},{8,9},{9,8},{10,11... | collective-permute-start | bytes 1572872 | tf_op jit(solution)/shard_map/ppermute | solution.py:451
  47.8 2.5 %collective-permute-start.11 = (bf16[256,1024]{1,0:T(8,128)(2,1)}, bf16[256,1024]{1,0:T(8,128)(2,1)S(1)}, u32[]{:S(2)}, u32[]{:S(2)}) collective-permute-start(bf16[256,1024]{1,0:T(8,128)(2,1)} %get-tuple-element.27), channel_id=1, source_target_pairs={{0,12},{2,14},{4,8},{6,10},{8,4},{10,6},{12,0},{14,2},{1,13},{3,15... | collective-permute-start | bytes 1572872 | tf_op jit(solution)/shard_map/ppermute | solution.py:443
  50.4 0.6 collective-permute-start.7
  51.0 18.5 %collective-permute-done.2.three_ref = bf16[128,1024]{1,0:T(8,128)(2,1)S(1)} collective-permute-done((bf16[128,1024]{1,0:T(8,128)(2,1)S(1)}, bf16[128,1024]{1,0:T(8,128)(2,1)S(1)}, u32[]{:S(2)}, u32[]{:S(2)}) %collective-permute-start.2) | collective-permute-done | bytes 262176 | tf_op jit(solution)/shard_map/ppermute | solution.py:443
  69.6 2.2 %chip_bias.1.mine_ref = f32[16,128]{1,0:T(8,128)S(1)} custom-call(bf16[4,128,256]{2,1,0:T(8,128)(2,1)S(1)} %copy-done.1, bf16[384,1024]{1,0:T(8,128)(2,1)S(1)} %collective-permute-done.one_ref.refs_0_, bf16[384,1024]{1,0:T(8,128)(2,1)S(1)} %collective-permute-done.1.two_ref.refs_4_, bf16[128,1024]{1,0:T(8,128)(2,1)S(1)} %collective-permute-done.2.three_ref, ...), custom_call_target="tpu_custom_call" | custom-call | tf_op jit(solution)/shard_map/chip_bias/pallas_call | solution.py:181
  71.8 0.1 collective-permute-start.5
  71.9 1.2 collective-permute-done.5.theirs_ref
  73.0 0.6 chip_field.1
  73.6 0.2 collective-permute-start.16
  73.8 0.5 collective-permute-start.18
  74.4 0.4 collective-permute-start.12
  74.8 0.5 walker_major.1.refs_0_
  75.4 0.2 collective-permute-done.16.refs_3_
  75.5 0.6 collective-permute-start.20
  76.2 1.5 %collective-permute-start.21 = (bf16[4,128,256]{2,1,0:T(8,128)(2,1)S(1)}, bf16[4,128,256]{2,1,0:T(8,128)(2,1)S(1)}, u32[]{:S(2)}, u32[]{:S(2)}) collective-permute-start(bf16[4,128,256]{2,1,0:T(8,128)(2,1)S(1)} %walker_major.1.refs_0_), channel_id=1, source_target_pairs={{0,8},{2,10},{4,12},{6,14},{8,0},{10,2},{12,4},{14,6},{1,9},{3,11}... | collective-permute-start | bytes 786440 | tf_op jit(solution)/shard_map/ppermute | solution.py:443
  77.6 10.3 %collective-permute-done.18.refs_1_ = bf16[256,1024]{1,0:T(8,128)(2,1)S(1)} collective-permute-done((bf16[256,1024]{1,0:T(8,128)(2,1)S(1)}, bf16[256,1024]{1,0:T(8,128)(2,1)S(1)}, u32[]{:S(2)}, u32[]{:S(2)}) %collective-permute-start.18) | collective-permute-done | bytes 524320 | tf_op jit(solution)/shard_map/ppermute | solution.py:451
  88.0 0.7 collective-permute-start.13
  88.7 1.5 %collective-permute-start.14 = (f32[16,128]{1,0:T(8,128)S(1)}, f32[16,128]{1,0:T(8,128)S(1)}, u32[]{:S(2)}, u32[]{:S(2)}) collective-permute-start(f32[16,128]{1,0:T(8,128)S(1)} %get-tuple-element.28.field_here), channel_id=1, source_target_pairs={{0,8},{2,10},{4,12},{6,14},{8,0},{10,2},{12,4},{14,6},{1,9},{3,11}... | collective-permute-start | bytes 24584 | tf_op jit(solution)/shard_map/ppermute | solution.py:443
  90.1 2.3 %collective-permute-start.17 = (f32[16,128]{1,0:T(8,128)S(1)}, f32[16,128]{1,0:T(8,128)S(1)}, u32[]{:S(2)}, u32[]{:S(2)}) collective-permute-start(f32[16,128]{1,0:T(8,128)S(1)} %get-tuple-element.28.field_here), channel_id=1, source_target_pairs={{0,12},{2,14},{4,8},{6,10},{8,4},{10,6},{12,0},{14,2},{1,13},{3,15... | collective-permute-start | bytes 24584 | tf_op jit(solution)/shard_map/ppermute | solution.py:443
  92.5 0.5 collective-permute-start.23
  93.0 0.3 collective-permute-done.14.field_two
  93.2 2.4 %collective-permute-done.17.field_ref = f32[16,128]{1,0:T(8,128)S(1)} collective-permute-done((f32[16,128]{1,0:T(8,128)S(1)}, f32[16,128]{1,0:T(8,128)S(1)}, u32[]{:S(2)}, u32[]{:S(2)}) %collective-permute-start.17) | collective-permute-done | bytes 8224 | tf_op jit(solution)/shard_map/ppermute | solution.py:443
  95.6 3.3 %early_operator.1.summed_ref = f32[4,128,1024]{2,1,0:T(8,128)S(1)} custom-call(f32[16,128]{1,0:T(8,128)S(1)} %get-tuple-element.28.field_here, f32[16,128]{1,0:T(8,128)S(1)} %collective-permute-done.13.field_one, f32[16,128]{1,0:T(8,128)S(1)} %collective-permute-done.14.field_two, bf16[2,128,1024]{2,1,0:T(8,128)(2,1)S(1)} %copy-done.3, ...), custom_call_target="tpu_custom_call" | custom-call | tf_op jit(solution)/shard_map/early_operator/pallas_call | solution.py:291
  99.0 1.6 %split_operator.1.operator_ref = bf16[4,256,1024]{2,1,0:T(8,128)(2,1)S(1)} custom-call(f32[4,128,1024]{2,1,0:T(8,128)S(1)} %early_operator.1.summed_ref, f32[16,128]{1,0:T(8,128)S(1)} %collective-permute-done.17.field_ref, bf16[256,1024]{1,0:T(8,128)(2,1)S(1)} %collective-permute-done.11.refs_0_, bf16[256,1024]{1,0:T(8,128)(2,1)S(1)} %collective-permute-done.18.refs_1_, ...), custom_call_target="tpu_custom_call" | custom-call | tf_op jit(solution)/shard_map/split_operator/pallas_call | solution.py:324
  100.6 0.7 near_application.1.partial_ref
  101.3 1.2 collective-permute-done.25.mine
  102.5 1.5 %collective-permute-done.26.theirs = bf16[4,128,256]{2,1,0:T(8,128)(2,1)S(1)} collective-permute-done((bf16[4,128,256]{2,1,0:T(8,128)(2,1)S(1)}, bf16[4,128,256]{2,1,0:T(8,128)(2,1)S(1)}, u32[]{:S(2)}, u32[]{:S(2)}) %collective-permute-start.26) | collective-permute-done | bytes 262176 | tf_op jit(solution)/shard_map/ppermute | solution.py:447
  104.1 0.4 first_application.1
  104.4 0.9 collective-permute-start.27
  105.4 2.0 %collective-permute-start.28 = (bf16[4,128,256]{2,1,0:T(8,128)(2,1)S(1)}, bf16[4,128,256]{2,1,0:T(8,128)(2,1)S(1)}, u32[]{:S(2)}, u32[]{:S(2)}) collective-permute-start(bf16[4,128,256]{2,1,0:T(8,128)(2,1)S(1)} %get-tuple-element.35.refs_0_), channel_id=1, source_target_pairs={{0,8},{2,10},{4,12},{6,14},{8,0},{10,2},{12,4},{14,6},{1,9},{3,11}... | collective-permute-start | bytes 786440 | tf_op jit(solution)/shard_map/ppermute | solution.py:443
  107.4 10.8 %collective-permute-done.27.refs_1_ = bf16[4,128,256]{2,1,0:T(8,128)(2,1)S(1)} collective-permute-done((bf16[4,128,256]{2,1,0:T(8,128)(2,1)S(1)}, bf16[4,128,256]{2,1,0:T(8,128)(2,1)S(1)}, u32[]{:S(2)}, u32[]{:S(2)}) %collective-permute-start.27) | collective-permute-done | bytes 262176 | tf_op jit(solution)/shard_map/ppermute | solution.py:443
  118.2 1.8 %collective-permute-done.28.refs_2_ = bf16[4,128,256]{2,1,0:T(8,128)(2,1)S(1)} collective-permute-done((bf16[4,128,256]{2,1,0:T(8,128)(2,1)S(1)}, bf16[4,128,256]{2,1,0:T(8,128)(2,1)S(1)}, u32[]{:S(2)}, u32[]{:S(2)}) %collective-permute-start.28) | collective-permute-done | bytes 262176 | tf_op jit(solution)/shard_map/ppermute | solution.py:443
  120.0 0.3 collective-permute-start.32
  120.3 1.2 collective-permute-done.31.refs_5_
  121.5 0.8 base_application.1.base_ref
  122.3 6.4 %collective-permute-done.32.mine = bf16[4,128,256]{2,1,0:T(8,128)(2,1)S(1)} collective-permute-done((bf16[4,128,256]{2,1,0:T(8,128)(2,1)S(1)}, bf16[4,128,256]{2,1,0:T(8,128)(2,1)S(1)}, u32[]{:S(2)}, u32[]{:S(2)}) %collective-permute-start.32) | collective-permute-done | bytes 262176 | tf_op jit(solution)/shard_map/ppermute | solution.py:443
  128.7 1.5 %collective-permute-done.33.theirs = bf16[4,128,256]{2,1,0:T(8,128)(2,1)S(1)} collective-permute-done((bf16[4,128,256]{2,1,0:T(8,128)(2,1)S(1)}, bf16[4,128,256]{2,1,0:T(8,128)(2,1)S(1)}, u32[]{:S(2)}, u32[]{:S(2)}) %collective-permute-start.33) | collective-permute-done | bytes 262176 | tf_op jit(solution)/shard_map/ppermute | solution.py:447
  130.3 1.2 second_application.1
  (50 shorter events, 0.6 us)
Async XLA Ops:
  0.6 10.4 %copy-start.5 = (f32[2]{0:T(128)S(1)}, f32[2]{0:T(128)}, u32[]{:S(2)}) copy-start(f32[2]{0:T(128)} %param.9) | copy-start | bytes 28
  0.6 10.5 %copy-start.4 = (f32[4,2]{0,1:T(2,128)S(1)}, f32[4,2]{0,1:T(2,128)}, u32[]{:S(2)}) copy-start(f32[4,2]{0,1:T(2,128)} %param.10) | copy-start | bytes 100
  0.7 42.4 %collective-permute-start.3 = (bf16[2,1024,256]{2,1,0:T(8,128)(2,1)}, bf16[2,1024,256]{2,1,0:T(8,128)(2,1)}, u32[]{:S(2)}, u32[]{:S(2)}) collective-permute-start(bf16[2,1024,256]{2,1,0:T(8,128)(2,1)} %mine_ref.1), channel_id=1, source_target_pairs={{0,2},{2,0},{4,6},{6,4},{8,10},{10,8},{12,14},{14,12},{1,3},{3,1},... | collective-permute-start | bytes 3145736 | tf_op jit(solution)/shard_map/ppermute | solution.py:447
  5.5 64.0 %copy-start.1 = (bf16[4,128,256]{2,1,0:T(8,128)(2,1)S(1)}, bf16[4,128,256]{2,1,0:T(8,128)(2,1)}, u32[]{:S(2)}) copy-start(bf16[4,128,256]{2,1,0:T(8,128)(2,1)} %here_ref.1) | copy-start | bytes 786436
  5.5 64.0 %copy-start.2 = (bf16[2,1024,256]{2,1,0:T(8,128)(2,1)S(1)}, bf16[2,1024,256]{2,1,0:T(8,128)(2,1)}, u32[]{:S(2)}) copy-start(bf16[2,1024,256]{2,1,0:T(8,128)(2,1)} %mine_ref.1) | copy-start | bytes 3145732
  5.5 37.5 %collective-permute-start = (bf16[384,1024]{1,0:T(8,128)(2,1)}, bf16[384,1024]{1,0:T(8,128)(2,1)S(1)}, u32[]{:S(2)}, u32[]{:S(2)}) collective-permute-start(bf16[384,1024]{1,0:T(8,128)(2,1)} %get-tuple-element.20), channel_id=1, source_target_pairs={{0,4},{2,6},{4,0},{6,2},{8,12},{10,14},{12,8},{14,10},{1,5},{3,7},... | collective-permute-start | bytes 2359304 | tf_op jit(solution)/shard_map/ppermute | solution.py:443
  8.2 4.4 %collective-permute-start.9 = (bf16[2,128,1024]{2,1,0:T(8,128)(2,1)}, bf16[2,128,1024]{2,1,0:T(8,128)(2,1)S(1)}, u32[]{:S(2)}, u32[]{:S(2)}) collective-permute-start(bf16[2,128,1024]{2,1,0:T(8,128)(2,1)} %get-tuple-element.25), channel_id=1, source_target_pairs={{0,2},{2,0},{4,6},{6,4},{8,10},{10,8},{12,14},{14,12},{1,3},{3,1},... | collective-permute-start | bytes 1572872 | tf_op jit(solution)/shard_map/ppermute | solution.py:447
  8.4 37.8 %collective-permute-start.1 = (bf16[384,1024]{1,0:T(8,128)(2,1)}, bf16[384,1024]{1,0:T(8,128)(2,1)S(1)}, u32[]{:S(2)}, u32[]{:S(2)}) collective-permute-start(bf16[384,1024]{1,0:T(8,128)(2,1)} %get-tuple-element.21), channel_id=1, source_target_pairs={{0,8},{2,10},{4,12},{6,14},{8,0},{10,2},{12,4},{14,6},{1,9},{3,11}... | collective-permute-start | bytes 2359304 | tf_op jit(solution)/shard_map/ppermute | solution.py:443
  11.4 1.2 collective-permute-start.6
  43.1 4.7 %collective-permute-start.10 = (bf16[384,1024]{1,0:T(8,128)(2,1)S(1)}, bf16[384,1024]{1,0:T(8,128)(2,1)S(1)}, u32[]{:S(2)}, u32[]{:S(2)}) collective-permute-start(bf16[384,1024]{1,0:T(8,128)(2,1)S(1)} %collective-permute-done.one_ref.refs_0_), channel_id=1, source_target_pairs={{0,2},{2,0},{4,6},{6,4},{8,10},{10,8},{12,14},{14,12},{1,3},{3,1},... | collective-permute-start | bytes 2359304 | tf_op jit(solution)/shard_map/ppermute | solution.py:447
  46.2 25.6 %collective-permute-start.4 = (bf16[384,1024]{1,0:T(8,128)(2,1)S(1)}, bf16[384,1024]{1,0:T(8,128)(2,1)S(1)}, u32[]{:S(2)}, u32[]{:S(2)}) collective-permute-start(bf16[384,1024]{1,0:T(8,128)(2,1)S(1)} %collective-permute-done.1.two_ref.refs_4_), channel_id=1, source_target_pairs={{0,2},{2,0},{4,6},{6,4},{8,10},{10,8},{12,14},{14,12},{1,3},{3,1},... | collective-permute-start | bytes 2359304 | tf_op jit(solution)/shard_map/ppermute | solution.py:447
  46.2 27.4 %collective-permute-start.15 = (bf16[256,1024]{1,0:T(8,128)(2,1)S(1)}, bf16[256,1024]{1,0:T(8,128)(2,1)S(1)}, u32[]{:S(2)}, u32[]{:S(2)}) collective-permute-start(bf16[256,1024]{1,0:T(8,128)(2,1)S(1)} %slice.14), channel_id=1, source_target_pairs={{0,1},{1,0},{2,3},{3,2},{4,5},{5,4},{6,7},{7,6},{8,9},{9,8},{10,11... | collective-permute-start | bytes 1572872 | tf_op jit(solution)/shard_map/ppermute | solution.py:451
  47.8 26.0 %collective-permute-start.11 = (bf16[256,1024]{1,0:T(8,128)(2,1)}, bf16[256,1024]{1,0:T(8,128)(2,1)S(1)}, u32[]{:S(2)}, u32[]{:S(2)}) collective-permute-start(bf16[256,1024]{1,0:T(8,128)(2,1)} %get-tuple-element.27), channel_id=1, source_target_pairs={{0,12},{2,14},{4,8},{6,10},{8,4},{10,6},{12,0},{14,2},{1,13},{3,15... | collective-permute-start | bytes 1572872 | tf_op jit(solution)/shard_map/ppermute | solution.py:443
  50.3 19.3 %collective-permute-start.2 = (bf16[128,1024]{1,0:T(8,128)(2,1)S(1)}, bf16[128,1024]{1,0:T(8,128)(2,1)S(1)}, u32[]{:S(2)}, u32[]{:S(2)}) collective-permute-start(bf16[128,1024]{1,0:T(8,128)(2,1)S(1)} %slice.12), channel_id=1, source_target_pairs={{0,4},{2,6},{4,0},{6,2},{8,12},{10,14},{12,8},{14,10},{1,5},{3,7},... | collective-permute-start | bytes 786440 | tf_op jit(solution)/shard_map/ppermute | solution.py:443
  50.4 24.4 %copy-start = (f32[1,128,4,256]{3,2,1,0:T(4,128)S(1)}, f32[1,128,4,256]{3,2,1,0:T(4,128)}, u32[]{:S(2)}) copy-start(f32[1,128,4,256]{3,2,1,0:T(4,128)} %orbitals_ref.3) | copy-start | bytes 1572868
  50.4 45.2 %copy-start.3 = (bf16[2,128,1024]{2,1,0:T(8,128)(2,1)S(1)}, bf16[2,128,1024]{2,1,0:T(8,128)(2,1)}, u32[]{:S(2)}) copy-start(bf16[2,128,1024]{2,1,0:T(8,128)(2,1)} %get-tuple-element.29.own) | copy-start | bytes 1572868
  50.4 23.9 %collective-permute-start.7 = (bf16[256,1024]{1,0:T(8,128)(2,1)S(1)}, bf16[256,1024]{1,0:T(8,128)(2,1)S(1)}, u32[]{:S(2)}, u32[]{:S(2)}) collective-permute-start(bf16[256,1024]{1,0:T(8,128)(2,1)S(1)} %slice.13), channel_id=1, source_target_pairs={{0,1},{1,0},{2,3},{3,2},{4,5},{5,4},{6,7},{7,6},{8,9},{9,8},{10,11... | collective-permute-start | bytes 1572872 | tf_op jit(solution)/shard_map/ppermute | solution.py:451
  71.8 1.2 collective-permute-start.5
  73.6 1.9 %collective-permute-start.16 = (bf16[256,1024]{1,0:T(8,128)(2,1)S(1)}, bf16[256,1024]{1,0:T(8,128)(2,1)S(1)}, u32[]{:S(2)}, u32[]{:S(2)}) collective-permute-start(bf16[256,1024]{1,0:T(8,128)(2,1)S(1)} %collective-permute-done.15.refs_1_), channel_id=1, source_target_pairs={{0,2},{2,0},{4,6},{6,4},{8,10},{10,8},{12,14},{14,12},{1,3},{3,1},... | collective-permute-start | bytes 1572872 | tf_op jit(solution)/shard_map/ppermute | solution.py:447
  73.8 14.2 %collective-permute-start.18 = (bf16[256,1024]{1,0:T(8,128)(2,1)S(1)}, bf16[256,1024]{1,0:T(8,128)(2,1)S(1)}, u32[]{:S(2)}, u32[]{:S(2)}) collective-permute-start(bf16[256,1024]{1,0:T(8,128)(2,1)S(1)} %collective-permute-done.11.refs_0_), channel_id=1, source_target_pairs={{0,1},{1,0},{2,3},{3,2},{4,5},{5,4},{6,7},{7,6},{8,9},{9,8},{10,11... | collective-permute-start | bytes 1572872 | tf_op jit(solution)/shard_map/ppermute | solution.py:451
  74.3 13.6 %collective-permute-start.8 = (bf16[256,1024]{1,0:T(8,128)(2,1)S(1)}, bf16[256,1024]{1,0:T(8,128)(2,1)S(1)}, u32[]{:S(2)}, u32[]{:S(2)}) collective-permute-start(bf16[256,1024]{1,0:T(8,128)(2,1)S(1)} %collective-permute-done.7.refs_5_), channel_id=1, source_target_pairs={{0,2},{2,0},{4,6},{6,4},{8,10},{10,8},{12,14},{14,12},{1,3},{3,1},... | collective-permute-start | bytes 1572872 | tf_op jit(solution)/shard_map/ppermute | solution.py:447
  74.4 13.6 %collective-permute-start.12 = (bf16[256,1024]{1,0:T(8,128)(2,1)S(1)}, bf16[256,1024]{1,0:T(8,128)(2,1)S(1)}, u32[]{:S(2)}, u32[]{:S(2)}) collective-permute-start(bf16[256,1024]{1,0:T(8,128)(2,1)S(1)} %collective-permute-done.11.refs_0_), channel_id=1, source_target_pairs={{0,2},{2,0},{4,6},{6,4},{8,10},{10,8},{12,14},{14,12},{1,3},{3,1},... | collective-permute-start | bytes 1572872 | tf_op jit(solution)/shard_map/ppermute | solution.py:447
  75.5 14.6 %collective-permute-start.20 = (bf16[4,128,256]{2,1,0:T(8,128)(2,1)S(1)}, bf16[4,128,256]{2,1,0:T(8,128)(2,1)S(1)}, u32[]{:S(2)}, u32[]{:S(2)}) collective-permute-start(bf16[4,128,256]{2,1,0:T(8,128)(2,1)S(1)} %walker_major.1.refs_0_), channel_id=1, source_target_pairs={{0,4},{2,6},{4,0},{6,2},{8,12},{10,14},{12,8},{14,10},{1,5},{3,7},... | collective-permute-start | bytes 786440 | tf_op jit(solution)/shard_map/ppermute | solution.py:443
  76.2 16.3 %collective-permute-start.21 = (bf16[4,128,256]{2,1,0:T(8,128)(2,1)S(1)}, bf16[4,128,256]{2,1,0:T(8,128)(2,1)S(1)}, u32[]{:S(2)}, u32[]{:S(2)}) collective-permute-start(bf16[4,128,256]{2,1,0:T(8,128)(2,1)S(1)} %walker_major.1.refs_0_), channel_id=1, source_target_pairs={{0,8},{2,10},{4,12},{6,14},{8,0},{10,2},{12,4},{14,6},{1,9},{3,11}... | collective-permute-start | bytes 786440 | tf_op jit(solution)/shard_map/ppermute | solution.py:443
  88.0 11.0 %collective-permute-start.19 = (bf16[256,1024]{1,0:T(8,128)(2,1)S(1)}, bf16[256,1024]{1,0:T(8,128)(2,1)S(1)}, u32[]{:S(2)}, u32[]{:S(2)}) collective-permute-start(bf16[256,1024]{1,0:T(8,128)(2,1)S(1)} %collective-permute-done.18.refs_1_), channel_id=1, source_target_pairs={{0,2},{2,0},{4,6},{6,4},{8,10},{10,8},{12,14},{14,12},{1,3},{3,1},... | collective-permute-start | bytes 1572872 | tf_op jit(solution)/shard_map/ppermute | solution.py:447
  88.0 4.5 %collective-permute-start.13 = (f32[16,128]{1,0:T(8,128)S(1)}, f32[16,128]{1,0:T(8,128)S(1)}, u32[]{:S(2)}, u32[]{:S(2)}) collective-permute-start(f32[16,128]{1,0:T(8,128)S(1)} %get-tuple-element.28.field_here), channel_id=1, source_target_pairs={{0,4},{2,6},{4,0},{6,2},{8,12},{10,14},{12,8},{14,10},{1,5},{3,7},... | collective-permute-start | bytes 24584 | tf_op jit(solution)/shard_map/ppermute | solution.py:443
  88.7 4.6 %collective-permute-start.14 = (f32[16,128]{1,0:T(8,128)S(1)}, f32[16,128]{1,0:T(8,128)S(1)}, u32[]{:S(2)}, u32[]{:S(2)}) collective-permute-start(f32[16,128]{1,0:T(8,128)S(1)} %get-tuple-element.28.field_here), channel_id=1, source_target_pairs={{0,8},{2,10},{4,12},{6,14},{8,0},{10,2},{12,4},{14,6},{1,9},{3,11}... | collective-permute-start | bytes 24584 | tf_op jit(solution)/shard_map/ppermute | solution.py:443
  90.1 5.4 %collective-permute-start.17 = (f32[16,128]{1,0:T(8,128)S(1)}, f32[16,128]{1,0:T(8,128)S(1)}, u32[]{:S(2)}, u32[]{:S(2)}) collective-permute-start(f32[16,128]{1,0:T(8,128)S(1)} %get-tuple-element.28.field_here), channel_id=1, source_target_pairs={{0,12},{2,14},{4,8},{6,10},{8,4},{10,6},{12,0},{14,2},{1,13},{3,15... | collective-permute-start | bytes 24584 | tf_op jit(solution)/shard_map/ppermute | solution.py:443
  92.4 8.1 %collective-permute-start.22 = (bf16[4,128,256]{2,1,0:T(8,128)(2,1)S(1)}, bf16[4,128,256]{2,1,0:T(8,128)(2,1)S(1)}, u32[]{:S(2)}, u32[]{:S(2)}) collective-permute-start(bf16[4,128,256]{2,1,0:T(8,128)(2,1)S(1)} %walker_major.1.refs_0_), channel_id=1, source_target_pairs={{0,2},{2,0},{4,6},{6,4},{8,10},{10,8},{12,14},{14,12},{1,3},{3,1},... | collective-permute-start | bytes 786440 | tf_op jit(solution)/shard_map/ppermute | solution.py:447
  92.5 8.1 %collective-permute-start.23 = (bf16[4,128,256]{2,1,0:T(8,128)(2,1)S(1)}, bf16[4,128,256]{2,1,0:T(8,128)(2,1)S(1)}, u32[]{:S(2)}, u32[]{:S(2)}) collective-permute-start(bf16[4,128,256]{2,1,0:T(8,128)(2,1)S(1)} %collective-permute-done.20.refs_1_), channel_id=1, source_target_pairs={{0,2},{2,0},{4,6},{6,4},{8,10},{10,8},{12,14},{14,12},{1,3},{3,1},... | collective-permute-start | bytes 786440 | tf_op jit(solution)/shard_map/ppermute | solution.py:447
  93.2 7.3 %collective-permute-start.24 = (bf16[4,128,256]{2,1,0:T(8,128)(2,1)S(1)}, bf16[4,128,256]{2,1,0:T(8,128)(2,1)S(1)}, u32[]{:S(2)}, u32[]{:S(2)}) collective-permute-start(bf16[4,128,256]{2,1,0:T(8,128)(2,1)S(1)} %collective-permute-done.21.refs_2_), channel_id=1, source_target_pairs={{0,2},{2,0},{4,6},{6,4},{8,10},{10,8},{12,14},{14,12},{1,3},{3,1},... | collective-permute-start | bytes 786440 | tf_op jit(solution)/shard_map/ppermute | solution.py:447
  95.6 6.9 %collective-permute-start.25 = (bf16[4,128,256]{2,1,0:T(8,128)(2,1)S(1)}, bf16[4,128,256]{2,1,0:T(8,128)(2,1)S(1)}, u32[]{:S(2)}, u32[]{:S(2)}) collective-permute-start(bf16[4,128,256]{2,1,0:T(8,128)(2,1)S(1)} %collective-permute-done.21.refs_2_), channel_id=1, source_target_pairs={{0,4},{2,6},{4,0},{6,2},{8,12},{10,14},{12,8},{14,10},{1,5},{3,7},... | collective-permute-start | bytes 786440 | tf_op jit(solution)/shard_map/ppermute | solution.py:443
  102.5 1.5 %collective-permute-start.26 = (bf16[4,128,256]{2,1,0:T(8,128)(2,1)S(1)}, bf16[4,128,256]{2,1,0:T(8,128)(2,1)S(1)}, u32[]{:S(2)}, u32[]{:S(2)}) collective-permute-start(bf16[4,128,256]{2,1,0:T(8,128)(2,1)S(1)} %collective-permute-done.25.mine), channel_id=1, source_target_pairs={{0,2},{2,0},{4,6},{6,4},{8,10},{10,8},{12,14},{14,12},{1,3},{3,1},... | collective-permute-start | bytes 786440 | tf_op jit(solution)/shard_map/ppermute | solution.py:447
  104.4 13.7 %collective-permute-start.27 = (bf16[4,128,256]{2,1,0:T(8,128)(2,1)S(1)}, bf16[4,128,256]{2,1,0:T(8,128)(2,1)S(1)}, u32[]{:S(2)}, u32[]{:S(2)}) collective-permute-start(bf16[4,128,256]{2,1,0:T(8,128)(2,1)S(1)} %get-tuple-element.35.refs_0_), channel_id=1, source_target_pairs={{0,4},{2,6},{4,0},{6,2},{8,12},{10,14},{12,8},{14,10},{1,5},{3,7},... | collective-permute-start | bytes 786440 | tf_op jit(solution)/shard_map/ppermute | solution.py:443
  105.4 14.6 %collective-permute-start.28 = (bf16[4,128,256]{2,1,0:T(8,128)(2,1)S(1)}, bf16[4,128,256]{2,1,0:T(8,128)(2,1)S(1)}, u32[]{:S(2)}, u32[]{:S(2)}) collective-permute-start(bf16[4,128,256]{2,1,0:T(8,128)(2,1)S(1)} %get-tuple-element.35.refs_0_), channel_id=1, source_target_pairs={{0,8},{2,10},{4,12},{6,14},{8,0},{10,2},{12,4},{14,6},{1,9},{3,11}... | collective-permute-start | bytes 786440 | tf_op jit(solution)/shard_map/ppermute | solution.py:443
  107.4 12.9 %collective-permute-start.29 = (bf16[4,128,256]{2,1,0:T(8,128)(2,1)S(1)}, bf16[4,128,256]{2,1,0:T(8,128)(2,1)S(1)}, u32[]{:S(2)}, u32[]{:S(2)}) collective-permute-start(bf16[4,128,256]{2,1,0:T(8,128)(2,1)S(1)} %get-tuple-element.35.refs_0_), channel_id=1, source_target_pairs={{0,2},{2,0},{4,6},{6,4},{8,10},{10,8},{12,14},{14,12},{1,3},{3,1},... | collective-permute-start | bytes 786440 | tf_op jit(solution)/shard_map/ppermute | solution.py:447
  118.2 2.1 %collective-permute-start.30 = (bf16[4,128,256]{2,1,0:T(8,128)(2,1)S(1)}, bf16[4,128,256]{2,1,0:T(8,128)(2,1)S(1)}, u32[]{:S(2)}, u32[]{:S(2)}) collective-permute-start(bf16[4,128,256]{2,1,0:T(8,128)(2,1)S(1)} %collective-permute-done.27.refs_1_), channel_id=1, source_target_pairs={{0,2},{2,0},{4,6},{6,4},{8,10},{10,8},{12,14},{14,12},{1,3},{3,1},... | collective-permute-start | bytes 786440 | tf_op jit(solution)/shard_map/ppermute | solution.py:447
  120.0 1.5 %collective-permute-start.31 = (bf16[4,128,256]{2,1,0:T(8,128)(2,1)S(1)}, bf16[4,128,256]{2,1,0:T(8,128)(2,1)S(1)}, u32[]{:S(2)}, u32[]{:S(2)}) collective-permute-start(bf16[4,128,256]{2,1,0:T(8,128)(2,1)S(1)} %collective-permute-done.28.refs_2_), channel_id=1, source_target_pairs={{0,2},{2,0},{4,6},{6,4},{8,10},{10,8},{12,14},{14,12},{1,3},{3,1},... | collective-permute-start | bytes 786440 | tf_op jit(solution)/shard_map/ppermute | solution.py:447
  120.0 8.7 %collective-permute-start.32 = (bf16[4,128,256]{2,1,0:T(8,128)(2,1)S(1)}, bf16[4,128,256]{2,1,0:T(8,128)(2,1)S(1)}, u32[]{:S(2)}, u32[]{:S(2)}) collective-permute-start(bf16[4,128,256]{2,1,0:T(8,128)(2,1)S(1)} %collective-permute-done.28.refs_2_), channel_id=1, source_target_pairs={{0,4},{2,6},{4,0},{6,2},{8,12},{10,14},{12,8},{14,10},{1,5},{3,7},... | collective-permute-start | bytes 786440 | tf_op jit(solution)/shard_map/ppermute | solution.py:443
  128.7 1.5 %collective-permute-start.33 = (bf16[4,128,256]{2,1,0:T(8,128)(2,1)S(1)}, bf16[4,128,256]{2,1,0:T(8,128)(2,1)S(1)}, u32[]{:S(2)}, u32[]{:S(2)}) collective-permute-start(bf16[4,128,256]{2,1,0:T(8,128)(2,1)S(1)} %collective-permute-done.32.mine), channel_id=1, source_target_pairs={{0,2},{2,0},{4,6},{6,4},{8,10},{10,8},{12,14},{14,12},{1,3},{3,1},... | collective-permute-start | bytes 786440 | tf_op jit(solution)/shard_map/ppermute | solution.py:447

commit v11 on v9

--- a/solution.py
+++ b/solution.py
@@ -80,9 +80,9 @@
     return lax.bitwise_xor(z, jnp.int32(step))
 
 
-def pack_kernel(full_ref, green_ref, one_ref, two_ref, three_ref, own_ref, cross_ref, sem):
+def pack_kernel(full_ref, one_ref, two_ref, three_ref, own_ref, cross_ref, sem):
     z, k, x = place()
-    walkers, rows, occupied = green_ref.shape
+    rows = own_ref.shape[1]
     copies = []
 
     def copy(source, target):
@@ -92,50 +92,63 @@
     def of_chip(step, core):
         return pl.ds(pl.multiple_of((2 * flipped(z, step) + core) * rows, rows), rows)
 
-    for step, message, top in ((2, two_ref, rows), (1, one_ref, rows), (3, three_ref, 0)):
+    for step, message in ((2, two_ref), (1, one_ref), (3, three_ref)):
         for index, core in enumerate((1 - k, k)):
-            copy(
-                full_ref.at[x, of_chip(step, core), :],
-                message.at[pl.ds(top + index * rows, rows), :],
-            )
+            target = message.at[pl.ds(index * rows, rows), :]
+            copy(full_ref.at[x, of_chip(step, core), :], target)
     copy(full_ref.at[:, of_chip(0, k), :], own_ref)
     copy(full_ref.at[:, of_chip(0, 1 - k), :], cross_ref)
     for each in copies:
         each.wait()
-    for message in (two_ref, one_ref):
-        for w in range(walkers):
-            message[:rows, w * occupied : (w + 1) * occupied] = green_ref[w]
-
-
-def packed(full_chol, green_blocks):
+
+
+def packed(full_chol, rows):
     order = full_chol.shape[2]
-    rows = green_blocks.shape[1]
-    shapes = [(3 * rows, order), (3 * rows, order), (2 * rows, order)] + [(2, rows, order)] * 2
+    shapes = [(2 * rows, order)] * 3 + [(2, rows, order)] * 2
     return pl.pallas_call(
         pack_kernel,
         out_shape=[jax.ShapeDtypeStruct(shape, narrow) for shape in shapes],
-        in_specs=[hbm_spec, vmem_spec],
+        in_specs=[hbm_spec],
         out_specs=[vmem_spec] * 5,
         scratch_shapes=[pltpu.SemaphoreType.DMA((8,))],
         name="packed",
-    )(full_chol, green_blocks)
-
-
-def start_kernel(orbitals_ref, out_ref):
-    for walker in range(out_ref.shape[0]):
-        out_ref[walker] = orbitals_ref[0, :, walker, :].astype(narrow)
-
-
-def walker_major(orbitals):
+    )(full_chol)
+
+
+field_rows = 16
+
+
+def start_kernel(orbitals_ref, field_ref, out_ref):
+    _, rows, walkers, occupied = orbitals_ref.shape
+    for w in range(walkers):
+        columns = slice(w * occupied, (w + 1) * occupied)
+        out_ref[:rows, columns] = orbitals_ref[0, :, w, :].astype(narrow)
+    rest = field_ref[...]
+    lanes = rest.shape[1]
+    for term in range(3):
+        part = rest.astype(narrow)
+        out_ref[rows:, term * lanes : (term + 1) * lanes] = part
+        rest = rest - part.astype(wide)
+
+
+def start_message(orbitals, field):
     _, rows, walkers, occupied = orbitals.shape
     return pl.pallas_call(
         start_kernel,
-        out_shape=jax.ShapeDtypeStruct((walkers, rows, occupied), narrow),
-        in_specs=[vmem_spec],
-        out_specs=vmem_spec,
-        compiler_params=small,
-        name="walker_major",
-    )(orbitals)
+        out_shape=jax.ShapeDtypeStruct((rows + field_rows, walkers * occupied), narrow),
+        in_specs=[vmem_spec] * 2,
+        out_specs=vmem_spec,
+        compiler_params=small,
+        name="start_message",
+    )(orbitals, field)
+
+
+def field_of(message_ref, rows):
+    lanes = 128
+    terms = [
+        message_ref[rows:, term * lanes : (term + 1) * lanes].astype(wide) for term in range(3)
+    ]
+    return terms[0] + terms[1] + terms[2]
 
 
 def bias_kernel(here_ref, one_ref, two_ref, three_ref, mine_ref, theirs_ref, out_ref):
@@ -147,14 +160,11 @@
     for step, green in enumerate((here_ref, one_ref, two_ref, three_ref)):
         base = (2 * flipped(z, step) + k) * rows
 
-        def add(index, totals, step=step, base=base, green=green):
+        def add(index, totals, base=base, green=green):
             here = pl.multiple_of(index * step_rows, step_rows)
             there = pl.multiple_of(base + index * step_rows, step_rows)
             picked = pl.ds(here, step_rows)
-            if step == 0:
-                greens = [green[w, picked, :] for w in range(walkers)]
-            else:
-                greens = [green[picked, w * occupied : (w + 1) * occupied] for w in range(walkers)]
+            greens = [green[w, picked, :] for w in range(walkers)]
             greens = [g.astype(wide) for g in greens]
             totals = list(totals)
             for c in range(2 * vectors):
@@ -259,21 +269,22 @@
 
 
 def both_cores(field_ref, rows, mine, mine_x, theirs, theirs_x):
-    top = mine.shape[0] - 2 * rows
     return [
-        (field_ref, 0, below(mine, top + rows), below(mine_x, rows)),
-        (field_ref, 1, below(theirs, top), below(theirs_x, 0)),
+        (field_ref, 0, below(mine, rows), below(mine_x, rows)),
+        (field_ref, 1, below(theirs, 0), below(theirs_x, 0)),
     ]
 
 
-def early_kernel(walkers, field_here, field_one, field_two, own, own_theirs, *refs):
-    blocks, summed_ref = refs[:-1], refs[-1]
+def early_kernel(walkers, field_here, start_one, start_two, own, own_theirs, *refs):
+    blocks, (summed_ref, field_one, field_two) = refs[:8], refs[8:]
     _, _, x = place()
+    rows = own.shape[1]
+    field_one[...] = field_of(start_one, rows)
+    field_two[...] = field_of(start_two, rows)
     sources = [
         (field_here, 0, of_pair(own, x), of_pair(own, 1 - x)),
         (field_here, 1, of_pair(own_theirs, x), of_pair(own_theirs, 1 - x)),
     ]
-    rows = own.shape[1]
     sources += both_cores(field_one, rows, *blocks[:4])
     sources += both_cores(field_two, rows, *blocks[4:])
 
@@ -286,22 +297,24 @@
     over_tiles(*summed_ref.shape[1:], body)
 
 
-def early_operator(walkers, fields, own, own_theirs, blocks):
+def early_operator(walkers, field, start_one, start_two, own, own_theirs, blocks):
     _, rows, order = own.shape
     return pl.pallas_call(
         functools.partial(early_kernel, walkers),
         out_shape=jax.ShapeDtypeStruct((walkers, rows, order), wide),
         in_specs=[vmem_spec] * (5 + len(blocks)),
         out_specs=vmem_spec,
+        scratch_shapes=[pltpu.VMEM((field_rows, 128), wide)] * 2,
         compiler_params=large,
         name="early_operator",
-    )(*fields, own, own_theirs, *blocks)
-
-
-def late_kernel(summed_ref, field_ref, *refs):
-    blocks, operator_ref = refs[:-1], refs[-1]
+    )(field, start_one, start_two, own, own_theirs, *blocks)
+
+
+def late_kernel(summed_ref, start_three, *refs):
+    blocks, (operator_ref, field_ref) = refs[:4], refs[4:]
     walkers, rows, order = summed_ref.shape
     _, _, x = place()
+    field_ref[...] = field_of(start_three, rows)
     sources = both_cores(field_ref, rows, *blocks)
 
     def body(picked):
@@ -319,29 +332,31 @@
     over_tiles(rows, order, body)
 
 
-def split_operator(summed, field, blocks):
+def split_operator(summed, start_three, blocks):
     walkers, rows, order = summed.shape
     return pl.pallas_call(
         late_kernel,
         out_shape=jax.ShapeDtypeStruct((walkers, 2 * rows, order), narrow),
         in_specs=[vmem_spec] * (2 + len(blocks)),
         out_specs=vmem_spec,
+        scratch_shapes=[pltpu.VMEM((field_rows, 128), wide)],
         compiler_params=large,
         name="split_operator",
-    )(summed, field, *blocks)
+    )(summed, start_three, *blocks)
 
 
 def applied(operator_ref, vector_ref, step, mine, theirs):
     z, k, _ = place()
-    _, rows, _ = mine.shape
-    vector_ref[:, pl.ds(pl.multiple_of(k * rows, rows), rows), :] = mine[...]
-    vector_ref[:, pl.ds(pl.multiple_of((1 - k) * rows, rows), rows), :] = theirs[...]
+    walkers, rows = operator_ref.shape[0], operator_ref.shape[1] // 2
+    occupied = mine.shape[1] // walkers
+    vector_ref[pl.ds(pl.multiple_of(k * rows, rows), rows), :] = mine[:rows, :]
+    vector_ref[pl.ds(pl.multiple_of((1 - k) * rows, rows), rows), :] = theirs[:rows, :]
     start = pl.multiple_of(flipped(z, step) * 2 * rows, 2 * rows)
 
     def of_walker(w):
         both = jnp.dot(
             operator_ref[w, :, pl.ds(start, 2 * rows)],
-            vector_ref[w],
+            vector_ref[:, w * occupied : (w + 1) * occupied],
             preferred_element_type=wide,
         )
         return both[:rows] + both[rows:]
@@ -360,13 +375,14 @@
 
 
 def near_application(operator, pieces):
-    walkers, rows, occupied = pieces[0].shape
+    walkers, rows = operator.shape[0], operator.shape[1] // 2
+    width = pieces[0].shape[1]
     return pl.pallas_call(
         near_kernel,
-        out_shape=jax.ShapeDtypeStruct((walkers, rows, occupied), wide),
+        out_shape=jax.ShapeDtypeStruct((walkers, rows, width // walkers), wide),
         in_specs=[vmem_spec] * 7,
         out_specs=vmem_spec,
-        scratch_shapes=[pltpu.VMEM((3, walkers, 2 * rows, occupied), narrow)],
+        scratch_shapes=[pltpu.VMEM((3, 2 * rows, width), narrow)],
         compiler_params=small,
         name="near_application",
     )(operator, *pieces)
@@ -374,23 +390,25 @@
 
 def first_kernel(operator_ref, partial_ref, mine, theirs, first_ref, narrow_ref, vector_ref):
     part = applied(operator_ref, vector_ref, 3, mine, theirs)
-    for w in range(first_ref.shape[0]):
+    walkers, _, occupied = first_ref.shape
+    for w in range(walkers):
         term = partial_ref[w] + part(w)
         first_ref[w] = term
-        narrow_ref[w] = term.astype(narrow)
+        narrow_ref[:, w * occupied : (w + 1) * occupied] = term.astype(narrow)
 
 
 def first_application(operator, partial, mine, theirs):
-    walkers, rows, occupied = mine.shape
+    _, rows, _ = partial.shape
+    width = mine.shape[1]
     return pl.pallas_call(
         first_kernel,
         out_shape=[
-            jax.ShapeDtypeStruct((walkers, rows, occupied), wide),
-            jax.ShapeDtypeStruct((walkers, rows, occupied), narrow),
+            jax.ShapeDtypeStruct(partial.shape, wide),
+            jax.ShapeDtypeStruct((rows, width), narrow),
         ],
         in_specs=[vmem_spec] * 4,
         out_specs=[vmem_spec] * 2,
-        scratch_shapes=[pltpu.VMEM((walkers, 2 * rows, occupied), narrow)],
+        scratch_shapes=[pltpu.VMEM((2 * rows, width), narrow)],
         compiler_params=small,
         name="first_application",
     )(operator, partial, mine, theirs)
@@ -408,13 +426,13 @@
 
 
 def base_application(operator, first_term, orbitals, pieces):
-    walkers, rows, occupied = first_term.shape
+    rows, width = pieces[0].shape
     return pl.pallas_call(
         base_kernel,
         out_shape=jax.ShapeDtypeStruct(first_term.shape, wide),
         in_specs=[vmem_spec] * 9,
         out_specs=vmem_spec,
-        scratch_shapes=[pltpu.VMEM((3, walkers, 2 * rows, occupied), narrow)],
+        scratch_shapes=[pltpu.VMEM((3, 2 * rows, width), narrow)],
         compiler_params=small,
         name="base_application",
     )(operator, first_term, orbitals, *pieces)
@@ -427,13 +445,13 @@
 
 
 def second_application(operator, base, mine, theirs):
-    walkers, rows, occupied = mine.shape
+    walkers, rows, occupied = base.shape
     return pl.pallas_call(
         second_kernel,
         out_shape=jax.ShapeDtypeStruct((1, rows, walkers, occupied), wide),
         in_specs=[vmem_spec] * 4,
         out_specs=vmem_spec,
-        scratch_shapes=[pltpu.VMEM((walkers, 2 * rows, occupied), narrow)],
+        scratch_shapes=[pltpu.VMEM((2 * rows, walkers * occupied), narrow)],
         compiler_params=small,
         name="second_application",
     )(operator, base, mine, theirs)
@@ -455,41 +473,51 @@
     walkers, rows, _ = green_blocks.shape
     vectors = half_chol.shape[0]
 
+    green_two, green_one = to_chip(green_blocks, 2), to_chip(green_blocks, 1)
     half_theirs = to_core(half_chol)
     constants = jnp.concatenate([noise_draws.T.reshape(-1), jnp.repeat(meanfield, walkers)])
     constants = jnp.broadcast_to(constants[:, None], (2 * vectors * walkers, 128))
     constants_theirs = to_core(constants)
-    one, two, three, own, own_cross = packed(full_chol, green_blocks)
-    two, one = to_chip(two, 2), to_chip(one, 1)
+    green_three = to_chip(green_two, 1)
+
+    one, two, three, own, own_cross = packed(full_chol, rows)
     own_theirs = to_core(own_cross)
-    three = to_chip(after(three, one, half_theirs, own_theirs, constants_theirs), 3)
-    green_three = to_chip(two[:rows], 1)
-
-    one_x, two_x, three_x = across(one[rows:]), across(two[rows:]), across(three)
-    messages = {1: (one, one_x), 2: (two, two_x), 3: (three, three_x)}
-    blocks = {step: [*both, *[to_core(each) for each in both]] for step, both in messages.items()}
-
-    bias = chip_bias((green_blocks, one, two, green_three), half_chol, half_theirs)
+    two = to_chip(two, 2)
+
+    green = (green_blocks, green_one, green_two, green_three)
+    bias = chip_bias(green, half_chol, after(half_theirs, own_theirs, constants_theirs))
     bias_shift, field = chip_field(bias, to_core(bias), constants, constants_theirs, vectors)
-    field_one, field_two, field_three = (to_chip(field, step) for step in (1, 2, 3))
-
-    start = after(walker_major(orbitals), field_two, blocks[1][2], blocks[2][2])
+
+    one = to_chip(after(one, green_three), 1)
+    three = to_chip(after(three, two, field), 3)
+    two_x, two_theirs = across(two), to_core(two)
+    one_x, one_theirs = across(one), to_core(one)
+
+    start = after(start_message(orbitals, field), two_x, two_theirs, one_theirs)
     start_two, start_one = to_chip(start, 2), to_chip(start, 1)
-    start_three = to_chip(after(start_two, blocks[1][3], blocks[2][3], blocks[3][2]), 1)
+    two_x_theirs, one_x_theirs = to_core(two_x), to_core(one_x)
+    three_x, three_theirs = across(three), to_core(three)
+    hops = (two_x_theirs, one_x_theirs, three_theirs)
+    start_three = to_chip(after(start_two, *hops), 1)
+    three_x_theirs = to_core(three_x)
 
     summed = early_operator(
         walkers,
-        (field, field_one, field_two),
+        field,
+        start_one,
+        start_two,
         own,
         own_theirs,
-        (*blocks[1], *blocks[2]),
-    )
-    operator = split_operator(summed, field_three, blocks[3])
+        (one, one_x, one_theirs, one_x_theirs, two, two_x, two_theirs, two_x_theirs),
+    )
+    operator = split_operator(
+        summed, start_three, (three, three_x, three_theirs, three_x_theirs)
+    )
 
     near = [start, start_one, start_two]
     partial = near_application(operator, [*near, *[to_core(piece) for piece in near]])
     first_term, first_narrow = first_application(
-        operator, partial, start_three, to_core(after(start_three, partial))
+        operator, partial, start_three, to_core(start_three)
     )
     first_two, first_one = to_chip(first_narrow, 2), to_chip(first_narrow, 1)
     first_three = to_chip(first_two, 1)

time: 144 us -> 145 us (level)
  waiting for transfers between devices: 92.4 us -> 102 us
  starting transfers between devices: 34.4 us -> 26.1 us
    ppermute x13 -> x12, waiting for transfers between devices: 68 us -> 78.3 us  [to_chip(): return lax.ppermute(value, 'chol', [(i, i ^ 2 * step) for i in range(8)])]
    ppermute x13 -> x12, starting transfers between devices: 27.4 us -> 19.8 us  [to_chip(): return lax.ppermute(value, 'chol', [(i, i ^ 2 * step) for i in range(8)])]
    ppermute x18, waiting for transfers between devices: 6.43 us -> 4.2 us  [to_core(): return lax.ppermute(value, 'chol', [(i, i ^ 1) for i in range(8)])]
    ppermute x3, waiting for transfers between devices: 17.9 us -> 19.4 us  [across(): return lax.ppermute(value, 'walk', [(0, 1), (1, 0)])]
  transfers between devices with their start and end apart: 34 -> 33, of which waited for: 16 -> 13; matrix products, arithmetic and copies ran while one was open for 0% -> 0% of each run, Pallas kernels for 10% -> 10%
where the time goes in v11:
time: 145 us
  waiting for transfers between devices  102 us (70%)
  starting transfers between devices  26.1 us (18%)
  Pallas kernels  15.9 us (11%)
    ppermute x12, waiting for transfers between devices, to_chip(): return lax.ppermute(value, 'chol', [(i, i ^ 2 * step) for i in range(8)])  78.3 us
    ppermute x12, starting transfers between devices, to_chip(): return lax.ppermute(value, 'chol', [(i, i ^ 2 * step) for i in range(8)])  19.8 us
    ppermute x3, waiting for transfers between devices, across(): return lax.ppermute(value, 'walk', [(0, 1), (1, 0)])  19.4 us
    pallas_call x1, Pallas kernels, early_operator(): pl.pallas_call(functools.partial(early_kernel, walkers), out_shape=jax.Sh...  4.69 us
    ppermute x18, waiting for transfers between devices, to_core(): return lax.ppermute(value, 'chol', [(i, i ^ 1) for i in range(8)])  4.2 us
    ppermute x3, starting transfers between devices, across(): return lax.ppermute(value, 'walk', [(0, 1), (1, 0)])  3.58 us
    pallas_call x1, Pallas kernels, packed(): pl.pallas_call(pack_kernel, out_shape=[jax.ShapeDtypeStruct(shape, narrow...  3.27 us
  transfers between devices with their start and end apart: 33, of which 13 were waited for; matrix products, arithmetic and copies ran while one was open for 0% of the time, Pallas kernels for 10%

profile of v11, /device:TPU:0, one launch (start us, length us, event | category | flops | bytes accessed | tf_op | source)
XLA Modules:
  0.0 145.2 jit_solution(10604622452399327666)
XLA Ops:
  0.7 0.5 collective-permute-start.3
  1.2 3.7 %collective-permute-start.1 = (bf16[4,128,256]{2,1,0:T(8,128)(2,1)}, bf16[4,128,256]{2,1,0:T(8,128)(2,1)}, u32[]{:S(2)}, u32[]{:S(2)}) collective-permute-start(bf16[4,128,256]{2,1,0:T(8,128)(2,1)} %here_ref.1), channel_id=1, source_target_pairs={{0,8},{2,10},{4,12},{6,14},{8,0},{10,2},{12,4},{14,6},{1,9},{3,11}... | collective-permute-start | bytes 786440 | tf_op jit(solution)/shard_map/ppermute | solution.py:461
  4.9 12.8 %collective-permute-done.1.two_ref = bf16[4,128,256]{2,1,0:T(8,128)(2,1)} collective-permute-done((bf16[4,128,256]{2,1,0:T(8,128)(2,1)}, bf16[4,128,256]{2,1,0:T(8,128)(2,1)}, u32[]{:S(2)}, u32[]{:S(2)}) %collective-permute-start.1) | collective-permute-done | bytes 262176 | tf_op jit(solution)/shard_map/ppermute | solution.py:461
  17.7 0.7 collective-permute-start.2
  18.4 3.3 %packed.1 = (bf16[256,1024]{1,0:T(8,128)(2,1)}, bf16[256,1024]{1,0:T(8,128)(2,1)}, bf16[256,1024]{1,0:T(8,128)(2,1)}, bf16[2,128,1024]{2,1,0:T(8,128)(2,1)}, bf16[2,128,1024]{2,1,0:T(8,128)(2,1)}) custom-call(bf16[2,1024,1024]{2,1,0:T(8,128)(2,1)} %full_ref.1), custom_call_target="tpu_custom_call" | custom-call | tf_op jit(solution)/shard_map/packed/pallas_call | solution.py:108
  21.7 0.1 collective-permute-start.4
  21.8 3.4 %collective-permute-start.7 = (bf16[256,1024]{1,0:T(8,128)(2,1)}, bf16[256,1024]{1,0:T(8,128)(2,1)}, u32[]{:S(2)}, u32[]{:S(2)}) collective-permute-start(bf16[256,1024]{1,0:T(8,128)(2,1)} %get-tuple-element.20), channel_id=1, source_target_pairs={{0,8},{2,10},{4,12},{6,14},{8,0},{10,2},{12,4},{14,6},{1,9},{3,11}... | collective-permute-start | bytes 1572872 | tf_op jit(solution)/shard_map/ppermute | solution.py:461
  25.3 0.8 collective-permute-done.2.three_ref
  26.1 1.0 collective-permute-start.10
  27.1 0.1 reshape.12
  27.2 0.1 reshape.11
  27.3 0.1 pad_maximum_fusion
  27.3 0.1 broadcast_in_dim.10.noise_ref
  27.4 1.2 collective-permute-done.5.noise_there_ref
  28.6 1.1 collective-permute-start
  29.7 25.6 %collective-permute-done.one_ref = bf16[4,128,256]{2,1,0:T(8,128)(2,1)S(1)} collective-permute-done((bf16[4,128,256]{2,1,0:T(8,128)(2,1)S(1)}, bf16[4,128,256]{2,1,0:T(8,128)(2,1)S(1)}, u32[]{:S(2)}, u32[]{:S(2)}) %collective-permute-start) | collective-permute-done | bytes 262176 | tf_op jit(solution)/shard_map/ppermute | solution.py:461
  55.2 2.0 %chip_bias.1.mine_ref = f32[16,128]{1,0:T(8,128)S(1)} custom-call(bf16[4,128,256]{2,1,0:T(8,128)(2,1)S(1)} %copy-done.3, bf16[4,128,256]{2,1,0:T(8,128)(2,1)S(1)} %collective-permute-done.one_ref, bf16[4,128,256]{2,1,0:T(8,128)(2,1)} %collective-permute-done.1.two_ref, bf16[4,128,256]{2,1,0:T(8,128)(2,1)} %collective-permute-done.2.three_ref, ...), custom_call_target="tpu_custom_call" | custom-call | tf_op jit(solution)/shard_map/chip_bias/pallas_call | solution.py:191
  57.3 1.6 %collective-permute-start.8 = (bf16[256,1024]{1,0:T(8,128)(2,1)}, bf16[256,1024]{1,0:T(8,128)(2,1)S(1)}, u32[]{:S(2)}, u32[]{:S(2)}) collective-permute-start(bf16[256,1024]{1,0:T(8,128)(2,1)} %collective-permute-done.7.refs_4_), channel_id=1, source_target_pairs={{0,1},{1,0},{2,3},{3,2},{4,5},{5,4},{6,7},{7,6},{8,9},{9,8},{10,11... | collective-permute-start | bytes 1572872 | tf_op jit(solution)/shard_map/ppermute | solution.py:469
  58.9 0.5 collective-permute-start.14
  59.4 0.6 chip_field.1
  60.0 3.2 %collective-permute-start.17 = (bf16[256,1024]{1,0:T(8,128)(2,1)S(1)}, bf16[256,1024]{1,0:T(8,128)(2,1)S(1)}, u32[]{:S(2)}, u32[]{:S(2)}) collective-permute-start(bf16[256,1024]{1,0:T(8,128)(2,1)S(1)} %copy-done.4), channel_id=1, source_target_pairs={{0,12},{2,14},{4,8},{6,10},{8,4},{10,6},{12,0},{14,2},{1,13},{3,15... | collective-permute-start | bytes 1572872 | tf_op jit(solution)/shard_map/ppermute | solution.py:461
  63.2 0.5 collective-permute-start.11
  63.7 8.6 %collective-permute-done.8.refs_5_ = bf16[256,1024]{1,0:T(8,128)(2,1)S(1)} collective-permute-done((bf16[256,1024]{1,0:T(8,128)(2,1)}, bf16[256,1024]{1,0:T(8,128)(2,1)S(1)}, u32[]{:S(2)}, u32[]{:S(2)}) %collective-permute-start.8) | collective-permute-done | bytes 524320 | tf_op jit(solution)/shard_map/ppermute | solution.py:469
  72.3 10.8 %collective-permute-done.14.refs_1_ = bf16[256,1024]{1,0:T(8,128)(2,1)S(1)} collective-permute-done((bf16[256,1024]{1,0:T(8,128)(2,1)}, bf16[256,1024]{1,0:T(8,128)(2,1)S(1)}, u32[]{:S(2)}, u32[]{:S(2)}) %collective-permute-start.14) | collective-permute-done | bytes 524320 | tf_op jit(solution)/shard_map/ppermute | solution.py:469
  83.1 0.5 collective-permute-start.18
  83.6 1.5 %collective-permute-start.20 = (bf16[256,1024]{1,0:T(8,128)(2,1)S(1)}, bf16[256,1024]{1,0:T(8,128)(2,1)S(1)}, u32[]{:S(2)}, u32[]{:S(2)}) collective-permute-start(bf16[256,1024]{1,0:T(8,128)(2,1)S(1)} %collective-permute-done.17.refs_0_), channel_id=1, source_target_pairs={{0,1},{1,0},{2,3},{3,2},{4,5},{5,4},{6,7},{7,6},{8,9},{9,8},{10,11... | collective-permute-start | bytes 1572872 | tf_op jit(solution)/shard_map/ppermute | solution.py:469
  85.1 0.5 start_message.1.refs_0_
  85.7 2.8 %collective-permute-start.13 = (bf16[144,1024]{1,0:T(8,128)(2,1)S(1)}, bf16[144,1024]{1,0:T(8,128)(2,1)S(1)}, u32[]{:S(2)}, u32[]{:S(2)}) collective-permute-start(bf16[144,1024]{1,0:T(8,128)(2,1)S(1)} %start_message.1.refs_0_), channel_id=1, source_target_pairs={{0,8},{2,10},{4,12},{6,14},{8,0},{10,2},{12,4},{14,6},{1,9},{3,11}... | collective-permute-start | bytes 884744 | tf_op jit(solution)/shard_map/ppermute | solution.py:461
  88.5 1.0 collective-permute-start.12
  89.5 12.7 %collective-permute-done.13.start_two.refs_2_ = bf16[144,1024]{1,0:T(8,128)(2,1)S(1)} collective-permute-done((bf16[144,1024]{1,0:T(8,128)(2,1)S(1)}, bf16[144,1024]{1,0:T(8,128)(2,1)S(1)}, u32[]{:S(2)}, u32[]{:S(2)}) %collective-permute-start.13) | collective-permute-done | bytes 294944 | tf_op jit(solution)/shard_map/ppermute | solution.py:461
  102.3 0.1 collective-permute-start.21
  102.3 0.5 collective-permute-start.22
  102.8 0.1 collective-permute-start.23
  102.9 0.4 collective-permute-start.24
  103.3 7.4 %collective-permute-done.19.start_three.mine = bf16[144,1024]{1,0:T(8,128)(2,1)S(1)} collective-permute-done((bf16[144,1024]{1,0:T(8,128)(2,1)S(1)}, bf16[144,1024]{1,0:T(8,128)(2,1)S(1)}, u32[]{:S(2)}, u32[]{:S(2)}) %collective-permute-start.19) | collective-permute-done | bytes 294944 | tf_op jit(solution)/shard_map/ppermute | solution.py:461
  110.7 4.7 %early_operator.1.summed_ref = f32[4,128,1024]{2,1,0:T(8,128)S(1)} custom-call(f32[16,128]{1,0:T(8,128)S(1)} %get-tuple-element.19.field_ref.field_here, bf16[144,1024]{1,0:T(8,128)(2,1)S(1)} %collective-permute-done.12.start_one.refs_1_, bf16[144,1024]{1,0:T(8,128)(2,1)S(1)} %collective-permute-done.13.start_two.refs_2_, ...), custom_call_target="tpu_custom_call" | custom-call | tf_op jit(solution)/shard_map/early_operator/pallas_call | solution.py:302
  115.4 1.6 %split_operator.1.operator_ref = bf16[4,256,1024]{2,1,0:T(8,128)(2,1)S(1)} custom-call(f32[4,128,1024]{2,1,0:T(8,128)S(1)} %early_operator.1.summed_ref, bf16[144,1024]{1,0:T(8,128)(2,1)S(1)} %collective-permute-done.19.start_three.mine, bf16[256,1024]{1,0:T(8,128)(2,1)S(1)} %collective-permute-done.17.refs_0_, ...), custom_call_target="tpu_custom_call" | custom-call | tf_op jit(solution)/shard_map/split_operator/pallas_call | solution.py:337
  117.1 0.8 near_application.1.partial_ref
  117.8 0.4 first_application.1
  118.2 0.4 collective-permute-start.26
  118.6 2.4 %collective-permute-start.27 = (bf16[128,1024]{1,0:T(8,128)(2,1)S(1)}, bf16[128,1024]{1,0:T(8,128)(2,1)S(1)}, u32[]{:S(2)}, u32[]{:S(2)}) collective-permute-start(bf16[128,1024]{1,0:T(8,128)(2,1)S(1)} %get-tuple-element.29.refs_0_), channel_id=1, source_target_pairs={{0,8},{2,10},{4,12},{6,14},{8,0},{10,2},{12,4},{14,6},{1,9},{3,11}... | collective-permute-start | bytes 786440 | tf_op jit(solution)/shard_map/ppermute | solution.py:461
  121.0 11.1 %collective-permute-done.26.refs_1_ = bf16[128,1024]{1,0:T(8,128)(2,1)S(1)} collective-permute-done((bf16[128,1024]{1,0:T(8,128)(2,1)S(1)}, bf16[128,1024]{1,0:T(8,128)(2,1)S(1)}, u32[]{:S(2)}, u32[]{:S(2)}) %collective-permute-start.26) | collective-permute-done | bytes 262176 | tf_op jit(solution)/shard_map/ppermute | solution.py:461
  132.1 1.5 %collective-permute-done.27.refs_2_ = bf16[128,1024]{1,0:T(8,128)(2,1)S(1)} collective-permute-done((bf16[128,1024]{1,0:T(8,128)(2,1)S(1)}, bf16[128,1024]{1,0:T(8,128)(2,1)S(1)}, u32[]{:S(2)}, u32[]{:S(2)}) %collective-permute-start.27) | collective-permute-done | bytes 262176 | tf_op jit(solution)/shard_map/ppermute | solution.py:461
  133.7 1.5 %collective-permute-done.30.refs_5_ = bf16[128,1024]{1,0:T(8,128)(2,1)S(1)} collective-permute-done((bf16[128,1024]{1,0:T(8,128)(2,1)S(1)}, bf16[128,1024]{1,0:T(8,128)(2,1)S(1)}, u32[]{:S(2)}, u32[]{:S(2)}) %collective-permute-start.30) | collective-permute-done | bytes 262176 | tf_op jit(solution)/shard_map/ppermute | solution.py:465
  135.2 0.9 base_application.1.base_ref
  136.1 6.3 %collective-permute-done.31.mine = bf16[128,1024]{1,0:T(8,128)(2,1)S(1)} collective-permute-done((bf16[128,1024]{1,0:T(8,128)(2,1)S(1)}, bf16[128,1024]{1,0:T(8,128)(2,1)S(1)}, u32[]{:S(2)}, u32[]{:S(2)}) %collective-permute-start.31) | collective-permute-done | bytes 262176 | tf_op jit(solution)/shard_map/ppermute | solution.py:461
  142.4 1.5 %collective-permute-done.32.theirs = bf16[128,1024]{1,0:T(8,128)(2,1)S(1)} collective-permute-done((bf16[128,1024]{1,0:T(8,128)(2,1)S(1)}, bf16[128,1024]{1,0:T(8,128)(2,1)S(1)}, u32[]{:S(2)}, u32[]{:S(2)}) %collective-permute-start.32) | collective-permute-done | bytes 262176 | tf_op jit(solution)/shard_map/ppermute | solution.py:465
  143.9 1.3 second_application.1
  (47 shorter events, 0.3 us)
Async XLA Ops:
  0.6 54.6 %copy-start.1 = (bf16[2,1024,256]{2,1,0:T(8,128)(2,1)S(1)}, bf16[2,1024,256]{2,1,0:T(8,128)(2,1)}, u32[]{:S(2)}) copy-start(bf16[2,1024,256]{2,1,0:T(8,128)(2,1)} %mine_ref.1) | copy-start | bytes 3145732
  0.6 27.9 %copy-start.3 = (bf16[4,128,256]{2,1,0:T(8,128)(2,1)S(1)}, bf16[4,128,256]{2,1,0:T(8,128)(2,1)}, u32[]{:S(2)}) copy-start(bf16[4,128,256]{2,1,0:T(8,128)(2,1)} %here_ref.1) | copy-start | bytes 786436
  0.7 26.4 %copy-start.6 = (f32[2]{0:T(128)S(1)}, f32[2]{0:T(128)}, u32[]{:S(2)}) copy-start(f32[2]{0:T(128)} %param.9) | copy-start | bytes 28
  0.7 26.5 %copy-start.5 = (f32[4,2]{0,1:T(2,128)S(1)}, f32[4,2]{0,1:T(2,128)}, u32[]{:S(2)}) copy-start(f32[4,2]{0,1:T(2,128)} %param.10) | copy-start | bytes 100
  0.7 29.0 %collective-permute-start.3 = (bf16[2,1024,256]{2,1,0:T(8,128)(2,1)}, bf16[2,1024,256]{2,1,0:T(8,128)(2,1)S(1)}, u32[]{:S(2)}, u32[]{:S(2)}) collective-permute-start(bf16[2,1024,256]{2,1,0:T(8,128)(2,1)} %mine_ref.1), channel_id=1, source_target_pairs={{0,2},{2,0},{4,6},{6,4},{8,10},{10,8},{12,14},{14,12},{1,3},{3,1},... | collective-permute-start | bytes 3145736 | tf_op jit(solution)/shard_map/ppermute | solution.py:465
  1.2 16.5 %collective-permute-start.1 = (bf16[4,128,256]{2,1,0:T(8,128)(2,1)}, bf16[4,128,256]{2,1,0:T(8,128)(2,1)}, u32[]{:S(2)}, u32[]{:S(2)}) collective-permute-start(bf16[4,128,256]{2,1,0:T(8,128)(2,1)} %here_ref.1), channel_id=1, source_target_pairs={{0,8},{2,10},{4,12},{6,14},{8,0},{10,2},{12,4},{14,6},{1,9},{3,11}... | collective-permute-start | bytes 786440 | tf_op jit(solution)/shard_map/ppermute | solution.py:461
  17.7 8.4 %collective-permute-start.2 = (bf16[4,128,256]{2,1,0:T(8,128)(2,1)}, bf16[4,128,256]{2,1,0:T(8,128)(2,1)}, u32[]{:S(2)}, u32[]{:S(2)}) collective-permute-start(bf16[4,128,256]{2,1,0:T(8,128)(2,1)} %collective-permute-done.1.two_ref), channel_id=1, source_target_pairs={{0,4},{2,6},{4,0},{6,2},{8,12},{10,14},{12,8},{14,10},{1,5},{3,7},... | collective-permute-start | bytes 786440 | tf_op jit(solution)/shard_map/ppermute | solution.py:461
  21.7 63.4 %copy-start = (f32[1,128,4,256]{3,2,1,0:T(4,128)S(1)}, f32[1,128,4,256]{3,2,1,0:T(4,128)}, u32[]{:S(2)}) copy-start(f32[1,128,4,256]{3,2,1,0:T(4,128)} %orbitals_ref.3) | copy-start | bytes 1572868
  21.7 89.0 %copy-start.2 = (bf16[2,128,1024]{2,1,0:T(8,128)(2,1)S(1)}, bf16[2,128,1024]{2,1,0:T(8,128)(2,1)}, u32[]{:S(2)}) copy-start(bf16[2,128,1024]{2,1,0:T(8,128)(2,1)} %get-tuple-element.24.own) | copy-start | bytes 1572868
  21.7 7.9 %collective-permute-start.4 = (bf16[2,128,1024]{2,1,0:T(8,128)(2,1)}, bf16[2,128,1024]{2,1,0:T(8,128)(2,1)}, u32[]{:S(2)}, u32[]{:S(2)}) collective-permute-start(bf16[2,128,1024]{2,1,0:T(8,128)(2,1)} %get-tuple-element.17), channel_id=1, source_target_pairs={{0,2},{2,0},{4,6},{6,4},{8,10},{10,8},{12,14},{14,12},{1,3},{3,1},... | collective-permute-start | bytes 1572872 | tf_op jit(solution)/shard_map/ppermute | solution.py:465
  21.8 35.5 %collective-permute-start.7 = (bf16[256,1024]{1,0:T(8,128)(2,1)}, bf16[256,1024]{1,0:T(8,128)(2,1)}, u32[]{:S(2)}, u32[]{:S(2)}) collective-permute-start(bf16[256,1024]{1,0:T(8,128)(2,1)} %get-tuple-element.20), channel_id=1, source_target_pairs={{0,8},{2,10},{4,12},{6,14},{8,0},{10,2},{12,4},{14,6},{1,9},{3,11}... | collective-permute-start | bytes 1572872 | tf_op jit(solution)/shard_map/ppermute | solution.py:461
  26.1 32.8 %collective-permute-start.10 = (bf16[256,1024]{1,0:T(8,128)(2,1)}, bf16[256,1024]{1,0:T(8,128)(2,1)}, u32[]{:S(2)}, u32[]{:S(2)}) collective-permute-start(bf16[256,1024]{1,0:T(8,128)(2,1)} %get-tuple-element.22), channel_id=1, source_target_pairs={{0,4},{2,6},{4,0},{6,2},{8,12},{10,14},{12,8},{14,10},{1,5},{3,7},... | collective-permute-start | bytes 1572872 | tf_op jit(solution)/shard_map/ppermute | solution.py:461
  27.3 32.8 %copy-start.4 = (bf16[256,1024]{1,0:T(8,128)(2,1)S(1)}, bf16[256,1024]{1,0:T(8,128)(2,1)}, u32[]{:S(2)}) copy-start(bf16[256,1024]{1,0:T(8,128)(2,1)} %get-tuple-element.26) | copy-start | bytes 1572868
  27.4 1.2 collective-permute-start.5
  28.6 26.6 %collective-permute-start = (bf16[4,128,256]{2,1,0:T(8,128)(2,1)S(1)}, bf16[4,128,256]{2,1,0:T(8,128)(2,1)S(1)}, u32[]{:S(2)}, u32[]{:S(2)}) collective-permute-start(bf16[4,128,256]{2,1,0:T(8,128)(2,1)S(1)} %copy-done.3), channel_id=1, source_target_pairs={{0,4},{2,6},{4,0},{6,2},{8,12},{10,14},{12,8},{14,10},{1,5},{3,7},... | collective-permute-start | bytes 786440 | tf_op jit(solution)/shard_map/ppermute | solution.py:461
  57.2 2.2 %collective-permute-start.6 = (f32[16,128]{1,0:T(8,128)S(1)}, f32[16,128]{1,0:T(8,128)S(1)}, u32[]{:S(2)}, u32[]{:S(2)}) collective-permute-start(f32[16,128]{1,0:T(8,128)S(1)} %chip_bias.1.mine_ref), channel_id=1, source_target_pairs={{0,2},{2,0},{4,6},{6,4},{8,10},{10,8},{12,14},{14,12},{1,3},{3,1},... | collective-permute-start | bytes 24584 | tf_op jit(solution)/shard_map/ppermute | solution.py:465
  57.3 15.0 %collective-permute-start.8 = (bf16[256,1024]{1,0:T(8,128)(2,1)}, bf16[256,1024]{1,0:T(8,128)(2,1)S(1)}, u32[]{:S(2)}, u32[]{:S(2)}) collective-permute-start(bf16[256,1024]{1,0:T(8,128)(2,1)} %collective-permute-done.7.refs_4_), channel_id=1, source_target_pairs={{0,1},{1,0},{2,3},{3,2},{4,5},{5,4},{6,7},{7,6},{8,9},{9,8},{10,11... | collective-permute-start | bytes 1572872 | tf_op jit(solution)/shard_map/ppermute | solution.py:469
  58.9 24.2 %collective-permute-start.14 = (bf16[256,1024]{1,0:T(8,128)(2,1)}, bf16[256,1024]{1,0:T(8,128)(2,1)S(1)}, u32[]{:S(2)}, u32[]{:S(2)}) collective-permute-start(bf16[256,1024]{1,0:T(8,128)(2,1)} %collective-permute-done.10.refs_0_), channel_id=1, source_target_pairs={{0,1},{1,0},{2,3},{3,2},{4,5},{5,4},{6,7},{7,6},{8,9},{9,8},{10,11... | collective-permute-start | bytes 1572872 | tf_op jit(solution)/shard_map/ppermute | solution.py:469
  60.0 23.1 %collective-permute-start.17 = (bf16[256,1024]{1,0:T(8,128)(2,1)S(1)}, bf16[256,1024]{1,0:T(8,128)(2,1)S(1)}, u32[]{:S(2)}, u32[]{:S(2)}) collective-permute-start(bf16[256,1024]{1,0:T(8,128)(2,1)S(1)} %copy-done.4), channel_id=1, source_target_pairs={{0,12},{2,14},{4,8},{6,10},{8,4},{10,6},{12,0},{14,2},{1,13},{3,15... | collective-permute-start | bytes 1572872 | tf_op jit(solution)/shard_map/ppermute | solution.py:461
  63.2 20.4 %collective-permute-start.9 = (bf16[256,1024]{1,0:T(8,128)(2,1)}, bf16[256,1024]{1,0:T(8,128)(2,1)S(1)}, u32[]{:S(2)}, u32[]{:S(2)}) collective-permute-start(bf16[256,1024]{1,0:T(8,128)(2,1)} %collective-permute-done.7.refs_4_), channel_id=1, source_target_pairs={{0,2},{2,0},{4,6},{6,4},{8,10},{10,8},{12,14},{14,12},{1,3},{3,1},... | collective-permute-start | bytes 1572872 | tf_op jit(solution)/shard_map/ppermute | solution.py:465
  63.2 22.4 %collective-permute-start.11 = (bf16[256,1024]{1,0:T(8,128)(2,1)}, bf16[256,1024]{1,0:T(8,128)(2,1)S(1)}, u32[]{:S(2)}, u32[]{:S(2)}) collective-permute-start(bf16[256,1024]{1,0:T(8,128)(2,1)} %collective-permute-done.10.refs_0_), channel_id=1, source_target_pairs={{0,2},{2,0},{4,6},{6,4},{8,10},{10,8},{12,14},{14,12},{1,3},{3,1},... | collective-permute-start | bytes 1572872 | tf_op jit(solution)/shard_map/ppermute | solution.py:465
  72.3 16.2 %collective-permute-start.16 = (bf16[256,1024]{1,0:T(8,128)(2,1)S(1)}, bf16[256,1024]{1,0:T(8,128)(2,1)S(1)}, u32[]{:S(2)}, u32[]{:S(2)}) collective-permute-start(bf16[256,1024]{1,0:T(8,128)(2,1)S(1)} %collective-permute-done.8.refs_5_), channel_id=1, source_target_pairs={{0,2},{2,0},{4,6},{6,4},{8,10},{10,8},{12,14},{14,12},{1,3},{3,1},... | collective-permute-start | bytes 1572872 | tf_op jit(solution)/shard_map/ppermute | solution.py:465
  83.1 19.1 %collective-permute-start.15 = (bf16[256,1024]{1,0:T(8,128)(2,1)S(1)}, bf16[256,1024]{1,0:T(8,128)(2,1)S(1)}, u32[]{:S(2)}, u32[]{:S(2)}) collective-permute-start(bf16[256,1024]{1,0:T(8,128)(2,1)S(1)} %collective-permute-done.14.refs_1_), channel_id=1, source_target_pairs={{0,2},{2,0},{4,6},{6,4},{8,10},{10,8},{12,14},{14,12},{1,3},{3,1},... | collective-permute-start | bytes 1572872 | tf_op jit(solution)/shard_map/ppermute | solution.py:465
  83.1 19.1 %collective-permute-start.18 = (bf16[256,1024]{1,0:T(8,128)(2,1)S(1)}, bf16[256,1024]{1,0:T(8,128)(2,1)S(1)}, u32[]{:S(2)}, u32[]{:S(2)}) collective-permute-start(bf16[256,1024]{1,0:T(8,128)(2,1)S(1)} %collective-permute-done.17.refs_0_), channel_id=1, source_target_pairs={{0,2},{2,0},{4,6},{6,4},{8,10},{10,8},{12,14},{14,12},{1,3},{3,1},... | collective-permute-start | bytes 1572872 | tf_op jit(solution)/shard_map/ppermute | solution.py:465
  83.6 18.6 %collective-permute-start.20 = (bf16[256,1024]{1,0:T(8,128)(2,1)S(1)}, bf16[256,1024]{1,0:T(8,128)(2,1)S(1)}, u32[]{:S(2)}, u32[]{:S(2)}) collective-permute-start(bf16[256,1024]{1,0:T(8,128)(2,1)S(1)} %collective-permute-done.17.refs_0_), channel_id=1, source_target_pairs={{0,1},{1,0},{2,3},{3,2},{4,5},{5,4},{6,7},{7,6},{8,9},{9,8},{10,11... | collective-permute-start | bytes 1572872 | tf_op jit(solution)/shard_map/ppermute | solution.py:469
  85.7 16.6 %collective-permute-start.13 = (bf16[144,1024]{1,0:T(8,128)(2,1)S(1)}, bf16[144,1024]{1,0:T(8,128)(2,1)S(1)}, u32[]{:S(2)}, u32[]{:S(2)}) collective-permute-start(bf16[144,1024]{1,0:T(8,128)(2,1)S(1)} %start_message.1.refs_0_), channel_id=1, source_target_pairs={{0,8},{2,10},{4,12},{6,14},{8,0},{10,2},{12,4},{14,6},{1,9},{3,11}... | collective-permute-start | bytes 884744 | tf_op jit(solution)/shard_map/ppermute | solution.py:461
  88.5 14.3 %collective-permute-start.12 = (bf16[144,1024]{1,0:T(8,128)(2,1)S(1)}, bf16[144,1024]{1,0:T(8,128)(2,1)S(1)}, u32[]{:S(2)}, u32[]{:S(2)}) collective-permute-start(bf16[144,1024]{1,0:T(8,128)(2,1)S(1)} %start_message.1.refs_0_), channel_id=1, source_target_pairs={{0,4},{2,6},{4,0},{6,2},{8,12},{10,14},{12,8},{14,10},{1,5},{3,7},... | collective-permute-start | bytes 884744 | tf_op jit(solution)/shard_map/ppermute | solution.py:461
  102.2 8.5 %collective-permute-start.19 = (bf16[144,1024]{1,0:T(8,128)(2,1)S(1)}, bf16[144,1024]{1,0:T(8,128)(2,1)S(1)}, u32[]{:S(2)}, u32[]{:S(2)}) collective-permute-start(bf16[144,1024]{1,0:T(8,128)(2,1)S(1)} %collective-permute-done.13.start_two.refs_2_), channel_id=1, source_target_pairs={{0,4},{2,6},{4,0},{6,2},{8,12},{10,14},{12,8},{14,10},{1,5},{3,7},... | collective-permute-start | bytes 884744 | tf_op jit(solution)/shard_map/ppermute | solution.py:461
  102.3 13.2 %collective-permute-start.21 = (bf16[256,1024]{1,0:T(8,128)(2,1)S(1)}, bf16[256,1024]{1,0:T(8,128)(2,1)S(1)}, u32[]{:S(2)}, u32[]{:S(2)}) collective-permute-start(bf16[256,1024]{1,0:T(8,128)(2,1)S(1)} %collective-permute-done.20.refs_1_), channel_id=1, source_target_pairs={{0,2},{2,0},{4,6},{6,4},{8,10},{10,8},{12,14},{14,12},{1,3},{3,1},... | collective-permute-start | bytes 1572872 | tf_op jit(solution)/shard_map/ppermute | solution.py:465
  102.3 14.7 %collective-permute-start.22 = (bf16[144,1024]{1,0:T(8,128)(2,1)S(1)}, bf16[144,1024]{1,0:T(8,128)(2,1)S(1)}, u32[]{:S(2)}, u32[]{:S(2)}) collective-permute-start(bf16[144,1024]{1,0:T(8,128)(2,1)S(1)} %start_message.1.refs_0_), channel_id=1, source_target_pairs={{0,2},{2,0},{4,6},{6,4},{8,10},{10,8},{12,14},{14,12},{1,3},{3,1},... | collective-permute-start | bytes 884744 | tf_op jit(solution)/shard_map/ppermute | solution.py:465
  102.8 14.2 %collective-permute-start.23 = (bf16[144,1024]{1,0:T(8,128)(2,1)S(1)}, bf16[144,1024]{1,0:T(8,128)(2,1)S(1)}, u32[]{:S(2)}, u32[]{:S(2)}) collective-permute-start(bf16[144,1024]{1,0:T(8,128)(2,1)S(1)} %collective-permute-done.12.start_one.refs_1_), channel_id=1, source_target_pairs={{0,2},{2,0},{4,6},{6,4},{8,10},{10,8},{12,14},{14,12},{1,3},{3,1},... | collective-permute-start | bytes 884744 | tf_op jit(solution)/shard_map/ppermute | solution.py:465
  102.9 14.1 %collective-permute-start.24 = (bf16[144,1024]{1,0:T(8,128)(2,1)S(1)}, bf16[144,1024]{1,0:T(8,128)(2,1)S(1)}, u32[]{:S(2)}, u32[]{:S(2)}) collective-permute-start(bf16[144,1024]{1,0:T(8,128)(2,1)S(1)} %collective-permute-done.13.start_two.refs_2_), channel_id=1, source_target_pairs={{0,2},{2,0},{4,6},{6,4},{8,10},{10,8},{12,14},{14,12},{1,3},{3,1},... | collective-permute-start | bytes 884744 | tf_op jit(solution)/shard_map/ppermute | solution.py:465
  110.7 7.1 %collective-permute-start.25 = (bf16[144,1024]{1,0:T(8,128)(2,1)S(1)}, bf16[144,1024]{1,0:T(8,128)(2,1)S(1)}, u32[]{:S(2)}, u32[]{:S(2)}) collective-permute-start(bf16[144,1024]{1,0:T(8,128)(2,1)S(1)} %collective-permute-done.19.start_three.mine), channel_id=1, source_target_pairs={{0,2},{2,0},{4,6},{6,4},{8,10},{10,8},{12,14},{14,12},{1,3},{3,1},... | collective-permute-start | bytes 884744 | tf_op jit(solution)/shard_map/ppermute | solution.py:465
  118.2 13.9 %collective-permute-start.26 = (bf16[128,1024]{1,0:T(8,128)(2,1)S(1)}, bf16[128,1024]{1,0:T(8,128)(2,1)S(1)}, u32[]{:S(2)}, u32[]{:S(2)}) collective-permute-start(bf16[128,1024]{1,0:T(8,128)(2,1)S(1)} %get-tuple-element.29.refs_0_), channel_id=1, source_target_pairs={{0,4},{2,6},{4,0},{6,2},{8,12},{10,14},{12,8},{14,10},{1,5},{3,7},... | collective-permute-start | bytes 786440 | tf_op jit(solution)/shard_map/ppermute | solution.py:461
  118.6 15.1 %collective-permute-start.27 = (bf16[128,1024]{1,0:T(8,128)(2,1)S(1)}, bf16[128,1024]{1,0:T(8,128)(2,1)S(1)}, u32[]{:S(2)}, u32[]{:S(2)}) collective-permute-start(bf16[128,1024]{1,0:T(8,128)(2,1)S(1)} %get-tuple-element.29.refs_0_), channel_id=1, source_target_pairs={{0,8},{2,10},{4,12},{6,14},{8,0},{10,2},{12,4},{14,6},{1,9},{3,11}... | collective-permute-start | bytes 786440 | tf_op jit(solution)/shard_map/ppermute | solution.py:461
  121.0 12.7 %collective-permute-start.28 = (bf16[128,1024]{1,0:T(8,128)(2,1)S(1)}, bf16[128,1024]{1,0:T(8,128)(2,1)S(1)}, u32[]{:S(2)}, u32[]{:S(2)}) collective-permute-start(bf16[128,1024]{1,0:T(8,128)(2,1)S(1)} %get-tuple-element.29.refs_0_), channel_id=1, source_target_pairs={{0,2},{2,0},{4,6},{6,4},{8,10},{10,8},{12,14},{14,12},{1,3},{3,1},... | collective-permute-start | bytes 786440 | tf_op jit(solution)/shard_map/ppermute | solution.py:465
  132.1 1.6 %collective-permute-start.29 = (bf16[128,1024]{1,0:T(8,128)(2,1)S(1)}, bf16[128,1024]{1,0:T(8,128)(2,1)S(1)}, u32[]{:S(2)}, u32[]{:S(2)}) collective-permute-start(bf16[128,1024]{1,0:T(8,128)(2,1)S(1)} %collective-permute-done.26.refs_1_), channel_id=1, source_target_pairs={{0,2},{2,0},{4,6},{6,4},{8,10},{10,8},{12,14},{14,12},{1,3},{3,1},... | collective-permute-start | bytes 786440 | tf_op jit(solution)/shard_map/ppermute | solution.py:465
  133.7 1.5 %collective-permute-start.30 = (bf16[128,1024]{1,0:T(8,128)(2,1)S(1)}, bf16[128,1024]{1,0:T(8,128)(2,1)S(1)}, u32[]{:S(2)}, u32[]{:S(2)}) collective-permute-start(bf16[128,1024]{1,0:T(8,128)(2,1)S(1)} %collective-permute-done.27.refs_2_), channel_id=1, source_target_pairs={{0,2},{2,0},{4,6},{6,4},{8,10},{10,8},{12,14},{14,12},{1,3},{3,1},... | collective-permute-start | bytes 786440 | tf_op jit(solution)/shard_map/ppermute | solution.py:465
  133.7 8.7 %collective-permute-start.31 = (bf16[128,1024]{1,0:T(8,128)(2,1)S(1)}, bf16[128,1024]{1,0:T(8,128)(2,1)S(1)}, u32[]{:S(2)}, u32[]{:S(2)}) collective-permute-start(bf16[128,1024]{1,0:T(8,128)(2,1)S(1)} %collective-permute-done.27.refs_2_), channel_id=1, source_target_pairs={{0,4},{2,6},{4,0},{6,2},{8,12},{10,14},{12,8},{14,10},{1,5},{3,7},... | collective-permute-start | bytes 786440 | tf_op jit(solution)/shard_map/ppermute | solution.py:461
  142.4 1.5 %collective-permute-start.32 = (bf16[128,1024]{1,0:T(8,128)(2,1)S(1)}, bf16[128,1024]{1,0:T(8,128)(2,1)S(1)}, u32[]{:S(2)}, u32[]{:S(2)}) collective-permute-start(bf16[128,1024]{1,0:T(8,128)(2,1)S(1)} %collective-permute-done.31.mine), channel_id=1, source_target_pairs={{0,2},{2,0},{4,6},{6,4},{8,10},{10,8},{12,14},{14,12},{1,3},{3,1},... | collective-permute-start | bytes 786440 | tf_op jit(solution)/shard_map/ppermute | solution.py:465

commit v12 on v10

--- a/solution.py
+++ b/solution.py
@@ -470,13 +470,13 @@
     green_three = to_chip(two[:rows], 1)
     two_theirs = to_core(two)
 
+    start = after(walker_major(orbitals), one_x, two_theirs)
+    start_two, start_one = to_chip(start, 2), to_chip(start, 1)
+    one_x_theirs = to_core(one_x)
+
+    green_three = after(green_three, one_x_theirs)
     bias = chip_bias((green_blocks, one, two, green_three), half_chol, half_theirs)
-    bias_theirs = to_core(after(bias, two_theirs))
-    bias_shift, field = chip_field(bias, bias_theirs, constants, constants_theirs, vectors)
-    one_x_theirs = to_core(after(one_x, field))
-
-    start = after(walker_major(orbitals), one_x_theirs)
-    start_two, start_one = to_chip(start, 2), to_chip(start, 1)
+    bias_shift, field = chip_field(bias, to_core(bias), constants, constants_theirs, vectors)
     two_x_theirs = to_core(two_x)
     three_x, three_theirs = across(three), to_core(three)
     late_field = after(field, two_x_theirs, three_theirs)

time: 132 us -> 150 us (1.14)
  waiting for transfers between devices: 92.2 us -> 107 us
  starting transfers between devices: 22.3 us -> 25.7 us
    ppermute x13, waiting for transfers between devices: 75 us -> 85.5 us  [to_chip(): return lax.ppermute(value, 'chol', [(i, i ^ 2 * step) for i in range(8)])]
    ppermute x3, waiting for transfers between devices: 10.4 us -> 15.4 us  [across(): return lax.ppermute(value, 'walk', [(0, 1), (1, 0)])]
    ppermute x13, starting transfers between devices: 17.6 us -> 19.1 us  [to_chip(): return lax.ppermute(value, 'chol', [(i, i ^ 2 * step) for i in range(8)])]
  transfers between devices with their start and end apart: 34 -> 34, of which waited for: 16 -> 16; matrix products, arithmetic and copies ran while one was open for 0% -> 0% of each run, Pallas kernels for 11% -> 9%
where the time goes in v12:
time: 150 us
  waiting for transfers between devices  107 us (71%)
  starting transfers between devices  25.7 us (17%)
  Pallas kernels  15.5 us (10%)
    ppermute x13, waiting for transfers between devices, to_chip(): return lax.ppermute(value, 'chol', [(i, i ^ 2 * step) for i in range(8)])  85.5 us
    ppermute x13, starting transfers between devices, to_chip(): return lax.ppermute(value, 'chol', [(i, i ^ 2 * step) for i in range(8)])  19.1 us
    ppermute x3, waiting for transfers between devices, across(): return lax.ppermute(value, 'walk', [(0, 1), (1, 0)])  15.4 us
    ppermute x18, waiting for transfers between devices, to_core(): return lax.ppermute(value, 'chol', [(i, i ^ 1) for i in range(8)])  6.48 us
    pallas_call x1, Pallas kernels, early_operator(): pl.pallas_call(functools.partial(early_kernel, walkers), out_shape=jax.Sh...  4.36 us
    pallas_call x1, Pallas kernels, packed(): pl.pallas_call(pack_kernel, out_shape=[jax.ShapeDtypeStruct(shape, narrow...  4.35 us
    ppermute x3, starting transfers between devices, across(): return lax.ppermute(value, 'walk', [(0, 1), (1, 0)])  3.83 us
  transfers between devices with their start and end apart: 34, of which 16 were waited for; matrix products, arithmetic and copies ran while one was open for 0% of the time, Pallas kernels for 9%

profile of v12, /device:TPU:0, one launch (start us, length us, event | category | flops | bytes accessed | tf_op | source)
XLA Modules:
  0.0 149.9 jit_solution(4592804555961992387)
XLA Ops:
  0.7 0.5 collective-permute-start.5
  1.2 4.3 %packed.1 = (bf16[384,1024]{1,0:T(8,128)(2,1)}, bf16[384,1024]{1,0:T(8,128)(2,1)}, bf16[256,1024]{1,0:T(8,128)(2,1)}, bf16[2,128,1024]{2,1,0:T(8,128)(2,1)}, bf16[2,128,1024]{2,1,0:T(8,128)(2,1)}) custom-call(bf16[2,1024,1024]{2,1,0:T(8,128)(2,1)} %full_ref.1, bf16[4,128,256]{2,1,0:T(8,128)(2,1)} %here_ref.1), custom_call_target="tpu_custom_call" | custom-call | tf_op jit(solution)/shard_map/packed/pallas_call | solution.py:114
  5.5 2.7 %collective-permute-start = (bf16[384,1024]{1,0:T(8,128)(2,1)}, bf16[384,1024]{1,0:T(8,128)(2,1)S(1)}, u32[]{:S(2)}, u32[]{:S(2)}) collective-permute-start(bf16[384,1024]{1,0:T(8,128)(2,1)} %get-tuple-element.19), channel_id=1, source_target_pairs={{0,4},{2,6},{4,0},{6,2},{8,12},{10,14},{12,8},{14,10},{1,5},{3,7},... | collective-permute-start | bytes 2359304 | tf_op jit(solution)/shard_map/ppermute | solution.py:443
  8.2 0.2 collective-permute-start.10
  8.5 0.1 reshape.12
  8.6 0.1 reshape.11
  8.7 0.1 pad_maximum_fusion
  8.8 0.3 collective-permute-start.7
  9.1 1.0 collective-permute-done.7.noise_there_ref
  10.1 0.3 collective-permute-done.10.own_theirs
  10.5 16.2 %collective-permute-done.one_ref.refs_0_ = bf16[384,1024]{1,0:T(8,128)(2,1)S(1)} collective-permute-done((bf16[384,1024]{1,0:T(8,128)(2,1)}, bf16[384,1024]{1,0:T(8,128)(2,1)S(1)}, u32[]{:S(2)}, u32[]{:S(2)}) %collective-permute-start) | collective-permute-done | bytes 786464 | tf_op jit(solution)/shard_map/ppermute | solution.py:443
  26.6 2.8 %collective-permute-start.1 = (bf16[384,1024]{1,0:T(8,128)(2,1)}, bf16[384,1024]{1,0:T(8,128)(2,1)S(1)}, u32[]{:S(2)}, u32[]{:S(2)}) collective-permute-start(bf16[384,1024]{1,0:T(8,128)(2,1)} %get-tuple-element.20), channel_id=1, source_target_pairs={{0,8},{2,10},{4,12},{6,14},{8,0},{10,2},{12,4},{14,6},{1,9},{3,11}... | collective-permute-start | bytes 2359304 | tf_op jit(solution)/shard_map/ppermute | solution.py:443
  29.4 1.6 %collective-permute-start.3 = (bf16[256,1024]{1,0:T(8,128)(2,1)S(1)}, bf16[256,1024]{1,0:T(8,128)(2,1)S(1)}, u32[]{:S(2)}, u32[]{:S(2)}) collective-permute-start(bf16[256,1024]{1,0:T(8,128)(2,1)S(1)} %slice.13), channel_id=1, source_target_pairs={{0,1},{1,0},{2,3},{3,2},{4,5},{5,4},{6,7},{7,6},{8,9},{9,8},{10,11... | collective-permute-start | bytes 1572872 | tf_op jit(solution)/shard_map/ppermute | solution.py:451
  31.0 1.7 %collective-permute-start.12 = (bf16[256,1024]{1,0:T(8,128)(2,1)}, bf16[256,1024]{1,0:T(8,128)(2,1)S(1)}, u32[]{:S(2)}, u32[]{:S(2)}) collective-permute-start(bf16[256,1024]{1,0:T(8,128)(2,1)} %get-tuple-element.26), channel_id=1, source_target_pairs={{0,12},{2,14},{4,8},{6,10},{8,4},{10,6},{12,0},{14,2},{1,13},{3,15... | collective-permute-start | bytes 1572872 | tf_op jit(solution)/shard_map/ppermute | solution.py:443
  32.7 43.5 %collective-permute-done.1.two_ref.refs_4_ = bf16[384,1024]{1,0:T(8,128)(2,1)S(1)} collective-permute-done((bf16[384,1024]{1,0:T(8,128)(2,1)}, bf16[384,1024]{1,0:T(8,128)(2,1)S(1)}, u32[]{:S(2)}, u32[]{:S(2)}) %collective-permute-start.1) | collective-permute-done | bytes 786464 | tf_op jit(solution)/shard_map/ppermute | solution.py:443
  76.2 1.7 %collective-permute-start.8 = (bf16[256,1024]{1,0:T(8,128)(2,1)S(1)}, bf16[256,1024]{1,0:T(8,128)(2,1)S(1)}, u32[]{:S(2)}, u32[]{:S(2)}) collective-permute-start(bf16[256,1024]{1,0:T(8,128)(2,1)S(1)} %slice.14), channel_id=1, source_target_pairs={{0,1},{1,0},{2,3},{3,2},{4,5},{5,4},{6,7},{7,6},{8,9},{9,8},{10,11... | collective-permute-start | bytes 1572872 | tf_op jit(solution)/shard_map/ppermute | solution.py:451
  77.9 0.5 collective-permute-start.4
  78.5 0.5 collective-permute-start.2
  79.0 0.5 collective-permute-start.18
  79.5 11.6 %collective-permute-done.8.refs_5_ = bf16[256,1024]{1,0:T(8,128)(2,1)S(1)} collective-permute-done((bf16[256,1024]{1,0:T(8,128)(2,1)S(1)}, bf16[256,1024]{1,0:T(8,128)(2,1)S(1)}, u32[]{:S(2)}, u32[]{:S(2)}) %collective-permute-start.8) | collective-permute-done | bytes 524320 | tf_op jit(solution)/shard_map/ppermute | solution.py:451
  91.1 0.5 collective-permute-start.13
  91.6 1.0 chip_bias.1.mine_ref
  92.7 0.5 walker_major.1.refs_0_
  93.3 0.5 collective-permute-done.6.theirs_ref
  93.9 3.3 %collective-permute-start.21 = (bf16[4,128,256]{2,1,0:T(8,128)(2,1)S(1)}, bf16[4,128,256]{2,1,0:T(8,128)(2,1)S(1)}, u32[]{:S(2)}, u32[]{:S(2)}) collective-permute-start(bf16[4,128,256]{2,1,0:T(8,128)(2,1)S(1)} %walker_major.1.refs_0_), channel_id=1, source_target_pairs={{0,8},{2,10},{4,12},{6,14},{8,0},{10,2},{12,4},{14,6},{1,9},{3,11}... | collective-permute-start | bytes 786440 | tf_op jit(solution)/shard_map/ppermute | solution.py:443
  97.1 3.8 %collective-permute-done.18.refs_1_ = bf16[256,1024]{1,0:T(8,128)(2,1)S(1)} collective-permute-done((bf16[256,1024]{1,0:T(8,128)(2,1)S(1)}, bf16[256,1024]{1,0:T(8,128)(2,1)S(1)}, u32[]{:S(2)}, u32[]{:S(2)}) %collective-permute-start.18) | collective-permute-done | bytes 524320 | tf_op jit(solution)/shard_map/ppermute | solution.py:451
  100.9 0.6 chip_field.1
  101.5 1.1 collective-permute-start.14
  102.5 3.3 %collective-permute-start.15 = (f32[16,128]{1,0:T(8,128)S(1)}, f32[16,128]{1,0:T(8,128)S(1)}, u32[]{:S(2)}, u32[]{:S(2)}) collective-permute-start(f32[16,128]{1,0:T(8,128)S(1)} %get-tuple-element.27.field_here), channel_id=1, source_target_pairs={{0,8},{2,10},{4,12},{6,14},{8,0},{10,2},{12,4},{14,6},{1,9},{3,11}... | collective-permute-start | bytes 24584 | tf_op jit(solution)/shard_map/ppermute | solution.py:443
  105.8 1.7 %collective-permute-done.20.refs_1_ = bf16[4,128,256]{2,1,0:T(8,128)(2,1)S(1)} collective-permute-done((bf16[4,128,256]{2,1,0:T(8,128)(2,1)S(1)}, bf16[4,128,256]{2,1,0:T(8,128)(2,1)S(1)}, u32[]{:S(2)}, u32[]{:S(2)}) %collective-permute-start.20) | collective-permute-done | bytes 262176 | tf_op jit(solution)/shard_map/ppermute | solution.py:443
  107.5 1.2 collective-permute-start.17
  108.7 1.1 collective-permute-done.21.refs_2_
  109.8 0.5 collective-permute-start.23
  110.4 2.5 %collective-permute-done.17.field_ref = f32[16,128]{1,0:T(8,128)S(1)} collective-permute-done((f32[16,128]{1,0:T(8,128)S(1)}, f32[16,128]{1,0:T(8,128)S(1)}, u32[]{:S(2)}, u32[]{:S(2)}) %collective-permute-start.17) | collective-permute-done | bytes 8224 | tf_op jit(solution)/shard_map/ppermute | solution.py:443
  112.9 4.4 %early_operator.1.summed_ref = f32[4,128,1024]{2,1,0:T(8,128)S(1)} custom-call(f32[16,128]{1,0:T(8,128)S(1)} %get-tuple-element.27.field_here, f32[16,128]{1,0:T(8,128)S(1)} %collective-permute-done.14.field_one, f32[16,128]{1,0:T(8,128)S(1)} %collective-permute-done.15.field_two, bf16[2,128,1024]{2,1,0:T(8,128)(2,1)S(1)} %copy-done.3, ...), custom_call_target="tpu_custom_call" | custom-call | tf_op jit(solution)/shard_map/early_operator/pallas_call | solution.py:291
  117.3 1.6 %split_operator.1.operator_ref = bf16[4,256,1024]{2,1,0:T(8,128)(2,1)S(1)} custom-call(f32[4,128,1024]{2,1,0:T(8,128)S(1)} %early_operator.1.summed_ref, f32[16,128]{1,0:T(8,128)S(1)} %collective-permute-done.17.field_ref, bf16[256,1024]{1,0:T(8,128)(2,1)S(1)} %collective-permute-done.12.refs_0_, bf16[256,1024]{1,0:T(8,128)(2,1)S(1)} %collective-permute-done.18.refs_1_, ...), custom_call_target="tpu_custom_call" | custom-call | tf_op jit(solution)/shard_map/split_operator/pallas_call | solution.py:324
  118.9 0.7 near_application.1.partial_ref
  119.8 1.5 %collective-permute-done.26.theirs = bf16[4,128,256]{2,1,0:T(8,128)(2,1)S(1)} collective-permute-done((bf16[4,128,256]{2,1,0:T(8,128)(2,1)S(1)}, bf16[4,128,256]{2,1,0:T(8,128)(2,1)S(1)}, u32[]{:S(2)}, u32[]{:S(2)}) %collective-permute-start.26) | collective-permute-done | bytes 262176 | tf_op jit(solution)/shard_map/ppermute | solution.py:447
  121.3 0.4 first_application.1
  121.6 2.1 %collective-permute-start.27 = (bf16[4,128,256]{2,1,0:T(8,128)(2,1)S(1)}, bf16[4,128,256]{2,1,0:T(8,128)(2,1)S(1)}, u32[]{:S(2)}, u32[]{:S(2)}) collective-permute-start(bf16[4,128,256]{2,1,0:T(8,128)(2,1)S(1)} %get-tuple-element.33.refs_0_), channel_id=1, source_target_pairs={{0,4},{2,6},{4,0},{6,2},{8,12},{10,14},{12,8},{14,10},{1,5},{3,7},... | collective-permute-start | bytes 786440 | tf_op jit(solution)/shard_map/ppermute | solution.py:443
  123.7 0.5 collective-permute-start.28
  124.2 10.4 %collective-permute-done.27.refs_1_ = bf16[4,128,256]{2,1,0:T(8,128)(2,1)S(1)} collective-permute-done((bf16[4,128,256]{2,1,0:T(8,128)(2,1)S(1)}, bf16[4,128,256]{2,1,0:T(8,128)(2,1)S(1)}, u32[]{:S(2)}, u32[]{:S(2)}) %collective-permute-start.27) | collective-permute-done | bytes 262176 | tf_op jit(solution)/shard_map/ppermute | solution.py:443
  134.6 3.8 %collective-permute-done.28.refs_2_ = bf16[4,128,256]{2,1,0:T(8,128)(2,1)S(1)} collective-permute-done((bf16[4,128,256]{2,1,0:T(8,128)(2,1)S(1)}, bf16[4,128,256]{2,1,0:T(8,128)(2,1)S(1)}, u32[]{:S(2)}, u32[]{:S(2)}) %collective-permute-start.28) | collective-permute-done | bytes 262176 | tf_op jit(solution)/shard_map/ppermute | solution.py:443
  138.4 1.5 %collective-permute-done.31.refs_5_ = bf16[4,128,256]{2,1,0:T(8,128)(2,1)S(1)} collective-permute-done((bf16[4,128,256]{2,1,0:T(8,128)(2,1)S(1)}, bf16[4,128,256]{2,1,0:T(8,128)(2,1)S(1)}, u32[]{:S(2)}, u32[]{:S(2)}) %collective-permute-start.31) | collective-permute-done | bytes 262176 | tf_op jit(solution)/shard_map/ppermute | solution.py:447
  139.9 0.8 base_application.1.base_ref
  140.7 6.4 %collective-permute-done.32.mine = bf16[4,128,256]{2,1,0:T(8,128)(2,1)S(1)} collective-permute-done((bf16[4,128,256]{2,1,0:T(8,128)(2,1)S(1)}, bf16[4,128,256]{2,1,0:T(8,128)(2,1)S(1)}, u32[]{:S(2)}, u32[]{:S(2)}) %collective-permute-start.32) | collective-permute-done | bytes 262176 | tf_op jit(solution)/shard_map/ppermute | solution.py:443
  147.1 1.5 %collective-permute-done.33.theirs = bf16[4,128,256]{2,1,0:T(8,128)(2,1)S(1)} collective-permute-done((bf16[4,128,256]{2,1,0:T(8,128)(2,1)S(1)}, bf16[4,128,256]{2,1,0:T(8,128)(2,1)S(1)}, u32[]{:S(2)}, u32[]{:S(2)}) %collective-permute-start.33) | collective-permute-done | bytes 262176 | tf_op jit(solution)/shard_map/ppermute | solution.py:447
  148.6 1.2 second_application.1
  (50 shorter events, 0.6 us)
Async XLA Ops:
  0.6 7.8 %copy-start.5 = (f32[2]{0:T(128)S(1)}, f32[2]{0:T(128)}, u32[]{:S(2)}) copy-start(f32[2]{0:T(128)} %param.9) | copy-start | bytes 28
  0.6 7.9 %copy-start.4 = (f32[4,2]{0,1:T(2,128)S(1)}, f32[4,2]{0,1:T(2,128)}, u32[]{:S(2)}) copy-start(f32[4,2]{0,1:T(2,128)} %param.10) | copy-start | bytes 100
  0.7 26.0 %collective-permute-start.5 = (bf16[2,1024,256]{2,1,0:T(8,128)(2,1)}, bf16[2,1024,256]{2,1,0:T(8,128)(2,1)S(1)}, u32[]{:S(2)}, u32[]{:S(2)}) collective-permute-start(bf16[2,1024,256]{2,1,0:T(8,128)(2,1)} %mine_ref.1), channel_id=1, source_target_pairs={{0,2},{2,0},{4,6},{6,4},{8,10},{10,8},{12,14},{14,12},{1,3},{3,1},... | collective-permute-start | bytes 3145736 | tf_op jit(solution)/shard_map/ppermute | solution.py:447
  5.5 86.1 %copy-start.1 = (bf16[4,128,256]{2,1,0:T(8,128)(2,1)S(1)}, bf16[4,128,256]{2,1,0:T(8,128)(2,1)}, u32[]{:S(2)}) copy-start(bf16[4,128,256]{2,1,0:T(8,128)(2,1)} %here_ref.1) | copy-start | bytes 786436
  5.5 86.1 %copy-start.2 = (bf16[2,1024,256]{2,1,0:T(8,128)(2,1)S(1)}, bf16[2,1024,256]{2,1,0:T(8,128)(2,1)}, u32[]{:S(2)}) copy-start(bf16[2,1024,256]{2,1,0:T(8,128)(2,1)} %mine_ref.1) | copy-start | bytes 3145732
  5.5 21.1 %collective-permute-start = (bf16[384,1024]{1,0:T(8,128)(2,1)}, bf16[384,1024]{1,0:T(8,128)(2,1)S(1)}, u32[]{:S(2)}, u32[]{:S(2)}) collective-permute-start(bf16[384,1024]{1,0:T(8,128)(2,1)} %get-tuple-element.19), channel_id=1, source_target_pairs={{0,4},{2,6},{4,0},{6,2},{8,12},{10,14},{12,8},{14,10},{1,5},{3,7},... | collective-permute-start | bytes 2359304 | tf_op jit(solution)/shard_map/ppermute | solution.py:443
  8.2 2.3 %collective-permute-start.10 = (bf16[2,128,1024]{2,1,0:T(8,128)(2,1)}, bf16[2,128,1024]{2,1,0:T(8,128)(2,1)}, u32[]{:S(2)}, u32[]{:S(2)}) collective-permute-start(bf16[2,128,1024]{2,1,0:T(8,128)(2,1)} %get-tuple-element.24), channel_id=1, source_target_pairs={{0,2},{2,0},{4,6},{6,4},{8,10},{10,8},{12,14},{14,12},{1,3},{3,1},... | collective-permute-start | bytes 1572872 | tf_op jit(solution)/shard_map/ppermute | solution.py:447
  8.8 1.3 collective-permute-start.7
  26.6 4.4 %collective-permute-start.11 = (bf16[384,1024]{1,0:T(8,128)(2,1)S(1)}, bf16[384,1024]{1,0:T(8,128)(2,1)S(1)}, u32[]{:S(2)}, u32[]{:S(2)}) collective-permute-start(bf16[384,1024]{1,0:T(8,128)(2,1)S(1)} %collective-permute-done.one_ref.refs_0_), channel_id=1, source_target_pairs={{0,2},{2,0},{4,6},{6,4},{8,10},{10,8},{12,14},{14,12},{1,3},{3,1},... | collective-permute-start | bytes 2359304 | tf_op jit(solution)/shard_map/ppermute | solution.py:447
  26.6 49.5 %collective-permute-start.1 = (bf16[384,1024]{1,0:T(8,128)(2,1)}, bf16[384,1024]{1,0:T(8,128)(2,1)S(1)}, u32[]{:S(2)}, u32[]{:S(2)}) collective-permute-start(bf16[384,1024]{1,0:T(8,128)(2,1)} %get-tuple-element.20), channel_id=1, source_target_pairs={{0,8},{2,10},{4,12},{6,14},{8,0},{10,2},{12,4},{14,6},{1,9},{3,11}... | collective-permute-start | bytes 2359304 | tf_op jit(solution)/shard_map/ppermute | solution.py:443
  29.4 48.5 %collective-permute-start.3 = (bf16[256,1024]{1,0:T(8,128)(2,1)S(1)}, bf16[256,1024]{1,0:T(8,128)(2,1)S(1)}, u32[]{:S(2)}, u32[]{:S(2)}) collective-permute-start(bf16[256,1024]{1,0:T(8,128)(2,1)S(1)} %slice.13), channel_id=1, source_target_pairs={{0,1},{1,0},{2,3},{3,2},{4,5},{5,4},{6,7},{7,6},{8,9},{9,8},{10,11... | collective-permute-start | bytes 1572872 | tf_op jit(solution)/shard_map/ppermute | solution.py:451
  31.0 48.0 %collective-permute-start.12 = (bf16[256,1024]{1,0:T(8,128)(2,1)}, bf16[256,1024]{1,0:T(8,128)(2,1)S(1)}, u32[]{:S(2)}, u32[]{:S(2)}) collective-permute-start(bf16[256,1024]{1,0:T(8,128)(2,1)} %get-tuple-element.26), channel_id=1, source_target_pairs={{0,12},{2,14},{4,8},{6,10},{8,4},{10,6},{12,0},{14,2},{1,13},{3,15... | collective-permute-start | bytes 1572872 | tf_op jit(solution)/shard_map/ppermute | solution.py:443
  76.2 14.9 %collective-permute-start.8 = (bf16[256,1024]{1,0:T(8,128)(2,1)S(1)}, bf16[256,1024]{1,0:T(8,128)(2,1)S(1)}, u32[]{:S(2)}, u32[]{:S(2)}) collective-permute-start(bf16[256,1024]{1,0:T(8,128)(2,1)S(1)} %slice.14), channel_id=1, source_target_pairs={{0,1},{1,0},{2,3},{3,2},{4,5},{5,4},{6,7},{7,6},{8,9},{9,8},{10,11... | collective-permute-start | bytes 1572872 | tf_op jit(solution)/shard_map/ppermute | solution.py:451
  77.9 15.3 %collective-permute-start.16 = (bf16[384,1024]{1,0:T(8,128)(2,1)S(1)}, bf16[384,1024]{1,0:T(8,128)(2,1)S(1)}, u32[]{:S(2)}, u32[]{:S(2)}) collective-permute-start(bf16[384,1024]{1,0:T(8,128)(2,1)S(1)} %collective-permute-done.1.two_ref.refs_4_), channel_id=1, source_target_pairs={{0,2},{2,0},{4,6},{6,4},{8,10},{10,8},{12,14},{14,12},{1,3},{3,1},... | collective-permute-start | bytes 2359304 | tf_op jit(solution)/shard_map/ppermute | solution.py:447
  77.9 13.7 %collective-permute-start.4 = (bf16[256,1024]{1,0:T(8,128)(2,1)S(1)}, bf16[256,1024]{1,0:T(8,128)(2,1)S(1)}, u32[]{:S(2)}, u32[]{:S(2)}) collective-permute-start(bf16[256,1024]{1,0:T(8,128)(2,1)S(1)} %collective-permute-done.3.refs_1_), channel_id=1, source_target_pairs={{0,2},{2,0},{4,6},{6,4},{8,10},{10,8},{12,14},{14,12},{1,3},{3,1},... | collective-permute-start | bytes 1572872 | tf_op jit(solution)/shard_map/ppermute | solution.py:447
  78.5 14.2 %copy-start = (f32[1,128,4,256]{3,2,1,0:T(4,128)S(1)}, f32[1,128,4,256]{3,2,1,0:T(4,128)}, u32[]{:S(2)}) copy-start(f32[1,128,4,256]{3,2,1,0:T(4,128)} %orbitals_ref.3) | copy-start | bytes 1572868
  78.5 34.5 %copy-start.3 = (bf16[2,128,1024]{2,1,0:T(8,128)(2,1)S(1)}, bf16[2,128,1024]{2,1,0:T(8,128)(2,1)}, u32[]{:S(2)}) copy-start(bf16[2,128,1024]{2,1,0:T(8,128)(2,1)} %get-tuple-element.28.own) | copy-start | bytes 1572868
  78.5 12.6 %collective-permute-start.2 = (bf16[128,1024]{1,0:T(8,128)(2,1)S(1)}, bf16[128,1024]{1,0:T(8,128)(2,1)S(1)}, u32[]{:S(2)}, u32[]{:S(2)}) collective-permute-start(bf16[128,1024]{1,0:T(8,128)(2,1)S(1)} %slice.12), channel_id=1, source_target_pairs={{0,4},{2,6},{4,0},{6,2},{8,12},{10,14},{12,8},{14,10},{1,5},{3,7},... | collective-permute-start | bytes 786440 | tf_op jit(solution)/shard_map/ppermute | solution.py:443
  79.0 21.9 %collective-permute-start.18 = (bf16[256,1024]{1,0:T(8,128)(2,1)S(1)}, bf16[256,1024]{1,0:T(8,128)(2,1)S(1)}, u32[]{:S(2)}, u32[]{:S(2)}) collective-permute-start(bf16[256,1024]{1,0:T(8,128)(2,1)S(1)} %collective-permute-done.12.refs_0_), channel_id=1, source_target_pairs={{0,1},{1,0},{2,3},{3,2},{4,5},{5,4},{6,7},{7,6},{8,9},{9,8},{10,11... | collective-permute-start | bytes 1572872 | tf_op jit(solution)/shard_map/ppermute | solution.py:451
  91.1 10.4 %collective-permute-start.9 = (bf16[256,1024]{1,0:T(8,128)(2,1)S(1)}, bf16[256,1024]{1,0:T(8,128)(2,1)S(1)}, u32[]{:S(2)}, u32[]{:S(2)}) collective-permute-start(bf16[256,1024]{1,0:T(8,128)(2,1)S(1)} %collective-permute-done.8.refs_5_), channel_id=1, source_target_pairs={{0,2},{2,0},{4,6},{6,4},{8,10},{10,8},{12,14},{14,12},{1,3},{3,1},... | collective-permute-start | bytes 1572872 | tf_op jit(solution)/shard_map/ppermute | solution.py:447
  91.1 10.4 %collective-permute-start.13 = (bf16[256,1024]{1,0:T(8,128)(2,1)S(1)}, bf16[256,1024]{1,0:T(8,128)(2,1)S(1)}, u32[]{:S(2)}, u32[]{:S(2)}) collective-permute-start(bf16[256,1024]{1,0:T(8,128)(2,1)S(1)} %collective-permute-done.12.refs_0_), channel_id=1, source_target_pairs={{0,2},{2,0},{4,6},{6,4},{8,10},{10,8},{12,14},{14,12},{1,3},{3,1},... | collective-permute-start | bytes 1572872 | tf_op jit(solution)/shard_map/ppermute | solution.py:447
  92.6 1.2 collective-permute-start.6
  93.2 14.2 %collective-permute-start.20 = (bf16[4,128,256]{2,1,0:T(8,128)(2,1)S(1)}, bf16[4,128,256]{2,1,0:T(8,128)(2,1)S(1)}, u32[]{:S(2)}, u32[]{:S(2)}) collective-permute-start(bf16[4,128,256]{2,1,0:T(8,128)(2,1)S(1)} %walker_major.1.refs_0_), channel_id=1, source_target_pairs={{0,4},{2,6},{4,0},{6,2},{8,12},{10,14},{12,8},{14,10},{1,5},{3,7},... | collective-permute-start | bytes 786440 | tf_op jit(solution)/shard_map/ppermute | solution.py:443
  93.9 16.0 %collective-permute-start.21 = (bf16[4,128,256]{2,1,0:T(8,128)(2,1)S(1)}, bf16[4,128,256]{2,1,0:T(8,128)(2,1)S(1)}, u32[]{:S(2)}, u32[]{:S(2)}) collective-permute-start(bf16[4,128,256]{2,1,0:T(8,128)(2,1)S(1)} %walker_major.1.refs_0_), channel_id=1, source_target_pairs={{0,8},{2,10},{4,12},{6,14},{8,0},{10,2},{12,4},{14,6},{1,9},{3,11}... | collective-permute-start | bytes 786440 | tf_op jit(solution)/shard_map/ppermute | solution.py:443
  100.9 16.4 %collective-permute-start.19 = (bf16[256,1024]{1,0:T(8,128)(2,1)S(1)}, bf16[256,1024]{1,0:T(8,128)(2,1)S(1)}, u32[]{:S(2)}, u32[]{:S(2)}) collective-permute-start(bf16[256,1024]{1,0:T(8,128)(2,1)S(1)} %collective-permute-done.18.refs_1_), channel_id=1, source_target_pairs={{0,2},{2,0},{4,6},{6,4},{8,10},{10,8},{12,14},{14,12},{1,3},{3,1},... | collective-permute-start | bytes 1572872 | tf_op jit(solution)/shard_map/ppermute | solution.py:447
  101.5 8.3 %collective-permute-start.14 = (f32[16,128]{1,0:T(8,128)S(1)}, f32[16,128]{1,0:T(8,128)S(1)}, u32[]{:S(2)}, u32[]{:S(2)}) collective-permute-start(f32[16,128]{1,0:T(8,128)S(1)} %get-tuple-element.27.field_here), channel_id=1, source_target_pairs={{0,4},{2,6},{4,0},{6,2},{8,12},{10,14},{12,8},{14,10},{1,5},{3,7},... | collective-permute-start | bytes 24584 | tf_op jit(solution)/shard_map/ppermute | solution.py:443
  102.5 7.8 %collective-permute-start.15 = (f32[16,128]{1,0:T(8,128)S(1)}, f32[16,128]{1,0:T(8,128)S(1)}, u32[]{:S(2)}, u32[]{:S(2)}) collective-permute-start(f32[16,128]{1,0:T(8,128)S(1)} %get-tuple-element.27.field_here), channel_id=1, source_target_pairs={{0,8},{2,10},{4,12},{6,14},{8,0},{10,2},{12,4},{14,6},{1,9},{3,11}... | collective-permute-start | bytes 24584 | tf_op jit(solution)/shard_map/ppermute | solution.py:443
  107.5 5.4 %collective-permute-start.17 = (f32[16,128]{1,0:T(8,128)S(1)}, f32[16,128]{1,0:T(8,128)S(1)}, u32[]{:S(2)}, u32[]{:S(2)}) collective-permute-start(f32[16,128]{1,0:T(8,128)S(1)} %get-tuple-element.27.field_here), channel_id=1, source_target_pairs={{0,12},{2,14},{4,8},{6,10},{8,4},{10,6},{12,0},{14,2},{1,13},{3,15... | collective-permute-start | bytes 24584 | tf_op jit(solution)/shard_map/ppermute | solution.py:443
  109.8 9.1 %collective-permute-start.22 = (bf16[4,128,256]{2,1,0:T(8,128)(2,1)S(1)}, bf16[4,128,256]{2,1,0:T(8,128)(2,1)S(1)}, u32[]{:S(2)}, u32[]{:S(2)}) collective-permute-start(bf16[4,128,256]{2,1,0:T(8,128)(2,1)S(1)} %walker_major.1.refs_0_), channel_id=1, source_target_pairs={{0,2},{2,0},{4,6},{6,4},{8,10},{10,8},{12,14},{14,12},{1,3},{3,1},... | collective-permute-start | bytes 786440 | tf_op jit(solution)/shard_map/ppermute | solution.py:447
  109.8 9.1 %collective-permute-start.23 = (bf16[4,128,256]{2,1,0:T(8,128)(2,1)S(1)}, bf16[4,128,256]{2,1,0:T(8,128)(2,1)S(1)}, u32[]{:S(2)}, u32[]{:S(2)}) collective-permute-start(bf16[4,128,256]{2,1,0:T(8,128)(2,1)S(1)} %collective-permute-done.20.refs_1_), channel_id=1, source_target_pairs={{0,2},{2,0},{4,6},{6,4},{8,10},{10,8},{12,14},{14,12},{1,3},{3,1},... | collective-permute-start | bytes 786440 | tf_op jit(solution)/shard_map/ppermute | solution.py:447
  110.3 8.6 %collective-permute-start.24 = (bf16[4,128,256]{2,1,0:T(8,128)(2,1)S(1)}, bf16[4,128,256]{2,1,0:T(8,128)(2,1)S(1)}, u32[]{:S(2)}, u32[]{:S(2)}) collective-permute-start(bf16[4,128,256]{2,1,0:T(8,128)(2,1)S(1)} %collective-permute-done.21.refs_2_), channel_id=1, source_target_pairs={{0,2},{2,0},{4,6},{6,4},{8,10},{10,8},{12,14},{14,12},{1,3},{3,1},... | collective-permute-start | bytes 786440 | tf_op jit(solution)/shard_map/ppermute | solution.py:447
  112.9 6.7 %collective-permute-start.25 = (bf16[4,128,256]{2,1,0:T(8,128)(2,1)S(1)}, bf16[4,128,256]{2,1,0:T(8,128)(2,1)S(1)}, u32[]{:S(2)}, u32[]{:S(2)}) collective-permute-start(bf16[4,128,256]{2,1,0:T(8,128)(2,1)S(1)} %collective-permute-done.21.refs_2_), channel_id=1, source_target_pairs={{0,4},{2,6},{4,0},{6,2},{8,12},{10,14},{12,8},{14,10},{1,5},{3,7},... | collective-permute-start | bytes 786440 | tf_op jit(solution)/shard_map/ppermute | solution.py:443
  119.7 1.6 %collective-permute-start.26 = (bf16[4,128,256]{2,1,0:T(8,128)(2,1)S(1)}, bf16[4,128,256]{2,1,0:T(8,128)(2,1)S(1)}, u32[]{:S(2)}, u32[]{:S(2)}) collective-permute-start(bf16[4,128,256]{2,1,0:T(8,128)(2,1)S(1)} %collective-permute-done.25.mine), channel_id=1, source_target_pairs={{0,2},{2,0},{4,6},{6,4},{8,10},{10,8},{12,14},{14,12},{1,3},{3,1},... | collective-permute-start | bytes 786440 | tf_op jit(solution)/shard_map/ppermute | solution.py:447
  121.6 13.0 %collective-permute-start.27 = (bf16[4,128,256]{2,1,0:T(8,128)(2,1)S(1)}, bf16[4,128,256]{2,1,0:T(8,128)(2,1)S(1)}, u32[]{:S(2)}, u32[]{:S(2)}) collective-permute-start(bf16[4,128,256]{2,1,0:T(8,128)(2,1)S(1)} %get-tuple-element.33.refs_0_), channel_id=1, source_target_pairs={{0,4},{2,6},{4,0},{6,2},{8,12},{10,14},{12,8},{14,10},{1,5},{3,7},... | collective-permute-start | bytes 786440 | tf_op jit(solution)/shard_map/ppermute | solution.py:443
  123.7 14.6 %collective-permute-start.28 = (bf16[4,128,256]{2,1,0:T(8,128)(2,1)S(1)}, bf16[4,128,256]{2,1,0:T(8,128)(2,1)S(1)}, u32[]{:S(2)}, u32[]{:S(2)}) collective-permute-start(bf16[4,128,256]{2,1,0:T(8,128)(2,1)S(1)} %get-tuple-element.33.refs_0_), channel_id=1, source_target_pairs={{0,8},{2,10},{4,12},{6,14},{8,0},{10,2},{12,4},{14,6},{1,9},{3,11}... | collective-permute-start | bytes 786440 | tf_op jit(solution)/shard_map/ppermute | solution.py:443
  124.2 14.2 %collective-permute-start.29 = (bf16[4,128,256]{2,1,0:T(8,128)(2,1)S(1)}, bf16[4,128,256]{2,1,0:T(8,128)(2,1)S(1)}, u32[]{:S(2)}, u32[]{:S(2)}) collective-permute-start(bf16[4,128,256]{2,1,0:T(8,128)(2,1)S(1)} %get-tuple-element.33.refs_0_), channel_id=1, source_target_pairs={{0,2},{2,0},{4,6},{6,4},{8,10},{10,8},{12,14},{14,12},{1,3},{3,1},... | collective-permute-start | bytes 786440 | tf_op jit(solution)/shard_map/ppermute | solution.py:447
  134.6 3.8 %collective-permute-start.30 = (bf16[4,128,256]{2,1,0:T(8,128)(2,1)S(1)}, bf16[4,128,256]{2,1,0:T(8,128)(2,1)S(1)}, u32[]{:S(2)}, u32[]{:S(2)}) collective-permute-start(bf16[4,128,256]{2,1,0:T(8,128)(2,1)S(1)} %collective-permute-done.27.refs_1_), channel_id=1, source_target_pairs={{0,2},{2,0},{4,6},{6,4},{8,10},{10,8},{12,14},{14,12},{1,3},{3,1},... | collective-permute-start | bytes 786440 | tf_op jit(solution)/shard_map/ppermute | solution.py:447
  138.4 1.5 %collective-permute-start.31 = (bf16[4,128,256]{2,1,0:T(8,128)(2,1)S(1)}, bf16[4,128,256]{2,1,0:T(8,128)(2,1)S(1)}, u32[]{:S(2)}, u32[]{:S(2)}) collective-permute-start(bf16[4,128,256]{2,1,0:T(8,128)(2,1)S(1)} %collective-permute-done.28.refs_2_), channel_id=1, source_target_pairs={{0,2},{2,0},{4,6},{6,4},{8,10},{10,8},{12,14},{14,12},{1,3},{3,1},... | collective-permute-start | bytes 786440 | tf_op jit(solution)/shard_map/ppermute | solution.py:447
  138.4 8.7 %collective-permute-start.32 = (bf16[4,128,256]{2,1,0:T(8,128)(2,1)S(1)}, bf16[4,128,256]{2,1,0:T(8,128)(2,1)S(1)}, u32[]{:S(2)}, u32[]{:S(2)}) collective-permute-start(bf16[4,128,256]{2,1,0:T(8,128)(2,1)S(1)} %collective-permute-done.28.refs_2_), channel_id=1, source_target_pairs={{0,4},{2,6},{4,0},{6,2},{8,12},{10,14},{12,8},{14,10},{1,5},{3,7},... | collective-permute-start | bytes 786440 | tf_op jit(solution)/shard_map/ppermute | solution.py:443
  147.1 1.5 %collective-permute-start.33 = (bf16[4,128,256]{2,1,0:T(8,128)(2,1)S(1)}, bf16[4,128,256]{2,1,0:T(8,128)(2,1)S(1)}, u32[]{:S(2)}, u32[]{:S(2)}) collective-permute-start(bf16[4,128,256]{2,1,0:T(8,128)(2,1)S(1)} %collective-permute-done.32.mine), channel_id=1, source_target_pairs={{0,2},{2,0},{4,6},{6,4},{8,10},{10,8},{12,14},{14,12},{1,3},{3,1},... | collective-permute-start | bytes 786440 | tf_op jit(solution)/shard_map/ppermute | solution.py:447

commit v13 on v9

--- a/solution.py
+++ b/solution.py
@@ -65,6 +65,7 @@
 narrow = jnp.bfloat16
 small = pltpu.CompilerParams(vmem_limit_bytes=8 << 20)
 large = pltpu.CompilerParams(vmem_limit_bytes=16 << 20)
+long = pl.CostEstimate(flops=10**11, bytes_accessed=0, transcendentals=0)
 
 
 def after(value, *others):
@@ -80,26 +81,24 @@
     return lax.bitwise_xor(z, jnp.int32(step))
 
 
-def pack_kernel(full_ref, green_ref, one_ref, two_ref, three_ref, own_ref, cross_ref, sem):
-    z, k, x = place()
+def chip_rows(step, core, rows):
+    z, _, _ = place()
+    return pl.ds(pl.multiple_of((2 * flipped(z, step) + core) * rows, rows), rows)
+
+
+def started(copies, source, target, sem):
+    copies.append(pltpu.make_async_copy(source, target, sem.at[len(copies)]))
+    copies[-1].start()
+
+
+def near_pack_kernel(full_ref, green_ref, one_ref, two_ref, sem):
+    _, k, x = place()
     walkers, rows, occupied = green_ref.shape
     copies = []
-
-    def copy(source, target):
-        copies.append(pltpu.make_async_copy(source, target, sem.at[len(copies)]))
-        copies[-1].start()
-
-    def of_chip(step, core):
-        return pl.ds(pl.multiple_of((2 * flipped(z, step) + core) * rows, rows), rows)
-
-    for step, message, top in ((2, two_ref, rows), (1, one_ref, rows), (3, three_ref, 0)):
+    for step, message in ((2, two_ref), (1, one_ref)):
         for index, core in enumerate((1 - k, k)):
-            copy(
-                full_ref.at[x, of_chip(step, core), :],
-                message.at[pl.ds(top + index * rows, rows), :],
-            )
-    copy(full_ref.at[:, of_chip(0, k), :], own_ref)
-    copy(full_ref.at[:, of_chip(0, 1 - k), :], cross_ref)
+            target = message.at[pl.ds((1 + index) * rows, rows), :]
+            started(copies, full_ref.at[x, chip_rows(step, core, rows), :], target, sem)
     for each in copies:
         each.wait()
     for message in (two_ref, one_ref):
@@ -107,18 +106,44 @@
             message[:rows, w * occupied : (w + 1) * occupied] = green_ref[w]
 
 
-def packed(full_chol, green_blocks):
+def near_packed(full_chol, green_blocks):
     order = full_chol.shape[2]
     rows = green_blocks.shape[1]
-    shapes = [(3 * rows, order), (3 * rows, order), (2 * rows, order)] + [(2, rows, order)] * 2
-    return pl.pallas_call(
-        pack_kernel,
+    return pl.pallas_call(
+        near_pack_kernel,
+        out_shape=[jax.ShapeDtypeStruct((3 * rows, order), narrow)] * 2,
+        in_specs=[hbm_spec, vmem_spec],
+        out_specs=[vmem_spec] * 2,
+        scratch_shapes=[pltpu.SemaphoreType.DMA((4,))],
+        name="near_packed",
+    )(full_chol, green_blocks)
+
+
+def far_pack_kernel(full_ref, three_ref, own_ref, cross_ref, sem):
+    _, k, x = place()
+    rows = own_ref.shape[1]
+    copies = []
+    for index, core in enumerate((1 - k, k)):
+        target = three_ref.at[pl.ds(index * rows, rows), :]
+        started(copies, full_ref.at[x, chip_rows(3, core, rows), :], target, sem)
+    started(copies, full_ref.at[:, chip_rows(0, k, rows), :], own_ref, sem)
+    started(copies, full_ref.at[:, chip_rows(0, 1 - k, rows), :], cross_ref, sem)
+    for each in copies:
+        each.wait()
+
+
+def far_packed(full_chol, rows):
+    order = full_chol.shape[2]
+    shapes = [(2 * rows, order), (2, rows, order), (2, rows, order)]
+    return pl.pallas_call(
+        far_pack_kernel,
         out_shape=[jax.ShapeDtypeStruct(shape, narrow) for shape in shapes],
-        in_specs=[hbm_spec, vmem_spec],
-        out_specs=[vmem_spec] * 5,
-        scratch_shapes=[pltpu.SemaphoreType.DMA((8,))],
-        name="packed",
-    )(full_chol, green_blocks)
+        in_specs=[hbm_spec],
+        out_specs=[vmem_spec] * 3,
+        scratch_shapes=[pltpu.SemaphoreType.DMA((4,))],
+        cost_estimate=long,
+        name="far_packed",
+    )(full_chol)
 
 
 def start_kernel(orbitals_ref, out_ref):
@@ -216,6 +241,7 @@
         in_specs=[vmem_spec] * 4,
         out_specs=[vmem_spec] * 2,
         compiler_params=small,
+        cost_estimate=long,
         name="chip_field",
     )(mine, theirs, noise, noise_there)
 
@@ -294,6 +320,7 @@
         in_specs=[vmem_spec] * (5 + len(blocks)),
         out_specs=vmem_spec,
         compiler_params=large,
+        cost_estimate=long,
         name="early_operator",
     )(*fields, own, own_theirs, *blocks)
 
@@ -333,9 +360,13 @@
 
 def applied(operator_ref, vector_ref, step, mine, theirs):
     z, k, _ = place()
-    _, rows, _ = mine.shape
-    vector_ref[:, pl.ds(pl.multiple_of(k * rows, rows), rows), :] = mine[...]
-    vector_ref[:, pl.ds(pl.multiple_of((1 - k) * rows, rows), rows), :] = theirs[...]
+    for core, refs in ((k, mine), (1 - k, theirs)):
+        first = 0
+        for ref in refs:
+            count, rows, _ = ref.shape
+            here = pl.ds(pl.multiple_of(core * rows, rows), rows)
+            vector_ref[first : first + count, here, :] = ref[...]
+            first += count
     start = pl.multiple_of(flipped(z, step) * 2 * rows, 2 * rows)
 
     def of_walker(w):
@@ -349,30 +380,60 @@
     return of_walker
 
 
-def near_kernel(operator_ref, *refs):
-    pieces, (out_ref, vector_ref) = refs[:6], refs[6:]
+def flat(groups):
+    return [each for group in groups for each in group]
+
+
+def grouped(counts, refs):
+    groups, refs = [], list(refs)
+    for count in counts:
+        groups.append(refs[:count])
+        refs = refs[count:]
+    return groups, refs
+
+
+def near_parts(counts, operator_ref, refs):
+    groups, (out_ref, vector_ref) = grouped(counts, refs)
     parts = [
-        applied(operator_ref, vector_ref.at[step], step, pieces[step], pieces[3 + step])
+        applied(operator_ref, vector_ref.at[step], step, groups[step], groups[3 + step])
         for step in range(3)
     ]
+    return (lambda w: parts[0](w) + parts[1](w) + parts[2](w)), out_ref
+
+
+def near_kernel(counts, operator_ref, *refs):
+    part, out_ref = near_parts(counts, operator_ref, refs)
     for w in range(out_ref.shape[0]):
-        out_ref[w] = parts[0](w) + parts[1](w) + parts[2](w)
-
-
-def near_application(operator, pieces):
-    walkers, rows, occupied = pieces[0].shape
-    return pl.pallas_call(
-        near_kernel,
+        out_ref[w] = part(w)
+
+
+def base_kernel(counts, operator_ref, first_ref, orbitals_ref, *refs):
+    part, out_ref = near_parts(counts, operator_ref, refs)
+    for w in range(first_ref.shape[0]):
+        out_ref[w] = orbitals_ref[0, :, w, :] + first_ref[w] + 0.5 * part(w)
+
+
+def near_application(operator, groups, first_term=None, orbitals=None):
+    walkers, rows = operator.shape[0], operator.shape[1] // 2
+    occupied = groups[0][0].shape[2]
+    counts = [len(group) for group in groups]
+    kernel, name, more = near_kernel, "near_application", ()
+    if first_term is not None:
+        kernel, name, more = base_kernel, "base_application", (first_term, orbitals)
+    pieces = flat(groups)
+    return pl.pallas_call(
+        functools.partial(kernel, counts),
         out_shape=jax.ShapeDtypeStruct((walkers, rows, occupied), wide),
-        in_specs=[vmem_spec] * 7,
+        in_specs=[vmem_spec] * (1 + len(more) + len(pieces)),
         out_specs=vmem_spec,
         scratch_shapes=[pltpu.VMEM((3, walkers, 2 * rows, occupied), narrow)],
         compiler_params=small,
-        name="near_application",
-    )(operator, *pieces)
-
-
-def first_kernel(operator_ref, partial_ref, mine, theirs, first_ref, narrow_ref, vector_ref):
+        name=name,
+    )(operator, *more, *pieces)
+
+
+def first_kernel(counts, operator_ref, partial_ref, *refs):
+    (mine, theirs), (first_ref, narrow_ref, vector_ref) = grouped(counts, refs)
     part = applied(operator_ref, vector_ref, 3, mine, theirs)
     for w in range(first_ref.shape[0]):
         term = partial_ref[w] + part(w)
@@ -381,62 +442,41 @@
 
 
 def first_application(operator, partial, mine, theirs):
-    walkers, rows, occupied = mine.shape
-    return pl.pallas_call(
-        first_kernel,
+    walkers, rows, occupied = partial.shape
+    counts, pieces = [len(mine), len(theirs)], [*mine, *theirs]
+    return pl.pallas_call(
+        functools.partial(first_kernel, counts),
         out_shape=[
             jax.ShapeDtypeStruct((walkers, rows, occupied), wide),
             jax.ShapeDtypeStruct((walkers, rows, occupied), narrow),
         ],
-        in_specs=[vmem_spec] * 4,
+        in_specs=[vmem_spec] * (2 + len(pieces)),
         out_specs=[vmem_spec] * 2,
         scratch_shapes=[pltpu.VMEM((walkers, 2 * rows, occupied), narrow)],
         compiler_params=small,
         name="first_application",
-    )(operator, partial, mine, theirs)
-
-
-def base_kernel(operator_ref, first_ref, orbitals_ref, *refs):
-    pieces, (out_ref, vector_ref) = refs[:6], refs[6:]
-    parts = [
-        applied(operator_ref, vector_ref.at[step], step, pieces[step], pieces[3 + step])
-        for step in range(3)
-    ]
-    for w in range(first_ref.shape[0]):
-        second = parts[0](w) + parts[1](w) + parts[2](w)
-        out_ref[w] = orbitals_ref[0, :, w, :] + first_ref[w] + 0.5 * second
-
-
-def base_application(operator, first_term, orbitals, pieces):
-    walkers, rows, occupied = first_term.shape
-    return pl.pallas_call(
-        base_kernel,
-        out_shape=jax.ShapeDtypeStruct(first_term.shape, wide),
-        in_specs=[vmem_spec] * 9,
-        out_specs=vmem_spec,
-        scratch_shapes=[pltpu.VMEM((3, walkers, 2 * rows, occupied), narrow)],
-        compiler_params=small,
-        name="base_application",
-    )(operator, first_term, orbitals, *pieces)
-
-
-def second_kernel(operator_ref, base_ref, mine, theirs, out_ref, vector_ref):
+    )(operator, partial, *pieces)
+
+
+def second_kernel(counts, operator_ref, base_ref, *refs):
+    (mine, theirs), (out_ref, vector_ref) = grouped(counts, refs)
     part = applied(operator_ref, vector_ref, 3, mine, theirs)
     for w in range(base_ref.shape[0]):
         out_ref[0, :, w, :] = base_ref[w] + 0.5 * part(w)
 
 
 def second_application(operator, base, mine, theirs):
-    walkers, rows, occupied = mine.shape
-    return pl.pallas_call(
-        second_kernel,
+    walkers, rows, occupied = base.shape
+    counts, pieces = [len(mine), len(theirs)], [*mine, *theirs]
+    return pl.pallas_call(
+        functools.partial(second_kernel, counts),
         out_shape=jax.ShapeDtypeStruct((1, rows, walkers, occupied), wide),
-        in_specs=[vmem_spec] * 4,
+        in_specs=[vmem_spec] * (2 + len(pieces)),
         out_specs=vmem_spec,
         scratch_shapes=[pltpu.VMEM((walkers, 2 * rows, occupied), narrow)],
         compiler_params=small,
         name="second_application",
-    )(operator, base, mine, theirs)
+    )(operator, base, *pieces)
 
 
 def to_chip(value, step):
@@ -455,51 +495,73 @@
     walkers, rows, _ = green_blocks.shape
     vectors = half_chol.shape[0]
 
-    half_theirs = to_core(half_chol)
     constants = jnp.concatenate([noise_draws.T.reshape(-1), jnp.repeat(meanfield, walkers)])
     constants = jnp.broadcast_to(constants[:, None], (2 * vectors * walkers, 128))
     constants_theirs = to_core(constants)
-    one, two, three, own, own_cross = packed(full_chol, green_blocks)
-    two, one = to_chip(two, 2), to_chip(one, 1)
-    own_theirs = to_core(own_cross)
-    three = to_chip(after(three, one, half_theirs, own_theirs, constants_theirs), 3)
-    green_three = to_chip(two[:rows], 1)
-
-    one_x, two_x, three_x = across(one[rows:]), across(two[rows:]), across(three)
-    messages = {1: (one, one_x), 2: (two, two_x), 3: (three, three_x)}
-    blocks = {step: [*both, *[to_core(each) for each in both]] for step, both in messages.items()}
-
-    bias = chip_bias((green_blocks, one, two, green_three), half_chol, half_theirs)
-    bias_shift, field = chip_field(bias, to_core(bias), constants, constants_theirs, vectors)
-    field_one, field_two, field_three = (to_chip(field, step) for step in (1, 2, 3))
-
-    start = after(walker_major(orbitals), field_two, blocks[1][2], blocks[2][2])
-    start_two, start_one = to_chip(start, 2), to_chip(start, 1)
-    start_three = to_chip(after(start_two, blocks[1][3], blocks[2][3], blocks[3][2]), 1)
-
+
+    near_messages = near_packed(full_chol, green_blocks)
+    one, two = to_chip(near_messages[0], 1), to_chip(near_messages[1], 2)
+    far_messages = far_packed(after(full_chol, *near_messages), rows)
+    own = far_messages[1]
+    green_three = to_chip(after(two, one, *far_messages)[:rows], 1)
+    one_theirs = to_core(after(one, two, *far_messages))
+    start = walker_major(orbitals)
+    two_theirs = to_core(after(two, one, *far_messages, start))
+    half_theirs = to_core(half_chol)
+
+    bias = chip_bias(
+        (green_blocks, one, two, after(green_three, one_theirs, two_theirs, start)),
+        half_chol,
+        half_theirs,
+    )
+
+    one_x = across(after(one, two, *far_messages)[rows:])
+    one_x_theirs = to_core(one_x)
+    two_x = across(after(two, one, *far_messages)[rows:])
+    two_x_theirs = to_core(two_x)
+    own_theirs = to_core(far_messages[2])
+    three = after(far_messages[0], half_theirs, own_theirs, constants_theirs, one, two)
+    three = to_chip(three, 3)
+    three_theirs = to_core(three)
+    bias_theirs = to_core(bias)
+
+    bias = after(bias, one_x_theirs, two_x_theirs, three_theirs)
+    bias_shift, field = chip_field(bias, bias_theirs, constants, constants_theirs, vectors)
+    field_one, field_two = to_chip(field, 1), to_chip(field, 2)
     summed = early_operator(
         walkers,
         (field, field_one, field_two),
         own,
         own_theirs,
-        (*blocks[1], *blocks[2]),
-    )
-    operator = split_operator(summed, field_three, blocks[3])
-
-    near = [start, start_one, start_two]
-    partial = near_application(operator, [*near, *[to_core(piece) for piece in near]])
-    first_term, first_narrow = first_application(
-        operator, partial, start_three, to_core(after(start_three, partial))
-    )
-    first_two, first_one = to_chip(first_narrow, 2), to_chip(first_narrow, 1)
-    first_three = to_chip(first_two, 1)
-    near = [first_narrow, first_one, first_two]
-    base = base_application(
-        operator, first_term, orbitals, [*near, *[to_core(piece) for piece in near]]
-    )
-    walkers_next = second_application(
-        operator, base, first_three, to_core(after(first_three, base))
-    )
+        (one, one_x, one_theirs, one_x_theirs, two, two_x, two_theirs, two_x_theirs),
+    )
+    field_three = to_chip(field, 3)
+    three_x = across(three)
+    three_x_theirs = to_core(after(three_x, field_one, field_two))
+    operator = split_operator(
+        summed, field_three, (three, three_x, three_theirs, three_x_theirs)
+    )
+
+    start_one, start_two = to_chip(after(start, one_x), 1), to_chip(after(start, one_x), 2)
+    theirs = [to_core(start), to_core(after(start_one, bias_shift, field)), to_core(start_two)]
+    groups = [[each] for each in (start, start_one, start_two, *theirs)]
+    partial = near_application(operator, groups)
+    start_three = to_chip(start_two, 1)
+    start_three_theirs = to_core(after(start_three, summed, partial))
+    first_term, first = first_application(
+        operator, partial, [start_three], [start_three_theirs]
+    )
+
+    half = walkers // 2
+    first_one = to_chip(first, 1)
+    first_two = [to_chip(first[:half], 2), to_chip(first[half:], 2)]
+    theirs = [[to_core(first)], [to_core(after(first_one, first_two[0]))]]
+    theirs.append([to_core(each) for each in first_two])
+    groups = [[first], [first_one], first_two, *theirs]
+    base = near_application(operator, groups, first_term, orbitals)
+    first_three = [to_chip(each, 1) for each in first_two]
+    theirs = [to_core(first_three[0]), to_core(after(first_three[1], base))]
+    walkers_next = second_application(operator, base, first_three, theirs)
     return (walkers_next, bias_shift.T)
 
 

time: 144 us -> 124 us (0.86)
  waiting for transfers between devices: 92.4 us -> 77.4 us
  starting transfers between devices: 34.4 us -> 26.5 us
  Pallas kernels: 15.7 us -> 18.4 us
    ppermute x13 -> x15, waiting for transfers between devices: 68 us -> 58.1 us  [to_chip(): return lax.ppermute(value, 'chol', [(i, i ^ 2 * step) for i in range(8)])]
    ppermute x13 -> x15, starting transfers between devices: 27.4 us -> 19.9 us  [to_chip(): return lax.ppermute(value, 'chol', [(i, i ^ 2 * step) for i in range(8)])]
    ppermute x18 -> x20, waiting for transfers between devices: 6.43 us -> 2.55 us  [to_core(): return lax.ppermute(value, 'chol', [(i, i ^ 1) for i in range(8)])]
    pallas_call x5 -> x6, Pallas kernels: 7.43 us -> 9.06 us  [the longest x1 3.45 us: near_packed(): pl.pallas_call(near_pack_kernel, out_shape=[jax.ShapeDtypeStruct((3 * row...]
    ppermute x18 -> x20, starting transfers between devices: 2.35 us -> 3 us  [to_core(): return lax.ppermute(value, 'chol', [(i, i ^ 1) for i in range(8)])]
  transfers between devices with their start and end apart: 34 -> 38, of which waited for: 16 -> 15; matrix products, arithmetic and copies ran while one was open for 0% -> 0% of each run, Pallas kernels for 10% -> 11%
where the time goes in v13:
time: 124 us
  waiting for transfers between devices  77.4 us (62%)
  starting transfers between devices  26.5 us (21%)
  Pallas kernels  18.4 us (15%)
    ppermute x15, waiting for transfers between devices, to_chip(): return lax.ppermute(value, 'chol', [(i, i ^ 2 * step) for i in range(8)])  58.1 us
    ppermute x15, starting transfers between devices, to_chip(): return lax.ppermute(value, 'chol', [(i, i ^ 2 * step) for i in range(8)])  19.9 us
    ppermute x3, waiting for transfers between devices, across(): return lax.ppermute(value, 'walk', [(0, 1), (1, 0)])  16.7 us
    pallas_call x1, Pallas kernels, early_operator(): pl.pallas_call(functools.partial(early_kernel, walkers), out_shape=jax.Sh...  4.4 us
    ppermute x3, starting transfers between devices, across(): return lax.ppermute(value, 'walk', [(0, 1), (1, 0)])  3.58 us
    pallas_call x1, Pallas kernels, near_packed(): pl.pallas_call(near_pack_kernel, out_shape=[jax.ShapeDtypeStruct((3 * row...  3.45 us
    ppermute x20, starting transfers between devices, to_core(): return lax.ppermute(value, 'chol', [(i, i ^ 1) for i in range(8)])  3 us
    ppermute x20, waiting for transfers between devices, to_core(): return lax.ppermute(value, 'chol', [(i, i ^ 1) for i in range(8)])  2.55 us
  transfers between devices with their start and end apart: 38, of which 15 were waited for; matrix products, arithmetic and copies ran while one was open for 0% of the time, Pallas kernels for 11%

profile of v13, /device:TPU:0, one launch (start us, length us, event | category | flops | bytes accessed | tf_op | source)
XLA Modules:
  0.0 123.8 jit_solution(9034294477278339826)
XLA Ops:
  0.6 3.5 %near_packed.1 = (bf16[384,1024]{1,0:T(8,128)(2,1)}, bf16[384,1024]{1,0:T(8,128)(2,1)}) custom-call(bf16[2,1024,1024]{2,1,0:T(8,128)(2,1)} %full_ref.2, bf16[4,128,256]{2,1,0:T(8,128)(2,1)} %here_ref.1), custom_call_target="tpu_custom_call" | custom-call | tf_op jit(solution)/shard_map/near_packed/pallas_call | solution.py:112
  4.1 3.1 %collective-permute-start = (bf16[384,1024]{1,0:T(8,128)(2,1)}, bf16[384,1024]{1,0:T(8,128)(2,1)S(1)}, u32[]{:S(2)}, u32[]{:S(2)}) collective-permute-start(bf16[384,1024]{1,0:T(8,128)(2,1)} %get-tuple-element.24), channel_id=1, source_target_pairs={{0,4},{2,6},{4,0},{6,2},{8,12},{10,14},{12,8},{14,10},{1,5},{3,7},... | collective-permute-start | bytes 2359304 | tf_op jit(solution)/shard_map/ppermute | solution.py:483
  7.2 2.6 %collective-permute-start.1 = (bf16[384,1024]{1,0:T(8,128)(2,1)}, bf16[384,1024]{1,0:T(8,128)(2,1)S(1)}, u32[]{:S(2)}, u32[]{:S(2)}) collective-permute-start(bf16[384,1024]{1,0:T(8,128)(2,1)} %get-tuple-element.25), channel_id=1, source_target_pairs={{0,8},{2,10},{4,12},{6,14},{8,0},{10,2},{12,4},{14,6},{1,9},{3,11}... | collective-permute-start | bytes 2359304 | tf_op jit(solution)/shard_map/ppermute | solution.py:483
  9.8 2.5 %far_packed.1 = (bf16[256,1024]{1,0:T(8,128)(2,1)}, bf16[2,128,1024]{2,1,0:T(8,128)(2,1)}, bf16[2,128,1024]{2,1,0:T(8,128)(2,1)}) custom-call(bf16[2,1024,1024]{2,1,0:T(8,128)(2,1)} %full_ref.2), custom_call_target="tpu_custom_call" | custom-call | flops 99999997952 | tf_op jit(solution)/shard_map/far_packed/pallas_call | solution.py:138
  12.3 0.6 collective-permute-start.10
  13.3 28.3 %collective-permute-done.one_ref.refs_0_ = bf16[384,1024]{1,0:T(8,128)(2,1)S(1)} collective-permute-done((bf16[384,1024]{1,0:T(8,128)(2,1)}, bf16[384,1024]{1,0:T(8,128)(2,1)S(1)}, u32[]{:S(2)}, u32[]{:S(2)}) %collective-permute-start) | collective-permute-done | bytes 786464 | tf_op jit(solution)/shard_map/ppermute | solution.py:483
  41.7 2.5 %collective-permute-done.1.two_ref.refs_4_ = bf16[384,1024]{1,0:T(8,128)(2,1)S(1)} collective-permute-done((bf16[384,1024]{1,0:T(8,128)(2,1)}, bf16[384,1024]{1,0:T(8,128)(2,1)S(1)}, u32[]{:S(2)}, u32[]{:S(2)}) %collective-permute-start.1) | collective-permute-done | bytes 786464 | tf_op jit(solution)/shard_map/ppermute | solution.py:483
  44.2 0.5 collective-permute-start.2
  44.8 1.6 %collective-permute-start.6 = (bf16[256,1024]{1,0:T(8,128)(2,1)S(1)}, bf16[256,1024]{1,0:T(8,128)(2,1)S(1)}, u32[]{:S(2)}, u32[]{:S(2)}) collective-permute-start(bf16[256,1024]{1,0:T(8,128)(2,1)S(1)} %slice.16), channel_id=1, source_target_pairs={{0,1},{1,0},{2,3},{3,2},{4,5},{5,4},{6,7},{7,6},{8,9},{9,8},{10,11... | collective-permute-start | bytes 1572872 | tf_op jit(solution)/shard_map/ppermute | solution.py:491
  46.4 0.5 collective-permute-start.8
  46.9 2.2 %collective-permute-start.12 = (bf16[256,1024]{1,0:T(8,128)(2,1)S(1)}, bf16[256,1024]{1,0:T(8,128)(2,1)S(1)}, u32[]{:S(2)}, u32[]{:S(2)}) collective-permute-start(bf16[256,1024]{1,0:T(8,128)(2,1)S(1)} %copy-done.6), channel_id=1, source_target_pairs={{0,12},{2,14},{4,8},{6,10},{8,4},{10,6},{12,0},{14,2},{1,13},{3,15... | collective-permute-start | bytes 1572872 | tf_op jit(solution)/shard_map/ppermute | solution.py:483
  49.1 0.5 walker_major.1.refs_0_
  49.7 2.1 %collective-permute-done.2.three_ref = bf16[128,1024]{1,0:T(8,128)(2,1)S(1)} collective-permute-done((bf16[128,1024]{1,0:T(8,128)(2,1)S(1)}, bf16[128,1024]{1,0:T(8,128)(2,1)S(1)}, u32[]{:S(2)}, u32[]{:S(2)}) %collective-permute-start.2) | collective-permute-done | bytes 262176 | tf_op jit(solution)/shard_map/ppermute | solution.py:483
  51.9 7.9 %collective-permute-done.6.refs_1_ = bf16[256,1024]{1,0:T(8,128)(2,1)S(1)} collective-permute-done((bf16[256,1024]{1,0:T(8,128)(2,1)S(1)}, bf16[256,1024]{1,0:T(8,128)(2,1)S(1)}, u32[]{:S(2)}, u32[]{:S(2)}) %collective-permute-start.6) | collective-permute-done | bytes 524320 | tf_op jit(solution)/shard_map/ppermute | solution.py:491
  59.8 8.8 %collective-permute-done.8.refs_5_ = bf16[256,1024]{1,0:T(8,128)(2,1)S(1)} collective-permute-done((bf16[256,1024]{1,0:T(8,128)(2,1)S(1)}, bf16[256,1024]{1,0:T(8,128)(2,1)S(1)}, u32[]{:S(2)}, u32[]{:S(2)}) %collective-permute-start.8) | collective-permute-done | bytes 524320 | tf_op jit(solution)/shard_map/ppermute | solution.py:491
  68.6 0.5 collective-permute-start.13
  69.1 2.2 %chip_bias.1.mine_ref = f32[16,128]{1,0:T(8,128)S(1)} custom-call(bf16[4,128,256]{2,1,0:T(8,128)(2,1)S(1)} %copy-done.1, bf16[384,1024]{1,0:T(8,128)(2,1)S(1)} %collective-permute-done.one_ref.refs_0_, bf16[384,1024]{1,0:T(8,128)(2,1)S(1)} %collective-permute-done.1.two_ref.refs_4_, bf16[128,1024]{1,0:T(8,128)(2,1)S(1)} %collective-permute-done.2.three_ref, ...), custom_call_target="tpu_custom_call" | custom-call | tf_op jit(solution)/shard_map/chip_bias/pallas_call | solution.py:206
  71.4 1.8 %collective-permute-start.20 = (bf16[4,128,256]{2,1,0:T(8,128)(2,1)S(1)}, bf16[4,128,256]{2,1,0:T(8,128)(2,1)S(1)}, u32[]{:S(2)}, u32[]{:S(2)}) collective-permute-start(bf16[4,128,256]{2,1,0:T(8,128)(2,1)S(1)} %walker_major.1.refs_0_), channel_id=1, source_target_pairs={{0,4},{2,6},{4,0},{6,2},{8,12},{10,14},{12,8},{14,10},{1,5},{3,7},... | collective-permute-start | bytes 786440 | tf_op jit(solution)/shard_map/ppermute | solution.py:483
  73.4 1.5 %collective-permute-start.18 = (bf16[256,1024]{1,0:T(8,128)(2,1)S(1)}, bf16[256,1024]{1,0:T(8,128)(2,1)S(1)}, u32[]{:S(2)}, u32[]{:S(2)}) collective-permute-start(bf16[256,1024]{1,0:T(8,128)(2,1)S(1)} %collective-permute-done.12.refs_0_), channel_id=1, source_target_pairs={{0,1},{1,0},{2,3},{3,2},{4,5},{5,4},{6,7},{7,6},{8,9},{9,8},{10,11... | collective-permute-start | bytes 1572872 | tf_op jit(solution)/shard_map/ppermute | solution.py:491
  74.9 0.6 chip_field.1
  75.5 0.2 copy-done.3
  75.7 1.9 %collective-permute-start.15 = (f32[16,128]{1,0:T(8,128)S(1)}, f32[16,128]{1,0:T(8,128)S(1)}, u32[]{:S(2)}, u32[]{:S(2)}) collective-permute-start(f32[16,128]{1,0:T(8,128)S(1)} %get-tuple-element.36.field_here), channel_id=1, source_target_pairs={{0,4},{2,6},{4,0},{6,2},{8,12},{10,14},{12,8},{14,10},{1,5},{3,7},... | collective-permute-start | bytes 24584 | tf_op jit(solution)/shard_map/ppermute | solution.py:483
  77.6 1.2 collective-permute-start.16
  78.7 6.0 %collective-permute-done.20.refs_1_ = bf16[4,128,256]{2,1,0:T(8,128)(2,1)S(1)} collective-permute-done((bf16[4,128,256]{2,1,0:T(8,128)(2,1)S(1)}, bf16[4,128,256]{2,1,0:T(8,128)(2,1)S(1)}, u32[]{:S(2)}, u32[]{:S(2)}) %collective-permute-start.20) | collective-permute-done | bytes 262176 | tf_op jit(solution)/shard_map/ppermute | solution.py:483
  84.7 2.3 %collective-permute-start.17 = (f32[16,128]{1,0:T(8,128)S(1)}, f32[16,128]{1,0:T(8,128)S(1)}, u32[]{:S(2)}, u32[]{:S(2)}) collective-permute-start(f32[16,128]{1,0:T(8,128)S(1)} %get-tuple-element.36.field_here), channel_id=1, source_target_pairs={{0,12},{2,14},{4,8},{6,10},{8,4},{10,6},{12,0},{14,2},{1,13},{3,15... | collective-permute-start | bytes 24584 | tf_op jit(solution)/shard_map/ppermute | solution.py:483
  87.0 1.2 collective-permute-done.21.refs_2_
  88.2 0.5 collective-permute-start.24
  88.7 0.2 collective-permute-start.23
  88.9 1.3 %collective-permute-done.17.field_ref = f32[16,128]{1,0:T(8,128)S(1)} collective-permute-done((f32[16,128]{1,0:T(8,128)S(1)}, f32[16,128]{1,0:T(8,128)S(1)}, u32[]{:S(2)}, u32[]{:S(2)}) %collective-permute-start.17) | collective-permute-done | bytes 8224 | tf_op jit(solution)/shard_map/ppermute | solution.py:483
  90.2 4.4 %early_operator.1.summed_ref = f32[4,128,1024]{2,1,0:T(8,128)S(1)} custom-call(f32[16,128]{1,0:T(8,128)S(1)} %get-tuple-element.36.field_here, f32[16,128]{1,0:T(8,128)S(1)} %collective-permute-done.15.field_one, f32[16,128]{1,0:T(8,128)S(1)} %collective-permute-done.16.field_two, bf16[2,128,1024]{2,1,0:T(8,128)(2,1)S(1)} %copy-done.5, ...), custom_call_target="tpu_custom_call" | custom-call | flops 99999997952 | tf_op jit(solution)/shard_map/early_operator/pallas_call | solution.py:317
  94.6 1.6 %split_operator.1.operator_ref = bf16[4,256,1024]{2,1,0:T(8,128)(2,1)S(1)} custom-call(f32[4,128,1024]{2,1,0:T(8,128)S(1)} %early_operator.1.summed_ref, f32[16,128]{1,0:T(8,128)S(1)} %collective-permute-done.17.field_ref, bf16[256,1024]{1,0:T(8,128)(2,1)S(1)} %collective-permute-done.12.refs_0_, bf16[256,1024]{1,0:T(8,128)(2,1)S(1)} %collective-permute-done.18.refs_1_, ...), custom_call_target="tpu_custom_call" | custom-call | tf_op jit(solution)/shard_map/split_operator/pallas_call | solution.py:351
  96.2 0.7 near_application.1.partial_ref
  97.0 0.5 collective-permute-start.26
  97.5 1.2 collective-permute-done.26.refs_1_
  98.7 0.4 first_application.1
  99.1 1.0 collective-permute-start.27
  100.1 2.0 %collective-permute-start.28 = (bf16[2,128,256]{2,1,0:T(8,128)(2,1)S(1)}, bf16[2,128,256]{2,1,0:T(8,128)(2,1)S(1)}, u32[]{:S(2)}, u32[]{:S(2)}) collective-permute-start(bf16[2,128,256]{2,1,0:T(8,128)(2,1)S(1)} %get-tuple-element.47), channel_id=1, source_target_pairs={{0,8},{2,10},{4,12},{6,14},{8,0},{10,2},{12,4},{14,6},{1,9},{3,11}... | collective-permute-start | bytes 393224 | tf_op jit(solution)/shard_map/ppermute | solution.py:483
  102.0 1.0 collective-permute-start.29
  103.1 6.5 %collective-permute-done.28.refs_2_ = bf16[2,128,256]{2,1,0:T(8,128)(2,1)S(1)} collective-permute-done((bf16[2,128,256]{2,1,0:T(8,128)(2,1)S(1)}, bf16[2,128,256]{2,1,0:T(8,128)(2,1)S(1)}, u32[]{:S(2)}, u32[]{:S(2)}) %collective-permute-start.28) | collective-permute-done | bytes 131104 | tf_op jit(solution)/shard_map/ppermute | solution.py:483
  109.6 2.9 %collective-permute-done.27.refs_1_ = bf16[4,128,256]{2,1,0:T(8,128)(2,1)S(1)} collective-permute-done((bf16[4,128,256]{2,1,0:T(8,128)(2,1)S(1)}, bf16[4,128,256]{2,1,0:T(8,128)(2,1)S(1)}, u32[]{:S(2)}, u32[]{:S(2)}) %collective-permute-start.27) | collective-permute-done | bytes 262176 | tf_op jit(solution)/shard_map/ppermute | solution.py:483
  112.5 0.5 collective-permute-start.32
  113.0 1.8 %collective-permute-done.29.refs_3_ = bf16[2,128,256]{2,1,0:T(8,128)(2,1)S(1)} collective-permute-done((bf16[2,128,256]{2,1,0:T(8,128)(2,1)S(1)}, bf16[2,128,256]{2,1,0:T(8,128)(2,1)S(1)}, u32[]{:S(2)}, u32[]{:S(2)}) %collective-permute-start.29) | collective-permute-done | bytes 131104 | tf_op jit(solution)/shard_map/ppermute | solution.py:483
  114.8 0.2 collective-permute-start.35
  115.0 3.7 %collective-permute-done.34.refs_0_ = bf16[2,128,256]{2,1,0:T(8,128)(2,1)S(1)} collective-permute-done((bf16[2,128,256]{2,1,0:T(8,128)(2,1)S(1)}, bf16[2,128,256]{2,1,0:T(8,128)(2,1)S(1)}, u32[]{:S(2)}, u32[]{:S(2)}) %collective-permute-start.34) | collective-permute-done | bytes 131104 | tf_op jit(solution)/shard_map/ppermute | solution.py:483
  118.8 0.8 base_application.1.base_ref
  119.6 1.6 %collective-permute-done.35.refs_1_ = bf16[2,128,256]{2,1,0:T(8,128)(2,1)S(1)} collective-permute-done((bf16[2,128,256]{2,1,0:T(8,128)(2,1)S(1)}, bf16[2,128,256]{2,1,0:T(8,128)(2,1)S(1)}, u32[]{:S(2)}, u32[]{:S(2)}) %collective-permute-start.35) | collective-permute-done | bytes 131104 | tf_op jit(solution)/shard_map/ppermute | solution.py:483
  121.2 1.3 %collective-permute-done.37.refs_3_ = bf16[2,128,256]{2,1,0:T(8,128)(2,1)S(1)} collective-permute-done((bf16[2,128,256]{2,1,0:T(8,128)(2,1)S(1)}, bf16[2,128,256]{2,1,0:T(8,128)(2,1)S(1)}, u32[]{:S(2)}, u32[]{:S(2)}) %collective-permute-start.37) | collective-permute-done | bytes 131104 | tf_op jit(solution)/shard_map/ppermute | solution.py:487
  122.5 1.2 %second_application.1 = f32[1,128,4,256]{3,2,1,0:T(4,128)} custom-call(bf16[4,256,1024]{2,1,0:T(8,128)(2,1)S(1)} %split_operator.1.operator_ref, f32[4,128,256]{2,1,0:T(8,128)S(1)} %base_application.1.base_ref, bf16[2,128,256]{2,1,0:T(8,128)(2,1)S(1)} %collective-permute-done.34.refs_0_, bf16[2,128,256]{2,1,0:T(8,128)(2,1)S(1)} %collective-permute-done.35.refs_1_, ...), custom_call_target="tpu_custom_call" | custom-call | tf_op jit(solution)/shard_map/second_application/pallas_call | solution.py:471
  (66 shorter events, 1.0 us)
Async XLA Ops:
  0.6 9.2 %copy-start.2 = (bf16[2,1024,256]{2,1,0:T(8,128)(2,1)S(1)}, bf16[2,1024,256]{2,1,0:T(8,128)(2,1)}, u32[]{:S(2)}) copy-start(bf16[2,1024,256]{2,1,0:T(8,128)(2,1)} %mine_ref.1) | copy-start | bytes 3145732
  4.1 37.6 %collective-permute-start = (bf16[384,1024]{1,0:T(8,128)(2,1)}, bf16[384,1024]{1,0:T(8,128)(2,1)S(1)}, u32[]{:S(2)}, u32[]{:S(2)}) collective-permute-start(bf16[384,1024]{1,0:T(8,128)(2,1)} %get-tuple-element.24), channel_id=1, source_target_pairs={{0,4},{2,6},{4,0},{6,2},{8,12},{10,14},{12,8},{14,10},{1,5},{3,7},... | collective-permute-start | bytes 2359304 | tf_op jit(solution)/shard_map/ppermute | solution.py:483
  7.2 5.7 %copy-start.8 = (f32[2]{0:T(128)S(1)}, f32[2]{0:T(128)}, u32[]{:S(2)}) copy-start(f32[2]{0:T(128)} %param.9) | copy-start | bytes 28
  7.2 5.9 %copy-start.7 = (f32[4,2]{0,1:T(2,128)S(1)}, f32[4,2]{0,1:T(2,128)}, u32[]{:S(2)}) copy-start(f32[4,2]{0,1:T(2,128)} %param.10) | copy-start | bytes 100
  7.2 37.0 %collective-permute-start.1 = (bf16[384,1024]{1,0:T(8,128)(2,1)}, bf16[384,1024]{1,0:T(8,128)(2,1)S(1)}, u32[]{:S(2)}, u32[]{:S(2)}) collective-permute-start(bf16[384,1024]{1,0:T(8,128)(2,1)} %get-tuple-element.25), channel_id=1, source_target_pairs={{0,8},{2,10},{4,12},{6,14},{8,0},{10,2},{12,4},{14,6},{1,9},{3,11}... | collective-permute-start | bytes 2359304 | tf_op jit(solution)/shard_map/ppermute | solution.py:483
  9.8 37.1 %collective-permute-start.5 = (bf16[2,1024,256]{2,1,0:T(8,128)(2,1)S(1)}, bf16[2,1024,256]{2,1,0:T(8,128)(2,1)}, u32[]{:S(2)}, u32[]{:S(2)}) collective-permute-start(bf16[2,1024,256]{2,1,0:T(8,128)(2,1)S(1)} %copy-done.2), channel_id=1, source_target_pairs={{0,2},{2,0},{4,6},{6,4},{8,10},{10,8},{12,14},{14,12},{1,3},{3,1},... | collective-permute-start | bytes 3145736 | tf_op jit(solution)/shard_map/ppermute | solution.py:487
  12.3 36.8 %copy-start = (f32[1,128,4,256]{3,2,1,0:T(4,128)S(1)}, f32[1,128,4,256]{3,2,1,0:T(4,128)}, u32[]{:S(2)}) copy-start(f32[1,128,4,256]{3,2,1,0:T(4,128)} %orbitals_ref.3) | copy-start | bytes 1572868
  12.3 56.8 %copy-start.1 = (bf16[4,128,256]{2,1,0:T(8,128)(2,1)S(1)}, bf16[4,128,256]{2,1,0:T(8,128)(2,1)}, u32[]{:S(2)}) copy-start(bf16[4,128,256]{2,1,0:T(8,128)(2,1)} %here_ref.1) | copy-start | bytes 786436
  12.3 34.6 %collective-permute-start.10 = (bf16[2,128,1024]{2,1,0:T(8,128)(2,1)}, bf16[2,128,1024]{2,1,0:T(8,128)(2,1)}, u32[]{:S(2)}, u32[]{:S(2)}) collective-permute-start(bf16[2,128,1024]{2,1,0:T(8,128)(2,1)} %get-tuple-element.29), channel_id=1, source_target_pairs={{0,2},{2,0},{4,6},{6,4},{8,10},{10,8},{12,14},{14,12},{1,3},{3,1},... | collective-permute-start | bytes 1572872 | tf_op jit(solution)/shard_map/ppermute | solution.py:487
  13.2 33.8 %copy-start.6 = (bf16[256,1024]{1,0:T(8,128)(2,1)S(1)}, bf16[256,1024]{1,0:T(8,128)(2,1)}, u32[]{:S(2)}) copy-start(bf16[256,1024]{1,0:T(8,128)(2,1)} %get-tuple-element.34) | copy-start | bytes 1572868
  13.3 33.1 %collective-permute-start.11 = (f32[16,128]{1,0:T(8,128)S(1)}, f32[16,128]{1,0:T(8,128)S(1)}, u32[]{:S(2)}, u32[]{:S(2)}) collective-permute-start(f32[16,128]{1,0:T(8,128)S(1)} %broadcast_in_dim.10.noise_ref), channel_id=1, source_target_pairs={{0,2},{2,0},{4,6},{6,4},{8,10},{10,8},{12,14},{14,12},{1,3},{3,1},... | collective-permute-start | bytes 24584 | tf_op jit(solution)/shard_map/ppermute | solution.py:487
  44.2 7.6 %collective-permute-start.2 = (bf16[128,1024]{1,0:T(8,128)(2,1)S(1)}, bf16[128,1024]{1,0:T(8,128)(2,1)S(1)}, u32[]{:S(2)}, u32[]{:S(2)}) collective-permute-start(bf16[128,1024]{1,0:T(8,128)(2,1)S(1)} %slice.15), channel_id=1, source_target_pairs={{0,4},{2,6},{4,0},{6,2},{8,12},{10,14},{12,8},{14,10},{1,5},{3,7},... | collective-permute-start | bytes 786440 | tf_op jit(solution)/shard_map/ppermute | solution.py:483
  44.8 14.9 %collective-permute-start.6 = (bf16[256,1024]{1,0:T(8,128)(2,1)S(1)}, bf16[256,1024]{1,0:T(8,128)(2,1)S(1)}, u32[]{:S(2)}, u32[]{:S(2)}) collective-permute-start(bf16[256,1024]{1,0:T(8,128)(2,1)S(1)} %slice.16), channel_id=1, source_target_pairs={{0,1},{1,0},{2,3},{3,2},{4,5},{5,4},{6,7},{7,6},{8,9},{9,8},{10,11... | collective-permute-start | bytes 1572872 | tf_op jit(solution)/shard_map/ppermute | solution.py:491
  46.4 22.2 %collective-permute-start.8 = (bf16[256,1024]{1,0:T(8,128)(2,1)S(1)}, bf16[256,1024]{1,0:T(8,128)(2,1)S(1)}, u32[]{:S(2)}, u32[]{:S(2)}) collective-permute-start(bf16[256,1024]{1,0:T(8,128)(2,1)S(1)} %slice.17), channel_id=1, source_target_pairs={{0,1},{1,0},{2,3},{3,2},{4,5},{5,4},{6,7},{7,6},{8,9},{9,8},{10,11... | collective-permute-start | bytes 1572872 | tf_op jit(solution)/shard_map/ppermute | solution.py:491
  46.9 21.7 %collective-permute-start.12 = (bf16[256,1024]{1,0:T(8,128)(2,1)S(1)}, bf16[256,1024]{1,0:T(8,128)(2,1)S(1)}, u32[]{:S(2)}, u32[]{:S(2)}) collective-permute-start(bf16[256,1024]{1,0:T(8,128)(2,1)S(1)} %copy-done.6), channel_id=1, source_target_pairs={{0,12},{2,14},{4,8},{6,10},{8,4},{10,6},{12,0},{14,2},{1,13},{3,15... | collective-permute-start | bytes 1572872 | tf_op jit(solution)/shard_map/ppermute | solution.py:483
  49.6 19.5 %collective-permute-start.3 = (bf16[384,1024]{1,0:T(8,128)(2,1)S(1)}, bf16[384,1024]{1,0:T(8,128)(2,1)S(1)}, u32[]{:S(2)}, u32[]{:S(2)}) collective-permute-start(bf16[384,1024]{1,0:T(8,128)(2,1)S(1)} %collective-permute-done.one_ref.refs_0_), channel_id=1, source_target_pairs={{0,2},{2,0},{4,6},{6,4},{8,10},{10,8},{12,14},{14,12},{1,3},{3,1},... | collective-permute-start | bytes 2359304 | tf_op jit(solution)/shard_map/ppermute | solution.py:487
  51.9 17.2 %collective-permute-start.4 = (bf16[384,1024]{1,0:T(8,128)(2,1)S(1)}, bf16[384,1024]{1,0:T(8,128)(2,1)S(1)}, u32[]{:S(2)}, u32[]{:S(2)}) collective-permute-start(bf16[384,1024]{1,0:T(8,128)(2,1)S(1)} %collective-permute-done.1.two_ref.refs_4_), channel_id=1, source_target_pairs={{0,2},{2,0},{4,6},{6,4},{8,10},{10,8},{12,14},{14,12},{1,3},{3,1},... | collective-permute-start | bytes 2359304 | tf_op jit(solution)/shard_map/ppermute | solution.py:487
  59.7 13.5 %collective-permute-start.7 = (bf16[256,1024]{1,0:T(8,128)(2,1)S(1)}, bf16[256,1024]{1,0:T(8,128)(2,1)S(1)}, u32[]{:S(2)}, u32[]{:S(2)}) collective-permute-start(bf16[256,1024]{1,0:T(8,128)(2,1)S(1)} %collective-permute-done.6.refs_1_), channel_id=1, source_target_pairs={{0,2},{2,0},{4,6},{6,4},{8,10},{10,8},{12,14},{14,12},{1,3},{3,1},... | collective-permute-start | bytes 1572872 | tf_op jit(solution)/shard_map/ppermute | solution.py:487
  68.6 4.8 %collective-permute-start.9 = (bf16[256,1024]{1,0:T(8,128)(2,1)S(1)}, bf16[256,1024]{1,0:T(8,128)(2,1)S(1)}, u32[]{:S(2)}, u32[]{:S(2)}) collective-permute-start(bf16[256,1024]{1,0:T(8,128)(2,1)S(1)} %collective-permute-done.8.refs_5_), channel_id=1, source_target_pairs={{0,2},{2,0},{4,6},{6,4},{8,10},{10,8},{12,14},{14,12},{1,3},{3,1},... | collective-permute-start | bytes 1572872 | tf_op jit(solution)/shard_map/ppermute | solution.py:487
  68.6 6.3 %collective-permute-start.13 = (bf16[256,1024]{1,0:T(8,128)(2,1)S(1)}, bf16[256,1024]{1,0:T(8,128)(2,1)S(1)}, u32[]{:S(2)}, u32[]{:S(2)}) collective-permute-start(bf16[256,1024]{1,0:T(8,128)(2,1)S(1)} %collective-permute-done.12.refs_0_), channel_id=1, source_target_pairs={{0,2},{2,0},{4,6},{6,4},{8,10},{10,8},{12,14},{14,12},{1,3},{3,1},... | collective-permute-start | bytes 1572872 | tf_op jit(solution)/shard_map/ppermute | solution.py:487
  71.3 18.8 %copy-start.5 = (bf16[2,128,1024]{2,1,0:T(8,128)(2,1)S(1)}, bf16[2,128,1024]{2,1,0:T(8,128)(2,1)}, u32[]{:S(2)}) copy-start(bf16[2,128,1024]{2,1,0:T(8,128)(2,1)} %get-tuple-element.28.own) | copy-start | bytes 1572868
  71.3 3.6 %collective-permute-start.14 = (f32[16,128]{1,0:T(8,128)S(1)}, f32[16,128]{1,0:T(8,128)S(1)}, u32[]{:S(2)}, u32[]{:S(2)}) collective-permute-start(f32[16,128]{1,0:T(8,128)S(1)} %chip_bias.1.mine_ref), channel_id=1, source_target_pairs={{0,2},{2,0},{4,6},{6,4},{8,10},{10,8},{12,14},{14,12},{1,3},{3,1},... | collective-permute-start | bytes 24584 | tf_op jit(solution)/shard_map/ppermute | solution.py:487
  71.4 13.3 %collective-permute-start.20 = (bf16[4,128,256]{2,1,0:T(8,128)(2,1)S(1)}, bf16[4,128,256]{2,1,0:T(8,128)(2,1)S(1)}, u32[]{:S(2)}, u32[]{:S(2)}) collective-permute-start(bf16[4,128,256]{2,1,0:T(8,128)(2,1)S(1)} %walker_major.1.refs_0_), channel_id=1, source_target_pairs={{0,4},{2,6},{4,0},{6,2},{8,12},{10,14},{12,8},{14,10},{1,5},{3,7},... | collective-permute-start | bytes 786440 | tf_op jit(solution)/shard_map/ppermute | solution.py:483
  73.3 14.9 %collective-permute-start.21 = (bf16[4,128,256]{2,1,0:T(8,128)(2,1)S(1)}, bf16[4,128,256]{2,1,0:T(8,128)(2,1)S(1)}, u32[]{:S(2)}, u32[]{:S(2)}) collective-permute-start(bf16[4,128,256]{2,1,0:T(8,128)(2,1)S(1)} %walker_major.1.refs_0_), channel_id=1, source_target_pairs={{0,8},{2,10},{4,12},{6,14},{8,0},{10,2},{12,4},{14,6},{1,9},{3,11}... | collective-permute-start | bytes 786440 | tf_op jit(solution)/shard_map/ppermute | solution.py:483
  73.4 14.8 %collective-permute-start.18 = (bf16[256,1024]{1,0:T(8,128)(2,1)S(1)}, bf16[256,1024]{1,0:T(8,128)(2,1)S(1)}, u32[]{:S(2)}, u32[]{:S(2)}) collective-permute-start(bf16[256,1024]{1,0:T(8,128)(2,1)S(1)} %collective-permute-done.12.refs_0_), channel_id=1, source_target_pairs={{0,1},{1,0},{2,3},{3,2},{4,5},{5,4},{6,7},{7,6},{8,9},{9,8},{10,11... | collective-permute-start | bytes 1572872 | tf_op jit(solution)/shard_map/ppermute | solution.py:491
  74.9 0.8 copy-start.3
  75.7 13.0 %collective-permute-start.15 = (f32[16,128]{1,0:T(8,128)S(1)}, f32[16,128]{1,0:T(8,128)S(1)}, u32[]{:S(2)}, u32[]{:S(2)}) collective-permute-start(f32[16,128]{1,0:T(8,128)S(1)} %get-tuple-element.36.field_here), channel_id=1, source_target_pairs={{0,4},{2,6},{4,0},{6,2},{8,12},{10,14},{12,8},{14,10},{1,5},{3,7},... | collective-permute-start | bytes 24584 | tf_op jit(solution)/shard_map/ppermute | solution.py:483
  77.6 11.1 %collective-permute-start.16 = (f32[16,128]{1,0:T(8,128)S(1)}, f32[16,128]{1,0:T(8,128)S(1)}, u32[]{:S(2)}, u32[]{:S(2)}) collective-permute-start(f32[16,128]{1,0:T(8,128)S(1)} %get-tuple-element.36.field_here), channel_id=1, source_target_pairs={{0,8},{2,10},{4,12},{6,14},{8,0},{10,2},{12,4},{14,6},{1,9},{3,11}... | collective-permute-start | bytes 24584 | tf_op jit(solution)/shard_map/ppermute | solution.py:483
  84.7 5.4 %collective-permute-start.17 = (f32[16,128]{1,0:T(8,128)S(1)}, f32[16,128]{1,0:T(8,128)S(1)}, u32[]{:S(2)}, u32[]{:S(2)}) collective-permute-start(f32[16,128]{1,0:T(8,128)S(1)} %get-tuple-element.36.field_here), channel_id=1, source_target_pairs={{0,12},{2,14},{4,8},{6,10},{8,4},{10,6},{12,0},{14,2},{1,13},{3,15... | collective-permute-start | bytes 24584 | tf_op jit(solution)/shard_map/ppermute | solution.py:483
  87.0 7.6 %copy-start.4 = (bf16[256,1024]{1,0:T(8,128)(2,1)S(1)}, bf16[256,1024]{1,0:T(8,128)(2,1)}, u32[]{:S(2)}) copy-start(bf16[256,1024]{1,0:T(8,128)(2,1)} %copy-done.3) | copy-start | bytes 1572868
  88.2 8.0 %collective-permute-start.22 = (bf16[4,128,256]{2,1,0:T(8,128)(2,1)S(1)}, bf16[4,128,256]{2,1,0:T(8,128)(2,1)S(1)}, u32[]{:S(2)}, u32[]{:S(2)}) collective-permute-start(bf16[4,128,256]{2,1,0:T(8,128)(2,1)S(1)} %walker_major.1.refs_0_), channel_id=1, source_target_pairs={{0,2},{2,0},{4,6},{6,4},{8,10},{10,8},{12,14},{14,12},{1,3},{3,1},... | collective-permute-start | bytes 786440 | tf_op jit(solution)/shard_map/ppermute | solution.py:487
  88.2 8.0 %collective-permute-start.24 = (bf16[4,128,256]{2,1,0:T(8,128)(2,1)S(1)}, bf16[4,128,256]{2,1,0:T(8,128)(2,1)S(1)}, u32[]{:S(2)}, u32[]{:S(2)}) collective-permute-start(bf16[4,128,256]{2,1,0:T(8,128)(2,1)S(1)} %collective-permute-done.21.refs_2_), channel_id=1, source_target_pairs={{0,2},{2,0},{4,6},{6,4},{8,10},{10,8},{12,14},{14,12},{1,3},{3,1},... | collective-permute-start | bytes 786440 | tf_op jit(solution)/shard_map/ppermute | solution.py:487
  88.7 8.3 %collective-permute-start.25 = (bf16[4,128,256]{2,1,0:T(8,128)(2,1)S(1)}, bf16[4,128,256]{2,1,0:T(8,128)(2,1)S(1)}, u32[]{:S(2)}, u32[]{:S(2)}) collective-permute-start(bf16[4,128,256]{2,1,0:T(8,128)(2,1)S(1)} %collective-permute-done.21.refs_2_), channel_id=1, source_target_pairs={{0,4},{2,6},{4,0},{6,2},{8,12},{10,14},{12,8},{14,10},{1,5},{3,7},... | collective-permute-start | bytes 786440 | tf_op jit(solution)/shard_map/ppermute | solution.py:483
  88.7 7.5 %collective-permute-start.23 = (bf16[4,128,256]{2,1,0:T(8,128)(2,1)S(1)}, bf16[4,128,256]{2,1,0:T(8,128)(2,1)S(1)}, u32[]{:S(2)}, u32[]{:S(2)}) collective-permute-start(bf16[4,128,256]{2,1,0:T(8,128)(2,1)S(1)} %collective-permute-done.20.refs_1_), channel_id=1, source_target_pairs={{0,2},{2,0},{4,6},{6,4},{8,10},{10,8},{12,14},{14,12},{1,3},{3,1},... | collective-permute-start | bytes 786440 | tf_op jit(solution)/shard_map/ppermute | solution.py:487
  90.2 4.4 %collective-permute-start.19 = (bf16[256,1024]{1,0:T(8,128)(2,1)S(1)}, bf16[256,1024]{1,0:T(8,128)(2,1)S(1)}, u32[]{:S(2)}, u32[]{:S(2)}) collective-permute-start(bf16[256,1024]{1,0:T(8,128)(2,1)S(1)} %collective-permute-done.18.refs_1_), channel_id=1, source_target_pairs={{0,2},{2,0},{4,6},{6,4},{8,10},{10,8},{12,14},{14,12},{1,3},{3,1},... | collective-permute-start | bytes 1572872 | tf_op jit(solution)/shard_map/ppermute | solution.py:487
  97.0 1.7 %collective-permute-start.26 = (bf16[4,128,256]{2,1,0:T(8,128)(2,1)S(1)}, bf16[4,128,256]{2,1,0:T(8,128)(2,1)S(1)}, u32[]{:S(2)}, u32[]{:S(2)}) collective-permute-start(bf16[4,128,256]{2,1,0:T(8,128)(2,1)S(1)} %collective-permute-done.25.refs_0_), channel_id=1, source_target_pairs={{0,2},{2,0},{4,6},{6,4},{8,10},{10,8},{12,14},{14,12},{1,3},{3,1},... | collective-permute-start | bytes 786440 | tf_op jit(solution)/shard_map/ppermute | solution.py:487
  99.1 13.4 %collective-permute-start.27 = (bf16[4,128,256]{2,1,0:T(8,128)(2,1)S(1)}, bf16[4,128,256]{2,1,0:T(8,128)(2,1)S(1)}, u32[]{:S(2)}, u32[]{:S(2)}) collective-permute-start(bf16[4,128,256]{2,1,0:T(8,128)(2,1)S(1)} %get-tuple-element.43.refs_0_), channel_id=1, source_target_pairs={{0,4},{2,6},{4,0},{6,2},{8,12},{10,14},{12,8},{14,10},{1,5},{3,7},... | collective-permute-start | bytes 786440 | tf_op jit(solution)/shard_map/ppermute | solution.py:483
  100.1 9.5 %collective-permute-start.28 = (bf16[2,128,256]{2,1,0:T(8,128)(2,1)S(1)}, bf16[2,128,256]{2,1,0:T(8,128)(2,1)S(1)}, u32[]{:S(2)}, u32[]{:S(2)}) collective-permute-start(bf16[2,128,256]{2,1,0:T(8,128)(2,1)S(1)} %get-tuple-element.47), channel_id=1, source_target_pairs={{0,8},{2,10},{4,12},{6,14},{8,0},{10,2},{12,4},{14,6},{1,9},{3,11}... | collective-permute-start | bytes 393224 | tf_op jit(solution)/shard_map/ppermute | solution.py:483
  102.0 12.7 %collective-permute-start.30 = (bf16[4,128,256]{2,1,0:T(8,128)(2,1)S(1)}, bf16[4,128,256]{2,1,0:T(8,128)(2,1)S(1)}, u32[]{:S(2)}, u32[]{:S(2)}) collective-permute-start(bf16[4,128,256]{2,1,0:T(8,128)(2,1)S(1)} %get-tuple-element.43.refs_0_), channel_id=1, source_target_pairs={{0,2},{2,0},{4,6},{6,4},{8,10},{10,8},{12,14},{14,12},{1,3},{3,1},... | collective-permute-start | bytes 786440 | tf_op jit(solution)/shard_map/ppermute | solution.py:487
  102.0 12.7 %collective-permute-start.29 = (bf16[2,128,256]{2,1,0:T(8,128)(2,1)S(1)}, bf16[2,128,256]{2,1,0:T(8,128)(2,1)S(1)}, u32[]{:S(2)}, u32[]{:S(2)}) collective-permute-start(bf16[2,128,256]{2,1,0:T(8,128)(2,1)S(1)} %get-tuple-element.46), channel_id=1, source_target_pairs={{0,8},{2,10},{4,12},{6,14},{8,0},{10,2},{12,4},{14,6},{1,9},{3,11}... | collective-permute-start | bytes 393224 | tf_op jit(solution)/shard_map/ppermute | solution.py:483
  112.5 6.3 %collective-permute-start.31 = (bf16[4,128,256]{2,1,0:T(8,128)(2,1)S(1)}, bf16[4,128,256]{2,1,0:T(8,128)(2,1)S(1)}, u32[]{:S(2)}, u32[]{:S(2)}) collective-permute-start(bf16[4,128,256]{2,1,0:T(8,128)(2,1)S(1)} %collective-permute-done.27.refs_1_), channel_id=1, source_target_pairs={{0,2},{2,0},{4,6},{6,4},{8,10},{10,8},{12,14},{14,12},{1,3},{3,1},... | collective-permute-start | bytes 786440 | tf_op jit(solution)/shard_map/ppermute | solution.py:487
  112.5 6.3 %collective-permute-start.34 = (bf16[2,128,256]{2,1,0:T(8,128)(2,1)S(1)}, bf16[2,128,256]{2,1,0:T(8,128)(2,1)S(1)}, u32[]{:S(2)}, u32[]{:S(2)}) collective-permute-start(bf16[2,128,256]{2,1,0:T(8,128)(2,1)S(1)} %collective-permute-done.28.refs_2_), channel_id=1, source_target_pairs={{0,4},{2,6},{4,0},{6,2},{8,12},{10,14},{12,8},{14,10},{1,5},{3,7},... | collective-permute-start | bytes 393224 | tf_op jit(solution)/shard_map/ppermute | solution.py:483
  112.5 6.3 %collective-permute-start.32 = (bf16[2,128,256]{2,1,0:T(8,128)(2,1)S(1)}, bf16[2,128,256]{2,1,0:T(8,128)(2,1)S(1)}, u32[]{:S(2)}, u32[]{:S(2)}) collective-permute-start(bf16[2,128,256]{2,1,0:T(8,128)(2,1)S(1)} %collective-permute-done.28.refs_2_), channel_id=1, source_target_pairs={{0,2},{2,0},{4,6},{6,4},{8,10},{10,8},{12,14},{14,12},{1,3},{3,1},... | collective-permute-start | bytes 393224 | tf_op jit(solution)/shard_map/ppermute | solution.py:487
  114.8 4.0 %collective-permute-start.33 = (bf16[2,128,256]{2,1,0:T(8,128)(2,1)S(1)}, bf16[2,128,256]{2,1,0:T(8,128)(2,1)S(1)}, u32[]{:S(2)}, u32[]{:S(2)}) collective-permute-start(bf16[2,128,256]{2,1,0:T(8,128)(2,1)S(1)} %collective-permute-done.29.refs_3_), channel_id=1, source_target_pairs={{0,2},{2,0},{4,6},{6,4},{8,10},{10,8},{12,14},{14,12},{1,3},{3,1},... | collective-permute-start | bytes 393224 | tf_op jit(solution)/shard_map/ppermute | solution.py:487
  114.8 6.4 %collective-permute-start.35 = (bf16[2,128,256]{2,1,0:T(8,128)(2,1)S(1)}, bf16[2,128,256]{2,1,0:T(8,128)(2,1)S(1)}, u32[]{:S(2)}, u32[]{:S(2)}) collective-permute-start(bf16[2,128,256]{2,1,0:T(8,128)(2,1)S(1)} %collective-permute-done.29.refs_3_), channel_id=1, source_target_pairs={{0,4},{2,6},{4,0},{6,2},{8,12},{10,14},{12,8},{14,10},{1,5},{3,7},... | collective-permute-start | bytes 393224 | tf_op jit(solution)/shard_map/ppermute | solution.py:483
  118.8 2.4 %collective-permute-start.36 = (bf16[2,128,256]{2,1,0:T(8,128)(2,1)S(1)}, bf16[2,128,256]{2,1,0:T(8,128)(2,1)S(1)}, u32[]{:S(2)}, u32[]{:S(2)}) collective-permute-start(bf16[2,128,256]{2,1,0:T(8,128)(2,1)S(1)} %collective-permute-done.34.refs_0_), channel_id=1, source_target_pairs={{0,2},{2,0},{4,6},{6,4},{8,10},{10,8},{12,14},{14,12},{1,3},{3,1},... | collective-permute-start | bytes 393224 | tf_op jit(solution)/shard_map/ppermute | solution.py:487
  121.2 1.3 %collective-permute-start.37 = (bf16[2,128,256]{2,1,0:T(8,128)(2,1)S(1)}, bf16[2,128,256]{2,1,0:T(8,128)(2,1)S(1)}, u32[]{:S(2)}, u32[]{:S(2)}) collective-permute-start(bf16[2,128,256]{2,1,0:T(8,128)(2,1)S(1)} %collective-permute-done.35.refs_1_), channel_id=1, source_target_pairs={{0,2},{2,0},{4,6},{6,4},{8,10},{10,8},{12,14},{14,12},{1,3},{3,1},... | collective-permute-start | bytes 393224 | tf_op jit(solution)/shard_map/ppermute | solution.py:487

commit v14 on v13

--- a/solution.py
+++ b/solution.py
@@ -119,12 +119,11 @@
     )(full_chol, green_blocks)
 
 
-def far_pack_kernel(full_ref, three_ref, own_ref, cross_ref, sem):
+def far_pack_kernel(full_ref, crossed_ref, straight_ref, own_ref, cross_ref, sem):
     _, k, x = place()
     rows = own_ref.shape[1]
     copies = []
-    for index, core in enumerate((1 - k, k)):
-        target = three_ref.at[pl.ds(index * rows, rows), :]
+    for target, core in ((crossed_ref, 1 - k), (straight_ref, k)):
         started(copies, full_ref.at[x, chip_rows(3, core, rows), :], target, sem)
     started(copies, full_ref.at[:, chip_rows(0, k, rows), :], own_ref, sem)
     started(copies, full_ref.at[:, chip_rows(0, 1 - k, rows), :], cross_ref, sem)
@@ -134,12 +133,12 @@
 
 def far_packed(full_chol, rows):
     order = full_chol.shape[2]
-    shapes = [(2 * rows, order), (2, rows, order), (2, rows, order)]
+    shapes = [(rows, order)] * 2 + [(2, rows, order)] * 2
     return pl.pallas_call(
         far_pack_kernel,
         out_shape=[jax.ShapeDtypeStruct(shape, narrow) for shape in shapes],
         in_specs=[hbm_spec],
-        out_specs=[vmem_spec] * 3,
+        out_specs=[vmem_spec] * 4,
         scratch_shapes=[pltpu.SemaphoreType.DMA((4,))],
         cost_estimate=long,
         name="far_packed",
@@ -209,6 +208,7 @@
         in_specs=[vmem_spec] * 6,
         out_specs=vmem_spec,
         compiler_params=small,
+        cost_estimate=long,
         name="chip_bias",
     )(*green, mine, theirs)
 
@@ -292,16 +292,25 @@
     ]
 
 
-def early_kernel(walkers, field_here, field_one, field_two, own, own_theirs, *refs):
-    blocks, summed_ref = refs[:-1], refs[-1]
+def of_one(ref):
+    return lambda picked: ref[picked]
+
+
+def early_kernel(walkers, field_here, field_one, field_two, field_three, own, own_theirs, *refs):
+    theirs, theirs_x, near, near_x, near_theirs, near_theirs_x, summed_ref = refs
     _, _, x = place()
+    rows = own.shape[1]
     sources = [
         (field_here, 0, of_pair(own, x), of_pair(own, 1 - x)),
         (field_here, 1, of_pair(own_theirs, x), of_pair(own_theirs, 1 - x)),
+        (field_three, 1, of_one(theirs), of_one(theirs_x)),
     ]
-    rows = own.shape[1]
-    sources += both_cores(field_one, rows, *blocks[:4])
-    sources += both_cores(field_two, rows, *blocks[4:])
+    for index, field_ref in enumerate((field_one, field_two)):
+        top = 2 * rows * index
+        sources += [
+            (field_ref, 0, below(near, top + rows), below(near_x, top + rows)),
+            (field_ref, 1, below(near_theirs, top), below(near_theirs_x, top)),
+        ]
 
     def body(picked):
         tiles = block_operators(x, walkers, sources, picked)
@@ -317,27 +326,23 @@
     return pl.pallas_call(
         functools.partial(early_kernel, walkers),
         out_shape=jax.ShapeDtypeStruct((walkers, rows, order), wide),
-        in_specs=[vmem_spec] * (5 + len(blocks)),
+        in_specs=[vmem_spec] * (6 + len(blocks)),
         out_specs=vmem_spec,
         compiler_params=large,
-        cost_estimate=long,
         name="early_operator",
     )(*fields, own, own_theirs, *blocks)
 
 
-def late_kernel(summed_ref, field_ref, *refs):
-    blocks, operator_ref = refs[:-1], refs[-1]
+def late_kernel(summed_ref, field_ref, mine, mine_x, operator_ref):
     walkers, rows, order = summed_ref.shape
     _, _, x = place()
-    sources = both_cores(field_ref, rows, *blocks)
+    sources = [(field_ref, 0, of_one(mine), of_one(mine_x))]
 
     def body(picked):
         tiles = block_operators(x, walkers, sources, picked)
         row, column = picked
         for w in range(walkers):
-            value = summed_ref[(w, *picked)]
-            for block in tiles:
-                value = value + block[w].astype(wide)
+            value = summed_ref[(w, *picked)] + tiles[0][w].astype(wide)
             top = value.astype(narrow)
             operator_ref[w, row, column] = top
             rest = (value - top.astype(wide)).astype(narrow)
@@ -346,16 +351,16 @@
     over_tiles(rows, order, body)
 
 
-def split_operator(summed, field, blocks):
+def split_operator(summed, field, mine, mine_x):
     walkers, rows, order = summed.shape
     return pl.pallas_call(
         late_kernel,
         out_shape=jax.ShapeDtypeStruct((walkers, 2 * rows, order), narrow),
-        in_specs=[vmem_spec] * (2 + len(blocks)),
+        in_specs=[vmem_spec] * 4,
         out_specs=vmem_spec,
         compiler_params=large,
         name="split_operator",
-    )(summed, field, *blocks)
+    )(summed, field, mine, mine_x)
 
 
 def applied(operator_ref, vector_ref, step, mine, theirs):
@@ -432,30 +437,35 @@
     )(operator, *more, *pieces)
 
 
-def first_kernel(counts, operator_ref, partial_ref, *refs):
-    (mine, theirs), (first_ref, narrow_ref, vector_ref) = grouped(counts, refs)
-    part = applied(operator_ref, vector_ref, 3, mine, theirs)
+def first_kernel(counts, operator_ref, *refs):
+    groups, (first_ref, narrow_ref, vector_ref) = grouped(counts, refs)
+    parts = [
+        applied(operator_ref, vector_ref.at[step], step, groups[step], groups[4 + step])
+        for step in range(4)
+    ]
     for w in range(first_ref.shape[0]):
-        term = partial_ref[w] + part(w)
+        term = (parts[0](w) + parts[1](w)) + (parts[2](w) + parts[3](w))
         first_ref[w] = term
         narrow_ref[w] = term.astype(narrow)
 
 
-def first_application(operator, partial, mine, theirs):
-    walkers, rows, occupied = partial.shape
-    counts, pieces = [len(mine), len(theirs)], [*mine, *theirs]
+def first_application(operator, groups):
+    walkers, rows = operator.shape[0], operator.shape[1] // 2
+    occupied = groups[0][0].shape[2]
+    counts = [len(group) for group in groups]
+    pieces = flat(groups)
     return pl.pallas_call(
         functools.partial(first_kernel, counts),
         out_shape=[
             jax.ShapeDtypeStruct((walkers, rows, occupied), wide),
             jax.ShapeDtypeStruct((walkers, rows, occupied), narrow),
         ],
-        in_specs=[vmem_spec] * (2 + len(pieces)),
+        in_specs=[vmem_spec] * (1 + len(pieces)),
         out_specs=[vmem_spec] * 2,
-        scratch_shapes=[pltpu.VMEM((walkers, 2 * rows, occupied), narrow)],
+        scratch_shapes=[pltpu.VMEM((4, walkers, 2 * rows, occupied), narrow)],
         compiler_params=small,
         name="first_application",
-    )(operator, partial, *pieces)
+    )(operator, *pieces)
 
 
 def second_kernel(counts, operator_ref, base_ref, *refs):
@@ -495,73 +505,72 @@
     walkers, rows, _ = green_blocks.shape
     vectors = half_chol.shape[0]
 
+    half = walkers // 2
+
     constants = jnp.concatenate([noise_draws.T.reshape(-1), jnp.repeat(meanfield, walkers)])
     constants = jnp.broadcast_to(constants[:, None], (2 * vectors * walkers, 128))
     constants_theirs = to_core(constants)
 
     near_messages = near_packed(full_chol, green_blocks)
-    one, two = to_chip(near_messages[0], 1), to_chip(near_messages[1], 2)
+    one = to_chip(near_messages[0], 1)
+    two = to_chip(near_messages[1], 2)
     far_messages = far_packed(after(full_chol, *near_messages), rows)
-    own = far_messages[1]
-    green_three = to_chip(after(two, one, *far_messages)[:rows], 1)
-    one_theirs = to_core(after(one, two, *far_messages))
+    half_theirs = to_core(half_chol)
+    own_theirs = to_core(far_messages[3])
+    green_three = to_chip(after(two, *far_messages, half_theirs, own_theirs, constants_theirs, one)[:rows], 1)
+    greens = (green_blocks, one, two, green_three)
+    bias = chip_bias(greens, half_chol, half_theirs)
     start = walker_major(orbitals)
-    two_theirs = to_core(after(two, one, *far_messages, start))
-    half_theirs = to_core(half_chol)
-
-    bias = chip_bias(
-        (green_blocks, one, two, after(green_three, one_theirs, two_theirs, start)),
-        half_chol,
-        half_theirs,
-    )
-
-    one_x = across(after(one, two, *far_messages)[rows:])
-    one_x_theirs = to_core(one_x)
-    two_x = across(after(two, one, *far_messages)[rows:])
-    two_x_theirs = to_core(two_x)
-    own_theirs = to_core(far_messages[2])
-    three = after(far_messages[0], half_theirs, own_theirs, constants_theirs, one, two)
-    three = to_chip(three, 3)
-    three_theirs = to_core(three)
+    start_two = to_chip(after(start, one, two), 2)
+    start_three = to_chip(after(start_two, bias), 1)
+    crossed = to_chip(after(far_messages[0], two), 3)
+    straight = to_chip(after(far_messages[1], crossed), 3)
+    start_one = to_chip(after(start, one, two), 1)
     bias_theirs = to_core(bias)
 
-    bias = after(bias, one_x_theirs, two_x_theirs, three_theirs)
-    bias_shift, field = chip_field(bias, bias_theirs, constants, constants_theirs, vectors)
-    field_one, field_two = to_chip(field, 1), to_chip(field, 2)
-    summed = early_operator(
-        walkers,
-        (field, field_one, field_two),
-        own,
-        own_theirs,
-        (one, one_x, one_theirs, one_x_theirs, two, two_x, two_theirs, two_x_theirs),
-    )
-    field_three = to_chip(field, 3)
-    three_x = across(three)
-    three_x_theirs = to_core(after(three_x, field_one, field_two))
-    operator = split_operator(
-        summed, field_three, (three, three_x, three_theirs, three_x_theirs)
-    )
-
-    start_one, start_two = to_chip(after(start, one_x), 1), to_chip(after(start, one_x), 2)
-    theirs = [to_core(start), to_core(after(start_one, bias_shift, field)), to_core(start_two)]
-    groups = [[each] for each in (start, start_one, start_two, *theirs)]
-    partial = near_application(operator, groups)
-    start_three = to_chip(start_two, 1)
-    start_three_theirs = to_core(after(start_three, summed, partial))
-    first_term, first = first_application(
-        operator, partial, [start_three], [start_three_theirs]
-    )
-
-    half = walkers // 2
+    bias_ready = after(bias, start_three, straight, start_one)
+    bias_shift, field = chip_field(bias_ready, bias_theirs, constants, constants_theirs, vectors)
+    near_rows = jnp.concatenate([after(one, *far_messages)[rows:], two[rows:]])
+    near_rows_theirs = to_core(after(near_rows, bias))
+    crossed_theirs = to_core(after(crossed, bias))
+    field_one = to_chip(after(field, near_rows_theirs, crossed_theirs), 1)
+    field_two = to_chip(after(field, near_rows_theirs, crossed_theirs), 2)
+    field_three = to_chip(after(field, near_rows_theirs, crossed_theirs), 3)
+    crossed_x = across(after(crossed, bias, one))
+    crossed_x_theirs = to_core(crossed_x)
+    near_rows_x = across(near_rows)
+    near_rows_x_theirs = to_core(after(near_rows_x, bias))
+    fields = (field, field_one, field_two, field_three)
+    blocks = (crossed_theirs, crossed_x_theirs, near_rows, near_rows_x)
+    blocks += (near_rows_theirs, near_rows_x_theirs)
+    summed = early_operator(walkers, fields, far_messages[2], own_theirs, blocks)
+    straight_x = across(after(straight, bias))
+    operator = split_operator(summed, field_three, straight, straight_x)
+    start_theirs = to_core(start)
+    start_one_theirs = to_core(after(start_one, bias))
+    start_two_theirs = to_core(start_two)
+    start_three_theirs = to_core(after(start_three, summed))
+
+    groups = (start, start_one, start_two, start_three)
+    groups += (start_theirs, start_one_theirs, start_two_theirs, start_three_theirs)
+    first_term, first = first_application(operator, [[each] for each in groups])
+
     first_one = to_chip(first, 1)
-    first_two = [to_chip(first[:half], 2), to_chip(first[half:], 2)]
-    theirs = [[to_core(first)], [to_core(after(first_one, first_two[0]))]]
-    theirs.append([to_core(each) for each in first_two])
-    groups = [[first], [first_one], first_two, *theirs]
+    first_two_low = to_chip(first[:half], 2)
+    first_two_high = to_chip(first[half:], 2)
+    first_theirs = to_core(first)
+    first_one_theirs = to_core(after(first_one, first_two_low))
+    two_low_theirs = to_core(first_two_low)
+    two_high_theirs = to_core(first_two_high)
+    groups = [[first], [first_one], [first_two_low, first_two_high]]
+    groups += [[first_theirs], [first_one_theirs], [two_low_theirs, two_high_theirs]]
     base = near_application(operator, groups, first_term, orbitals)
-    first_three = [to_chip(each, 1) for each in first_two]
-    theirs = [to_core(first_three[0]), to_core(after(first_three[1], base))]
-    walkers_next = second_application(operator, base, first_three, theirs)
+    first_three_low = to_chip(first_two_low, 1)
+    first_three_high = to_chip(first_two_high, 1)
+    three_low_theirs = to_core(first_three_low)
+    three_high_theirs = to_core(after(first_three_high, base))
+    mine, theirs = [first_three_low, first_three_high], [three_low_theirs, three_high_theirs]
+    walkers_next = second_application(operator, base, mine, theirs)
     return (walkers_next, bias_shift.T)
 
 

time: 124 us -> 121 us (0.976)
  waiting for transfers between devices: 77.4 us -> 70.9 us
  starting transfers between devices: 26.5 us -> 29.9 us
    ppermute x3, waiting for transfers between devices: 16.7 us -> 0.98 us  [across(): return lax.ppermute(value, 'walk', [(0, 1), (1, 0)])]
    ppermute x15 -> x16, waiting for transfers between devices: 58.1 us -> 68.1 us  [to_chip(): return lax.ppermute(value, 'chol', [(i, i ^ 2 * step) for i in range(8)])]
    ppermute x15 -> x16, starting transfers between devices: 19.9 us -> 22.1 us  [to_chip(): return lax.ppermute(value, 'chol', [(i, i ^ 2 * step) for i in range(8)])]
    pallas_call x1, Pallas kernels: 0.37 us -> 1.82 us  [first_application(): pl.pallas_call(functools.partial(first_kernel, counts), out_shape=[jax.Sh...]
    ppermute x20 -> x18, waiting for transfers between devices: 2.55 us -> 1.75 us  [to_core(): return lax.ppermute(value, 'chol', [(i, i ^ 1) for i in range(8)])]
    ppermute x20 -> x18, starting transfers between devices: 3 us -> 3.27 us  [to_core(): return lax.ppermute(value, 'chol', [(i, i ^ 1) for i in range(8)])]
  transfers between devices with their start and end apart: 38 -> 37, of which waited for: 15 -> 15; matrix products, arithmetic and copies ran while one was open for 0% -> 0% of each run, Pallas kernels for 11% -> 10%
where the time goes in v14:
time: 121 us
  waiting for transfers between devices  70.9 us (59%)
  starting transfers between devices  29.9 us (25%)
  Pallas kernels  18.8 us (16%)
    ppermute x16, waiting for transfers between devices, to_chip(): return lax.ppermute(value, 'chol', [(i, i ^ 2 * step) for i in range(8)])  68.1 us
    ppermute x16, starting transfers between devices, to_chip(): return lax.ppermute(value, 'chol', [(i, i ^ 2 * step) for i in range(8)])  22.1 us
    ppermute x3, starting transfers between devices, across(): return lax.ppermute(value, 'walk', [(0, 1), (1, 0)])  4.54 us
    pallas_call x1, Pallas kernels, early_operator(): pl.pallas_call(functools.partial(early_kernel, walkers), out_shape=jax.Sh...  3.91 us
    pallas_call x1, Pallas kernels, near_packed(): pl.pallas_call(near_pack_kernel, out_shape=[jax.ShapeDtypeStruct((3 * row...  3.38 us
    ppermute x18, starting transfers between devices, to_core(): return lax.ppermute(value, 'chol', [(i, i ^ 1) for i in range(8)])  3.27 us
    pallas_call x1, Pallas kernels, far_packed(): pl.pallas_call(far_pack_kernel, out_shape=[jax.ShapeDtypeStruct(shape, na...  2.54 us
  transfers between devices with their start and end apart: 37, of which 15 were waited for; matrix products, arithmetic and copies ran while one was open for 0% of the time, Pallas kernels for 10%

profile of v14, /device:TPU:0, one launch (start us, length us, event | category | flops | bytes accessed | tf_op | source)
XLA Modules:
  0.0 121.0 jit_solution(14686990891320697984)
XLA Ops:
  0.6 3.4 %near_packed.1 = (bf16[384,1024]{1,0:T(8,128)(2,1)}, bf16[384,1024]{1,0:T(8,128)(2,1)}) custom-call(bf16[2,1024,1024]{2,1,0:T(8,128)(2,1)} %full_ref.2, bf16[4,128,256]{2,1,0:T(8,128)(2,1)} %here_ref.1), custom_call_target="tpu_custom_call" | custom-call | tf_op jit(solution)/shard_map/near_packed/pallas_call | solution.py:112
  4.0 3.1 %collective-permute-start = (bf16[384,1024]{1,0:T(8,128)(2,1)}, bf16[384,1024]{1,0:T(8,128)(2,1)S(1)}, u32[]{:S(2)}, u32[]{:S(2)}) collective-permute-start(bf16[384,1024]{1,0:T(8,128)(2,1)} %get-tuple-element.30), channel_id=1, source_target_pairs={{0,4},{2,6},{4,0},{6,2},{8,12},{10,14},{12,8},{14,10},{1,5},{3,7},... | collective-permute-start | bytes 2359304 | tf_op jit(solution)/shard_map/ppermute | solution.py:493
  7.1 2.6 %collective-permute-start.1 = (bf16[384,1024]{1,0:T(8,128)(2,1)}, bf16[384,1024]{1,0:T(8,128)(2,1)S(1)}, u32[]{:S(2)}, u32[]{:S(2)}) collective-permute-start(bf16[384,1024]{1,0:T(8,128)(2,1)} %get-tuple-element.31), channel_id=1, source_target_pairs={{0,8},{2,10},{4,12},{6,14},{8,0},{10,2},{12,4},{14,6},{1,9},{3,11}... | collective-permute-start | bytes 2359304 | tf_op jit(solution)/shard_map/ppermute | solution.py:493
  9.7 2.5 %far_packed.1 = (bf16[128,1024]{1,0:T(8,128)(2,1)}, bf16[128,1024]{1,0:T(8,128)(2,1)}, bf16[2,128,1024]{2,1,0:T(8,128)(2,1)}, bf16[2,128,1024]{2,1,0:T(8,128)(2,1)}) custom-call(bf16[2,1024,1024]{2,1,0:T(8,128)(2,1)} %full_ref.2), custom_call_target="tpu_custom_call" | custom-call | flops 99999997952 | tf_op jit(solution)/shard_map/far_packed/pallas_call | solution.py:137
  12.2 0.6 collective-permute-start.3
  12.9 0.1 reshape.12
  13.2 30.9 %collective-permute-done.1.two_ref = bf16[384,1024]{1,0:T(8,128)(2,1)S(1)} collective-permute-done((bf16[384,1024]{1,0:T(8,128)(2,1)}, bf16[384,1024]{1,0:T(8,128)(2,1)S(1)}, u32[]{:S(2)}, u32[]{:S(2)}) %collective-permute-start.1) | collective-permute-done | bytes 786464 | tf_op jit(solution)/shard_map/ppermute | solution.py:493
  44.1 2.5 %collective-permute-start.8 = (bf16[128,1024]{1,0:T(8,128)(2,1)}, bf16[128,1024]{1,0:T(8,128)(2,1)S(1)}, u32[]{:S(2)}, u32[]{:S(2)}) collective-permute-start(bf16[128,1024]{1,0:T(8,128)(2,1)} %get-tuple-element.40), channel_id=1, source_target_pairs={{0,12},{2,14},{4,8},{6,10},{8,4},{10,6},{12,0},{14,2},{1,13},{3,15... | collective-permute-start | bytes 786440 | tf_op jit(solution)/shard_map/ppermute | solution.py:493
  46.7 1.2 %walker_major.1.refs_0_ = bf16[4,128,256]{2,1,0:T(8,128)(2,1)} custom-call(f32[1,128,4,256]{3,2,1,0:T(4,128)S(1)} %copy-done), custom_call_target="tpu_custom_call" | custom-call | tf_op jit(solution)/shard_map/walker_major/pallas_call | solution.py:155
  48.0 1.9 %collective-permute-start.6 = (bf16[4,128,256]{2,1,0:T(8,128)(2,1)}, bf16[4,128,256]{2,1,0:T(8,128)(2,1)S(1)}, u32[]{:S(2)}, u32[]{:S(2)}) collective-permute-start(bf16[4,128,256]{2,1,0:T(8,128)(2,1)} %walker_major.1.refs_0_), channel_id=1, source_target_pairs={{0,8},{2,10},{4,12},{6,14},{8,0},{10,2},{12,4},{14,6},{1,9},{3,11}... | collective-permute-start | bytes 786440 | tf_op jit(solution)/shard_map/ppermute | solution.py:493
  49.9 0.2 collective-permute-start.10
  50.2 1.6 %collective-permute-start.19 = (bf16[512,1024]{1,0:T(8,128)(2,1)S(1)}, bf16[512,1024]{1,0:T(8,128)(2,1)S(1)}, u32[]{:S(2)}, u32[]{:S(2)}) collective-permute-start(bf16[512,1024]{1,0:T(8,128)(2,1)S(1)} %pad_maximum_fusion.refs_2_), channel_id=1, source_target_pairs={{0,1},{1,0},{2,3},{3,2},{4,5},{5,4},{6,7},{7,6},{8,9},{9,8},{10,11... | collective-permute-start | bytes 3145736 | tf_op jit(solution)/shard_map/ppermute | solution.py:501
  51.8 3.7 %collective-permute-done.8 = bf16[128,1024]{1,0:T(8,128)(2,1)S(1)} collective-permute-done((bf16[128,1024]{1,0:T(8,128)(2,1)}, bf16[128,1024]{1,0:T(8,128)(2,1)S(1)}, u32[]{:S(2)}, u32[]{:S(2)}) %collective-permute-start.8) | collective-permute-done | bytes 262176 | tf_op jit(solution)/shard_map/ppermute | solution.py:493
  55.5 2.5 %collective-permute-start.9 = (bf16[128,1024]{1,0:T(8,128)(2,1)S(1)}, bf16[128,1024]{1,0:T(8,128)(2,1)S(1)}, u32[]{:S(2)}, u32[]{:S(2)}) collective-permute-start(bf16[128,1024]{1,0:T(8,128)(2,1)S(1)} %copy-done.4), channel_id=1, source_target_pairs={{0,12},{2,14},{4,8},{6,10},{8,4},{10,6},{12,0},{14,2},{1,13},{3,15... | collective-permute-start | bytes 786440 | tf_op jit(solution)/shard_map/ppermute | solution.py:493
  58.0 1.3 %collective-permute-done.5.three_ref = bf16[128,1024]{1,0:T(8,128)(2,1)S(1)} collective-permute-done((bf16[128,1024]{1,0:T(8,128)(2,1)S(1)}, bf16[128,1024]{1,0:T(8,128)(2,1)S(1)}, u32[]{:S(2)}, u32[]{:S(2)}) %collective-permute-start.5) | collective-permute-done | bytes 262176 | tf_op jit(solution)/shard_map/ppermute | solution.py:493
  59.2 2.2 %chip_bias.1.mine_ref = f32[16,128]{1,0:T(8,128)S(1)} custom-call(bf16[4,128,256]{2,1,0:T(8,128)(2,1)S(1)} %copy-done.2, bf16[384,1024]{1,0:T(8,128)(2,1)S(1)} %collective-permute-done.one_ref, bf16[384,1024]{1,0:T(8,128)(2,1)S(1)} %collective-permute-done.1.two_ref, bf16[128,1024]{1,0:T(8,128)(2,1)S(1)} %collective-permute-done.5.three_ref, ...), custom_call_target="tpu_custom_call" | custom-call | flops 99999997952 | tf_op jit(solution)/shard_map/chip_bias/pallas_call | solution.py:205
  61.5 11.6 %collective-permute-done.6.refs_2_ = bf16[4,128,256]{2,1,0:T(8,128)(2,1)S(1)} collective-permute-done((bf16[4,128,256]{2,1,0:T(8,128)(2,1)}, bf16[4,128,256]{2,1,0:T(8,128)(2,1)S(1)}, u32[]{:S(2)}, u32[]{:S(2)}) %collective-permute-start.6) | collective-permute-done | bytes 262176 | tf_op jit(solution)/shard_map/ppermute | solution.py:493
  73.1 1.5 %collective-permute-start.17 = (bf16[128,1024]{1,0:T(8,128)(2,1)S(1)}, bf16[128,1024]{1,0:T(8,128)(2,1)S(1)}, u32[]{:S(2)}, u32[]{:S(2)}) collective-permute-start(bf16[128,1024]{1,0:T(8,128)(2,1)S(1)} %collective-permute-done.8), channel_id=1, source_target_pairs={{0,1},{1,0},{2,3},{3,2},{4,5},{5,4},{6,7},{7,6},{8,9},{9,8},{10,11... | collective-permute-start | bytes 786440 | tf_op jit(solution)/shard_map/ppermute | solution.py:501
  74.6 0.5 collective-permute-start.12
  75.1 4.4 %collective-permute-done.7.refs_3_ = bf16[4,128,256]{2,1,0:T(8,128)(2,1)S(1)} collective-permute-done((bf16[4,128,256]{2,1,0:T(8,128)(2,1)S(1)}, bf16[4,128,256]{2,1,0:T(8,128)(2,1)S(1)}, u32[]{:S(2)}, u32[]{:S(2)}) %collective-permute-start.7) | collective-permute-done | bytes 262176 | tf_op jit(solution)/shard_map/ppermute | solution.py:493
  79.5 0.5 collective-permute-start.18
  80.1 0.6 chip_field.1
  80.7 0.4 collective-permute-done.13.refs_0_
  81.0 1.6 %collective-permute-start.14 = (f32[16,128]{1,0:T(8,128)S(1)}, f32[16,128]{1,0:T(8,128)S(1)}, u32[]{:S(2)}, u32[]{:S(2)}) collective-permute-start(f32[16,128]{1,0:T(8,128)S(1)} %get-tuple-element.47.field_here), channel_id=1, source_target_pairs={{0,4},{2,6},{4,0},{6,2},{8,12},{10,14},{12,8},{14,10},{1,5},{3,7},... | collective-permute-start | bytes 24584 | tf_op jit(solution)/shard_map/ppermute | solution.py:493
  82.6 0.7 collective-permute-start.15
  83.3 2.1 %collective-permute-start.16 = (f32[16,128]{1,0:T(8,128)S(1)}, f32[16,128]{1,0:T(8,128)S(1)}, u32[]{:S(2)}, u32[]{:S(2)}) collective-permute-start(f32[16,128]{1,0:T(8,128)S(1)} %get-tuple-element.47.field_here), channel_id=1, source_target_pairs={{0,12},{2,14},{4,8},{6,10},{8,4},{10,6},{12,0},{14,2},{1,13},{3,15... | collective-permute-start | bytes 24584 | tf_op jit(solution)/shard_map/ppermute | solution.py:493
  85.4 0.5 collective-permute-start.24
  85.9 1.2 %collective-permute-done.15.field_two = f32[16,128]{1,0:T(8,128)S(1)} collective-permute-done((f32[16,128]{1,0:T(8,128)S(1)}, f32[16,128]{1,0:T(8,128)S(1)}, u32[]{:S(2)}, u32[]{:S(2)}) %collective-permute-start.15) | collective-permute-done | bytes 8224 | tf_op jit(solution)/shard_map/ppermute | solution.py:493
  87.2 1.5 %collective-permute-start.21 = (bf16[128,1024]{1,0:T(8,128)(2,1)S(1)}, bf16[128,1024]{1,0:T(8,128)(2,1)S(1)}, u32[]{:S(2)}, u32[]{:S(2)}) collective-permute-start(bf16[128,1024]{1,0:T(8,128)(2,1)S(1)} %collective-permute-done.9.mine), channel_id=1, source_target_pairs={{0,1},{1,0},{2,3},{3,2},{4,5},{5,4},{6,7},{7,6},{8,9},{9,8},{10,11... | collective-permute-start | bytes 786440 | tf_op jit(solution)/shard_map/ppermute | solution.py:501
  88.7 0.1 collective-permute-done.16.field_three.field_ref
  88.8 3.9 %early_operator.1.summed_ref = f32[4,128,1024]{2,1,0:T(8,128)S(1)} custom-call(f32[16,128]{1,0:T(8,128)S(1)} %get-tuple-element.47.field_here, f32[16,128]{1,0:T(8,128)S(1)} %collective-permute-done.14.field_one, f32[16,128]{1,0:T(8,128)S(1)} %collective-permute-done.15.field_two, f32[16,128]{1,0:T(8,128)S(1)} %collective-permute-done.16.field_three.field_ref, ...), custom_call_target="tpu_custom_call" | custom-call | tf_op jit(solution)/shard_map/early_operator/pallas_call | solution.py:326
  92.7 0.6 collective-permute-start.25
  93.2 1.0 collective-permute-done.21.mine_x
  94.2 1.1 split_operator.1.operator_ref
  95.4 1.8 %first_application.1 = (f32[4,128,256]{2,1,0:T(8,128)S(1)}, bf16[4,128,256]{2,1,0:T(8,128)(2,1)S(1)}) custom-call(bf16[4,256,1024]{2,1,0:T(8,128)(2,1)S(1)} %split_operator.1.operator_ref, bf16[4,128,256]{2,1,0:T(8,128)(2,1)} %walker_major.1.refs_0_, bf16[4,128,256]{2,1,0:T(8,128)(2,1)S(1)} %collective-permute-done.10.refs_1_, ...), custom_call_target="tpu_custom_call" | custom-call | tf_op jit(solution)/shard_map/first_application/pallas_call | solution.py:457
  97.2 0.9 collective-permute-start.26
  98.1 1.6 %collective-permute-start.27 = (bf16[2,128,256]{2,1,0:T(8,128)(2,1)S(1)}, bf16[2,128,256]{2,1,0:T(8,128)(2,1)S(1)}, u32[]{:S(2)}, u32[]{:S(2)}) collective-permute-start(bf16[2,128,256]{2,1,0:T(8,128)(2,1)S(1)} %get-tuple-element.59), channel_id=1, source_target_pairs={{0,8},{2,10},{4,12},{6,14},{8,0},{10,2},{12,4},{14,6},{1,9},{3,11}... | collective-permute-start | bytes 393224 | tf_op jit(solution)/shard_map/ppermute | solution.py:493
  99.6 1.4 %collective-permute-start.28 = (bf16[2,128,256]{2,1,0:T(8,128)(2,1)S(1)}, bf16[2,128,256]{2,1,0:T(8,128)(2,1)S(1)}, u32[]{:S(2)}, u32[]{:S(2)}) collective-permute-start(bf16[2,128,256]{2,1,0:T(8,128)(2,1)S(1)} %get-tuple-element.58), channel_id=1, source_target_pairs={{0,8},{2,10},{4,12},{6,14},{8,0},{10,2},{12,4},{14,6},{1,9},{3,11}... | collective-permute-start | bytes 393224 | tf_op jit(solution)/shard_map/ppermute | solution.py:493
  101.0 6.0 %collective-permute-done.27.refs_2_ = bf16[2,128,256]{2,1,0:T(8,128)(2,1)S(1)} collective-permute-done((bf16[2,128,256]{2,1,0:T(8,128)(2,1)S(1)}, bf16[2,128,256]{2,1,0:T(8,128)(2,1)S(1)}, u32[]{:S(2)}, u32[]{:S(2)}) %collective-permute-start.27) | collective-permute-done | bytes 131104 | tf_op jit(solution)/shard_map/ppermute | solution.py:493
  107.0 2.0 %collective-permute-done.26.refs_1_ = bf16[4,128,256]{2,1,0:T(8,128)(2,1)S(1)} collective-permute-done((bf16[4,128,256]{2,1,0:T(8,128)(2,1)S(1)}, bf16[4,128,256]{2,1,0:T(8,128)(2,1)S(1)}, u32[]{:S(2)}, u32[]{:S(2)}) %collective-permute-start.26) | collective-permute-done | bytes 262176 | tf_op jit(solution)/shard_map/ppermute | solution.py:493
  109.0 0.5 collective-permute-start.31
  109.6 1.1 collective-permute-start.33
  110.6 1.8 %collective-permute-done.28.refs_3_ = bf16[2,128,256]{2,1,0:T(8,128)(2,1)S(1)} collective-permute-done((bf16[2,128,256]{2,1,0:T(8,128)(2,1)S(1)}, bf16[2,128,256]{2,1,0:T(8,128)(2,1)S(1)}, u32[]{:S(2)}, u32[]{:S(2)}) %collective-permute-start.28) | collective-permute-done | bytes 131104 | tf_op jit(solution)/shard_map/ppermute | solution.py:493
  112.5 2.8 %collective-permute-done.33.refs_0_ = bf16[2,128,256]{2,1,0:T(8,128)(2,1)S(1)} collective-permute-done((bf16[2,128,256]{2,1,0:T(8,128)(2,1)S(1)}, bf16[2,128,256]{2,1,0:T(8,128)(2,1)S(1)}, u32[]{:S(2)}, u32[]{:S(2)}) %collective-permute-start.33) | collective-permute-done | bytes 131104 | tf_op jit(solution)/shard_map/ppermute | solution.py:493
  115.2 0.7 base_application.1.base_ref
  116.0 2.4 %collective-permute-done.34.refs_1_ = bf16[2,128,256]{2,1,0:T(8,128)(2,1)S(1)} collective-permute-done((bf16[2,128,256]{2,1,0:T(8,128)(2,1)S(1)}, bf16[2,128,256]{2,1,0:T(8,128)(2,1)S(1)}, u32[]{:S(2)}, u32[]{:S(2)}) %collective-permute-start.34) | collective-permute-done | bytes 131104 | tf_op jit(solution)/shard_map/ppermute | solution.py:493
  118.4 1.3 %collective-permute-done.36.refs_3_ = bf16[2,128,256]{2,1,0:T(8,128)(2,1)S(1)} collective-permute-done((bf16[2,128,256]{2,1,0:T(8,128)(2,1)S(1)}, bf16[2,128,256]{2,1,0:T(8,128)(2,1)S(1)}, u32[]{:S(2)}, u32[]{:S(2)}) %collective-permute-start.36) | collective-permute-done | bytes 131104 | tf_op jit(solution)/shard_map/ppermute | solution.py:497
  119.7 1.2 %second_application.1 = f32[1,128,4,256]{3,2,1,0:T(4,128)} custom-call(bf16[4,256,1024]{2,1,0:T(8,128)(2,1)S(1)} %split_operator.1.operator_ref, f32[4,128,256]{2,1,0:T(8,128)S(1)} %base_application.1.base_ref, bf16[2,128,256]{2,1,0:T(8,128)(2,1)S(1)} %collective-permute-done.33.refs_0_, bf16[2,128,256]{2,1,0:T(8,128)(2,1)S(1)} %collective-permute-done.34.refs_1_, ...), custom_call_target="tpu_custom_call" | custom-call | tf_op jit(solution)/shard_map/second_application/pallas_call | solution.py:481
  (60 shorter events, 0.8 us)
Async XLA Ops:
  4.0 42.6 %collective-permute-start = (bf16[384,1024]{1,0:T(8,128)(2,1)}, bf16[384,1024]{1,0:T(8,128)(2,1)S(1)}, u32[]{:S(2)}, u32[]{:S(2)}) collective-permute-start(bf16[384,1024]{1,0:T(8,128)(2,1)} %get-tuple-element.30), channel_id=1, source_target_pairs={{0,4},{2,6},{4,0},{6,2},{8,12},{10,14},{12,8},{14,10},{1,5},{3,7},... | collective-permute-start | bytes 2359304 | tf_op jit(solution)/shard_map/ppermute | solution.py:493
  7.1 5.7 %copy-start.6 = (f32[2]{0:T(128)S(1)}, f32[2]{0:T(128)}, u32[]{:S(2)}) copy-start(f32[2]{0:T(128)} %param.9) | copy-start | bytes 28
  7.1 5.9 %copy-start.5 = (f32[4,2]{0,1:T(2,128)S(1)}, f32[4,2]{0,1:T(2,128)}, u32[]{:S(2)}) copy-start(f32[4,2]{0,1:T(2,128)} %param.10) | copy-start | bytes 100
  7.1 39.6 %copy-start = (f32[1,128,4,256]{3,2,1,0:T(4,128)S(1)}, f32[1,128,4,256]{3,2,1,0:T(4,128)}, u32[]{:S(2)}) copy-start(f32[1,128,4,256]{3,2,1,0:T(4,128)} %orbitals_ref.3) | copy-start | bytes 1572868
  7.1 37.0 %collective-permute-start.1 = (bf16[384,1024]{1,0:T(8,128)(2,1)}, bf16[384,1024]{1,0:T(8,128)(2,1)S(1)}, u32[]{:S(2)}, u32[]{:S(2)}) collective-permute-start(bf16[384,1024]{1,0:T(8,128)(2,1)} %get-tuple-element.31), channel_id=1, source_target_pairs={{0,8},{2,10},{4,12},{6,14},{8,0},{10,2},{12,4},{14,6},{1,9},{3,11}... | collective-permute-start | bytes 2359304 | tf_op jit(solution)/shard_map/ppermute | solution.py:493
  9.7 36.9 %collective-permute-start.2 = (bf16[2,1024,256]{2,1,0:T(8,128)(2,1)}, bf16[2,1024,256]{2,1,0:T(8,128)(2,1)}, u32[]{:S(2)}, u32[]{:S(2)}) collective-permute-start(bf16[2,1024,256]{2,1,0:T(8,128)(2,1)} %mine_ref.1), channel_id=1, source_target_pairs={{0,2},{2,0},{4,6},{6,4},{8,10},{10,8},{12,14},{14,12},{1,3},{3,1},... | collective-permute-start | bytes 3145736 | tf_op jit(solution)/shard_map/ppermute | solution.py:497
  12.2 34.4 %collective-permute-start.3 = (bf16[2,128,1024]{2,1,0:T(8,128)(2,1)}, bf16[2,128,1024]{2,1,0:T(8,128)(2,1)S(1)}, u32[]{:S(2)}, u32[]{:S(2)}) collective-permute-start(bf16[2,128,1024]{2,1,0:T(8,128)(2,1)} %get-tuple-element.36), channel_id=1, source_target_pairs={{0,2},{2,0},{4,6},{6,4},{8,10},{10,8},{12,14},{14,12},{1,3},{3,1},... | collective-permute-start | bytes 1572872 | tf_op jit(solution)/shard_map/ppermute | solution.py:497
  13.2 33.4 %collective-permute-start.4 = (f32[16,128]{1,0:T(8,128)S(1)}, f32[16,128]{1,0:T(8,128)S(1)}, u32[]{:S(2)}, u32[]{:S(2)}) collective-permute-start(f32[16,128]{1,0:T(8,128)S(1)} %broadcast_in_dim.10.noise_ref), channel_id=1, source_target_pairs={{0,2},{2,0},{4,6},{6,4},{8,10},{10,8},{12,14},{14,12},{1,3},{3,1},... | collective-permute-start | bytes 24584 | tf_op jit(solution)/shard_map/ppermute | solution.py:497
  44.1 11.4 %collective-permute-start.8 = (bf16[128,1024]{1,0:T(8,128)(2,1)}, bf16[128,1024]{1,0:T(8,128)(2,1)S(1)}, u32[]{:S(2)}, u32[]{:S(2)}) collective-permute-start(bf16[128,1024]{1,0:T(8,128)(2,1)} %get-tuple-element.40), channel_id=1, source_target_pairs={{0,12},{2,14},{4,8},{6,10},{8,4},{10,6},{12,0},{14,2},{1,13},{3,15... | collective-permute-start | bytes 786440 | tf_op jit(solution)/shard_map/ppermute | solution.py:493
  46.6 12.6 %collective-permute-start.5 = (bf16[128,1024]{1,0:T(8,128)(2,1)S(1)}, bf16[128,1024]{1,0:T(8,128)(2,1)S(1)}, u32[]{:S(2)}, u32[]{:S(2)}) collective-permute-start(bf16[128,1024]{1,0:T(8,128)(2,1)S(1)} %slice.15), channel_id=1, source_target_pairs={{0,4},{2,6},{4,0},{6,2},{8,12},{10,14},{12,8},{14,10},{1,5},{3,7},... | collective-permute-start | bytes 786440 | tf_op jit(solution)/shard_map/ppermute | solution.py:493
  48.0 7.5 %copy-start.4 = (bf16[128,1024]{1,0:T(8,128)(2,1)S(1)}, bf16[128,1024]{1,0:T(8,128)(2,1)}, u32[]{:S(2)}) copy-start(bf16[128,1024]{1,0:T(8,128)(2,1)} %get-tuple-element.41) | copy-start | bytes 786436
  48.0 11.3 %copy-start.2 = (bf16[4,128,256]{2,1,0:T(8,128)(2,1)S(1)}, bf16[4,128,256]{2,1,0:T(8,128)(2,1)}, u32[]{:S(2)}) copy-start(bf16[4,128,256]{2,1,0:T(8,128)(2,1)} %here_ref.1) | copy-start | bytes 786436
  48.0 11.3 %copy-start.3 = (bf16[2,1024,256]{2,1,0:T(8,128)(2,1)S(1)}, bf16[2,1024,256]{2,1,0:T(8,128)(2,1)}, u32[]{:S(2)}) copy-start(bf16[2,1024,256]{2,1,0:T(8,128)(2,1)} %mine_ref.1) | copy-start | bytes 3145732
  48.0 25.1 %collective-permute-start.6 = (bf16[4,128,256]{2,1,0:T(8,128)(2,1)}, bf16[4,128,256]{2,1,0:T(8,128)(2,1)S(1)}, u32[]{:S(2)}, u32[]{:S(2)}) collective-permute-start(bf16[4,128,256]{2,1,0:T(8,128)(2,1)} %walker_major.1.refs_0_), channel_id=1, source_target_pairs={{0,8},{2,10},{4,12},{6,14},{8,0},{10,2},{12,4},{14,6},{1,9},{3,11}... | collective-permute-start | bytes 786440 | tf_op jit(solution)/shard_map/ppermute | solution.py:493
  49.9 24.8 %collective-permute-start.10 = (bf16[4,128,256]{2,1,0:T(8,128)(2,1)}, bf16[4,128,256]{2,1,0:T(8,128)(2,1)S(1)}, u32[]{:S(2)}, u32[]{:S(2)}) collective-permute-start(bf16[4,128,256]{2,1,0:T(8,128)(2,1)} %walker_major.1.refs_0_), channel_id=1, source_target_pairs={{0,4},{2,6},{4,0},{6,2},{8,12},{10,14},{12,8},{14,10},{1,5},{3,7},... | collective-permute-start | bytes 786440 | tf_op jit(solution)/shard_map/ppermute | solution.py:493
  50.2 29.8 %collective-permute-start.19 = (bf16[512,1024]{1,0:T(8,128)(2,1)S(1)}, bf16[512,1024]{1,0:T(8,128)(2,1)S(1)}, u32[]{:S(2)}, u32[]{:S(2)}) collective-permute-start(bf16[512,1024]{1,0:T(8,128)(2,1)S(1)} %pad_maximum_fusion.refs_2_), channel_id=1, source_target_pairs={{0,1},{1,0},{2,3},{3,2},{4,5},{5,4},{6,7},{7,6},{8,9},{9,8},{10,11... | collective-permute-start | bytes 3145736 | tf_op jit(solution)/shard_map/ppermute | solution.py:501
  55.5 19.1 %collective-permute-start.9 = (bf16[128,1024]{1,0:T(8,128)(2,1)S(1)}, bf16[128,1024]{1,0:T(8,128)(2,1)S(1)}, u32[]{:S(2)}, u32[]{:S(2)}) collective-permute-start(bf16[128,1024]{1,0:T(8,128)(2,1)S(1)} %copy-done.4), channel_id=1, source_target_pairs={{0,12},{2,14},{4,8},{6,10},{8,4},{10,6},{12,0},{14,2},{1,13},{3,15... | collective-permute-start | bytes 786440 | tf_op jit(solution)/shard_map/ppermute | solution.py:493
  61.5 27.3 %copy-start.1 = (bf16[2,128,1024]{2,1,0:T(8,128)(2,1)S(1)}, bf16[2,128,1024]{2,1,0:T(8,128)(2,1)}, u32[]{:S(2)}) copy-start(bf16[2,128,1024]{2,1,0:T(8,128)(2,1)} %get-tuple-element.35.own) | copy-start | bytes 1572868
  73.1 6.4 %collective-permute-start.7 = (bf16[4,128,256]{2,1,0:T(8,128)(2,1)S(1)}, bf16[4,128,256]{2,1,0:T(8,128)(2,1)S(1)}, u32[]{:S(2)}, u32[]{:S(2)}) collective-permute-start(bf16[4,128,256]{2,1,0:T(8,128)(2,1)S(1)} %collective-permute-done.6.refs_2_), channel_id=1, source_target_pairs={{0,4},{2,6},{4,0},{6,2},{8,12},{10,14},{12,8},{14,10},{1,5},{3,7},... | collective-permute-start | bytes 786440 | tf_op jit(solution)/shard_map/ppermute | solution.py:493
  73.1 6.4 %collective-permute-start.17 = (bf16[128,1024]{1,0:T(8,128)(2,1)S(1)}, bf16[128,1024]{1,0:T(8,128)(2,1)S(1)}, u32[]{:S(2)}, u32[]{:S(2)}) collective-permute-start(bf16[128,1024]{1,0:T(8,128)(2,1)S(1)} %collective-permute-done.8), channel_id=1, source_target_pairs={{0,1},{1,0},{2,3},{3,2},{4,5},{5,4},{6,7},{7,6},{8,9},{9,8},{10,11... | collective-permute-start | bytes 786440 | tf_op jit(solution)/shard_map/ppermute | solution.py:501
  74.6 5.5 %collective-permute-start.11 = (f32[16,128]{1,0:T(8,128)S(1)}, f32[16,128]{1,0:T(8,128)S(1)}, u32[]{:S(2)}, u32[]{:S(2)}) collective-permute-start(f32[16,128]{1,0:T(8,128)S(1)} %chip_bias.1.mine_ref), channel_id=1, source_target_pairs={{0,2},{2,0},{4,6},{6,4},{8,10},{10,8},{12,14},{14,12},{1,3},{3,1},... | collective-permute-start | bytes 24584 | tf_op jit(solution)/shard_map/ppermute | solution.py:497
  74.6 6.4 %collective-permute-start.12 = (bf16[512,1024]{1,0:T(8,128)(2,1)S(1)}, bf16[512,1024]{1,0:T(8,128)(2,1)S(1)}, u32[]{:S(2)}, u32[]{:S(2)}) collective-permute-start(bf16[512,1024]{1,0:T(8,128)(2,1)S(1)} %pad_maximum_fusion.refs_2_), channel_id=1, source_target_pairs={{0,2},{2,0},{4,6},{6,4},{8,10},{10,8},{12,14},{14,12},{1,3},{3,1},... | collective-permute-start | bytes 3145736 | tf_op jit(solution)/shard_map/ppermute | solution.py:497
  79.5 1.5 %collective-permute-start.13 = (bf16[128,1024]{1,0:T(8,128)(2,1)S(1)}, bf16[128,1024]{1,0:T(8,128)(2,1)S(1)}, u32[]{:S(2)}, u32[]{:S(2)}) collective-permute-start(bf16[128,1024]{1,0:T(8,128)(2,1)S(1)} %collective-permute-done.8), channel_id=1, source_target_pairs={{0,2},{2,0},{4,6},{6,4},{8,10},{10,8},{12,14},{14,12},{1,3},{3,1},... | collective-permute-start | bytes 786440 | tf_op jit(solution)/shard_map/ppermute | solution.py:497
  79.5 5.9 %collective-permute-start.18 = (bf16[128,1024]{1,0:T(8,128)(2,1)S(1)}, bf16[128,1024]{1,0:T(8,128)(2,1)S(1)}, u32[]{:S(2)}, u32[]{:S(2)}) collective-permute-start(bf16[128,1024]{1,0:T(8,128)(2,1)S(1)} %collective-permute-done.17), channel_id=1, source_target_pairs={{0,2},{2,0},{4,6},{6,4},{8,10},{10,8},{12,14},{14,12},{1,3},{3,1},... | collective-permute-start | bytes 786440 | tf_op jit(solution)/shard_map/ppermute | solution.py:497
  80.0 8.8 %collective-permute-start.20 = (bf16[512,1024]{1,0:T(8,128)(2,1)S(1)}, bf16[512,1024]{1,0:T(8,128)(2,1)S(1)}, u32[]{:S(2)}, u32[]{:S(2)}) collective-permute-start(bf16[512,1024]{1,0:T(8,128)(2,1)S(1)} %collective-permute-done.19.refs_3_), channel_id=1, source_target_pairs={{0,2},{2,0},{4,6},{6,4},{8,10},{10,8},{12,14},{14,12},{1,3},{3,1},... | collective-permute-start | bytes 3145736 | tf_op jit(solution)/shard_map/ppermute | solution.py:497
  81.0 4.4 %collective-permute-start.14 = (f32[16,128]{1,0:T(8,128)S(1)}, f32[16,128]{1,0:T(8,128)S(1)}, u32[]{:S(2)}, u32[]{:S(2)}) collective-permute-start(f32[16,128]{1,0:T(8,128)S(1)} %get-tuple-element.47.field_here), channel_id=1, source_target_pairs={{0,4},{2,6},{4,0},{6,2},{8,12},{10,14},{12,8},{14,10},{1,5},{3,7},... | collective-permute-start | bytes 24584 | tf_op jit(solution)/shard_map/ppermute | solution.py:493
  82.6 4.5 %collective-permute-start.15 = (f32[16,128]{1,0:T(8,128)S(1)}, f32[16,128]{1,0:T(8,128)S(1)}, u32[]{:S(2)}, u32[]{:S(2)}) collective-permute-start(f32[16,128]{1,0:T(8,128)S(1)} %get-tuple-element.47.field_here), channel_id=1, source_target_pairs={{0,8},{2,10},{4,12},{6,14},{8,0},{10,2},{12,4},{14,6},{1,9},{3,11}... | collective-permute-start | bytes 24584 | tf_op jit(solution)/shard_map/ppermute | solution.py:493
  83.3 5.4 %collective-permute-start.16 = (f32[16,128]{1,0:T(8,128)S(1)}, f32[16,128]{1,0:T(8,128)S(1)}, u32[]{:S(2)}, u32[]{:S(2)}) collective-permute-start(f32[16,128]{1,0:T(8,128)S(1)} %get-tuple-element.47.field_here), channel_id=1, source_target_pairs={{0,12},{2,14},{4,8},{6,10},{8,4},{10,6},{12,0},{14,2},{1,13},{3,15... | collective-permute-start | bytes 24584 | tf_op jit(solution)/shard_map/ppermute | solution.py:493
  85.4 9.9 %collective-permute-start.22 = (bf16[4,128,256]{2,1,0:T(8,128)(2,1)}, bf16[4,128,256]{2,1,0:T(8,128)(2,1)S(1)}, u32[]{:S(2)}, u32[]{:S(2)}) collective-permute-start(bf16[4,128,256]{2,1,0:T(8,128)(2,1)} %walker_major.1.refs_0_), channel_id=1, source_target_pairs={{0,2},{2,0},{4,6},{6,4},{8,10},{10,8},{12,14},{14,12},{1,3},{3,1},... | collective-permute-start | bytes 786440 | tf_op jit(solution)/shard_map/ppermute | solution.py:497
  85.4 9.9 %collective-permute-start.24 = (bf16[4,128,256]{2,1,0:T(8,128)(2,1)S(1)}, bf16[4,128,256]{2,1,0:T(8,128)(2,1)S(1)}, u32[]{:S(2)}, u32[]{:S(2)}) collective-permute-start(bf16[4,128,256]{2,1,0:T(8,128)(2,1)S(1)} %collective-permute-done.6.refs_2_), channel_id=1, source_target_pairs={{0,2},{2,0},{4,6},{6,4},{8,10},{10,8},{12,14},{14,12},{1,3},{3,1},... | collective-permute-start | bytes 786440 | tf_op jit(solution)/shard_map/ppermute | solution.py:497
  87.2 7.1 %collective-permute-start.21 = (bf16[128,1024]{1,0:T(8,128)(2,1)S(1)}, bf16[128,1024]{1,0:T(8,128)(2,1)S(1)}, u32[]{:S(2)}, u32[]{:S(2)}) collective-permute-start(bf16[128,1024]{1,0:T(8,128)(2,1)S(1)} %collective-permute-done.9.mine), channel_id=1, source_target_pairs={{0,1},{1,0},{2,3},{3,2},{4,5},{5,4},{6,7},{7,6},{8,9},{9,8},{10,11... | collective-permute-start | bytes 786440 | tf_op jit(solution)/shard_map/ppermute | solution.py:501
  88.8 6.6 %collective-permute-start.23 = (bf16[4,128,256]{2,1,0:T(8,128)(2,1)S(1)}, bf16[4,128,256]{2,1,0:T(8,128)(2,1)S(1)}, u32[]{:S(2)}, u32[]{:S(2)}) collective-permute-start(bf16[4,128,256]{2,1,0:T(8,128)(2,1)S(1)} %collective-permute-done.10.refs_1_), channel_id=1, source_target_pairs={{0,2},{2,0},{4,6},{6,4},{8,10},{10,8},{12,14},{14,12},{1,3},{3,1},... | collective-permute-start | bytes 786440 | tf_op jit(solution)/shard_map/ppermute | solution.py:497
  92.7 2.7 %collective-permute-start.25 = (bf16[4,128,256]{2,1,0:T(8,128)(2,1)S(1)}, bf16[4,128,256]{2,1,0:T(8,128)(2,1)S(1)}, u32[]{:S(2)}, u32[]{:S(2)}) collective-permute-start(bf16[4,128,256]{2,1,0:T(8,128)(2,1)S(1)} %collective-permute-done.7.refs_3_), channel_id=1, source_target_pairs={{0,2},{2,0},{4,6},{6,4},{8,10},{10,8},{12,14},{14,12},{1,3},{3,1},... | collective-permute-start | bytes 786440 | tf_op jit(solution)/shard_map/ppermute | solution.py:497
  97.2 11.9 %collective-permute-start.26 = (bf16[4,128,256]{2,1,0:T(8,128)(2,1)S(1)}, bf16[4,128,256]{2,1,0:T(8,128)(2,1)S(1)}, u32[]{:S(2)}, u32[]{:S(2)}) collective-permute-start(bf16[4,128,256]{2,1,0:T(8,128)(2,1)S(1)} %get-tuple-element.54.refs_0_), channel_id=1, source_target_pairs={{0,4},{2,6},{4,0},{6,2},{8,12},{10,14},{12,8},{14,10},{1,5},{3,7},... | collective-permute-start | bytes 786440 | tf_op jit(solution)/shard_map/ppermute | solution.py:493
  98.1 8.9 %collective-permute-start.27 = (bf16[2,128,256]{2,1,0:T(8,128)(2,1)S(1)}, bf16[2,128,256]{2,1,0:T(8,128)(2,1)S(1)}, u32[]{:S(2)}, u32[]{:S(2)}) collective-permute-start(bf16[2,128,256]{2,1,0:T(8,128)(2,1)S(1)} %get-tuple-element.59), channel_id=1, source_target_pairs={{0,8},{2,10},{4,12},{6,14},{8,0},{10,2},{12,4},{14,6},{1,9},{3,11}... | collective-permute-start | bytes 393224 | tf_op jit(solution)/shard_map/ppermute | solution.py:493
  99.6 15.6 %collective-permute-start.29 = (bf16[4,128,256]{2,1,0:T(8,128)(2,1)S(1)}, bf16[4,128,256]{2,1,0:T(8,128)(2,1)S(1)}, u32[]{:S(2)}, u32[]{:S(2)}) collective-permute-start(bf16[4,128,256]{2,1,0:T(8,128)(2,1)S(1)} %get-tuple-element.54.refs_0_), channel_id=1, source_target_pairs={{0,2},{2,0},{4,6},{6,4},{8,10},{10,8},{12,14},{14,12},{1,3},{3,1},... | collective-permute-start | bytes 786440 | tf_op jit(solution)/shard_map/ppermute | solution.py:497
  99.6 12.8 %collective-permute-start.28 = (bf16[2,128,256]{2,1,0:T(8,128)(2,1)S(1)}, bf16[2,128,256]{2,1,0:T(8,128)(2,1)S(1)}, u32[]{:S(2)}, u32[]{:S(2)}) collective-permute-start(bf16[2,128,256]{2,1,0:T(8,128)(2,1)S(1)} %get-tuple-element.58), channel_id=1, source_target_pairs={{0,8},{2,10},{4,12},{6,14},{8,0},{10,2},{12,4},{14,6},{1,9},{3,11}... | collective-permute-start | bytes 393224 | tf_op jit(solution)/shard_map/ppermute | solution.py:493
  109.0 6.2 %collective-permute-start.30 = (bf16[4,128,256]{2,1,0:T(8,128)(2,1)S(1)}, bf16[4,128,256]{2,1,0:T(8,128)(2,1)S(1)}, u32[]{:S(2)}, u32[]{:S(2)}) collective-permute-start(bf16[4,128,256]{2,1,0:T(8,128)(2,1)S(1)} %collective-permute-done.26.refs_1_), channel_id=1, source_target_pairs={{0,2},{2,0},{4,6},{6,4},{8,10},{10,8},{12,14},{14,12},{1,3},{3,1},... | collective-permute-start | bytes 786440 | tf_op jit(solution)/shard_map/ppermute | solution.py:497
  109.0 3.4 %collective-permute-start.31 = (bf16[2,128,256]{2,1,0:T(8,128)(2,1)S(1)}, bf16[2,128,256]{2,1,0:T(8,128)(2,1)S(1)}, u32[]{:S(2)}, u32[]{:S(2)}) collective-permute-start(bf16[2,128,256]{2,1,0:T(8,128)(2,1)S(1)} %collective-permute-done.27.refs_2_), channel_id=1, source_target_pairs={{0,2},{2,0},{4,6},{6,4},{8,10},{10,8},{12,14},{14,12},{1,3},{3,1},... | collective-permute-start | bytes 393224 | tf_op jit(solution)/shard_map/ppermute | solution.py:497
  109.6 5.7 %collective-permute-start.33 = (bf16[2,128,256]{2,1,0:T(8,128)(2,1)S(1)}, bf16[2,128,256]{2,1,0:T(8,128)(2,1)S(1)}, u32[]{:S(2)}, u32[]{:S(2)}) collective-permute-start(bf16[2,128,256]{2,1,0:T(8,128)(2,1)S(1)} %collective-permute-done.27.refs_2_), channel_id=1, source_target_pairs={{0,4},{2,6},{4,0},{6,2},{8,12},{10,14},{12,8},{14,10},{1,5},{3,7},... | collective-permute-start | bytes 393224 | tf_op jit(solution)/shard_map/ppermute | solution.py:493
  112.4 2.8 %collective-permute-start.32 = (bf16[2,128,256]{2,1,0:T(8,128)(2,1)S(1)}, bf16[2,128,256]{2,1,0:T(8,128)(2,1)S(1)}, u32[]{:S(2)}, u32[]{:S(2)}) collective-permute-start(bf16[2,128,256]{2,1,0:T(8,128)(2,1)S(1)} %collective-permute-done.28.refs_3_), channel_id=1, source_target_pairs={{0,2},{2,0},{4,6},{6,4},{8,10},{10,8},{12,14},{14,12},{1,3},{3,1},... | collective-permute-start | bytes 393224 | tf_op jit(solution)/shard_map/ppermute | solution.py:497
  112.4 5.9 %collective-permute-start.34 = (bf16[2,128,256]{2,1,0:T(8,128)(2,1)S(1)}, bf16[2,128,256]{2,1,0:T(8,128)(2,1)S(1)}, u32[]{:S(2)}, u32[]{:S(2)}) collective-permute-start(bf16[2,128,256]{2,1,0:T(8,128)(2,1)S(1)} %collective-permute-done.28.refs_3_), channel_id=1, source_target_pairs={{0,4},{2,6},{4,0},{6,2},{8,12},{10,14},{12,8},{14,10},{1,5},{3,7},... | collective-permute-start | bytes 393224 | tf_op jit(solution)/shard_map/ppermute | solution.py:493
  115.2 3.1 %collective-permute-start.35 = (bf16[2,128,256]{2,1,0:T(8,128)(2,1)S(1)}, bf16[2,128,256]{2,1,0:T(8,128)(2,1)S(1)}, u32[]{:S(2)}, u32[]{:S(2)}) collective-permute-start(bf16[2,128,256]{2,1,0:T(8,128)(2,1)S(1)} %collective-permute-done.33.refs_0_), channel_id=1, source_target_pairs={{0,2},{2,0},{4,6},{6,4},{8,10},{10,8},{12,14},{14,12},{1,3},{3,1},... | collective-permute-start | bytes 393224 | tf_op jit(solution)/shard_map/ppermute | solution.py:497
  118.4 1.3 %collective-permute-start.36 = (bf16[2,128,256]{2,1,0:T(8,128)(2,1)S(1)}, bf16[2,128,256]{2,1,0:T(8,128)(2,1)S(1)}, u32[]{:S(2)}, u32[]{:S(2)}) collective-permute-start(bf16[2,128,256]{2,1,0:T(8,128)(2,1)S(1)} %collective-permute-done.34.refs_1_), channel_id=1, source_target_pairs={{0,2},{2,0},{4,6},{6,4},{8,10},{10,8},{12,14},{14,12},{1,3},{3,1},... | collective-permute-start | bytes 393224 | tf_op jit(solution)/shard_map/ppermute | solution.py:497

commit v15 on v14

--- a/solution.py
+++ b/solution.py
@@ -158,6 +158,7 @@
         in_specs=[vmem_spec],
         out_specs=vmem_spec,
         compiler_params=small,
+        cost_estimate=long,
         name="walker_major",
     )(orbitals)
 
@@ -296,15 +297,38 @@
     return lambda picked: ref[picked]
 
 
-def early_kernel(walkers, field_here, field_one, field_two, field_three, own, own_theirs, *refs):
-    theirs, theirs_x, near, near_x, near_theirs, near_theirs_x, summed_ref = refs
+def own_kernel(walkers, field_ref, own, own_theirs, summed_ref):
     _, _, x = place()
-    rows = own.shape[1]
     sources = [
-        (field_here, 0, of_pair(own, x), of_pair(own, 1 - x)),
-        (field_here, 1, of_pair(own_theirs, x), of_pair(own_theirs, 1 - x)),
-        (field_three, 1, of_one(theirs), of_one(theirs_x)),
+        (field_ref, 0, of_pair(own, x), of_pair(own, 1 - x)),
+        (field_ref, 1, of_pair(own_theirs, x), of_pair(own_theirs, 1 - x)),
     ]
+
+    def body(picked):
+        tiles = block_operators(x, walkers, sources, picked)
+        for w in range(walkers):
+            summed_ref[(w, *picked)] = tiles[0][w].astype(wide) + tiles[1][w].astype(wide)
+
+    over_tiles(*summed_ref.shape[1:], body)
+
+
+def own_operator(walkers, field, own, own_theirs):
+    _, rows, order = own.shape
+    return pl.pallas_call(
+        functools.partial(own_kernel, walkers),
+        out_shape=jax.ShapeDtypeStruct((walkers, rows, order), wide),
+        in_specs=[vmem_spec] * 3,
+        out_specs=vmem_spec,
+        compiler_params=large,
+        name="own_operator",
+    )(field, own, own_theirs)
+
+
+def early_kernel(summed_ref, field_one, field_two, field_three, *refs):
+    theirs, theirs_x, near, near_x, near_theirs, near_theirs_x, out_ref = refs
+    walkers, rows, order = summed_ref.shape
+    _, _, x = place()
+    sources = [(field_three, 1, of_one(theirs), of_one(theirs_x))]
     for index, field_ref in enumerate((field_one, field_two)):
         top = 2 * rows * index
         sources += [
@@ -316,21 +340,20 @@
         tiles = block_operators(x, walkers, sources, picked)
         for w in range(walkers):
             parts = [block[w].astype(wide) for block in tiles]
-            summed_ref[(w, *picked)] = sum(parts[1:], parts[0])
-
-    over_tiles(*summed_ref.shape[1:], body)
-
-
-def early_operator(walkers, fields, own, own_theirs, blocks):
-    _, rows, order = own.shape
-    return pl.pallas_call(
-        functools.partial(early_kernel, walkers),
-        out_shape=jax.ShapeDtypeStruct((walkers, rows, order), wide),
-        in_specs=[vmem_spec] * (6 + len(blocks)),
+            out_ref[(w, *picked)] = summed_ref[(w, *picked)] + sum(parts[1:], parts[0])
+
+    over_tiles(rows, order, body)
+
+
+def early_operator(summed, fields, blocks):
+    return pl.pallas_call(
+        early_kernel,
+        out_shape=jax.ShapeDtypeStruct(summed.shape, wide),
+        in_specs=[vmem_spec] * (4 + len(blocks)),
         out_specs=vmem_spec,
         compiler_params=large,
         name="early_operator",
-    )(*fields, own, own_theirs, *blocks)
+    )(summed, *fields, *blocks)
 
 
 def late_kernel(summed_ref, field_ref, mine, mine_x, operator_ref):
@@ -521,17 +544,15 @@
     greens = (green_blocks, one, two, green_three)
     bias = chip_bias(greens, half_chol, half_theirs)
     start = walker_major(orbitals)
-    start_two = to_chip(after(start, one, two), 2)
-    start_three = to_chip(after(start_two, bias), 1)
-    crossed = to_chip(after(far_messages[0], two), 3)
-    straight = to_chip(after(far_messages[1], crossed), 3)
     start_one = to_chip(after(start, one, two), 1)
     bias_theirs = to_core(bias)
 
-    bias_ready = after(bias, start_three, straight, start_one)
+    bias_ready = after(bias, start_one)
     bias_shift, field = chip_field(bias_ready, bias_theirs, constants, constants_theirs, vectors)
+    own_summed = own_operator(walkers, field, far_messages[2], own_theirs)
     near_rows = jnp.concatenate([after(one, *far_messages)[rows:], two[rows:]])
     near_rows_theirs = to_core(after(near_rows, bias))
+    crossed = to_chip(far_messages[0], 3)
     crossed_theirs = to_core(after(crossed, bias))
     field_one = to_chip(after(field, near_rows_theirs, crossed_theirs), 1)
     field_two = to_chip(after(field, near_rows_theirs, crossed_theirs), 2)
@@ -540,15 +561,18 @@
     crossed_x_theirs = to_core(crossed_x)
     near_rows_x = across(near_rows)
     near_rows_x_theirs = to_core(after(near_rows_x, bias))
-    fields = (field, field_one, field_two, field_three)
+    fields = (field_one, field_two, field_three)
     blocks = (crossed_theirs, crossed_x_theirs, near_rows, near_rows_x)
     blocks += (near_rows_theirs, near_rows_x_theirs)
-    summed = early_operator(walkers, fields, far_messages[2], own_theirs, blocks)
+    summed = early_operator(own_summed, fields, blocks)
+    straight = to_chip(after(far_messages[1], crossed), 3)
     straight_x = across(after(straight, bias))
     operator = split_operator(summed, field_three, straight, straight_x)
+    start_two = to_chip(after(start, one, two), 2)
+    start_three = to_chip(after(start_two, bias), 1)
     start_theirs = to_core(start)
     start_one_theirs = to_core(after(start_one, bias))
-    start_two_theirs = to_core(start_two)
+    start_two_theirs = to_core(after(start_two, near_rows_x))
     start_three_theirs = to_core(after(start_three, summed))
 
     groups = (start, start_one, start_two, start_three)

time: 121 us -> 119 us (0.983)
  starting transfers between devices: 29.9 us -> 25.5 us
  waiting for transfers between devices: 70.9 us -> 73.9 us
  Pallas kernels: 18.8 us -> 17.5 us
    ppermute x3, waiting for transfers between devices: 0.98 us -> 10.1 us  [across(): return lax.ppermute(value, 'walk', [(0, 1), (1, 0)])]
    ppermute x16, waiting for transfers between devices: 68.1 us -> 61.2 us  [to_chip(): return lax.ppermute(value, 'chol', [(i, i ^ 2 * step) for i in range(8)])]
    ppermute x16, starting transfers between devices: 22.1 us -> 18 us  [to_chip(): return lax.ppermute(value, 'chol', [(i, i ^ 2 * step) for i in range(8)])]
    pallas_call x1 -> x2, Pallas kernels: 3.91 us -> 4.26 us  [the longest x1 2.92 us: early_operator(): pl.pallas_call(early_kernel, out_shape=jax.ShapeDtypeStruct(summed.shape,...]
where the time goes in v15:
time: 119 us
  waiting for transfers between devices  73.9 us (62%)
  starting transfers between devices  25.5 us (21%)
  Pallas kernels  17.5 us (15%)
    ppermute x16, waiting for transfers between devices, to_chip(): return lax.ppermute(value, 'chol', [(i, i ^ 2 * step) for i in range(8)])  61.2 us
    ppermute x16, starting transfers between devices, to_chip(): return lax.ppermute(value, 'chol', [(i, i ^ 2 * step) for i in range(8)])  18 us
    ppermute x3, waiting for transfers between devices, across(): return lax.ppermute(value, 'walk', [(0, 1), (1, 0)])  10.1 us
    ppermute x3, starting transfers between devices, across(): return lax.ppermute(value, 'walk', [(0, 1), (1, 0)])  4.58 us
    pallas_call x1, Pallas kernels, near_packed(): pl.pallas_call(near_pack_kernel, out_shape=[jax.ShapeDtypeStruct((3 * row...  3.37 us
    ppermute x18, starting transfers between devices, to_core(): return lax.ppermute(value, 'chol', [(i, i ^ 1) for i in range(8)])  2.95 us
    pallas_call x1, Pallas kernels, early_operator(): pl.pallas_call(early_kernel, out_shape=jax.ShapeDtypeStruct(summed.shape,...  2.92 us
    ppermute x18, waiting for transfers between devices, to_core(): return lax.ppermute(value, 'chol', [(i, i ^ 1) for i in range(8)])  2.54 us
  transfers between devices with their start and end apart: 37, of which 15 were waited for; matrix products, arithmetic and copies ran while one was open for 0% of the time, Pallas kernels for 10%

profile of v15, /device:TPU:0, one launch (start us, length us, event | category | flops | bytes accessed | tf_op | source)
XLA Modules:
  0.0 119.0 jit_solution(1910082966956286522)
XLA Ops:
  0.6 3.4 %near_packed.1 = (bf16[384,1024]{1,0:T(8,128)(2,1)}, bf16[384,1024]{1,0:T(8,128)(2,1)}) custom-call(bf16[2,1024,1024]{2,1,0:T(8,128)(2,1)} %full_ref.2, bf16[4,128,256]{2,1,0:T(8,128)(2,1)} %here_ref.1), custom_call_target="tpu_custom_call" | custom-call | tf_op jit(solution)/shard_map/near_packed/pallas_call | solution.py:112
  4.0 3.1 %collective-permute-start = (bf16[384,1024]{1,0:T(8,128)(2,1)}, bf16[384,1024]{1,0:T(8,128)(2,1)S(1)}, u32[]{:S(2)}, u32[]{:S(2)}) collective-permute-start(bf16[384,1024]{1,0:T(8,128)(2,1)} %get-tuple-element.30), channel_id=1, source_target_pairs={{0,4},{2,6},{4,0},{6,2},{8,12},{10,14},{12,8},{14,10},{1,5},{3,7},... | collective-permute-start | bytes 2359304 | tf_op jit(solution)/shard_map/ppermute | solution.py:516
  7.1 2.6 %collective-permute-start.1 = (bf16[384,1024]{1,0:T(8,128)(2,1)}, bf16[384,1024]{1,0:T(8,128)(2,1)S(1)}, u32[]{:S(2)}, u32[]{:S(2)}) collective-permute-start(bf16[384,1024]{1,0:T(8,128)(2,1)} %get-tuple-element.31), channel_id=1, source_target_pairs={{0,8},{2,10},{4,12},{6,14},{8,0},{10,2},{12,4},{14,6},{1,9},{3,11}... | collective-permute-start | bytes 2359304 | tf_op jit(solution)/shard_map/ppermute | solution.py:516
  9.7 2.5 %far_packed.1 = (bf16[128,1024]{1,0:T(8,128)(2,1)}, bf16[128,1024]{1,0:T(8,128)(2,1)}, bf16[2,128,1024]{2,1,0:T(8,128)(2,1)}, bf16[2,128,1024]{2,1,0:T(8,128)(2,1)}) custom-call(bf16[2,1024,1024]{2,1,0:T(8,128)(2,1)} %full_ref.2), custom_call_target="tpu_custom_call" | custom-call | flops 99999997952 | tf_op jit(solution)/shard_map/far_packed/pallas_call | solution.py:137
  12.2 0.6 collective-permute-start.3
  13.2 1.2 collective-permute-done.4.noise_there_ref
  14.4 0.6 copy-done.8
  15.0 25.9 %collective-permute-done.one_ref = bf16[384,1024]{1,0:T(8,128)(2,1)S(1)} collective-permute-done((bf16[384,1024]{1,0:T(8,128)(2,1)}, bf16[384,1024]{1,0:T(8,128)(2,1)S(1)}, u32[]{:S(2)}, u32[]{:S(2)}) %collective-permute-start) | collective-permute-done | bytes 786464 | tf_op jit(solution)/shard_map/ppermute | solution.py:516
  40.9 10.3 %collective-permute-done.1.two_ref = bf16[384,1024]{1,0:T(8,128)(2,1)S(1)} collective-permute-done((bf16[384,1024]{1,0:T(8,128)(2,1)}, bf16[384,1024]{1,0:T(8,128)(2,1)S(1)}, u32[]{:S(2)}, u32[]{:S(2)}) %collective-permute-start.1) | collective-permute-done | bytes 786464 | tf_op jit(solution)/shard_map/ppermute | solution.py:516
  51.3 0.5 walker_major.1.refs_0_
  51.9 2.1 %collective-permute-start.6 = (bf16[4,128,256]{2,1,0:T(8,128)(2,1)S(1)}, bf16[4,128,256]{2,1,0:T(8,128)(2,1)S(1)}, u32[]{:S(2)}, u32[]{:S(2)}) collective-permute-start(bf16[4,128,256]{2,1,0:T(8,128)(2,1)S(1)} %walker_major.1.refs_0_), channel_id=1, source_target_pairs={{0,4},{2,6},{4,0},{6,2},{8,12},{10,14},{12,8},{14,10},{1,5},{3,7},... | collective-permute-start | bytes 786440 | tf_op jit(solution)/shard_map/ppermute | solution.py:516
  54.0 1.1 collective-permute-start.20
  55.2 1.6 %collective-permute-start.16 = (bf16[512,1024]{1,0:T(8,128)(2,1)S(1)}, bf16[512,1024]{1,0:T(8,128)(2,1)S(1)}, u32[]{:S(2)}, u32[]{:S(2)}) collective-permute-start(bf16[512,1024]{1,0:T(8,128)(2,1)S(1)} %pad_maximum_fusion.refs_2_), channel_id=1, source_target_pairs={{0,1},{1,0},{2,3},{3,2},{4,5},{5,4},{6,7},{7,6},{8,9},{9,8},{10,11... | collective-permute-start | bytes 3145736 | tf_op jit(solution)/shard_map/ppermute | solution.py:524
  56.8 7.1 %collective-permute-done.5.three_ref = bf16[128,1024]{1,0:T(8,128)(2,1)S(1)} collective-permute-done((bf16[128,1024]{1,0:T(8,128)(2,1)S(1)}, bf16[128,1024]{1,0:T(8,128)(2,1)S(1)}, u32[]{:S(2)}, u32[]{:S(2)}) %collective-permute-start.5) | collective-permute-done | bytes 262176 | tf_op jit(solution)/shard_map/ppermute | solution.py:516
  63.9 2.2 %chip_bias.1.mine_ref = f32[16,128]{1,0:T(8,128)S(1)} custom-call(bf16[4,128,256]{2,1,0:T(8,128)(2,1)S(1)} %copy-done.2, bf16[384,1024]{1,0:T(8,128)(2,1)S(1)} %collective-permute-done.one_ref, bf16[384,1024]{1,0:T(8,128)(2,1)S(1)} %collective-permute-done.1.two_ref, bf16[128,1024]{1,0:T(8,128)(2,1)S(1)} %collective-permute-done.5.three_ref, ...), custom_call_target="tpu_custom_call" | custom-call | flops 99999997952 | tf_op jit(solution)/shard_map/chip_bias/pallas_call | solution.py:206
  66.2 1.6 %collective-permute-start.14 = (bf16[128,1024]{1,0:T(8,128)(2,1)}, bf16[128,1024]{1,0:T(8,128)(2,1)S(1)}, u32[]{:S(2)}, u32[]{:S(2)}) collective-permute-start(bf16[128,1024]{1,0:T(8,128)(2,1)} %collective-permute-done.9), channel_id=1, source_target_pairs={{0,1},{1,0},{2,3},{3,2},{4,5},{5,4},{6,7},{7,6},{8,9},{9,8},{10,11... | collective-permute-start | bytes 786440 | tf_op jit(solution)/shard_map/ppermute | solution.py:524
  67.8 0.5 collective-permute-start.7
  68.3 0.9 collective-permute-start.18
  69.2 4.2 %collective-permute-done.16.refs_3_ = bf16[512,1024]{1,0:T(8,128)(2,1)S(1)} collective-permute-done((bf16[512,1024]{1,0:T(8,128)(2,1)S(1)}, bf16[512,1024]{1,0:T(8,128)(2,1)S(1)}, u32[]{:S(2)}, u32[]{:S(2)}) %collective-permute-start.16) | collective-permute-done | bytes 1048608 | tf_op jit(solution)/shard_map/ppermute | solution.py:524
  73.4 0.4 collective-permute-start.21
  73.8 2.4 %collective-permute-done.14 = bf16[128,1024]{1,0:T(8,128)(2,1)S(1)} collective-permute-done((bf16[128,1024]{1,0:T(8,128)(2,1)}, bf16[128,1024]{1,0:T(8,128)(2,1)S(1)}, u32[]{:S(2)}, u32[]{:S(2)}) %collective-permute-start.14) | collective-permute-done | bytes 262176 | tf_op jit(solution)/shard_map/ppermute | solution.py:524
  76.2 0.5 collective-permute-start.17
  76.7 0.6 chip_field.1
  77.3 0.4 collective-permute-start.11
  77.7 1.6 %collective-permute-done.18.mine = bf16[128,1024]{1,0:T(8,128)(2,1)S(1)} collective-permute-done((bf16[128,1024]{1,0:T(8,128)(2,1)S(1)}, bf16[128,1024]{1,0:T(8,128)(2,1)S(1)}, u32[]{:S(2)}, u32[]{:S(2)}) %collective-permute-start.18) | collective-permute-done | bytes 262176 | tf_op jit(solution)/shard_map/ppermute | solution.py:516
  79.3 1.1 collective-permute-start.12
  80.4 2.6 %collective-permute-start.13 = (f32[16,128]{1,0:T(8,128)S(1)}, f32[16,128]{1,0:T(8,128)S(1)}, u32[]{:S(2)}, u32[]{:S(2)}) collective-permute-start(f32[16,128]{1,0:T(8,128)S(1)} %get-tuple-element.44.field_ref), channel_id=1, source_target_pairs={{0,12},{2,14},{4,8},{6,10},{8,4},{10,6},{12,0},{14,2},{1,13},{3,15... | collective-permute-start | bytes 24584 | tf_op jit(solution)/shard_map/ppermute | solution.py:516
  83.1 1.3 %own_operator.1.summed_ref = f32[4,128,1024]{2,1,0:T(8,128)S(1)} custom-call(f32[16,128]{1,0:T(8,128)S(1)} %get-tuple-element.44.field_ref, bf16[2,128,1024]{2,1,0:T(8,128)(2,1)S(1)} %copy-done.1, bf16[2,128,1024]{2,1,0:T(8,128)(2,1)S(1)} %collective-permute-done.3.own_theirs), custom_call_target="tpu_custom_call" | custom-call | tf_op jit(solution)/shard_map/own_operator/pallas_call | solution.py:317
  84.6 1.5 %collective-permute-start.19 = (bf16[128,1024]{1,0:T(8,128)(2,1)S(1)}, bf16[128,1024]{1,0:T(8,128)(2,1)S(1)}, u32[]{:S(2)}, u32[]{:S(2)}) collective-permute-start(bf16[128,1024]{1,0:T(8,128)(2,1)S(1)} %collective-permute-done.18.mine), channel_id=1, source_target_pairs={{0,1},{1,0},{2,3},{3,2},{4,5},{5,4},{6,7},{7,6},{8,9},{9,8},{10,11... | collective-permute-start | bytes 786440 | tf_op jit(solution)/shard_map/ppermute | solution.py:524
  86.1 0.2 collective-permute-start.23
  86.2 0.4 collective-permute-start.24
  86.6 2.9 %early_operator.1.summed_ref = f32[4,128,1024]{2,1,0:T(8,128)S(1)} custom-call(f32[4,128,1024]{2,1,0:T(8,128)S(1)} %own_operator.1.summed_ref, f32[16,128]{1,0:T(8,128)S(1)} %collective-permute-done.11.field_one, f32[16,128]{1,0:T(8,128)S(1)} %collective-permute-done.12.field_two, f32[16,128]{1,0:T(8,128)S(1)} %collective-permute-done.13.field_three.field_ref, ...), custom_call_target="tpu_custom_call" | custom-call | tf_op jit(solution)/shard_map/early_operator/pallas_call | solution.py:349
  89.5 0.2 collective-permute-start.25
  89.7 3.5 %collective-permute-done.19.mine_x = bf16[128,1024]{1,0:T(8,128)(2,1)S(1)} collective-permute-done((bf16[128,1024]{1,0:T(8,128)(2,1)S(1)}, bf16[128,1024]{1,0:T(8,128)(2,1)S(1)}, u32[]{:S(2)}, u32[]{:S(2)}) %collective-permute-start.19) | collective-permute-done | bytes 262176 | tf_op jit(solution)/shard_map/ppermute | solution.py:524
  93.3 1.1 split_operator.1.operator_ref
  94.4 0.9 first_application.1
  95.4 1.8 %collective-permute-start.27 = (bf16[2,128,256]{2,1,0:T(8,128)(2,1)S(1)}, bf16[2,128,256]{2,1,0:T(8,128)(2,1)S(1)}, u32[]{:S(2)}, u32[]{:S(2)}) collective-permute-start(bf16[2,128,256]{2,1,0:T(8,128)(2,1)S(1)} %get-tuple-element.59), channel_id=1, source_target_pairs={{0,8},{2,10},{4,12},{6,14},{8,0},{10,2},{12,4},{14,6},{1,9},{3,11}... | collective-permute-start | bytes 393224 | tf_op jit(solution)/shard_map/ppermute | solution.py:516
  97.1 1.2 %collective-permute-start.28 = (bf16[2,128,256]{2,1,0:T(8,128)(2,1)S(1)}, bf16[2,128,256]{2,1,0:T(8,128)(2,1)S(1)}, u32[]{:S(2)}, u32[]{:S(2)}) collective-permute-start(bf16[2,128,256]{2,1,0:T(8,128)(2,1)S(1)} %get-tuple-element.58), channel_id=1, source_target_pairs={{0,8},{2,10},{4,12},{6,14},{8,0},{10,2},{12,4},{14,6},{1,9},{3,11}... | collective-permute-start | bytes 393224 | tf_op jit(solution)/shard_map/ppermute | solution.py:516
  98.4 6.5 %collective-permute-done.27.refs_2_ = bf16[2,128,256]{2,1,0:T(8,128)(2,1)S(1)} collective-permute-done((bf16[2,128,256]{2,1,0:T(8,128)(2,1)S(1)}, bf16[2,128,256]{2,1,0:T(8,128)(2,1)S(1)}, u32[]{:S(2)}, u32[]{:S(2)}) %collective-permute-start.27) | collective-permute-done | bytes 131104 | tf_op jit(solution)/shard_map/ppermute | solution.py:516
  104.9 2.8 %collective-permute-done.26.refs_1_ = bf16[4,128,256]{2,1,0:T(8,128)(2,1)S(1)} collective-permute-done((bf16[4,128,256]{2,1,0:T(8,128)(2,1)S(1)}, bf16[4,128,256]{2,1,0:T(8,128)(2,1)S(1)}, u32[]{:S(2)}, u32[]{:S(2)}) %collective-permute-start.26) | collective-permute-done | bytes 262176 | tf_op jit(solution)/shard_map/ppermute | solution.py:516
  107.7 0.5 collective-permute-start.31
  108.3 1.5 %collective-permute-done.28.refs_3_ = bf16[2,128,256]{2,1,0:T(8,128)(2,1)S(1)} collective-permute-done((bf16[2,128,256]{2,1,0:T(8,128)(2,1)S(1)}, bf16[2,128,256]{2,1,0:T(8,128)(2,1)S(1)}, u32[]{:S(2)}, u32[]{:S(2)}) %collective-permute-start.28) | collective-permute-done | bytes 131104 | tf_op jit(solution)/shard_map/ppermute | solution.py:516
  109.9 0.4 collective-permute-start.34
  110.3 3.9 %collective-permute-done.33.refs_0_ = bf16[2,128,256]{2,1,0:T(8,128)(2,1)S(1)} collective-permute-done((bf16[2,128,256]{2,1,0:T(8,128)(2,1)S(1)}, bf16[2,128,256]{2,1,0:T(8,128)(2,1)S(1)}, u32[]{:S(2)}, u32[]{:S(2)}) %collective-permute-start.33) | collective-permute-done | bytes 131104 | tf_op jit(solution)/shard_map/ppermute | solution.py:516
  114.2 0.8 base_application.1.base_ref
  115.0 1.4 %collective-permute-done.34.refs_1_ = bf16[2,128,256]{2,1,0:T(8,128)(2,1)S(1)} collective-permute-done((bf16[2,128,256]{2,1,0:T(8,128)(2,1)S(1)}, bf16[2,128,256]{2,1,0:T(8,128)(2,1)S(1)}, u32[]{:S(2)}, u32[]{:S(2)}) %collective-permute-start.34) | collective-permute-done | bytes 131104 | tf_op jit(solution)/shard_map/ppermute | solution.py:516
  116.4 1.3 %collective-permute-done.36.refs_3_ = bf16[2,128,256]{2,1,0:T(8,128)(2,1)S(1)} collective-permute-done((bf16[2,128,256]{2,1,0:T(8,128)(2,1)S(1)}, bf16[2,128,256]{2,1,0:T(8,128)(2,1)S(1)}, u32[]{:S(2)}, u32[]{:S(2)}) %collective-permute-start.36) | collective-permute-done | bytes 131104 | tf_op jit(solution)/shard_map/ppermute | solution.py:520
  117.7 1.2 %second_application.1 = f32[1,128,4,256]{3,2,1,0:T(4,128)} custom-call(bf16[4,256,1024]{2,1,0:T(8,128)(2,1)S(1)} %split_operator.1.operator_ref, f32[4,128,256]{2,1,0:T(8,128)S(1)} %base_application.1.base_ref, bf16[2,128,256]{2,1,0:T(8,128)(2,1)S(1)} %collective-permute-done.33.refs_0_, bf16[2,128,256]{2,1,0:T(8,128)(2,1)S(1)} %collective-permute-done.34.refs_1_, ...), custom_call_target="tpu_custom_call" | custom-call | tf_op jit(solution)/shard_map/second_application/pallas_call | solution.py:504
  (73 shorter events, 1.2 us)
Async XLA Ops:
  4.0 36.9 %collective-permute-start = (bf16[384,1024]{1,0:T(8,128)(2,1)}, bf16[384,1024]{1,0:T(8,128)(2,1)S(1)}, u32[]{:S(2)}, u32[]{:S(2)}) collective-permute-start(bf16[384,1024]{1,0:T(8,128)(2,1)} %get-tuple-element.30), channel_id=1, source_target_pairs={{0,4},{2,6},{4,0},{6,2},{8,12},{10,14},{12,8},{14,10},{1,5},{3,7},... | collective-permute-start | bytes 2359304 | tf_op jit(solution)/shard_map/ppermute | solution.py:516
  7.1 5.7 %copy-start.12 = (f32[2]{0:T(128)S(1)}, f32[2]{0:T(128)}, u32[]{:S(2)}) copy-start(f32[2]{0:T(128)} %param.9) | copy-start | bytes 28
  7.1 5.9 %copy-start.11 = (f32[4,2]{0,1:T(2,128)S(1)}, f32[4,2]{0,1:T(2,128)}, u32[]{:S(2)}) copy-start(f32[4,2]{0,1:T(2,128)} %param.10) | copy-start | bytes 100
  7.1 44.2 %copy-start = (f32[1,128,4,256]{3,2,1,0:T(4,128)S(1)}, f32[1,128,4,256]{3,2,1,0:T(4,128)}, u32[]{:S(2)}) copy-start(f32[1,128,4,256]{3,2,1,0:T(4,128)} %orbitals_ref.3) | copy-start | bytes 1572868
  7.1 44.1 %collective-permute-start.1 = (bf16[384,1024]{1,0:T(8,128)(2,1)}, bf16[384,1024]{1,0:T(8,128)(2,1)S(1)}, u32[]{:S(2)}, u32[]{:S(2)}) collective-permute-start(bf16[384,1024]{1,0:T(8,128)(2,1)} %get-tuple-element.31), channel_id=1, source_target_pairs={{0,8},{2,10},{4,12},{6,14},{8,0},{10,2},{12,4},{14,6},{1,9},{3,11}... | collective-permute-start | bytes 2359304 | tf_op jit(solution)/shard_map/ppermute | solution.py:516
  9.7 41.5 %collective-permute-start.2 = (bf16[2,1024,256]{2,1,0:T(8,128)(2,1)}, bf16[2,1024,256]{2,1,0:T(8,128)(2,1)}, u32[]{:S(2)}, u32[]{:S(2)}) collective-permute-start(bf16[2,1024,256]{2,1,0:T(8,128)(2,1)} %mine_ref.1), channel_id=1, source_target_pairs={{0,2},{2,0},{4,6},{6,4},{8,10},{10,8},{12,14},{14,12},{1,3},{3,1},... | collective-permute-start | bytes 3145736 | tf_op jit(solution)/shard_map/ppermute | solution.py:520
  12.2 2.7 %collective-permute-start.3 = (bf16[2,128,1024]{2,1,0:T(8,128)(2,1)}, bf16[2,128,1024]{2,1,0:T(8,128)(2,1)S(1)}, u32[]{:S(2)}, u32[]{:S(2)}) collective-permute-start(bf16[2,128,1024]{2,1,0:T(8,128)(2,1)} %get-tuple-element.36), channel_id=1, source_target_pairs={{0,2},{2,0},{4,6},{6,4},{8,10},{10,8},{12,14},{14,12},{1,3},{3,1},... | collective-permute-start | bytes 1572872 | tf_op jit(solution)/shard_map/ppermute | solution.py:520
  13.2 38.6 %copy-start.5 = (f32[16,128]{1,0:T(8,128)}, f32[16,128]{1,0:T(8,128)S(1)}, u32[]{:S(2)}) copy-start(f32[16,128]{1,0:T(8,128)S(1)} %broadcast_in_dim.10.noise_ref) | copy-start | bytes 24580
  13.2 1.2 collective-permute-start.4
  15.0 51.2 %collective-permute-start.9 = (bf16[128,1024]{1,0:T(8,128)(2,1)}, bf16[128,1024]{1,0:T(8,128)(2,1)}, u32[]{:S(2)}, u32[]{:S(2)}) collective-permute-start(bf16[128,1024]{1,0:T(8,128)(2,1)} %get-tuple-element.33), channel_id=1, source_target_pairs={{0,12},{2,14},{4,8},{6,10},{8,4},{10,6},{12,0},{14,2},{1,13},{3,15... | collective-permute-start | bytes 786440 | tf_op jit(solution)/shard_map/ppermute | solution.py:516
  51.2 12.7 %collective-permute-start.5 = (bf16[128,1024]{1,0:T(8,128)(2,1)S(1)}, bf16[128,1024]{1,0:T(8,128)(2,1)S(1)}, u32[]{:S(2)}, u32[]{:S(2)}) collective-permute-start(bf16[128,1024]{1,0:T(8,128)(2,1)S(1)} %slice.15), channel_id=1, source_target_pairs={{0,4},{2,6},{4,0},{6,2},{8,12},{10,14},{12,8},{14,10},{1,5},{3,7},... | collective-permute-start | bytes 786440 | tf_op jit(solution)/shard_map/ppermute | solution.py:516
  51.9 12.1 %copy-start.2 = (bf16[4,128,256]{2,1,0:T(8,128)(2,1)S(1)}, bf16[4,128,256]{2,1,0:T(8,128)(2,1)}, u32[]{:S(2)}) copy-start(bf16[4,128,256]{2,1,0:T(8,128)(2,1)} %here_ref.1) | copy-start | bytes 786436
  51.9 12.1 %copy-start.7 = (bf16[2,1024,256]{2,1,0:T(8,128)(2,1)S(1)}, bf16[2,1024,256]{2,1,0:T(8,128)(2,1)}, u32[]{:S(2)}) copy-start(bf16[2,1024,256]{2,1,0:T(8,128)(2,1)} %mine_ref.1) | copy-start | bytes 3145732
  51.9 15.9 %collective-permute-start.6 = (bf16[4,128,256]{2,1,0:T(8,128)(2,1)S(1)}, bf16[4,128,256]{2,1,0:T(8,128)(2,1)S(1)}, u32[]{:S(2)}, u32[]{:S(2)}) collective-permute-start(bf16[4,128,256]{2,1,0:T(8,128)(2,1)S(1)} %walker_major.1.refs_0_), channel_id=1, source_target_pairs={{0,4},{2,6},{4,0},{6,2},{8,12},{10,14},{12,8},{14,10},{1,5},{3,7},... | collective-permute-start | bytes 786440 | tf_op jit(solution)/shard_map/ppermute | solution.py:516
  54.0 14.3 %collective-permute-start.20 = (bf16[4,128,256]{2,1,0:T(8,128)(2,1)S(1)}, bf16[4,128,256]{2,1,0:T(8,128)(2,1)S(1)}, u32[]{:S(2)}, u32[]{:S(2)}) collective-permute-start(bf16[4,128,256]{2,1,0:T(8,128)(2,1)S(1)} %walker_major.1.refs_0_), channel_id=1, source_target_pairs={{0,8},{2,10},{4,12},{6,14},{8,0},{10,2},{12,4},{14,6},{1,9},{3,11}... | collective-permute-start | bytes 786440 | tf_op jit(solution)/shard_map/ppermute | solution.py:516
  55.2 13.1 %copy-start.10 = (bf16[128,1024]{1,0:T(8,128)(2,1)S(1)}, bf16[128,1024]{1,0:T(8,128)(2,1)}, u32[]{:S(2)}) copy-start(bf16[128,1024]{1,0:T(8,128)(2,1)} %get-tuple-element.47) | copy-start | bytes 786436
  55.2 21.5 %copy-start.6 = (f32[16,128]{1,0:T(8,128)S(1)}, f32[16,128]{1,0:T(8,128)}, u32[]{:S(2)}) copy-start(f32[16,128]{1,0:T(8,128)} %copy-done.5) | copy-start | bytes 24580
  55.2 21.5 %copy-start.9 = (f32[16,128]{1,0:T(8,128)S(1)}, f32[16,128]{1,0:T(8,128)}, u32[]{:S(2)}) copy-start(f32[16,128]{1,0:T(8,128)} %copy-done.8) | copy-start | bytes 24580
  55.2 18.2 %collective-permute-start.16 = (bf16[512,1024]{1,0:T(8,128)(2,1)S(1)}, bf16[512,1024]{1,0:T(8,128)(2,1)S(1)}, u32[]{:S(2)}, u32[]{:S(2)}) collective-permute-start(bf16[512,1024]{1,0:T(8,128)(2,1)S(1)} %pad_maximum_fusion.refs_2_), channel_id=1, source_target_pairs={{0,1},{1,0},{2,3},{3,2},{4,5},{5,4},{6,7},{7,6},{8,9},{9,8},{10,11... | collective-permute-start | bytes 3145736 | tf_op jit(solution)/shard_map/ppermute | solution.py:524
  66.2 16.9 %copy-start.1 = (bf16[2,128,1024]{2,1,0:T(8,128)(2,1)S(1)}, bf16[2,128,1024]{2,1,0:T(8,128)(2,1)}, u32[]{:S(2)}) copy-start(bf16[2,128,1024]{2,1,0:T(8,128)(2,1)} %get-tuple-element.35.own) | copy-start | bytes 1572868
  66.2 10.0 %collective-permute-start.14 = (bf16[128,1024]{1,0:T(8,128)(2,1)}, bf16[128,1024]{1,0:T(8,128)(2,1)S(1)}, u32[]{:S(2)}, u32[]{:S(2)}) collective-permute-start(bf16[128,1024]{1,0:T(8,128)(2,1)} %collective-permute-done.9), channel_id=1, source_target_pairs={{0,1},{1,0},{2,3},{3,2},{4,5},{5,4},{6,7},{7,6},{8,9},{9,8},{10,11... | collective-permute-start | bytes 786440 | tf_op jit(solution)/shard_map/ppermute | solution.py:524
  67.8 8.5 %collective-permute-start.10 = (bf16[128,1024]{1,0:T(8,128)(2,1)}, bf16[128,1024]{1,0:T(8,128)(2,1)S(1)}, u32[]{:S(2)}, u32[]{:S(2)}) collective-permute-start(bf16[128,1024]{1,0:T(8,128)(2,1)} %collective-permute-done.9), channel_id=1, source_target_pairs={{0,2},{2,0},{4,6},{6,4},{8,10},{10,8},{12,14},{14,12},{1,3},{3,1},... | collective-permute-start | bytes 786440 | tf_op jit(solution)/shard_map/ppermute | solution.py:520
  67.8 5.6 %collective-permute-start.7 = (f32[16,128]{1,0:T(8,128)S(1)}, f32[16,128]{1,0:T(8,128)S(1)}, u32[]{:S(2)}, u32[]{:S(2)}) collective-permute-start(f32[16,128]{1,0:T(8,128)S(1)} %chip_bias.1.mine_ref), channel_id=1, source_target_pairs={{0,2},{2,0},{4,6},{6,4},{8,10},{10,8},{12,14},{14,12},{1,3},{3,1},... | collective-permute-start | bytes 24584 | tf_op jit(solution)/shard_map/ppermute | solution.py:520
  68.3 11.0 %collective-permute-start.18 = (bf16[128,1024]{1,0:T(8,128)(2,1)S(1)}, bf16[128,1024]{1,0:T(8,128)(2,1)S(1)}, u32[]{:S(2)}, u32[]{:S(2)}) collective-permute-start(bf16[128,1024]{1,0:T(8,128)(2,1)S(1)} %copy-done.10), channel_id=1, source_target_pairs={{0,12},{2,14},{4,8},{6,10},{8,4},{10,6},{12,0},{14,2},{1,13},{3,15... | collective-permute-start | bytes 786440 | tf_op jit(solution)/shard_map/ppermute | solution.py:516
  73.4 3.9 %collective-permute-start.8 = (bf16[512,1024]{1,0:T(8,128)(2,1)S(1)}, bf16[512,1024]{1,0:T(8,128)(2,1)S(1)}, u32[]{:S(2)}, u32[]{:S(2)}) collective-permute-start(bf16[512,1024]{1,0:T(8,128)(2,1)S(1)} %pad_maximum_fusion.refs_2_), channel_id=1, source_target_pairs={{0,2},{2,0},{4,6},{6,4},{8,10},{10,8},{12,14},{14,12},{1,3},{3,1},... | collective-permute-start | bytes 3145736 | tf_op jit(solution)/shard_map/ppermute | solution.py:520
  73.4 16.1 %collective-permute-start.21 = (bf16[4,128,256]{2,1,0:T(8,128)(2,1)S(1)}, bf16[4,128,256]{2,1,0:T(8,128)(2,1)S(1)}, u32[]{:S(2)}, u32[]{:S(2)}) collective-permute-start(bf16[4,128,256]{2,1,0:T(8,128)(2,1)S(1)} %collective-permute-done.20.refs_2_), channel_id=1, source_target_pairs={{0,4},{2,6},{4,0},{6,2},{8,12},{10,14},{12,8},{14,10},{1,5},{3,7},... | collective-permute-start | bytes 786440 | tf_op jit(solution)/shard_map/ppermute | solution.py:516
  76.2 4.2 %collective-permute-start.15 = (bf16[128,1024]{1,0:T(8,128)(2,1)S(1)}, bf16[128,1024]{1,0:T(8,128)(2,1)S(1)}, u32[]{:S(2)}, u32[]{:S(2)}) collective-permute-start(bf16[128,1024]{1,0:T(8,128)(2,1)S(1)} %collective-permute-done.14), channel_id=1, source_target_pairs={{0,2},{2,0},{4,6},{6,4},{8,10},{10,8},{12,14},{14,12},{1,3},{3,1},... | collective-permute-start | bytes 786440 | tf_op jit(solution)/shard_map/ppermute | solution.py:520
  76.2 10.0 %collective-permute-start.17 = (bf16[512,1024]{1,0:T(8,128)(2,1)S(1)}, bf16[512,1024]{1,0:T(8,128)(2,1)S(1)}, u32[]{:S(2)}, u32[]{:S(2)}) collective-permute-start(bf16[512,1024]{1,0:T(8,128)(2,1)S(1)} %collective-permute-done.16.refs_3_), channel_id=1, source_target_pairs={{0,2},{2,0},{4,6},{6,4},{8,10},{10,8},{12,14},{14,12},{1,3},{3,1},... | collective-permute-start | bytes 3145736 | tf_op jit(solution)/shard_map/ppermute | solution.py:520
  77.3 7.2 %copy-start.4 = (bf16[4,128,256]{2,1,0:T(8,128)(2,1)S(1)}, bf16[4,128,256]{2,1,0:T(8,128)(2,1)}, u32[]{:S(2)}) copy-start(bf16[4,128,256]{2,1,0:T(8,128)(2,1)} %copy-done.3) | copy-start | bytes 786436
  77.3 7.2 %collective-permute-start.11 = (f32[16,128]{1,0:T(8,128)S(1)}, f32[16,128]{1,0:T(8,128)S(1)}, u32[]{:S(2)}, u32[]{:S(2)}) collective-permute-start(f32[16,128]{1,0:T(8,128)S(1)} %get-tuple-element.44.field_ref), channel_id=1, source_target_pairs={{0,4},{2,6},{4,0},{6,2},{8,12},{10,14},{12,8},{14,10},{1,5},{3,7},... | collective-permute-start | bytes 24584 | tf_op jit(solution)/shard_map/ppermute | solution.py:516
  79.3 5.3 %collective-permute-start.12 = (f32[16,128]{1,0:T(8,128)S(1)}, f32[16,128]{1,0:T(8,128)S(1)}, u32[]{:S(2)}, u32[]{:S(2)}) collective-permute-start(f32[16,128]{1,0:T(8,128)S(1)} %get-tuple-element.44.field_ref), channel_id=1, source_target_pairs={{0,8},{2,10},{4,12},{6,14},{8,0},{10,2},{12,4},{14,6},{1,9},{3,11}... | collective-permute-start | bytes 24584 | tf_op jit(solution)/shard_map/ppermute | solution.py:516
  80.4 5.7 %collective-permute-start.13 = (f32[16,128]{1,0:T(8,128)S(1)}, f32[16,128]{1,0:T(8,128)S(1)}, u32[]{:S(2)}, u32[]{:S(2)}) collective-permute-start(f32[16,128]{1,0:T(8,128)S(1)} %get-tuple-element.44.field_ref), channel_id=1, source_target_pairs={{0,12},{2,14},{4,8},{6,10},{8,4},{10,6},{12,0},{14,2},{1,13},{3,15... | collective-permute-start | bytes 24584 | tf_op jit(solution)/shard_map/ppermute | solution.py:516
  84.5 9.8 %collective-permute-start.22 = (bf16[4,128,256]{2,1,0:T(8,128)(2,1)S(1)}, bf16[4,128,256]{2,1,0:T(8,128)(2,1)S(1)}, u32[]{:S(2)}, u32[]{:S(2)}) collective-permute-start(bf16[4,128,256]{2,1,0:T(8,128)(2,1)S(1)} %copy-done.4), channel_id=1, source_target_pairs={{0,2},{2,0},{4,6},{6,4},{8,10},{10,8},{12,14},{14,12},{1,3},{3,1},... | collective-permute-start | bytes 786440 | tf_op jit(solution)/shard_map/ppermute | solution.py:520
  84.6 8.7 %collective-permute-start.19 = (bf16[128,1024]{1,0:T(8,128)(2,1)S(1)}, bf16[128,1024]{1,0:T(8,128)(2,1)S(1)}, u32[]{:S(2)}, u32[]{:S(2)}) collective-permute-start(bf16[128,1024]{1,0:T(8,128)(2,1)S(1)} %collective-permute-done.18.mine), channel_id=1, source_target_pairs={{0,1},{1,0},{2,3},{3,2},{4,5},{5,4},{6,7},{7,6},{8,9},{9,8},{10,11... | collective-permute-start | bytes 786440 | tf_op jit(solution)/shard_map/ppermute | solution.py:524
  86.1 8.3 %collective-permute-start.23 = (bf16[4,128,256]{2,1,0:T(8,128)(2,1)S(1)}, bf16[4,128,256]{2,1,0:T(8,128)(2,1)S(1)}, u32[]{:S(2)}, u32[]{:S(2)}) collective-permute-start(bf16[4,128,256]{2,1,0:T(8,128)(2,1)S(1)} %collective-permute-done.6.refs_1_), channel_id=1, source_target_pairs={{0,2},{2,0},{4,6},{6,4},{8,10},{10,8},{12,14},{14,12},{1,3},{3,1},... | collective-permute-start | bytes 786440 | tf_op jit(solution)/shard_map/ppermute | solution.py:520
  86.2 8.1 %collective-permute-start.24 = (bf16[4,128,256]{2,1,0:T(8,128)(2,1)S(1)}, bf16[4,128,256]{2,1,0:T(8,128)(2,1)S(1)}, u32[]{:S(2)}, u32[]{:S(2)}) collective-permute-start(bf16[4,128,256]{2,1,0:T(8,128)(2,1)S(1)} %collective-permute-done.20.refs_2_), channel_id=1, source_target_pairs={{0,2},{2,0},{4,6},{6,4},{8,10},{10,8},{12,14},{14,12},{1,3},{3,1},... | collective-permute-start | bytes 786440 | tf_op jit(solution)/shard_map/ppermute | solution.py:520
  89.5 4.9 %collective-permute-start.25 = (bf16[4,128,256]{2,1,0:T(8,128)(2,1)S(1)}, bf16[4,128,256]{2,1,0:T(8,128)(2,1)S(1)}, u32[]{:S(2)}, u32[]{:S(2)}) collective-permute-start(bf16[4,128,256]{2,1,0:T(8,128)(2,1)S(1)} %collective-permute-done.21.refs_3_), channel_id=1, source_target_pairs={{0,2},{2,0},{4,6},{6,4},{8,10},{10,8},{12,14},{14,12},{1,3},{3,1},... | collective-permute-start | bytes 786440 | tf_op jit(solution)/shard_map/ppermute | solution.py:520
  95.3 12.4 %collective-permute-start.26 = (bf16[4,128,256]{2,1,0:T(8,128)(2,1)S(1)}, bf16[4,128,256]{2,1,0:T(8,128)(2,1)S(1)}, u32[]{:S(2)}, u32[]{:S(2)}) collective-permute-start(bf16[4,128,256]{2,1,0:T(8,128)(2,1)S(1)} %get-tuple-element.54.refs_0_), channel_id=1, source_target_pairs={{0,4},{2,6},{4,0},{6,2},{8,12},{10,14},{12,8},{14,10},{1,5},{3,7},... | collective-permute-start | bytes 786440 | tf_op jit(solution)/shard_map/ppermute | solution.py:516
  95.4 9.5 %collective-permute-start.27 = (bf16[2,128,256]{2,1,0:T(8,128)(2,1)S(1)}, bf16[2,128,256]{2,1,0:T(8,128)(2,1)S(1)}, u32[]{:S(2)}, u32[]{:S(2)}) collective-permute-start(bf16[2,128,256]{2,1,0:T(8,128)(2,1)S(1)} %get-tuple-element.59), channel_id=1, source_target_pairs={{0,8},{2,10},{4,12},{6,14},{8,0},{10,2},{12,4},{14,6},{1,9},{3,11}... | collective-permute-start | bytes 393224 | tf_op jit(solution)/shard_map/ppermute | solution.py:516
  97.1 17.1 %collective-permute-start.29 = (bf16[4,128,256]{2,1,0:T(8,128)(2,1)S(1)}, bf16[4,128,256]{2,1,0:T(8,128)(2,1)S(1)}, u32[]{:S(2)}, u32[]{:S(2)}) collective-permute-start(bf16[4,128,256]{2,1,0:T(8,128)(2,1)S(1)} %get-tuple-element.54.refs_0_), channel_id=1, source_target_pairs={{0,2},{2,0},{4,6},{6,4},{8,10},{10,8},{12,14},{14,12},{1,3},{3,1},... | collective-permute-start | bytes 786440 | tf_op jit(solution)/shard_map/ppermute | solution.py:520
  97.1 12.7 %collective-permute-start.28 = (bf16[2,128,256]{2,1,0:T(8,128)(2,1)S(1)}, bf16[2,128,256]{2,1,0:T(8,128)(2,1)S(1)}, u32[]{:S(2)}, u32[]{:S(2)}) collective-permute-start(bf16[2,128,256]{2,1,0:T(8,128)(2,1)S(1)} %get-tuple-element.58), channel_id=1, source_target_pairs={{0,8},{2,10},{4,12},{6,14},{8,0},{10,2},{12,4},{14,6},{1,9},{3,11}... | collective-permute-start | bytes 393224 | tf_op jit(solution)/shard_map/ppermute | solution.py:516
  107.7 6.5 %collective-permute-start.30 = (bf16[4,128,256]{2,1,0:T(8,128)(2,1)S(1)}, bf16[4,128,256]{2,1,0:T(8,128)(2,1)S(1)}, u32[]{:S(2)}, u32[]{:S(2)}) collective-permute-start(bf16[4,128,256]{2,1,0:T(8,128)(2,1)S(1)} %collective-permute-done.26.refs_1_), channel_id=1, source_target_pairs={{0,2},{2,0},{4,6},{6,4},{8,10},{10,8},{12,14},{14,12},{1,3},{3,1},... | collective-permute-start | bytes 786440 | tf_op jit(solution)/shard_map/ppermute | solution.py:520
  107.7 2.2 %collective-permute-start.31 = (bf16[2,128,256]{2,1,0:T(8,128)(2,1)S(1)}, bf16[2,128,256]{2,1,0:T(8,128)(2,1)S(1)}, u32[]{:S(2)}, u32[]{:S(2)}) collective-permute-start(bf16[2,128,256]{2,1,0:T(8,128)(2,1)S(1)} %collective-permute-done.27.refs_2_), channel_id=1, source_target_pairs={{0,2},{2,0},{4,6},{6,4},{8,10},{10,8},{12,14},{14,12},{1,3},{3,1},... | collective-permute-start | bytes 393224 | tf_op jit(solution)/shard_map/ppermute | solution.py:520
  108.2 6.0 %collective-permute-start.33 = (bf16[2,128,256]{2,1,0:T(8,128)(2,1)S(1)}, bf16[2,128,256]{2,1,0:T(8,128)(2,1)S(1)}, u32[]{:S(2)}, u32[]{:S(2)}) collective-permute-start(bf16[2,128,256]{2,1,0:T(8,128)(2,1)S(1)} %collective-permute-done.27.refs_2_), channel_id=1, source_target_pairs={{0,4},{2,6},{4,0},{6,2},{8,12},{10,14},{12,8},{14,10},{1,5},{3,7},... | collective-permute-start | bytes 393224 | tf_op jit(solution)/shard_map/ppermute | solution.py:516
  109.9 4.3 %collective-permute-start.32 = (bf16[2,128,256]{2,1,0:T(8,128)(2,1)S(1)}, bf16[2,128,256]{2,1,0:T(8,128)(2,1)S(1)}, u32[]{:S(2)}, u32[]{:S(2)}) collective-permute-start(bf16[2,128,256]{2,1,0:T(8,128)(2,1)S(1)} %collective-permute-done.28.refs_3_), channel_id=1, source_target_pairs={{0,2},{2,0},{4,6},{6,4},{8,10},{10,8},{12,14},{14,12},{1,3},{3,1},... | collective-permute-start | bytes 393224 | tf_op jit(solution)/shard_map/ppermute | solution.py:520
  109.9 6.5 %collective-permute-start.34 = (bf16[2,128,256]{2,1,0:T(8,128)(2,1)S(1)}, bf16[2,128,256]{2,1,0:T(8,128)(2,1)S(1)}, u32[]{:S(2)}, u32[]{:S(2)}) collective-permute-start(bf16[2,128,256]{2,1,0:T(8,128)(2,1)S(1)} %collective-permute-done.28.refs_3_), channel_id=1, source_target_pairs={{0,4},{2,6},{4,0},{6,2},{8,12},{10,14},{12,8},{14,10},{1,5},{3,7},... | collective-permute-start | bytes 393224 | tf_op jit(solution)/shard_map/ppermute | solution.py:516
  114.2 2.2 %collective-permute-start.35 = (bf16[2,128,256]{2,1,0:T(8,128)(2,1)S(1)}, bf16[2,128,256]{2,1,0:T(8,128)(2,1)S(1)}, u32[]{:S(2)}, u32[]{:S(2)}) collective-permute-start(bf16[2,128,256]{2,1,0:T(8,128)(2,1)S(1)} %collective-permute-done.33.refs_0_), channel_id=1, source_target_pairs={{0,2},{2,0},{4,6},{6,4},{8,10},{10,8},{12,14},{14,12},{1,3},{3,1},... | collective-permute-start | bytes 393224 | tf_op jit(solution)/shard_map/ppermute | solution.py:520
  116.4 1.3 %collective-permute-start.36 = (bf16[2,128,256]{2,1,0:T(8,128)(2,1)S(1)}, bf16[2,128,256]{2,1,0:T(8,128)(2,1)S(1)}, u32[]{:S(2)}, u32[]{:S(2)}) collective-permute-start(bf16[2,128,256]{2,1,0:T(8,128)(2,1)S(1)} %collective-permute-done.34.refs_1_), channel_id=1, source_target_pairs={{0,2},{2,0},{4,6},{6,4},{8,10},{10,8},{12,14},{14,12},{1,3},{3,1},... | collective-permute-start | bytes 393224 | tf_op jit(solution)/shard_map/ppermute | solution.py:520
  (2 other events, 4.0 us)
